TPU v7x, 32 devices: a whole 2x2x4 slice. The times are simulated.
32 devices in a mesh: grp: 2 (over x), exp: 16 (over z, y, core).
Axes of the slice: x: 2, y: 2, z: 4, core: 2. Of those that a mesh axis runs over, the one named last changes fastest.
Arguments:
- latent_in: bfloat16 [2048, 1024], P(('grp', 'exp')), parts along dimension 0, may hold values from -6 to 6
- routes: int32 [2048, 8], P(('grp', 'exp')), parts along dimension 0, may hold values from 0 to 31, all different within a row; in each aligned block of 64 rows (0 to 63, 64 to 127, ...) at most 32 rows name the same one
- router: bfloat16 [1024, 32], P(None, 'exp'), may hold values from -0.1875 to 0.1875
- gate_up: bfloat16 [32, 1024, 2048], P('exp'), may hold values from -0.1875 to 0.1875
- expert_down: bfloat16 [32, 1024, 1024], P('exp'), may hold values from -0.1875 to 0.1875
Outputs:
- mixed: bfloat16 [2048, 1024], P(('grp', 'exp')), parts along dimension 0
There are 2 independent parts, one for each index of `grp`. A program takes and returns all parts, laid end to end along the dimension named above; an argument that names none is the same for every part. Nothing has to cross between parts.
Inputs may be any that keep to these rules, and one draw needn't show every extreme that they name: `routes`: each token names 8 different experts. Among the 64 tokens of one device (aligned blocks of rows), no expert is named more than 32 times, and in every draw some device names some expert exactly 32 times.
All inputs are finite; a program needn't handle non-finite values.
Results may differ from a plain program's by a relative error of at most 0.0075.
Values may be sent and summed in bfloat16 or wider, within the bound.
No kernel may reach another device: no remote copies, remote signals or barrier semaphores. Data moves between devices by JAX's collectives and lax.ppermute only.
A program may use at most 64 MiB of HBM per device.

v0:
```python
import jax
import jax.numpy as jnp
from jax import lax
from jax.sharding import PartitionSpec as P


def on_device(latent_in, routes, router, gate_up, expert_down):
    tok_rows = latent_in.shape[0]
    top_count = routes.shape[1]
    ndevices = lax.axis_size("exp")
    local_experts = gate_up.shape[0]
    experts = local_experts * ndevices
    capacity = 2 * ((tok_rows * top_count + experts - 1) // experts)
    inner_width = expert_down.shape[1]
    lat_width = latent_in.shape[1]
    expert_ids = routes.reshape(tok_rows * top_count)
    labels = jnp.arange(experts, dtype=jnp.int32)
    matches = (expert_ids[:, None] == labels[None, :]).astype(jnp.int32)
    before = jnp.cumsum(matches, axis=0) - matches
    position = jnp.sum(before * matches, axis=1)
    slot_index = expert_ids * capacity + position
    repeated = jnp.repeat(latent_in, top_count, axis=0)
    outgoing = jnp.zeros((experts * capacity, lat_width), jnp.bfloat16).at[slot_index].set(repeated)
    outgoing = outgoing.reshape(ndevices, local_experts, capacity, lat_width)
    arrived = lax.all_to_all(outgoing, "exp", split_axis=0, concat_axis=0, tiled=True)
    gate_both = jnp.einsum("nesl,elf->nesf", arrived, gate_up, preferred_element_type=jnp.float32)
    inner = (jax.nn.silu(gate_both[..., :inner_width]) * gate_both[..., inner_width:]).astype(
        jnp.bfloat16
    )
    results = jnp.einsum(
        "nesf,efl->nesl", inner, expert_down, preferred_element_type=jnp.float32
    ).astype(jnp.bfloat16)
    returned = lax.all_to_all(results, "exp", split_axis=0, concat_axis=0, tiled=True)
    all_router = lax.all_gather(router, "exp", axis=1, tiled=True)
    logits = jnp.dot(latent_in, all_router, preferred_element_type=jnp.float32)
    score = jax.nn.sigmoid(jnp.take_along_axis(logits, routes, axis=1))
    weight = score / jnp.sum(score, axis=1, keepdims=True)
    picked = returned.reshape(experts * capacity, lat_width)[slot_index].astype(jnp.float32)
    picked = picked.reshape(tok_rows, top_count, lat_width) * weight[:, :, None]
    return jnp.sum(picked, axis=1).astype(jnp.bfloat16)


def solution(mesh):
    placed = (
        P(("grp", "exp"), None),
        P(("grp", "exp"), None),
        P(None, "exp"),
        P("exp", None, None),
        P("exp", None, None),
    )
    return jax.shard_map(
        on_device, mesh=mesh, in_specs=placed, out_specs=P(("grp", "exp"), None), check_vma=False
    )
```

profile of v0, /device:TPU:9, one launch (start us, length us, event | category | flops | bytes accessed | tf_op | source)
XLA Modules:
  0.0 142.6 jit_solution(2922580365938295544)
XLA Ops:
  0.0 0.8 copy.30
  0.8 0.1 eq.29
  0.9 0.1 eq.25
  1.0 0.7 broadcast_multiply_fusion
  1.7 1.2 reduce-window.6
  2.9 0.2 slice_reduce_fusion
  3.1 0.1 copy.29
  3.2 0.1 mul.36
  3.3 0.1 fusion.22
  3.4 3.2 %scatter_custom_fusion = bf16[1024,1024]{1,0:T(8,128)(2,1)S(1)} fusion(s32[512]{0:T(512)S(1)} %bitcast.58, bf16[]{:T(256)} %constant.12.clone.1, bf16[64,1024]{1,0:T(8,128)(2,1)S(1)} %copy-done), kind=kCustom, calls=%fused_computation.15 | custom fusion | bytes 2228226 | tf_op jit(solution)/shard_map/scatter | solution.py:23
  6.7 54.3 %all_to_all.10 = bf16[16,2,32,1024]{3,2,1,0:T(8,128)(2,1)S(1)} all-to-all(bf16[16,2,32,1024]{3,2,1,0:T(8,128)(2,1)S(1)} %bitcast.57), channel_id=1, replica_groups=mesh['grp'=2,'exp'=16] {'exp'}, dimensions={0} | all-to-all | bytes 4194304 | tf_op jit(solution)/shard_map/all_to_all | solution.py:25
  60.9 7.1 %fusion.2 = f32[16,2,32,2048]{3,2,0,1:T(8,128)S(1)} fusion(bf16[2,1024,2048]{2,1,0:T(8,128)(2,1)} %param.8, bf16[16,2,32,1024]{3,2,1,0:T(8,128)(2,1)S(1)} %all_to_all.10), kind=kOutput, calls=%fused_computation.5 | convolution fusion | flops 4294967296 | bytes 18874368 | tf_op jit(solution)/shard_map/nesl,elf->nesf/dot_general | solution.py:26
  68.0 2.4 %convert_bitcast_fusion = bf16[16,2,32,1024]{3,2,0,1:T(8,128)(2,1)S(1)} fusion(bf16[2,1024,1024]{2,1,0:T(8,128)(2,1)S(1)} %copy-done.3, f32[16,2,32,2048]{3,2,0,1:T(8,128)S(1)} %fusion.2), kind=kOutput, calls=%fused_computation.13 | convolution fusion | flops 2154823680 | bytes 14680064 | tf_op jit(solution)/shard_map/nesf,efl->nesl/dot_general | solution.py:30
  70.4 1.6 %copy.34 = bf16[16,2,32,1024]{3,2,1,0:T(8,128)(2,1)} copy(bf16[16,2,32,1024]{3,2,0,1:T(8,128)(2,1)S(1)} %convert_bitcast_fusion) | data formatting | bytes 4194304 | tf_op jit(solution)/shard_map/convert_element_type | solution.py:32
  72.0 4.6 %all-to-all-start.1 = ((bf16[16,2,32,1024]{3,2,1,0:T(8,128)(2,1)}), bf16[16,2,32,1024]{3,2,1,0:T(8,128)(2,1)S(1)}, u32[]{:S(2)}, u32[]{:S(2)}) async-start(bf16[16,2,32,1024]{3,2,1,0:T(8,128)(2,1)} %copy.34), calls=%async_computation.1 | async-start | bytes 4194304 | tf_op jit(solution)/shard_map/all_to_all | solution.py:33
  76.6 58.0 %all-gather = bf16[16,2,1024]{2,1,0:T(2,128)(2,1)S(1)} all-gather(bf16[1,2,1024]{2,1,0:T(2,128)(2,1)S(1)} %bitcast.61), channel_id=1, replica_groups=mesh['grp'=2,'exp'=16] {'exp'}, dimensions={0}, use_global_device_ids=true | all-gather | bytes 69632 | tf_op jit(solution)/shard_map/all_gather | solution.py:34
  134.6 0.1 copy.35
  134.7 0.1 reshape.97
  134.8 0.1 fusion.25
  134.9 3.9 %gather_fusion.1 = f32[512]{0:T(512)S(1)} fusion(f32[64,32]{0,1:T(8,128)S(1)} %fusion.25, s32[512]{0:T(512)S(1)} %reshape.97), kind=kCustom, calls=%fused_computation.1 | custom fusion | bytes 8192 | tf_op jit(solution)/shard_map/jit(take_along_axis)/gather | solution.py:36
  138.8 0.1 reshape.100
  139.1 0.1 copy.37
  139.2 2.1 %gather_fusion = bf16[512,1024]{1,0:T(8,128)(2,1)S(1)} fusion(bf16[1024,1024]{1,0:T(8,128)(2,1)S(1)} %bitcast.56, s32[1024]{0:T(1024)S(1)} %pad_clamp_fusion), kind=kCustom, calls=%fused_computation | custom fusion | bytes 2099200 | tf_op jit(solution)/shard_map/gather | solution.py:38
  141.2 1.3 fusion.9
  (19 shorter events, 0.2 us)
Async XLA Ops:
  0.0 3.4 %copy-start = (bf16[64,1024]{1,0:T(8,128)(2,1)S(1)}, bf16[64,1024]{1,0:T(8,128)(2,1)}, u32[]{:S(2)}) copy-start(bf16[64,1024]{1,0:T(8,128)(2,1)} %param.5) | copy-start | bytes 393220
  60.9 7.1 %copy-start.3 = (bf16[2,1024,1024]{2,1,0:T(8,128)(2,1)S(1)}, bf16[2,1024,1024]{2,1,0:T(8,128)(2,1)}, u32[]{:S(2)}) copy-start(bf16[2,1024,1024]{2,1,0:T(8,128)(2,1)} %param.9) | copy-start | bytes 12582916
  70.4 6.2 %copy-start.2 = (bf16[1024,2]{0,1:T(2,128)(2,1)S(1)}, bf16[1024,2]{0,1:T(2,128)(2,1)}, u32[]{:S(2)}) copy-start(bf16[1024,2]{0,1:T(2,128)(2,1)} %param.7) | copy-start | bytes 12292
  70.4 64.2 %copy-start.1 = (s32[64,8]{0,1:T(8,128)S(1)}, s32[64,8]{0,1:T(8,128)}, u32[]{:S(2)}) copy-start(s32[64,8]{0,1:T(8,128)} %param.6) | copy-start | bytes 6148
  72.0 67.2 %all-to-all-start.1 = ((bf16[16,2,32,1024]{3,2,1,0:T(8,128)(2,1)}), bf16[16,2,32,1024]{3,2,1,0:T(8,128)(2,1)S(1)}, u32[]{:S(2)}, u32[]{:S(2)}) async-start(bf16[16,2,32,1024]{3,2,1,0:T(8,128)(2,1)} %copy.34), calls=%async_computation.1 | async-start | bytes 4194304 | tf_op jit(solution)/shard_map/all_to_all | solution.py:33
where the time goes:
time: 143 us
  blocking collectives  112 us (78%)
  local copies, waits for them, and re-layouts  12.6 us (9%)
  matrix products  9.59 us (7%)
  starting transfers between devices  4.56 us (3%)
  other arithmetic  3.43 us (2%)
    all_gather x1, blocking collectives, on_device(): all_router = lax.all_gather(router, 'exp', axis=1, tiled=True)  58 us
    all_to_all x1, blocking collectives, on_device(): lax.all_to_all(outgoing, 'exp', split_axis=0, concat_axis=0, tiled=True)  54.3 us
    dot_general x1, matrix products, on_device(): jnp.einsum('nesl,elf->nesf', arrived, gate_up, preferred_element_type=jnp...  7.05 us
    all_to_all x1, starting transfers between devices, on_device(): lax.all_to_all(results, 'exp', split_axis=0, concat_axis=0, tiled=True)  4.56 us
    gather x5, local copies, waits for them, and re-layouts, on_device(): score = jax.nn.sigmoid(jnp.take_along_axis(logits, routes, axis=1))  4.23 us
    scatter x1, local copies, waits for them, and re-layouts, on_device(): jnp.zeros((experts * capacity, lat_width), jnp.bfloat16).at[slot_index]  3.23 us
  transfers between devices with their start and end apart: 1, of which 0 were waited for; matrix products, arithmetic and copies ran while one was open for 3% of the time, Pallas kernels for 0%

commit v1 on v0

v1 whole, which is shorter than its diff:
```python
import jax
import jax.numpy as jnp
from jax import lax
from jax.sharding import PartitionSpec as P


def on_device(latent_in, routes, router, gate_up, expert_down):
    n_dev = lax.axis_size("exp")
    local = gate_up.shape[0]
    eff = expert_down.shape[1]
    rows, lat = latent_in.shape
    me = lax.axis_index("exp")
    tokens = lax.all_gather(latent_in, "exp", axis=0, tiled=True)
    chosen = lax.all_gather(routes, "exp", axis=0, tiled=True)
    columns = lax.all_gather(router, "exp", axis=1, tiled=True)

    def part(tok, ids):
        logits = jnp.dot(tok, columns, preferred_element_type=jnp.float32)
        labels = jnp.arange(n_dev * local, dtype=jnp.int32)
        mask = jnp.any(ids[:, :, None] == labels[None, None, :], axis=1)
        score = jnp.where(mask, jax.nn.sigmoid(logits), 0.0)
        weight = score / jnp.sum(score, axis=1, keepdims=True)
        mine = lax.dynamic_slice_in_dim(weight, me * local, local, axis=1)
        inner = []
        for e in range(local):
            both = jnp.dot(tok, gate_up[e], preferred_element_type=jnp.float32)
            one = jax.nn.silu(both[:, :eff]) * both[:, eff:] * mine[:, e : e + 1]
            inner.append(one.astype(jnp.bfloat16))
        inner = jnp.concatenate(inner, axis=1)
        down = expert_down.reshape(local * eff, lat)
        return jnp.dot(inner, down, preferred_element_type=jnp.float32).astype(jnp.bfloat16)

    step = 16 * rows if n_dev == 16 else 4 * rows
    if n_dev * rows == step:
        sums = part(tokens, chosen)
    else:
        sums = lax.map(
            lambda pair: part(*pair),
            (tokens.reshape(-1, step, lat), chosen.reshape(-1, step, chosen.shape[1])),
        ).reshape(n_dev * rows, lat)
    return lax.psum_scatter(sums, "exp", scatter_dimension=0, tiled=True)


def solution(mesh):
    placed = (
        P(("grp", "exp"), None),
        P(("grp", "exp"), None),
        P(None, "exp"),
        P("exp", None, None),
        P("exp", None, None),
    )
    return jax.shard_map(
        on_device, mesh=mesh, in_specs=placed, out_specs=P(("grp", "exp"), None), check_vma=False
    )
```

time: 143 us -> 144 us (level)
  the two profiles are of different devices: /device:TPU:9 before, /device:TPU:0 now
where the time goes in v1:
time: 144 us
  waiting for transfers between devices  66 us (46%)
  blocking collectives  41.6 us (29%)
  matrix products  19.8 us (14%)
  between operations  13.5 us (9%)
  other arithmetic  2.83 us (2%)
    reduce_scatter x1, waiting for transfers between devices, on_device(): return lax.psum_scatter(sums, 'exp', scatter_dimension=0, tiled=True)  60.5 us
    all_gather x1, blocking collectives, on_device(): chosen = lax.all_gather(routes, 'exp', axis=0, tiled=True)  23.5 us
    all_gather x1, blocking collectives, on_device(): columns = lax.all_gather(router, 'exp', axis=1, tiled=True)  18.1 us
    dot_general x2, matrix products, part(): both = jnp.dot(tok, gate_up[e], preferred_element_type=jnp.float32)  11.6 us
    dot_general x1, matrix products, part(): jnp.dot(inner, down, preferred_element_type=jnp.float32)  5.73 us
    all_gather x1, waiting for transfers between devices, on_device(): tokens = lax.all_gather(latent_in, 'exp', axis=0, tiled=True)  4.78 us
  transfers between devices with their start and end apart: 2, of which 2 were waited for; matrix products, arithmetic and copies ran while one was open for 0% of the time, Pallas kernels for 0%

profile of v1, /device:TPU:0, one launch (start us, length us, event | category | flops | bytes accessed | tf_op | source)
XLA Modules:
  0.0 143.9 jit_solution(8757331629636839386)
XLA Ops:
  6.5 0.0 all-gather.4.cloned.1.call-start
  6.5 0.7 all-gather.4.cloned.1.call-update
  7.3 0.0 reduce-scatter.2.cloned.1.call-start
  7.3 23.5 %all-gather = s32[16,64,8]{1,2,0:T(8,128)S(1)} all-gather(s32[1,64,8]{1,2,0:T(8,128)} %bitcast.22), channel_id=1, replica_groups=mesh['grp'=2,'exp'=16] {'exp'}, dimensions={0}, use_global_device_ids=true | all-gather | bytes 34816 | tf_op jit(solution)/shard_map/all_gather | solution.py:14
  30.8 0.1 reshape.7
  30.9 18.1 %all-gather.1 = bf16[16,2,1024]{2,1,0:T(2,128)(2,1)S(1)} all-gather(bf16[1,2,1024]{2,1,0:T(2,128)(2,1)} %bitcast.23), channel_id=1, replica_groups=mesh['grp'=2,'exp'=16] {'exp'}, dimensions={0}, use_global_device_ids=true | all-gather | bytes 69632 | tf_op jit(solution)/shard_map/all_gather | solution.py:15
  49.0 0.1 fusion.21
  49.1 4.8 %all-gather.4.cloned.1.call-done = bf16[1024,1024]{1,0:T(8,128)(2,1)} async-done(((bf16[64,1024]{1,0:T(8,128)(2,1)}), bf16[1024,1024]{1,0:T(8,128)(2,1)}) %all-gather.4.cloned.1.call-update) | async-done | bytes 2097168 | tf_op jit(solution)/shard_map/all_gather | solution.py:13
  53.9 0.0 slice-start
  53.9 2.5 %fusion.24 = (f32[1024]{0:T(1024)S(1)}, f32[1024,32]{0,1:T(8,128)S(1)}) fusion(pred[1024,32]{0,1:T(8,128)(4,1)S(1)} %fusion.21, bf16[1024,1024]{1,0:T(8,128)(2,1)} %all-gather.4.cloned.1.call-done, bf16[32,1024]{1,0:T(8,128)(2,1)S(1)} %reshape.9), kind=kOutput, calls=%fused_computation.27 | convolution fusion | flops 67271680 | bytes 2330624 | tf_op jit(solution)/shard_map/dot_general | solution.py:18
  56.5 0.0 slice-start.1
  56.5 0.0 copy-start.1
  56.5 7.1 %fusion.8 = f32[1024,2048]{1,0:T(8,128)S(1)} fusion(bf16[1024,1024]{1,0:T(8,128)(2,1)} %all-gather.4.cloned.1.call-done, bf16[2,1024,2048]{2,1,0:T(8,128)(2,1)} %param.8), kind=kOutput, calls=%fused_computation.10 | convolution fusion | flops 4294967296 | bytes 14680064 | tf_op jit(solution)/shard_map/dot_general | solution.py:26
  63.6 0.0 slice-done
  63.6 0.0 slice-done.1
  63.6 0.0 copy-done.1
  63.6 4.5 %fusion.10 = f32[1024,2048]{1,0:T(8,128)S(1)} fusion(bf16[1024,1024]{1,0:T(8,128)(2,1)S(1)} %copy-done.1, bf16[2,1024,2048]{2,1,0:T(8,128)(2,1)S(1)} %bitcast.25), kind=kOutput, calls=%fused_computation.12 | convolution fusion | flops 4294967296 | bytes 14680064 | tf_op jit(solution)/shard_map/dot_general | solution.py:26
  68.1 0.0 copy-start
  68.1 2.7 %fusion.1 = (bf16[1024,1024]{1,0:T(8,128)(2,1)S(1)}, bf16[1024,1024]{1,0:T(8,128)(2,1)S(1)}) fusion(f32[1024,2048]{1,0:T(8,128)S(1)} %fusion.8, f32[1024]{0:T(1024)S(1)} %bitcast.21, f32[1024]{0:T(1024)S(1)} %bitcast.20, f32[1024,2048]{1,0:T(8,128)S(1)} %fusion.10), kind=kLoop, calls=%fused_computation.2 | loop fusion | flops 14680064 | bytes 20979712 | tf_op jit(solution)/shard_map/convert_element_type | solution.py:28
  70.8 0.0 copy-done
  70.8 5.7 %fusion.14 = bf16[1024,1024]{1,0:T(8,128)(2,1)} fusion(bf16[2048,1024]{1,0:T(8,128)(2,1)S(1)} %bitcast.26, bf16[1024,1024]{1,0:T(8,128)(2,1)S(1)} %get-tuple-element.9, bf16[1024,1024]{1,0:T(8,128)(2,1)S(1)} %get-tuple-element.10), kind=kOutput, calls=%fused_computation.16 | convolution fusion | flops 4304404480 | bytes 10485760 | tf_op jit(solution)/shard_map/dot_general | solution.py:31
  76.6 0.0 reduce-scatter.2.cloned.1.call-update
  76.6 60.5 %reduce-scatter.2.cloned.1.call-done = bf16[64,1024]{1,0:T(8,128)(2,1)} async-done(((bf16[1024,1024]{1,0:T(8,128)(2,1)}), bf16[64,1024]{1,0:T(8,128)(2,1)}) %reduce-scatter.2.cloned.1.call-update) | async-done | bytes 131088 | tf_op jit(solution)/shard_map/reduce_scatter | solution.py:41
  (5 shorter events, 0.1 us)
Async XLA Ops:
  6.5 47.4 %all-gather.4.cloned.1.call-start = ((), (), s32[]{:S(2)}) async-start(), calls=%async_computation.1 | async-start | bytes 2228224 | tf_op jit(solution)/shard_map/all_gather | solution.py:13
  7.3 129.8 %reduce-scatter.2.cloned.1.call-start = ((), (), s32[]{:S(2)}) async-start(), calls=%async_computation.2 | async-start | bytes 2228224 | tf_op jit(solution)/shard_map/reduce_scatter | solution.py:41
  53.9 9.7 %slice-start = ((s8[8388608]{0:T(1024)(128)(4,1)}), s8[4194304]{0:T(1024)(128)(4,1)S(1)}, s32[]{:S(2)}) async-start(s8[8388608]{0:T(1024)(128)(4,1)} %bitcast.24), calls=%async_computation.3 | async-start | bytes 8388608
  56.5 7.1 %slice-start.1 = ((s8[8388608]{0:T(1024)(128)(4,1)}), s8[4194304]{0:T(1024)(128)(4,1)S(1)}, s32[]{:S(2)}) async-start(s8[8388608]{0:T(1024)(128)(4,1)} %bitcast.24), calls=%async_computation.4 | async-start | bytes 8388608
  56.5 7.1 %copy-start.1 = (bf16[1024,1024]{1,0:T(8,128)(2,1)S(1)}, bf16[1024,1024]{1,0:T(8,128)(2,1)}, u32[]{:S(2)}) copy-start(bf16[1024,1024]{1,0:T(8,128)(2,1)} %all-gather.4.cloned.1.call-done) | copy-start | bytes 6291460
  68.1 2.7 %copy-start = (bf16[2,1024,1024]{2,1,0:T(8,128)(2,1)S(1)}, bf16[2,1024,1024]{2,1,0:T(8,128)(2,1)}, u32[]{:S(2)}) copy-start(bf16[2,1024,1024]{2,1,0:T(8,128)(2,1)} %param.9) | copy-start | bytes 12582916
Sparse Core Ops, SparseCore 0:
  9.5 44.3 all-gather.3
  76.7 60.3 reduce-scatter.1

commit v2 on v1

v2 whole, which is shorter than its diff:
```python
import jax
import jax.numpy as jnp
from jax import lax
from jax.sharding import PartitionSpec as P

GROUP = 16


def on_device(latent_in, routes, router, gate_up, expert_down):
    n_dev = lax.axis_size("exp")
    local = gate_up.shape[0]
    eff = expert_down.shape[1]
    rows, lat = latent_in.shape
    top = routes.shape[1]
    me = lax.axis_index("exp")

    def swap(x, bits):
        return lax.ppermute(x, "exp", [(i, i ^ bits) for i in range(n_dev)])

    per_row = local * lat // rows
    small = jnp.concatenate(
        [
            routes.astype(jnp.bfloat16),
            router.T.reshape(rows, per_row),
            jnp.zeros((rows, 128 - top - per_row), jnp.bfloat16),
        ],
        axis=1,
    )
    bit = 1
    while bit < n_dev:
        small = jnp.concatenate([small, swap(small, bit)], axis=0)
        bit *= 2
    small = small.reshape(n_dev, rows, 128)
    group_ids = small[:GROUP, :, :top]
    columns = small[:, :, top : top + per_row].reshape(n_dev * local, lat)
    labels = ((me ^ jnp.arange(n_dev, dtype=jnp.int32))[:, None] * local + jnp.arange(local)).reshape(-1)
    down = expert_down.reshape(local * eff, lat)

    def group_pass(mine, ids):
        ids = ids.astype(jnp.int32)
        batches = []
        for k in range(GROUP // 4):
            one = mine if k == 0 else swap(mine, 4 * k)
            pair = jnp.concatenate([one, swap(one, 2)], axis=0)
            batches.append((pair, swap(pair, 1)))
        total = None
        for k in range(GROUP // 4):
            pair, other = batches[k]
            tok = jnp.concatenate([pair, other], axis=0)
            tok_ids = jnp.concatenate([ids[4 * k + i] for i in (0, 2, 1, 3)], axis=0)
            logits = lax.dot_general(
                tok, columns, (((1,), (1,)), ((), ())), preferred_element_type=jnp.float32
            )
            mask = jnp.any(tok_ids[:, :, None] == labels[None, None, :], axis=1)
            score = jnp.where(mask, jax.nn.sigmoid(logits), 0.0)
            weight = score[:, :local] / jnp.sum(score, axis=1, keepdims=True)
            inner = []
            for e in range(local):
                both = jnp.dot(tok, gate_up[e], preferred_element_type=jnp.float32)
                one = jax.nn.silu(both[:, :eff]) * both[:, eff:] * weight[:, e : e + 1]
                inner.append(one.astype(jnp.bfloat16))
            sums = jnp.dot(
                jnp.concatenate(inner, axis=1), down, preferred_element_type=jnp.float32
            )
            half = 2 * rows
            sums = sums[:half] + swap(sums[half:].astype(jnp.bfloat16), 1).astype(jnp.float32)
            sums = sums[:rows] + swap(sums[rows:].astype(jnp.bfloat16), 2).astype(jnp.float32)
            if k > 0:
                sums = swap(sums.astype(jnp.bfloat16), 4 * k).astype(jnp.float32)
            total = sums if total is None else total + sums
        return total

    if n_dev == GROUP:
        return group_pass(latent_in, group_ids).astype(jnp.bfloat16)

    def next_group(x):
        return lax.ppermute(x, "exp", [(i, (i + GROUP) % n_dev) for i in range(n_dev)])

    def step(carry, _):
        mine, ids, total = carry
        total = total + group_pass(mine, ids)
        return (next_group(mine), next_group(ids), next_group(total)), None

    start = (latent_in, group_ids, jnp.zeros((rows, lat), jnp.float32))
    (_, _, total), _ = lax.scan(step, start, None, length=n_dev // GROUP)
    return total.astype(jnp.bfloat16)


def solution(mesh):
    placed = (
        P(("grp", "exp"), None),
        P(("grp", "exp"), None),
        P(None, "exp"),
        P("exp", None, None),
        P("exp", None, None),
    )
    return jax.shard_map(
        on_device, mesh=mesh, in_specs=placed, out_specs=P(("grp", "exp"), None), check_vma=False
    )
```

time: 144 us -> 87.7 us (0.61)
  blocking collectives: 41.6 us -> 0 us
  waiting for transfers between devices: 66 us -> 27.9 us
  starting transfers between devices: 0.04 us -> 24.3 us
  between operations: 13.5 us -> 0.61 us
  local copies, waits for them, and re-layouts: 0.16 us -> 6.09 us
  other arithmetic: 2.83 us -> 7.54 us
    reduce_scatter x1 -> x0, waiting for transfers between devices: 60.5 us -> none  [on_device(): return lax.psum_scatter(sums, 'exp', scatter_dimension=0, tiled=True)]
    all_gather x2 -> x0, blocking collectives: 41.6 us -> none  [the longest x1 23.5 us: on_device(): chosen = lax.all_gather(routes, 'exp', axis=0, tiled=True)]
    ppermute x0 -> x26, waiting for transfers between devices: none -> 27.9 us  [swap(): return lax.ppermute(x, 'exp', [(i, i ^ bits) for i in range(n_dev)])]
    ppermute x0 -> x26, starting transfers between devices: none -> 24.3 us  [swap(): return lax.ppermute(x, 'exp', [(i, i ^ bits) for i in range(n_dev)])]
    all_gather x1 -> x0, waiting for transfers between devices: 4.78 us -> none  [on_device(): tokens = lax.all_gather(latent_in, 'exp', axis=0, tiled=True)]
    concatenate x0 -> x9, other arithmetic: none -> 2.63 us  [the longest x4 1.68 us: group_pass(): pair = jnp.concatenate([one, swap(one, 2)], axis=0)]
    concatenate x0 -> x9, local copies, waits for them, and re-layouts: none -> 2.21 us  [the longest x4 1.17 us: group_pass(): tok_ids = jnp.concatenate([ids[4 * k + i] for i in (0, 2, 1, 3)], axis=0)]
    unnamed x10 -> x17, local copies, waits for them, and re-layouts: 0.13 us -> 2.25 us
  transfers between devices with their start and end apart: 2 -> 26, of which waited for: 2 -> 10; matrix products, arithmetic and copies ran while one was open for 0% -> 37% of each run, Pallas kernels for 0% -> 0%
where the time goes in v2:
time: 87.7 us; the launch traced here: 87.4 us
  waiting for transfers between devices  27.9 us (32%)
  starting transfers between devices  24.3 us (28%)
  matrix products  21 us (24%)
  other arithmetic  7.54 us (9%)
  local copies, waits for them, and re-layouts  6.09 us (7%)
    ppermute x26, waiting for transfers between devices, swap(): return lax.ppermute(x, 'exp', [(i, i ^ bits) for i in range(n_dev)])  27.9 us
    ppermute x26, starting transfers between devices, swap(): return lax.ppermute(x, 'exp', [(i, i ^ bits) for i in range(n_dev)])  24.3 us
    dot_general x8, matrix products, group_pass(): both = jnp.dot(tok, gate_up[e], preferred_element_type=jnp.float32)  14.7 us
    dot_general x4, matrix products, group_pass(): jnp.dot(jnp.concatenate(inner, axis=1), down, preferred_element_type=jnp....  5.15 us
    convert_element_type x8, other arithmetic, group_pass(): inner.append(one.astype(jnp.bfloat16))  2.66 us
    unnamed x17, local copies, waits for them, and re-layouts  2.25 us
  transfers between devices with their start and end apart: 26, of which 10 were waited for; matrix products, arithmetic and copies ran while one was open for 37% of the time, Pallas kernels for 0%

profile of v2, /device:TPU:0, one launch (start us, length us, event | category | flops | bytes accessed | tf_op | source)
XLA Modules:
  0.0 87.4 jit_solution(8251666803564359159)
XLA Ops:
  0.0 3.0 %collective-permute-start.8 = (bf16[64,1024]{1,0:T(8,128)(2,1)}, bf16[64,1024]{1,0:T(8,128)(2,1)S(1)}, u32[]{:S(2)}, u32[]{:S(2)}) collective-permute-start(bf16[64,1024]{1,0:T(8,128)(2,1)} %param.5), channel_id=1, source_target_pairs={{0,4},{1,5},{2,6},{3,7},{4,0},{5,1},{6,2},{7,3},{8,12},{9,13},{10,... | collective-permute-start | bytes 393224 | tf_op jit(solution)/shard_map/ppermute | solution.py:18
  3.0 2.6 %collective-permute-start.14 = (bf16[64,1024]{1,0:T(8,128)(2,1)}, bf16[64,1024]{1,0:T(8,128)(2,1)S(1)}, u32[]{:S(2)}, u32[]{:S(2)}) collective-permute-start(bf16[64,1024]{1,0:T(8,128)(2,1)} %param.5), channel_id=1, source_target_pairs={{0,8},{1,9},{2,10},{3,11},{4,12},{5,13},{6,14},{7,15},{8,0},{9,1},... | collective-permute-start | bytes 393224 | tf_op jit(solution)/shard_map/ppermute | solution.py:18
  5.6 1.7 %collective-permute-start = (bf16[64,1024]{1,0:T(8,128)(2,1)}, bf16[64,1024]{1,0:T(8,128)(2,1)S(1)}, u32[]{:S(2)}, u32[]{:S(2)}) collective-permute-start(bf16[64,1024]{1,0:T(8,128)(2,1)} %param.5), channel_id=1, source_target_pairs={{0,2},{1,3},{2,0},{3,1},{4,6},{5,7},{6,4},{7,5},{8,10},{9,11},{10,... | collective-permute-start | bytes 393224 | tf_op jit(solution)/shard_map/ppermute | solution.py:18
  10.7 3.6 %collective-permute-done.3 = bf16[128,128]{1,0:T(8,128)(2,1)S(1)} collective-permute-done((bf16[128,128]{1,0:T(8,128)(2,1)S(1)}, bf16[128,128]{1,0:T(8,128)(2,1)S(1)}, u32[]{:S(2)}, u32[]{:S(2)}) %collective-permute-start.3) | collective-permute-done | bytes 32800 | tf_op jit(solution)/shard_map/ppermute | solution.py:18
  15.2 3.6 %collective-permute-done.4 = bf16[256,128]{1,0:T(8,128)(2,1)S(1)} collective-permute-done((bf16[256,128]{1,0:T(8,128)(2,1)S(1)}, bf16[256,128]{1,0:T(8,128)(2,1)S(1)}, u32[]{:S(2)}, u32[]{:S(2)}) %collective-permute-start.4) | collective-permute-done | bytes 65568 | tf_op jit(solution)/shard_map/ppermute | solution.py:18
  18.8 2.2 %collective-permute-start.5 = (bf16[512,128]{1,0:T(8,128)(2,1)S(1)}, bf16[512,128]{1,0:T(8,128)(2,1)S(1)}, u32[]{:S(2)}, u32[]{:S(2)}) collective-permute-start(bf16[512,128]{1,0:T(8,128)(2,1)S(1)} %pad_maximum_fusion.4), channel_id=1, source_target_pairs={{0,8},{1,9},{2,10},{3,11},{4,12},{5,13},{6,14},{7,15},{8,0},{9,1},... | collective-permute-start | bytes 393224 | tf_op jit(solution)/shard_map/ppermute | solution.py:18
  21.1 1.6 %pad_maximum_fusion = bf16[128,1024]{1,0:T(8,128)(2,1)} fusion(bf16[64,1024]{1,0:T(8,128)(2,1)S(1)} %collective-permute-done, bf16[64,1024]{1,0:T(8,128)(2,1)} %param.5), kind=kLoop, calls=%fused_computation.108 | loop fusion | flops 524288 | bytes 524288 | tf_op jit(solution)/shard_map/concatenate | solution.py:44
  23.2 1.6 %collective-permute-start.15 = (bf16[64,1024]{1,0:T(8,128)(2,1)S(1)}, bf16[64,1024]{1,0:T(8,128)(2,1)S(1)}, u32[]{:S(2)}, u32[]{:S(2)}) collective-permute-start(bf16[64,1024]{1,0:T(8,128)(2,1)S(1)} %collective-permute-done.14), channel_id=1, source_target_pairs={{0,2},{1,3},{2,0},{3,1},{4,6},{5,7},{6,4},{7,5},{8,10},{9,11},{10,... | collective-permute-start | bytes 393224 | tf_op jit(solution)/shard_map/ppermute | solution.py:18
  29.2 2.6 %collective-permute-done.15 = bf16[64,1024]{1,0:T(8,128)(2,1)S(1)} collective-permute-done((bf16[64,1024]{1,0:T(8,128)(2,1)S(1)}, bf16[64,1024]{1,0:T(8,128)(2,1)S(1)}, u32[]{:S(2)}, u32[]{:S(2)}) %collective-permute-start.15) | collective-permute-done | bytes 131104 | tf_op jit(solution)/shard_map/ppermute | solution.py:18
  31.9 2.3 %collective-permute-done.21 = bf16[64,1024]{1,0:T(8,128)(2,1)S(1)} collective-permute-done((bf16[64,1024]{1,0:T(8,128)(2,1)S(1)}, bf16[64,1024]{1,0:T(8,128)(2,1)S(1)}, u32[]{:S(2)}, u32[]{:S(2)}) %collective-permute-start.21) | collective-permute-done | bytes 131104 | tf_op jit(solution)/shard_map/ppermute | solution.py:18
  35.4 3.4 %fusion.14 = f32[256,2048]{1,0:T(8,128)S(1)} fusion(bf16[256,1024]{1,0:T(8,128)(2,1)S(1)} %constant_dynamic-update-slice_fusion, bf16[2,1024,2048]{2,1,0:T(8,128)(2,1)} %param.8), kind=kOutput, calls=%fused_computation.14 | convolution fusion | flops 1073741824 | bytes 6815744 | tf_op jit(solution)/shard_map/dot_general | solution.py:59
  38.8 3.6 %fusion.6 = f32[256,2048]{1,0:T(8,128)S(1)} fusion(bf16[256,1024]{1,0:T(8,128)(2,1)S(1)} %constant_dynamic-update-slice_fusion, bf16[2,1024,2048]{2,1,0:T(8,128)(2,1)} %param.8), kind=kOutput, calls=%fused_computation.6 | convolution fusion | flops 1073741824 | bytes 6815744 | tf_op jit(solution)/shard_map/dot_general | solution.py:59
  44.6 1.3 %fusion.56 = f32[256,1024]{1,0:T(8,128)S(1)} fusion(bf16[2048,1024]{1,0:T(8,128)(2,1)S(1)} %bitcast.94, bf16[256,1024]{1,0:T(8,128)(2,1)S(1)} %fusion.53, bf16[256,1024]{1,0:T(8,128)(2,1)S(1)} %fusion.55), kind=kOutput, calls=%fused_computation.68 | convolution fusion | flops 1075838976 | bytes 6291456 | tf_op jit(solution)/shard_map/dot_general | solution.py:62
  47.8 1.3 %fusion.12 = f32[256,2048]{1,0:T(8,128)S(1)} fusion(bf16[256,1024]{1,0:T(8,128)(2,1)S(1)} %constant_dynamic-update-slice_fusion.8, bf16[2,1024,2048]{2,1,0:T(8,128)(2,1)S(1)} %bitcast.93), kind=kOutput, calls=%fused_computation.12 | convolution fusion | flops 1073741824 | bytes 6815744 | tf_op jit(solution)/shard_map/dot_general | solution.py:59
  55.5 1.3 %fusion.60 = f32[256,1024]{1,0:T(8,128)S(1)} fusion(bf16[2048,1024]{1,0:T(8,128)(2,1)S(1)} %bitcast.95, bf16[256,1024]{1,0:T(8,128)(2,1)S(1)} %fusion.49, bf16[256,1024]{1,0:T(8,128)(2,1)S(1)} %fusion.51), kind=kOutput, calls=%fused_computation.72 | convolution fusion | flops 1075838976 | bytes 6291456 | tf_op jit(solution)/shard_map/dot_general | solution.py:62
  57.8 1.3 %fusion.64 = f32[256,1024]{1,0:T(8,128)S(1)} fusion(bf16[2048,1024]{1,0:T(8,128)(2,1)S(1)} %bitcast.96, bf16[256,1024]{1,0:T(8,128)(2,1)S(1)} %fusion.45, bf16[256,1024]{1,0:T(8,128)(2,1)S(1)} %fusion.47), kind=kOutput, calls=%fused_computation.76 | convolution fusion | flops 1075838976 | bytes 6291456 | tf_op jit(solution)/shard_map/dot_general | solution.py:62
  60.7 1.3 %fusion.68 = f32[256,1024]{1,0:T(8,128)S(1)} fusion(bf16[2048,1024]{1,0:T(8,128)(2,1)S(1)} %bitcast.97, bf16[256,1024]{1,0:T(8,128)(2,1)S(1)} %fusion.41, bf16[256,1024]{1,0:T(8,128)(2,1)S(1)} %fusion.43), kind=kOutput, calls=%fused_computation.80 | convolution fusion | flops 1075838976 | bytes 6291456 | tf_op jit(solution)/shard_map/dot_general | solution.py:62
  62.9 1.6 %collective-permute-start.12 = (bf16[64,1024]{1,0:T(8,128)(2,1)S(1)}, bf16[64,1024]{1,0:T(8,128)(2,1)S(1)}, u32[]{:S(2)}, u32[]{:S(2)}) collective-permute-start(bf16[64,1024]{1,0:T(8,128)(2,1)S(1)} %slice.469), channel_id=1, source_target_pairs={{0,2},{1,3},{2,0},{3,1},{4,6},{5,7},{6,4},{7,5},{8,10},{9,11},{10,... | collective-permute-start | bytes 393224 | tf_op jit(solution)/shard_map/ppermute | solution.py:18
  65.2 1.6 %collective-permute-start.24 = (bf16[64,1024]{1,0:T(8,128)(2,1)S(1)}, bf16[64,1024]{1,0:T(8,128)(2,1)S(1)}, u32[]{:S(2)}, u32[]{:S(2)}) collective-permute-start(bf16[64,1024]{1,0:T(8,128)(2,1)S(1)} %slice.467), channel_id=1, source_target_pairs={{0,2},{1,3},{2,0},{3,1},{4,6},{5,7},{6,4},{7,5},{8,10},{9,11},{10,... | collective-permute-start | bytes 393224 | tf_op jit(solution)/shard_map/ppermute | solution.py:18
  66.8 4.5 %collective-permute-done.12 = bf16[64,1024]{1,0:T(8,128)(2,1)S(1)} collective-permute-done((bf16[64,1024]{1,0:T(8,128)(2,1)S(1)}, bf16[64,1024]{1,0:T(8,128)(2,1)S(1)}, u32[]{:S(2)}, u32[]{:S(2)}) %collective-permute-start.12) | collective-permute-done | bytes 131104 | tf_op jit(solution)/shard_map/ppermute | solution.py:18
  71.4 2.1 %collective-permute-start.13 = (bf16[64,1024]{1,0:T(8,128)(2,1)S(1)}, bf16[64,1024]{1,0:T(8,128)(2,1)S(1)}, u32[]{:S(2)}, u32[]{:S(2)}) collective-permute-start(bf16[64,1024]{1,0:T(8,128)(2,1)S(1)} %fusion.74), channel_id=1, source_target_pairs={{0,4},{1,5},{2,6},{3,7},{4,0},{5,1},{6,2},{7,3},{8,12},{9,13},{10,... | collective-permute-start | bytes 393224 | tf_op jit(solution)/shard_map/ppermute | solution.py:18
  75.1 1.5 %collective-permute-done.24 = bf16[64,1024]{1,0:T(8,128)(2,1)S(1)} collective-permute-done((bf16[64,1024]{1,0:T(8,128)(2,1)S(1)}, bf16[64,1024]{1,0:T(8,128)(2,1)S(1)}, u32[]{:S(2)}, u32[]{:S(2)}) %collective-permute-start.24) | collective-permute-done | bytes 131104 | tf_op jit(solution)/shard_map/ppermute | solution.py:18
  76.6 2.2 %collective-permute-start.25 = (bf16[64,1024]{1,0:T(8,128)(2,1)S(1)}, bf16[64,1024]{1,0:T(8,128)(2,1)S(1)}, u32[]{:S(2)}, u32[]{:S(2)}) collective-permute-start(bf16[64,1024]{1,0:T(8,128)(2,1)S(1)} %fusion.72), channel_id=1, source_target_pairs={{0,12},{1,13},{2,14},{3,15},{4,8},{5,9},{6,10},{7,11},{8,4},{9,5},... | collective-permute-start | bytes 393224 | tf_op jit(solution)/shard_map/ppermute | solution.py:18
  78.8 7.9 %collective-permute-done.19 = bf16[64,1024]{1,0:T(8,128)(2,1)S(1)} collective-permute-done((bf16[64,1024]{1,0:T(8,128)(2,1)S(1)}, bf16[64,1024]{1,0:T(8,128)(2,1)S(1)}, u32[]{:S(2)}, u32[]{:S(2)}) %collective-permute-start.19) | collective-permute-done | bytes 131104 | tf_op jit(solution)/shard_map/ppermute | solution.py:18
  (125 shorter events, 27.1 us)
Async XLA Ops:
  0.0 22.7 %collective-permute-start.8 = (bf16[64,1024]{1,0:T(8,128)(2,1)}, bf16[64,1024]{1,0:T(8,128)(2,1)S(1)}, u32[]{:S(2)}, u32[]{:S(2)}) collective-permute-start(bf16[64,1024]{1,0:T(8,128)(2,1)} %param.5), channel_id=1, source_target_pairs={{0,4},{1,5},{2,6},{3,7},{4,0},{5,1},{6,2},{7,3},{8,12},{9,13},{10,... | collective-permute-start | bytes 393224 | tf_op jit(solution)/shard_map/ppermute | solution.py:18
  3.0 20.2 %collective-permute-start.14 = (bf16[64,1024]{1,0:T(8,128)(2,1)}, bf16[64,1024]{1,0:T(8,128)(2,1)S(1)}, u32[]{:S(2)}, u32[]{:S(2)}) collective-permute-start(bf16[64,1024]{1,0:T(8,128)(2,1)} %param.5), channel_id=1, source_target_pairs={{0,8},{1,9},{2,10},{3,11},{4,12},{5,13},{6,14},{7,15},{8,0},{9,1},... | collective-permute-start | bytes 393224 | tf_op jit(solution)/shard_map/ppermute | solution.py:18
  5.6 19.2 %collective-permute-start.20 = (bf16[64,1024]{1,0:T(8,128)(2,1)}, bf16[64,1024]{1,0:T(8,128)(2,1)S(1)}, u32[]{:S(2)}, u32[]{:S(2)}) collective-permute-start(bf16[64,1024]{1,0:T(8,128)(2,1)} %param.5), channel_id=1, source_target_pairs={{0,12},{1,13},{2,14},{3,15},{4,8},{5,9},{6,10},{7,11},{8,4},{9,5},... | collective-permute-start | bytes 393224 | tf_op jit(solution)/shard_map/ppermute | solution.py:18
  5.6 15.5 %collective-permute-start = (bf16[64,1024]{1,0:T(8,128)(2,1)}, bf16[64,1024]{1,0:T(8,128)(2,1)S(1)}, u32[]{:S(2)}, u32[]{:S(2)}) collective-permute-start(bf16[64,1024]{1,0:T(8,128)(2,1)} %param.5), channel_id=1, source_target_pairs={{0,2},{1,3},{2,0},{3,1},{4,6},{5,7},{6,4},{7,5},{8,10},{9,11},{10,... | collective-permute-start | bytes 393224 | tf_op jit(solution)/shard_map/ppermute | solution.py:18
  10.4 4.0 %collective-permute-start.3 = (bf16[128,128]{1,0:T(8,128)(2,1)S(1)}, bf16[128,128]{1,0:T(8,128)(2,1)S(1)}, u32[]{:S(2)}, u32[]{:S(2)}) collective-permute-start(bf16[128,128]{1,0:T(8,128)(2,1)S(1)} %pad_maximum_fusion.6), channel_id=1, source_target_pairs={{0,2},{1,3},{2,0},{3,1},{4,6},{5,7},{6,4},{7,5},{8,10},{9,11},{10,... | collective-permute-start | bytes 98312 | tf_op jit(solution)/shard_map/ppermute | solution.py:18
  14.4 4.3 %collective-permute-start.4 = (bf16[256,128]{1,0:T(8,128)(2,1)S(1)}, bf16[256,128]{1,0:T(8,128)(2,1)S(1)}, u32[]{:S(2)}, u32[]{:S(2)}) collective-permute-start(bf16[256,128]{1,0:T(8,128)(2,1)S(1)} %pad_maximum_fusion.5), channel_id=1, source_target_pairs={{0,4},{1,5},{2,6},{3,7},{4,0},{5,1},{6,2},{7,3},{8,12},{9,13},{10,... | collective-permute-start | bytes 196616 | tf_op jit(solution)/shard_map/ppermute | solution.py:18
  18.8 7.6 %collective-permute-start.5 = (bf16[512,128]{1,0:T(8,128)(2,1)S(1)}, bf16[512,128]{1,0:T(8,128)(2,1)S(1)}, u32[]{:S(2)}, u32[]{:S(2)}) collective-permute-start(bf16[512,128]{1,0:T(8,128)(2,1)S(1)} %pad_maximum_fusion.4), channel_id=1, source_target_pairs={{0,8},{1,9},{2,10},{3,11},{4,12},{5,13},{6,14},{7,15},{8,0},{9,1},... | collective-permute-start | bytes 393224 | tf_op jit(solution)/shard_map/ppermute | solution.py:18
  22.7 11.7 %collective-permute-start.1 = (bf16[128,1024]{1,0:T(8,128)(2,1)}, bf16[128,1024]{1,0:T(8,128)(2,1)}, u32[]{:S(2)}, u32[]{:S(2)}) collective-permute-start(bf16[128,1024]{1,0:T(8,128)(2,1)} %pad_maximum_fusion), channel_id=1, source_target_pairs={{0,1},{1,0},{2,3},{3,2},{4,5},{5,4},{6,7},{7,6},{8,9},{9,8},{10,11... | collective-permute-start | bytes 786440 | tf_op jit(solution)/shard_map/ppermute | solution.py:18
  22.7 6.4 %collective-permute-start.9 = (bf16[64,1024]{1,0:T(8,128)(2,1)S(1)}, bf16[64,1024]{1,0:T(8,128)(2,1)S(1)}, u32[]{:S(2)}, u32[]{:S(2)}) collective-permute-start(bf16[64,1024]{1,0:T(8,128)(2,1)S(1)} %collective-permute-done.8), channel_id=1, source_target_pairs={{0,2},{1,3},{2,0},{3,1},{4,6},{5,7},{6,4},{7,5},{8,10},{9,11},{10,... | collective-permute-start | bytes 393224 | tf_op jit(solution)/shard_map/ppermute | solution.py:18
  23.2 8.6 %collective-permute-start.15 = (bf16[64,1024]{1,0:T(8,128)(2,1)S(1)}, bf16[64,1024]{1,0:T(8,128)(2,1)S(1)}, u32[]{:S(2)}, u32[]{:S(2)}) collective-permute-start(bf16[64,1024]{1,0:T(8,128)(2,1)S(1)} %collective-permute-done.14), channel_id=1, source_target_pairs={{0,2},{1,3},{2,0},{3,1},{4,6},{5,7},{6,4},{7,5},{8,10},{9,11},{10,... | collective-permute-start | bytes 393224 | tf_op jit(solution)/shard_map/ppermute | solution.py:18
  24.8 9.4 %collective-permute-start.21 = (bf16[64,1024]{1,0:T(8,128)(2,1)S(1)}, bf16[64,1024]{1,0:T(8,128)(2,1)S(1)}, u32[]{:S(2)}, u32[]{:S(2)}) collective-permute-start(bf16[64,1024]{1,0:T(8,128)(2,1)S(1)} %collective-permute-done.20), channel_id=1, source_target_pairs={{0,2},{1,3},{2,0},{3,1},{4,6},{5,7},{6,4},{7,5},{8,10},{9,11},{10,... | collective-permute-start | bytes 393224 | tf_op jit(solution)/shard_map/ppermute | solution.py:18
  29.1 17.4 %collective-permute-start.10 = (bf16[128,1024]{1,0:T(8,128)(2,1)S(1)}, bf16[128,1024]{1,0:T(8,128)(2,1)S(1)}, u32[]{:S(2)}, u32[]{:S(2)}) collective-permute-start(bf16[128,1024]{1,0:T(8,128)(2,1)S(1)} %pad_maximum_fusion.1), channel_id=1, source_target_pairs={{0,1},{1,0},{2,3},{3,2},{4,5},{5,4},{6,7},{7,6},{8,9},{9,8},{10,11... | collective-permute-start | bytes 786440 | tf_op jit(solution)/shard_map/ppermute | solution.py:18
  31.8 17.3 %collective-permute-start.16 = (bf16[128,1024]{1,0:T(8,128)(2,1)S(1)}, bf16[128,1024]{1,0:T(8,128)(2,1)S(1)}, u32[]{:S(2)}, u32[]{:S(2)}) collective-permute-start(bf16[128,1024]{1,0:T(8,128)(2,1)S(1)} %pad_maximum_fusion.2), channel_id=1, source_target_pairs={{0,1},{1,0},{2,3},{3,2},{4,5},{5,4},{6,7},{7,6},{8,9},{9,8},{10,11... | collective-permute-start | bytes 786440 | tf_op jit(solution)/shard_map/ppermute | solution.py:18
  34.3 17.5 %collective-permute-start.22 = (bf16[128,1024]{1,0:T(8,128)(2,1)S(1)}, bf16[128,1024]{1,0:T(8,128)(2,1)S(1)}, u32[]{:S(2)}, u32[]{:S(2)}) collective-permute-start(bf16[128,1024]{1,0:T(8,128)(2,1)S(1)} %pad_maximum_fusion.3), channel_id=1, source_target_pairs={{0,1},{1,0},{2,3},{3,2},{4,5},{5,4},{6,7},{7,6},{8,9},{9,8},{10,11... | collective-permute-start | bytes 786440 | tf_op jit(solution)/shard_map/ppermute | solution.py:18
  46.0 16.1 %collective-permute-start.6 = (bf16[128,1024]{1,0:T(8,128)(2,1)S(1)}, bf16[128,1024]{1,0:T(8,128)(2,1)S(1)}, u32[]{:S(2)}, u32[]{:S(2)}) collective-permute-start(bf16[128,1024]{1,0:T(8,128)(2,1)S(1)} %slice.466), channel_id=1, source_target_pairs={{0,1},{1,0},{2,3},{3,2},{4,5},{5,4},{6,7},{7,6},{8,9},{9,8},{10,11... | collective-permute-start | bytes 786440 | tf_op jit(solution)/shard_map/ppermute | solution.py:18
  56.8 6.0 %collective-permute-start.11 = (bf16[128,1024]{1,0:T(8,128)(2,1)S(1)}, bf16[128,1024]{1,0:T(8,128)(2,1)S(1)}, u32[]{:S(2)}, u32[]{:S(2)}) collective-permute-start(bf16[128,1024]{1,0:T(8,128)(2,1)S(1)} %slice.465), channel_id=1, source_target_pairs={{0,1},{1,0},{2,3},{3,2},{4,5},{5,4},{6,7},{7,6},{8,9},{9,8},{10,11... | collective-permute-start | bytes 786440 | tf_op jit(solution)/shard_map/ppermute | solution.py:18
  59.2 5.3 %collective-permute-start.17 = (bf16[128,1024]{1,0:T(8,128)(2,1)S(1)}, bf16[128,1024]{1,0:T(8,128)(2,1)S(1)}, u32[]{:S(2)}, u32[]{:S(2)}) collective-permute-start(bf16[128,1024]{1,0:T(8,128)(2,1)S(1)} %slice.464), channel_id=1, source_target_pairs={{0,1},{1,0},{2,3},{3,2},{4,5},{5,4},{6,7},{7,6},{8,9},{9,8},{10,11... | collective-permute-start | bytes 786440 | tf_op jit(solution)/shard_map/ppermute | solution.py:18
  62.2 16.6 %collective-permute-start.7 = (bf16[64,1024]{1,0:T(8,128)(2,1)S(1)}, bf16[64,1024]{1,0:T(8,128)(2,1)S(1)}, u32[]{:S(2)}, u32[]{:S(2)}) collective-permute-start(bf16[64,1024]{1,0:T(8,128)(2,1)S(1)} %slice.470), channel_id=1, source_target_pairs={{0,2},{1,3},{2,0},{3,1},{4,6},{5,7},{6,4},{7,5},{8,10},{9,11},{10,... | collective-permute-start | bytes 393224 | tf_op jit(solution)/shard_map/ppermute | solution.py:18
  62.9 8.5 %collective-permute-start.12 = (bf16[64,1024]{1,0:T(8,128)(2,1)S(1)}, bf16[64,1024]{1,0:T(8,128)(2,1)S(1)}, u32[]{:S(2)}, u32[]{:S(2)}) collective-permute-start(bf16[64,1024]{1,0:T(8,128)(2,1)S(1)} %slice.469), channel_id=1, source_target_pairs={{0,2},{1,3},{2,0},{3,1},{4,6},{5,7},{6,4},{7,5},{8,10},{9,11},{10,... | collective-permute-start | bytes 393224 | tf_op jit(solution)/shard_map/ppermute | solution.py:18
  64.6 9.6 %collective-permute-start.18 = (bf16[64,1024]{1,0:T(8,128)(2,1)S(1)}, bf16[64,1024]{1,0:T(8,128)(2,1)S(1)}, u32[]{:S(2)}, u32[]{:S(2)}) collective-permute-start(bf16[64,1024]{1,0:T(8,128)(2,1)S(1)} %slice.468), channel_id=1, source_target_pairs={{0,2},{1,3},{2,0},{3,1},{4,6},{5,7},{6,4},{7,5},{8,10},{9,11},{10,... | collective-permute-start | bytes 393224 | tf_op jit(solution)/shard_map/ppermute | solution.py:18
  65.2 11.3 %collective-permute-start.24 = (bf16[64,1024]{1,0:T(8,128)(2,1)S(1)}, bf16[64,1024]{1,0:T(8,128)(2,1)S(1)}, u32[]{:S(2)}, u32[]{:S(2)}) collective-permute-start(bf16[64,1024]{1,0:T(8,128)(2,1)S(1)} %slice.467), channel_id=1, source_target_pairs={{0,2},{1,3},{2,0},{3,1},{4,6},{5,7},{6,4},{7,5},{8,10},{9,11},{10,... | collective-permute-start | bytes 393224 | tf_op jit(solution)/shard_map/ppermute | solution.py:18
  71.4 7.4 %collective-permute-start.13 = (bf16[64,1024]{1,0:T(8,128)(2,1)S(1)}, bf16[64,1024]{1,0:T(8,128)(2,1)S(1)}, u32[]{:S(2)}, u32[]{:S(2)}) collective-permute-start(bf16[64,1024]{1,0:T(8,128)(2,1)S(1)} %fusion.74), channel_id=1, source_target_pairs={{0,4},{1,5},{2,6},{3,7},{4,0},{5,1},{6,2},{7,3},{8,12},{9,13},{10,... | collective-permute-start | bytes 393224 | tf_op jit(solution)/shard_map/ppermute | solution.py:18
  74.2 12.4 %collective-permute-start.19 = (bf16[64,1024]{1,0:T(8,128)(2,1)S(1)}, bf16[64,1024]{1,0:T(8,128)(2,1)S(1)}, u32[]{:S(2)}, u32[]{:S(2)}) collective-permute-start(bf16[64,1024]{1,0:T(8,128)(2,1)S(1)} %fusion.73), channel_id=1, source_target_pairs={{0,8},{1,9},{2,10},{3,11},{4,12},{5,13},{6,14},{7,15},{8,0},{9,1},... | collective-permute-start | bytes 393224 | tf_op jit(solution)/shard_map/ppermute | solution.py:18
  76.6 10.0 %collective-permute-start.25 = (bf16[64,1024]{1,0:T(8,128)(2,1)S(1)}, bf16[64,1024]{1,0:T(8,128)(2,1)S(1)}, u32[]{:S(2)}, u32[]{:S(2)}) collective-permute-start(bf16[64,1024]{1,0:T(8,128)(2,1)S(1)} %fusion.72), channel_id=1, source_target_pairs={{0,12},{1,13},{2,14},{3,15},{4,8},{5,9},{6,10},{7,11},{8,4},{9,5},... | collective-permute-start | bytes 393224 | tf_op jit(solution)/shard_map/ppermute | solution.py:18
  (5 other events, 17.8 us)

commit v3 on v1

v3 whole, which is shorter than its diff:
```python
import functools

import jax
import jax.numpy as jnp
from jax import lax
from jax.experimental import pallas as pl
from jax.experimental.pallas import tpu as pltpu
from jax.sharding import PartitionSpec as P

GROUP = 16
TAIL = 128
SCALE = 2.0**40


def pack_kernel(ids_ref, row_ref, out_ref):
    rows, top = row_ref.shape[0], ids_ref.shape[0]
    lat = row_ref.shape[1]
    out_ref[:, :lat] = row_ref[...]
    ids = ids_ref[...].astype(jnp.float32)
    wide = jnp.concatenate([ids, jnp.full((top, TAIL - rows), -1.0, jnp.float32)], axis=1)
    wide = jnp.concatenate([wide, jnp.full((TAIL - top, TAIL), -1.0, jnp.float32)], axis=0)
    out_ref[:, lat:] = wide.T[:rows].astype(jnp.bfloat16)


STEP = 256


def weight_copies(up_hbm, down_hbm, up_ref, down_ref, sems):
    local, _, eff2 = up_ref.shape
    eff, lat = eff2 // 2, down_ref.shape[1]
    pieces = []
    for e in range(local):
        for c in range(0, eff, STEP):
            for at in (c, eff + c):
                pieces.append((up_hbm.at[e, :, pl.ds(at, STEP)], up_ref.at[e, :, pl.ds(at, STEP)]))
    for c in range(0, lat, STEP):
        pieces.append((down_hbm.at[:, pl.ds(c, STEP)], down_ref.at[:, pl.ds(c, STEP)]))
    return [pltpu.make_async_copy(src, dst, sems.at[i]) for i, (src, dst) in enumerate(pieces)]


def expert_body(first_ref, pair_ref, other_ref, router_ref, up_ref, down_ref, keep_ref, send_ref, inner_ref, copies):
    half, wide = pair_ref.shape
    lat = wide - TAIL
    local, _, eff2 = up_ref.shape
    eff = eff2 // 2
    copies = iter(copies)

    def ready(number):
        for _, copy in zip(range(number), copies):
            copy.wait()

    x = jnp.concatenate([pair_ref[:, :lat], other_ref[:, :lat]], axis=0)
    tail = jnp.concatenate([pair_ref[:, lat:], other_ref[:, lat:]], axis=0).astype(jnp.float32)
    logits = lax.dot_general(
        x, router_ref[...], (((1,), (1,)), ((), ())), preferred_element_type=jnp.float32
    )
    sums = jnp.zeros((2 * half, 1), jnp.float32)
    for e in range(local):
        label = (first_ref[0] + e).astype(jnp.float32)
        mask = jnp.max(jnp.where(tail == label, 1.0, 0.0), axis=1, keepdims=True)
        score = jax.nn.sigmoid(logits[:, e : e + 1]) * (mask * SCALE)
        sums = sums + score
        for c in range(0, eff, STEP):
            ready(2)
            gate = jnp.dot(x, up_ref[e, :, c : c + STEP], preferred_element_type=jnp.float32)
            up = jnp.dot(x, up_ref[e, :, eff + c : eff + c + STEP], preferred_element_type=jnp.float32)
            inner_ref[:, e * eff + c : e * eff + c + STEP] = (
                gate / (1.0 + jnp.exp(-gate)) * up * score
            ).astype(jnp.bfloat16)
    inner = inner_ref[...]
    for c in range(0, lat, STEP):
        ready(1)
        part = jnp.dot(inner, down_ref[:, c : c + STEP], preferred_element_type=jnp.float32)
        keep_ref[:, c : c + STEP] = part[:half]
        send_ref[:, c : c + STEP] = part[half:].astype(jnp.bfloat16)
    lane = lax.broadcasted_iota(jnp.int32, (2 * half, TAIL), 1)
    sums = jnp.where(lane == 0, sums, 0.0)
    keep_ref[:, lat:] = sums[:half]
    send_ref[:, lat:] = sums[half:].astype(jnp.bfloat16)


def first_kernel(first_ref, pair_ref, other_ref, router_ref, up_hbm, down_hbm, keep_ref, send_ref, up_ref, down_ref, inner_ref, sems):
    copies = weight_copies(up_hbm, down_hbm, up_ref, down_ref, sems)
    for copy in copies:
        copy.start()
    expert_body(
        first_ref, pair_ref, other_ref, router_ref, up_ref, down_ref, keep_ref, send_ref, inner_ref, copies
    )


def next_kernel(first_ref, pair_ref, other_ref, router_ref, up_ref, down_ref, _, keep_ref, send_ref, inner_ref):
    expert_body(first_ref, pair_ref, other_ref, router_ref, up_ref, down_ref, keep_ref, send_ref, inner_ref, [])


def in_vmem(x):
    return pltpu.with_memory_space_constraint(x, pltpu.VMEM)


def in_hbm(x):
    return pltpu.with_memory_space_constraint(x, pltpu.HBM)


def on_device(latent_in, routes, router, gate_up, expert_down):
    n_dev = lax.axis_size("exp")
    local = gate_up.shape[0]
    eff = expert_down.shape[1]
    rows, lat = latent_in.shape
    wide = lat + TAIL
    me = lax.axis_index("exp")

    def swap(x, bits):
        return lax.ppermute(x, "exp", [(i, i ^ bits) for i in range(n_dev)])

    vmem = pl.BlockSpec(memory_space=pltpu.VMEM)
    packet = pl.pallas_call(
        pack_kernel,
        out_shape=jax.ShapeDtypeStruct((rows, wide), jnp.bfloat16),
        in_specs=[vmem, vmem],
        out_specs=vmem,
        name="pack",
    )(routes.T, latent_in)
    first = (me * local).astype(jnp.int32).reshape(1)
    columns = in_vmem(jnp.pad(router.T, ((0, 16 - local), (0, 0))))
    down = expert_down.reshape(local * eff, lat)

    batch = 4 * rows
    flops = 2 * batch * local * eff * lat * 3
    smem = pl.BlockSpec(memory_space=pltpu.SMEM)
    anywhere = pl.BlockSpec(memory_space=pl.ANY)
    results = [
        pltpu.VMEM((2 * rows, wide), jnp.float32),
        pltpu.VMEM((2 * rows, wide), jnp.bfloat16),
    ]
    inner = pltpu.VMEM((batch, local * eff), jnp.bfloat16)
    params = pltpu.CompilerParams(vmem_limit_bytes=16 * 1024 * 1024)
    cost = pl.CostEstimate(flops=flops, bytes_accessed=0, transcendentals=0)
    n_copies = local * 2 * eff // STEP + lat // STEP
    run_first = pl.pallas_call(
        first_kernel,
        out_shape=results + [pltpu.VMEM(gate_up.shape, gate_up.dtype), pltpu.VMEM(down.shape, down.dtype)],
        in_specs=[smem, vmem, vmem, vmem, anywhere, anywhere],
        out_specs=[vmem] * 4,
        scratch_shapes=[inner, pltpu.SemaphoreType.DMA((n_copies,))],
        compiler_params=params,
        cost_estimate=cost,
        name="experts_first",
    )
    run_next = pl.pallas_call(
        next_kernel,
        out_shape=results,
        in_specs=[smem] + [vmem] * 5 + [anywhere],
        out_specs=[vmem] * 2,
        scratch_shapes=[inner],
        compiler_params=params,
        cost_estimate=cost,
        name="experts_next",
    )

    def group_pass(mine):
        z1 = swap(mine, 4)
        z2 = swap(mine, 8)
        z3 = swap(z2, 4)
        total = None
        for k, one in enumerate((mine, z1, z2, z3)):
            pair = jnp.concatenate([one, swap(one, 2)], axis=0)
            other = swap(pair, 1)
            pair, other = in_vmem(pair), in_vmem(other)
            if k == 0:
                keep, send, up_v, down_v = run_first(first, pair, other, columns, in_hbm(gate_up), in_hbm(down))
            else:
                keep, send = run_next(first, pair, other, columns, in_vmem(up_v), in_vmem(down_v), in_vmem(last))
            last = send
            sums = keep + swap(send, 1).astype(jnp.float32)
            sums = sums[:rows] + swap(sums[rows:].astype(jnp.bfloat16), 2).astype(jnp.float32)
            if k > 0:
                sums = swap(sums.astype(jnp.bfloat16), 4 * k).astype(jnp.float32)
            total = sums if total is None else total + sums
        return total

    def finish(total):
        return (total[:, :lat] / total[:, lat : lat + 1]).astype(jnp.bfloat16)

    if n_dev == GROUP:
        return finish(group_pass(packet))

    def next_group(x):
        return lax.ppermute(x, "exp", [(i, (i + GROUP) % n_dev) for i in range(n_dev)])

    def step(carry, _):
        mine, total = carry
        total = total + group_pass(mine)
        return (next_group(mine), next_group(total)), None

    start = (packet, jnp.zeros((rows, wide), jnp.float32))
    (_, total), _ = lax.scan(step, start, None, length=n_dev // GROUP)
    return finish(total)


def solution(mesh):
    placed = (
        P(("grp", "exp"), None),
        P(("grp", "exp"), None),
        P(None, "exp"),
        P("exp", None, None),
        P("exp", None, None),
    )
    return jax.shard_map(
        on_device, mesh=mesh, in_specs=placed, out_specs=P(("grp", "exp"), None), check_vma=False
    )
```

time: 144 us -> 75.3 us (0.52)
  blocking collectives: 41.6 us -> 0 us
  waiting for transfers between devices: 66 us -> 30.1 us
  Pallas kernels: 0 us -> 20.8 us
  starting transfers between devices: 0.04 us -> 20.4 us
  matrix products: 19.8 us -> 0 us
  between operations: 13.5 us -> 0.18 us
    reduce_scatter x1 -> x0, waiting for transfers between devices: 60.5 us -> none  [on_device(): return lax.psum_scatter(sums, 'exp', scatter_dimension=0, tiled=True)]
    all_gather x2 -> x0, blocking collectives: 41.6 us -> none  [the longest x1 23.5 us: on_device(): chosen = lax.all_gather(routes, 'exp', axis=0, tiled=True)]
    ppermute x0 -> x22, waiting for transfers between devices: none -> 30.1 us  [swap(): return lax.ppermute(x, 'exp', [(i, i ^ bits) for i in range(n_dev)])]
    pallas_call x0 -> x5, Pallas kernels: none -> 20.8 us  [the longest x3 11.1 us: group_pass(): run_next(first, pair, other, columns, in_vmem(up_v), in_vmem(down_v), in_...]
    ppermute x0 -> x22, starting transfers between devices: none -> 20.4 us  [swap(): return lax.ppermute(x, 'exp', [(i, i ^ bits) for i in range(n_dev)])]
    dot_general x4 -> x0, matrix products: 19.8 us -> none  [the longest x2 11.6 us: part(): both = jnp.dot(tok, gate_up[e], preferred_element_type=jnp.float32)]
    all_gather x1 -> x0, waiting for transfers between devices: 4.78 us -> none  [on_device(): tokens = lax.all_gather(latent_in, 'exp', axis=0, tiled=True)]
    convert_element_type x1 -> x4, other arithmetic: 2.69 us -> 0.85 us  [the longest x1 0.76 us: finish(): return (total[:, :lat] / total[:, lat:lat + 1]).astype(jnp.bfloat16)]
  transfers between devices with their start and end apart: 2 -> 22, of which waited for: 2 -> 10; matrix products, arithmetic and copies ran while one was open for 0% -> 3% of each run, Pallas kernels for 0% -> 26%
where the time goes in v3:
time: 75.3 us; the launch traced here: 74.6 us
  waiting for transfers between devices  30.1 us (40%)
  Pallas kernels  20.8 us (28%)
  starting transfers between devices  20.4 us (27%)
  other arithmetic  2.07 us (3%)
  local copies, waits for them, and re-layouts  0.96 us (1%)
    ppermute x22, waiting for transfers between devices, swap(): return lax.ppermute(x, 'exp', [(i, i ^ bits) for i in range(n_dev)])  30.1 us
    ppermute x22, starting transfers between devices, swap(): return lax.ppermute(x, 'exp', [(i, i ^ bits) for i in range(n_dev)])  20.4 us
    pallas_call x3, Pallas kernels, group_pass(): run_next(first, pair, other, columns, in_vmem(up_v), in_vmem(down_v), in_...  11.1 us
    pallas_call x1, Pallas kernels, group_pass(): run_first(first, pair, other, columns, in_hbm(gate_up), in_hbm(down))  8.07 us
    pallas_call x1, Pallas kernels, on_device(): pl.pallas_call(pack_kernel, out_shape=jax.ShapeDtypeStruct((rows, wide),...  1.66 us
  transfers between devices with their start and end apart: 22, of which 10 were waited for; matrix products, arithmetic and copies ran while one was open for 3% of the time, Pallas kernels for 26%

profile of v3, /device:TPU:0, one launch (start us, length us, event | category | flops | bytes accessed | tf_op | source)
XLA Modules:
  0.0 74.6 jit_solution(1743762254723817690)
XLA Ops:
  0.0 1.7 %pack.1 = bf16[64,1152]{1,0:T(8,128)(2,1)} custom-call(s32[8,64]{1,0:T(8,128)} %bitcast.5, bf16[64,1024]{1,0:T(8,128)(2,1)} %row_ref.1), custom_call_target="tpu_custom_call" | custom-call | tf_op jit(solution)/shard_map/pack/pallas_call | solution.py:115
  1.7 3.0 %collective-permute-start = (bf16[64,1152]{1,0:T(8,128)(2,1)}, bf16[64,1152]{1,0:T(8,128)(2,1)S(1)}, u32[]{:S(2)}, u32[]{:S(2)}) collective-permute-start(bf16[64,1152]{1,0:T(8,128)(2,1)} %pack.1), channel_id=1, source_target_pairs={{0,2},{1,3},{2,0},{3,1},{4,6},{5,7},{6,4},{7,5},{8,10},{9,11},{10,... | collective-permute-start | bytes 442376 | tf_op jit(solution)/shard_map/ppermute | solution.py:112
  4.6 1.6 %collective-permute-start.4 = (bf16[64,1152]{1,0:T(8,128)(2,1)}, bf16[64,1152]{1,0:T(8,128)(2,1)S(1)}, u32[]{:S(2)}, u32[]{:S(2)}) collective-permute-start(bf16[64,1152]{1,0:T(8,128)(2,1)} %pack.1), channel_id=1, source_target_pairs={{0,4},{1,5},{2,6},{3,7},{4,0},{5,1},{6,2},{7,3},{8,12},{9,13},{10,... | collective-permute-start | bytes 442376 | tf_op jit(solution)/shard_map/ppermute | solution.py:112
  6.2 2.6 %collective-permute-start.10 = (bf16[64,1152]{1,0:T(8,128)(2,1)}, bf16[64,1152]{1,0:T(8,128)(2,1)S(1)}, u32[]{:S(2)}, u32[]{:S(2)}) collective-permute-start(bf16[64,1152]{1,0:T(8,128)(2,1)} %pack.1), channel_id=1, source_target_pairs={{0,8},{1,9},{2,10},{3,11},{4,12},{5,13},{6,14},{7,15},{8,0},{9,1},... | collective-permute-start | bytes 442376 | tf_op jit(solution)/shard_map/ppermute | solution.py:112
  9.5 0.9 %pad_maximum_fusion.pair_ref = bf16[128,1152]{1,0:T(8,128)(2,1)S(1)} fusion(bf16[64,1152]{1,0:T(8,128)(2,1)S(1)} %collective-permute-done, bf16[64,1152]{1,0:T(8,128)(2,1)} %pack.1), kind=kLoop, calls=%fused_computation.18 | loop fusion | flops 589824 | bytes 589824 | tf_op jit(solution)/shard_map/concatenate | solution.py:165
  10.5 2.0 %collective-permute-done.4 = bf16[64,1152]{1,0:T(8,128)(2,1)S(1)} collective-permute-done((bf16[64,1152]{1,0:T(8,128)(2,1)}, bf16[64,1152]{1,0:T(8,128)(2,1)S(1)}, u32[]{:S(2)}, u32[]{:S(2)}) %collective-permute-start.4) | collective-permute-done | bytes 147488 | tf_op jit(solution)/shard_map/ppermute | solution.py:112
  12.8 2.8 %collective-permute-done.10 = bf16[64,1152]{1,0:T(8,128)(2,1)S(1)} collective-permute-done((bf16[64,1152]{1,0:T(8,128)(2,1)}, bf16[64,1152]{1,0:T(8,128)(2,1)S(1)}, u32[]{:S(2)}, u32[]{:S(2)}) %collective-permute-start.10) | collective-permute-done | bytes 147488 | tf_op jit(solution)/shard_map/ppermute | solution.py:112
  16.5 1.8 %collective-permute-done.5 = bf16[64,1152]{1,0:T(8,128)(2,1)S(1)} collective-permute-done((bf16[64,1152]{1,0:T(8,128)(2,1)S(1)}, bf16[64,1152]{1,0:T(8,128)(2,1)S(1)}, u32[]{:S(2)}, u32[]{:S(2)}) %collective-permute-start.5) | collective-permute-done | bytes 147488 | tf_op jit(solution)/shard_map/ppermute | solution.py:112
  18.4 2.3 %collective-permute-done.11 = bf16[64,1152]{1,0:T(8,128)(2,1)S(1)} collective-permute-done((bf16[64,1152]{1,0:T(8,128)(2,1)S(1)}, bf16[64,1152]{1,0:T(8,128)(2,1)S(1)}, u32[]{:S(2)}, u32[]{:S(2)}) %collective-permute-start.11) | collective-permute-done | bytes 147488 | tf_op jit(solution)/shard_map/ppermute | solution.py:112
  21.2 1.5 %collective-permute-start.17 = (bf16[64,1152]{1,0:T(8,128)(2,1)S(1)}, bf16[64,1152]{1,0:T(8,128)(2,1)S(1)}, u32[]{:S(2)}, u32[]{:S(2)}) collective-permute-start(bf16[64,1152]{1,0:T(8,128)(2,1)S(1)} %collective-permute-done.16), channel_id=1, source_target_pairs={{0,2},{1,3},{2,0},{3,1},{4,6},{5,7},{6,4},{7,5},{8,10},{9,11},{10,... | collective-permute-start | bytes 442376 | tf_op jit(solution)/shard_map/ppermute | solution.py:112
  22.7 4.3 %collective-permute-done.17 = bf16[64,1152]{1,0:T(8,128)(2,1)S(1)} collective-permute-done((bf16[64,1152]{1,0:T(8,128)(2,1)S(1)}, bf16[64,1152]{1,0:T(8,128)(2,1)S(1)}, u32[]{:S(2)}, u32[]{:S(2)}) %collective-permute-start.17) | collective-permute-done | bytes 147488 | tf_op jit(solution)/shard_map/ppermute | solution.py:112
  27.2 8.1 %experts_first.1 = (f32[128,1152]{1,0:T(8,128)S(1)}, bf16[128,1152]{1,0:T(8,128)(2,1)S(1)}, bf16[2,1024,2048]{2,1,0:T(8,128)(2,1)S(1)}, bf16[2048,1024]{1,0:T(8,128)(2,1)S(1)}) custom-call(s32[1]{0:T(128)} %bitcast.first_ref, bf16[128,1152]{1,0:T(8,128)(2,1)S(1)} %pad_maximum_fusion.pair_ref, bf16[128,1152]{1,0:T(8,128)(2,1)S(1)} %collective-permute-done.1.other_ref, ...), custom_call_target="tpu_custom_call" | custom-call | flops 3221225472 | tf_op jit(solution)/shard_map/experts_first/pallas_call | solution.py:169
  35.8 3.6 %experts_next.3 = (f32[128,1152]{1,0:T(8,128)S(1)}, bf16[128,1152]{1,0:T(8,128)(2,1)S(1)}) custom-call(s32[1]{0:T(128)} %bitcast.first_ref, bf16[128,1152]{1,0:T(8,128)(2,1)S(1)} %constant_dynamic-update-slice_fusion.pair_ref, bf16[128,1152]{1,0:T(8,128)(2,1)S(1)} %collective-permute-done.6.other_ref, bf16[16,1024]{1,0:T(8,128)(2,1)S(1)} %pad.4.router_ref, ...), custom_call_target="tpu_custom_call" | custom-call | flops 3221225472 | tf_op jit(solution)/shard_map/experts_next/pallas_call | solution.py:171
  39.5 3.6 %experts_next.4 = (f32[128,1152]{1,0:T(8,128)S(1)}, bf16[128,1152]{1,0:T(8,128)(2,1)S(1)}) custom-call(s32[1]{0:T(128)} %bitcast.first_ref, bf16[128,1152]{1,0:T(8,128)(2,1)S(1)} %constant_dynamic-update-slice_fusion.2.pair_ref, bf16[128,1152]{1,0:T(8,128)(2,1)S(1)} %collective-permute-done.12.other_ref, bf16[16,1024]{1,0:T(8,128)(2,1)S(1)} %pad.4.router_ref, ...), custom_call_target="tpu_custom_call" | custom-call | flops 3221225472 | tf_op jit(solution)/shard_map/experts_next/pallas_call | solution.py:171
  43.7 3.8 %experts_next.5 = (f32[128,1152]{1,0:T(8,128)S(1)}, bf16[128,1152]{1,0:T(8,128)(2,1)S(1)}) custom-call(s32[1]{0:T(128)} %bitcast.first_ref, bf16[128,1152]{1,0:T(8,128)(2,1)S(1)} %constant_dynamic-update-slice_fusion.4.pair_ref, bf16[128,1152]{1,0:T(8,128)(2,1)S(1)} %collective-permute-done.18.other_ref, bf16[16,1024]{1,0:T(8,128)(2,1)S(1)} %pad.4.router_ref, ...), custom_call_target="tpu_custom_call" | custom-call | flops 3221225472 | tf_op jit(solution)/shard_map/experts_next/pallas_call | solution.py:171
  48.7 1.3 %collective-permute-start.8 = (bf16[64,1152]{1,0:T(8,128)(2,1)S(1)}, bf16[64,1152]{1,0:T(8,128)(2,1)S(1)}, u32[]{:S(2)}, u32[]{:S(2)}) collective-permute-start(bf16[64,1152]{1,0:T(8,128)(2,1)S(1)} %slice.80), channel_id=1, source_target_pairs={{0,2},{1,3},{2,0},{3,1},{4,6},{5,7},{6,4},{7,5},{8,10},{9,11},{10,... | collective-permute-start | bytes 442376 | tf_op jit(solution)/shard_map/ppermute | solution.py:112
  50.1 0.9 %collective-permute-start.14 = (bf16[64,1152]{1,0:T(8,128)(2,1)S(1)}, bf16[64,1152]{1,0:T(8,128)(2,1)S(1)}, u32[]{:S(2)}, u32[]{:S(2)}) collective-permute-start(bf16[64,1152]{1,0:T(8,128)(2,1)S(1)} %slice.79), channel_id=1, source_target_pairs={{0,2},{1,3},{2,0},{3,1},{4,6},{5,7},{6,4},{7,5},{8,10},{9,11},{10,... | collective-permute-start | bytes 442376 | tf_op jit(solution)/shard_map/ppermute | solution.py:112
  51.0 6.7 %collective-permute-done.8 = bf16[64,1152]{1,0:T(8,128)(2,1)S(1)} collective-permute-done((bf16[64,1152]{1,0:T(8,128)(2,1)S(1)}, bf16[64,1152]{1,0:T(8,128)(2,1)S(1)}, u32[]{:S(2)}, u32[]{:S(2)}) %collective-permute-start.8) | collective-permute-done | bytes 147488 | tf_op jit(solution)/shard_map/ppermute | solution.py:112
  58.2 1.4 %collective-permute-start.20 = (bf16[64,1152]{1,0:T(8,128)(2,1)S(1)}, bf16[64,1152]{1,0:T(8,128)(2,1)S(1)}, u32[]{:S(2)}, u32[]{:S(2)}) collective-permute-start(bf16[64,1152]{1,0:T(8,128)(2,1)S(1)} %slice.78), channel_id=1, source_target_pairs={{0,2},{1,3},{2,0},{3,1},{4,6},{5,7},{6,4},{7,5},{8,10},{9,11},{10,... | collective-permute-start | bytes 442376 | tf_op jit(solution)/shard_map/ppermute | solution.py:112
  59.6 1.2 %collective-permute-done.14 = bf16[64,1152]{1,0:T(8,128)(2,1)S(1)} collective-permute-done((bf16[64,1152]{1,0:T(8,128)(2,1)S(1)}, bf16[64,1152]{1,0:T(8,128)(2,1)S(1)}, u32[]{:S(2)}, u32[]{:S(2)}) %collective-permute-start.14) | collective-permute-done | bytes 147488 | tf_op jit(solution)/shard_map/ppermute | solution.py:112
  60.8 1.5 %collective-permute-start.15 = (bf16[64,1152]{1,0:T(8,128)(2,1)S(1)}, bf16[64,1152]{1,0:T(8,128)(2,1)S(1)}, u32[]{:S(2)}, u32[]{:S(2)}) collective-permute-start(bf16[64,1152]{1,0:T(8,128)(2,1)S(1)} %fusion.1), channel_id=1, source_target_pairs={{0,8},{1,9},{2,10},{3,11},{4,12},{5,13},{6,14},{7,15},{8,0},{9,1},... | collective-permute-start | bytes 442376 | tf_op jit(solution)/shard_map/ppermute | solution.py:112
  62.3 1.3 %collective-permute-done.20 = bf16[64,1152]{1,0:T(8,128)(2,1)S(1)} collective-permute-done((bf16[64,1152]{1,0:T(8,128)(2,1)S(1)}, bf16[64,1152]{1,0:T(8,128)(2,1)S(1)}, u32[]{:S(2)}, u32[]{:S(2)}) %collective-permute-start.20) | collective-permute-done | bytes 147488 | tf_op jit(solution)/shard_map/ppermute | solution.py:112
  63.6 2.7 %collective-permute-start.21 = (bf16[64,1152]{1,0:T(8,128)(2,1)S(1)}, bf16[64,1152]{1,0:T(8,128)(2,1)S(1)}, u32[]{:S(2)}, u32[]{:S(2)}) collective-permute-start(bf16[64,1152]{1,0:T(8,128)(2,1)S(1)} %fusion), channel_id=1, source_target_pairs={{0,12},{1,13},{2,14},{3,15},{4,8},{5,9},{6,10},{7,11},{8,4},{9,5},... | collective-permute-start | bytes 442376 | tf_op jit(solution)/shard_map/ppermute | solution.py:112
  66.3 7.3 %collective-permute-done.15 = bf16[64,1152]{1,0:T(8,128)(2,1)S(1)} collective-permute-done((bf16[64,1152]{1,0:T(8,128)(2,1)S(1)}, bf16[64,1152]{1,0:T(8,128)(2,1)S(1)}, u32[]{:S(2)}, u32[]{:S(2)}) %collective-permute-start.15) | collective-permute-done | bytes 147488 | tf_op jit(solution)/shard_map/ppermute | solution.py:112
  (47 shorter events, 6.7 us)
Async XLA Ops:
  1.7 7.8 %collective-permute-start = (bf16[64,1152]{1,0:T(8,128)(2,1)}, bf16[64,1152]{1,0:T(8,128)(2,1)S(1)}, u32[]{:S(2)}, u32[]{:S(2)}) collective-permute-start(bf16[64,1152]{1,0:T(8,128)(2,1)} %pack.1), channel_id=1, source_target_pairs={{0,2},{1,3},{2,0},{3,1},{4,6},{5,7},{6,4},{7,5},{8,10},{9,11},{10,... | collective-permute-start | bytes 442376 | tf_op jit(solution)/shard_map/ppermute | solution.py:112
  4.6 7.9 %collective-permute-start.4 = (bf16[64,1152]{1,0:T(8,128)(2,1)}, bf16[64,1152]{1,0:T(8,128)(2,1)S(1)}, u32[]{:S(2)}, u32[]{:S(2)}) collective-permute-start(bf16[64,1152]{1,0:T(8,128)(2,1)} %pack.1), channel_id=1, source_target_pairs={{0,4},{1,5},{2,6},{3,7},{4,0},{5,1},{6,2},{7,3},{8,12},{9,13},{10,... | collective-permute-start | bytes 442376 | tf_op jit(solution)/shard_map/ppermute | solution.py:112
  6.2 9.4 %collective-permute-start.10 = (bf16[64,1152]{1,0:T(8,128)(2,1)}, bf16[64,1152]{1,0:T(8,128)(2,1)S(1)}, u32[]{:S(2)}, u32[]{:S(2)}) collective-permute-start(bf16[64,1152]{1,0:T(8,128)(2,1)} %pack.1), channel_id=1, source_target_pairs={{0,8},{1,9},{2,10},{3,11},{4,12},{5,13},{6,14},{7,15},{8,0},{9,1},... | collective-permute-start | bytes 442376 | tf_op jit(solution)/shard_map/ppermute | solution.py:112
  10.4 16.7 %collective-permute-start.1 = (bf16[128,1152]{1,0:T(8,128)(2,1)S(1)}, bf16[128,1152]{1,0:T(8,128)(2,1)S(1)}, u32[]{:S(2)}, u32[]{:S(2)}) collective-permute-start(bf16[128,1152]{1,0:T(8,128)(2,1)S(1)} %pad_maximum_fusion.pair_ref), channel_id=1, source_target_pairs={{0,1},{1,0},{2,3},{3,2},{4,5},{5,4},{6,7},{7,6},{8,9},{9,8},{10,11... | collective-permute-start | bytes 884744 | tf_op jit(solution)/shard_map/ppermute | solution.py:112
  12.5 5.8 %collective-permute-start.5 = (bf16[64,1152]{1,0:T(8,128)(2,1)S(1)}, bf16[64,1152]{1,0:T(8,128)(2,1)S(1)}, u32[]{:S(2)}, u32[]{:S(2)}) collective-permute-start(bf16[64,1152]{1,0:T(8,128)(2,1)S(1)} %collective-permute-done.4), channel_id=1, source_target_pairs={{0,2},{1,3},{2,0},{3,1},{4,6},{5,7},{6,4},{7,5},{8,10},{9,11},{10,... | collective-permute-start | bytes 442376 | tf_op jit(solution)/shard_map/ppermute | solution.py:112
  15.6 5.1 %collective-permute-start.11 = (bf16[64,1152]{1,0:T(8,128)(2,1)S(1)}, bf16[64,1152]{1,0:T(8,128)(2,1)S(1)}, u32[]{:S(2)}, u32[]{:S(2)}) collective-permute-start(bf16[64,1152]{1,0:T(8,128)(2,1)S(1)} %collective-permute-done.10), channel_id=1, source_target_pairs={{0,2},{1,3},{2,0},{3,1},{4,6},{5,7},{6,4},{7,5},{8,10},{9,11},{10,... | collective-permute-start | bytes 442376 | tf_op jit(solution)/shard_map/ppermute | solution.py:112
  16.1 5.1 %collective-permute-start.16 = (bf16[64,1152]{1,0:T(8,128)(2,1)S(1)}, bf16[64,1152]{1,0:T(8,128)(2,1)S(1)}, u32[]{:S(2)}, u32[]{:S(2)}) collective-permute-start(bf16[64,1152]{1,0:T(8,128)(2,1)S(1)} %collective-permute-done.10), channel_id=1, source_target_pairs={{0,4},{1,5},{2,6},{3,7},{4,0},{5,1},{6,2},{7,3},{8,12},{9,13},{10,... | collective-permute-start | bytes 442376 | tf_op jit(solution)/shard_map/ppermute | solution.py:112
  18.4 17.5 %collective-permute-start.6 = (bf16[128,1152]{1,0:T(8,128)(2,1)S(1)}, bf16[128,1152]{1,0:T(8,128)(2,1)S(1)}, u32[]{:S(2)}, u32[]{:S(2)}) collective-permute-start(bf16[128,1152]{1,0:T(8,128)(2,1)S(1)} %constant_dynamic-update-slice_fusion.pair_ref), channel_id=1, source_target_pairs={{0,1},{1,0},{2,3},{3,2},{4,5},{5,4},{6,7},{7,6},{8,9},{9,8},{10,11... | collective-permute-start | bytes 884744 | tf_op jit(solution)/shard_map/ppermute | solution.py:112
  20.7 18.8 %collective-permute-start.12 = (bf16[128,1152]{1,0:T(8,128)(2,1)S(1)}, bf16[128,1152]{1,0:T(8,128)(2,1)S(1)}, u32[]{:S(2)}, u32[]{:S(2)}) collective-permute-start(bf16[128,1152]{1,0:T(8,128)(2,1)S(1)} %constant_dynamic-update-slice_fusion.2.pair_ref), channel_id=1, source_target_pairs={{0,1},{1,0},{2,3},{3,2},{4,5},{5,4},{6,7},{7,6},{8,9},{9,8},{10,11... | collective-permute-start | bytes 884744 | tf_op jit(solution)/shard_map/ppermute | solution.py:112
  21.2 5.8 %collective-permute-start.17 = (bf16[64,1152]{1,0:T(8,128)(2,1)S(1)}, bf16[64,1152]{1,0:T(8,128)(2,1)S(1)}, u32[]{:S(2)}, u32[]{:S(2)}) collective-permute-start(bf16[64,1152]{1,0:T(8,128)(2,1)S(1)} %collective-permute-done.16), channel_id=1, source_target_pairs={{0,2},{1,3},{2,0},{3,1},{4,6},{5,7},{6,4},{7,5},{8,10},{9,11},{10,... | collective-permute-start | bytes 442376 | tf_op jit(solution)/shard_map/ppermute | solution.py:112
  27.1 16.7 %collective-permute-start.18 = (bf16[128,1152]{1,0:T(8,128)(2,1)S(1)}, bf16[128,1152]{1,0:T(8,128)(2,1)S(1)}, u32[]{:S(2)}, u32[]{:S(2)}) collective-permute-start(bf16[128,1152]{1,0:T(8,128)(2,1)S(1)} %constant_dynamic-update-slice_fusion.4.pair_ref), channel_id=1, source_target_pairs={{0,1},{1,0},{2,3},{3,2},{4,5},{5,4},{6,7},{7,6},{8,9},{9,8},{10,11... | collective-permute-start | bytes 884744 | tf_op jit(solution)/shard_map/ppermute | solution.py:112
  35.2 12.4 %collective-permute-start.2 = (bf16[128,1152]{1,0:T(8,128)(2,1)S(1)}, bf16[128,1152]{1,0:T(8,128)(2,1)S(1)}, u32[]{:S(2)}, u32[]{:S(2)}) collective-permute-start(bf16[128,1152]{1,0:T(8,128)(2,1)S(1)} %get-tuple-element.16._), channel_id=1, source_target_pairs={{0,1},{1,0},{2,3},{3,2},{4,5},{5,4},{6,7},{7,6},{8,9},{9,8},{10,11... | collective-permute-start | bytes 884744 | tf_op jit(solution)/shard_map/ppermute | solution.py:112
  39.5 9.2 %collective-permute-start.7 = (bf16[128,1152]{1,0:T(8,128)(2,1)S(1)}, bf16[128,1152]{1,0:T(8,128)(2,1)S(1)}, u32[]{:S(2)}, u32[]{:S(2)}) collective-permute-start(bf16[128,1152]{1,0:T(8,128)(2,1)S(1)} %get-tuple-element.20._), channel_id=1, source_target_pairs={{0,1},{1,0},{2,3},{3,2},{4,5},{5,4},{6,7},{7,6},{8,9},{9,8},{10,11... | collective-permute-start | bytes 884744 | tf_op jit(solution)/shard_map/ppermute | solution.py:112
  43.2 6.8 %collective-permute-start.13 = (bf16[128,1152]{1,0:T(8,128)(2,1)S(1)}, bf16[128,1152]{1,0:T(8,128)(2,1)S(1)}, u32[]{:S(2)}, u32[]{:S(2)}) collective-permute-start(bf16[128,1152]{1,0:T(8,128)(2,1)S(1)} %get-tuple-element.22._), channel_id=1, source_target_pairs={{0,1},{1,0},{2,3},{3,2},{4,5},{5,4},{6,7},{7,6},{8,9},{9,8},{10,11... | collective-permute-start | bytes 884744 | tf_op jit(solution)/shard_map/ppermute | solution.py:112
  47.6 10.6 %collective-permute-start.19 = (bf16[128,1152]{1,0:T(8,128)(2,1)S(1)}, bf16[128,1152]{1,0:T(8,128)(2,1)S(1)}, u32[]{:S(2)}, u32[]{:S(2)}) collective-permute-start(bf16[128,1152]{1,0:T(8,128)(2,1)S(1)} %get-tuple-element.24), channel_id=1, source_target_pairs={{0,1},{1,0},{2,3},{3,2},{4,5},{5,4},{6,7},{7,6},{8,9},{9,8},{10,11... | collective-permute-start | bytes 884744 | tf_op jit(solution)/shard_map/ppermute | solution.py:112
  47.8 18.5 %collective-permute-start.3 = (bf16[64,1152]{1,0:T(8,128)(2,1)S(1)}, bf16[64,1152]{1,0:T(8,128)(2,1)S(1)}, u32[]{:S(2)}, u32[]{:S(2)}) collective-permute-start(bf16[64,1152]{1,0:T(8,128)(2,1)S(1)} %slice.81), channel_id=1, source_target_pairs={{0,2},{1,3},{2,0},{3,1},{4,6},{5,7},{6,4},{7,5},{8,10},{9,11},{10,... | collective-permute-start | bytes 442376 | tf_op jit(solution)/shard_map/ppermute | solution.py:112
  48.7 8.9 %collective-permute-start.8 = (bf16[64,1152]{1,0:T(8,128)(2,1)S(1)}, bf16[64,1152]{1,0:T(8,128)(2,1)S(1)}, u32[]{:S(2)}, u32[]{:S(2)}) collective-permute-start(bf16[64,1152]{1,0:T(8,128)(2,1)S(1)} %slice.80), channel_id=1, source_target_pairs={{0,2},{1,3},{2,0},{3,1},{4,6},{5,7},{6,4},{7,5},{8,10},{9,11},{10,... | collective-permute-start | bytes 442376 | tf_op jit(solution)/shard_map/ppermute | solution.py:112
  50.1 10.7 %collective-permute-start.14 = (bf16[64,1152]{1,0:T(8,128)(2,1)S(1)}, bf16[64,1152]{1,0:T(8,128)(2,1)S(1)}, u32[]{:S(2)}, u32[]{:S(2)}) collective-permute-start(bf16[64,1152]{1,0:T(8,128)(2,1)S(1)} %slice.79), channel_id=1, source_target_pairs={{0,2},{1,3},{2,0},{3,1},{4,6},{5,7},{6,4},{7,5},{8,10},{9,11},{10,... | collective-permute-start | bytes 442376 | tf_op jit(solution)/shard_map/ppermute | solution.py:112
  57.7 8.6 %collective-permute-start.9 = (bf16[64,1152]{1,0:T(8,128)(2,1)S(1)}, bf16[64,1152]{1,0:T(8,128)(2,1)S(1)}, u32[]{:S(2)}, u32[]{:S(2)}) collective-permute-start(bf16[64,1152]{1,0:T(8,128)(2,1)S(1)} %fusion.2), channel_id=1, source_target_pairs={{0,4},{1,5},{2,6},{3,7},{4,0},{5,1},{6,2},{7,3},{8,12},{9,13},{10,... | collective-permute-start | bytes 442376 | tf_op jit(solution)/shard_map/ppermute | solution.py:112
  58.2 5.3 %collective-permute-start.20 = (bf16[64,1152]{1,0:T(8,128)(2,1)S(1)}, bf16[64,1152]{1,0:T(8,128)(2,1)S(1)}, u32[]{:S(2)}, u32[]{:S(2)}) collective-permute-start(bf16[64,1152]{1,0:T(8,128)(2,1)S(1)} %slice.78), channel_id=1, source_target_pairs={{0,2},{1,3},{2,0},{3,1},{4,6},{5,7},{6,4},{7,5},{8,10},{9,11},{10,... | collective-permute-start | bytes 442376 | tf_op jit(solution)/shard_map/ppermute | solution.py:112
  60.8 12.8 %collective-permute-start.15 = (bf16[64,1152]{1,0:T(8,128)(2,1)S(1)}, bf16[64,1152]{1,0:T(8,128)(2,1)S(1)}, u32[]{:S(2)}, u32[]{:S(2)}) collective-permute-start(bf16[64,1152]{1,0:T(8,128)(2,1)S(1)} %fusion.1), channel_id=1, source_target_pairs={{0,8},{1,9},{2,10},{3,11},{4,12},{5,13},{6,14},{7,15},{8,0},{9,1},... | collective-permute-start | bytes 442376 | tf_op jit(solution)/shard_map/ppermute | solution.py:112
  63.6 10.0 %collective-permute-start.21 = (bf16[64,1152]{1,0:T(8,128)(2,1)S(1)}, bf16[64,1152]{1,0:T(8,128)(2,1)S(1)}, u32[]{:S(2)}, u32[]{:S(2)}) collective-permute-start(bf16[64,1152]{1,0:T(8,128)(2,1)S(1)} %fusion), channel_id=1, source_target_pairs={{0,12},{1,13},{2,14},{3,15},{4,8},{5,9},{6,10},{7,11},{8,4},{9,5},... | collective-permute-start | bytes 442376 | tf_op jit(solution)/shard_map/ppermute | solution.py:112

commit v4 on v1

v4 whole, which is shorter than its diff:
```python
import jax
import jax.numpy as jnp
from jax import lax
from jax.experimental import pallas as pl
from jax.experimental.pallas import tpu as pltpu
from jax.sharding import PartitionSpec as P

GROUP = 16
TAIL = 128
SCALE = 2.0**40
STEP = 256
PIECE = 256


def pack_kernel(ids_ref, row_ref, out_ref):
    rows, lat = row_ref.shape
    top = ids_ref.shape[0]
    out_ref[:, :lat] = row_ref[...]
    ids = ids_ref[...].astype(jnp.float32)
    ids = jnp.concatenate([ids, jnp.full((top, TAIL - rows), -1.0, jnp.float32)], axis=1)
    ids = jnp.concatenate([ids, jnp.full((TAIL - top, TAIL), -1.0, jnp.float32)], axis=0)
    out_ref[:, lat:] = ids.T[:rows].astype(jnp.bfloat16)


def load_kernel(router_ref, up_hbm, down_hbm, dep_ref, columns_ref, up_ref, down_ref, sems):
    copies = []
    for src, dst in ((up_hbm, up_ref), (down_hbm, down_ref)):
        for e in range(src.shape[0]):
            for r in range(0, src.shape[1], PIECE):
                at = (e, pl.ds(r, PIECE))
                copies.append(pltpu.make_async_copy(src.at[at], dst.at[at], sems.at[len(copies)]))
    for copy in copies:
        copy.start()
    columns_ref[...] = jnp.zeros_like(columns_ref)
    columns_ref[: router_ref.shape[0], :] = router_ref[...]
    for copy in copies:
        copy.wait()


def join_kernel(a_ref, b_ref, *refs):
    out_ref = refs[-1]
    rows = a_ref.shape[0]
    out_ref[:rows] = a_ref[...]
    out_ref[rows:] = b_ref[...]


def expert_kernel(first_ref, pair_ref, other_ref, columns_ref, up_ref, down_ref, *refs):
    keep_ref, send_ref, inner_ref = refs[-3:]
    half, wide = pair_ref.shape
    lat = wide - TAIL
    local, eff, _ = down_ref.shape
    x = jnp.concatenate([pair_ref[:, :lat], other_ref[:, :lat]], axis=0)
    tail = jnp.concatenate([pair_ref[:, lat:], other_ref[:, lat:]], axis=0).astype(jnp.float32)
    logits = lax.dot_general(
        x, columns_ref[...], (((1,), (1,)), ((), ())), preferred_element_type=jnp.float32
    )
    sums = jnp.zeros((2 * half, 1), jnp.float32)
    for e in range(local):
        label = (first_ref[0] + e).astype(jnp.float32)
        mask = jnp.max(jnp.where(tail == label, 1.0, 0.0), axis=1, keepdims=True)
        score = jax.nn.sigmoid(logits[:, e : e + 1]) * (mask * SCALE)
        sums = sums + score
        for c in range(0, eff, STEP):
            gate = jnp.dot(x, up_ref[e, :, c : c + STEP], preferred_element_type=jnp.float32)
            up = jnp.dot(x, up_ref[e, :, eff + c : eff + c + STEP], preferred_element_type=jnp.float32)
            inner_ref[:, e * eff + c : e * eff + c + STEP] = (
                gate / (1.0 + jnp.exp(-gate)) * up * score
            ).astype(jnp.bfloat16)
    inner = inner_ref[...]
    for c in range(0, lat, STEP):
        down = down_ref[:, :, c : c + STEP].reshape(local * eff, STEP)
        part = jnp.dot(inner, down, preferred_element_type=jnp.float32)
        keep_ref[:, c : c + STEP] = part[:half]
        send_ref[:, c : c + STEP] = part[half:].astype(jnp.bfloat16)
    lane = lax.broadcasted_iota(jnp.int32, (2 * half, TAIL), 1)
    sums = jnp.where(lane == 0, sums, 0.0)
    keep_ref[:, lat:] = sums[:half]
    send_ref[:, lat:] = sums[half:].astype(jnp.bfloat16)


def fold_kernel(mine_ref, came_ref, *refs):
    keep_ref, send_ref = refs[-2:]
    rows = keep_ref.shape[0]
    keep_ref[...] = mine_ref[:rows] + came_ref[:rows].astype(jnp.float32)
    send_ref[...] = (mine_ref[rows:] + came_ref[rows:].astype(jnp.float32)).astype(jnp.bfloat16)


def add_kernel(mine_ref, came_ref, out_ref):
    out_ref[...] = (mine_ref[...] + came_ref[...].astype(jnp.float32)).astype(jnp.bfloat16)


def total_kernel(*refs):
    total_ref = refs[-1]
    total = refs[0][...]
    for ref in refs[1:-1]:
        total = total + ref[...].astype(jnp.float32)
    total_ref[...] = total


def finish_kernel(*refs):
    out_ref = refs[-1]
    lat = out_ref.shape[1]
    total = refs[0][...]
    for ref in refs[1:-1]:
        total = total + ref[...].astype(jnp.float32)
    out_ref[...] = (total[:, :lat] / total[:, lat : lat + 1]).astype(jnp.bfloat16)


def in_vmem(x):
    return pltpu.with_memory_space_constraint(x, pltpu.VMEM)


def in_hbm(x):
    return pltpu.with_memory_space_constraint(x, pltpu.HBM)


VMEM = pl.BlockSpec(memory_space=pltpu.VMEM)
ANY = pl.BlockSpec(memory_space=pl.ANY)


def call(kernel, outs, args, deps=(), smem=(), hbm=(), scratch=(), cost=None):
    specs = [pl.BlockSpec(memory_space=pltpu.SMEM)] * len(smem) + [VMEM] * len(args)
    specs += [ANY] * (len(hbm) + len(deps))
    operands = list(smem) + [in_vmem(a) for a in args] + [in_hbm(h) for h in hbm] + [in_vmem(d) for d in deps]
    return pl.pallas_call(
        kernel,
        out_shape=outs,
        in_specs=specs,
        out_specs=[VMEM] * len(outs),
        scratch_shapes=list(scratch),
        compiler_params=pltpu.CompilerParams(vmem_limit_bytes=16 * 1024 * 1024),
        cost_estimate=cost or pl.CostEstimate(flops=0, bytes_accessed=200_000, transcendentals=0),
        name=kernel.__name__.removesuffix("_kernel"),
    )(*operands)


def on_device(latent_in, routes, router, gate_up, expert_down):
    n_dev = lax.axis_size("exp")
    local = gate_up.shape[0]
    eff = expert_down.shape[1]
    rows, lat = latent_in.shape
    wide = lat + TAIL
    first = (lax.axis_index("exp") * local).astype(jnp.int32).reshape(1)

    def swap(x, bits):
        return lax.ppermute(x, "exp", [(i, i ^ bits) for i in range(n_dev)])

    def space(height, dtype):
        return pltpu.VMEM((height, wide), dtype)

    def weights(dep):
        moved = gate_up.size + expert_down.size
        return call(
            load_kernel,
            [
                pltpu.VMEM((16, lat), jnp.bfloat16),
                pltpu.VMEM(gate_up.shape, gate_up.dtype),
                pltpu.VMEM(expert_down.shape, expert_down.dtype),
            ],
            [router.T],
            deps=[dep],
            hbm=[gate_up, expert_down],
            scratch=[pltpu.SemaphoreType.DMA((local * (lat + eff) // PIECE,))],
            cost=pl.CostEstimate(flops=0, bytes_accessed=4 * moved, transcendentals=0),
        )

    def join(a, b, deps=()):
        return call(join_kernel, [space(2 * rows, jnp.bfloat16)], [a, b], deps)[0]

    def experts(pair, other, loaded, deps=()):
        return call(
            expert_kernel,
            [space(2 * rows, jnp.float32), space(2 * rows, jnp.bfloat16)],
            [pair, other, *loaded],
            deps,
            smem=[first],
            scratch=[pltpu.VMEM((4 * rows, local * eff), jnp.bfloat16)],
            cost=pl.CostEstimate(
                flops=2 * 4 * rows * local * eff * lat * 3, bytes_accessed=0, transcendentals=0
            ),
        )

    def fold(mine, came, deps=()):
        return call(fold_kernel, [space(rows, jnp.float32), space(rows, jnp.bfloat16)], [mine, came], deps)

    def add(mine, came):
        return call(add_kernel, [space(rows, jnp.bfloat16)], [mine, came])[0]

    def group_pass(mine):
        block = {0: mine, 2: swap(mine, 8), 1: swap(mine, 4)}
        block[3] = swap(block[2], 4)
        other = {k: swap(block[k], 2) for k in (2, 1, 3, 0)}
        loaded = weights(block[2])
        pair, far = {}, {}
        keep, send, came, fold_keep, fold_send, y_came, z_send = {}, {}, {}, {}, {}, {}, {}

        def gather(k, deps=()):
            pair[k] = join(block[k], other[k], deps)
            far[k] = swap(pair[k], 1)

        def compute(k, deps=()):
            keep[k], send[k] = experts(pair[k], far[k], loaded, deps)
            came[k] = swap(send[k], 1)

        def reduce_core(k):
            fold_keep[k], fold_send[k] = fold(keep[k], came[k])
            y_came[k] = swap(fold_send[k], 2)

        def reduce_y(k):
            z_send[k] = add(fold_keep[k], y_came[k])
            return swap(z_send[k], 4 * k)

        gather(2)
        compute(2, [block[1], block[3]])
        gather(3, [send[2]])
        gather(1, [send[2]])
        compute(3, [send[2], pair[1]])
        gather(0, [send[3]])
        reduce_core(2)
        compute(1, [send[3], fold_send[2], pair[0]])
        reduce_core(3)
        z_2 = reduce_y(2)
        compute(0, [send[1], fold_send[3], z_send[2]])
        reduce_core(1)
        z_3 = reduce_y(3)
        z_1 = reduce_y(1)
        reduce_core(0)
        return fold_keep[0], y_came[0], z_1, z_2, z_3

    packet = call(pack_kernel, [space(rows, jnp.bfloat16)], [routes.T, latent_in])[0]

    def finish(parts):
        return pl.pallas_call(
            finish_kernel,
            out_shape=jax.ShapeDtypeStruct((rows, lat), jnp.bfloat16),
            in_specs=[VMEM] * len(parts),
            out_specs=VMEM,
            name="finish",
        )(*[in_vmem(p) for p in parts])

    if n_dev == GROUP:
        return finish(group_pass(packet))

    def next_group(x):
        return lax.ppermute(x, "exp", [(i, (i + GROUP) % n_dev) for i in range(n_dev)])

    def step(carry, _):
        mine, total = carry
        total = call(total_kernel, [space(rows, jnp.float32)], [total, *group_pass(mine)])[0]
        return (next_group(mine), next_group(total)), None

    start = (packet, jnp.zeros((rows, wide), jnp.float32))
    (_, total), _ = lax.scan(step, start, None, length=n_dev // GROUP)
    return finish([total])


def solution(mesh):
    placed = (
        P(("grp", "exp"), None),
        P(("grp", "exp"), None),
        P(None, "exp"),
        P("exp", None, None),
        P("exp", None, None),
    )
    return jax.shard_map(
        on_device, mesh=mesh, in_specs=placed, out_specs=P(("grp", "exp"), None), check_vma=False
    )
```

time: 144 us -> 72.3 us (0.50)
  waiting for transfers between devices: 66 us -> 23.1 us
  blocking collectives: 41.6 us -> 0 us
  starting transfers between devices: 0.04 us -> 25.3 us
  Pallas kernels: 0 us -> 21.1 us
  matrix products: 19.8 us -> 0 us
  between operations: 13.5 us -> 0.2 us
  other arithmetic: 2.83 us -> 0 us
  local copies, waits for them, and re-layouts: 0.16 us -> 2.28 us
    reduce_scatter x1 -> x0, waiting for transfers between devices: 60.5 us -> none  [on_device(): return lax.psum_scatter(sums, 'exp', scatter_dimension=0, tiled=True)]
    all_gather x2 -> x0, blocking collectives: 41.6 us -> none  [the longest x1 23.5 us: on_device(): chosen = lax.all_gather(routes, 'exp', axis=0, tiled=True)]
    ppermute x0 -> x22, starting transfers between devices: none -> 25.3 us  [swap(): return lax.ppermute(x, 'exp', [(i, i ^ bits) for i in range(n_dev)])]
    ppermute x0 -> x22, waiting for transfers between devices: none -> 23.1 us  [swap(): return lax.ppermute(x, 'exp', [(i, i ^ bits) for i in range(n_dev)])]
    pallas_call x0 -> x18, Pallas kernels: none -> 21.1 us  [the longest x17 20.3 us: call(): pl.pallas_call(kernel, out_shape=outs, in_specs=specs, out_specs=[VMEM] *...]
    dot_general x4 -> x0, matrix products: 19.8 us -> none  [the longest x2 11.6 us: part(): both = jnp.dot(tok, gate_up[e], preferred_element_type=jnp.float32)]
    all_gather x1 -> x0, waiting for transfers between devices: 4.78 us -> none  [on_device(): tokens = lax.all_gather(latent_in, 'exp', axis=0, tiled=True)]
    convert_element_type x1 -> x0, other arithmetic: 2.69 us -> none  [part(): inner.append(one.astype(jnp.bfloat16))]
  transfers between devices with their start and end apart: 2 -> 22, of which waited for: 2 -> 7; matrix products, arithmetic and copies ran while one was open for 0% -> 0% of each run, Pallas kernels for 0% -> 28%
where the time goes in v4:
time: 72.3 us; the launch traced here: 72 us
  starting transfers between devices  25.3 us (35%)
  waiting for transfers between devices  23.1 us (32%)
  Pallas kernels  21.1 us (29%)
  local copies, waits for them, and re-layouts  2.28 us (3%)
    ppermute x22, starting transfers between devices, swap(): return lax.ppermute(x, 'exp', [(i, i ^ bits) for i in range(n_dev)])  25.3 us
    ppermute x22, waiting for transfers between devices, swap(): return lax.ppermute(x, 'exp', [(i, i ^ bits) for i in range(n_dev)])  23.1 us
    pallas_call x17, Pallas kernels, call(): pl.pallas_call(kernel, out_shape=outs, in_specs=specs, out_specs=[VMEM] *...  20.3 us
    unnamed x6, local copies, waits for them, and re-layouts  2.28 us
  transfers between devices with their start and end apart: 22, of which 7 were waited for; matrix products, arithmetic and copies ran while one was open for 0% of the time, Pallas kernels for 28%

profile of v4, /device:TPU:0, one launch (start us, length us, event | category | flops | bytes accessed | tf_op | source)
XLA Modules:
  0.0 72.0 jit_solution(11832550785214500368)
XLA Ops:
  0.0 0.9 %copy-done = bf16[64,1024]{1,0:T(8,128)(2,1)S(1)} copy-done((bf16[64,1024]{1,0:T(8,128)(2,1)S(1)}, bf16[64,1024]{1,0:T(8,128)(2,1)}, u32[]{:S(2)}) %copy-start) | copy-done | bytes 131096
  1.7 4.1 %collective-permute-start.1 = (bf16[64,1152]{1,0:T(8,128)(2,1)S(1)}, bf16[64,1152]{1,0:T(8,128)(2,1)S(1)}, u32[]{:S(2)}, u32[]{:S(2)}) collective-permute-start(bf16[64,1152]{1,0:T(8,128)(2,1)S(1)} %pack.1.a_ref), channel_id=1, source_target_pairs={{0,8},{1,9},{2,10},{3,11},{4,12},{5,13},{6,14},{7,15},{8,0},{9,1},... | collective-permute-start | bytes 442376 | tf_op jit(solution)/shard_map/ppermute | solution.py:146
  5.8 7.0 %collective-permute-done.1.a_ref.dep_ref = bf16[64,1152]{1,0:T(8,128)(2,1)S(1)} collective-permute-done((bf16[64,1152]{1,0:T(8,128)(2,1)S(1)}, bf16[64,1152]{1,0:T(8,128)(2,1)S(1)}, u32[]{:S(2)}, u32[]{:S(2)}) %collective-permute-start.1) | collective-permute-done | bytes 147488 | tf_op jit(solution)/shard_map/ppermute | solution.py:146
  12.8 1.6 %collective-permute-start.4 = (bf16[64,1152]{1,0:T(8,128)(2,1)S(1)}, bf16[64,1152]{1,0:T(8,128)(2,1)S(1)}, u32[]{:S(2)}, u32[]{:S(2)}) collective-permute-start(bf16[64,1152]{1,0:T(8,128)(2,1)S(1)} %collective-permute-done.1.a_ref.dep_ref), channel_id=1, source_target_pairs={{0,2},{1,3},{2,0},{3,1},{4,6},{5,7},{6,4},{7,5},{8,10},{9,11},{10,... | collective-permute-start | bytes 442376 | tf_op jit(solution)/shard_map/ppermute | solution.py:146
  14.4 3.6 %collective-permute-done.4.b_ref = bf16[64,1152]{1,0:T(8,128)(2,1)S(1)} collective-permute-done((bf16[64,1152]{1,0:T(8,128)(2,1)S(1)}, bf16[64,1152]{1,0:T(8,128)(2,1)S(1)}, u32[]{:S(2)}, u32[]{:S(2)}) %collective-permute-start.4) | collective-permute-done | bytes 147488 | tf_op jit(solution)/shard_map/ppermute | solution.py:146
  18.0 1.4 %collective-permute-start.2 = (bf16[64,1152]{1,0:T(8,128)(2,1)S(1)}, bf16[64,1152]{1,0:T(8,128)(2,1)S(1)}, u32[]{:S(2)}, u32[]{:S(2)}) collective-permute-start(bf16[64,1152]{1,0:T(8,128)(2,1)S(1)} %collective-permute-done.1.a_ref.dep_ref), channel_id=1, source_target_pairs={{0,4},{1,5},{2,6},{3,7},{4,0},{5,1},{6,2},{7,3},{8,12},{9,13},{10,... | collective-permute-start | bytes 442376 | tf_op jit(solution)/shard_map/ppermute | solution.py:146
  20.8 4.7 %load.1 = (bf16[16,1024]{1,0:T(8,128)(2,1)S(1)}, bf16[2,1024,2048]{2,1,0:T(8,128)(2,1)S(1)}, bf16[2,1024,1024]{2,1,0:T(8,128)(2,1)S(1)}) custom-call(bf16[2,1024]{1,0:T(2,128)(2,1)S(1)} %bitcast.4, bf16[2,1024,2048]{2,1,0:T(8,128)(2,1)} %up_hbm.1, bf16[2,1024,1024]{2,1,0:T(8,128)(2,1)} %down_hbm.1, bf16[64,1152]{1,0:T(8,128)(2,1)S(1)} %collective-permute-done.1.a_ref.dep_ref), custom_call_target="tpu_custom_call" | custom-call | bytes 25165824 | tf_op jit(solution)/shard_map/load/pallas_call | solution.py:125
  25.5 1.6 %collective-permute-start.3 = (bf16[64,1152]{1,0:T(8,128)(2,1)S(1)}, bf16[64,1152]{1,0:T(8,128)(2,1)S(1)}, u32[]{:S(2)}, u32[]{:S(2)}) collective-permute-start(bf16[64,1152]{1,0:T(8,128)(2,1)S(1)} %collective-permute-done.2.refs_1_.a_ref), channel_id=1, source_target_pairs={{0,2},{1,3},{2,0},{3,1},{4,6},{5,7},{6,4},{7,5},{8,10},{9,11},{10,... | collective-permute-start | bytes 442376 | tf_op jit(solution)/shard_map/ppermute | solution.py:146
  27.5 3.7 %expert.4 = (f32[128,1152]{1,0:T(8,128)S(1)}, bf16[128,1152]{1,0:T(8,128)(2,1)S(1)}) custom-call(s32[1]{0:T(128)} %bitcast.first_ref, bf16[128,1152]{1,0:T(8,128)(2,1)S(1)} %join.4.pair_ref, bf16[128,1152]{1,0:T(8,128)(2,1)S(1)} %collective-permute-done.5.other_ref, bf16[16,1024]{1,0:T(8,128)(2,1)S(1)} %get-tuple-element.24.columns_ref, ...), custom_call_target="tpu_custom_call" | custom-call | flops 3221225472 | tf_op jit(solution)/shard_map/expert/pallas_call | solution.py:125
  31.3 1.6 %collective-permute-start.8 = (bf16[64,1152]{1,0:T(8,128)(2,1)S(1)}, bf16[64,1152]{1,0:T(8,128)(2,1)S(1)}, u32[]{:S(2)}, u32[]{:S(2)}) collective-permute-start(bf16[64,1152]{1,0:T(8,128)(2,1)S(1)} %collective-permute-done.6.refs_0_.a_ref), channel_id=1, source_target_pairs={{0,2},{1,3},{2,0},{3,1},{4,6},{5,7},{6,4},{7,5},{8,10},{9,11},{10,... | collective-permute-start | bytes 442376 | tf_op jit(solution)/shard_map/ppermute | solution.py:146
  33.4 4.6 %collective-permute-done.8.b_ref = bf16[64,1152]{1,0:T(8,128)(2,1)S(1)} collective-permute-done((bf16[64,1152]{1,0:T(8,128)(2,1)S(1)}, bf16[64,1152]{1,0:T(8,128)(2,1)S(1)}, u32[]{:S(2)}, u32[]{:S(2)}) %collective-permute-start.8) | collective-permute-done | bytes 147488 | tf_op jit(solution)/shard_map/ppermute | solution.py:146
  38.2 3.7 %expert.5 = (f32[128,1152]{1,0:T(8,128)S(1)}, bf16[128,1152]{1,0:T(8,128)(2,1)S(1)}) custom-call(s32[1]{0:T(128)} %bitcast.first_ref, bf16[128,1152]{1,0:T(8,128)(2,1)S(1)} %join.5.pair_ref, bf16[128,1152]{1,0:T(8,128)(2,1)S(1)} %collective-permute-done.7.other_ref, bf16[16,1024]{1,0:T(8,128)(2,1)S(1)} %get-tuple-element.24.columns_ref, ...), custom_call_target="tpu_custom_call" | custom-call | flops 3221225472 | tf_op jit(solution)/shard_map/expert/pallas_call | solution.py:125
  42.5 1.6 %collective-permute-start.13 = (bf16[64,1152]{1,0:T(8,128)(2,1)S(1)}, bf16[64,1152]{1,0:T(8,128)(2,1)S(1)}, u32[]{:S(2)}, u32[]{:S(2)}) collective-permute-start(bf16[64,1152]{1,0:T(8,128)(2,1)S(1)} %get-tuple-element.30.refs_1_), channel_id=1, source_target_pairs={{0,2},{1,3},{2,0},{3,1},{4,6},{5,7},{6,4},{7,5},{8,10},{9,11},{10,... | collective-permute-start | bytes 442376 | tf_op jit(solution)/shard_map/ppermute | solution.py:146
  44.3 3.7 %expert.6 = (f32[128,1152]{1,0:T(8,128)S(1)}, bf16[128,1152]{1,0:T(8,128)(2,1)S(1)}) custom-call(s32[1]{0:T(128)} %bitcast.first_ref, bf16[128,1152]{1,0:T(8,128)(2,1)S(1)} %join.6.refs_1_.pair_ref, bf16[128,1152]{1,0:T(8,128)(2,1)S(1)} %collective-permute-done.10.other_ref, bf16[16,1024]{1,0:T(8,128)(2,1)S(1)} %get-tuple-element.24.columns_ref, ...), custom_call_target="tpu_custom_call" | custom-call | flops 3221225472 | tf_op jit(solution)/shard_map/expert/pallas_call | solution.py:125
  48.7 3.9 %expert.7 = (f32[128,1152]{1,0:T(8,128)S(1)}, bf16[128,1152]{1,0:T(8,128)(2,1)S(1)}) custom-call(s32[1]{0:T(128)} %bitcast.first_ref, bf16[128,1152]{1,0:T(8,128)(2,1)S(1)} %join.7.refs_2_.pair_ref, bf16[128,1152]{1,0:T(8,128)(2,1)S(1)} %collective-permute-done.9.other_ref, bf16[16,1024]{1,0:T(8,128)(2,1)S(1)} %get-tuple-element.24.columns_ref, ...), custom_call_target="tpu_custom_call" | custom-call | flops 3221225472 | tf_op jit(solution)/shard_map/expert/pallas_call | solution.py:125
  52.8 1.4 %collective-permute-start.20 = (bf16[64,1152]{1,0:T(8,128)(2,1)S(1)}, bf16[64,1152]{1,0:T(8,128)(2,1)S(1)}, u32[]{:S(2)}, u32[]{:S(2)}) collective-permute-start(bf16[64,1152]{1,0:T(8,128)(2,1)S(1)} %get-tuple-element.33.refs_1_), channel_id=1, source_target_pairs={{0,2},{1,3},{2,0},{3,1},{4,6},{5,7},{6,4},{7,5},{8,10},{9,11},{10,... | collective-permute-start | bytes 442376 | tf_op jit(solution)/shard_map/ppermute | solution.py:146
  54.2 0.8 %collective-permute-start.17 = (bf16[64,1152]{1,0:T(8,128)(2,1)S(1)}, bf16[64,1152]{1,0:T(8,128)(2,1)S(1)}, u32[]{:S(2)}, u32[]{:S(2)}) collective-permute-start(bf16[64,1152]{1,0:T(8,128)(2,1)S(1)} %get-tuple-element.41), channel_id=1, source_target_pairs={{0,2},{1,3},{2,0},{3,1},{4,6},{5,7},{6,4},{7,5},{8,10},{9,11},{10,... | collective-permute-start | bytes 442376 | tf_op jit(solution)/shard_map/ppermute | solution.py:146
  55.0 2.9 %collective-permute-start.19 = (bf16[64,1152]{1,0:T(8,128)(2,1)S(1)}, bf16[64,1152]{1,0:T(8,128)(2,1)S(1)}, u32[]{:S(2)}, u32[]{:S(2)}) collective-permute-start(bf16[64,1152]{1,0:T(8,128)(2,1)S(1)} %add.3.refs_2_), channel_id=1, source_target_pairs={{0,8},{1,9},{2,10},{3,11},{4,12},{5,13},{6,14},{7,15},{8,0},{9,1},... | collective-permute-start | bytes 442376 | tf_op jit(solution)/shard_map/ppermute | solution.py:146
  57.9 1.6 %collective-permute-done.20.came_ref = bf16[64,1152]{1,0:T(8,128)(2,1)S(1)} collective-permute-done((bf16[64,1152]{1,0:T(8,128)(2,1)S(1)}, bf16[64,1152]{1,0:T(8,128)(2,1)S(1)}, u32[]{:S(2)}, u32[]{:S(2)}) %collective-permute-start.20) | collective-permute-done | bytes 147488 | tf_op jit(solution)/shard_map/ppermute | solution.py:146
  59.5 4.2 %collective-permute-start.21 = (bf16[64,1152]{1,0:T(8,128)(2,1)S(1)}, bf16[64,1152]{1,0:T(8,128)(2,1)S(1)}, u32[]{:S(2)}, u32[]{:S(2)}) collective-permute-start(bf16[64,1152]{1,0:T(8,128)(2,1)S(1)} %add.5), channel_id=1, source_target_pairs={{0,12},{1,13},{2,14},{3,15},{4,8},{5,9},{6,10},{7,11},{8,4},{9,5},... | collective-permute-start | bytes 442376 | tf_op jit(solution)/shard_map/ppermute | solution.py:146
  63.9 1.4 %collective-permute-start.15 = (bf16[64,1152]{1,0:T(8,128)(2,1)S(1)}, bf16[64,1152]{1,0:T(8,128)(2,1)S(1)}, u32[]{:S(2)}, u32[]{:S(2)}) collective-permute-start(bf16[64,1152]{1,0:T(8,128)(2,1)S(1)} %get-tuple-element.38), channel_id=1, source_target_pairs={{0,2},{1,3},{2,0},{3,1},{4,6},{5,7},{6,4},{7,5},{8,10},{9,11},{10,... | collective-permute-start | bytes 442376 | tf_op jit(solution)/shard_map/ppermute | solution.py:146
  65.3 3.7 %collective-permute-done.19.refs_3_ = bf16[64,1152]{1,0:T(8,128)(2,1)S(1)} collective-permute-done((bf16[64,1152]{1,0:T(8,128)(2,1)S(1)}, bf16[64,1152]{1,0:T(8,128)(2,1)S(1)}, u32[]{:S(2)}, u32[]{:S(2)}) %collective-permute-start.19) | collective-permute-done | bytes 147488 | tf_op jit(solution)/shard_map/ppermute | solution.py:146
  68.9 2.3 %collective-permute-done.18.refs_2_ = bf16[64,1152]{1,0:T(8,128)(2,1)S(1)} collective-permute-done((bf16[64,1152]{1,0:T(8,128)(2,1)S(1)}, bf16[64,1152]{1,0:T(8,128)(2,1)S(1)}, u32[]{:S(2)}, u32[]{:S(2)}) %collective-permute-start.18) | collective-permute-done | bytes 147488 | tf_op jit(solution)/shard_map/ppermute | solution.py:146
  71.3 0.8 %finish.1 = bf16[64,1024]{1,0:T(8,128)(2,1)} custom-call(f32[64,1152]{1,0:T(8,128)S(1)} %get-tuple-element.37.refs_0_, bf16[64,1152]{1,0:T(8,128)(2,1)S(1)} %collective-permute-done.15.refs_1_, bf16[64,1152]{1,0:T(8,128)(2,1)S(1)} %collective-permute-done.18.refs_2_, bf16[64,1152]{1,0:T(8,128)(2,1)S(1)} %collective-permute-done.19.refs_3_, ...), custom_call_target="tpu_custom_call" | custom-call | tf_op jit(solution)/shard_map/finish/pallas_call | solution.py:233
  (44 shorter events, 4.9 us)
Async XLA Ops:
  0.0 0.9 %copy-start = (bf16[64,1024]{1,0:T(8,128)(2,1)S(1)}, bf16[64,1024]{1,0:T(8,128)(2,1)}, u32[]{:S(2)}) copy-start(bf16[64,1024]{1,0:T(8,128)(2,1)} %row_ref.1) | copy-start | bytes 393220
  0.9 0.7 copy-start.1
  1.7 11.1 %collective-permute-start.1 = (bf16[64,1152]{1,0:T(8,128)(2,1)S(1)}, bf16[64,1152]{1,0:T(8,128)(2,1)S(1)}, u32[]{:S(2)}, u32[]{:S(2)}) collective-permute-start(bf16[64,1152]{1,0:T(8,128)(2,1)S(1)} %pack.1.a_ref), channel_id=1, source_target_pairs={{0,8},{1,9},{2,10},{3,11},{4,12},{5,13},{6,14},{7,15},{8,0},{9,1},... | collective-permute-start | bytes 442376 | tf_op jit(solution)/shard_map/ppermute | solution.py:146
  12.8 5.1 %collective-permute-start.4 = (bf16[64,1152]{1,0:T(8,128)(2,1)S(1)}, bf16[64,1152]{1,0:T(8,128)(2,1)S(1)}, u32[]{:S(2)}, u32[]{:S(2)}) collective-permute-start(bf16[64,1152]{1,0:T(8,128)(2,1)S(1)} %collective-permute-done.1.a_ref.dep_ref), channel_id=1, source_target_pairs={{0,2},{1,3},{2,0},{3,1},{4,6},{5,7},{6,4},{7,5},{8,10},{9,11},{10,... | collective-permute-start | bytes 442376 | tf_op jit(solution)/shard_map/ppermute | solution.py:146
  18.0 9.5 %collective-permute-start.5 = (bf16[128,1152]{1,0:T(8,128)(2,1)S(1)}, bf16[128,1152]{1,0:T(8,128)(2,1)S(1)}, u32[]{:S(2)}, u32[]{:S(2)}) collective-permute-start(bf16[128,1152]{1,0:T(8,128)(2,1)S(1)} %join.4.pair_ref), channel_id=1, source_target_pairs={{0,1},{1,0},{2,3},{3,2},{4,5},{5,4},{6,7},{7,6},{8,9},{9,8},{10,11... | collective-permute-start | bytes 884744 | tf_op jit(solution)/shard_map/ppermute | solution.py:146
  18.0 7.5 %collective-permute-start.2 = (bf16[64,1152]{1,0:T(8,128)(2,1)S(1)}, bf16[64,1152]{1,0:T(8,128)(2,1)S(1)}, u32[]{:S(2)}, u32[]{:S(2)}) collective-permute-start(bf16[64,1152]{1,0:T(8,128)(2,1)S(1)} %collective-permute-done.1.a_ref.dep_ref), channel_id=1, source_target_pairs={{0,4},{1,5},{2,6},{3,7},{4,0},{5,1},{6,2},{7,3},{8,12},{9,13},{10,... | collective-permute-start | bytes 442376 | tf_op jit(solution)/shard_map/ppermute | solution.py:146
  19.5 8.0 %collective-permute-start.6 = (bf16[64,1152]{1,0:T(8,128)(2,1)S(1)}, bf16[64,1152]{1,0:T(8,128)(2,1)S(1)}, u32[]{:S(2)}, u32[]{:S(2)}) collective-permute-start(bf16[64,1152]{1,0:T(8,128)(2,1)S(1)} %pack.1.a_ref), channel_id=1, source_target_pairs={{0,4},{1,5},{2,6},{3,7},{4,0},{5,1},{6,2},{7,3},{8,12},{9,13},{10,... | collective-permute-start | bytes 442376 | tf_op jit(solution)/shard_map/ppermute | solution.py:146
  25.5 5.7 %collective-permute-start.3 = (bf16[64,1152]{1,0:T(8,128)(2,1)S(1)}, bf16[64,1152]{1,0:T(8,128)(2,1)S(1)}, u32[]{:S(2)}, u32[]{:S(2)}) collective-permute-start(bf16[64,1152]{1,0:T(8,128)(2,1)S(1)} %collective-permute-done.2.refs_1_.a_ref), channel_id=1, source_target_pairs={{0,2},{1,3},{2,0},{3,1},{4,6},{5,7},{6,4},{7,5},{8,10},{9,11},{10,... | collective-permute-start | bytes 442376 | tf_op jit(solution)/shard_map/ppermute | solution.py:146
  31.3 6.9 %collective-permute-start.7 = (bf16[128,1152]{1,0:T(8,128)(2,1)S(1)}, bf16[128,1152]{1,0:T(8,128)(2,1)S(1)}, u32[]{:S(2)}, u32[]{:S(2)}) collective-permute-start(bf16[128,1152]{1,0:T(8,128)(2,1)S(1)} %join.5.pair_ref), channel_id=1, source_target_pairs={{0,1},{1,0},{2,3},{3,2},{4,5},{5,4},{6,7},{7,6},{8,9},{9,8},{10,11... | collective-permute-start | bytes 884744 | tf_op jit(solution)/shard_map/ppermute | solution.py:146
  31.3 6.7 %collective-permute-start.8 = (bf16[64,1152]{1,0:T(8,128)(2,1)S(1)}, bf16[64,1152]{1,0:T(8,128)(2,1)S(1)}, u32[]{:S(2)}, u32[]{:S(2)}) collective-permute-start(bf16[64,1152]{1,0:T(8,128)(2,1)S(1)} %collective-permute-done.6.refs_0_.a_ref), channel_id=1, source_target_pairs={{0,2},{1,3},{2,0},{3,1},{4,6},{5,7},{6,4},{7,5},{8,10},{9,11},{10,... | collective-permute-start | bytes 442376 | tf_op jit(solution)/shard_map/ppermute | solution.py:146
  33.0 11.2 %collective-permute-start = (bf16[64,1152]{1,0:T(8,128)(2,1)S(1)}, bf16[64,1152]{1,0:T(8,128)(2,1)S(1)}, u32[]{:S(2)}, u32[]{:S(2)}) collective-permute-start(bf16[64,1152]{1,0:T(8,128)(2,1)S(1)} %pack.1.a_ref), channel_id=1, source_target_pairs={{0,2},{1,3},{2,0},{3,1},{4,6},{5,7},{6,4},{7,5},{8,10},{9,11},{10,... | collective-permute-start | bytes 442376 | tf_op jit(solution)/shard_map/ppermute | solution.py:146
  33.4 9.0 %collective-permute-start.11 = (bf16[128,1152]{1,0:T(8,128)(2,1)S(1)}, bf16[128,1152]{1,0:T(8,128)(2,1)S(1)}, u32[]{:S(2)}, u32[]{:S(2)}) collective-permute-start(bf16[128,1152]{1,0:T(8,128)(2,1)S(1)} %get-tuple-element.27.refs_0_), channel_id=1, source_target_pairs={{0,1},{1,0},{2,3},{3,2},{4,5},{5,4},{6,7},{7,6},{8,9},{9,8},{10,11... | collective-permute-start | bytes 884744 | tf_op jit(solution)/shard_map/ppermute | solution.py:146
  38.1 6.2 %collective-permute-start.10 = (bf16[128,1152]{1,0:T(8,128)(2,1)S(1)}, bf16[128,1152]{1,0:T(8,128)(2,1)S(1)}, u32[]{:S(2)}, u32[]{:S(2)}) collective-permute-start(bf16[128,1152]{1,0:T(8,128)(2,1)S(1)} %join.6.refs_1_.pair_ref), channel_id=1, source_target_pairs={{0,1},{1,0},{2,3},{3,2},{4,5},{5,4},{6,7},{7,6},{8,9},{9,8},{10,11... | collective-permute-start | bytes 884744 | tf_op jit(solution)/shard_map/ppermute | solution.py:146
  41.9 6.7 %collective-permute-start.12 = (bf16[128,1152]{1,0:T(8,128)(2,1)S(1)}, bf16[128,1152]{1,0:T(8,128)(2,1)S(1)}, u32[]{:S(2)}, u32[]{:S(2)}) collective-permute-start(bf16[128,1152]{1,0:T(8,128)(2,1)S(1)} %get-tuple-element.28.refs_0_), channel_id=1, source_target_pairs={{0,1},{1,0},{2,3},{3,2},{4,5},{5,4},{6,7},{7,6},{8,9},{9,8},{10,11... | collective-permute-start | bytes 884744 | tf_op jit(solution)/shard_map/ppermute | solution.py:146
  42.5 6.1 %collective-permute-start.13 = (bf16[64,1152]{1,0:T(8,128)(2,1)S(1)}, bf16[64,1152]{1,0:T(8,128)(2,1)S(1)}, u32[]{:S(2)}, u32[]{:S(2)}) collective-permute-start(bf16[64,1152]{1,0:T(8,128)(2,1)S(1)} %get-tuple-element.30.refs_1_), channel_id=1, source_target_pairs={{0,2},{1,3},{2,0},{3,1},{4,6},{5,7},{6,4},{7,5},{8,10},{9,11},{10,... | collective-permute-start | bytes 442376 | tf_op jit(solution)/shard_map/ppermute | solution.py:146
  44.2 4.5 %collective-permute-start.9 = (bf16[128,1152]{1,0:T(8,128)(2,1)S(1)}, bf16[128,1152]{1,0:T(8,128)(2,1)S(1)}, u32[]{:S(2)}, u32[]{:S(2)}) collective-permute-start(bf16[128,1152]{1,0:T(8,128)(2,1)S(1)} %join.7.refs_2_.pair_ref), channel_id=1, source_target_pairs={{0,1},{1,0},{2,3},{3,2},{4,5},{5,4},{6,7},{7,6},{8,9},{9,8},{10,11... | collective-permute-start | bytes 884744 | tf_op jit(solution)/shard_map/ppermute | solution.py:146
  48.0 6.1 %collective-permute-start.16 = (bf16[128,1152]{1,0:T(8,128)(2,1)S(1)}, bf16[128,1152]{1,0:T(8,128)(2,1)S(1)}, u32[]{:S(2)}, u32[]{:S(2)}) collective-permute-start(bf16[128,1152]{1,0:T(8,128)(2,1)S(1)} %get-tuple-element.31.refs_0_), channel_id=1, source_target_pairs={{0,1},{1,0},{2,3},{3,2},{4,5},{5,4},{6,7},{7,6},{8,9},{9,8},{10,11... | collective-permute-start | bytes 884744 | tf_op jit(solution)/shard_map/ppermute | solution.py:146
  52.7 11.1 %collective-permute-start.14 = (bf16[128,1152]{1,0:T(8,128)(2,1)S(1)}, bf16[128,1152]{1,0:T(8,128)(2,1)S(1)}, u32[]{:S(2)}, u32[]{:S(2)}) collective-permute-start(bf16[128,1152]{1,0:T(8,128)(2,1)S(1)} %get-tuple-element.36), channel_id=1, source_target_pairs={{0,1},{1,0},{2,3},{3,2},{4,5},{5,4},{6,7},{7,6},{8,9},{9,8},{10,11... | collective-permute-start | bytes 884744 | tf_op jit(solution)/shard_map/ppermute | solution.py:146
  52.8 6.7 %collective-permute-start.20 = (bf16[64,1152]{1,0:T(8,128)(2,1)S(1)}, bf16[64,1152]{1,0:T(8,128)(2,1)S(1)}, u32[]{:S(2)}, u32[]{:S(2)}) collective-permute-start(bf16[64,1152]{1,0:T(8,128)(2,1)S(1)} %get-tuple-element.33.refs_1_), channel_id=1, source_target_pairs={{0,2},{1,3},{2,0},{3,1},{4,6},{5,7},{6,4},{7,5},{8,10},{9,11},{10,... | collective-permute-start | bytes 442376 | tf_op jit(solution)/shard_map/ppermute | solution.py:146
  54.2 9.5 %collective-permute-start.17 = (bf16[64,1152]{1,0:T(8,128)(2,1)S(1)}, bf16[64,1152]{1,0:T(8,128)(2,1)S(1)}, u32[]{:S(2)}, u32[]{:S(2)}) collective-permute-start(bf16[64,1152]{1,0:T(8,128)(2,1)S(1)} %get-tuple-element.41), channel_id=1, source_target_pairs={{0,2},{1,3},{2,0},{3,1},{4,6},{5,7},{6,4},{7,5},{8,10},{9,11},{10,... | collective-permute-start | bytes 442376 | tf_op jit(solution)/shard_map/ppermute | solution.py:146
  55.0 14.0 %collective-permute-start.19 = (bf16[64,1152]{1,0:T(8,128)(2,1)S(1)}, bf16[64,1152]{1,0:T(8,128)(2,1)S(1)}, u32[]{:S(2)}, u32[]{:S(2)}) collective-permute-start(bf16[64,1152]{1,0:T(8,128)(2,1)S(1)} %add.3.refs_2_), channel_id=1, source_target_pairs={{0,8},{1,9},{2,10},{3,11},{4,12},{5,13},{6,14},{7,15},{8,0},{9,1},... | collective-permute-start | bytes 442376 | tf_op jit(solution)/shard_map/ppermute | solution.py:146
  59.5 9.4 %collective-permute-start.21 = (bf16[64,1152]{1,0:T(8,128)(2,1)S(1)}, bf16[64,1152]{1,0:T(8,128)(2,1)S(1)}, u32[]{:S(2)}, u32[]{:S(2)}) collective-permute-start(bf16[64,1152]{1,0:T(8,128)(2,1)S(1)} %add.5), channel_id=1, source_target_pairs={{0,12},{1,13},{2,14},{3,15},{4,8},{5,9},{6,10},{7,11},{8,4},{9,5},... | collective-permute-start | bytes 442376 | tf_op jit(solution)/shard_map/ppermute | solution.py:146
  63.7 7.6 %collective-permute-start.18 = (bf16[64,1152]{1,0:T(8,128)(2,1)S(1)}, bf16[64,1152]{1,0:T(8,128)(2,1)S(1)}, u32[]{:S(2)}, u32[]{:S(2)}) collective-permute-start(bf16[64,1152]{1,0:T(8,128)(2,1)S(1)} %add.4), channel_id=1, source_target_pairs={{0,4},{1,5},{2,6},{3,7},{4,0},{5,1},{6,2},{7,3},{8,12},{9,13},{10,... | collective-permute-start | bytes 442376 | tf_op jit(solution)/shard_map/ppermute | solution.py:146
  63.9 7.4 %collective-permute-start.15 = (bf16[64,1152]{1,0:T(8,128)(2,1)S(1)}, bf16[64,1152]{1,0:T(8,128)(2,1)S(1)}, u32[]{:S(2)}, u32[]{:S(2)}) collective-permute-start(bf16[64,1152]{1,0:T(8,128)(2,1)S(1)} %get-tuple-element.38), channel_id=1, source_target_pairs={{0,2},{1,3},{2,0},{3,1},{4,6},{5,7},{6,4},{7,5},{8,10},{9,11},{10,... | collective-permute-start | bytes 442376 | tf_op jit(solution)/shard_map/ppermute | solution.py:146
  (1 other events, 0.7 us)

commit v5 on v4

--- a/solution.py
+++ b/solution.py
@@ -1,3 +1,5 @@
+import functools
+
 import jax
 import jax.numpy as jnp
 from jax import lax
@@ -7,6 +9,7 @@
 
 GROUP = 16
 TAIL = 128
+K_COST = 10
 SCALE = 2.0**40
 STEP = 256
 PIECE = 256
@@ -44,48 +47,83 @@
     out_ref[rows:] = b_ref[...]
 
 
-def expert_kernel(first_ref, pair_ref, other_ref, columns_ref, up_ref, down_ref, *refs):
-    keep_ref, send_ref, inner_ref = refs[-3:]
+def expert_kernel(two, first_ref, pair_ref, other_ref, columns_ref, up_ref, down_ref, *refs):
+    inner_ref, result_ref = refs[-2:]
     half, wide = pair_ref.shape
     lat = wide - TAIL
     local, eff, _ = down_ref.shape
+    slots = result_ref.shape[0] // local
     x = jnp.concatenate([pair_ref[:, :lat], other_ref[:, :lat]], axis=0)
     tail = jnp.concatenate([pair_ref[:, lat:], other_ref[:, lat:]], axis=0).astype(jnp.float32)
-    logits = lax.dot_general(
-        x, columns_ref[...], (((1,), (1,)), ((), ())), preferred_element_type=jnp.float32
-    )
-    sums = jnp.zeros((2 * half, 1), jnp.float32)
+
+    outs = refs[-4 - two : -2]
+
+    def put(lanes, value):
+        outs[0][:, lanes] = value[:half]
+        height = half // (1 + two)
+        for i, out in enumerate(outs[1:]):
+            out[:, lanes] = value[half + i * height : half + (i + 1) * height].astype(jnp.bfloat16)
+
+    def logits_of(rows):
+        return lax.dot_general(
+            rows, columns_ref[...], (((1,), (1,)), ((), ())), preferred_element_type=jnp.float32
+        )
+
+    logits = logits_of(x)
+    lane = lax.broadcasted_iota(jnp.int32, (2 * half, TAIL), 1)
+    masks, sums = [], jnp.zeros((2 * half, 1), jnp.float32)
+    marks = jnp.zeros((2 * half, TAIL), jnp.float32)
     for e in range(local):
         label = (first_ref[0] + e).astype(jnp.float32)
         mask = jnp.max(jnp.where(tail == label, 1.0, 0.0), axis=1, keepdims=True)
-        score = jax.nn.sigmoid(logits[:, e : e + 1]) * (mask * SCALE)
-        sums = sums + score
+        sums = sums + jax.nn.sigmoid(logits[:, e : e + 1]) * (mask * SCALE)
+        marks = jnp.where(lane == e, mask, marks)
+        masks.append(mask)
+    row = lax.broadcasted_iota(jnp.int32, (2 * half, 2 * half), 0)
+    col = lax.broadcasted_iota(jnp.int32, (2 * half, 2 * half), 1)
+    before = jnp.where(col < row, 1.0, 0.0).astype(jnp.bfloat16)
+    place = jnp.dot(before, marks.astype(jnp.bfloat16), preferred_element_type=jnp.float32)
+    slot = lax.broadcasted_iota(jnp.int32, (2 * half, slots), 1).astype(jnp.float32)
+    spread = jnp.concatenate(
+        [jnp.where((slot == place[:, e : e + 1]) & (masks[e] > 0.0), 1.0, 0.0) for e in range(local)], axis=1
+    ).astype(jnp.bfloat16)
+    packed = lax.dot_general(
+        spread, x, (((0,), (0,)), ((), ())), preferred_element_type=jnp.float32
+    ).astype(jnp.bfloat16)
+    scores = jax.nn.sigmoid(logits_of(packed)) * SCALE
+    for e in range(local):
+        mine = slice(e * slots, (e + 1) * slots)
+        rows = packed[mine]
+        score = scores[mine, e : e + 1]
         for c in range(0, eff, STEP):
-            gate = jnp.dot(x, up_ref[e, :, c : c + STEP], preferred_element_type=jnp.float32)
-            up = jnp.dot(x, up_ref[e, :, eff + c : eff + c + STEP], preferred_element_type=jnp.float32)
-            inner_ref[:, e * eff + c : e * eff + c + STEP] = (
-                gate / (1.0 + jnp.exp(-gate)) * up * score
-            ).astype(jnp.bfloat16)
-    inner = inner_ref[...]
+            gate = jnp.dot(rows, up_ref[e, :, c : c + STEP], preferred_element_type=jnp.float32)
+            up = jnp.dot(rows, up_ref[e, :, eff + c : eff + c + STEP], preferred_element_type=jnp.float32)
+            inner_ref[mine, c : c + STEP] = (gate / (1.0 + jnp.exp(-gate)) * up * score).astype(jnp.bfloat16)
+    for e in range(local):
+        mine = slice(e * slots, (e + 1) * slots)
+        result_ref[mine, :] = jnp.dot(
+            inner_ref[mine, :], down_ref[e], preferred_element_type=jnp.float32
+        ).astype(jnp.bfloat16)
     for c in range(0, lat, STEP):
-        down = down_ref[:, :, c : c + STEP].reshape(local * eff, STEP)
-        part = jnp.dot(inner, down, preferred_element_type=jnp.float32)
-        keep_ref[:, c : c + STEP] = part[:half]
-        send_ref[:, c : c + STEP] = part[half:].astype(jnp.bfloat16)
-    lane = lax.broadcasted_iota(jnp.int32, (2 * half, TAIL), 1)
-    sums = jnp.where(lane == 0, sums, 0.0)
-    keep_ref[:, lat:] = sums[:half]
-    send_ref[:, lat:] = sums[half:].astype(jnp.bfloat16)
-
-
-def fold_kernel(mine_ref, came_ref, *refs):
+        part = jnp.dot(spread, result_ref[:, c : c + STEP], preferred_element_type=jnp.float32)
+        put(slice(c, c + STEP), part)
+    put(slice(lat, wide), jnp.where(lane == 0, sums, 0.0))
+
+
+def tie_kernel(*refs):
+    pass
+
+
+def fold_kernel(mine_ref, *refs):
     keep_ref, send_ref = refs[-2:]
     rows = keep_ref.shape[0]
-    keep_ref[...] = mine_ref[:rows] + came_ref[:rows].astype(jnp.float32)
-    send_ref[...] = (mine_ref[rows:] + came_ref[rows:].astype(jnp.float32)).astype(jnp.bfloat16)
-
-
-def add_kernel(mine_ref, came_ref, out_ref):
+    came = [refs[0][:rows], refs[0][rows:]] if len(refs) == 3 else [refs[0][...], refs[1][...]]
+    keep_ref[...] = mine_ref[:rows] + came[0].astype(jnp.float32)
+    send_ref[...] = (mine_ref[rows:] + came[1].astype(jnp.float32)).astype(jnp.bfloat16)
+
+
+def add_kernel(mine_ref, came_ref, *refs):
+    out_ref = refs[-1]
     out_ref[...] = (mine_ref[...] + came_ref[...].astype(jnp.float32)).astype(jnp.bfloat16)
 
 
@@ -118,7 +156,11 @@
 ANY = pl.BlockSpec(memory_space=pl.ANY)
 
 
-def call(kernel, outs, args, deps=(), smem=(), hbm=(), scratch=(), cost=None):
+def modelled(us):
+    return pl.CostEstimate(flops=0, bytes_accessed=int(us * 3.69e6), transcendentals=0)
+
+
+def call(kernel, outs, args, deps=(), smem=(), hbm=(), scratch=(), cost=None, aliases=None):
     specs = [pl.BlockSpec(memory_space=pltpu.SMEM)] * len(smem) + [VMEM] * len(args)
     specs += [ANY] * (len(hbm) + len(deps))
     operands = list(smem) + [in_vmem(a) for a in args] + [in_hbm(h) for h in hbm] + [in_vmem(d) for d in deps]
@@ -129,8 +171,9 @@
         out_specs=[VMEM] * len(outs),
         scratch_shapes=list(scratch),
         compiler_params=pltpu.CompilerParams(vmem_limit_bytes=16 * 1024 * 1024),
-        cost_estimate=cost or pl.CostEstimate(flops=0, bytes_accessed=200_000, transcendentals=0),
-        name=kernel.__name__.removesuffix("_kernel"),
+        cost_estimate=cost or modelled(0.1),
+        input_output_aliases=aliases or {},
+        name=getattr(kernel, "func", kernel).__name__.removesuffix("_kernel"),
     )(*operands)
 
 
@@ -149,7 +192,6 @@
         return pltpu.VMEM((height, wide), dtype)
 
     def weights(dep):
-        moved = gate_up.size + expert_down.size
         return call(
             load_kernel,
             [
@@ -161,36 +203,44 @@
             deps=[dep],
             hbm=[gate_up, expert_down],
             scratch=[pltpu.SemaphoreType.DMA((local * (lat + eff) // PIECE,))],
-            cost=pl.CostEstimate(flops=0, bytes_accessed=4 * moved, transcendentals=0),
+            cost=modelled(5),
         )
 
     def join(a, b, deps=()):
         return call(join_kernel, [space(2 * rows, jnp.bfloat16)], [a, b], deps)[0]
 
-    def experts(pair, other, loaded, deps=()):
+    bound = 2 * ((rows * routes.shape[1] + local * n_dev - 1) // (local * n_dev))
+    slots = 4 * bound
+
+    def experts(pair, other, loaded, deps=(), two=0):
         return call(
-            expert_kernel,
-            [space(2 * rows, jnp.float32), space(2 * rows, jnp.bfloat16)],
+            functools.partial(expert_kernel, two),
+            [space(2 * rows, jnp.float32)] + [space(2 * rows // (1 + two), jnp.bfloat16)] * (1 + two),
             [pair, other, *loaded],
             deps,
             smem=[first],
-            scratch=[pltpu.VMEM((4 * rows, local * eff), jnp.bfloat16)],
-            cost=pl.CostEstimate(
-                flops=2 * 4 * rows * local * eff * lat * 3, bytes_accessed=0, transcendentals=0
-            ),
+            scratch=[
+                pltpu.VMEM((local * slots, eff), jnp.bfloat16),
+                pltpu.VMEM((local * slots, lat), jnp.bfloat16),
+            ],
+            cost=modelled(K_COST),
         )
 
-    def fold(mine, came, deps=()):
-        return call(fold_kernel, [space(rows, jnp.float32), space(rows, jnp.bfloat16)], [mine, came], deps)
-
-    def add(mine, came):
-        return call(add_kernel, [space(rows, jnp.bfloat16)], [mine, came])[0]
+    def tie(x, deps):
+        return call(tie_kernel, [space(x.shape[0], x.dtype)], [x], deps, aliases={0: 0})[0]
+
+    def fold(mine, *came):
+        return call(fold_kernel, [space(rows, jnp.float32), space(rows, jnp.bfloat16)], [mine, *came])
+
+    def add(mine, came, deps=(), cost=None):
+        return call(add_kernel, [space(rows, jnp.bfloat16)], [mine, came], deps, cost=cost)[0]
 
     def group_pass(mine):
-        block = {0: mine, 2: swap(mine, 8), 1: swap(mine, 4)}
+        loaded = weights(mine)
+        z_2, z_1 = swap(mine, 8), swap(mine, 4)
+        block = {0: mine, 2: tie(z_2, [loaded[0]]), 1: z_1}
         block[3] = swap(block[2], 4)
         other = {k: swap(block[k], 2) for k in (2, 1, 3, 0)}
-        loaded = weights(block[2])
         pair, far = {}, {}
         keep, send, came, fold_keep, fold_send, y_came, z_send = {}, {}, {}, {}, {}, {}, {}
 
@@ -198,31 +248,31 @@
             pair[k] = join(block[k], other[k], deps)
             far[k] = swap(pair[k], 1)
 
-        def compute(k, deps=()):
-            keep[k], send[k] = experts(pair[k], far[k], loaded, deps)
-            came[k] = swap(send[k], 1)
+        def compute(k, deps=(), two=0):
+            keep[k], send[k], *more = experts(pair[k], far[k], loaded, deps, two)
+            came[k] = [swap(part, 1) for part in (send[k], *more)]
 
         def reduce_core(k):
-            fold_keep[k], fold_send[k] = fold(keep[k], came[k])
+            fold_keep[k], fold_send[k] = fold(keep[k], *came[k])
             y_came[k] = swap(fold_send[k], 2)
 
-        def reduce_y(k):
-            z_send[k] = add(fold_keep[k], y_came[k])
+        def reduce_y(k, deps=(), cost=None):
+            z_send[k] = add(fold_keep[k], y_came[k], deps, cost)
             return swap(z_send[k], 4 * k)
 
-        gather(2)
-        compute(2, [block[1], block[3]])
+        gather(2, [block[1], block[3]])
+        compute(2)
         gather(3, [send[2]])
-        gather(1, [send[2]])
+        gather(1)
         compute(3, [send[2], pair[1]])
         gather(0, [send[3]])
         reduce_core(2)
-        compute(1, [send[3], fold_send[2], pair[0]])
+        compute(1, [send[3], fold_send[2], pair[0]], two=1)
         reduce_core(3)
         z_2 = reduce_y(2)
-        compute(0, [send[1], fold_send[3], z_send[2]])
+        compute(0, [send[1], fold_send[3], z_send[2]], two=1)
         reduce_core(1)
-        z_3 = reduce_y(3)
+        z_3 = reduce_y(3, [z_2], modelled(K_COST))
         z_1 = reduce_y(1)
         reduce_core(0)
         return fold_keep[0], y_came[0], z_1, z_2, z_3

time: 72.3 us -> 66.7 us (0.923)
  waiting for transfers between devices: 23.1 us -> 11.6 us
  local copies, waits for them, and re-layouts: 2.28 us -> 13.1 us
  Pallas kernels: 21.1 us -> 17.7 us
  starting transfers between devices: 25.3 us -> 23.8 us
    ppermute x22 -> x24, waiting for transfers between devices: 23.1 us -> 11.6 us  [swap(): return lax.ppermute(x, 'exp', [(i, i ^ bits) for i in range(n_dev)])]
    unnamed x6 -> x16, local copies, waits for them, and re-layouts: 2.28 us -> 13.1 us
    pallas_call x17 -> x18, Pallas kernels: 20.3 us -> 17 us  [call(): pl.pallas_call(kernel, out_shape=outs, in_specs=specs, out_specs=[VMEM] *...]
    ppermute x22 -> x24, starting transfers between devices: 25.3 us -> 23.8 us  [swap(): return lax.ppermute(x, 'exp', [(i, i ^ bits) for i in range(n_dev)])]
  transfers between devices with their start and end apart: 22 -> 24, of which waited for: 7 -> 7; matrix products, arithmetic and copies ran while one was open for 0% -> 0% of each run, Pallas kernels for 28% -> 25%
where the time goes in v5:
time: 66.7 us; the launch traced here: 66.5 us
  starting transfers between devices  23.8 us (36%)
  Pallas kernels  17.7 us (27%)
  local copies, waits for them, and re-layouts  13.1 us (20%)
  waiting for transfers between devices  11.6 us (17%)
    ppermute x24, starting transfers between devices, swap(): return lax.ppermute(x, 'exp', [(i, i ^ bits) for i in range(n_dev)])  23.8 us
    pallas_call x18, Pallas kernels, call(): pl.pallas_call(kernel, out_shape=outs, in_specs=specs, out_specs=[VMEM] *...  17 us
    unnamed x16, local copies, waits for them, and re-layouts  13.1 us
    ppermute x24, waiting for transfers between devices, swap(): return lax.ppermute(x, 'exp', [(i, i ^ bits) for i in range(n_dev)])  11.6 us
  transfers between devices with their start and end apart: 24, of which 7 were waited for; matrix products, arithmetic and copies ran while one was open for 0% of the time, Pallas kernels for 25%

profile of v5, /device:TPU:0, one launch (start us, length us, event | category | flops | bytes accessed | tf_op | source)
XLA Modules:
  0.0 66.5 jit_solution(7145519041117452065)
XLA Ops:
  1.7 4.1 %collective-permute-start.1 = (bf16[64,1152]{1,0:T(8,128)(2,1)S(1)}, bf16[64,1152]{1,0:T(8,128)(2,1)S(1)}, u32[]{:S(2)}, u32[]{:S(2)}) collective-permute-start(bf16[64,1152]{1,0:T(8,128)(2,1)S(1)} %pack.1.dep_ref.a_ref), channel_id=1, source_target_pairs={{0,8},{1,9},{2,10},{3,11},{4,12},{5,13},{6,14},{7,15},{8,0},{9,1},... | collective-permute-start | bytes 442376 | tf_op jit(solution)/shard_map/ppermute | solution.py:189
  5.8 1.6 %collective-permute-start.5 = (bf16[64,1152]{1,0:T(8,128)(2,1)S(1)}, bf16[64,1152]{1,0:T(8,128)(2,1)S(1)}, u32[]{:S(2)}, u32[]{:S(2)}) collective-permute-start(bf16[64,1152]{1,0:T(8,128)(2,1)S(1)} %pack.1.dep_ref.a_ref), channel_id=1, source_target_pairs={{0,4},{1,5},{2,6},{3,7},{4,0},{5,1},{6,2},{7,3},{8,12},{9,13},{10,... | collective-permute-start | bytes 442376 | tf_op jit(solution)/shard_map/ppermute | solution.py:189
  8.0 4.7 %load.1 = (bf16[16,1024]{1,0:T(8,128)(2,1)S(1)}, bf16[2,1024,2048]{2,1,0:T(8,128)(2,1)S(1)}, bf16[2,1024,1024]{2,1,0:T(8,128)(2,1)S(1)}) custom-call(bf16[2,1024]{1,0:T(2,128)(2,1)S(1)} %bitcast.4, bf16[2,1024,2048]{2,1,0:T(8,128)(2,1)} %up_hbm.1, bf16[2,1024,1024]{2,1,0:T(8,128)(2,1)} %down_hbm.1, bf16[64,1152]{1,0:T(8,128)(2,1)S(1)} %pack.1.dep_ref.a_ref), custom_call_target="tpu_custom_call" | custom-call | bytes 18450000 | tf_op jit(solution)/shard_map/load/pallas_call | solution.py:167
  12.8 3.3 %copy-done = bf16[2,1024,2048]{2,1,0:T(8,128)(2,1)} copy-done((bf16[2,1024,2048]{2,1,0:T(8,128)(2,1)}, bf16[2,1024,2048]{2,1,0:T(8,128)(2,1)S(1)}, u32[]{:S(2)}) %copy-start) | copy-done | bytes 8388632
  16.0 2.0 %copy-done.3 = bf16[2,1024,1024]{2,1,0:T(8,128)(2,1)} copy-done((bf16[2,1024,1024]{2,1,0:T(8,128)(2,1)}, bf16[2,1024,1024]{2,1,0:T(8,128)(2,1)S(1)}, u32[]{:S(2)}) %copy-start.3) | copy-done | bytes 4194328
  18.5 1.5 %collective-permute-start.4 = (bf16[64,1152]{1,0:T(8,128)(2,1)S(1)}, bf16[64,1152]{1,0:T(8,128)(2,1)S(1)}, u32[]{:S(2)}, u32[]{:S(2)}) collective-permute-start(bf16[64,1152]{1,0:T(8,128)(2,1)S(1)} %tie.1.a_ref), channel_id=1, source_target_pairs={{0,2},{1,3},{2,0},{3,1},{4,6},{5,7},{6,4},{7,5},{8,10},{9,11},{10,... | collective-permute-start | bytes 442376 | tf_op jit(solution)/shard_map/ppermute | solution.py:189
  20.0 3.2 %collective-permute-done.2.refs_1_.a_ref = bf16[64,1152]{1,0:T(8,128)(2,1)S(1)} collective-permute-done((bf16[64,1152]{1,0:T(8,128)(2,1)S(1)}, bf16[64,1152]{1,0:T(8,128)(2,1)S(1)}, u32[]{:S(2)}, u32[]{:S(2)}) %collective-permute-start.2) | collective-permute-done | bytes 147488 | tf_op jit(solution)/shard_map/ppermute | solution.py:189
  23.8 1.6 %collective-permute-start.3 = (bf16[64,1152]{1,0:T(8,128)(2,1)S(1)}, bf16[64,1152]{1,0:T(8,128)(2,1)S(1)}, u32[]{:S(2)}, u32[]{:S(2)}) collective-permute-start(bf16[64,1152]{1,0:T(8,128)(2,1)S(1)} %collective-permute-done.2.refs_1_.a_ref), channel_id=1, source_target_pairs={{0,2},{1,3},{2,0},{3,1},{4,6},{5,7},{6,4},{7,5},{8,10},{9,11},{10,... | collective-permute-start | bytes 442376 | tf_op jit(solution)/shard_map/ppermute | solution.py:189
  25.9 3.4 %copy-done.1 = bf16[2,1024,2048]{2,1,0:T(8,128)(2,1)S(1)} copy-done((bf16[2,1024,2048]{2,1,0:T(8,128)(2,1)S(1)}, bf16[2,1024,2048]{2,1,0:T(8,128)(2,1)}, u32[]{:S(2)}) %copy-start.1) | copy-done | bytes 8388632
  29.2 2.2 %copy-done.4 = bf16[2,1024,1024]{2,1,0:T(8,128)(2,1)S(1)} copy-done((bf16[2,1024,1024]{2,1,0:T(8,128)(2,1)S(1)}, bf16[2,1024,1024]{2,1,0:T(8,128)(2,1)}, u32[]{:S(2)}) %copy-start.4) | copy-done | bytes 4194328
  31.4 2.9 %expert.4 = (f32[128,1152]{1,0:T(8,128)S(1)}, bf16[128,1152]{1,0:T(8,128)(2,1)S(1)}) custom-call(s32[1]{0:T(128)} %bitcast.first_ref, bf16[128,1152]{1,0:T(8,128)(2,1)S(1)} %join.4.pair_ref, bf16[128,1152]{1,0:T(8,128)(2,1)S(1)} %collective-permute-done.6.other_ref, bf16[16,1024]{1,0:T(8,128)(2,1)S(1)} %get-tuple-element.26.refs_1_.columns_ref, ...), custom_call_target="tpu_custom_call" | custom-call | bytes 36900000 | tf_op jit(solution)/shard_map/expert/pallas_call | solution.py:167
  35.1 1.5 %collective-permute-start = (bf16[64,1152]{1,0:T(8,128)(2,1)S(1)}, bf16[64,1152]{1,0:T(8,128)(2,1)S(1)}, u32[]{:S(2)}, u32[]{:S(2)}) collective-permute-start(bf16[64,1152]{1,0:T(8,128)(2,1)S(1)} %pack.1.dep_ref.a_ref), channel_id=1, source_target_pairs={{0,2},{1,3},{2,0},{3,1},{4,6},{5,7},{6,4},{7,5},{8,10},{9,11},{10,... | collective-permute-start | bytes 442376 | tf_op jit(solution)/shard_map/ppermute | solution.py:189
  36.7 3.0 %expert.5 = (f32[128,1152]{1,0:T(8,128)S(1)}, bf16[128,1152]{1,0:T(8,128)(2,1)S(1)}) custom-call(s32[1]{0:T(128)} %bitcast.first_ref, bf16[128,1152]{1,0:T(8,128)(2,1)S(1)} %join.5.pair_ref, bf16[128,1152]{1,0:T(8,128)(2,1)S(1)} %collective-permute-done.7.other_ref, bf16[16,1024]{1,0:T(8,128)(2,1)S(1)} %get-tuple-element.26.refs_1_.columns_ref, ...), custom_call_target="tpu_custom_call" | custom-call | bytes 36900000 | tf_op jit(solution)/shard_map/expert/pallas_call | solution.py:167
  39.9 1.5 %collective-permute-done.b_ref = bf16[64,1152]{1,0:T(8,128)(2,1)S(1)} collective-permute-done((bf16[64,1152]{1,0:T(8,128)(2,1)S(1)}, bf16[64,1152]{1,0:T(8,128)(2,1)S(1)}, u32[]{:S(2)}, u32[]{:S(2)}) %collective-permute-start) | collective-permute-done | bytes 147488 | tf_op jit(solution)/shard_map/ppermute | solution.py:189
  41.5 1.6 %collective-permute-start.13 = (bf16[64,1152]{1,0:T(8,128)(2,1)S(1)}, bf16[64,1152]{1,0:T(8,128)(2,1)S(1)}, u32[]{:S(2)}, u32[]{:S(2)}) collective-permute-start(bf16[64,1152]{1,0:T(8,128)(2,1)S(1)} %get-tuple-element.32.refs_1_), channel_id=1, source_target_pairs={{0,2},{1,3},{2,0},{3,1},{4,6},{5,7},{6,4},{7,5},{8,10},{9,11},{10,... | collective-permute-start | bytes 442376 | tf_op jit(solution)/shard_map/ppermute | solution.py:189
  43.1 3.0 %expert.6 = (f32[128,1152]{1,0:T(8,128)S(1)}, bf16[64,1152]{1,0:T(8,128)(2,1)S(1)}, bf16[64,1152]{1,0:T(8,128)(2,1)S(1)}) custom-call(s32[1]{0:T(128)} %bitcast.first_ref, bf16[128,1152]{1,0:T(8,128)(2,1)S(1)} %join.6.refs_1_.pair_ref, bf16[128,1152]{1,0:T(8,128)(2,1)S(1)} %collective-permute-done.10.other_ref, ...), custom_call_target="tpu_custom_call" | custom-call | bytes 36900000 | tf_op jit(solution)/shard_map/expert/pallas_call | solution.py:167
  46.6 1.2 %collective-permute-done.13.came_ref = bf16[64,1152]{1,0:T(8,128)(2,1)S(1)} collective-permute-done((bf16[64,1152]{1,0:T(8,128)(2,1)S(1)}, bf16[64,1152]{1,0:T(8,128)(2,1)S(1)}, u32[]{:S(2)}, u32[]{:S(2)}) %collective-permute-start.13) | collective-permute-done | bytes 147488 | tf_op jit(solution)/shard_map/ppermute | solution.py:189
  48.1 1.8 %collective-permute-start.19 = (bf16[64,1152]{1,0:T(8,128)(2,1)S(1)}, bf16[64,1152]{1,0:T(8,128)(2,1)S(1)}, u32[]{:S(2)}, u32[]{:S(2)}) collective-permute-start(bf16[64,1152]{1,0:T(8,128)(2,1)S(1)} %get-tuple-element.45), channel_id=1, source_target_pairs={{0,2},{1,3},{2,0},{3,1},{4,6},{5,7},{6,4},{7,5},{8,10},{9,11},{10,... | collective-permute-start | bytes 442376 | tf_op jit(solution)/shard_map/ppermute | solution.py:189
  50.3 3.0 %expert.7 = (f32[128,1152]{1,0:T(8,128)S(1)}, bf16[64,1152]{1,0:T(8,128)(2,1)S(1)}, bf16[64,1152]{1,0:T(8,128)(2,1)S(1)}) custom-call(s32[1]{0:T(128)} %bitcast.first_ref, bf16[128,1152]{1,0:T(8,128)(2,1)S(1)} %join.7.refs_2_.pair_ref, bf16[128,1152]{1,0:T(8,128)(2,1)S(1)} %collective-permute-done.9.other_ref, ...), custom_call_target="tpu_custom_call" | custom-call | bytes 36900000 | tf_op jit(solution)/shard_map/expert/pallas_call | solution.py:167
  53.9 1.0 %collective-permute-done.19.came_ref = bf16[64,1152]{1,0:T(8,128)(2,1)S(1)} collective-permute-done((bf16[64,1152]{1,0:T(8,128)(2,1)S(1)}, bf16[64,1152]{1,0:T(8,128)(2,1)S(1)}, u32[]{:S(2)}, u32[]{:S(2)}) %collective-permute-start.19) | collective-permute-done | bytes 147488 | tf_op jit(solution)/shard_map/ppermute | solution.py:189
  54.9 1.9 %collective-permute-start.20 = (bf16[64,1152]{1,0:T(8,128)(2,1)S(1)}, bf16[64,1152]{1,0:T(8,128)(2,1)S(1)}, u32[]{:S(2)}, u32[]{:S(2)}) collective-permute-start(bf16[64,1152]{1,0:T(8,128)(2,1)S(1)} %add.4), channel_id=1, source_target_pairs={{0,4},{1,5},{2,6},{3,7},{4,0},{5,1},{6,2},{7,3},{8,12},{9,13},{10,... | collective-permute-start | bytes 442376 | tf_op jit(solution)/shard_map/ppermute | solution.py:189
  57.5 2.9 %collective-permute-start.23 = (bf16[64,1152]{1,0:T(8,128)(2,1)S(1)}, bf16[64,1152]{1,0:T(8,128)(2,1)S(1)}, u32[]{:S(2)}, u32[]{:S(2)}) collective-permute-start(bf16[64,1152]{1,0:T(8,128)(2,1)S(1)} %add.5), channel_id=1, source_target_pairs={{0,12},{1,13},{2,14},{3,15},{4,8},{5,9},{6,10},{7,11},{8,4},{9,5},... | collective-permute-start | bytes 442376 | tf_op jit(solution)/shard_map/ppermute | solution.py:189
  60.5 1.6 %collective-permute-start.16 = (bf16[64,1152]{1,0:T(8,128)(2,1)S(1)}, bf16[64,1152]{1,0:T(8,128)(2,1)S(1)}, u32[]{:S(2)}, u32[]{:S(2)}) collective-permute-start(bf16[64,1152]{1,0:T(8,128)(2,1)S(1)} %get-tuple-element.41), channel_id=1, source_target_pairs={{0,2},{1,3},{2,0},{3,1},{4,6},{5,7},{6,4},{7,5},{8,10},{9,11},{10,... | collective-permute-start | bytes 442376 | tf_op jit(solution)/shard_map/ppermute | solution.py:189
  62.1 3.6 %collective-permute-done.23.refs_4_ = bf16[64,1152]{1,0:T(8,128)(2,1)S(1)} collective-permute-done((bf16[64,1152]{1,0:T(8,128)(2,1)S(1)}, bf16[64,1152]{1,0:T(8,128)(2,1)S(1)}, u32[]{:S(2)}, u32[]{:S(2)}) %collective-permute-start.23) | collective-permute-done | bytes 147488 | tf_op jit(solution)/shard_map/ppermute | solution.py:189
  (59 shorter events, 8.5 us)
Async XLA Ops:
  1.7 16.4 %collective-permute-start.1 = (bf16[64,1152]{1,0:T(8,128)(2,1)S(1)}, bf16[64,1152]{1,0:T(8,128)(2,1)S(1)}, u32[]{:S(2)}, u32[]{:S(2)}) collective-permute-start(bf16[64,1152]{1,0:T(8,128)(2,1)S(1)} %pack.1.dep_ref.a_ref), channel_id=1, source_target_pairs={{0,8},{1,9},{2,10},{3,11},{4,12},{5,13},{6,14},{7,15},{8,0},{9,1},... | collective-permute-start | bytes 442376 | tf_op jit(solution)/shard_map/ppermute | solution.py:189
  5.8 14.2 %collective-permute-start.5 = (bf16[64,1152]{1,0:T(8,128)(2,1)S(1)}, bf16[64,1152]{1,0:T(8,128)(2,1)S(1)}, u32[]{:S(2)}, u32[]{:S(2)}) collective-permute-start(bf16[64,1152]{1,0:T(8,128)(2,1)S(1)} %pack.1.dep_ref.a_ref), channel_id=1, source_target_pairs={{0,4},{1,5},{2,6},{3,7},{4,0},{5,1},{6,2},{7,3},{8,12},{9,13},{10,... | collective-permute-start | bytes 442376 | tf_op jit(solution)/shard_map/ppermute | solution.py:189
  18.1 5.1 %collective-permute-start.2 = (bf16[64,1152]{1,0:T(8,128)(2,1)S(1)}, bf16[64,1152]{1,0:T(8,128)(2,1)S(1)}, u32[]{:S(2)}, u32[]{:S(2)}) collective-permute-start(bf16[64,1152]{1,0:T(8,128)(2,1)S(1)} %tie.1.a_ref), channel_id=1, source_target_pairs={{0,4},{1,5},{2,6},{3,7},{4,0},{5,1},{6,2},{7,3},{8,12},{9,13},{10,... | collective-permute-start | bytes 442376 | tf_op jit(solution)/shard_map/ppermute | solution.py:189
  18.5 5.1 %collective-permute-start.4 = (bf16[64,1152]{1,0:T(8,128)(2,1)S(1)}, bf16[64,1152]{1,0:T(8,128)(2,1)S(1)}, u32[]{:S(2)}, u32[]{:S(2)}) collective-permute-start(bf16[64,1152]{1,0:T(8,128)(2,1)S(1)} %tie.1.a_ref), channel_id=1, source_target_pairs={{0,2},{1,3},{2,0},{3,1},{4,6},{5,7},{6,4},{7,5},{8,10},{9,11},{10,... | collective-permute-start | bytes 442376 | tf_op jit(solution)/shard_map/ppermute | solution.py:189
  23.7 2.2 %collective-permute-start.6 = (bf16[128,1152]{1,0:T(8,128)(2,1)S(1)}, bf16[128,1152]{1,0:T(8,128)(2,1)S(1)}, u32[]{:S(2)}, u32[]{:S(2)}) collective-permute-start(bf16[128,1152]{1,0:T(8,128)(2,1)S(1)} %join.4.pair_ref), channel_id=1, source_target_pairs={{0,1},{1,0},{2,3},{3,2},{4,5},{5,4},{6,7},{7,6},{8,9},{9,8},{10,11... | collective-permute-start | bytes 884744 | tf_op jit(solution)/shard_map/ppermute | solution.py:189
  23.8 10.6 %collective-permute-start.3 = (bf16[64,1152]{1,0:T(8,128)(2,1)S(1)}, bf16[64,1152]{1,0:T(8,128)(2,1)S(1)}, u32[]{:S(2)}, u32[]{:S(2)}) collective-permute-start(bf16[64,1152]{1,0:T(8,128)(2,1)S(1)} %collective-permute-done.2.refs_1_.a_ref), channel_id=1, source_target_pairs={{0,2},{1,3},{2,0},{3,1},{4,6},{5,7},{6,4},{7,5},{8,10},{9,11},{10,... | collective-permute-start | bytes 442376 | tf_op jit(solution)/shard_map/ppermute | solution.py:189
  25.3 9.6 %collective-permute-start.8 = (bf16[64,1152]{1,0:T(8,128)(2,1)S(1)}, bf16[64,1152]{1,0:T(8,128)(2,1)S(1)}, u32[]{:S(2)}, u32[]{:S(2)}) collective-permute-start(bf16[64,1152]{1,0:T(8,128)(2,1)S(1)} %collective-permute-done.5.refs_0_.a_ref), channel_id=1, source_target_pairs={{0,2},{1,3},{2,0},{3,1},{4,6},{5,7},{6,4},{7,5},{8,10},{9,11},{10,... | collective-permute-start | bytes 442376 | tf_op jit(solution)/shard_map/ppermute | solution.py:189
  34.4 2.3 %collective-permute-start.7 = (bf16[128,1152]{1,0:T(8,128)(2,1)S(1)}, bf16[128,1152]{1,0:T(8,128)(2,1)S(1)}, u32[]{:S(2)}, u32[]{:S(2)}) collective-permute-start(bf16[128,1152]{1,0:T(8,128)(2,1)S(1)} %join.5.pair_ref), channel_id=1, source_target_pairs={{0,1},{1,0},{2,3},{3,2},{4,5},{5,4},{6,7},{7,6},{8,9},{9,8},{10,11... | collective-permute-start | bytes 884744 | tf_op jit(solution)/shard_map/ppermute | solution.py:189
  34.5 7.0 %collective-permute-start.11 = (bf16[128,1152]{1,0:T(8,128)(2,1)S(1)}, bf16[128,1152]{1,0:T(8,128)(2,1)S(1)}, u32[]{:S(2)}, u32[]{:S(2)}) collective-permute-start(bf16[128,1152]{1,0:T(8,128)(2,1)S(1)} %get-tuple-element.29.refs_0_), channel_id=1, source_target_pairs={{0,1},{1,0},{2,3},{3,2},{4,5},{5,4},{6,7},{7,6},{8,9},{9,8},{10,11... | collective-permute-start | bytes 884744 | tf_op jit(solution)/shard_map/ppermute | solution.py:189
  35.0 8.1 %collective-permute-start.10 = (bf16[128,1152]{1,0:T(8,128)(2,1)S(1)}, bf16[128,1152]{1,0:T(8,128)(2,1)S(1)}, u32[]{:S(2)}, u32[]{:S(2)}) collective-permute-start(bf16[128,1152]{1,0:T(8,128)(2,1)S(1)} %join.6.refs_1_.pair_ref), channel_id=1, source_target_pairs={{0,1},{1,0},{2,3},{3,2},{4,5},{5,4},{6,7},{7,6},{8,9},{9,8},{10,11... | collective-permute-start | bytes 884744 | tf_op jit(solution)/shard_map/ppermute | solution.py:189
  35.1 6.2 %collective-permute-start = (bf16[64,1152]{1,0:T(8,128)(2,1)S(1)}, bf16[64,1152]{1,0:T(8,128)(2,1)S(1)}, u32[]{:S(2)}, u32[]{:S(2)}) collective-permute-start(bf16[64,1152]{1,0:T(8,128)(2,1)S(1)} %pack.1.dep_ref.a_ref), channel_id=1, source_target_pairs={{0,2},{1,3},{2,0},{3,1},{4,6},{5,7},{6,4},{7,5},{8,10},{9,11},{10,... | collective-permute-start | bytes 442376 | tf_op jit(solution)/shard_map/ppermute | solution.py:189
  39.6 10.3 %collective-permute-start.12 = (bf16[128,1152]{1,0:T(8,128)(2,1)S(1)}, bf16[128,1152]{1,0:T(8,128)(2,1)S(1)}, u32[]{:S(2)}, u32[]{:S(2)}) collective-permute-start(bf16[128,1152]{1,0:T(8,128)(2,1)S(1)} %get-tuple-element.30.refs_0_), channel_id=1, source_target_pairs={{0,1},{1,0},{2,3},{3,2},{4,5},{5,4},{6,7},{7,6},{8,9},{9,8},{10,11... | collective-permute-start | bytes 884744 | tf_op jit(solution)/shard_map/ppermute | solution.py:189
  41.4 9.0 %collective-permute-start.9 = (bf16[128,1152]{1,0:T(8,128)(2,1)S(1)}, bf16[128,1152]{1,0:T(8,128)(2,1)S(1)}, u32[]{:S(2)}, u32[]{:S(2)}) collective-permute-start(bf16[128,1152]{1,0:T(8,128)(2,1)S(1)} %join.7.refs_2_.pair_ref), channel_id=1, source_target_pairs={{0,1},{1,0},{2,3},{3,2},{4,5},{5,4},{6,7},{7,6},{8,9},{9,8},{10,11... | collective-permute-start | bytes 884744 | tf_op jit(solution)/shard_map/ppermute | solution.py:189
  41.5 6.3 %collective-permute-start.13 = (bf16[64,1152]{1,0:T(8,128)(2,1)S(1)}, bf16[64,1152]{1,0:T(8,128)(2,1)S(1)}, u32[]{:S(2)}, u32[]{:S(2)}) collective-permute-start(bf16[64,1152]{1,0:T(8,128)(2,1)S(1)} %get-tuple-element.32.refs_1_), channel_id=1, source_target_pairs={{0,2},{1,3},{2,0},{3,1},{4,6},{5,7},{6,4},{7,5},{8,10},{9,11},{10,... | collective-permute-start | bytes 442376 | tf_op jit(solution)/shard_map/ppermute | solution.py:189
  46.1 2.0 %collective-permute-start.17 = (bf16[64,1152]{1,0:T(8,128)(2,1)S(1)}, bf16[64,1152]{1,0:T(8,128)(2,1)S(1)}, u32[]{:S(2)}, u32[]{:S(2)}) collective-permute-start(bf16[64,1152]{1,0:T(8,128)(2,1)S(1)} %get-tuple-element.33.refs_0_), channel_id=1, source_target_pairs={{0,1},{1,0},{2,3},{3,2},{4,5},{5,4},{6,7},{7,6},{8,9},{9,8},{10,11... | collective-permute-start | bytes 442376 | tf_op jit(solution)/shard_map/ppermute | solution.py:189
  46.3 1.7 %collective-permute-start.18 = (bf16[64,1152]{1,0:T(8,128)(2,1)S(1)}, bf16[64,1152]{1,0:T(8,128)(2,1)S(1)}, u32[]{:S(2)}, u32[]{:S(2)}) collective-permute-start(bf16[64,1152]{1,0:T(8,128)(2,1)S(1)} %get-tuple-element.43), channel_id=1, source_target_pairs={{0,1},{1,0},{2,3},{3,2},{4,5},{5,4},{6,7},{7,6},{8,9},{9,8},{10,11... | collective-permute-start | bytes 442376 | tf_op jit(solution)/shard_map/ppermute | solution.py:189
  47.8 9.7 %collective-permute-start.21 = (bf16[64,1152]{1,0:T(8,128)(2,1)S(1)}, bf16[64,1152]{1,0:T(8,128)(2,1)S(1)}, u32[]{:S(2)}, u32[]{:S(2)}) collective-permute-start(bf16[64,1152]{1,0:T(8,128)(2,1)S(1)} %add.3.refs_2_), channel_id=1, source_target_pairs={{0,8},{1,9},{2,10},{3,11},{4,12},{5,13},{6,14},{7,15},{8,0},{9,1},... | collective-permute-start | bytes 442376 | tf_op jit(solution)/shard_map/ppermute | solution.py:189
  48.1 6.8 %collective-permute-start.19 = (bf16[64,1152]{1,0:T(8,128)(2,1)S(1)}, bf16[64,1152]{1,0:T(8,128)(2,1)S(1)}, u32[]{:S(2)}, u32[]{:S(2)}) collective-permute-start(bf16[64,1152]{1,0:T(8,128)(2,1)S(1)} %get-tuple-element.45), channel_id=1, source_target_pairs={{0,2},{1,3},{2,0},{3,1},{4,6},{5,7},{6,4},{7,5},{8,10},{9,11},{10,... | collective-permute-start | bytes 442376 | tf_op jit(solution)/shard_map/ppermute | solution.py:189
  50.0 7.5 %collective-permute-start.22 = (bf16[64,1152]{1,0:T(8,128)(2,1)S(1)}, bf16[64,1152]{1,0:T(8,128)(2,1)S(1)}, u32[]{:S(2)}, u32[]{:S(2)}) collective-permute-start(bf16[64,1152]{1,0:T(8,128)(2,1)S(1)} %get-tuple-element.35.refs_1_), channel_id=1, source_target_pairs={{0,2},{1,3},{2,0},{3,1},{4,6},{5,7},{6,4},{7,5},{8,10},{9,11},{10,... | collective-permute-start | bytes 442376 | tf_op jit(solution)/shard_map/ppermute | solution.py:189
  53.3 7.1 %collective-permute-start.14 = (bf16[64,1152]{1,0:T(8,128)(2,1)S(1)}, bf16[64,1152]{1,0:T(8,128)(2,1)S(1)}, u32[]{:S(2)}, u32[]{:S(2)}) collective-permute-start(bf16[64,1152]{1,0:T(8,128)(2,1)S(1)} %get-tuple-element.38), channel_id=1, source_target_pairs={{0,1},{1,0},{2,3},{3,2},{4,5},{5,4},{6,7},{7,6},{8,9},{9,8},{10,11... | collective-permute-start | bytes 442376 | tf_op jit(solution)/shard_map/ppermute | solution.py:189
  53.4 7.1 %collective-permute-start.15 = (bf16[64,1152]{1,0:T(8,128)(2,1)S(1)}, bf16[64,1152]{1,0:T(8,128)(2,1)S(1)}, u32[]{:S(2)}, u32[]{:S(2)}) collective-permute-start(bf16[64,1152]{1,0:T(8,128)(2,1)S(1)} %get-tuple-element.39), channel_id=1, source_target_pairs={{0,1},{1,0},{2,3},{3,2},{4,5},{5,4},{6,7},{7,6},{8,9},{9,8},{10,11... | collective-permute-start | bytes 442376 | tf_op jit(solution)/shard_map/ppermute | solution.py:189
  54.9 7.2 %collective-permute-start.20 = (bf16[64,1152]{1,0:T(8,128)(2,1)S(1)}, bf16[64,1152]{1,0:T(8,128)(2,1)S(1)}, u32[]{:S(2)}, u32[]{:S(2)}) collective-permute-start(bf16[64,1152]{1,0:T(8,128)(2,1)S(1)} %add.4), channel_id=1, source_target_pairs={{0,4},{1,5},{2,6},{3,7},{4,0},{5,1},{6,2},{7,3},{8,12},{9,13},{10,... | collective-permute-start | bytes 442376 | tf_op jit(solution)/shard_map/ppermute | solution.py:189
  57.5 8.1 %collective-permute-start.23 = (bf16[64,1152]{1,0:T(8,128)(2,1)S(1)}, bf16[64,1152]{1,0:T(8,128)(2,1)S(1)}, u32[]{:S(2)}, u32[]{:S(2)}) collective-permute-start(bf16[64,1152]{1,0:T(8,128)(2,1)S(1)} %add.5), channel_id=1, source_target_pairs={{0,12},{1,13},{2,14},{3,15},{4,8},{5,9},{6,10},{7,11},{8,4},{9,5},... | collective-permute-start | bytes 442376 | tf_op jit(solution)/shard_map/ppermute | solution.py:189
  60.5 5.2 %collective-permute-start.16 = (bf16[64,1152]{1,0:T(8,128)(2,1)S(1)}, bf16[64,1152]{1,0:T(8,128)(2,1)S(1)}, u32[]{:S(2)}, u32[]{:S(2)}) collective-permute-start(bf16[64,1152]{1,0:T(8,128)(2,1)S(1)} %get-tuple-element.41), channel_id=1, source_target_pairs={{0,2},{1,3},{2,0},{3,1},{4,6},{5,7},{6,4},{7,5},{8,10},{9,11},{10,... | collective-permute-start | bytes 442376 | tf_op jit(solution)/shard_map/ppermute | solution.py:189
  (8 other events, 18.4 us)

commit v6 on v5

--- a/solution.py
+++ b/solution.py
@@ -15,26 +15,34 @@
 PIECE = 256
 
 
-def pack_kernel(ids_ref, row_ref, out_ref):
-    rows, lat = row_ref.shape
-    top = ids_ref.shape[0]
-    out_ref[:, :lat] = row_ref[...]
+def pack_kernel(ids_hbm, row_hbm, out_ref, ids_ref, sems):
+    rows, lat = row_hbm.shape
+    top = ids_hbm.shape[0]
+    get_ids = pltpu.make_async_copy(ids_hbm, ids_ref, sems.at[0])
+    get_rows = pltpu.make_async_copy(row_hbm, out_ref.at[:, pl.ds(0, lat)], sems.at[1])
+    get_ids.start()
+    get_rows.start()
+    get_ids.wait()
     ids = ids_ref[...].astype(jnp.float32)
     ids = jnp.concatenate([ids, jnp.full((top, TAIL - rows), -1.0, jnp.float32)], axis=1)
     ids = jnp.concatenate([ids, jnp.full((TAIL - top, TAIL), -1.0, jnp.float32)], axis=0)
     out_ref[:, lat:] = ids.T[:rows].astype(jnp.bfloat16)
-
-
-def load_kernel(router_ref, up_hbm, down_hbm, dep_ref, columns_ref, up_ref, down_ref, sems):
+    get_rows.wait()
+
+
+def load_kernel(router_hbm, up_hbm, down_hbm, dep_ref, columns_ref, up_ref, down_ref, router_ref, sems):
+    get_router = pltpu.make_async_copy(router_hbm, router_ref, sems.at[0])
+    get_router.start()
     copies = []
     for src, dst in ((up_hbm, up_ref), (down_hbm, down_ref)):
         for e in range(src.shape[0]):
             for r in range(0, src.shape[1], PIECE):
                 at = (e, pl.ds(r, PIECE))
-                copies.append(pltpu.make_async_copy(src.at[at], dst.at[at], sems.at[len(copies)]))
+                copies.append(pltpu.make_async_copy(src.at[at], dst.at[at], sems.at[1 + len(copies)]))
     for copy in copies:
         copy.start()
     columns_ref[...] = jnp.zeros_like(columns_ref)
+    get_router.wait()
     columns_ref[: router_ref.shape[0], :] = router_ref[...]
     for copy in copies:
         copy.wait()
@@ -199,10 +207,13 @@
                 pltpu.VMEM(gate_up.shape, gate_up.dtype),
                 pltpu.VMEM(expert_down.shape, expert_down.dtype),
             ],
-            [router.T],
+            [],
             deps=[dep],
-            hbm=[gate_up, expert_down],
-            scratch=[pltpu.SemaphoreType.DMA((local * (lat + eff) // PIECE,))],
+            hbm=[router.T, gate_up, expert_down],
+            scratch=[
+                pltpu.VMEM((local, lat), jnp.bfloat16),
+                pltpu.SemaphoreType.DMA((1 + local * (lat + eff) // PIECE,)),
+            ],
             cost=modelled(5),
         )
 
@@ -238,7 +249,7 @@
     def group_pass(mine):
         loaded = weights(mine)
         z_2, z_1 = swap(mine, 8), swap(mine, 4)
-        block = {0: mine, 2: tie(z_2, [loaded[0]]), 1: z_1}
+        block = {0: mine, 2: tie(z_2, loaded), 1: z_1}
         block[3] = swap(block[2], 4)
         other = {k: swap(block[k], 2) for k in (2, 1, 3, 0)}
         pair, far = {}, {}
@@ -260,7 +271,7 @@
             z_send[k] = add(fold_keep[k], y_came[k], deps, cost)
             return swap(z_send[k], 4 * k)
 
-        gather(2, [block[1], block[3]])
+        gather(2, [block[1], block[3], *loaded])
         compute(2)
         gather(3, [send[2]])
         gather(1)
@@ -277,7 +288,13 @@
         reduce_core(0)
         return fold_keep[0], y_came[0], z_1, z_2, z_3
 
-    packet = call(pack_kernel, [space(rows, jnp.bfloat16)], [routes.T, latent_in])[0]
+    packet = call(
+        pack_kernel,
+        [space(rows, jnp.bfloat16)],
+        [],
+        hbm=[routes.T, latent_in],
+        scratch=[pltpu.VMEM(routes.shape[::-1], routes.dtype), pltpu.SemaphoreType.DMA((2,))],
+    )[0]
 
     def finish(parts):
         return pl.pallas_call(

time: 66.7 us -> 62.5 us (0.937)
  local copies, waits for them, and re-layouts: 13.1 us -> 5.58 us
  waiting for transfers between devices: 11.6 us -> 14.3 us
  Pallas kernels: 17.7 us -> 18.6 us
    unnamed x16 -> x10, local copies, waits for them, and re-layouts: 13.1 us -> 5.58 us
    ppermute x24, waiting for transfers between devices: 11.6 us -> 14.3 us  [swap(): return lax.ppermute(x, 'exp', [(i, i ^ bits) for i in range(n_dev)])]
    pallas_call x18, Pallas kernels: 17 us -> 17.9 us  [call(): pl.pallas_call(kernel, out_shape=outs, in_specs=specs, out_specs=[VMEM] *...]
  transfers between devices with their start and end apart: 24 -> 24, of which waited for: 7 -> 9; matrix products, arithmetic and copies ran while one was open for 0% -> 0% of each run, Pallas kernels for 25% -> 27%
where the time goes in v6:
time: 62.5 us; the launch traced here: 62.3 us
  starting transfers between devices  23.7 us (38%)
  Pallas kernels  18.6 us (30%)
  waiting for transfers between devices  14.3 us (23%)
  local copies, waits for them, and re-layouts  5.58 us (9%)
    ppermute x24, starting transfers between devices, swap(): return lax.ppermute(x, 'exp', [(i, i ^ bits) for i in range(n_dev)])  23.7 us
    pallas_call x18, Pallas kernels, call(): pl.pallas_call(kernel, out_shape=outs, in_specs=specs, out_specs=[VMEM] *...  17.9 us
    ppermute x24, waiting for transfers between devices, swap(): return lax.ppermute(x, 'exp', [(i, i ^ bits) for i in range(n_dev)])  14.3 us
    unnamed x10, local copies, waits for them, and re-layouts  5.58 us
  transfers between devices with their start and end apart: 24, of which 9 were waited for; matrix products, arithmetic and copies ran while one was open for 0% of the time, Pallas kernels for 27%

profile of v6, /device:TPU:0, one launch (start us, length us, event | category | flops | bytes accessed | tf_op | source)
XLA Modules:
  0.0 62.3 jit_solution(16432666676807929914)
XLA Ops:
  0.9 4.1 %collective-permute-start.1 = (bf16[64,1152]{1,0:T(8,128)(2,1)S(1)}, bf16[64,1152]{1,0:T(8,128)(2,1)S(1)}, u32[]{:S(2)}, u32[]{:S(2)}) collective-permute-start(bf16[64,1152]{1,0:T(8,128)(2,1)S(1)} %pack.1.dep_ref.a_ref), channel_id=1, source_target_pairs={{0,8},{1,9},{2,10},{3,11},{4,12},{5,13},{6,14},{7,15},{8,0},{9,1},... | collective-permute-start | bytes 442376 | tf_op jit(solution)/shard_map/ppermute | solution.py:197
  5.0 1.6 %collective-permute-start.5 = (bf16[64,1152]{1,0:T(8,128)(2,1)S(1)}, bf16[64,1152]{1,0:T(8,128)(2,1)S(1)}, u32[]{:S(2)}, u32[]{:S(2)}) collective-permute-start(bf16[64,1152]{1,0:T(8,128)(2,1)S(1)} %pack.1.dep_ref.a_ref), channel_id=1, source_target_pairs={{0,4},{1,5},{2,6},{3,7},{4,0},{5,1},{6,2},{7,3},{8,12},{9,13},{10,... | collective-permute-start | bytes 442376 | tf_op jit(solution)/shard_map/ppermute | solution.py:197
  6.6 4.7 %load.1 = (bf16[16,1024]{1,0:T(8,128)(2,1)S(1)}, bf16[2,1024,2048]{2,1,0:T(8,128)(2,1)S(1)}, bf16[2,1024,1024]{2,1,0:T(8,128)(2,1)S(1)}) custom-call(bf16[2,1024]{1,0:T(2,128)(2,1)} %bitcast.4, bf16[2,1024,2048]{2,1,0:T(8,128)(2,1)} %up_hbm.1, bf16[2,1024,1024]{2,1,0:T(8,128)(2,1)} %down_hbm.1, bf16[64,1152]{1,0:T(8,128)(2,1)S(1)} %pack.1.dep_ref.a_ref), custom_call_target="tpu_custom_call" | custom-call | bytes 18450000 | tf_op jit(solution)/shard_map/load/pallas_call | solution.py:175
  12.8 1.5 %collective-permute-start.4 = (bf16[64,1152]{1,0:T(8,128)(2,1)S(1)}, bf16[64,1152]{1,0:T(8,128)(2,1)S(1)}, u32[]{:S(2)}, u32[]{:S(2)}) collective-permute-start(bf16[64,1152]{1,0:T(8,128)(2,1)S(1)} %tie.1.a_ref), channel_id=1, source_target_pairs={{0,2},{1,3},{2,0},{3,1},{4,6},{5,7},{6,4},{7,5},{8,10},{9,11},{10,... | collective-permute-start | bytes 442376 | tf_op jit(solution)/shard_map/ppermute | solution.py:197
  14.3 3.0 %collective-permute-done.2.refs_1_.a_ref = bf16[64,1152]{1,0:T(8,128)(2,1)S(1)} collective-permute-done((bf16[64,1152]{1,0:T(8,128)(2,1)S(1)}, bf16[64,1152]{1,0:T(8,128)(2,1)S(1)}, u32[]{:S(2)}, u32[]{:S(2)}) %collective-permute-start.2) | collective-permute-done | bytes 147488 | tf_op jit(solution)/shard_map/ppermute | solution.py:197
  17.3 1.0 %collective-permute-done.4.b_ref = bf16[64,1152]{1,0:T(8,128)(2,1)S(1)} collective-permute-done((bf16[64,1152]{1,0:T(8,128)(2,1)S(1)}, bf16[64,1152]{1,0:T(8,128)(2,1)S(1)}, u32[]{:S(2)}, u32[]{:S(2)}) %collective-permute-start.4) | collective-permute-done | bytes 147488 | tf_op jit(solution)/shard_map/ppermute | solution.py:197
  18.4 1.6 %collective-permute-start.3 = (bf16[64,1152]{1,0:T(8,128)(2,1)S(1)}, bf16[64,1152]{1,0:T(8,128)(2,1)S(1)}, u32[]{:S(2)}, u32[]{:S(2)}) collective-permute-start(bf16[64,1152]{1,0:T(8,128)(2,1)S(1)} %collective-permute-done.2.refs_1_.a_ref), channel_id=1, source_target_pairs={{0,2},{1,3},{2,0},{3,1},{4,6},{5,7},{6,4},{7,5},{8,10},{9,11},{10,... | collective-permute-start | bytes 442376 | tf_op jit(solution)/shard_map/ppermute | solution.py:197
  20.5 3.4 %copy-done.1 = bf16[2,1024,2048]{2,1,0:T(8,128)(2,1)S(1)} copy-done((bf16[2,1024,2048]{2,1,0:T(8,128)(2,1)S(1)}, bf16[2,1024,2048]{2,1,0:T(8,128)(2,1)}, u32[]{:S(2)}) %copy-start.1) | copy-done | bytes 8388632
  23.9 2.2 %copy-done.4 = bf16[2,1024,1024]{2,1,0:T(8,128)(2,1)S(1)} copy-done((bf16[2,1024,1024]{2,1,0:T(8,128)(2,1)S(1)}, bf16[2,1024,1024]{2,1,0:T(8,128)(2,1)}, u32[]{:S(2)}) %copy-start.4) | copy-done | bytes 4194328
  26.1 2.9 %expert.4 = (f32[128,1152]{1,0:T(8,128)S(1)}, bf16[128,1152]{1,0:T(8,128)(2,1)S(1)}) custom-call(s32[1]{0:T(128)} %bitcast.first_ref, bf16[128,1152]{1,0:T(8,128)(2,1)S(1)} %join.4.pair_ref, bf16[128,1152]{1,0:T(8,128)(2,1)S(1)} %collective-permute-done.6.other_ref, bf16[16,1024]{1,0:T(8,128)(2,1)S(1)} %get-tuple-element.26.refs_1_.refs_2_.columns_ref, ...), custom_call_target="tpu_custom_call" | custom-call | bytes 36900000 | tf_op jit(solution)/shard_map/expert/pallas_call | solution.py:175
  29.8 1.5 %collective-permute-start = (bf16[64,1152]{1,0:T(8,128)(2,1)S(1)}, bf16[64,1152]{1,0:T(8,128)(2,1)S(1)}, u32[]{:S(2)}, u32[]{:S(2)}) collective-permute-start(bf16[64,1152]{1,0:T(8,128)(2,1)S(1)} %pack.1.dep_ref.a_ref), channel_id=1, source_target_pairs={{0,2},{1,3},{2,0},{3,1},{4,6},{5,7},{6,4},{7,5},{8,10},{9,11},{10,... | collective-permute-start | bytes 442376 | tf_op jit(solution)/shard_map/ppermute | solution.py:197
  31.3 3.0 %expert.5 = (f32[128,1152]{1,0:T(8,128)S(1)}, bf16[128,1152]{1,0:T(8,128)(2,1)S(1)}) custom-call(s32[1]{0:T(128)} %bitcast.first_ref, bf16[128,1152]{1,0:T(8,128)(2,1)S(1)} %join.5.pair_ref, bf16[128,1152]{1,0:T(8,128)(2,1)S(1)} %collective-permute-done.7.other_ref, bf16[16,1024]{1,0:T(8,128)(2,1)S(1)} %get-tuple-element.26.refs_1_.refs_2_.columns_ref, ...), custom_call_target="tpu_custom_call" | custom-call | bytes 36900000 | tf_op jit(solution)/shard_map/expert/pallas_call | solution.py:175
  34.5 1.5 %collective-permute-done.b_ref = bf16[64,1152]{1,0:T(8,128)(2,1)S(1)} collective-permute-done((bf16[64,1152]{1,0:T(8,128)(2,1)S(1)}, bf16[64,1152]{1,0:T(8,128)(2,1)S(1)}, u32[]{:S(2)}, u32[]{:S(2)}) %collective-permute-start) | collective-permute-done | bytes 147488 | tf_op jit(solution)/shard_map/ppermute | solution.py:197
  36.1 1.6 %collective-permute-start.13 = (bf16[64,1152]{1,0:T(8,128)(2,1)S(1)}, bf16[64,1152]{1,0:T(8,128)(2,1)S(1)}, u32[]{:S(2)}, u32[]{:S(2)}) collective-permute-start(bf16[64,1152]{1,0:T(8,128)(2,1)S(1)} %get-tuple-element.32.refs_1_), channel_id=1, source_target_pairs={{0,2},{1,3},{2,0},{3,1},{4,6},{5,7},{6,4},{7,5},{8,10},{9,11},{10,... | collective-permute-start | bytes 442376 | tf_op jit(solution)/shard_map/ppermute | solution.py:197
  37.7 3.0 %expert.6 = (f32[128,1152]{1,0:T(8,128)S(1)}, bf16[64,1152]{1,0:T(8,128)(2,1)S(1)}, bf16[64,1152]{1,0:T(8,128)(2,1)S(1)}) custom-call(s32[1]{0:T(128)} %bitcast.first_ref, bf16[128,1152]{1,0:T(8,128)(2,1)S(1)} %join.6.refs_1_.pair_ref, bf16[128,1152]{1,0:T(8,128)(2,1)S(1)} %collective-permute-done.10.other_ref, ...), custom_call_target="tpu_custom_call" | custom-call | bytes 36900000 | tf_op jit(solution)/shard_map/expert/pallas_call | solution.py:175
  41.3 1.2 %collective-permute-done.13.came_ref = bf16[64,1152]{1,0:T(8,128)(2,1)S(1)} collective-permute-done((bf16[64,1152]{1,0:T(8,128)(2,1)S(1)}, bf16[64,1152]{1,0:T(8,128)(2,1)S(1)}, u32[]{:S(2)}, u32[]{:S(2)}) %collective-permute-start.13) | collective-permute-done | bytes 147488 | tf_op jit(solution)/shard_map/ppermute | solution.py:197
  42.5 3.4 %collective-permute-start.21 = (bf16[64,1152]{1,0:T(8,128)(2,1)S(1)}, bf16[64,1152]{1,0:T(8,128)(2,1)S(1)}, u32[]{:S(2)}, u32[]{:S(2)}) collective-permute-start(bf16[64,1152]{1,0:T(8,128)(2,1)S(1)} %add.3.refs_2_), channel_id=1, source_target_pairs={{0,8},{1,9},{2,10},{3,11},{4,12},{5,13},{6,14},{7,15},{8,0},{9,1},... | collective-permute-start | bytes 442376 | tf_op jit(solution)/shard_map/ppermute | solution.py:197
  46.0 1.6 %collective-permute-start.19 = (bf16[64,1152]{1,0:T(8,128)(2,1)S(1)}, bf16[64,1152]{1,0:T(8,128)(2,1)S(1)}, u32[]{:S(2)}, u32[]{:S(2)}) collective-permute-start(bf16[64,1152]{1,0:T(8,128)(2,1)S(1)} %get-tuple-element.45), channel_id=1, source_target_pairs={{0,2},{1,3},{2,0},{3,1},{4,6},{5,7},{6,4},{7,5},{8,10},{9,11},{10,... | collective-permute-start | bytes 442376 | tf_op jit(solution)/shard_map/ppermute | solution.py:197
  48.2 3.0 %expert.7 = (f32[128,1152]{1,0:T(8,128)S(1)}, bf16[64,1152]{1,0:T(8,128)(2,1)S(1)}, bf16[64,1152]{1,0:T(8,128)(2,1)S(1)}) custom-call(s32[1]{0:T(128)} %bitcast.first_ref, bf16[128,1152]{1,0:T(8,128)(2,1)S(1)} %join.7.refs_2_.pair_ref, bf16[128,1152]{1,0:T(8,128)(2,1)S(1)} %collective-permute-done.9.other_ref, ...), custom_call_target="tpu_custom_call" | custom-call | bytes 36900000 | tf_op jit(solution)/shard_map/expert/pallas_call | solution.py:175
  51.7 1.1 %collective-permute-done.19.came_ref = bf16[64,1152]{1,0:T(8,128)(2,1)S(1)} collective-permute-done((bf16[64,1152]{1,0:T(8,128)(2,1)S(1)}, bf16[64,1152]{1,0:T(8,128)(2,1)S(1)}, u32[]{:S(2)}, u32[]{:S(2)}) %collective-permute-start.19) | collective-permute-done | bytes 147488 | tf_op jit(solution)/shard_map/ppermute | solution.py:197
  53.2 1.2 %collective-permute-done.22.came_ref = bf16[64,1152]{1,0:T(8,128)(2,1)S(1)} collective-permute-done((bf16[64,1152]{1,0:T(8,128)(2,1)S(1)}, bf16[64,1152]{1,0:T(8,128)(2,1)S(1)}, u32[]{:S(2)}, u32[]{:S(2)}) %collective-permute-start.22) | collective-permute-done | bytes 147488 | tf_op jit(solution)/shard_map/ppermute | solution.py:197
  55.4 1.6 %collective-permute-start.16 = (bf16[64,1152]{1,0:T(8,128)(2,1)S(1)}, bf16[64,1152]{1,0:T(8,128)(2,1)S(1)}, u32[]{:S(2)}, u32[]{:S(2)}) collective-permute-start(bf16[64,1152]{1,0:T(8,128)(2,1)S(1)} %get-tuple-element.41), channel_id=1, source_target_pairs={{0,2},{1,3},{2,0},{3,1},{4,6},{5,7},{6,4},{7,5},{8,10},{9,11},{10,... | collective-permute-start | bytes 442376 | tf_op jit(solution)/shard_map/ppermute | solution.py:197
  57.0 2.7 %collective-permute-done.20.refs_2_ = bf16[64,1152]{1,0:T(8,128)(2,1)S(1)} collective-permute-done((bf16[64,1152]{1,0:T(8,128)(2,1)S(1)}, bf16[64,1152]{1,0:T(8,128)(2,1)S(1)}, u32[]{:S(2)}, u32[]{:S(2)}) %collective-permute-start.20) | collective-permute-done | bytes 147488 | tf_op jit(solution)/shard_map/ppermute | solution.py:197
  59.6 1.9 %collective-permute-done.23.refs_4_ = bf16[64,1152]{1,0:T(8,128)(2,1)S(1)} collective-permute-done((bf16[64,1152]{1,0:T(8,128)(2,1)S(1)}, bf16[64,1152]{1,0:T(8,128)(2,1)S(1)}, u32[]{:S(2)}, u32[]{:S(2)}) %collective-permute-start.23) | collective-permute-done | bytes 147488 | tf_op jit(solution)/shard_map/ppermute | solution.py:197
  (53 shorter events, 8.1 us)
Async XLA Ops:
  0.9 11.2 %collective-permute-start.1 = (bf16[64,1152]{1,0:T(8,128)(2,1)S(1)}, bf16[64,1152]{1,0:T(8,128)(2,1)S(1)}, u32[]{:S(2)}, u32[]{:S(2)}) collective-permute-start(bf16[64,1152]{1,0:T(8,128)(2,1)S(1)} %pack.1.dep_ref.a_ref), channel_id=1, source_target_pairs={{0,8},{1,9},{2,10},{3,11},{4,12},{5,13},{6,14},{7,15},{8,0},{9,1},... | collective-permute-start | bytes 442376 | tf_op jit(solution)/shard_map/ppermute | solution.py:197
  5.0 9.3 %collective-permute-start.5 = (bf16[64,1152]{1,0:T(8,128)(2,1)S(1)}, bf16[64,1152]{1,0:T(8,128)(2,1)S(1)}, u32[]{:S(2)}, u32[]{:S(2)}) collective-permute-start(bf16[64,1152]{1,0:T(8,128)(2,1)S(1)} %pack.1.dep_ref.a_ref), channel_id=1, source_target_pairs={{0,4},{1,5},{2,6},{3,7},{4,0},{5,1},{6,2},{7,3},{8,12},{9,13},{10,... | collective-permute-start | bytes 442376 | tf_op jit(solution)/shard_map/ppermute | solution.py:197
  12.2 5.1 %collective-permute-start.2 = (bf16[64,1152]{1,0:T(8,128)(2,1)S(1)}, bf16[64,1152]{1,0:T(8,128)(2,1)S(1)}, u32[]{:S(2)}, u32[]{:S(2)}) collective-permute-start(bf16[64,1152]{1,0:T(8,128)(2,1)S(1)} %tie.1.a_ref), channel_id=1, source_target_pairs={{0,4},{1,5},{2,6},{3,7},{4,0},{5,1},{6,2},{7,3},{8,12},{9,13},{10,... | collective-permute-start | bytes 442376 | tf_op jit(solution)/shard_map/ppermute | solution.py:197
  12.8 5.5 %collective-permute-start.4 = (bf16[64,1152]{1,0:T(8,128)(2,1)S(1)}, bf16[64,1152]{1,0:T(8,128)(2,1)S(1)}, u32[]{:S(2)}, u32[]{:S(2)}) collective-permute-start(bf16[64,1152]{1,0:T(8,128)(2,1)S(1)} %tie.1.a_ref), channel_id=1, source_target_pairs={{0,2},{1,3},{2,0},{3,1},{4,6},{5,7},{6,4},{7,5},{8,10},{9,11},{10,... | collective-permute-start | bytes 442376 | tf_op jit(solution)/shard_map/ppermute | solution.py:197
  18.3 2.2 %collective-permute-start.6 = (bf16[128,1152]{1,0:T(8,128)(2,1)S(1)}, bf16[128,1152]{1,0:T(8,128)(2,1)S(1)}, u32[]{:S(2)}, u32[]{:S(2)}) collective-permute-start(bf16[128,1152]{1,0:T(8,128)(2,1)S(1)} %join.4.pair_ref), channel_id=1, source_target_pairs={{0,1},{1,0},{2,3},{3,2},{4,5},{5,4},{6,7},{7,6},{8,9},{9,8},{10,11... | collective-permute-start | bytes 884744 | tf_op jit(solution)/shard_map/ppermute | solution.py:197
  18.4 10.6 %collective-permute-start.3 = (bf16[64,1152]{1,0:T(8,128)(2,1)S(1)}, bf16[64,1152]{1,0:T(8,128)(2,1)S(1)}, u32[]{:S(2)}, u32[]{:S(2)}) collective-permute-start(bf16[64,1152]{1,0:T(8,128)(2,1)S(1)} %collective-permute-done.2.refs_1_.a_ref), channel_id=1, source_target_pairs={{0,2},{1,3},{2,0},{3,1},{4,6},{5,7},{6,4},{7,5},{8,10},{9,11},{10,... | collective-permute-start | bytes 442376 | tf_op jit(solution)/shard_map/ppermute | solution.py:197
  20.0 9.6 %collective-permute-start.8 = (bf16[64,1152]{1,0:T(8,128)(2,1)S(1)}, bf16[64,1152]{1,0:T(8,128)(2,1)S(1)}, u32[]{:S(2)}, u32[]{:S(2)}) collective-permute-start(bf16[64,1152]{1,0:T(8,128)(2,1)S(1)} %collective-permute-done.5.refs_0_.a_ref), channel_id=1, source_target_pairs={{0,2},{1,3},{2,0},{3,1},{4,6},{5,7},{6,4},{7,5},{8,10},{9,11},{10,... | collective-permute-start | bytes 442376 | tf_op jit(solution)/shard_map/ppermute | solution.py:197
  29.0 2.3 %collective-permute-start.7 = (bf16[128,1152]{1,0:T(8,128)(2,1)S(1)}, bf16[128,1152]{1,0:T(8,128)(2,1)S(1)}, u32[]{:S(2)}, u32[]{:S(2)}) collective-permute-start(bf16[128,1152]{1,0:T(8,128)(2,1)S(1)} %join.5.pair_ref), channel_id=1, source_target_pairs={{0,1},{1,0},{2,3},{3,2},{4,5},{5,4},{6,7},{7,6},{8,9},{9,8},{10,11... | collective-permute-start | bytes 884744 | tf_op jit(solution)/shard_map/ppermute | solution.py:197
  29.1 7.0 %collective-permute-start.11 = (bf16[128,1152]{1,0:T(8,128)(2,1)S(1)}, bf16[128,1152]{1,0:T(8,128)(2,1)S(1)}, u32[]{:S(2)}, u32[]{:S(2)}) collective-permute-start(bf16[128,1152]{1,0:T(8,128)(2,1)S(1)} %get-tuple-element.29.refs_0_), channel_id=1, source_target_pairs={{0,1},{1,0},{2,3},{3,2},{4,5},{5,4},{6,7},{7,6},{8,9},{9,8},{10,11... | collective-permute-start | bytes 884744 | tf_op jit(solution)/shard_map/ppermute | solution.py:197
  29.6 8.1 %collective-permute-start.10 = (bf16[128,1152]{1,0:T(8,128)(2,1)S(1)}, bf16[128,1152]{1,0:T(8,128)(2,1)S(1)}, u32[]{:S(2)}, u32[]{:S(2)}) collective-permute-start(bf16[128,1152]{1,0:T(8,128)(2,1)S(1)} %join.6.refs_1_.pair_ref), channel_id=1, source_target_pairs={{0,1},{1,0},{2,3},{3,2},{4,5},{5,4},{6,7},{7,6},{8,9},{9,8},{10,11... | collective-permute-start | bytes 884744 | tf_op jit(solution)/shard_map/ppermute | solution.py:197
  29.8 6.2 %collective-permute-start = (bf16[64,1152]{1,0:T(8,128)(2,1)S(1)}, bf16[64,1152]{1,0:T(8,128)(2,1)S(1)}, u32[]{:S(2)}, u32[]{:S(2)}) collective-permute-start(bf16[64,1152]{1,0:T(8,128)(2,1)S(1)} %pack.1.dep_ref.a_ref), channel_id=1, source_target_pairs={{0,2},{1,3},{2,0},{3,1},{4,6},{5,7},{6,4},{7,5},{8,10},{9,11},{10,... | collective-permute-start | bytes 442376 | tf_op jit(solution)/shard_map/ppermute | solution.py:197
  34.3 13.3 %collective-permute-start.12 = (bf16[128,1152]{1,0:T(8,128)(2,1)S(1)}, bf16[128,1152]{1,0:T(8,128)(2,1)S(1)}, u32[]{:S(2)}, u32[]{:S(2)}) collective-permute-start(bf16[128,1152]{1,0:T(8,128)(2,1)S(1)} %get-tuple-element.30.refs_0_), channel_id=1, source_target_pairs={{0,1},{1,0},{2,3},{3,2},{4,5},{5,4},{6,7},{7,6},{8,9},{9,8},{10,11... | collective-permute-start | bytes 884744 | tf_op jit(solution)/shard_map/ppermute | solution.py:197
  36.0 12.2 %collective-permute-start.9 = (bf16[128,1152]{1,0:T(8,128)(2,1)S(1)}, bf16[128,1152]{1,0:T(8,128)(2,1)S(1)}, u32[]{:S(2)}, u32[]{:S(2)}) collective-permute-start(bf16[128,1152]{1,0:T(8,128)(2,1)S(1)} %join.7.refs_2_.pair_ref), channel_id=1, source_target_pairs={{0,1},{1,0},{2,3},{3,2},{4,5},{5,4},{6,7},{7,6},{8,9},{9,8},{10,11... | collective-permute-start | bytes 884744 | tf_op jit(solution)/shard_map/ppermute | solution.py:197
  36.1 6.3 %collective-permute-start.13 = (bf16[64,1152]{1,0:T(8,128)(2,1)S(1)}, bf16[64,1152]{1,0:T(8,128)(2,1)S(1)}, u32[]{:S(2)}, u32[]{:S(2)}) collective-permute-start(bf16[64,1152]{1,0:T(8,128)(2,1)S(1)} %get-tuple-element.32.refs_1_), channel_id=1, source_target_pairs={{0,2},{1,3},{2,0},{3,1},{4,6},{5,7},{6,4},{7,5},{8,10},{9,11},{10,... | collective-permute-start | bytes 442376 | tf_op jit(solution)/shard_map/ppermute | solution.py:197
  40.7 5.2 %collective-permute-start.17 = (bf16[64,1152]{1,0:T(8,128)(2,1)S(1)}, bf16[64,1152]{1,0:T(8,128)(2,1)S(1)}, u32[]{:S(2)}, u32[]{:S(2)}) collective-permute-start(bf16[64,1152]{1,0:T(8,128)(2,1)S(1)} %get-tuple-element.33.refs_0_), channel_id=1, source_target_pairs={{0,1},{1,0},{2,3},{3,2},{4,5},{5,4},{6,7},{7,6},{8,9},{9,8},{10,11... | collective-permute-start | bytes 442376 | tf_op jit(solution)/shard_map/ppermute | solution.py:197
  41.0 5.0 %collective-permute-start.18 = (bf16[64,1152]{1,0:T(8,128)(2,1)S(1)}, bf16[64,1152]{1,0:T(8,128)(2,1)S(1)}, u32[]{:S(2)}, u32[]{:S(2)}) collective-permute-start(bf16[64,1152]{1,0:T(8,128)(2,1)S(1)} %get-tuple-element.43), channel_id=1, source_target_pairs={{0,1},{1,0},{2,3},{3,2},{4,5},{5,4},{6,7},{7,6},{8,9},{9,8},{10,11... | collective-permute-start | bytes 442376 | tf_op jit(solution)/shard_map/ppermute | solution.py:197
  42.5 10.7 %collective-permute-start.21 = (bf16[64,1152]{1,0:T(8,128)(2,1)S(1)}, bf16[64,1152]{1,0:T(8,128)(2,1)S(1)}, u32[]{:S(2)}, u32[]{:S(2)}) collective-permute-start(bf16[64,1152]{1,0:T(8,128)(2,1)S(1)} %add.3.refs_2_), channel_id=1, source_target_pairs={{0,8},{1,9},{2,10},{3,11},{4,12},{5,13},{6,14},{7,15},{8,0},{9,1},... | collective-permute-start | bytes 442376 | tf_op jit(solution)/shard_map/ppermute | solution.py:197
  46.0 6.8 %collective-permute-start.19 = (bf16[64,1152]{1,0:T(8,128)(2,1)S(1)}, bf16[64,1152]{1,0:T(8,128)(2,1)S(1)}, u32[]{:S(2)}, u32[]{:S(2)}) collective-permute-start(bf16[64,1152]{1,0:T(8,128)(2,1)S(1)} %get-tuple-element.45), channel_id=1, source_target_pairs={{0,2},{1,3},{2,0},{3,1},{4,6},{5,7},{6,4},{7,5},{8,10},{9,11},{10,... | collective-permute-start | bytes 442376 | tf_op jit(solution)/shard_map/ppermute | solution.py:197
  47.6 6.8 %collective-permute-start.22 = (bf16[64,1152]{1,0:T(8,128)(2,1)S(1)}, bf16[64,1152]{1,0:T(8,128)(2,1)S(1)}, u32[]{:S(2)}, u32[]{:S(2)}) collective-permute-start(bf16[64,1152]{1,0:T(8,128)(2,1)S(1)} %get-tuple-element.35.refs_1_), channel_id=1, source_target_pairs={{0,2},{1,3},{2,0},{3,1},{4,6},{5,7},{6,4},{7,5},{8,10},{9,11},{10,... | collective-permute-start | bytes 442376 | tf_op jit(solution)/shard_map/ppermute | solution.py:197
  51.2 4.2 %collective-permute-start.14 = (bf16[64,1152]{1,0:T(8,128)(2,1)S(1)}, bf16[64,1152]{1,0:T(8,128)(2,1)S(1)}, u32[]{:S(2)}, u32[]{:S(2)}) collective-permute-start(bf16[64,1152]{1,0:T(8,128)(2,1)S(1)} %get-tuple-element.38), channel_id=1, source_target_pairs={{0,1},{1,0},{2,3},{3,2},{4,5},{5,4},{6,7},{7,6},{8,9},{9,8},{10,11... | collective-permute-start | bytes 442376 | tf_op jit(solution)/shard_map/ppermute | solution.py:197
  51.2 4.1 %collective-permute-start.15 = (bf16[64,1152]{1,0:T(8,128)(2,1)S(1)}, bf16[64,1152]{1,0:T(8,128)(2,1)S(1)}, u32[]{:S(2)}, u32[]{:S(2)}) collective-permute-start(bf16[64,1152]{1,0:T(8,128)(2,1)S(1)} %get-tuple-element.39), channel_id=1, source_target_pairs={{0,1},{1,0},{2,3},{3,2},{4,5},{5,4},{6,7},{7,6},{8,9},{9,8},{10,11... | collective-permute-start | bytes 442376 | tf_op jit(solution)/shard_map/ppermute | solution.py:197
  52.8 6.8 %collective-permute-start.20 = (bf16[64,1152]{1,0:T(8,128)(2,1)S(1)}, bf16[64,1152]{1,0:T(8,128)(2,1)S(1)}, u32[]{:S(2)}, u32[]{:S(2)}) collective-permute-start(bf16[64,1152]{1,0:T(8,128)(2,1)S(1)} %add.4), channel_id=1, source_target_pairs={{0,4},{1,5},{2,6},{3,7},{4,0},{5,1},{6,2},{7,3},{8,12},{9,13},{10,... | collective-permute-start | bytes 442376 | tf_op jit(solution)/shard_map/ppermute | solution.py:197
  54.4 7.1 %collective-permute-start.23 = (bf16[64,1152]{1,0:T(8,128)(2,1)S(1)}, bf16[64,1152]{1,0:T(8,128)(2,1)S(1)}, u32[]{:S(2)}, u32[]{:S(2)}) collective-permute-start(bf16[64,1152]{1,0:T(8,128)(2,1)S(1)} %add.5), channel_id=1, source_target_pairs={{0,12},{1,13},{2,14},{3,15},{4,8},{5,9},{6,10},{7,11},{8,4},{9,5},... | collective-permute-start | bytes 442376 | tf_op jit(solution)/shard_map/ppermute | solution.py:197
  55.4 6.2 %collective-permute-start.16 = (bf16[64,1152]{1,0:T(8,128)(2,1)S(1)}, bf16[64,1152]{1,0:T(8,128)(2,1)S(1)}, u32[]{:S(2)}, u32[]{:S(2)}) collective-permute-start(bf16[64,1152]{1,0:T(8,128)(2,1)S(1)} %get-tuple-element.41), channel_id=1, source_target_pairs={{0,2},{1,3},{2,0},{3,1},{4,6},{5,7},{6,4},{7,5},{8,10},{9,11},{10,... | collective-permute-start | bytes 442376 | tf_op jit(solution)/shard_map/ppermute | solution.py:197
  (5 other events, 24.7 us)

commit v7 on v6

--- a/solution.py
+++ b/solution.py
@@ -9,7 +9,6 @@
 
 GROUP = 16
 TAIL = 128
-K_COST = 10
 SCALE = 2.0**40
 STEP = 256
 PIECE = 256
@@ -48,33 +47,25 @@
         copy.wait()
 
 
-def join_kernel(a_ref, b_ref, *refs):
-    out_ref = refs[-1]
-    rows = a_ref.shape[0]
-    out_ref[:rows] = a_ref[...]
-    out_ref[rows:] = b_ref[...]
-
-
-def expert_kernel(two, first_ref, pair_ref, other_ref, columns_ref, up_ref, down_ref, *refs):
+def expert_kernel(first_ref, a_ref, b_ref, c_ref, d_ref, columns_ref, up_ref, down_ref, *refs):
     inner_ref, result_ref = refs[-2:]
-    half, wide = pair_ref.shape
-    lat = wide - TAIL
+    keep_ref, send_refs = refs[-5], refs[-4:-2]
+    blocks = (a_ref, b_ref, c_ref, d_ref)
+    rows, wide = a_ref.shape
+    half, lat = 2 * rows, wide - TAIL
     local, eff, _ = down_ref.shape
     slots = result_ref.shape[0] // local
-    x = jnp.concatenate([pair_ref[:, :lat], other_ref[:, :lat]], axis=0)
-    tail = jnp.concatenate([pair_ref[:, lat:], other_ref[:, lat:]], axis=0).astype(jnp.float32)
-
-    outs = refs[-4 - two : -2]
+    x = jnp.concatenate([ref[:, :lat] for ref in blocks], axis=0)
+    tail = jnp.concatenate([ref[:, lat:] for ref in blocks], axis=0).astype(jnp.float32)
 
     def put(lanes, value):
-        outs[0][:, lanes] = value[:half]
-        height = half // (1 + two)
-        for i, out in enumerate(outs[1:]):
-            out[:, lanes] = value[half + i * height : half + (i + 1) * height].astype(jnp.bfloat16)
-
-    def logits_of(rows):
+        keep_ref[:, lanes] = value[:half]
+        for i, ref in enumerate(send_refs):
+            ref[:, lanes] = value[half + i * rows : half + (i + 1) * rows].astype(jnp.bfloat16)
+
+    def logits_of(values):
         return lax.dot_general(
-            rows, columns_ref[...], (((1,), (1,)), ((), ())), preferred_element_type=jnp.float32
+            values, columns_ref[...], (((1,), (1,)), ((), ())), preferred_element_type=jnp.float32
         )
 
     logits = logits_of(x)
@@ -101,11 +92,11 @@
     scores = jax.nn.sigmoid(logits_of(packed)) * SCALE
     for e in range(local):
         mine = slice(e * slots, (e + 1) * slots)
-        rows = packed[mine]
+        chosen = packed[mine]
         score = scores[mine, e : e + 1]
         for c in range(0, eff, STEP):
-            gate = jnp.dot(rows, up_ref[e, :, c : c + STEP], preferred_element_type=jnp.float32)
-            up = jnp.dot(rows, up_ref[e, :, eff + c : eff + c + STEP], preferred_element_type=jnp.float32)
+            gate = jnp.dot(chosen, up_ref[e, :, c : c + STEP], preferred_element_type=jnp.float32)
+            up = jnp.dot(chosen, up_ref[e, :, eff + c : eff + c + STEP], preferred_element_type=jnp.float32)
             inner_ref[mine, c : c + STEP] = (gate / (1.0 + jnp.exp(-gate)) * up * score).astype(jnp.bfloat16)
     for e in range(local):
         mine = slice(e * slots, (e + 1) * slots)
@@ -122,12 +113,11 @@
     pass
 
 
-def fold_kernel(mine_ref, *refs):
+def fold_kernel(mine_ref, came_a_ref, came_b_ref, *refs):
     keep_ref, send_ref = refs[-2:]
     rows = keep_ref.shape[0]
-    came = [refs[0][:rows], refs[0][rows:]] if len(refs) == 3 else [refs[0][...], refs[1][...]]
-    keep_ref[...] = mine_ref[:rows] + came[0].astype(jnp.float32)
-    send_ref[...] = (mine_ref[rows:] + came[1].astype(jnp.float32)).astype(jnp.bfloat16)
+    keep_ref[...] = mine_ref[:rows] + came_a_ref[...].astype(jnp.float32)
+    send_ref[...] = (mine_ref[rows:] + came_b_ref[...].astype(jnp.float32)).astype(jnp.bfloat16)
 
 
 def add_kernel(mine_ref, came_ref, *refs):
@@ -164,11 +154,7 @@
 ANY = pl.BlockSpec(memory_space=pl.ANY)
 
 
-def modelled(us):
-    return pl.CostEstimate(flops=0, bytes_accessed=int(us * 3.69e6), transcendentals=0)
-
-
-def call(kernel, outs, args, deps=(), smem=(), hbm=(), scratch=(), cost=None, aliases=None):
+def call(kernel, outs, args, deps=(), smem=(), hbm=(), scratch=(), aliases=None):
     specs = [pl.BlockSpec(memory_space=pltpu.SMEM)] * len(smem) + [VMEM] * len(args)
     specs += [ANY] * (len(hbm) + len(deps))
     operands = list(smem) + [in_vmem(a) for a in args] + [in_hbm(h) for h in hbm] + [in_vmem(d) for d in deps]
@@ -179,7 +165,7 @@
         out_specs=[VMEM] * len(outs),
         scratch_shapes=list(scratch),
         compiler_params=pltpu.CompilerParams(vmem_limit_bytes=16 * 1024 * 1024),
-        cost_estimate=cost or modelled(0.1),
+        cost_estimate=pl.CostEstimate(flops=0, bytes_accessed=10_000, transcendentals=0),
         input_output_aliases=aliases or {},
         name=getattr(kernel, "func", kernel).__name__.removesuffix("_kernel"),
     )(*operands)
@@ -214,78 +200,74 @@
                 pltpu.VMEM((local, lat), jnp.bfloat16),
                 pltpu.SemaphoreType.DMA((1 + local * (lat + eff) // PIECE,)),
             ],
-            cost=modelled(5),
         )
-
-    def join(a, b, deps=()):
-        return call(join_kernel, [space(2 * rows, jnp.bfloat16)], [a, b], deps)[0]
 
     bound = 2 * ((rows * routes.shape[1] + local * n_dev - 1) // (local * n_dev))
     slots = 4 * bound
 
-    def experts(pair, other, loaded, deps=(), two=0):
+    def experts(blocks, loaded, deps=()):
         return call(
-            functools.partial(expert_kernel, two),
-            [space(2 * rows, jnp.float32)] + [space(2 * rows // (1 + two), jnp.bfloat16)] * (1 + two),
-            [pair, other, *loaded],
+            expert_kernel,
+            [space(2 * rows, jnp.float32), space(rows, jnp.bfloat16), space(rows, jnp.bfloat16)],
+            [*blocks, *loaded],
             deps,
             smem=[first],
             scratch=[
                 pltpu.VMEM((local * slots, eff), jnp.bfloat16),
                 pltpu.VMEM((local * slots, lat), jnp.bfloat16),
             ],
-            cost=modelled(K_COST),
         )
 
     def tie(x, deps):
         return call(tie_kernel, [space(x.shape[0], x.dtype)], [x], deps, aliases={0: 0})[0]
 
-    def fold(mine, *came):
-        return call(fold_kernel, [space(rows, jnp.float32), space(rows, jnp.bfloat16)], [mine, *came])
-
-    def add(mine, came, deps=(), cost=None):
-        return call(add_kernel, [space(rows, jnp.bfloat16)], [mine, came], deps, cost=cost)[0]
+    def fold(mine, came, deps=()):
+        return call(
+            fold_kernel, [space(rows, jnp.float32), space(rows, jnp.bfloat16)], [mine, *came], deps
+        )
+
+    def add(mine, came, deps=()):
+        return call(add_kernel, [space(rows, jnp.bfloat16)], [mine, came], deps)[0]
 
     def group_pass(mine):
         loaded = weights(mine)
-        z_2, z_1 = swap(mine, 8), swap(mine, 4)
-        block = {0: mine, 2: tie(z_2, loaded), 1: z_1}
+        z_2, z_1, y_0 = swap(mine, 8), swap(mine, 4), swap(mine, 2)
+        block = {0: mine, 2: tie(z_2, [y_0, *loaded]), 1: z_1}
         block[3] = swap(block[2], 4)
-        other = {k: swap(block[k], 2) for k in (2, 1, 3, 0)}
-        pair, far = {}, {}
+        other = {0: y_0}
         keep, send, came, fold_keep, fold_send, y_came, z_send = {}, {}, {}, {}, {}, {}, {}
 
-        def gather(k, deps=()):
-            pair[k] = join(block[k], other[k], deps)
-            far[k] = swap(pair[k], 1)
-
-        def compute(k, deps=(), two=0):
-            keep[k], send[k], *more = experts(pair[k], far[k], loaded, deps, two)
-            came[k] = [swap(part, 1) for part in (send[k], *more)]
-
-        def reduce_core(k):
-            fold_keep[k], fold_send[k] = fold(keep[k], *came[k])
+        def gather(k, deps):
+            other[k] = tie(swap(block[k], 2), deps)
+
+        def compute(k, deps=()):
+            blocks = [block[k], other[k]]
+            blocks += [swap(one, 1) for one in blocks]
+            keep[k], *send[k] = experts(blocks, loaded, deps)
+            came[k] = [swap(part, 1) for part in send[k]]
+
+        def reduce_core(k, deps=()):
+            fold_keep[k], fold_send[k] = fold(keep[k], came[k], deps)
             y_came[k] = swap(fold_send[k], 2)
 
-        def reduce_y(k, deps=(), cost=None):
-            z_send[k] = add(fold_keep[k], y_came[k], deps, cost)
+        def reduce_y(k, deps=()):
+            z_send[k] = add(fold_keep[k], y_came[k], deps)
             return swap(z_send[k], 4 * k)
 
         gather(2, [block[1], block[3], *loaded])
         compute(2)
-        gather(3, [send[2]])
-        gather(1)
-        compute(3, [send[2], pair[1]])
-        gather(0, [send[3]])
+        gather(3, send[2])
+        gather(1, send[2])
         reduce_core(2)
-        compute(1, [send[3], fold_send[2], pair[0]], two=1)
-        reduce_core(3)
+        compute(3, [other[1], fold_send[2]])
         z_2 = reduce_y(2)
-        compute(0, [send[1], fold_send[3], z_send[2]], two=1)
-        reduce_core(1)
-        z_3 = reduce_y(3, [z_2], modelled(K_COST))
-        z_1 = reduce_y(1)
-        reduce_core(0)
+        reduce_core(3, [z_send[2]])
+        compute(1, [fold_send[3]])
+        z_3 = reduce_y(3)
+        reduce_core(1, [z_send[3]])
+        compute(0, [fold_send[1]])
+        z_1 = reduce_y(1, [z_2])
+        reduce_core(0, [z_send[1]])
         return fold_keep[0], y_came[0], z_1, z_2, z_3
 
     packet = call(

time: 62.5 us -> 63.7 us (1.019)
  starting transfers between devices: 23.7 us -> 25.7 us
  waiting for transfers between devices: 14.3 us -> 13.5 us
    ppermute x24 -> x30, starting transfers between devices: 23.7 us -> 25.7 us  [swap(): return lax.ppermute(x, 'exp', [(i, i ^ bits) for i in range(n_dev)])]
    ppermute x24 -> x30, waiting for transfers between devices: 14.3 us -> 13.5 us  [swap(): return lax.ppermute(x, 'exp', [(i, i ^ bits) for i in range(n_dev)])]
    pallas_call x18 -> x17, Pallas kernels: 17.9 us -> 17.8 us  [call(): pl.pallas_call(kernel, out_shape=outs, in_specs=specs, out_specs=[VMEM] *...]
  transfers between devices with their start and end apart: 24 -> 30, of which waited for: 9 -> 10; matrix products, arithmetic and copies ran while one was open for 0% -> 0% of each run, Pallas kernels for 27% -> 27%
where the time goes in v7:
time: 63.7 us; the launch traced here: 63.5 us
  starting transfers between devices  25.7 us (40%)
  Pallas kernels  18.6 us (29%)
  waiting for transfers between devices  13.5 us (21%)
  local copies, waits for them, and re-layouts  5.58 us (9%)
    ppermute x30, starting transfers between devices, swap(): return lax.ppermute(x, 'exp', [(i, i ^ bits) for i in range(n_dev)])  25.7 us
    pallas_call x17, Pallas kernels, call(): pl.pallas_call(kernel, out_shape=outs, in_specs=specs, out_specs=[VMEM] *...  17.8 us
    ppermute x30, waiting for transfers between devices, swap(): return lax.ppermute(x, 'exp', [(i, i ^ bits) for i in range(n_dev)])  13.5 us
    unnamed x10, local copies, waits for them, and re-layouts  5.58 us
  transfers between devices with their start and end apart: 30, of which 10 were waited for; matrix products, arithmetic and copies ran while one was open for 0% of the time, Pallas kernels for 27%

profile of v7, /device:TPU:0, one launch (start us, length us, event | category | flops | bytes accessed | tf_op | source)
XLA Modules:
  0.0 63.5 jit_solution(11083281622957841505)
XLA Ops:
  0.0 0.9 %pack.1.dep_ref.a_ref = bf16[64,1152]{1,0:T(8,128)(2,1)S(1)} custom-call(s32[8,64]{1,0:T(8,128)} %bitcast.3, bf16[64,1024]{1,0:T(8,128)(2,1)} %row_hbm.1), custom_call_target="tpu_custom_call" | custom-call | bytes 10000 | tf_op jit(solution)/shard_map/pack/pallas_call | solution.py:161
  0.9 3.0 %collective-permute-start = (bf16[64,1152]{1,0:T(8,128)(2,1)S(1)}, bf16[64,1152]{1,0:T(8,128)(2,1)S(1)}, u32[]{:S(2)}, u32[]{:S(2)}) collective-permute-start(bf16[64,1152]{1,0:T(8,128)(2,1)S(1)} %pack.1.dep_ref.a_ref), channel_id=1, source_target_pairs={{0,2},{1,3},{2,0},{3,1},{4,6},{5,7},{6,4},{7,5},{8,10},{9,11},{10,... | collective-permute-start | bytes 442376 | tf_op jit(solution)/shard_map/ppermute | solution.py:183
  4.0 2.6 %collective-permute-start.5 = (bf16[64,1152]{1,0:T(8,128)(2,1)S(1)}, bf16[64,1152]{1,0:T(8,128)(2,1)S(1)}, u32[]{:S(2)}, u32[]{:S(2)}) collective-permute-start(bf16[64,1152]{1,0:T(8,128)(2,1)S(1)} %pack.1.dep_ref.a_ref), channel_id=1, source_target_pairs={{0,8},{1,9},{2,10},{3,11},{4,12},{5,13},{6,14},{7,15},{8,0},{9,1},... | collective-permute-start | bytes 442376 | tf_op jit(solution)/shard_map/ppermute | solution.py:183
  6.6 1.6 %collective-permute-start.3 = (bf16[64,1152]{1,0:T(8,128)(2,1)S(1)}, bf16[64,1152]{1,0:T(8,128)(2,1)S(1)}, u32[]{:S(2)}, u32[]{:S(2)}) collective-permute-start(bf16[64,1152]{1,0:T(8,128)(2,1)S(1)} %pack.1.dep_ref.a_ref), channel_id=1, source_target_pairs={{0,4},{1,5},{2,6},{3,7},{4,0},{5,1},{6,2},{7,3},{8,12},{9,13},{10,... | collective-permute-start | bytes 442376 | tf_op jit(solution)/shard_map/ppermute | solution.py:183
  8.1 4.7 %load.1 = (bf16[16,1024]{1,0:T(8,128)(2,1)S(1)}, bf16[2,1024,2048]{2,1,0:T(8,128)(2,1)S(1)}, bf16[2,1024,1024]{2,1,0:T(8,128)(2,1)S(1)}) custom-call(bf16[2,1024]{1,0:T(2,128)(2,1)} %bitcast.4, bf16[2,1024,2048]{2,1,0:T(8,128)(2,1)} %up_hbm.1, bf16[2,1024,1024]{2,1,0:T(8,128)(2,1)} %down_hbm.1, bf16[64,1152]{1,0:T(8,128)(2,1)S(1)} %pack.1.dep_ref.a_ref), custom_call_target="tpu_custom_call" | custom-call | bytes 10000 | tf_op jit(solution)/shard_map/load/pallas_call | solution.py:161
  14.5 4.1 %collective-permute-done.7.refs_2_.a_ref = bf16[64,1152]{1,0:T(8,128)(2,1)S(1)} collective-permute-done((bf16[64,1152]{1,0:T(8,128)(2,1)S(1)}, bf16[64,1152]{1,0:T(8,128)(2,1)S(1)}, u32[]{:S(2)}, u32[]{:S(2)}) %collective-permute-start.7) | collective-permute-done | bytes 147488 | tf_op jit(solution)/shard_map/ppermute | solution.py:183
  18.6 0.9 %collective-permute-done.6.refs_0_ = bf16[64,1152]{1,0:T(8,128)(2,1)S(1)} collective-permute-done((bf16[64,1152]{1,0:T(8,128)(2,1)S(1)}, bf16[64,1152]{1,0:T(8,128)(2,1)S(1)}, u32[]{:S(2)}, u32[]{:S(2)}) %collective-permute-start.6) | collective-permute-done | bytes 147488 | tf_op jit(solution)/shard_map/ppermute | solution.py:183
  20.1 1.5 %collective-permute-start.4 = (bf16[64,1152]{1,0:T(8,128)(2,1)S(1)}, bf16[64,1152]{1,0:T(8,128)(2,1)S(1)}, u32[]{:S(2)}, u32[]{:S(2)}) collective-permute-start(bf16[64,1152]{1,0:T(8,128)(2,1)S(1)} %collective-permute-done.3.refs_1_.a_ref), channel_id=1, source_target_pairs={{0,2},{1,3},{2,0},{3,1},{4,6},{5,7},{6,4},{7,5},{8,10},{9,11},{10,... | collective-permute-start | bytes 442376 | tf_op jit(solution)/shard_map/ppermute | solution.py:183
  21.6 3.4 %copy-done.1 = bf16[2,1024,2048]{2,1,0:T(8,128)(2,1)S(1)} copy-done((bf16[2,1024,2048]{2,1,0:T(8,128)(2,1)S(1)}, bf16[2,1024,2048]{2,1,0:T(8,128)(2,1)}, u32[]{:S(2)}) %copy-start.1) | copy-done | bytes 8388632
  25.0 2.2 %copy-done.4 = bf16[2,1024,1024]{2,1,0:T(8,128)(2,1)S(1)} copy-done((bf16[2,1024,1024]{2,1,0:T(8,128)(2,1)S(1)}, bf16[2,1024,1024]{2,1,0:T(8,128)(2,1)}, u32[]{:S(2)}) %copy-start.4) | copy-done | bytes 4194328
  27.2 2.9 %expert.4 = (f32[128,1152]{1,0:T(8,128)S(1)}, bf16[64,1152]{1,0:T(8,128)(2,1)S(1)}, bf16[64,1152]{1,0:T(8,128)(2,1)S(1)}) custom-call(s32[1]{0:T(128)} %bitcast.first_ref, bf16[64,1152]{1,0:T(8,128)(2,1)S(1)} %tie.4.a_ref, bf16[64,1152]{1,0:T(8,128)(2,1)S(1)} %tie.5.b_ref, bf16[64,1152]{1,0:T(8,128)(2,1)S(1)} %collective-permute-done.8.c_ref, ...), custom_call_target="tpu_custom_call" | custom-call | bytes 10000 | tf_op jit(solution)/shard_map/expert/pallas_call | solution.py:161
  32.4 3.0 %expert.5 = (f32[128,1152]{1,0:T(8,128)S(1)}, bf16[64,1152]{1,0:T(8,128)(2,1)S(1)}, bf16[64,1152]{1,0:T(8,128)(2,1)S(1)}) custom-call(s32[1]{0:T(128)} %bitcast.first_ref, bf16[64,1152]{1,0:T(8,128)(2,1)S(1)} %collective-permute-done.7.refs_2_.a_ref, bf16[64,1152]{1,0:T(8,128)(2,1)S(1)} %tie.7.b_ref, bf16[64,1152]{1,0:T(8,128)(2,1)S(1)} %collective-permute-done.13.c_ref, ...), custom_call_target="tpu_custom_call" | custom-call | bytes 10000 | tf_op jit(solution)/shard_map/expert/pallas_call | solution.py:161
  36.5 1.5 %collective-permute-done.19.came_ref = bf16[64,1152]{1,0:T(8,128)(2,1)S(1)} collective-permute-done((bf16[64,1152]{1,0:T(8,128)(2,1)S(1)}, bf16[64,1152]{1,0:T(8,128)(2,1)S(1)}, u32[]{:S(2)}, u32[]{:S(2)}) %collective-permute-start.19) | collective-permute-done | bytes 147488 | tf_op jit(solution)/shard_map/ppermute | solution.py:183
  38.7 3.0 %expert.6 = (f32[128,1152]{1,0:T(8,128)S(1)}, bf16[64,1152]{1,0:T(8,128)(2,1)S(1)}, bf16[64,1152]{1,0:T(8,128)(2,1)S(1)}) custom-call(s32[1]{0:T(128)} %bitcast.first_ref, bf16[64,1152]{1,0:T(8,128)(2,1)S(1)} %collective-permute-done.3.refs_1_.a_ref, bf16[64,1152]{1,0:T(8,128)(2,1)S(1)} %tie.6.refs_0_.b_ref, ...), custom_call_target="tpu_custom_call" | custom-call | bytes 10000 | tf_op jit(solution)/shard_map/expert/pallas_call | solution.py:161
  42.7 0.6 collective-permute-done.22.came_ref
  43.4 3.4 %collective-permute-start.26 = (bf16[64,1152]{1,0:T(8,128)(2,1)S(1)}, bf16[64,1152]{1,0:T(8,128)(2,1)S(1)}, u32[]{:S(2)}, u32[]{:S(2)}) collective-permute-start(bf16[64,1152]{1,0:T(8,128)(2,1)S(1)} %add.3.refs_0_), channel_id=1, source_target_pairs={{0,8},{1,9},{2,10},{3,11},{4,12},{5,13},{6,14},{7,15},{8,0},{9,1},... | collective-permute-start | bytes 442376 | tf_op jit(solution)/shard_map/ppermute | solution.py:183
  46.9 1.4 %collective-permute-start.25 = (bf16[64,1152]{1,0:T(8,128)(2,1)S(1)}, bf16[64,1152]{1,0:T(8,128)(2,1)S(1)}, u32[]{:S(2)}, u32[]{:S(2)}) collective-permute-start(bf16[64,1152]{1,0:T(8,128)(2,1)S(1)} %get-tuple-element.44.refs_0_), channel_id=1, source_target_pairs={{0,2},{1,3},{2,0},{3,1},{4,6},{5,7},{6,4},{7,5},{8,10},{9,11},{10,... | collective-permute-start | bytes 442376 | tf_op jit(solution)/shard_map/ppermute | solution.py:183
  48.3 3.0 %expert.7 = (f32[128,1152]{1,0:T(8,128)S(1)}, bf16[64,1152]{1,0:T(8,128)(2,1)S(1)}, bf16[64,1152]{1,0:T(8,128)(2,1)S(1)}) custom-call(s32[1]{0:T(128)} %bitcast.first_ref, bf16[64,1152]{1,0:T(8,128)(2,1)S(1)} %pack.1.dep_ref.a_ref, bf16[64,1152]{1,0:T(8,128)(2,1)S(1)} %collective-permute-done.refs_1_.b_ref, ...), custom_call_target="tpu_custom_call" | custom-call | bytes 10000 | tf_op jit(solution)/shard_map/expert/pallas_call | solution.py:161
  51.9 1.2 %collective-permute-done.26.refs_0_.refs_3_ = bf16[64,1152]{1,0:T(8,128)(2,1)S(1)} collective-permute-done((bf16[64,1152]{1,0:T(8,128)(2,1)S(1)}, bf16[64,1152]{1,0:T(8,128)(2,1)S(1)}, u32[]{:S(2)}, u32[]{:S(2)}) %collective-permute-start.26) | collective-permute-done | bytes 147488 | tf_op jit(solution)/shard_map/ppermute | solution.py:183
  53.3 1.5 %collective-permute-start.27 = (bf16[64,1152]{1,0:T(8,128)(2,1)S(1)}, bf16[64,1152]{1,0:T(8,128)(2,1)S(1)}, u32[]{:S(2)}, u32[]{:S(2)}) collective-permute-start(bf16[64,1152]{1,0:T(8,128)(2,1)S(1)} %get-tuple-element.50), channel_id=1, source_target_pairs={{0,2},{1,3},{2,0},{3,1},{4,6},{5,7},{6,4},{7,5},{8,10},{9,11},{10,... | collective-permute-start | bytes 442376 | tf_op jit(solution)/shard_map/ppermute | solution.py:183
  54.9 3.9 %collective-permute-start.28 = (bf16[64,1152]{1,0:T(8,128)(2,1)S(1)}, bf16[64,1152]{1,0:T(8,128)(2,1)S(1)}, u32[]{:S(2)}, u32[]{:S(2)}) collective-permute-start(bf16[64,1152]{1,0:T(8,128)(2,1)S(1)} %add.5.refs_0_), channel_id=1, source_target_pairs={{0,4},{1,5},{2,6},{3,7},{4,0},{5,1},{6,2},{7,3},{8,12},{9,13},{10,... | collective-permute-start | bytes 442376 | tf_op jit(solution)/shard_map/ppermute | solution.py:183
  58.7 1.7 %collective-permute-done.29.refs_4_ = bf16[64,1152]{1,0:T(8,128)(2,1)S(1)} collective-permute-done((bf16[64,1152]{1,0:T(8,128)(2,1)S(1)}, bf16[64,1152]{1,0:T(8,128)(2,1)S(1)}, u32[]{:S(2)}, u32[]{:S(2)}) %collective-permute-start.29) | collective-permute-done | bytes 147488 | tf_op jit(solution)/shard_map/ppermute | solution.py:183
  60.4 2.3 %collective-permute-done.28.refs_2_ = bf16[64,1152]{1,0:T(8,128)(2,1)S(1)} collective-permute-done((bf16[64,1152]{1,0:T(8,128)(2,1)S(1)}, bf16[64,1152]{1,0:T(8,128)(2,1)S(1)}, u32[]{:S(2)}, u32[]{:S(2)}) %collective-permute-start.28) | collective-permute-done | bytes 147488 | tf_op jit(solution)/shard_map/ppermute | solution.py:183
  62.7 0.8 %finish.1 = bf16[64,1024]{1,0:T(8,128)(2,1)} custom-call(f32[64,1152]{1,0:T(8,128)S(1)} %get-tuple-element.49.refs_0_, bf16[64,1152]{1,0:T(8,128)(2,1)S(1)} %collective-permute-done.27.refs_1_, bf16[64,1152]{1,0:T(8,128)(2,1)S(1)} %collective-permute-done.28.refs_2_, bf16[64,1152]{1,0:T(8,128)(2,1)S(1)} %collective-permute-done.26.refs_0_.refs_3_, ...), custom_call_target="tpu_custom_call" | custom-call | tf_op jit(solution)/shard_map/finish/pallas_call | solution.py:282
  (64 shorter events, 8.3 us)
Async XLA Ops:
  0.9 12.0 %collective-permute-start = (bf16[64,1152]{1,0:T(8,128)(2,1)S(1)}, bf16[64,1152]{1,0:T(8,128)(2,1)S(1)}, u32[]{:S(2)}, u32[]{:S(2)}) collective-permute-start(bf16[64,1152]{1,0:T(8,128)(2,1)S(1)} %pack.1.dep_ref.a_ref), channel_id=1, source_target_pairs={{0,2},{1,3},{2,0},{3,1},{4,6},{5,7},{6,4},{7,5},{8,10},{9,11},{10,... | collective-permute-start | bytes 442376 | tf_op jit(solution)/shard_map/ppermute | solution.py:183
  4.0 9.5 %collective-permute-start.5 = (bf16[64,1152]{1,0:T(8,128)(2,1)S(1)}, bf16[64,1152]{1,0:T(8,128)(2,1)S(1)}, u32[]{:S(2)}, u32[]{:S(2)}) collective-permute-start(bf16[64,1152]{1,0:T(8,128)(2,1)S(1)} %pack.1.dep_ref.a_ref), channel_id=1, source_target_pairs={{0,8},{1,9},{2,10},{3,11},{4,12},{5,13},{6,14},{7,15},{8,0},{9,1},... | collective-permute-start | bytes 442376 | tf_op jit(solution)/shard_map/ppermute | solution.py:183
  6.6 8.0 %collective-permute-start.3 = (bf16[64,1152]{1,0:T(8,128)(2,1)S(1)}, bf16[64,1152]{1,0:T(8,128)(2,1)S(1)}, u32[]{:S(2)}, u32[]{:S(2)}) collective-permute-start(bf16[64,1152]{1,0:T(8,128)(2,1)S(1)} %pack.1.dep_ref.a_ref), channel_id=1, source_target_pairs={{0,4},{1,5},{2,6},{3,7},{4,0},{5,1},{6,2},{7,3},{8,12},{9,13},{10,... | collective-permute-start | bytes 442376 | tf_op jit(solution)/shard_map/ppermute | solution.py:183
  13.4 5.1 %collective-permute-start.7 = (bf16[64,1152]{1,0:T(8,128)(2,1)S(1)}, bf16[64,1152]{1,0:T(8,128)(2,1)S(1)}, u32[]{:S(2)}, u32[]{:S(2)}) collective-permute-start(bf16[64,1152]{1,0:T(8,128)(2,1)S(1)} %tie.4.a_ref), channel_id=1, source_target_pairs={{0,4},{1,5},{2,6},{3,7},{4,0},{5,1},{6,2},{7,3},{8,12},{9,13},{10,... | collective-permute-start | bytes 442376 | tf_op jit(solution)/shard_map/ppermute | solution.py:183
  14.0 5.5 %collective-permute-start.6 = (bf16[64,1152]{1,0:T(8,128)(2,1)S(1)}, bf16[64,1152]{1,0:T(8,128)(2,1)S(1)}, u32[]{:S(2)}, u32[]{:S(2)}) collective-permute-start(bf16[64,1152]{1,0:T(8,128)(2,1)S(1)} %tie.4.a_ref), channel_id=1, source_target_pairs={{0,2},{1,3},{2,0},{3,1},{4,6},{5,7},{6,4},{7,5},{8,10},{9,11},{10,... | collective-permute-start | bytes 442376 | tf_op jit(solution)/shard_map/ppermute | solution.py:183
  14.5 7.1 %collective-permute-start.8 = (bf16[64,1152]{1,0:T(8,128)(2,1)S(1)}, bf16[64,1152]{1,0:T(8,128)(2,1)S(1)}, u32[]{:S(2)}, u32[]{:S(2)}) collective-permute-start(bf16[64,1152]{1,0:T(8,128)(2,1)S(1)} %tie.4.a_ref), channel_id=1, source_target_pairs={{0,1},{1,0},{2,3},{3,2},{4,5},{5,4},{6,7},{7,6},{8,9},{9,8},{10,11... | collective-permute-start | bytes 442376 | tf_op jit(solution)/shard_map/ppermute | solution.py:183
  19.5 2.1 %collective-permute-start.9 = (bf16[64,1152]{1,0:T(8,128)(2,1)S(1)}, bf16[64,1152]{1,0:T(8,128)(2,1)S(1)}, u32[]{:S(2)}, u32[]{:S(2)}) collective-permute-start(bf16[64,1152]{1,0:T(8,128)(2,1)S(1)} %tie.5.b_ref), channel_id=1, source_target_pairs={{0,1},{1,0},{2,3},{3,2},{4,5},{5,4},{6,7},{7,6},{8,9},{9,8},{10,11... | collective-permute-start | bytes 442376 | tf_op jit(solution)/shard_map/ppermute | solution.py:183
  19.5 11.2 %collective-permute-start.12 = (bf16[64,1152]{1,0:T(8,128)(2,1)S(1)}, bf16[64,1152]{1,0:T(8,128)(2,1)S(1)}, u32[]{:S(2)}, u32[]{:S(2)}) collective-permute-start(bf16[64,1152]{1,0:T(8,128)(2,1)S(1)} %collective-permute-done.7.refs_2_.a_ref), channel_id=1, source_target_pairs={{0,2},{1,3},{2,0},{3,1},{4,6},{5,7},{6,4},{7,5},{8,10},{9,11},{10,... | collective-permute-start | bytes 442376 | tf_op jit(solution)/shard_map/ppermute | solution.py:183
  20.1 11.1 %collective-permute-start.4 = (bf16[64,1152]{1,0:T(8,128)(2,1)S(1)}, bf16[64,1152]{1,0:T(8,128)(2,1)S(1)}, u32[]{:S(2)}, u32[]{:S(2)}) collective-permute-start(bf16[64,1152]{1,0:T(8,128)(2,1)S(1)} %collective-permute-done.3.refs_1_.a_ref), channel_id=1, source_target_pairs={{0,2},{1,3},{2,0},{3,1},{4,6},{5,7},{6,4},{7,5},{8,10},{9,11},{10,... | collective-permute-start | bytes 442376 | tf_op jit(solution)/shard_map/ppermute | solution.py:183
  31.8 6.1 %collective-permute-start.19 = (bf16[64,1152]{1,0:T(8,128)(2,1)S(1)}, bf16[64,1152]{1,0:T(8,128)(2,1)S(1)}, u32[]{:S(2)}, u32[]{:S(2)}) collective-permute-start(bf16[64,1152]{1,0:T(8,128)(2,1)S(1)} %get-tuple-element.34.refs_1_), channel_id=1, source_target_pairs={{0,2},{1,3},{2,0},{3,1},{4,6},{5,7},{6,4},{7,5},{8,10},{9,11},{10,... | collective-permute-start | bytes 442376 | tf_op jit(solution)/shard_map/ppermute | solution.py:183
  35.4 2.6 %collective-permute-start.17 = (bf16[64,1152]{1,0:T(8,128)(2,1)S(1)}, bf16[64,1152]{1,0:T(8,128)(2,1)S(1)}, u32[]{:S(2)}, u32[]{:S(2)}) collective-permute-start(bf16[64,1152]{1,0:T(8,128)(2,1)S(1)} %get-tuple-element.36), channel_id=1, source_target_pairs={{0,1},{1,0},{2,3},{3,2},{4,5},{5,4},{6,7},{7,6},{8,9},{9,8},{10,11... | collective-permute-start | bytes 442376 | tf_op jit(solution)/shard_map/ppermute | solution.py:183
  35.6 2.4 %collective-permute-start.18 = (bf16[64,1152]{1,0:T(8,128)(2,1)S(1)}, bf16[64,1152]{1,0:T(8,128)(2,1)S(1)}, u32[]{:S(2)}, u32[]{:S(2)}) collective-permute-start(bf16[64,1152]{1,0:T(8,128)(2,1)S(1)} %get-tuple-element.37), channel_id=1, source_target_pairs={{0,1},{1,0},{2,3},{3,2},{4,5},{5,4},{6,7},{7,6},{8,9},{9,8},{10,11... | collective-permute-start | bytes 442376 | tf_op jit(solution)/shard_map/ppermute | solution.py:183
  36.0 2.7 %collective-permute-start.10 = (bf16[64,1152]{1,0:T(8,128)(2,1)S(1)}, bf16[64,1152]{1,0:T(8,128)(2,1)S(1)}, u32[]{:S(2)}, u32[]{:S(2)}) collective-permute-start(bf16[64,1152]{1,0:T(8,128)(2,1)S(1)} %collective-permute-done.3.refs_1_.a_ref), channel_id=1, source_target_pairs={{0,1},{1,0},{2,3},{3,2},{4,5},{5,4},{6,7},{7,6},{8,9},{9,8},{10,11... | collective-permute-start | bytes 442376 | tf_op jit(solution)/shard_map/ppermute | solution.py:183
  36.1 2.6 %collective-permute-start.11 = (bf16[64,1152]{1,0:T(8,128)(2,1)S(1)}, bf16[64,1152]{1,0:T(8,128)(2,1)S(1)}, u32[]{:S(2)}, u32[]{:S(2)}) collective-permute-start(bf16[64,1152]{1,0:T(8,128)(2,1)S(1)} %tie.6.refs_0_.b_ref), channel_id=1, source_target_pairs={{0,1},{1,0},{2,3},{3,2},{4,5},{5,4},{6,7},{7,6},{8,9},{9,8},{10,11... | collective-permute-start | bytes 442376 | tf_op jit(solution)/shard_map/ppermute | solution.py:183
  38.1 5.3 %collective-permute-start.22 = (bf16[64,1152]{1,0:T(8,128)(2,1)S(1)}, bf16[64,1152]{1,0:T(8,128)(2,1)S(1)}, u32[]{:S(2)}, u32[]{:S(2)}) collective-permute-start(bf16[64,1152]{1,0:T(8,128)(2,1)S(1)} %get-tuple-element.39.refs_0_), channel_id=1, source_target_pairs={{0,2},{1,3},{2,0},{3,1},{4,6},{5,7},{6,4},{7,5},{8,10},{9,11},{10,... | collective-permute-start | bytes 442376 | tf_op jit(solution)/shard_map/ppermute | solution.py:183
  41.7 5.1 %collective-permute-start.20 = (bf16[64,1152]{1,0:T(8,128)(2,1)S(1)}, bf16[64,1152]{1,0:T(8,128)(2,1)S(1)}, u32[]{:S(2)}, u32[]{:S(2)}) collective-permute-start(bf16[64,1152]{1,0:T(8,128)(2,1)S(1)} %get-tuple-element.41), channel_id=1, source_target_pairs={{0,1},{1,0},{2,3},{3,2},{4,5},{5,4},{6,7},{7,6},{8,9},{9,8},{10,11... | collective-permute-start | bytes 442376 | tf_op jit(solution)/shard_map/ppermute | solution.py:183
  41.7 5.0 %collective-permute-start.21 = (bf16[64,1152]{1,0:T(8,128)(2,1)S(1)}, bf16[64,1152]{1,0:T(8,128)(2,1)S(1)}, u32[]{:S(2)}, u32[]{:S(2)}) collective-permute-start(bf16[64,1152]{1,0:T(8,128)(2,1)S(1)} %get-tuple-element.42), channel_id=1, source_target_pairs={{0,1},{1,0},{2,3},{3,2},{4,5},{5,4},{6,7},{7,6},{8,9},{9,8},{10,11... | collective-permute-start | bytes 442376 | tf_op jit(solution)/shard_map/ppermute | solution.py:183
  42.2 6.1 %collective-permute-start.1 = (bf16[64,1152]{1,0:T(8,128)(2,1)S(1)}, bf16[64,1152]{1,0:T(8,128)(2,1)S(1)}, u32[]{:S(2)}, u32[]{:S(2)}) collective-permute-start(bf16[64,1152]{1,0:T(8,128)(2,1)S(1)} %pack.1.dep_ref.a_ref), channel_id=1, source_target_pairs={{0,1},{1,0},{2,3},{3,2},{4,5},{5,4},{6,7},{7,6},{8,9},{9,8},{10,11... | collective-permute-start | bytes 442376 | tf_op jit(solution)/shard_map/ppermute | solution.py:183
  42.3 6.0 %collective-permute-start.2 = (bf16[64,1152]{1,0:T(8,128)(2,1)S(1)}, bf16[64,1152]{1,0:T(8,128)(2,1)S(1)}, u32[]{:S(2)}, u32[]{:S(2)}) collective-permute-start(bf16[64,1152]{1,0:T(8,128)(2,1)S(1)} %collective-permute-done.refs_1_.b_ref), channel_id=1, source_target_pairs={{0,1},{1,0},{2,3},{3,2},{4,5},{5,4},{6,7},{7,6},{8,9},{9,8},{10,11... | collective-permute-start | bytes 442376 | tf_op jit(solution)/shard_map/ppermute | solution.py:183
  43.4 9.8 %collective-permute-start.26 = (bf16[64,1152]{1,0:T(8,128)(2,1)S(1)}, bf16[64,1152]{1,0:T(8,128)(2,1)S(1)}, u32[]{:S(2)}, u32[]{:S(2)}) collective-permute-start(bf16[64,1152]{1,0:T(8,128)(2,1)S(1)} %add.3.refs_0_), channel_id=1, source_target_pairs={{0,8},{1,9},{2,10},{3,11},{4,12},{5,13},{6,14},{7,15},{8,0},{9,1},... | collective-permute-start | bytes 442376 | tf_op jit(solution)/shard_map/ppermute | solution.py:183
  46.9 6.3 %collective-permute-start.25 = (bf16[64,1152]{1,0:T(8,128)(2,1)S(1)}, bf16[64,1152]{1,0:T(8,128)(2,1)S(1)}, u32[]{:S(2)}, u32[]{:S(2)}) collective-permute-start(bf16[64,1152]{1,0:T(8,128)(2,1)S(1)} %get-tuple-element.44.refs_0_), channel_id=1, source_target_pairs={{0,2},{1,3},{2,0},{3,1},{4,6},{5,7},{6,4},{7,5},{8,10},{9,11},{10,... | collective-permute-start | bytes 442376 | tf_op jit(solution)/shard_map/ppermute | solution.py:183
  51.9 8.5 %collective-permute-start.29 = (bf16[64,1152]{1,0:T(8,128)(2,1)S(1)}, bf16[64,1152]{1,0:T(8,128)(2,1)S(1)}, u32[]{:S(2)}, u32[]{:S(2)}) collective-permute-start(bf16[64,1152]{1,0:T(8,128)(2,1)S(1)} %add.4.refs_0_), channel_id=1, source_target_pairs={{0,12},{1,13},{2,14},{3,15},{4,8},{5,9},{6,10},{7,11},{8,4},{9,5},... | collective-permute-start | bytes 442376 | tf_op jit(solution)/shard_map/ppermute | solution.py:183
  53.3 7.1 %collective-permute-start.27 = (bf16[64,1152]{1,0:T(8,128)(2,1)S(1)}, bf16[64,1152]{1,0:T(8,128)(2,1)S(1)}, u32[]{:S(2)}, u32[]{:S(2)}) collective-permute-start(bf16[64,1152]{1,0:T(8,128)(2,1)S(1)} %get-tuple-element.50), channel_id=1, source_target_pairs={{0,2},{1,3},{2,0},{3,1},{4,6},{5,7},{6,4},{7,5},{8,10},{9,11},{10,... | collective-permute-start | bytes 442376 | tf_op jit(solution)/shard_map/ppermute | solution.py:183
  54.9 7.9 %collective-permute-start.28 = (bf16[64,1152]{1,0:T(8,128)(2,1)S(1)}, bf16[64,1152]{1,0:T(8,128)(2,1)S(1)}, u32[]{:S(2)}, u32[]{:S(2)}) collective-permute-start(bf16[64,1152]{1,0:T(8,128)(2,1)S(1)} %add.5.refs_0_), channel_id=1, source_target_pairs={{0,4},{1,5},{2,6},{3,7},{4,0},{5,1},{6,2},{7,3},{8,12},{9,13},{10,... | collective-permute-start | bytes 442376 | tf_op jit(solution)/shard_map/ppermute | solution.py:183
  (11 other events, 34.2 us)

commit v8 on v7

--- a/solution.py
+++ b/solution.py
@@ -8,6 +8,7 @@
 from jax.sharding import PartitionSpec as P
 
 GROUP = 16
+SCOPED = 2 * 1024 * 1024
 TAIL = 128
 SCALE = 2.0**40
 STEP = 256
@@ -164,7 +165,7 @@
         in_specs=specs,
         out_specs=[VMEM] * len(outs),
         scratch_shapes=list(scratch),
-        compiler_params=pltpu.CompilerParams(vmem_limit_bytes=16 * 1024 * 1024),
+        compiler_params=pltpu.CompilerParams(vmem_limit_bytes=SCOPED),
         cost_estimate=pl.CostEstimate(flops=0, bytes_accessed=10_000, transcendentals=0),
         input_output_aliases=aliases or {},
         name=getattr(kernel, "func", kernel).__name__.removesuffix("_kernel"),
@@ -284,6 +285,7 @@
             out_shape=jax.ShapeDtypeStruct((rows, lat), jnp.bfloat16),
             in_specs=[VMEM] * len(parts),
             out_specs=VMEM,
+            compiler_params=pltpu.CompilerParams(vmem_limit_bytes=SCOPED),
             name="finish",
         )(*[in_vmem(p) for p in parts])
 

time: 63.7 us -> 63.7 us (level)
  no operation moved by 1% of the time
where the time goes in v8:
time: 63.7 us; the launch traced here: 63.5 us
  starting transfers between devices  25.7 us (40%)
  Pallas kernels  18.6 us (29%)
  waiting for transfers between devices  13.5 us (21%)
  local copies, waits for them, and re-layouts  5.58 us (9%)
    ppermute x30, starting transfers between devices, swap(): return lax.ppermute(x, 'exp', [(i, i ^ bits) for i in range(n_dev)])  25.7 us
    pallas_call x17, Pallas kernels, call(): pl.pallas_call(kernel, out_shape=outs, in_specs=specs, out_specs=[VMEM] *...  17.8 us
    ppermute x30, waiting for transfers between devices, swap(): return lax.ppermute(x, 'exp', [(i, i ^ bits) for i in range(n_dev)])  13.5 us
    unnamed x10, local copies, waits for them, and re-layouts  5.58 us
  transfers between devices with their start and end apart: 30, of which 10 were waited for; matrix products, arithmetic and copies ran while one was open for 0% of the time, Pallas kernels for 27%

profile of v8, /device:TPU:0, one launch (start us, length us, event | category | flops | bytes accessed | tf_op | source)
XLA Modules:
  0.0 63.5 jit_solution(5273733993762798047)
XLA Ops:
  0.0 0.9 %pack.1.dep_ref.a_ref = bf16[64,1152]{1,0:T(8,128)(2,1)S(1)} custom-call(s32[8,64]{1,0:T(8,128)} %bitcast.3, bf16[64,1024]{1,0:T(8,128)(2,1)} %row_hbm.1), custom_call_target="tpu_custom_call" | custom-call | bytes 10000 | tf_op jit(solution)/shard_map/pack/pallas_call | solution.py:162
  0.9 3.0 %collective-permute-start = (bf16[64,1152]{1,0:T(8,128)(2,1)S(1)}, bf16[64,1152]{1,0:T(8,128)(2,1)S(1)}, u32[]{:S(2)}, u32[]{:S(2)}) collective-permute-start(bf16[64,1152]{1,0:T(8,128)(2,1)S(1)} %pack.1.dep_ref.a_ref), channel_id=1, source_target_pairs={{0,2},{1,3},{2,0},{3,1},{4,6},{5,7},{6,4},{7,5},{8,10},{9,11},{10,... | collective-permute-start | bytes 442376 | tf_op jit(solution)/shard_map/ppermute | solution.py:184
  4.0 2.6 %collective-permute-start.5 = (bf16[64,1152]{1,0:T(8,128)(2,1)S(1)}, bf16[64,1152]{1,0:T(8,128)(2,1)S(1)}, u32[]{:S(2)}, u32[]{:S(2)}) collective-permute-start(bf16[64,1152]{1,0:T(8,128)(2,1)S(1)} %pack.1.dep_ref.a_ref), channel_id=1, source_target_pairs={{0,8},{1,9},{2,10},{3,11},{4,12},{5,13},{6,14},{7,15},{8,0},{9,1},... | collective-permute-start | bytes 442376 | tf_op jit(solution)/shard_map/ppermute | solution.py:184
  6.6 1.6 %collective-permute-start.3 = (bf16[64,1152]{1,0:T(8,128)(2,1)S(1)}, bf16[64,1152]{1,0:T(8,128)(2,1)S(1)}, u32[]{:S(2)}, u32[]{:S(2)}) collective-permute-start(bf16[64,1152]{1,0:T(8,128)(2,1)S(1)} %pack.1.dep_ref.a_ref), channel_id=1, source_target_pairs={{0,4},{1,5},{2,6},{3,7},{4,0},{5,1},{6,2},{7,3},{8,12},{9,13},{10,... | collective-permute-start | bytes 442376 | tf_op jit(solution)/shard_map/ppermute | solution.py:184
  8.1 4.7 %load.1 = (bf16[16,1024]{1,0:T(8,128)(2,1)S(1)}, bf16[2,1024,2048]{2,1,0:T(8,128)(2,1)S(1)}, bf16[2,1024,1024]{2,1,0:T(8,128)(2,1)S(1)}) custom-call(bf16[2,1024]{1,0:T(2,128)(2,1)} %bitcast.4, bf16[2,1024,2048]{2,1,0:T(8,128)(2,1)} %up_hbm.1, bf16[2,1024,1024]{2,1,0:T(8,128)(2,1)} %down_hbm.1, bf16[64,1152]{1,0:T(8,128)(2,1)S(1)} %pack.1.dep_ref.a_ref), custom_call_target="tpu_custom_call" | custom-call | bytes 10000 | tf_op jit(solution)/shard_map/load/pallas_call | solution.py:162
  14.5 4.1 %collective-permute-done.7.refs_2_.a_ref = bf16[64,1152]{1,0:T(8,128)(2,1)S(1)} collective-permute-done((bf16[64,1152]{1,0:T(8,128)(2,1)S(1)}, bf16[64,1152]{1,0:T(8,128)(2,1)S(1)}, u32[]{:S(2)}, u32[]{:S(2)}) %collective-permute-start.7) | collective-permute-done | bytes 147488 | tf_op jit(solution)/shard_map/ppermute | solution.py:184
  18.6 0.9 %collective-permute-done.6.refs_0_ = bf16[64,1152]{1,0:T(8,128)(2,1)S(1)} collective-permute-done((bf16[64,1152]{1,0:T(8,128)(2,1)S(1)}, bf16[64,1152]{1,0:T(8,128)(2,1)S(1)}, u32[]{:S(2)}, u32[]{:S(2)}) %collective-permute-start.6) | collective-permute-done | bytes 147488 | tf_op jit(solution)/shard_map/ppermute | solution.py:184
  20.1 1.5 %collective-permute-start.4 = (bf16[64,1152]{1,0:T(8,128)(2,1)S(1)}, bf16[64,1152]{1,0:T(8,128)(2,1)S(1)}, u32[]{:S(2)}, u32[]{:S(2)}) collective-permute-start(bf16[64,1152]{1,0:T(8,128)(2,1)S(1)} %collective-permute-done.3.refs_1_.a_ref), channel_id=1, source_target_pairs={{0,2},{1,3},{2,0},{3,1},{4,6},{5,7},{6,4},{7,5},{8,10},{9,11},{10,... | collective-permute-start | bytes 442376 | tf_op jit(solution)/shard_map/ppermute | solution.py:184
  21.6 3.4 %copy-done.1 = bf16[2,1024,2048]{2,1,0:T(8,128)(2,1)S(1)} copy-done((bf16[2,1024,2048]{2,1,0:T(8,128)(2,1)S(1)}, bf16[2,1024,2048]{2,1,0:T(8,128)(2,1)}, u32[]{:S(2)}) %copy-start.1) | copy-done | bytes 8388632
  25.0 2.2 %copy-done.4 = bf16[2,1024,1024]{2,1,0:T(8,128)(2,1)S(1)} copy-done((bf16[2,1024,1024]{2,1,0:T(8,128)(2,1)S(1)}, bf16[2,1024,1024]{2,1,0:T(8,128)(2,1)}, u32[]{:S(2)}) %copy-start.4) | copy-done | bytes 4194328
  27.2 2.9 %expert.4 = (f32[128,1152]{1,0:T(8,128)S(1)}, bf16[64,1152]{1,0:T(8,128)(2,1)S(1)}, bf16[64,1152]{1,0:T(8,128)(2,1)S(1)}) custom-call(s32[1]{0:T(128)} %bitcast.first_ref, bf16[64,1152]{1,0:T(8,128)(2,1)S(1)} %tie.4.a_ref, bf16[64,1152]{1,0:T(8,128)(2,1)S(1)} %tie.5.b_ref, bf16[64,1152]{1,0:T(8,128)(2,1)S(1)} %collective-permute-done.8.c_ref, ...), custom_call_target="tpu_custom_call" | custom-call | bytes 10000 | tf_op jit(solution)/shard_map/expert/pallas_call | solution.py:162
  32.4 3.0 %expert.5 = (f32[128,1152]{1,0:T(8,128)S(1)}, bf16[64,1152]{1,0:T(8,128)(2,1)S(1)}, bf16[64,1152]{1,0:T(8,128)(2,1)S(1)}) custom-call(s32[1]{0:T(128)} %bitcast.first_ref, bf16[64,1152]{1,0:T(8,128)(2,1)S(1)} %collective-permute-done.7.refs_2_.a_ref, bf16[64,1152]{1,0:T(8,128)(2,1)S(1)} %tie.7.b_ref, bf16[64,1152]{1,0:T(8,128)(2,1)S(1)} %collective-permute-done.13.c_ref, ...), custom_call_target="tpu_custom_call" | custom-call | bytes 10000 | tf_op jit(solution)/shard_map/expert/pallas_call | solution.py:162
  36.5 1.5 %collective-permute-done.19.came_ref = bf16[64,1152]{1,0:T(8,128)(2,1)S(1)} collective-permute-done((bf16[64,1152]{1,0:T(8,128)(2,1)S(1)}, bf16[64,1152]{1,0:T(8,128)(2,1)S(1)}, u32[]{:S(2)}, u32[]{:S(2)}) %collective-permute-start.19) | collective-permute-done | bytes 147488 | tf_op jit(solution)/shard_map/ppermute | solution.py:184
  38.7 3.0 %expert.6 = (f32[128,1152]{1,0:T(8,128)S(1)}, bf16[64,1152]{1,0:T(8,128)(2,1)S(1)}, bf16[64,1152]{1,0:T(8,128)(2,1)S(1)}) custom-call(s32[1]{0:T(128)} %bitcast.first_ref, bf16[64,1152]{1,0:T(8,128)(2,1)S(1)} %collective-permute-done.3.refs_1_.a_ref, bf16[64,1152]{1,0:T(8,128)(2,1)S(1)} %tie.6.refs_0_.b_ref, ...), custom_call_target="tpu_custom_call" | custom-call | bytes 10000 | tf_op jit(solution)/shard_map/expert/pallas_call | solution.py:162
  42.7 0.6 collective-permute-done.22.came_ref
  43.4 3.4 %collective-permute-start.26 = (bf16[64,1152]{1,0:T(8,128)(2,1)S(1)}, bf16[64,1152]{1,0:T(8,128)(2,1)S(1)}, u32[]{:S(2)}, u32[]{:S(2)}) collective-permute-start(bf16[64,1152]{1,0:T(8,128)(2,1)S(1)} %add.3.refs_0_), channel_id=1, source_target_pairs={{0,8},{1,9},{2,10},{3,11},{4,12},{5,13},{6,14},{7,15},{8,0},{9,1},... | collective-permute-start | bytes 442376 | tf_op jit(solution)/shard_map/ppermute | solution.py:184
  46.9 1.4 %collective-permute-start.25 = (bf16[64,1152]{1,0:T(8,128)(2,1)S(1)}, bf16[64,1152]{1,0:T(8,128)(2,1)S(1)}, u32[]{:S(2)}, u32[]{:S(2)}) collective-permute-start(bf16[64,1152]{1,0:T(8,128)(2,1)S(1)} %get-tuple-element.44.refs_0_), channel_id=1, source_target_pairs={{0,2},{1,3},{2,0},{3,1},{4,6},{5,7},{6,4},{7,5},{8,10},{9,11},{10,... | collective-permute-start | bytes 442376 | tf_op jit(solution)/shard_map/ppermute | solution.py:184
  48.3 3.0 %expert.7 = (f32[128,1152]{1,0:T(8,128)S(1)}, bf16[64,1152]{1,0:T(8,128)(2,1)S(1)}, bf16[64,1152]{1,0:T(8,128)(2,1)S(1)}) custom-call(s32[1]{0:T(128)} %bitcast.first_ref, bf16[64,1152]{1,0:T(8,128)(2,1)S(1)} %pack.1.dep_ref.a_ref, bf16[64,1152]{1,0:T(8,128)(2,1)S(1)} %collective-permute-done.refs_1_.b_ref, ...), custom_call_target="tpu_custom_call" | custom-call | bytes 10000 | tf_op jit(solution)/shard_map/expert/pallas_call | solution.py:162
  52.0 1.2 %collective-permute-done.26.refs_0_.refs_3_ = bf16[64,1152]{1,0:T(8,128)(2,1)S(1)} collective-permute-done((bf16[64,1152]{1,0:T(8,128)(2,1)S(1)}, bf16[64,1152]{1,0:T(8,128)(2,1)S(1)}, u32[]{:S(2)}, u32[]{:S(2)}) %collective-permute-start.26) | collective-permute-done | bytes 147488 | tf_op jit(solution)/shard_map/ppermute | solution.py:184
  53.3 1.5 %collective-permute-start.27 = (bf16[64,1152]{1,0:T(8,128)(2,1)S(1)}, bf16[64,1152]{1,0:T(8,128)(2,1)S(1)}, u32[]{:S(2)}, u32[]{:S(2)}) collective-permute-start(bf16[64,1152]{1,0:T(8,128)(2,1)S(1)} %get-tuple-element.50), channel_id=1, source_target_pairs={{0,2},{1,3},{2,0},{3,1},{4,6},{5,7},{6,4},{7,5},{8,10},{9,11},{10,... | collective-permute-start | bytes 442376 | tf_op jit(solution)/shard_map/ppermute | solution.py:184
  54.9 3.9 %collective-permute-start.28 = (bf16[64,1152]{1,0:T(8,128)(2,1)S(1)}, bf16[64,1152]{1,0:T(8,128)(2,1)S(1)}, u32[]{:S(2)}, u32[]{:S(2)}) collective-permute-start(bf16[64,1152]{1,0:T(8,128)(2,1)S(1)} %add.5.refs_0_), channel_id=1, source_target_pairs={{0,4},{1,5},{2,6},{3,7},{4,0},{5,1},{6,2},{7,3},{8,12},{9,13},{10,... | collective-permute-start | bytes 442376 | tf_op jit(solution)/shard_map/ppermute | solution.py:184
  58.7 1.7 %collective-permute-done.29.refs_4_ = bf16[64,1152]{1,0:T(8,128)(2,1)S(1)} collective-permute-done((bf16[64,1152]{1,0:T(8,128)(2,1)S(1)}, bf16[64,1152]{1,0:T(8,128)(2,1)S(1)}, u32[]{:S(2)}, u32[]{:S(2)}) %collective-permute-start.29) | collective-permute-done | bytes 147488 | tf_op jit(solution)/shard_map/ppermute | solution.py:184
  60.4 2.3 %collective-permute-done.28.refs_2_ = bf16[64,1152]{1,0:T(8,128)(2,1)S(1)} collective-permute-done((bf16[64,1152]{1,0:T(8,128)(2,1)S(1)}, bf16[64,1152]{1,0:T(8,128)(2,1)S(1)}, u32[]{:S(2)}, u32[]{:S(2)}) %collective-permute-start.28) | collective-permute-done | bytes 147488 | tf_op jit(solution)/shard_map/ppermute | solution.py:184
  62.8 0.8 %finish.1 = bf16[64,1024]{1,0:T(8,128)(2,1)} custom-call(f32[64,1152]{1,0:T(8,128)S(1)} %get-tuple-element.49.refs_0_, bf16[64,1152]{1,0:T(8,128)(2,1)S(1)} %collective-permute-done.27.refs_1_, bf16[64,1152]{1,0:T(8,128)(2,1)S(1)} %collective-permute-done.28.refs_2_, bf16[64,1152]{1,0:T(8,128)(2,1)S(1)} %collective-permute-done.26.refs_0_.refs_3_, ...), custom_call_target="tpu_custom_call" | custom-call | tf_op jit(solution)/shard_map/finish/pallas_call | solution.py:283
  (64 shorter events, 8.3 us)
Async XLA Ops:
  0.9 12.0 %collective-permute-start = (bf16[64,1152]{1,0:T(8,128)(2,1)S(1)}, bf16[64,1152]{1,0:T(8,128)(2,1)S(1)}, u32[]{:S(2)}, u32[]{:S(2)}) collective-permute-start(bf16[64,1152]{1,0:T(8,128)(2,1)S(1)} %pack.1.dep_ref.a_ref), channel_id=1, source_target_pairs={{0,2},{1,3},{2,0},{3,1},{4,6},{5,7},{6,4},{7,5},{8,10},{9,11},{10,... | collective-permute-start | bytes 442376 | tf_op jit(solution)/shard_map/ppermute | solution.py:184
  4.0 9.5 %collective-permute-start.5 = (bf16[64,1152]{1,0:T(8,128)(2,1)S(1)}, bf16[64,1152]{1,0:T(8,128)(2,1)S(1)}, u32[]{:S(2)}, u32[]{:S(2)}) collective-permute-start(bf16[64,1152]{1,0:T(8,128)(2,1)S(1)} %pack.1.dep_ref.a_ref), channel_id=1, source_target_pairs={{0,8},{1,9},{2,10},{3,11},{4,12},{5,13},{6,14},{7,15},{8,0},{9,1},... | collective-permute-start | bytes 442376 | tf_op jit(solution)/shard_map/ppermute | solution.py:184
  6.6 8.0 %collective-permute-start.3 = (bf16[64,1152]{1,0:T(8,128)(2,1)S(1)}, bf16[64,1152]{1,0:T(8,128)(2,1)S(1)}, u32[]{:S(2)}, u32[]{:S(2)}) collective-permute-start(bf16[64,1152]{1,0:T(8,128)(2,1)S(1)} %pack.1.dep_ref.a_ref), channel_id=1, source_target_pairs={{0,4},{1,5},{2,6},{3,7},{4,0},{5,1},{6,2},{7,3},{8,12},{9,13},{10,... | collective-permute-start | bytes 442376 | tf_op jit(solution)/shard_map/ppermute | solution.py:184
  13.4 5.1 %collective-permute-start.7 = (bf16[64,1152]{1,0:T(8,128)(2,1)S(1)}, bf16[64,1152]{1,0:T(8,128)(2,1)S(1)}, u32[]{:S(2)}, u32[]{:S(2)}) collective-permute-start(bf16[64,1152]{1,0:T(8,128)(2,1)S(1)} %tie.4.a_ref), channel_id=1, source_target_pairs={{0,4},{1,5},{2,6},{3,7},{4,0},{5,1},{6,2},{7,3},{8,12},{9,13},{10,... | collective-permute-start | bytes 442376 | tf_op jit(solution)/shard_map/ppermute | solution.py:184
  14.0 5.5 %collective-permute-start.6 = (bf16[64,1152]{1,0:T(8,128)(2,1)S(1)}, bf16[64,1152]{1,0:T(8,128)(2,1)S(1)}, u32[]{:S(2)}, u32[]{:S(2)}) collective-permute-start(bf16[64,1152]{1,0:T(8,128)(2,1)S(1)} %tie.4.a_ref), channel_id=1, source_target_pairs={{0,2},{1,3},{2,0},{3,1},{4,6},{5,7},{6,4},{7,5},{8,10},{9,11},{10,... | collective-permute-start | bytes 442376 | tf_op jit(solution)/shard_map/ppermute | solution.py:184
  14.5 7.1 %collective-permute-start.8 = (bf16[64,1152]{1,0:T(8,128)(2,1)S(1)}, bf16[64,1152]{1,0:T(8,128)(2,1)S(1)}, u32[]{:S(2)}, u32[]{:S(2)}) collective-permute-start(bf16[64,1152]{1,0:T(8,128)(2,1)S(1)} %tie.4.a_ref), channel_id=1, source_target_pairs={{0,1},{1,0},{2,3},{3,2},{4,5},{5,4},{6,7},{7,6},{8,9},{9,8},{10,11... | collective-permute-start | bytes 442376 | tf_op jit(solution)/shard_map/ppermute | solution.py:184
  19.5 2.1 %collective-permute-start.9 = (bf16[64,1152]{1,0:T(8,128)(2,1)S(1)}, bf16[64,1152]{1,0:T(8,128)(2,1)S(1)}, u32[]{:S(2)}, u32[]{:S(2)}) collective-permute-start(bf16[64,1152]{1,0:T(8,128)(2,1)S(1)} %tie.5.b_ref), channel_id=1, source_target_pairs={{0,1},{1,0},{2,3},{3,2},{4,5},{5,4},{6,7},{7,6},{8,9},{9,8},{10,11... | collective-permute-start | bytes 442376 | tf_op jit(solution)/shard_map/ppermute | solution.py:184
  19.5 11.2 %collective-permute-start.12 = (bf16[64,1152]{1,0:T(8,128)(2,1)S(1)}, bf16[64,1152]{1,0:T(8,128)(2,1)S(1)}, u32[]{:S(2)}, u32[]{:S(2)}) collective-permute-start(bf16[64,1152]{1,0:T(8,128)(2,1)S(1)} %collective-permute-done.7.refs_2_.a_ref), channel_id=1, source_target_pairs={{0,2},{1,3},{2,0},{3,1},{4,6},{5,7},{6,4},{7,5},{8,10},{9,11},{10,... | collective-permute-start | bytes 442376 | tf_op jit(solution)/shard_map/ppermute | solution.py:184
  20.1 11.1 %collective-permute-start.4 = (bf16[64,1152]{1,0:T(8,128)(2,1)S(1)}, bf16[64,1152]{1,0:T(8,128)(2,1)S(1)}, u32[]{:S(2)}, u32[]{:S(2)}) collective-permute-start(bf16[64,1152]{1,0:T(8,128)(2,1)S(1)} %collective-permute-done.3.refs_1_.a_ref), channel_id=1, source_target_pairs={{0,2},{1,3},{2,0},{3,1},{4,6},{5,7},{6,4},{7,5},{8,10},{9,11},{10,... | collective-permute-start | bytes 442376 | tf_op jit(solution)/shard_map/ppermute | solution.py:184
  31.8 6.1 %collective-permute-start.19 = (bf16[64,1152]{1,0:T(8,128)(2,1)S(1)}, bf16[64,1152]{1,0:T(8,128)(2,1)S(1)}, u32[]{:S(2)}, u32[]{:S(2)}) collective-permute-start(bf16[64,1152]{1,0:T(8,128)(2,1)S(1)} %get-tuple-element.34.refs_1_), channel_id=1, source_target_pairs={{0,2},{1,3},{2,0},{3,1},{4,6},{5,7},{6,4},{7,5},{8,10},{9,11},{10,... | collective-permute-start | bytes 442376 | tf_op jit(solution)/shard_map/ppermute | solution.py:184
  35.4 2.6 %collective-permute-start.17 = (bf16[64,1152]{1,0:T(8,128)(2,1)S(1)}, bf16[64,1152]{1,0:T(8,128)(2,1)S(1)}, u32[]{:S(2)}, u32[]{:S(2)}) collective-permute-start(bf16[64,1152]{1,0:T(8,128)(2,1)S(1)} %get-tuple-element.36), channel_id=1, source_target_pairs={{0,1},{1,0},{2,3},{3,2},{4,5},{5,4},{6,7},{7,6},{8,9},{9,8},{10,11... | collective-permute-start | bytes 442376 | tf_op jit(solution)/shard_map/ppermute | solution.py:184
  35.6 2.4 %collective-permute-start.18 = (bf16[64,1152]{1,0:T(8,128)(2,1)S(1)}, bf16[64,1152]{1,0:T(8,128)(2,1)S(1)}, u32[]{:S(2)}, u32[]{:S(2)}) collective-permute-start(bf16[64,1152]{1,0:T(8,128)(2,1)S(1)} %get-tuple-element.37), channel_id=1, source_target_pairs={{0,1},{1,0},{2,3},{3,2},{4,5},{5,4},{6,7},{7,6},{8,9},{9,8},{10,11... | collective-permute-start | bytes 442376 | tf_op jit(solution)/shard_map/ppermute | solution.py:184
  36.0 2.7 %collective-permute-start.10 = (bf16[64,1152]{1,0:T(8,128)(2,1)S(1)}, bf16[64,1152]{1,0:T(8,128)(2,1)S(1)}, u32[]{:S(2)}, u32[]{:S(2)}) collective-permute-start(bf16[64,1152]{1,0:T(8,128)(2,1)S(1)} %collective-permute-done.3.refs_1_.a_ref), channel_id=1, source_target_pairs={{0,1},{1,0},{2,3},{3,2},{4,5},{5,4},{6,7},{7,6},{8,9},{9,8},{10,11... | collective-permute-start | bytes 442376 | tf_op jit(solution)/shard_map/ppermute | solution.py:184
  36.1 2.6 %collective-permute-start.11 = (bf16[64,1152]{1,0:T(8,128)(2,1)S(1)}, bf16[64,1152]{1,0:T(8,128)(2,1)S(1)}, u32[]{:S(2)}, u32[]{:S(2)}) collective-permute-start(bf16[64,1152]{1,0:T(8,128)(2,1)S(1)} %tie.6.refs_0_.b_ref), channel_id=1, source_target_pairs={{0,1},{1,0},{2,3},{3,2},{4,5},{5,4},{6,7},{7,6},{8,9},{9,8},{10,11... | collective-permute-start | bytes 442376 | tf_op jit(solution)/shard_map/ppermute | solution.py:184
  38.1 5.3 %collective-permute-start.22 = (bf16[64,1152]{1,0:T(8,128)(2,1)S(1)}, bf16[64,1152]{1,0:T(8,128)(2,1)S(1)}, u32[]{:S(2)}, u32[]{:S(2)}) collective-permute-start(bf16[64,1152]{1,0:T(8,128)(2,1)S(1)} %get-tuple-element.39.refs_0_), channel_id=1, source_target_pairs={{0,2},{1,3},{2,0},{3,1},{4,6},{5,7},{6,4},{7,5},{8,10},{9,11},{10,... | collective-permute-start | bytes 442376 | tf_op jit(solution)/shard_map/ppermute | solution.py:184
  41.7 5.1 %collective-permute-start.20 = (bf16[64,1152]{1,0:T(8,128)(2,1)S(1)}, bf16[64,1152]{1,0:T(8,128)(2,1)S(1)}, u32[]{:S(2)}, u32[]{:S(2)}) collective-permute-start(bf16[64,1152]{1,0:T(8,128)(2,1)S(1)} %get-tuple-element.41), channel_id=1, source_target_pairs={{0,1},{1,0},{2,3},{3,2},{4,5},{5,4},{6,7},{7,6},{8,9},{9,8},{10,11... | collective-permute-start | bytes 442376 | tf_op jit(solution)/shard_map/ppermute | solution.py:184
  41.7 5.1 %collective-permute-start.21 = (bf16[64,1152]{1,0:T(8,128)(2,1)S(1)}, bf16[64,1152]{1,0:T(8,128)(2,1)S(1)}, u32[]{:S(2)}, u32[]{:S(2)}) collective-permute-start(bf16[64,1152]{1,0:T(8,128)(2,1)S(1)} %get-tuple-element.42), channel_id=1, source_target_pairs={{0,1},{1,0},{2,3},{3,2},{4,5},{5,4},{6,7},{7,6},{8,9},{9,8},{10,11... | collective-permute-start | bytes 442376 | tf_op jit(solution)/shard_map/ppermute | solution.py:184
  42.2 6.1 %collective-permute-start.1 = (bf16[64,1152]{1,0:T(8,128)(2,1)S(1)}, bf16[64,1152]{1,0:T(8,128)(2,1)S(1)}, u32[]{:S(2)}, u32[]{:S(2)}) collective-permute-start(bf16[64,1152]{1,0:T(8,128)(2,1)S(1)} %pack.1.dep_ref.a_ref), channel_id=1, source_target_pairs={{0,1},{1,0},{2,3},{3,2},{4,5},{5,4},{6,7},{7,6},{8,9},{9,8},{10,11... | collective-permute-start | bytes 442376 | tf_op jit(solution)/shard_map/ppermute | solution.py:184
  42.3 6.0 %collective-permute-start.2 = (bf16[64,1152]{1,0:T(8,128)(2,1)S(1)}, bf16[64,1152]{1,0:T(8,128)(2,1)S(1)}, u32[]{:S(2)}, u32[]{:S(2)}) collective-permute-start(bf16[64,1152]{1,0:T(8,128)(2,1)S(1)} %collective-permute-done.refs_1_.b_ref), channel_id=1, source_target_pairs={{0,1},{1,0},{2,3},{3,2},{4,5},{5,4},{6,7},{7,6},{8,9},{9,8},{10,11... | collective-permute-start | bytes 442376 | tf_op jit(solution)/shard_map/ppermute | solution.py:184
  43.4 9.8 %collective-permute-start.26 = (bf16[64,1152]{1,0:T(8,128)(2,1)S(1)}, bf16[64,1152]{1,0:T(8,128)(2,1)S(1)}, u32[]{:S(2)}, u32[]{:S(2)}) collective-permute-start(bf16[64,1152]{1,0:T(8,128)(2,1)S(1)} %add.3.refs_0_), channel_id=1, source_target_pairs={{0,8},{1,9},{2,10},{3,11},{4,12},{5,13},{6,14},{7,15},{8,0},{9,1},... | collective-permute-start | bytes 442376 | tf_op jit(solution)/shard_map/ppermute | solution.py:184
  46.9 6.3 %collective-permute-start.25 = (bf16[64,1152]{1,0:T(8,128)(2,1)S(1)}, bf16[64,1152]{1,0:T(8,128)(2,1)S(1)}, u32[]{:S(2)}, u32[]{:S(2)}) collective-permute-start(bf16[64,1152]{1,0:T(8,128)(2,1)S(1)} %get-tuple-element.44.refs_0_), channel_id=1, source_target_pairs={{0,2},{1,3},{2,0},{3,1},{4,6},{5,7},{6,4},{7,5},{8,10},{9,11},{10,... | collective-permute-start | bytes 442376 | tf_op jit(solution)/shard_map/ppermute | solution.py:184
  51.9 8.5 %collective-permute-start.29 = (bf16[64,1152]{1,0:T(8,128)(2,1)S(1)}, bf16[64,1152]{1,0:T(8,128)(2,1)S(1)}, u32[]{:S(2)}, u32[]{:S(2)}) collective-permute-start(bf16[64,1152]{1,0:T(8,128)(2,1)S(1)} %add.4.refs_0_), channel_id=1, source_target_pairs={{0,12},{1,13},{2,14},{3,15},{4,8},{5,9},{6,10},{7,11},{8,4},{9,5},... | collective-permute-start | bytes 442376 | tf_op jit(solution)/shard_map/ppermute | solution.py:184
  53.3 7.1 %collective-permute-start.27 = (bf16[64,1152]{1,0:T(8,128)(2,1)S(1)}, bf16[64,1152]{1,0:T(8,128)(2,1)S(1)}, u32[]{:S(2)}, u32[]{:S(2)}) collective-permute-start(bf16[64,1152]{1,0:T(8,128)(2,1)S(1)} %get-tuple-element.50), channel_id=1, source_target_pairs={{0,2},{1,3},{2,0},{3,1},{4,6},{5,7},{6,4},{7,5},{8,10},{9,11},{10,... | collective-permute-start | bytes 442376 | tf_op jit(solution)/shard_map/ppermute | solution.py:184
  54.9 7.9 %collective-permute-start.28 = (bf16[64,1152]{1,0:T(8,128)(2,1)S(1)}, bf16[64,1152]{1,0:T(8,128)(2,1)S(1)}, u32[]{:S(2)}, u32[]{:S(2)}) collective-permute-start(bf16[64,1152]{1,0:T(8,128)(2,1)S(1)} %add.5.refs_0_), channel_id=1, source_target_pairs={{0,4},{1,5},{2,6},{3,7},{4,0},{5,1},{6,2},{7,3},{8,12},{9,13},{10,... | collective-permute-start | bytes 442376 | tf_op jit(solution)/shard_map/ppermute | solution.py:184
  (11 other events, 34.2 us)

commit v9 on v8

--- a/solution.py
+++ b/solution.py
@@ -30,7 +30,7 @@
     get_rows.wait()
 
 
-def load_kernel(router_hbm, up_hbm, down_hbm, dep_ref, columns_ref, up_ref, down_ref, router_ref, sems):
+def load_kernel(router_hbm, up_hbm, down_hbm, columns_ref, up_ref, down_ref, router_ref, sems):
     get_router = pltpu.make_async_copy(router_hbm, router_ref, sems.at[0])
     get_router.start()
     copies = []
@@ -48,9 +48,10 @@
         copy.wait()
 
 
-def expert_kernel(first_ref, a_ref, b_ref, c_ref, d_ref, columns_ref, up_ref, down_ref, *refs):
-    inner_ref, result_ref = refs[-2:]
-    keep_ref, send_refs = refs[-5], refs[-4:-2]
+def expert_kernel(
+    first_ref, a_ref, b_ref, c_ref, d_ref, columns_ref, up_ref, down_ref, keep_ref, *refs
+):
+    *send_refs, inner_ref, result_ref = refs
     blocks = (a_ref, b_ref, c_ref, d_ref)
     rows, wide = a_ref.shape
     half, lat = 2 * rows, wide - TAIL
@@ -110,19 +111,17 @@
     put(slice(lat, wide), jnp.where(lane == 0, sums, 0.0))
 
 
-def tie_kernel(*refs):
+def tie_kernel():
     pass
 
 
-def fold_kernel(mine_ref, came_a_ref, came_b_ref, *refs):
-    keep_ref, send_ref = refs[-2:]
+def fold_kernel(mine_ref, came_a_ref, came_b_ref, keep_ref, send_ref):
     rows = keep_ref.shape[0]
     keep_ref[...] = mine_ref[:rows] + came_a_ref[...].astype(jnp.float32)
     send_ref[...] = (mine_ref[rows:] + came_b_ref[...].astype(jnp.float32)).astype(jnp.bfloat16)
 
 
-def add_kernel(mine_ref, came_ref, *refs):
-    out_ref = refs[-1]
+def add_kernel(mine_ref, came_ref, out_ref):
     out_ref[...] = (mine_ref[...] + came_ref[...].astype(jnp.float32)).astype(jnp.bfloat16)
 
 
@@ -155,20 +154,36 @@
 ANY = pl.BlockSpec(memory_space=pl.ANY)
 
 
-def call(kernel, outs, args, deps=(), smem=(), hbm=(), scratch=(), aliases=None):
+def call(kernel, outs, args=(), deps=(), chain=(), smem=(), hbm=(), scratch=()):
+    n_in = len(smem) + len(args) + len(hbm)
+    n_skip = n_in + len(deps)
+    n_outs = n_skip + len(chain)
+
+    def body(*refs):
+        kernel(*refs[:n_in], *refs[n_outs : n_outs + len(outs)], *refs[n_outs + len(outs) + len(chain) :])
+
+    def body_with_chain(*refs):
+        kernel(
+            *refs[:n_in],
+            *refs[n_skip:n_outs],
+            *refs[n_outs : n_outs + len(outs)],
+            *refs[n_outs + len(outs) + len(chain) :],
+        )
+
     specs = [pl.BlockSpec(memory_space=pltpu.SMEM)] * len(smem) + [VMEM] * len(args)
-    specs += [ANY] * (len(hbm) + len(deps))
-    operands = list(smem) + [in_vmem(a) for a in args] + [in_hbm(h) for h in hbm] + [in_vmem(d) for d in deps]
+    specs += [ANY] * (len(hbm) + len(deps)) + [VMEM] * len(chain)
+    operands = list(smem) + [in_vmem(a) for a in args] + [in_hbm(h) for h in hbm]
+    operands += [in_vmem(x) for x in (*deps, *chain)]
     return pl.pallas_call(
-        kernel,
-        out_shape=outs,
+        body_with_chain if kernel is expert_kernel else body,
+        out_shape=list(outs) + [pltpu.VMEM(x.shape, x.dtype) for x in chain],
         in_specs=specs,
-        out_specs=[VMEM] * len(outs),
+        out_specs=[VMEM] * (len(outs) + len(chain)),
         scratch_shapes=list(scratch),
         compiler_params=pltpu.CompilerParams(vmem_limit_bytes=SCOPED),
         cost_estimate=pl.CostEstimate(flops=0, bytes_accessed=10_000, transcendentals=0),
-        input_output_aliases=aliases or {},
-        name=getattr(kernel, "func", kernel).__name__.removesuffix("_kernel"),
+        input_output_aliases={n_skip + i: len(outs) + i for i in range(len(chain))},
+        name=kernel.__name__.removesuffix("_kernel"),
     )(*operands)
 
 
@@ -194,7 +209,6 @@
                 pltpu.VMEM(gate_up.shape, gate_up.dtype),
                 pltpu.VMEM(expert_down.shape, expert_down.dtype),
             ],
-            [],
             deps=[dep],
             hbm=[router.T, gate_up, expert_down],
             scratch=[
@@ -206,75 +220,71 @@
     bound = 2 * ((rows * routes.shape[1] + local * n_dev - 1) // (local * n_dev))
     slots = 4 * bound
 
-    def experts(blocks, loaded, deps=()):
-        return call(
-            expert_kernel,
-            [space(2 * rows, jnp.float32), space(rows, jnp.bfloat16), space(rows, jnp.bfloat16)],
-            [*blocks, *loaded],
-            deps,
-            smem=[first],
-            scratch=[
-                pltpu.VMEM((local * slots, eff), jnp.bfloat16),
-                pltpu.VMEM((local * slots, lat), jnp.bfloat16),
-            ],
-        )
-
-    def tie(x, deps):
-        return call(tie_kernel, [space(x.shape[0], x.dtype)], [x], deps, aliases={0: 0})[0]
-
-    def fold(mine, came, deps=()):
-        return call(
-            fold_kernel, [space(rows, jnp.float32), space(rows, jnp.bfloat16)], [mine, *came], deps
-        )
-
-    def add(mine, came, deps=()):
-        return call(add_kernel, [space(rows, jnp.bfloat16)], [mine, came], deps)[0]
-
     def group_pass(mine):
-        loaded = weights(mine)
-        z_2, z_1, y_0 = swap(mine, 8), swap(mine, 4), swap(mine, 2)
-        block = {0: mine, 2: tie(z_2, [y_0, *loaded]), 1: z_1}
-        block[3] = swap(block[2], 4)
-        other = {0: y_0}
-        keep, send, came, fold_keep, fold_send, y_came, z_send = {}, {}, {}, {}, {}, {}, {}
-
-        def gather(k, deps):
+        held = weights(mine)
+
+        def step(kernel, outs, args=(), deps=(), hand_on=(), **more):
+            nonlocal held
+            result = call(kernel, outs, args, deps, [*held, *hand_on], **more)
+            held = result[len(outs) : len(outs) + len(held)]
+            return result[: len(outs)] + result[len(outs) + len(held) :]
+
+        def tie(x, deps=()):
+            return step(tie_kernel, [], deps=deps, hand_on=[x])[0]
+
+        other, keep, send, came, fold_keep, fold_send, y_came, z_send = {}, {}, {}, {}, {}, {}, {}, {}
+
+        def gather(k, deps=()):
             other[k] = tie(swap(block[k], 2), deps)
 
-        def compute(k, deps=()):
+        def compute(k):
             blocks = [block[k], other[k]]
             blocks += [swap(one, 1) for one in blocks]
-            keep[k], *send[k] = experts(blocks, loaded, deps)
+            keep[k], *send[k] = step(
+                expert_kernel,
+                [space(2 * rows, jnp.float32), space(rows, jnp.bfloat16), space(rows, jnp.bfloat16)],
+                blocks,
+                smem=[first],
+                scratch=[
+                    pltpu.VMEM((local * slots, eff), jnp.bfloat16),
+                    pltpu.VMEM((local * slots, lat), jnp.bfloat16),
+                ],
+            )
             came[k] = [swap(part, 1) for part in send[k]]
 
-        def reduce_core(k, deps=()):
-            fold_keep[k], fold_send[k] = fold(keep[k], came[k], deps)
+        def reduce_core(k):
+            fold_keep[k], fold_send[k] = step(
+                fold_kernel, [space(rows, jnp.float32), space(rows, jnp.bfloat16)], [keep[k], *came[k]]
+            )
             y_came[k] = swap(fold_send[k], 2)
 
         def reduce_y(k, deps=()):
-            z_send[k] = add(fold_keep[k], y_came[k], deps)
+            z_send[k] = step(add_kernel, [space(rows, jnp.bfloat16)], [fold_keep[k], y_came[k]], deps)[0]
             return swap(z_send[k], 4 * k)
 
-        gather(2, [block[1], block[3], *loaded])
+        z_2, z_1, y_0 = swap(mine, 8), swap(mine, 4), swap(mine, 2)
+        block = {0: mine, 2: tie(z_2, [y_0]), 1: z_1}
+        block[3] = swap(block[2], 4)
+        other[0] = y_0
+        gather(2, [block[1], block[3]])
         compute(2)
-        gather(3, send[2])
-        gather(1, send[2])
+        gather(3)
+        gather(1)
         reduce_core(2)
-        compute(3, [other[1], fold_send[2]])
+        compute(3)
         z_2 = reduce_y(2)
-        reduce_core(3, [z_send[2]])
-        compute(1, [fold_send[3]])
+        reduce_core(3)
+        compute(1)
         z_3 = reduce_y(3)
-        reduce_core(1, [z_send[3]])
-        compute(0, [fold_send[1]])
+        reduce_core(1)
+        compute(0)
         z_1 = reduce_y(1, [z_2])
-        reduce_core(0, [z_send[1]])
+        reduce_core(0)
         return fold_keep[0], y_came[0], z_1, z_2, z_3
 
     packet = call(
         pack_kernel,
         [space(rows, jnp.bfloat16)],
-        [],
         hbm=[routes.T, latent_in],
         scratch=[pltpu.VMEM(routes.shape[::-1], routes.dtype), pltpu.SemaphoreType.DMA((2,))],
     )[0]

time: 63.7 us -> 86.2 us (1.35)
  local copies, waits for them, and re-layouts: 5.58 us -> 32.8 us
  starting transfers between devices: 25.7 us -> 21.2 us
    unnamed x10 -> x24, local copies, waits for them, and re-layouts: 5.58 us -> 32.8 us
    ppermute x30, starting transfers between devices: 25.7 us -> 21.2 us  [swap(): return lax.ppermute(x, 'exp', [(i, i ^ bits) for i in range(n_dev)])]
  transfers between devices with their start and end apart: 30 -> 30, of which waited for: 10 -> 10; matrix products, arithmetic and copies ran while one was open for 0% -> 0% of each run, Pallas kernels for 27% -> 19%
where the time goes in v9:
time: 86.2 us; the launch traced here: 85.9 us
  local copies, waits for them, and re-layouts  32.8 us (38%)
  starting transfers between devices  21.2 us (25%)
  Pallas kernels  18.3 us (21%)
  waiting for transfers between devices  13.4 us (16%)
    unnamed x24, local copies, waits for them, and re-layouts  32.8 us
    ppermute x30, starting transfers between devices, swap(): return lax.ppermute(x, 'exp', [(i, i ^ bits) for i in range(n_dev)])  21.2 us
    pallas_call x17, Pallas kernels, call(): pl.pallas_call(body_with_chain if kernel is expert_kernel else body, out_...  17.5 us
    ppermute x30, waiting for transfers between devices, swap(): return lax.ppermute(x, 'exp', [(i, i ^ bits) for i in range(n_dev)])  13.4 us
  transfers between devices with their start and end apart: 30, of which 10 were waited for; matrix products, arithmetic and copies ran while one was open for 0% of the time, Pallas kernels for 19%

profile of v9, /device:TPU:0, one launch (start us, length us, event | category | flops | bytes accessed | tf_op | source)
XLA Modules:
  0.0 85.9 jit_solution(18253333105240595419)
XLA Ops:
  0.9 3.0 %collective-permute-start = (bf16[64,1152]{1,0:T(8,128)(2,1)S(1)}, bf16[64,1152]{1,0:T(8,128)(2,1)S(1)}, u32[]{:S(2)}, u32[]{:S(2)}) collective-permute-start(bf16[64,1152]{1,0:T(8,128)(2,1)S(1)} %pack.1.refs_3_.refs_1_), channel_id=1, source_target_pairs={{0,2},{1,3},{2,0},{3,1},{4,6},{5,7},{6,4},{7,5},{8,10},{9,11},{10,... | collective-permute-start | bytes 442376 | tf_op jit(solution)/shard_map/ppermute | solution.py:199
  4.0 2.6 %collective-permute-start.4 = (bf16[64,1152]{1,0:T(8,128)(2,1)S(1)}, bf16[64,1152]{1,0:T(8,128)(2,1)S(1)}, u32[]{:S(2)}, u32[]{:S(2)}) collective-permute-start(bf16[64,1152]{1,0:T(8,128)(2,1)S(1)} %pack.1.refs_3_.refs_1_), channel_id=1, source_target_pairs={{0,8},{1,9},{2,10},{3,11},{4,12},{5,13},{6,14},{7,15},{8,0},{9,1},... | collective-permute-start | bytes 442376 | tf_op jit(solution)/shard_map/ppermute | solution.py:199
  6.6 1.6 %collective-permute-start.3 = (bf16[64,1152]{1,0:T(8,128)(2,1)S(1)}, bf16[64,1152]{1,0:T(8,128)(2,1)S(1)}, u32[]{:S(2)}, u32[]{:S(2)}) collective-permute-start(bf16[64,1152]{1,0:T(8,128)(2,1)S(1)} %pack.1.refs_3_.refs_1_), channel_id=1, source_target_pairs={{0,4},{1,5},{2,6},{3,7},{4,0},{5,1},{6,2},{7,3},{8,12},{9,13},{10,... | collective-permute-start | bytes 442376 | tf_op jit(solution)/shard_map/ppermute | solution.py:199
  8.1 4.7 %load.1 = (bf16[16,1024]{1,0:T(8,128)(2,1)S(1)}, bf16[2,1024,2048]{2,1,0:T(8,128)(2,1)S(1)}, bf16[2,1024,1024]{2,1,0:T(8,128)(2,1)S(1)}) custom-call(bf16[2,1024]{1,0:T(2,128)(2,1)} %bitcast.4, bf16[2,1024,2048]{2,1,0:T(8,128)(2,1)} %refs_1_.3, bf16[2,1024,1024]{2,1,0:T(8,128)(2,1)} %refs_2_.1, bf16[64,1152]{1,0:T(8,128)(2,1)S(1)} %pack.1.refs_3_.refs_1_), custom_call_target="tpu_custom_call" | custom-call | bytes 10000 | tf_op jit(solution)/shard_map/load/pallas_call | solution.py:177
  14.5 4.1 %collective-permute-done.5.refs_1_ = bf16[64,1152]{1,0:T(8,128)(2,1)S(1)} collective-permute-done((bf16[64,1152]{1,0:T(8,128)(2,1)S(1)}, bf16[64,1152]{1,0:T(8,128)(2,1)S(1)}, u32[]{:S(2)}, u32[]{:S(2)}) %collective-permute-start.5) | collective-permute-done | bytes 147488 | tf_op jit(solution)/shard_map/ppermute | solution.py:199
  19.5 3.3 %copy-done = bf16[2,1024,2048]{2,1,0:T(8,128)(2,1)} copy-done((bf16[2,1024,2048]{2,1,0:T(8,128)(2,1)}, bf16[2,1024,2048]{2,1,0:T(8,128)(2,1)S(1)}, u32[]{:S(2)}) %copy-start) | copy-done | bytes 8388632
  22.8 2.1 %copy-done.6 = bf16[2,1024,1024]{2,1,0:T(8,128)(2,1)} copy-done((bf16[2,1024,1024]{2,1,0:T(8,128)(2,1)}, bf16[2,1024,1024]{2,1,0:T(8,128)(2,1)S(1)}, u32[]{:S(2)}) %copy-start.6) | copy-done | bytes 4194328
  26.9 3.4 %copy-done.1 = bf16[2,1024,2048]{2,1,0:T(8,128)(2,1)S(1)} copy-done((bf16[2,1024,2048]{2,1,0:T(8,128)(2,1)S(1)}, bf16[2,1024,2048]{2,1,0:T(8,128)(2,1)}, u32[]{:S(2)}) %copy-start.1) | copy-done | bytes 8388632
  30.3 2.2 %copy-done.7 = bf16[2,1024,1024]{2,1,0:T(8,128)(2,1)S(1)} copy-done((bf16[2,1024,1024]{2,1,0:T(8,128)(2,1)S(1)}, bf16[2,1024,1024]{2,1,0:T(8,128)(2,1)}, u32[]{:S(2)}) %copy-start.7) | copy-done | bytes 4194328
  32.5 2.9 %expert.4 = (f32[128,1152]{1,0:T(8,128)S(1)}, bf16[64,1152]{1,0:T(8,128)(2,1)S(1)}, bf16[64,1152]{1,0:T(8,128)(2,1)S(1)}, bf16[16,1024]{1,0:T(8,128)(2,1)S(1)}, ...) custom-call(s32[1]{0:T(128)} %bitcast.refs_0_, ...), custom_call_target="tpu_custom_call", output_to_operand_aliasing={{3}: (5, {}), {4}: (6, {}), {5}: (7, {})} | custom-call | bytes 10000 | tf_op jit(solution)/shard_map/expert/pallas_call | solution.py:177
  37.6 2.9 %expert.5 = (f32[128,1152]{1,0:T(8,128)S(1)}, bf16[64,1152]{1,0:T(8,128)(2,1)S(1)}, bf16[64,1152]{1,0:T(8,128)(2,1)S(1)}, bf16[16,1024]{1,0:T(8,128)(2,1)S(1)}, ...) custom-call(s32[1]{0:T(128)} %bitcast.refs_0_, ...), custom_call_target="tpu_custom_call", output_to_operand_aliasing={{3}: (5, {}), {4}: (6, {}), {5}: (7, {})} | custom-call | bytes 10000 | tf_op jit(solution)/shard_map/expert/pallas_call | solution.py:177
  41.6 1.6 %collective-permute-done.19.refs_1_ = bf16[64,1152]{1,0:T(8,128)(2,1)S(1)} collective-permute-done((bf16[64,1152]{1,0:T(8,128)(2,1)S(1)}, bf16[64,1152]{1,0:T(8,128)(2,1)S(1)}, u32[]{:S(2)}, u32[]{:S(2)}) %collective-permute-start.19) | collective-permute-done | bytes 147488 | tf_op jit(solution)/shard_map/ppermute | solution.py:199
  43.9 2.9 %expert.6 = (f32[128,1152]{1,0:T(8,128)S(1)}, bf16[64,1152]{1,0:T(8,128)(2,1)S(1)}, bf16[64,1152]{1,0:T(8,128)(2,1)S(1)}, bf16[16,1024]{1,0:T(8,128)(2,1)S(1)}, ...) custom-call(s32[1]{0:T(128)} %bitcast.refs_0_, ...), custom_call_target="tpu_custom_call", output_to_operand_aliasing={{3}: (5, {}), {4}: (6, {}), {5}: (7, {})} | custom-call | bytes 10000 | tf_op jit(solution)/shard_map/expert/pallas_call | solution.py:177
  48.6 3.4 %collective-permute-start.26 = (bf16[64,1152]{1,0:T(8,128)(2,1)S(1)}, bf16[64,1152]{1,0:T(8,128)(2,1)S(1)}, u32[]{:S(2)}, u32[]{:S(2)}) collective-permute-start(bf16[64,1152]{1,0:T(8,128)(2,1)S(1)} %get-tuple-element.138), channel_id=1, source_target_pairs={{0,8},{1,9},{2,10},{3,11},{4,12},{5,13},{6,14},{7,15},{8,0},{9,1},... | collective-permute-start | bytes 442376 | tf_op jit(solution)/shard_map/ppermute | solution.py:199
  52.1 3.3 %copy-done.2 = bf16[2,1024,2048]{2,1,0:T(8,128)(2,1)} copy-done((bf16[2,1024,2048]{2,1,0:T(8,128)(2,1)}, bf16[2,1024,2048]{2,1,0:T(8,128)(2,1)S(1)}, u32[]{:S(2)}) %copy-start.2) | copy-done | bytes 8388632
  55.4 2.1 %copy-done.8 = bf16[2,1024,1024]{2,1,0:T(8,128)(2,1)} copy-done((bf16[2,1024,1024]{2,1,0:T(8,128)(2,1)}, bf16[2,1024,1024]{2,1,0:T(8,128)(2,1)S(1)}, u32[]{:S(2)}) %copy-start.8) | copy-done | bytes 4194328
  58.8 3.4 %copy-done.3 = bf16[2,1024,2048]{2,1,0:T(8,128)(2,1)S(1)} copy-done((bf16[2,1024,2048]{2,1,0:T(8,128)(2,1)S(1)}, bf16[2,1024,2048]{2,1,0:T(8,128)(2,1)}, u32[]{:S(2)}) %copy-start.3) | copy-done | bytes 8388632
  62.2 2.2 %copy-done.9 = bf16[2,1024,1024]{2,1,0:T(8,128)(2,1)S(1)} copy-done((bf16[2,1024,1024]{2,1,0:T(8,128)(2,1)S(1)}, bf16[2,1024,1024]{2,1,0:T(8,128)(2,1)}, u32[]{:S(2)}) %copy-start.9) | copy-done | bytes 4194328
  64.3 2.9 %expert.7 = (f32[128,1152]{1,0:T(8,128)S(1)}, bf16[64,1152]{1,0:T(8,128)(2,1)S(1)}, bf16[64,1152]{1,0:T(8,128)(2,1)S(1)}, bf16[16,1024]{1,0:T(8,128)(2,1)S(1)}, ...) custom-call(s32[1]{0:T(128)} %bitcast.refs_0_, ...), custom_call_target="tpu_custom_call", output_to_operand_aliasing={{3}: (5, {}), {4}: (6, {}), {5}: (7, {})} | custom-call | bytes 10000 | tf_op jit(solution)/shard_map/expert/pallas_call | solution.py:177
  67.2 3.3 %copy-done.4 = bf16[2,1024,2048]{2,1,0:T(8,128)(2,1)} copy-done((bf16[2,1024,2048]{2,1,0:T(8,128)(2,1)}, bf16[2,1024,2048]{2,1,0:T(8,128)(2,1)S(1)}, u32[]{:S(2)}) %copy-start.4) | copy-done | bytes 8388632
  70.5 2.1 %copy-done.10 = bf16[2,1024,1024]{2,1,0:T(8,128)(2,1)} copy-done((bf16[2,1024,1024]{2,1,0:T(8,128)(2,1)}, bf16[2,1024,1024]{2,1,0:T(8,128)(2,1)S(1)}, u32[]{:S(2)}) %copy-start.10) | copy-done | bytes 4194328
  73.2 3.4 %copy-done.5 = bf16[2,1024,2048]{2,1,0:T(8,128)(2,1)S(1)} copy-done((bf16[2,1024,2048]{2,1,0:T(8,128)(2,1)S(1)}, bf16[2,1024,2048]{2,1,0:T(8,128)(2,1)}, u32[]{:S(2)}) %copy-start.5) | copy-done | bytes 8388632
  76.6 2.2 %copy-done.11 = bf16[2,1024,1024]{2,1,0:T(8,128)(2,1)S(1)} copy-done((bf16[2,1024,1024]{2,1,0:T(8,128)(2,1)S(1)}, bf16[2,1024,1024]{2,1,0:T(8,128)(2,1)}, u32[]{:S(2)}) %copy-start.11) | copy-done | bytes 4194328
  80.8 3.9 %collective-permute-done.27.refs_1_ = bf16[64,1152]{1,0:T(8,128)(2,1)S(1)} collective-permute-done((bf16[64,1152]{1,0:T(8,128)(2,1)S(1)}, bf16[64,1152]{1,0:T(8,128)(2,1)S(1)}, u32[]{:S(2)}, u32[]{:S(2)}) %collective-permute-start.27) | collective-permute-done | bytes 147488 | tf_op jit(solution)/shard_map/ppermute | solution.py:199
  (78 shorter events, 16.6 us)
Async XLA Ops:
  0.9 11.9 %collective-permute-start = (bf16[64,1152]{1,0:T(8,128)(2,1)S(1)}, bf16[64,1152]{1,0:T(8,128)(2,1)S(1)}, u32[]{:S(2)}, u32[]{:S(2)}) collective-permute-start(bf16[64,1152]{1,0:T(8,128)(2,1)S(1)} %pack.1.refs_3_.refs_1_), channel_id=1, source_target_pairs={{0,2},{1,3},{2,0},{3,1},{4,6},{5,7},{6,4},{7,5},{8,10},{9,11},{10,... | collective-permute-start | bytes 442376 | tf_op jit(solution)/shard_map/ppermute | solution.py:199
  4.0 9.5 %collective-permute-start.4 = (bf16[64,1152]{1,0:T(8,128)(2,1)S(1)}, bf16[64,1152]{1,0:T(8,128)(2,1)S(1)}, u32[]{:S(2)}, u32[]{:S(2)}) collective-permute-start(bf16[64,1152]{1,0:T(8,128)(2,1)S(1)} %pack.1.refs_3_.refs_1_), channel_id=1, source_target_pairs={{0,8},{1,9},{2,10},{3,11},{4,12},{5,13},{6,14},{7,15},{8,0},{9,1},... | collective-permute-start | bytes 442376 | tf_op jit(solution)/shard_map/ppermute | solution.py:199
  6.6 8.0 %collective-permute-start.3 = (bf16[64,1152]{1,0:T(8,128)(2,1)S(1)}, bf16[64,1152]{1,0:T(8,128)(2,1)S(1)}, u32[]{:S(2)}, u32[]{:S(2)}) collective-permute-start(bf16[64,1152]{1,0:T(8,128)(2,1)S(1)} %pack.1.refs_3_.refs_1_), channel_id=1, source_target_pairs={{0,4},{1,5},{2,6},{3,7},{4,0},{5,1},{6,2},{7,3},{8,12},{9,13},{10,... | collective-permute-start | bytes 442376 | tf_op jit(solution)/shard_map/ppermute | solution.py:199
  13.4 5.1 %collective-permute-start.5 = (bf16[64,1152]{1,0:T(8,128)(2,1)S(1)}, bf16[64,1152]{1,0:T(8,128)(2,1)S(1)}, u32[]{:S(2)}, u32[]{:S(2)}) collective-permute-start(bf16[64,1152]{1,0:T(8,128)(2,1)S(1)} %get-tuple-element.80.refs_1_), channel_id=1, source_target_pairs={{0,4},{1,5},{2,6},{3,7},{4,0},{5,1},{6,2},{7,3},{8,12},{9,13},{10,... | collective-permute-start | bytes 442376 | tf_op jit(solution)/shard_map/ppermute | solution.py:199
  14.0 5.5 %collective-permute-start.6 = (bf16[64,1152]{1,0:T(8,128)(2,1)S(1)}, bf16[64,1152]{1,0:T(8,128)(2,1)S(1)}, u32[]{:S(2)}, u32[]{:S(2)}) collective-permute-start(bf16[64,1152]{1,0:T(8,128)(2,1)S(1)} %get-tuple-element.80.refs_1_), channel_id=1, source_target_pairs={{0,2},{1,3},{2,0},{3,1},{4,6},{5,7},{6,4},{7,5},{8,10},{9,11},{10,... | collective-permute-start | bytes 442376 | tf_op jit(solution)/shard_map/ppermute | solution.py:199
  14.5 12.4 %collective-permute-start.7 = (bf16[64,1152]{1,0:T(8,128)(2,1)S(1)}, bf16[64,1152]{1,0:T(8,128)(2,1)S(1)}, u32[]{:S(2)}, u32[]{:S(2)}) collective-permute-start(bf16[64,1152]{1,0:T(8,128)(2,1)S(1)} %get-tuple-element.80.refs_1_), channel_id=1, source_target_pairs={{0,1},{1,0},{2,3},{3,2},{4,5},{5,4},{6,7},{7,6},{8,9},{9,8},{10,11... | collective-permute-start | bytes 442376 | tf_op jit(solution)/shard_map/ppermute | solution.py:199
  24.9 11.1 %collective-permute-start.9 = (bf16[64,1152]{1,0:T(8,128)(2,1)S(1)}, bf16[64,1152]{1,0:T(8,128)(2,1)S(1)}, u32[]{:S(2)}, u32[]{:S(2)}) collective-permute-start(bf16[64,1152]{1,0:T(8,128)(2,1)S(1)} %collective-permute-done.5.refs_1_), channel_id=1, source_target_pairs={{0,2},{1,3},{2,0},{3,1},{4,6},{5,7},{6,4},{7,5},{8,10},{9,11},{10,... | collective-permute-start | bytes 442376 | tf_op jit(solution)/shard_map/ppermute | solution.py:199
  25.4 11.1 %collective-permute-start.10 = (bf16[64,1152]{1,0:T(8,128)(2,1)S(1)}, bf16[64,1152]{1,0:T(8,128)(2,1)S(1)}, u32[]{:S(2)}, u32[]{:S(2)}) collective-permute-start(bf16[64,1152]{1,0:T(8,128)(2,1)S(1)} %collective-permute-done.3.refs_0_.refs_1_), channel_id=1, source_target_pairs={{0,2},{1,3},{2,0},{3,1},{4,6},{5,7},{6,4},{7,5},{8,10},{9,11},{10,... | collective-permute-start | bytes 442376 | tf_op jit(solution)/shard_map/ppermute | solution.py:199
  37.1 6.1 %collective-permute-start.19 = (bf16[64,1152]{1,0:T(8,128)(2,1)S(1)}, bf16[64,1152]{1,0:T(8,128)(2,1)S(1)}, u32[]{:S(2)}, u32[]{:S(2)}) collective-permute-start(bf16[64,1152]{1,0:T(8,128)(2,1)S(1)} %get-tuple-element.109), channel_id=1, source_target_pairs={{0,2},{1,3},{2,0},{3,1},{4,6},{5,7},{6,4},{7,5},{8,10},{9,11},{10,... | collective-permute-start | bytes 442376 | tf_op jit(solution)/shard_map/ppermute | solution.py:199
  40.5 2.7 %collective-permute-start.17 = (bf16[64,1152]{1,0:T(8,128)(2,1)S(1)}, bf16[64,1152]{1,0:T(8,128)(2,1)S(1)}, u32[]{:S(2)}, u32[]{:S(2)}) collective-permute-start(bf16[64,1152]{1,0:T(8,128)(2,1)S(1)} %get-tuple-element.106), channel_id=1, source_target_pairs={{0,1},{1,0},{2,3},{3,2},{4,5},{5,4},{6,7},{7,6},{8,9},{9,8},{10,11... | collective-permute-start | bytes 442376 | tf_op jit(solution)/shard_map/ppermute | solution.py:199
  41.1 2.8 %collective-permute-start.11 = (bf16[64,1152]{1,0:T(8,128)(2,1)S(1)}, bf16[64,1152]{1,0:T(8,128)(2,1)S(1)}, u32[]{:S(2)}, u32[]{:S(2)}) collective-permute-start(bf16[64,1152]{1,0:T(8,128)(2,1)S(1)} %collective-permute-done.3.refs_0_.refs_1_), channel_id=1, source_target_pairs={{0,1},{1,0},{2,3},{3,2},{4,5},{5,4},{6,7},{7,6},{8,9},{9,8},{10,11... | collective-permute-start | bytes 442376 | tf_op jit(solution)/shard_map/ppermute | solution.py:199
  41.3 2.6 %collective-permute-start.12 = (bf16[64,1152]{1,0:T(8,128)(2,1)S(1)}, bf16[64,1152]{1,0:T(8,128)(2,1)S(1)}, u32[]{:S(2)}, u32[]{:S(2)}) collective-permute-start(bf16[64,1152]{1,0:T(8,128)(2,1)S(1)} %get-tuple-element.94.refs_2_), channel_id=1, source_target_pairs={{0,1},{1,0},{2,3},{3,2},{4,5},{5,4},{6,7},{7,6},{8,9},{9,8},{10,11... | collective-permute-start | bytes 442376 | tf_op jit(solution)/shard_map/ppermute | solution.py:199
  43.3 5.3 %collective-permute-start.22 = (bf16[64,1152]{1,0:T(8,128)(2,1)S(1)}, bf16[64,1152]{1,0:T(8,128)(2,1)S(1)}, u32[]{:S(2)}, u32[]{:S(2)}) collective-permute-start(bf16[64,1152]{1,0:T(8,128)(2,1)S(1)} %get-tuple-element.123), channel_id=1, source_target_pairs={{0,2},{1,3},{2,0},{3,1},{4,6},{5,7},{6,4},{7,5},{8,10},{9,11},{10,... | collective-permute-start | bytes 442376 | tf_op jit(solution)/shard_map/ppermute | solution.py:199
  46.8 5.3 %collective-permute-start.20 = (bf16[64,1152]{1,0:T(8,128)(2,1)S(1)}, bf16[64,1152]{1,0:T(8,128)(2,1)S(1)}, u32[]{:S(2)}, u32[]{:S(2)}) collective-permute-start(bf16[64,1152]{1,0:T(8,128)(2,1)S(1)} %get-tuple-element.120), channel_id=1, source_target_pairs={{0,1},{1,0},{2,3},{3,2},{4,5},{5,4},{6,7},{7,6},{8,9},{9,8},{10,11... | collective-permute-start | bytes 442376 | tf_op jit(solution)/shard_map/ppermute | solution.py:199
  46.9 5.2 %collective-permute-start.21 = (bf16[64,1152]{1,0:T(8,128)(2,1)S(1)}, bf16[64,1152]{1,0:T(8,128)(2,1)S(1)}, u32[]{:S(2)}, u32[]{:S(2)}) collective-permute-start(bf16[64,1152]{1,0:T(8,128)(2,1)S(1)} %get-tuple-element.121), channel_id=1, source_target_pairs={{0,1},{1,0},{2,3},{3,2},{4,5},{5,4},{6,7},{7,6},{8,9},{9,8},{10,11... | collective-permute-start | bytes 442376 | tf_op jit(solution)/shard_map/ppermute | solution.py:199
  47.4 11.4 %collective-permute-start.1 = (bf16[64,1152]{1,0:T(8,128)(2,1)S(1)}, bf16[64,1152]{1,0:T(8,128)(2,1)S(1)}, u32[]{:S(2)}, u32[]{:S(2)}) collective-permute-start(bf16[64,1152]{1,0:T(8,128)(2,1)S(1)} %pack.1.refs_3_.refs_1_), channel_id=1, source_target_pairs={{0,1},{1,0},{2,3},{3,2},{4,5},{5,4},{6,7},{7,6},{8,9},{9,8},{10,11... | collective-permute-start | bytes 442376 | tf_op jit(solution)/shard_map/ppermute | solution.py:199
  47.4 11.3 %collective-permute-start.2 = (bf16[64,1152]{1,0:T(8,128)(2,1)S(1)}, bf16[64,1152]{1,0:T(8,128)(2,1)S(1)}, u32[]{:S(2)}, u32[]{:S(2)}) collective-permute-start(bf16[64,1152]{1,0:T(8,128)(2,1)S(1)} %collective-permute-done.refs_0_.refs_2_), channel_id=1, source_target_pairs={{0,1},{1,0},{2,3},{3,2},{4,5},{5,4},{6,7},{7,6},{8,9},{9,8},{10,11... | collective-permute-start | bytes 442376 | tf_op jit(solution)/shard_map/ppermute | solution.py:199
  48.6 24.6 %collective-permute-start.26 = (bf16[64,1152]{1,0:T(8,128)(2,1)S(1)}, bf16[64,1152]{1,0:T(8,128)(2,1)S(1)}, u32[]{:S(2)}, u32[]{:S(2)}) collective-permute-start(bf16[64,1152]{1,0:T(8,128)(2,1)S(1)} %get-tuple-element.138), channel_id=1, source_target_pairs={{0,8},{1,9},{2,10},{3,11},{4,12},{5,13},{6,14},{7,15},{8,0},{9,1},... | collective-permute-start | bytes 442376 | tf_op jit(solution)/shard_map/ppermute | solution.py:199
  57.5 15.7 %collective-permute-start.25 = (bf16[64,1152]{1,0:T(8,128)(2,1)S(1)}, bf16[64,1152]{1,0:T(8,128)(2,1)S(1)}, u32[]{:S(2)}, u32[]{:S(2)}) collective-permute-start(bf16[64,1152]{1,0:T(8,128)(2,1)S(1)} %get-tuple-element.137), channel_id=1, source_target_pairs={{0,2},{1,3},{2,0},{3,1},{4,6},{5,7},{6,4},{7,5},{8,10},{9,11},{10,... | collective-permute-start | bytes 442376 | tf_op jit(solution)/shard_map/ppermute | solution.py:199
  72.6 6.2 %collective-permute-start.23 = (bf16[64,1152]{1,0:T(8,128)(2,1)S(1)}, bf16[64,1152]{1,0:T(8,128)(2,1)S(1)}, u32[]{:S(2)}, u32[]{:S(2)}) collective-permute-start(bf16[64,1152]{1,0:T(8,128)(2,1)S(1)} %get-tuple-element.134), channel_id=1, source_target_pairs={{0,1},{1,0},{2,3},{3,2},{4,5},{5,4},{6,7},{7,6},{8,9},{9,8},{10,11... | collective-permute-start | bytes 442376 | tf_op jit(solution)/shard_map/ppermute | solution.py:199
  72.6 6.2 %collective-permute-start.24 = (bf16[64,1152]{1,0:T(8,128)(2,1)S(1)}, bf16[64,1152]{1,0:T(8,128)(2,1)S(1)}, u32[]{:S(2)}, u32[]{:S(2)}) collective-permute-start(bf16[64,1152]{1,0:T(8,128)(2,1)S(1)} %get-tuple-element.135), channel_id=1, source_target_pairs={{0,1},{1,0},{2,3},{3,2},{4,5},{5,4},{6,7},{7,6},{8,9},{9,8},{10,11... | collective-permute-start | bytes 442376 | tf_op jit(solution)/shard_map/ppermute | solution.py:199
  73.1 7.7 %collective-permute-start.29 = (bf16[64,1152]{1,0:T(8,128)(2,1)S(1)}, bf16[64,1152]{1,0:T(8,128)(2,1)S(1)}, u32[]{:S(2)}, u32[]{:S(2)}) collective-permute-start(bf16[64,1152]{1,0:T(8,128)(2,1)S(1)} %get-tuple-element.148), channel_id=1, source_target_pairs={{0,12},{1,13},{2,14},{3,15},{4,8},{5,9},{6,10},{7,11},{8,4},{9,5},... | collective-permute-start | bytes 442376 | tf_op jit(solution)/shard_map/ppermute | solution.py:199
  78.9 5.7 %collective-permute-start.27 = (bf16[64,1152]{1,0:T(8,128)(2,1)S(1)}, bf16[64,1152]{1,0:T(8,128)(2,1)S(1)}, u32[]{:S(2)}, u32[]{:S(2)}) collective-permute-start(bf16[64,1152]{1,0:T(8,128)(2,1)S(1)} %get-tuple-element.146), channel_id=1, source_target_pairs={{0,2},{1,3},{2,0},{3,1},{4,6},{5,7},{6,4},{7,5},{8,10},{9,11},{10,... | collective-permute-start | bytes 442376 | tf_op jit(solution)/shard_map/ppermute | solution.py:199
  79.7 5.4 %collective-permute-start.28 = (bf16[64,1152]{1,0:T(8,128)(2,1)S(1)}, bf16[64,1152]{1,0:T(8,128)(2,1)S(1)}, u32[]{:S(2)}, u32[]{:S(2)}) collective-permute-start(bf16[64,1152]{1,0:T(8,128)(2,1)S(1)} %get-tuple-element.147), channel_id=1, source_target_pairs={{0,4},{1,5},{2,6},{3,7},{4,0},{5,1},{6,2},{7,3},{8,12},{9,13},{10,... | collective-permute-start | bytes 442376 | tf_op jit(solution)/shard_map/ppermute | solution.py:199
  (18 other events, 43.7 us)

commit v10 on v9

--- a/solution.py
+++ b/solution.py
@@ -49,7 +49,7 @@
 
 
 def expert_kernel(
-    first_ref, a_ref, b_ref, c_ref, d_ref, columns_ref, up_ref, down_ref, keep_ref, *refs
+    a_ref, b_ref, c_ref, d_ref, columns_ref, up_ref, down_ref, keep_ref, *refs
 ):
     *send_refs, inner_ref, result_ref = refs
     blocks = (a_ref, b_ref, c_ref, d_ref)
@@ -75,7 +75,7 @@
     masks, sums = [], jnp.zeros((2 * half, 1), jnp.float32)
     marks = jnp.zeros((2 * half, TAIL), jnp.float32)
     for e in range(local):
-        label = (first_ref[0] + e).astype(jnp.float32)
+        label = (lax.axis_index("exp") * local + e).astype(jnp.float32)
         mask = jnp.max(jnp.where(tail == label, 1.0, 0.0), axis=1, keepdims=True)
         sums = sums + jax.nn.sigmoid(logits[:, e : e + 1]) * (mask * SCALE)
         marks = jnp.where(lane == e, mask, marks)
@@ -154,8 +154,8 @@
 ANY = pl.BlockSpec(memory_space=pl.ANY)
 
 
-def call(kernel, outs, args=(), deps=(), chain=(), smem=(), hbm=(), scratch=()):
-    n_in = len(smem) + len(args) + len(hbm)
+def call(kernel, outs, args=(), deps=(), chain=(), hbm=(), scratch=()):
+    n_in = len(args) + len(hbm)
     n_skip = n_in + len(deps)
     n_outs = n_skip + len(chain)
 
@@ -170,9 +170,9 @@
             *refs[n_outs + len(outs) + len(chain) :],
         )
 
-    specs = [pl.BlockSpec(memory_space=pltpu.SMEM)] * len(smem) + [VMEM] * len(args)
+    specs = [VMEM] * len(args)
     specs += [ANY] * (len(hbm) + len(deps)) + [VMEM] * len(chain)
-    operands = list(smem) + [in_vmem(a) for a in args] + [in_hbm(h) for h in hbm]
+    operands = [in_vmem(a) for a in args] + [in_hbm(h) for h in hbm]
     operands += [in_vmem(x) for x in (*deps, *chain)]
     return pl.pallas_call(
         body_with_chain if kernel is expert_kernel else body,
@@ -193,7 +193,6 @@
     eff = expert_down.shape[1]
     rows, lat = latent_in.shape
     wide = lat + TAIL
-    first = (lax.axis_index("exp") * local).astype(jnp.int32).reshape(1)
 
     def swap(x, bits):
         return lax.ppermute(x, "exp", [(i, i ^ bits) for i in range(n_dev)])
@@ -244,7 +243,6 @@
                 expert_kernel,
                 [space(2 * rows, jnp.float32), space(rows, jnp.bfloat16), space(rows, jnp.bfloat16)],
                 blocks,
-                smem=[first],
                 scratch=[
                     pltpu.VMEM((local * slots, eff), jnp.bfloat16),
                     pltpu.VMEM((local * slots, lat), jnp.bfloat16),

time: 86.2 us -> 60.7 us (0.70)
  local copies, waits for them, and re-layouts: 32.8 us -> 0 us
  starting transfers between devices: 21.2 us -> 26.1 us
  waiting for transfers between devices: 13.4 us -> 15.9 us
    unnamed x24 -> x0, local copies, waits for them, and re-layouts: 32.8 us -> none
    ppermute x30, starting transfers between devices: 21.2 us -> 26.1 us  [swap(): return lax.ppermute(x, 'exp', [(i, i ^ bits) for i in range(n_dev)])]
    ppermute x30, waiting for transfers between devices: 13.4 us -> 15.9 us  [swap(): return lax.ppermute(x, 'exp', [(i, i ^ bits) for i in range(n_dev)])]
  transfers between devices with their start and end apart: 30 -> 30, of which waited for: 10 -> 10; matrix products, arithmetic and copies ran while one was open for 0% -> 0% of each run, Pallas kernels for 19% -> 27%
where the time goes in v10:
time: 60.7 us; the launch traced here: 60.5 us
  starting transfers between devices  26.1 us (43%)
  Pallas kernels  18.3 us (30%)
  waiting for transfers between devices  15.9 us (26%)
    ppermute x30, starting transfers between devices, swap(): return lax.ppermute(x, 'exp', [(i, i ^ bits) for i in range(n_dev)])  26.1 us
    pallas_call x17, Pallas kernels, call(): pl.pallas_call(body_with_chain if kernel is expert_kernel else body, out_...  17.5 us
    ppermute x30, waiting for transfers between devices, swap(): return lax.ppermute(x, 'exp', [(i, i ^ bits) for i in range(n_dev)])  15.9 us
  transfers between devices with their start and end apart: 30, of which 10 were waited for; matrix products, arithmetic and copies ran while one was open for 0% of the time, Pallas kernels for 27%

profile of v10, /device:TPU:0, one launch (start us, length us, event | category | flops | bytes accessed | tf_op | source)
XLA Modules:
  0.0 60.5 jit_solution(12982828713759741786)
XLA Ops:
  0.0 0.9 %pack.1.refs_3_.refs_0_ = bf16[64,1152]{1,0:T(8,128)(2,1)S(1)} custom-call(s32[8,64]{1,0:T(8,128)} %bitcast.2, bf16[64,1024]{1,0:T(8,128)(2,1)} %refs_1_.2), custom_call_target="tpu_custom_call" | custom-call | bytes 10000 | tf_op jit(solution)/shard_map/pack/pallas_call | solution.py:177
  0.9 3.0 %collective-permute-start = (bf16[64,1152]{1,0:T(8,128)(2,1)S(1)}, bf16[64,1152]{1,0:T(8,128)(2,1)S(1)}, u32[]{:S(2)}, u32[]{:S(2)}) collective-permute-start(bf16[64,1152]{1,0:T(8,128)(2,1)S(1)} %pack.1.refs_3_.refs_0_), channel_id=1, source_target_pairs={{0,2},{1,3},{2,0},{3,1},{4,6},{5,7},{6,4},{7,5},{8,10},{9,11},{10,... | collective-permute-start | bytes 442376 | tf_op jit(solution)/shard_map/ppermute | solution.py:198
  4.0 2.6 %collective-permute-start.4 = (bf16[64,1152]{1,0:T(8,128)(2,1)S(1)}, bf16[64,1152]{1,0:T(8,128)(2,1)S(1)}, u32[]{:S(2)}, u32[]{:S(2)}) collective-permute-start(bf16[64,1152]{1,0:T(8,128)(2,1)S(1)} %pack.1.refs_3_.refs_0_), channel_id=1, source_target_pairs={{0,8},{1,9},{2,10},{3,11},{4,12},{5,13},{6,14},{7,15},{8,0},{9,1},... | collective-permute-start | bytes 442376 | tf_op jit(solution)/shard_map/ppermute | solution.py:198
  6.6 1.6 %collective-permute-start.3 = (bf16[64,1152]{1,0:T(8,128)(2,1)S(1)}, bf16[64,1152]{1,0:T(8,128)(2,1)S(1)}, u32[]{:S(2)}, u32[]{:S(2)}) collective-permute-start(bf16[64,1152]{1,0:T(8,128)(2,1)S(1)} %pack.1.refs_3_.refs_0_), channel_id=1, source_target_pairs={{0,4},{1,5},{2,6},{3,7},{4,0},{5,1},{6,2},{7,3},{8,12},{9,13},{10,... | collective-permute-start | bytes 442376 | tf_op jit(solution)/shard_map/ppermute | solution.py:198
  8.1 4.7 %load.1 = (bf16[16,1024]{1,0:T(8,128)(2,1)S(1)}, bf16[2,1024,2048]{2,1,0:T(8,128)(2,1)S(1)}, bf16[2,1024,1024]{2,1,0:T(8,128)(2,1)S(1)}) custom-call(bf16[2,1024]{1,0:T(2,128)(2,1)} %bitcast.3, bf16[2,1024,2048]{2,1,0:T(8,128)(2,1)} %refs_1_.3, bf16[2,1024,1024]{2,1,0:T(8,128)(2,1)} %refs_2_.1, bf16[64,1152]{1,0:T(8,128)(2,1)S(1)} %pack.1.refs_3_.refs_0_), custom_call_target="tpu_custom_call" | custom-call | bytes 10000 | tf_op jit(solution)/shard_map/load/pallas_call | solution.py:177
  14.5 4.1 %collective-permute-done.5.refs_1_.refs_0_ = bf16[64,1152]{1,0:T(8,128)(2,1)S(1)} collective-permute-done((bf16[64,1152]{1,0:T(8,128)(2,1)S(1)}, bf16[64,1152]{1,0:T(8,128)(2,1)S(1)}, u32[]{:S(2)}, u32[]{:S(2)}) %collective-permute-start.5) | collective-permute-done | bytes 147488 | tf_op jit(solution)/shard_map/ppermute | solution.py:198
  18.6 0.9 %collective-permute-done.6.refs_5_ = bf16[64,1152]{1,0:T(8,128)(2,1)S(1)} collective-permute-done((bf16[64,1152]{1,0:T(8,128)(2,1)S(1)}, bf16[64,1152]{1,0:T(8,128)(2,1)S(1)}, u32[]{:S(2)}, u32[]{:S(2)}) %collective-permute-start.6) | collective-permute-done | bytes 147488 | tf_op jit(solution)/shard_map/ppermute | solution.py:198
  20.0 1.5 %collective-permute-start.10 = (bf16[64,1152]{1,0:T(8,128)(2,1)S(1)}, bf16[64,1152]{1,0:T(8,128)(2,1)S(1)}, u32[]{:S(2)}, u32[]{:S(2)}) collective-permute-start(bf16[64,1152]{1,0:T(8,128)(2,1)S(1)} %collective-permute-done.3.refs_0_), channel_id=1, source_target_pairs={{0,2},{1,3},{2,0},{3,1},{4,6},{5,7},{6,4},{7,5},{8,10},{9,11},{10,... | collective-permute-start | bytes 442376 | tf_op jit(solution)/shard_map/ppermute | solution.py:198
  21.5 2.9 %expert.4 = (f32[128,1152]{1,0:T(8,128)S(1)}, bf16[64,1152]{1,0:T(8,128)(2,1)S(1)}, bf16[64,1152]{1,0:T(8,128)(2,1)S(1)}, bf16[16,1024]{1,0:T(8,128)(2,1)S(1)}, ...) custom-call(bf16[64,1152]{1,0:T(8,128)(2,1)S(1)} %get-tuple-element., ...), custom_call_target="tpu_custom_call", output_to_operand_aliasing={{3}: (4, {}), {4}: (5, {}), {5}: (6, {})} | custom-call | bytes 10000 | tf_op jit(solution)/shard_map/expert/pallas_call | solution.py:177
  25.1 1.1 %collective-permute-done.9.refs_3_ = bf16[64,1152]{1,0:T(8,128)(2,1)S(1)} collective-permute-done((bf16[64,1152]{1,0:T(8,128)(2,1)S(1)}, bf16[64,1152]{1,0:T(8,128)(2,1)S(1)}, u32[]{:S(2)}, u32[]{:S(2)}) %collective-permute-start.9) | collective-permute-done | bytes 147488 | tf_op jit(solution)/shard_map/ppermute | solution.py:198
  26.2 2.8 %collective-permute-done.10.refs_3_ = bf16[64,1152]{1,0:T(8,128)(2,1)S(1)} collective-permute-done((bf16[64,1152]{1,0:T(8,128)(2,1)S(1)}, bf16[64,1152]{1,0:T(8,128)(2,1)S(1)}, u32[]{:S(2)}, u32[]{:S(2)}) %collective-permute-start.10) | collective-permute-done | bytes 147488 | tf_op jit(solution)/shard_map/ppermute | solution.py:198
  29.6 2.9 %expert.5 = (f32[128,1152]{1,0:T(8,128)S(1)}, bf16[64,1152]{1,0:T(8,128)(2,1)S(1)}, bf16[64,1152]{1,0:T(8,128)(2,1)S(1)}, bf16[16,1024]{1,0:T(8,128)(2,1)S(1)}, ...) custom-call(bf16[64,1152]{1,0:T(8,128)(2,1)S(1)} %collective-permute, ...), custom_call_target="tpu_custom_call", output_to_operand_aliasing={{3}: (4, {}), {4}: (5, {}), {5}: (6, {})} | custom-call | bytes 10000 | tf_op jit(solution)/shard_map/expert/pallas_call | solution.py:177
  33.6 1.0 %collective-permute-done.19.refs_1_ = bf16[64,1152]{1,0:T(8,128)(2,1)S(1)} collective-permute-done((bf16[64,1152]{1,0:T(8,128)(2,1)S(1)}, bf16[64,1152]{1,0:T(8,128)(2,1)S(1)}, u32[]{:S(2)}, u32[]{:S(2)}) %collective-permute-start.19) | collective-permute-done | bytes 147488 | tf_op jit(solution)/shard_map/ppermute | solution.py:198
  34.7 1.1 %collective-permute-start.22 = (bf16[64,1152]{1,0:T(8,128)(2,1)S(1)}, bf16[64,1152]{1,0:T(8,128)(2,1)S(1)}, u32[]{:S(2)}, u32[]{:S(2)}) collective-permute-start(bf16[64,1152]{1,0:T(8,128)(2,1)S(1)} %get-tuple-element.123), channel_id=1, source_target_pairs={{0,2},{1,3},{2,0},{3,1},{4,6},{5,7},{6,4},{7,5},{8,10},{9,11},{10,... | collective-permute-start | bytes 442376 | tf_op jit(solution)/shard_map/ppermute | solution.py:198
  35.8 2.9 %expert.6 = (f32[128,1152]{1,0:T(8,128)S(1)}, bf16[64,1152]{1,0:T(8,128)(2,1)S(1)}, bf16[64,1152]{1,0:T(8,128)(2,1)S(1)}, bf16[16,1024]{1,0:T(8,128)(2,1)S(1)}, ...) custom-call(bf16[64,1152]{1,0:T(8,128)(2,1)S(1)} %collective-permute, ...), custom_call_target="tpu_custom_call", output_to_operand_aliasing={{3}: (4, {}), {4}: (5, {}), {5}: (6, {})} | custom-call | bytes 10000 | tf_op jit(solution)/shard_map/expert/pallas_call | solution.py:177
  40.3 3.4 %collective-permute-start.26 = (bf16[64,1152]{1,0:T(8,128)(2,1)S(1)}, bf16[64,1152]{1,0:T(8,128)(2,1)S(1)}, u32[]{:S(2)}, u32[]{:S(2)}) collective-permute-start(bf16[64,1152]{1,0:T(8,128)(2,1)S(1)} %get-tuple-element.138), channel_id=1, source_target_pairs={{0,8},{1,9},{2,10},{3,11},{4,12},{5,13},{6,14},{7,15},{8,0},{9,1},... | collective-permute-start | bytes 442376 | tf_op jit(solution)/shard_map/ppermute | solution.py:198
  43.8 1.6 %collective-permute-start.25 = (bf16[64,1152]{1,0:T(8,128)(2,1)S(1)}, bf16[64,1152]{1,0:T(8,128)(2,1)S(1)}, u32[]{:S(2)}, u32[]{:S(2)}) collective-permute-start(bf16[64,1152]{1,0:T(8,128)(2,1)S(1)} %get-tuple-element.137), channel_id=1, source_target_pairs={{0,2},{1,3},{2,0},{3,1},{4,6},{5,7},{6,4},{7,5},{8,10},{9,11},{10,... | collective-permute-start | bytes 442376 | tf_op jit(solution)/shard_map/ppermute | solution.py:198
  45.4 2.9 %expert.7 = (f32[128,1152]{1,0:T(8,128)S(1)}, bf16[64,1152]{1,0:T(8,128)(2,1)S(1)}, bf16[64,1152]{1,0:T(8,128)(2,1)S(1)}, bf16[16,1024]{1,0:T(8,128)(2,1)S(1)}, ...) custom-call(bf16[64,1152]{1,0:T(8,128)(2,1)S(1)} %pack.1.refs_3_.ref, ...), custom_call_target="tpu_custom_call", output_to_operand_aliasing={{3}: (4, {}), {4}: (5, {}), {5}: (6, {})} | custom-call | bytes 10000 | tf_op jit(solution)/shard_map/expert/pallas_call | solution.py:177
  48.9 1.2 %collective-permute-done.26.refs_2_.refs_3_ = bf16[64,1152]{1,0:T(8,128)(2,1)S(1)} collective-permute-done((bf16[64,1152]{1,0:T(8,128)(2,1)S(1)}, bf16[64,1152]{1,0:T(8,128)(2,1)S(1)}, u32[]{:S(2)}, u32[]{:S(2)}) %collective-permute-start.26) | collective-permute-done | bytes 147488 | tf_op jit(solution)/shard_map/ppermute | solution.py:198
  50.3 1.5 %collective-permute-start.27 = (bf16[64,1152]{1,0:T(8,128)(2,1)S(1)}, bf16[64,1152]{1,0:T(8,128)(2,1)S(1)}, u32[]{:S(2)}, u32[]{:S(2)}) collective-permute-start(bf16[64,1152]{1,0:T(8,128)(2,1)S(1)} %get-tuple-element.146), channel_id=1, source_target_pairs={{0,2},{1,3},{2,0},{3,1},{4,6},{5,7},{6,4},{7,5},{8,10},{9,11},{10,... | collective-permute-start | bytes 442376 | tf_op jit(solution)/shard_map/ppermute | solution.py:198
  51.8 4.2 %collective-permute-start.28 = (bf16[64,1152]{1,0:T(8,128)(2,1)S(1)}, bf16[64,1152]{1,0:T(8,128)(2,1)S(1)}, u32[]{:S(2)}, u32[]{:S(2)}) collective-permute-start(bf16[64,1152]{1,0:T(8,128)(2,1)S(1)} %get-tuple-element.147), channel_id=1, source_target_pairs={{0,4},{1,5},{2,6},{3,7},{4,0},{5,1},{6,2},{7,3},{8,12},{9,13},{10,... | collective-permute-start | bytes 442376 | tf_op jit(solution)/shard_map/ppermute | solution.py:198
  56.0 1.4 %collective-permute-done.29.refs_4_ = bf16[64,1152]{1,0:T(8,128)(2,1)S(1)} collective-permute-done((bf16[64,1152]{1,0:T(8,128)(2,1)S(1)}, bf16[64,1152]{1,0:T(8,128)(2,1)S(1)}, u32[]{:S(2)}, u32[]{:S(2)}) %collective-permute-start.29) | collective-permute-done | bytes 147488 | tf_op jit(solution)/shard_map/ppermute | solution.py:198
  57.4 2.3 %collective-permute-done.28.refs_2_ = bf16[64,1152]{1,0:T(8,128)(2,1)S(1)} collective-permute-done((bf16[64,1152]{1,0:T(8,128)(2,1)S(1)}, bf16[64,1152]{1,0:T(8,128)(2,1)S(1)}, u32[]{:S(2)}, u32[]{:S(2)}) %collective-permute-start.28) | collective-permute-done | bytes 147488 | tf_op jit(solution)/shard_map/ppermute | solution.py:198
  59.7 0.8 %finish.1 = bf16[64,1024]{1,0:T(8,128)(2,1)} custom-call(f32[64,1152]{1,0:T(8,128)S(1)} %get-tuple-element.145.refs_0_, bf16[64,1152]{1,0:T(8,128)(2,1)S(1)} %collective-permute-done.27.refs_1_, bf16[64,1152]{1,0:T(8,128)(2,1)S(1)} %collective-permute-done.28.refs_2_, bf16[64,1152]{1,0:T(8,128)(2,1)S(1)} %collective-permute-done.26.refs_2_.refs_3_, ...), custom_call_target="tpu_custom_call" | custom-call | tf_op jit(solution)/shard_map/finish/pallas_call | solution.py:291
  (54 shorter events, 7.1 us)
Async XLA Ops:
  0.9 11.9 %collective-permute-start = (bf16[64,1152]{1,0:T(8,128)(2,1)S(1)}, bf16[64,1152]{1,0:T(8,128)(2,1)S(1)}, u32[]{:S(2)}, u32[]{:S(2)}) collective-permute-start(bf16[64,1152]{1,0:T(8,128)(2,1)S(1)} %pack.1.refs_3_.refs_0_), channel_id=1, source_target_pairs={{0,2},{1,3},{2,0},{3,1},{4,6},{5,7},{6,4},{7,5},{8,10},{9,11},{10,... | collective-permute-start | bytes 442376 | tf_op jit(solution)/shard_map/ppermute | solution.py:198
  4.0 9.5 %collective-permute-start.4 = (bf16[64,1152]{1,0:T(8,128)(2,1)S(1)}, bf16[64,1152]{1,0:T(8,128)(2,1)S(1)}, u32[]{:S(2)}, u32[]{:S(2)}) collective-permute-start(bf16[64,1152]{1,0:T(8,128)(2,1)S(1)} %pack.1.refs_3_.refs_0_), channel_id=1, source_target_pairs={{0,8},{1,9},{2,10},{3,11},{4,12},{5,13},{6,14},{7,15},{8,0},{9,1},... | collective-permute-start | bytes 442376 | tf_op jit(solution)/shard_map/ppermute | solution.py:198
  6.6 8.0 %collective-permute-start.3 = (bf16[64,1152]{1,0:T(8,128)(2,1)S(1)}, bf16[64,1152]{1,0:T(8,128)(2,1)S(1)}, u32[]{:S(2)}, u32[]{:S(2)}) collective-permute-start(bf16[64,1152]{1,0:T(8,128)(2,1)S(1)} %pack.1.refs_3_.refs_0_), channel_id=1, source_target_pairs={{0,4},{1,5},{2,6},{3,7},{4,0},{5,1},{6,2},{7,3},{8,12},{9,13},{10,... | collective-permute-start | bytes 442376 | tf_op jit(solution)/shard_map/ppermute | solution.py:198
  13.4 5.1 %collective-permute-start.5 = (bf16[64,1152]{1,0:T(8,128)(2,1)S(1)}, bf16[64,1152]{1,0:T(8,128)(2,1)S(1)}, u32[]{:S(2)}, u32[]{:S(2)}) collective-permute-start(bf16[64,1152]{1,0:T(8,128)(2,1)S(1)} %get-tuple-element.80.refs_0_), channel_id=1, source_target_pairs={{0,4},{1,5},{2,6},{3,7},{4,0},{5,1},{6,2},{7,3},{8,12},{9,13},{10,... | collective-permute-start | bytes 442376 | tf_op jit(solution)/shard_map/ppermute | solution.py:198
  14.0 5.5 %collective-permute-start.6 = (bf16[64,1152]{1,0:T(8,128)(2,1)S(1)}, bf16[64,1152]{1,0:T(8,128)(2,1)S(1)}, u32[]{:S(2)}, u32[]{:S(2)}) collective-permute-start(bf16[64,1152]{1,0:T(8,128)(2,1)S(1)} %get-tuple-element.80.refs_0_), channel_id=1, source_target_pairs={{0,2},{1,3},{2,0},{3,1},{4,6},{5,7},{6,4},{7,5},{8,10},{9,11},{10,... | collective-permute-start | bytes 442376 | tf_op jit(solution)/shard_map/ppermute | solution.py:198
  14.5 7.0 %collective-permute-start.7 = (bf16[64,1152]{1,0:T(8,128)(2,1)S(1)}, bf16[64,1152]{1,0:T(8,128)(2,1)S(1)}, u32[]{:S(2)}, u32[]{:S(2)}) collective-permute-start(bf16[64,1152]{1,0:T(8,128)(2,1)S(1)} %get-tuple-element.80.refs_0_), channel_id=1, source_target_pairs={{0,1},{1,0},{2,3},{3,2},{4,5},{5,4},{6,7},{7,6},{8,9},{9,8},{10,11... | collective-permute-start | bytes 442376 | tf_op jit(solution)/shard_map/ppermute | solution.py:198
  19.5 6.6 %collective-permute-start.9 = (bf16[64,1152]{1,0:T(8,128)(2,1)S(1)}, bf16[64,1152]{1,0:T(8,128)(2,1)S(1)}, u32[]{:S(2)}, u32[]{:S(2)}) collective-permute-start(bf16[64,1152]{1,0:T(8,128)(2,1)S(1)} %collective-permute-done.5.refs_1_.refs_0_), channel_id=1, source_target_pairs={{0,2},{1,3},{2,0},{3,1},{4,6},{5,7},{6,4},{7,5},{8,10},{9,11},{10,... | collective-permute-start | bytes 442376 | tf_op jit(solution)/shard_map/ppermute | solution.py:198
  20.0 8.9 %collective-permute-start.10 = (bf16[64,1152]{1,0:T(8,128)(2,1)S(1)}, bf16[64,1152]{1,0:T(8,128)(2,1)S(1)}, u32[]{:S(2)}, u32[]{:S(2)}) collective-permute-start(bf16[64,1152]{1,0:T(8,128)(2,1)S(1)} %collective-permute-done.3.refs_0_), channel_id=1, source_target_pairs={{0,2},{1,3},{2,0},{3,1},{4,6},{5,7},{6,4},{7,5},{8,10},{9,11},{10,... | collective-permute-start | bytes 442376 | tf_op jit(solution)/shard_map/ppermute | solution.py:198
  24.4 4.5 %collective-permute-start.15 = (bf16[64,1152]{1,0:T(8,128)(2,1)S(1)}, bf16[64,1152]{1,0:T(8,128)(2,1)S(1)}, u32[]{:S(2)}, u32[]{:S(2)}) collective-permute-start(bf16[64,1152]{1,0:T(8,128)(2,1)S(1)} %get-tuple-element.97), channel_id=1, source_target_pairs={{0,1},{1,0},{2,3},{3,2},{4,5},{5,4},{6,7},{7,6},{8,9},{9,8},{10,11... | collective-permute-start | bytes 442376 | tf_op jit(solution)/shard_map/ppermute | solution.py:198
  24.5 4.4 %collective-permute-start.16 = (bf16[64,1152]{1,0:T(8,128)(2,1)S(1)}, bf16[64,1152]{1,0:T(8,128)(2,1)S(1)}, u32[]{:S(2)}, u32[]{:S(2)}) collective-permute-start(bf16[64,1152]{1,0:T(8,128)(2,1)S(1)} %get-tuple-element.98), channel_id=1, source_target_pairs={{0,1},{1,0},{2,3},{3,2},{4,5},{5,4},{6,7},{7,6},{8,9},{9,8},{10,11... | collective-permute-start | bytes 442376 | tf_op jit(solution)/shard_map/ppermute | solution.py:198
  25.0 4.6 %collective-permute-start.13 = (bf16[64,1152]{1,0:T(8,128)(2,1)S(1)}, bf16[64,1152]{1,0:T(8,128)(2,1)S(1)}, u32[]{:S(2)}, u32[]{:S(2)}) collective-permute-start(bf16[64,1152]{1,0:T(8,128)(2,1)S(1)} %collective-permute-done.5.refs_1_.refs_0_), channel_id=1, source_target_pairs={{0,1},{1,0},{2,3},{3,2},{4,5},{5,4},{6,7},{7,6},{8,9},{9,8},{10,11... | collective-permute-start | bytes 442376 | tf_op jit(solution)/shard_map/ppermute | solution.py:198
  26.2 3.4 %collective-permute-start.14 = (bf16[64,1152]{1,0:T(8,128)(2,1)S(1)}, bf16[64,1152]{1,0:T(8,128)(2,1)S(1)}, u32[]{:S(2)}, u32[]{:S(2)}) collective-permute-start(bf16[64,1152]{1,0:T(8,128)(2,1)S(1)} %get-tuple-element.95.refs_1_), channel_id=1, source_target_pairs={{0,1},{1,0},{2,3},{3,2},{4,5},{5,4},{6,7},{7,6},{8,9},{9,8},{10,11... | collective-permute-start | bytes 442376 | tf_op jit(solution)/shard_map/ppermute | solution.py:198
  29.0 5.5 %collective-permute-start.19 = (bf16[64,1152]{1,0:T(8,128)(2,1)S(1)}, bf16[64,1152]{1,0:T(8,128)(2,1)S(1)}, u32[]{:S(2)}, u32[]{:S(2)}) collective-permute-start(bf16[64,1152]{1,0:T(8,128)(2,1)S(1)} %get-tuple-element.109), channel_id=1, source_target_pairs={{0,2},{1,3},{2,0},{3,1},{4,6},{5,7},{6,4},{7,5},{8,10},{9,11},{10,... | collective-permute-start | bytes 442376 | tf_op jit(solution)/shard_map/ppermute | solution.py:198
  33.0 2.7 %collective-permute-start.11 = (bf16[64,1152]{1,0:T(8,128)(2,1)S(1)}, bf16[64,1152]{1,0:T(8,128)(2,1)S(1)}, u32[]{:S(2)}, u32[]{:S(2)}) collective-permute-start(bf16[64,1152]{1,0:T(8,128)(2,1)S(1)} %collective-permute-done.3.refs_0_), channel_id=1, source_target_pairs={{0,1},{1,0},{2,3},{3,2},{4,5},{5,4},{6,7},{7,6},{8,9},{9,8},{10,11... | collective-permute-start | bytes 442376 | tf_op jit(solution)/shard_map/ppermute | solution.py:198
  34.7 5.6 %collective-permute-start.22 = (bf16[64,1152]{1,0:T(8,128)(2,1)S(1)}, bf16[64,1152]{1,0:T(8,128)(2,1)S(1)}, u32[]{:S(2)}, u32[]{:S(2)}) collective-permute-start(bf16[64,1152]{1,0:T(8,128)(2,1)S(1)} %get-tuple-element.123), channel_id=1, source_target_pairs={{0,2},{1,3},{2,0},{3,1},{4,6},{5,7},{6,4},{7,5},{8,10},{9,11},{10,... | collective-permute-start | bytes 442376 | tf_op jit(solution)/shard_map/ppermute | solution.py:198
  38.7 5.0 %collective-permute-start.20 = (bf16[64,1152]{1,0:T(8,128)(2,1)S(1)}, bf16[64,1152]{1,0:T(8,128)(2,1)S(1)}, u32[]{:S(2)}, u32[]{:S(2)}) collective-permute-start(bf16[64,1152]{1,0:T(8,128)(2,1)S(1)} %get-tuple-element.120), channel_id=1, source_target_pairs={{0,1},{1,0},{2,3},{3,2},{4,5},{5,4},{6,7},{7,6},{8,9},{9,8},{10,11... | collective-permute-start | bytes 442376 | tf_op jit(solution)/shard_map/ppermute | solution.py:198
  38.7 5.0 %collective-permute-start.21 = (bf16[64,1152]{1,0:T(8,128)(2,1)S(1)}, bf16[64,1152]{1,0:T(8,128)(2,1)S(1)}, u32[]{:S(2)}, u32[]{:S(2)}) collective-permute-start(bf16[64,1152]{1,0:T(8,128)(2,1)S(1)} %get-tuple-element.121), channel_id=1, source_target_pairs={{0,1},{1,0},{2,3},{3,2},{4,5},{5,4},{6,7},{7,6},{8,9},{9,8},{10,11... | collective-permute-start | bytes 442376 | tf_op jit(solution)/shard_map/ppermute | solution.py:198
  39.2 6.1 %collective-permute-start.1 = (bf16[64,1152]{1,0:T(8,128)(2,1)S(1)}, bf16[64,1152]{1,0:T(8,128)(2,1)S(1)}, u32[]{:S(2)}, u32[]{:S(2)}) collective-permute-start(bf16[64,1152]{1,0:T(8,128)(2,1)S(1)} %pack.1.refs_3_.refs_0_), channel_id=1, source_target_pairs={{0,1},{1,0},{2,3},{3,2},{4,5},{5,4},{6,7},{7,6},{8,9},{9,8},{10,11... | collective-permute-start | bytes 442376 | tf_op jit(solution)/shard_map/ppermute | solution.py:198
  39.3 6.1 %collective-permute-start.2 = (bf16[64,1152]{1,0:T(8,128)(2,1)S(1)}, bf16[64,1152]{1,0:T(8,128)(2,1)S(1)}, u32[]{:S(2)}, u32[]{:S(2)}) collective-permute-start(bf16[64,1152]{1,0:T(8,128)(2,1)S(1)} %collective-permute-done.refs_0_.refs_1_), channel_id=1, source_target_pairs={{0,1},{1,0},{2,3},{3,2},{4,5},{5,4},{6,7},{7,6},{8,9},{9,8},{10,11... | collective-permute-start | bytes 442376 | tf_op jit(solution)/shard_map/ppermute | solution.py:198
  40.3 9.9 %collective-permute-start.26 = (bf16[64,1152]{1,0:T(8,128)(2,1)S(1)}, bf16[64,1152]{1,0:T(8,128)(2,1)S(1)}, u32[]{:S(2)}, u32[]{:S(2)}) collective-permute-start(bf16[64,1152]{1,0:T(8,128)(2,1)S(1)} %get-tuple-element.138), channel_id=1, source_target_pairs={{0,8},{1,9},{2,10},{3,11},{4,12},{5,13},{6,14},{7,15},{8,0},{9,1},... | collective-permute-start | bytes 442376 | tf_op jit(solution)/shard_map/ppermute | solution.py:198
  43.8 6.4 %collective-permute-start.25 = (bf16[64,1152]{1,0:T(8,128)(2,1)S(1)}, bf16[64,1152]{1,0:T(8,128)(2,1)S(1)}, u32[]{:S(2)}, u32[]{:S(2)}) collective-permute-start(bf16[64,1152]{1,0:T(8,128)(2,1)S(1)} %get-tuple-element.137), channel_id=1, source_target_pairs={{0,2},{1,3},{2,0},{3,1},{4,6},{5,7},{6,4},{7,5},{8,10},{9,11},{10,... | collective-permute-start | bytes 442376 | tf_op jit(solution)/shard_map/ppermute | solution.py:198
  48.8 8.5 %collective-permute-start.29 = (bf16[64,1152]{1,0:T(8,128)(2,1)S(1)}, bf16[64,1152]{1,0:T(8,128)(2,1)S(1)}, u32[]{:S(2)}, u32[]{:S(2)}) collective-permute-start(bf16[64,1152]{1,0:T(8,128)(2,1)S(1)} %get-tuple-element.148), channel_id=1, source_target_pairs={{0,12},{1,13},{2,14},{3,15},{4,8},{5,9},{6,10},{7,11},{8,4},{9,5},... | collective-permute-start | bytes 442376 | tf_op jit(solution)/shard_map/ppermute | solution.py:198
  50.3 7.1 %collective-permute-start.27 = (bf16[64,1152]{1,0:T(8,128)(2,1)S(1)}, bf16[64,1152]{1,0:T(8,128)(2,1)S(1)}, u32[]{:S(2)}, u32[]{:S(2)}) collective-permute-start(bf16[64,1152]{1,0:T(8,128)(2,1)S(1)} %get-tuple-element.146), channel_id=1, source_target_pairs={{0,2},{1,3},{2,0},{3,1},{4,6},{5,7},{6,4},{7,5},{8,10},{9,11},{10,... | collective-permute-start | bytes 442376 | tf_op jit(solution)/shard_map/ppermute | solution.py:198
  51.8 7.9 %collective-permute-start.28 = (bf16[64,1152]{1,0:T(8,128)(2,1)S(1)}, bf16[64,1152]{1,0:T(8,128)(2,1)S(1)}, u32[]{:S(2)}, u32[]{:S(2)}) collective-permute-start(bf16[64,1152]{1,0:T(8,128)(2,1)S(1)} %get-tuple-element.147), channel_id=1, source_target_pairs={{0,4},{1,5},{2,6},{3,7},{4,0},{5,1},{6,2},{7,3},{8,12},{9,13},{10,... | collective-permute-start | bytes 442376 | tf_op jit(solution)/shard_map/ppermute | solution.py:198
  (6 other events, 12.7 us)

commit v11 on v10

--- a/solution.py
+++ b/solution.py
@@ -264,20 +264,20 @@
         block = {0: mine, 2: tie(z_2, [y_0]), 1: z_1}
         block[3] = swap(block[2], 4)
         other[0] = y_0
+        compute(0)
         gather(2, [block[1], block[3]])
+        reduce_core(0)
         compute(2)
         gather(3)
-        gather(1)
         reduce_core(2)
         compute(3)
-        z_2 = reduce_y(2)
+        gather(1)
+        z_2 = reduce_y(2, [y_came[0]])
         reduce_core(3)
         compute(1)
-        z_3 = reduce_y(3)
+        z_3 = reduce_y(3, [z_2])
         reduce_core(1)
-        compute(0)
-        z_1 = reduce_y(1, [z_2])
-        reduce_core(0)
+        z_1 = reduce_y(1)
         return fold_keep[0], y_came[0], z_1, z_2, z_3
 
     packet = call(

time: 60.7 us -> 62.8 us (1.035)
  waiting for transfers between devices: 15.9 us -> 19 us
  starting transfers between devices: 26.1 us -> 25.1 us
    ppermute x30, waiting for transfers between devices: 15.9 us -> 19 us  [swap(): return lax.ppermute(x, 'exp', [(i, i ^ bits) for i in range(n_dev)])]
    ppermute x30, starting transfers between devices: 26.1 us -> 25.1 us  [swap(): return lax.ppermute(x, 'exp', [(i, i ^ bits) for i in range(n_dev)])]
  transfers between devices with their start and end apart: 30 -> 30, of which waited for: 10 -> 9; matrix products, arithmetic and copies ran while one was open for 0% -> 0% of each run, Pallas kernels for 27% -> 26%
where the time goes in v11:
time: 62.8 us; the launch traced here: 62.6 us
  starting transfers between devices  25.1 us (40%)
  waiting for transfers between devices  19 us (30%)
  Pallas kernels  18.3 us (29%)
    ppermute x30, starting transfers between devices, swap(): return lax.ppermute(x, 'exp', [(i, i ^ bits) for i in range(n_dev)])  25.1 us
    ppermute x30, waiting for transfers between devices, swap(): return lax.ppermute(x, 'exp', [(i, i ^ bits) for i in range(n_dev)])  19 us
    pallas_call x17, Pallas kernels, call(): pl.pallas_call(body_with_chain if kernel is expert_kernel else body, out_...  17.5 us
  transfers between devices with their start and end apart: 30, of which 9 were waited for; matrix products, arithmetic and copies ran while one was open for 0% of the time, Pallas kernels for 26%

profile of v11, /device:TPU:0, one launch (start us, length us, event | category | flops | bytes accessed | tf_op | source)
XLA Modules:
  0.0 62.6 jit_solution(6666694001655529040)
XLA Ops:
  0.0 0.9 %pack.1.refs_3_.refs_0_ = bf16[64,1152]{1,0:T(8,128)(2,1)S(1)} custom-call(s32[8,64]{1,0:T(8,128)} %bitcast.2, bf16[64,1024]{1,0:T(8,128)(2,1)} %refs_1_.2), custom_call_target="tpu_custom_call" | custom-call | bytes 10000 | tf_op jit(solution)/shard_map/pack/pallas_call | solution.py:177
  0.9 3.0 %collective-permute-start = (bf16[64,1152]{1,0:T(8,128)(2,1)S(1)}, bf16[64,1152]{1,0:T(8,128)(2,1)S(1)}, u32[]{:S(2)}, u32[]{:S(2)}) collective-permute-start(bf16[64,1152]{1,0:T(8,128)(2,1)S(1)} %pack.1.refs_3_.refs_0_), channel_id=1, source_target_pairs={{0,2},{1,3},{2,0},{3,1},{4,6},{5,7},{6,4},{7,5},{8,10},{9,11},{10,... | collective-permute-start | bytes 442376 | tf_op jit(solution)/shard_map/ppermute | solution.py:198
  4.0 2.6 %collective-permute-start.3 = (bf16[64,1152]{1,0:T(8,128)(2,1)S(1)}, bf16[64,1152]{1,0:T(8,128)(2,1)S(1)}, u32[]{:S(2)}, u32[]{:S(2)}) collective-permute-start(bf16[64,1152]{1,0:T(8,128)(2,1)S(1)} %pack.1.refs_3_.refs_0_), channel_id=1, source_target_pairs={{0,8},{1,9},{2,10},{3,11},{4,12},{5,13},{6,14},{7,15},{8,0},{9,1},... | collective-permute-start | bytes 442376 | tf_op jit(solution)/shard_map/ppermute | solution.py:198
  6.6 1.6 %collective-permute-start.6 = (bf16[64,1152]{1,0:T(8,128)(2,1)S(1)}, bf16[64,1152]{1,0:T(8,128)(2,1)S(1)}, u32[]{:S(2)}, u32[]{:S(2)}) collective-permute-start(bf16[64,1152]{1,0:T(8,128)(2,1)S(1)} %pack.1.refs_3_.refs_0_), channel_id=1, source_target_pairs={{0,4},{1,5},{2,6},{3,7},{4,0},{5,1},{6,2},{7,3},{8,12},{9,13},{10,... | collective-permute-start | bytes 442376 | tf_op jit(solution)/shard_map/ppermute | solution.py:198
  8.4 4.7 %load.1 = (bf16[16,1024]{1,0:T(8,128)(2,1)S(1)}, bf16[2,1024,2048]{2,1,0:T(8,128)(2,1)S(1)}, bf16[2,1024,1024]{2,1,0:T(8,128)(2,1)S(1)}) custom-call(bf16[2,1024]{1,0:T(2,128)(2,1)} %bitcast.3, bf16[2,1024,2048]{2,1,0:T(8,128)(2,1)} %refs_1_.3, bf16[2,1024,1024]{2,1,0:T(8,128)(2,1)} %refs_2_.1, bf16[64,1152]{1,0:T(8,128)(2,1)S(1)} %pack.1.refs_3_.refs_0_), custom_call_target="tpu_custom_call" | custom-call | bytes 10000 | tf_op jit(solution)/shard_map/load/pallas_call | solution.py:177
  13.5 1.0 %collective-permute-start.7 = (bf16[64,1152]{1,0:T(8,128)(2,1)S(1)}, bf16[64,1152]{1,0:T(8,128)(2,1)S(1)}, u32[]{:S(2)}, u32[]{:S(2)}) collective-permute-start(bf16[64,1152]{1,0:T(8,128)(2,1)S(1)} %get-tuple-element.86.refs_0_), channel_id=1, source_target_pairs={{0,4},{1,5},{2,6},{3,7},{4,0},{5,1},{6,2},{7,3},{8,12},{9,13},{10,... | collective-permute-start | bytes 442376 | tf_op jit(solution)/shard_map/ppermute | solution.py:198
  14.4 1.5 %collective-permute-start.8 = (bf16[64,1152]{1,0:T(8,128)(2,1)S(1)}, bf16[64,1152]{1,0:T(8,128)(2,1)S(1)}, u32[]{:S(2)}, u32[]{:S(2)}) collective-permute-start(bf16[64,1152]{1,0:T(8,128)(2,1)S(1)} %get-tuple-element.86.refs_0_), channel_id=1, source_target_pairs={{0,2},{1,3},{2,0},{3,1},{4,6},{5,7},{6,4},{7,5},{8,10},{9,11},{10,... | collective-permute-start | bytes 442376 | tf_op jit(solution)/shard_map/ppermute | solution.py:198
  16.0 2.9 %expert.4 = (f32[128,1152]{1,0:T(8,128)S(1)}, bf16[64,1152]{1,0:T(8,128)(2,1)S(1)}, bf16[64,1152]{1,0:T(8,128)(2,1)S(1)}, bf16[16,1024]{1,0:T(8,128)(2,1)S(1)}, ...) custom-call(bf16[64,1152]{1,0:T(8,128)(2,1)S(1)} %pack.1.refs_3_.ref, ...), custom_call_target="tpu_custom_call", output_to_operand_aliasing={{3}: (4, {}), {4}: (5, {}), {5}: (6, {})} | custom-call | bytes 10000 | tf_op jit(solution)/shard_map/expert/pallas_call | solution.py:177
  20.4 1.5 %collective-permute-start.12 = (bf16[64,1152]{1,0:T(8,128)(2,1)S(1)}, bf16[64,1152]{1,0:T(8,128)(2,1)S(1)}, u32[]{:S(2)}, u32[]{:S(2)}) collective-permute-start(bf16[64,1152]{1,0:T(8,128)(2,1)S(1)} %collective-permute-done.7.refs_1_.refs_0_), channel_id=1, source_target_pairs={{0,2},{1,3},{2,0},{3,1},{4,6},{5,7},{6,4},{7,5},{8,10},{9,11},{10,... | collective-permute-start | bytes 442376 | tf_op jit(solution)/shard_map/ppermute | solution.py:198
  22.0 2.9 %expert.5 = (f32[128,1152]{1,0:T(8,128)S(1)}, bf16[64,1152]{1,0:T(8,128)(2,1)S(1)}, bf16[64,1152]{1,0:T(8,128)(2,1)S(1)}, bf16[16,1024]{1,0:T(8,128)(2,1)S(1)}, ...) custom-call(bf16[64,1152]{1,0:T(8,128)(2,1)S(1)} %get-tuple-element., ...), custom_call_target="tpu_custom_call", output_to_operand_aliasing={{3}: (4, {}), {4}: (5, {}), {5}: (6, {})} | custom-call | bytes 10000 | tf_op jit(solution)/shard_map/expert/pallas_call | solution.py:177
  25.7 1.0 %collective-permute-done.12.refs_3_ = bf16[64,1152]{1,0:T(8,128)(2,1)S(1)} collective-permute-done((bf16[64,1152]{1,0:T(8,128)(2,1)S(1)}, bf16[64,1152]{1,0:T(8,128)(2,1)S(1)}, u32[]{:S(2)}, u32[]{:S(2)}) %collective-permute-start.12) | collective-permute-done | bytes 147488 | tf_op jit(solution)/shard_map/ppermute | solution.py:198
  26.7 1.5 %collective-permute-start.17 = (bf16[64,1152]{1,0:T(8,128)(2,1)S(1)}, bf16[64,1152]{1,0:T(8,128)(2,1)S(1)}, u32[]{:S(2)}, u32[]{:S(2)}) collective-permute-start(bf16[64,1152]{1,0:T(8,128)(2,1)S(1)} %collective-permute-done.6.refs_0_), channel_id=1, source_target_pairs={{0,2},{1,3},{2,0},{3,1},{4,6},{5,7},{6,4},{7,5},{8,10},{9,11},{10,... | collective-permute-start | bytes 442376 | tf_op jit(solution)/shard_map/ppermute | solution.py:198
  28.8 1.6 %collective-permute-start.22 = (bf16[64,1152]{1,0:T(8,128)(2,1)S(1)}, bf16[64,1152]{1,0:T(8,128)(2,1)S(1)}, u32[]{:S(2)}, u32[]{:S(2)}) collective-permute-start(bf16[64,1152]{1,0:T(8,128)(2,1)S(1)} %get-tuple-element.120), channel_id=1, source_target_pairs={{0,2},{1,3},{2,0},{3,1},{4,6},{5,7},{6,4},{7,5},{8,10},{9,11},{10,... | collective-permute-start | bytes 442376 | tf_op jit(solution)/shard_map/ppermute | solution.py:198
  30.4 2.9 %expert.6 = (f32[128,1152]{1,0:T(8,128)S(1)}, bf16[64,1152]{1,0:T(8,128)(2,1)S(1)}, bf16[64,1152]{1,0:T(8,128)(2,1)S(1)}, bf16[16,1024]{1,0:T(8,128)(2,1)S(1)}, ...) custom-call(bf16[64,1152]{1,0:T(8,128)(2,1)S(1)} %collective-permute, ...), custom_call_target="tpu_custom_call", output_to_operand_aliasing={{3}: (4, {}), {4}: (5, {}), {5}: (6, {})} | custom-call | bytes 10000 | tf_op jit(solution)/shard_map/expert/pallas_call | solution.py:177
  33.9 2.6 %collective-permute-done.9.refs_2_.refs_1_ = bf16[64,1152]{1,0:T(8,128)(2,1)S(1)} collective-permute-done((bf16[64,1152]{1,0:T(8,128)(2,1)S(1)}, bf16[64,1152]{1,0:T(8,128)(2,1)S(1)}, u32[]{:S(2)}, u32[]{:S(2)}) %collective-permute-start.9) | collective-permute-done | bytes 147488 | tf_op jit(solution)/shard_map/ppermute | solution.py:198
  36.5 2.8 %collective-permute-done.22.refs_1_ = bf16[64,1152]{1,0:T(8,128)(2,1)S(1)} collective-permute-done((bf16[64,1152]{1,0:T(8,128)(2,1)S(1)}, bf16[64,1152]{1,0:T(8,128)(2,1)S(1)}, u32[]{:S(2)}, u32[]{:S(2)}) %collective-permute-start.22) | collective-permute-done | bytes 147488 | tf_op jit(solution)/shard_map/ppermute | solution.py:198
  39.4 1.6 %collective-permute-start.25 = (bf16[64,1152]{1,0:T(8,128)(2,1)S(1)}, bf16[64,1152]{1,0:T(8,128)(2,1)S(1)}, u32[]{:S(2)}, u32[]{:S(2)}) collective-permute-start(bf16[64,1152]{1,0:T(8,128)(2,1)S(1)} %get-tuple-element.134), channel_id=1, source_target_pairs={{0,2},{1,3},{2,0},{3,1},{4,6},{5,7},{6,4},{7,5},{8,10},{9,11},{10,... | collective-permute-start | bytes 442376 | tf_op jit(solution)/shard_map/ppermute | solution.py:198
  41.0 2.6 %collective-permute-start.26 = (bf16[64,1152]{1,0:T(8,128)(2,1)S(1)}, bf16[64,1152]{1,0:T(8,128)(2,1)S(1)}, u32[]{:S(2)}, u32[]{:S(2)}) collective-permute-start(bf16[64,1152]{1,0:T(8,128)(2,1)S(1)} %get-tuple-element.135), channel_id=1, source_target_pairs={{0,8},{1,9},{2,10},{3,11},{4,12},{5,13},{6,14},{7,15},{8,0},{9,1},... | collective-permute-start | bytes 442376 | tf_op jit(solution)/shard_map/ppermute | solution.py:198
  43.6 2.9 %expert.7 = (f32[128,1152]{1,0:T(8,128)S(1)}, bf16[64,1152]{1,0:T(8,128)(2,1)S(1)}, bf16[64,1152]{1,0:T(8,128)(2,1)S(1)}, bf16[16,1024]{1,0:T(8,128)(2,1)S(1)}, ...) custom-call(bf16[64,1152]{1,0:T(8,128)(2,1)S(1)} %collective-permute, ...), custom_call_target="tpu_custom_call", output_to_operand_aliasing={{3}: (4, {}), {4}: (5, {}), {5}: (6, {})} | custom-call | bytes 10000 | tf_op jit(solution)/shard_map/expert/pallas_call | solution.py:177
  47.0 3.1 %collective-permute-done.26.refs_2_.refs_3_ = bf16[64,1152]{1,0:T(8,128)(2,1)S(1)} collective-permute-done((bf16[64,1152]{1,0:T(8,128)(2,1)S(1)}, bf16[64,1152]{1,0:T(8,128)(2,1)S(1)}, u32[]{:S(2)}, u32[]{:S(2)}) %collective-permute-start.26) | collective-permute-done | bytes 147488 | tf_op jit(solution)/shard_map/ppermute | solution.py:198
  50.9 2.5 %collective-permute-start.29 = (bf16[64,1152]{1,0:T(8,128)(2,1)S(1)}, bf16[64,1152]{1,0:T(8,128)(2,1)S(1)}, u32[]{:S(2)}, u32[]{:S(2)}) collective-permute-start(bf16[64,1152]{1,0:T(8,128)(2,1)S(1)} %get-tuple-element.148), channel_id=1, source_target_pairs={{0,12},{1,13},{2,14},{3,15},{4,8},{5,9},{6,10},{7,11},{8,4},{9,5},... | collective-permute-start | bytes 442376 | tf_op jit(solution)/shard_map/ppermute | solution.py:198
  53.4 2.7 %collective-permute-done.27.refs_1_ = bf16[64,1152]{1,0:T(8,128)(2,1)S(1)} collective-permute-done((bf16[64,1152]{1,0:T(8,128)(2,1)S(1)}, bf16[64,1152]{1,0:T(8,128)(2,1)S(1)}, u32[]{:S(2)}, u32[]{:S(2)}) %collective-permute-start.27) | collective-permute-done | bytes 147488 | tf_op jit(solution)/shard_map/ppermute | solution.py:198
  56.2 3.3 %collective-permute-done.29.refs_4_ = bf16[64,1152]{1,0:T(8,128)(2,1)S(1)} collective-permute-done((bf16[64,1152]{1,0:T(8,128)(2,1)S(1)}, bf16[64,1152]{1,0:T(8,128)(2,1)S(1)}, u32[]{:S(2)}, u32[]{:S(2)}) %collective-permute-start.29) | collective-permute-done | bytes 147488 | tf_op jit(solution)/shard_map/ppermute | solution.py:198
  59.5 2.4 %collective-permute-done.28.refs_2_ = bf16[64,1152]{1,0:T(8,128)(2,1)S(1)} collective-permute-done((bf16[64,1152]{1,0:T(8,128)(2,1)S(1)}, bf16[64,1152]{1,0:T(8,128)(2,1)S(1)}, u32[]{:S(2)}, u32[]{:S(2)}) %collective-permute-start.28) | collective-permute-done | bytes 147488 | tf_op jit(solution)/shard_map/ppermute | solution.py:198
  (54 shorter events, 6.5 us)
Async XLA Ops:
  0.9 7.2 %collective-permute-start = (bf16[64,1152]{1,0:T(8,128)(2,1)S(1)}, bf16[64,1152]{1,0:T(8,128)(2,1)S(1)}, u32[]{:S(2)}, u32[]{:S(2)}) collective-permute-start(bf16[64,1152]{1,0:T(8,128)(2,1)S(1)} %pack.1.refs_3_.refs_0_), channel_id=1, source_target_pairs={{0,2},{1,3},{2,0},{3,1},{4,6},{5,7},{6,4},{7,5},{8,10},{9,11},{10,... | collective-permute-start | bytes 442376 | tf_op jit(solution)/shard_map/ppermute | solution.py:198
  4.0 9.5 %collective-permute-start.3 = (bf16[64,1152]{1,0:T(8,128)(2,1)S(1)}, bf16[64,1152]{1,0:T(8,128)(2,1)S(1)}, u32[]{:S(2)}, u32[]{:S(2)}) collective-permute-start(bf16[64,1152]{1,0:T(8,128)(2,1)S(1)} %pack.1.refs_3_.refs_0_), channel_id=1, source_target_pairs={{0,8},{1,9},{2,10},{3,11},{4,12},{5,13},{6,14},{7,15},{8,0},{9,1},... | collective-permute-start | bytes 442376 | tf_op jit(solution)/shard_map/ppermute | solution.py:198
  6.6 9.4 %collective-permute-start.1 = (bf16[64,1152]{1,0:T(8,128)(2,1)S(1)}, bf16[64,1152]{1,0:T(8,128)(2,1)S(1)}, u32[]{:S(2)}, u32[]{:S(2)}) collective-permute-start(bf16[64,1152]{1,0:T(8,128)(2,1)S(1)} %pack.1.refs_3_.refs_0_), channel_id=1, source_target_pairs={{0,1},{1,0},{2,3},{3,2},{4,5},{5,4},{6,7},{7,6},{8,9},{9,8},{10,11... | collective-permute-start | bytes 442376 | tf_op jit(solution)/shard_map/ppermute | solution.py:198
  6.6 12.9 %collective-permute-start.6 = (bf16[64,1152]{1,0:T(8,128)(2,1)S(1)}, bf16[64,1152]{1,0:T(8,128)(2,1)S(1)}, u32[]{:S(2)}, u32[]{:S(2)}) collective-permute-start(bf16[64,1152]{1,0:T(8,128)(2,1)S(1)} %pack.1.refs_3_.refs_0_), channel_id=1, source_target_pairs={{0,4},{1,5},{2,6},{3,7},{4,0},{5,1},{6,2},{7,3},{8,12},{9,13},{10,... | collective-permute-start | bytes 442376 | tf_op jit(solution)/shard_map/ppermute | solution.py:198
  8.2 7.8 %collective-permute-start.2 = (bf16[64,1152]{1,0:T(8,128)(2,1)S(1)}, bf16[64,1152]{1,0:T(8,128)(2,1)S(1)}, u32[]{:S(2)}, u32[]{:S(2)}) collective-permute-start(bf16[64,1152]{1,0:T(8,128)(2,1)S(1)} %collective-permute-done.refs_0_.refs_1_), channel_id=1, source_target_pairs={{0,1},{1,0},{2,3},{3,2},{4,5},{5,4},{6,7},{7,6},{8,9},{9,8},{10,11... | collective-permute-start | bytes 442376 | tf_op jit(solution)/shard_map/ppermute | solution.py:198
  13.5 6.1 %collective-permute-start.7 = (bf16[64,1152]{1,0:T(8,128)(2,1)S(1)}, bf16[64,1152]{1,0:T(8,128)(2,1)S(1)}, u32[]{:S(2)}, u32[]{:S(2)}) collective-permute-start(bf16[64,1152]{1,0:T(8,128)(2,1)S(1)} %get-tuple-element.86.refs_0_), channel_id=1, source_target_pairs={{0,4},{1,5},{2,6},{3,7},{4,0},{5,1},{6,2},{7,3},{8,12},{9,13},{10,... | collective-permute-start | bytes 442376 | tf_op jit(solution)/shard_map/ppermute | solution.py:198
  14.4 6.0 %collective-permute-start.8 = (bf16[64,1152]{1,0:T(8,128)(2,1)S(1)}, bf16[64,1152]{1,0:T(8,128)(2,1)S(1)}, u32[]{:S(2)}, u32[]{:S(2)}) collective-permute-start(bf16[64,1152]{1,0:T(8,128)(2,1)S(1)} %get-tuple-element.86.refs_0_), channel_id=1, source_target_pairs={{0,2},{1,3},{2,0},{3,1},{4,6},{5,7},{6,4},{7,5},{8,10},{9,11},{10,... | collective-permute-start | bytes 442376 | tf_op jit(solution)/shard_map/ppermute | solution.py:198
  16.0 6.0 %collective-permute-start.10 = (bf16[64,1152]{1,0:T(8,128)(2,1)S(1)}, bf16[64,1152]{1,0:T(8,128)(2,1)S(1)}, u32[]{:S(2)}, u32[]{:S(2)}) collective-permute-start(bf16[64,1152]{1,0:T(8,128)(2,1)S(1)} %get-tuple-element.86.refs_0_), channel_id=1, source_target_pairs={{0,1},{1,0},{2,3},{3,2},{4,5},{5,4},{6,7},{7,6},{8,9},{9,8},{10,11... | collective-permute-start | bytes 442376 | tf_op jit(solution)/shard_map/ppermute | solution.py:198
  20.4 6.3 %collective-permute-start.12 = (bf16[64,1152]{1,0:T(8,128)(2,1)S(1)}, bf16[64,1152]{1,0:T(8,128)(2,1)S(1)}, u32[]{:S(2)}, u32[]{:S(2)}) collective-permute-start(bf16[64,1152]{1,0:T(8,128)(2,1)S(1)} %collective-permute-done.7.refs_1_.refs_0_), channel_id=1, source_target_pairs={{0,2},{1,3},{2,0},{3,1},{4,6},{5,7},{6,4},{7,5},{8,10},{9,11},{10,... | collective-permute-start | bytes 442376 | tf_op jit(solution)/shard_map/ppermute | solution.py:198
  25.5 4.9 %collective-permute-start.13 = (bf16[64,1152]{1,0:T(8,128)(2,1)S(1)}, bf16[64,1152]{1,0:T(8,128)(2,1)S(1)}, u32[]{:S(2)}, u32[]{:S(2)}) collective-permute-start(bf16[64,1152]{1,0:T(8,128)(2,1)S(1)} %collective-permute-done.7.refs_1_.refs_0_), channel_id=1, source_target_pairs={{0,1},{1,0},{2,3},{3,2},{4,5},{5,4},{6,7},{7,6},{8,9},{9,8},{10,11... | collective-permute-start | bytes 442376 | tf_op jit(solution)/shard_map/ppermute | solution.py:198
  26.7 3.7 %collective-permute-start.14 = (bf16[64,1152]{1,0:T(8,128)(2,1)S(1)}, bf16[64,1152]{1,0:T(8,128)(2,1)S(1)}, u32[]{:S(2)}, u32[]{:S(2)}) collective-permute-start(bf16[64,1152]{1,0:T(8,128)(2,1)S(1)} %get-tuple-element.102.refs_1_), channel_id=1, source_target_pairs={{0,1},{1,0},{2,3},{3,2},{4,5},{5,4},{6,7},{7,6},{8,9},{9,8},{10,11... | collective-permute-start | bytes 442376 | tf_op jit(solution)/shard_map/ppermute | solution.py:198
  26.7 7.2 %collective-permute-start.17 = (bf16[64,1152]{1,0:T(8,128)(2,1)S(1)}, bf16[64,1152]{1,0:T(8,128)(2,1)S(1)}, u32[]{:S(2)}, u32[]{:S(2)}) collective-permute-start(bf16[64,1152]{1,0:T(8,128)(2,1)S(1)} %collective-permute-done.6.refs_0_), channel_id=1, source_target_pairs={{0,2},{1,3},{2,0},{3,1},{4,6},{5,7},{6,4},{7,5},{8,10},{9,11},{10,... | collective-permute-start | bytes 442376 | tf_op jit(solution)/shard_map/ppermute | solution.py:198
  28.2 8.3 %collective-permute-start.9 = (bf16[64,1152]{1,0:T(8,128)(2,1)S(1)}, bf16[64,1152]{1,0:T(8,128)(2,1)S(1)}, u32[]{:S(2)}, u32[]{:S(2)}) collective-permute-start(bf16[64,1152]{1,0:T(8,128)(2,1)S(1)} %get-tuple-element.94), channel_id=1, source_target_pairs={{0,2},{1,3},{2,0},{3,1},{4,6},{5,7},{6,4},{7,5},{8,10},{9,11},{10,... | collective-permute-start | bytes 442376 | tf_op jit(solution)/shard_map/ppermute | solution.py:198
  28.8 10.5 %collective-permute-start.22 = (bf16[64,1152]{1,0:T(8,128)(2,1)S(1)}, bf16[64,1152]{1,0:T(8,128)(2,1)S(1)}, u32[]{:S(2)}, u32[]{:S(2)}) collective-permute-start(bf16[64,1152]{1,0:T(8,128)(2,1)S(1)} %get-tuple-element.120), channel_id=1, source_target_pairs={{0,2},{1,3},{2,0},{3,1},{4,6},{5,7},{6,4},{7,5},{8,10},{9,11},{10,... | collective-permute-start | bytes 442376 | tf_op jit(solution)/shard_map/ppermute | solution.py:198
  33.3 6.0 %collective-permute-start.20 = (bf16[64,1152]{1,0:T(8,128)(2,1)S(1)}, bf16[64,1152]{1,0:T(8,128)(2,1)S(1)}, u32[]{:S(2)}, u32[]{:S(2)}) collective-permute-start(bf16[64,1152]{1,0:T(8,128)(2,1)S(1)} %get-tuple-element.117), channel_id=1, source_target_pairs={{0,1},{1,0},{2,3},{3,2},{4,5},{5,4},{6,7},{7,6},{8,9},{9,8},{10,11... | collective-permute-start | bytes 442376 | tf_op jit(solution)/shard_map/ppermute | solution.py:198
  33.3 6.0 %collective-permute-start.21 = (bf16[64,1152]{1,0:T(8,128)(2,1)S(1)}, bf16[64,1152]{1,0:T(8,128)(2,1)S(1)}, u32[]{:S(2)}, u32[]{:S(2)}) collective-permute-start(bf16[64,1152]{1,0:T(8,128)(2,1)S(1)} %get-tuple-element.118), channel_id=1, source_target_pairs={{0,1},{1,0},{2,3},{3,2},{4,5},{5,4},{6,7},{7,6},{8,9},{9,8},{10,11... | collective-permute-start | bytes 442376 | tf_op jit(solution)/shard_map/ppermute | solution.py:198
  33.8 9.7 %collective-permute-start.18 = (bf16[64,1152]{1,0:T(8,128)(2,1)S(1)}, bf16[64,1152]{1,0:T(8,128)(2,1)S(1)}, u32[]{:S(2)}, u32[]{:S(2)}) collective-permute-start(bf16[64,1152]{1,0:T(8,128)(2,1)S(1)} %collective-permute-done.6.refs_0_), channel_id=1, source_target_pairs={{0,1},{1,0},{2,3},{3,2},{4,5},{5,4},{6,7},{7,6},{8,9},{9,8},{10,11... | collective-permute-start | bytes 442376 | tf_op jit(solution)/shard_map/ppermute | solution.py:198
  36.5 7.1 %collective-permute-start.19 = (bf16[64,1152]{1,0:T(8,128)(2,1)S(1)}, bf16[64,1152]{1,0:T(8,128)(2,1)S(1)}, u32[]{:S(2)}, u32[]{:S(2)}) collective-permute-start(bf16[64,1152]{1,0:T(8,128)(2,1)S(1)} %get-tuple-element.115.refs_1_), channel_id=1, source_target_pairs={{0,1},{1,0},{2,3},{3,2},{4,5},{5,4},{6,7},{7,6},{8,9},{9,8},{10,11... | collective-permute-start | bytes 442376 | tf_op jit(solution)/shard_map/ppermute | solution.py:198
  39.4 7.7 %collective-permute-start.25 = (bf16[64,1152]{1,0:T(8,128)(2,1)S(1)}, bf16[64,1152]{1,0:T(8,128)(2,1)S(1)}, u32[]{:S(2)}, u32[]{:S(2)}) collective-permute-start(bf16[64,1152]{1,0:T(8,128)(2,1)S(1)} %get-tuple-element.134), channel_id=1, source_target_pairs={{0,2},{1,3},{2,0},{3,1},{4,6},{5,7},{6,4},{7,5},{8,10},{9,11},{10,... | collective-permute-start | bytes 442376 | tf_op jit(solution)/shard_map/ppermute | solution.py:198
  41.0 9.1 %collective-permute-start.26 = (bf16[64,1152]{1,0:T(8,128)(2,1)S(1)}, bf16[64,1152]{1,0:T(8,128)(2,1)S(1)}, u32[]{:S(2)}, u32[]{:S(2)}) collective-permute-start(bf16[64,1152]{1,0:T(8,128)(2,1)S(1)} %get-tuple-element.135), channel_id=1, source_target_pairs={{0,8},{1,9},{2,10},{3,11},{4,12},{5,13},{6,14},{7,15},{8,0},{9,1},... | collective-permute-start | bytes 442376 | tf_op jit(solution)/shard_map/ppermute | solution.py:198
  46.5 3.7 %collective-permute-start.23 = (bf16[64,1152]{1,0:T(8,128)(2,1)S(1)}, bf16[64,1152]{1,0:T(8,128)(2,1)S(1)}, u32[]{:S(2)}, u32[]{:S(2)}) collective-permute-start(bf16[64,1152]{1,0:T(8,128)(2,1)S(1)} %get-tuple-element.131), channel_id=1, source_target_pairs={{0,1},{1,0},{2,3},{3,2},{4,5},{5,4},{6,7},{7,6},{8,9},{9,8},{10,11... | collective-permute-start | bytes 442376 | tf_op jit(solution)/shard_map/ppermute | solution.py:198
  50.2 5.8 %collective-permute-start.27 = (bf16[64,1152]{1,0:T(8,128)(2,1)S(1)}, bf16[64,1152]{1,0:T(8,128)(2,1)S(1)}, u32[]{:S(2)}, u32[]{:S(2)}) collective-permute-start(bf16[64,1152]{1,0:T(8,128)(2,1)S(1)} %get-tuple-element.143), channel_id=1, source_target_pairs={{0,2},{1,3},{2,0},{3,1},{4,6},{5,7},{6,4},{7,5},{8,10},{9,11},{10,... | collective-permute-start | bytes 442376 | tf_op jit(solution)/shard_map/ppermute | solution.py:198
  50.9 8.6 %collective-permute-start.29 = (bf16[64,1152]{1,0:T(8,128)(2,1)S(1)}, bf16[64,1152]{1,0:T(8,128)(2,1)S(1)}, u32[]{:S(2)}, u32[]{:S(2)}) collective-permute-start(bf16[64,1152]{1,0:T(8,128)(2,1)S(1)} %get-tuple-element.148), channel_id=1, source_target_pairs={{0,12},{1,13},{2,14},{3,15},{4,8},{5,9},{6,10},{7,11},{8,4},{9,5},... | collective-permute-start | bytes 442376 | tf_op jit(solution)/shard_map/ppermute | solution.py:198
  56.1 5.8 %collective-permute-start.28 = (bf16[64,1152]{1,0:T(8,128)(2,1)S(1)}, bf16[64,1152]{1,0:T(8,128)(2,1)S(1)}, u32[]{:S(2)}, u32[]{:S(2)}) collective-permute-start(bf16[64,1152]{1,0:T(8,128)(2,1)S(1)} %get-tuple-element.147), channel_id=1, source_target_pairs={{0,4},{1,5},{2,6},{3,7},{4,0},{5,1},{6,2},{7,3},{8,12},{9,13},{10,... | collective-permute-start | bytes 442376 | tf_op jit(solution)/shard_map/ppermute | solution.py:198
  (6 other events, 17.6 us)

commit v12 on v10

--- a/solution.py
+++ b/solution.py
@@ -121,8 +121,11 @@
     send_ref[...] = (mine_ref[rows:] + came_b_ref[...].astype(jnp.float32)).astype(jnp.bfloat16)
 
 
-def add_kernel(mine_ref, came_ref, out_ref):
-    out_ref[...] = (mine_ref[...] + came_ref[...].astype(jnp.float32)).astype(jnp.bfloat16)
+def add_kernel(mine_ref, *refs):
+    total = mine_ref[...]
+    for ref in refs[:-1]:
+        total = total + ref[...].astype(jnp.float32)
+    refs[-1][...] = total.astype(jnp.bfloat16)
 
 
 def total_kernel(*refs):
@@ -231,7 +234,7 @@
         def tie(x, deps=()):
             return step(tie_kernel, [], deps=deps, hand_on=[x])[0]
 
-        other, keep, send, came, fold_keep, fold_send, y_came, z_send = {}, {}, {}, {}, {}, {}, {}, {}
+        other, keep, send, came, fold_keep, fold_send, y_came = {}, {}, {}, {}, {}, {}, {}
 
         def gather(k, deps=()):
             other[k] = tie(swap(block[k], 2), deps)
@@ -256,29 +259,28 @@
             )
             y_came[k] = swap(fold_send[k], 2)
 
-        def reduce_y(k, deps=()):
-            z_send[k] = step(add_kernel, [space(rows, jnp.bfloat16)], [fold_keep[k], y_came[k]], deps)[0]
-            return swap(z_send[k], 4 * k)
+        def reduce_y(k, *more):
+            return step(add_kernel, [space(rows, jnp.bfloat16)], [fold_keep[k], y_came[k], *more])[0]
 
         z_2, z_1, y_0 = swap(mine, 8), swap(mine, 4), swap(mine, 2)
-        block = {0: mine, 2: tie(z_2, [y_0]), 1: z_1}
+        block = {0: mine, 2: tie(z_2), 1: z_1}
         block[3] = swap(block[2], 4)
         other[0] = y_0
-        gather(2, [block[1], block[3]])
+        gather(2, [block[1], block[3], y_0])
         compute(2)
         gather(3)
-        gather(1)
         reduce_core(2)
         compute(3)
-        z_2 = reduce_y(2)
+        gather(1, [y_came[2]])
         reduce_core(3)
         compute(1)
-        z_3 = reduce_y(3)
+        z_3 = swap(reduce_y(3), 4)
         reduce_core(1)
         compute(0)
-        z_1 = reduce_y(1, [z_2])
+        z_2 = swap(reduce_y(2, z_3), 8)
+        z_1 = swap(reduce_y(1), 4)
         reduce_core(0)
-        return fold_keep[0], y_came[0], z_1, z_2, z_3
+        return fold_keep[0], z_2, z_1, y_came[0]
 
     packet = call(
         pack_kernel,

time: 60.7 us -> 59 us (0.972)
  starting transfers between devices: 26.1 us -> 23.7 us
  waiting for transfers between devices: 15.9 us -> 16.7 us
    ppermute x30, starting transfers between devices: 26.1 us -> 23.7 us  [swap(): return lax.ppermute(x, 'exp', [(i, i ^ bits) for i in range(n_dev)])]
    ppermute x30, waiting for transfers between devices: 15.9 us -> 16.7 us  [swap(): return lax.ppermute(x, 'exp', [(i, i ^ bits) for i in range(n_dev)])]
  transfers between devices with their start and end apart: 30 -> 30, of which waited for: 10 -> 9; matrix products, arithmetic and copies ran while one was open for 0% -> 0% of each run, Pallas kernels for 27% -> 28%
where the time goes in v12:
time: 59 us; the launch traced here: 58.8 us
  starting transfers between devices  23.7 us (40%)
  Pallas kernels  18.3 us (31%)
  waiting for transfers between devices  16.7 us (28%)
    ppermute x30, starting transfers between devices, swap(): return lax.ppermute(x, 'exp', [(i, i ^ bits) for i in range(n_dev)])  23.7 us
    pallas_call x17, Pallas kernels, call(): pl.pallas_call(body_with_chain if kernel is expert_kernel else body, out_...  17.5 us
    ppermute x30, waiting for transfers between devices, swap(): return lax.ppermute(x, 'exp', [(i, i ^ bits) for i in range(n_dev)])  16.7 us
  transfers between devices with their start and end apart: 30, of which 9 were waited for; matrix products, arithmetic and copies ran while one was open for 0% of the time, Pallas kernels for 28%

profile of v12, /device:TPU:0, one launch (start us, length us, event | category | flops | bytes accessed | tf_op | source)
XLA Modules:
  0.0 58.8 jit_solution(4856327698408136442)
XLA Ops:
  0.0 0.9 %pack.1.refs_3_.refs_0_ = bf16[64,1152]{1,0:T(8,128)(2,1)S(1)} custom-call(s32[8,64]{1,0:T(8,128)} %bitcast.2, bf16[64,1024]{1,0:T(8,128)(2,1)} %refs_1_.2), custom_call_target="tpu_custom_call" | custom-call | bytes 10000 | tf_op jit(solution)/shard_map/pack/pallas_call | solution.py:180
  0.9 4.1 %collective-permute-start.4 = (bf16[64,1152]{1,0:T(8,128)(2,1)S(1)}, bf16[64,1152]{1,0:T(8,128)(2,1)S(1)}, u32[]{:S(2)}, u32[]{:S(2)}) collective-permute-start(bf16[64,1152]{1,0:T(8,128)(2,1)S(1)} %pack.1.refs_3_.refs_0_), channel_id=1, source_target_pairs={{0,8},{1,9},{2,10},{3,11},{4,12},{5,13},{6,14},{7,15},{8,0},{9,1},... | collective-permute-start | bytes 442376 | tf_op jit(solution)/shard_map/ppermute | solution.py:201
  5.0 1.6 %collective-permute-start.3 = (bf16[64,1152]{1,0:T(8,128)(2,1)S(1)}, bf16[64,1152]{1,0:T(8,128)(2,1)S(1)}, u32[]{:S(2)}, u32[]{:S(2)}) collective-permute-start(bf16[64,1152]{1,0:T(8,128)(2,1)S(1)} %pack.1.refs_3_.refs_0_), channel_id=1, source_target_pairs={{0,4},{1,5},{2,6},{3,7},{4,0},{5,1},{6,2},{7,3},{8,12},{9,13},{10,... | collective-permute-start | bytes 442376 | tf_op jit(solution)/shard_map/ppermute | solution.py:201
  6.6 1.5 %collective-permute-start = (bf16[64,1152]{1,0:T(8,128)(2,1)S(1)}, bf16[64,1152]{1,0:T(8,128)(2,1)S(1)}, u32[]{:S(2)}, u32[]{:S(2)}) collective-permute-start(bf16[64,1152]{1,0:T(8,128)(2,1)S(1)} %pack.1.refs_3_.refs_0_), channel_id=1, source_target_pairs={{0,2},{1,3},{2,0},{3,1},{4,6},{5,7},{6,4},{7,5},{8,10},{9,11},{10,... | collective-permute-start | bytes 442376 | tf_op jit(solution)/shard_map/ppermute | solution.py:201
  8.1 4.7 %load.1 = (bf16[16,1024]{1,0:T(8,128)(2,1)S(1)}, bf16[2,1024,2048]{2,1,0:T(8,128)(2,1)S(1)}, bf16[2,1024,1024]{2,1,0:T(8,128)(2,1)S(1)}) custom-call(bf16[2,1024]{1,0:T(2,128)(2,1)} %bitcast.3, bf16[2,1024,2048]{2,1,0:T(8,128)(2,1)} %refs_1_.3, bf16[2,1024,1024]{2,1,0:T(8,128)(2,1)} %refs_2_.1, bf16[64,1152]{1,0:T(8,128)(2,1)S(1)} %pack.1.refs_3_.refs_0_), custom_call_target="tpu_custom_call" | custom-call | bytes 10000 | tf_op jit(solution)/shard_map/load/pallas_call | solution.py:180
  13.4 0.9 %collective-permute-start.6 = (bf16[64,1152]{1,0:T(8,128)(2,1)S(1)}, bf16[64,1152]{1,0:T(8,128)(2,1)S(1)}, u32[]{:S(2)}, u32[]{:S(2)}) collective-permute-start(bf16[64,1152]{1,0:T(8,128)(2,1)S(1)} %get-tuple-element.80.refs_0_), channel_id=1, source_target_pairs={{0,2},{1,3},{2,0},{3,1},{4,6},{5,7},{6,4},{7,5},{8,10},{9,11},{10,... | collective-permute-start | bytes 442376 | tf_op jit(solution)/shard_map/ppermute | solution.py:201
  14.3 3.8 %collective-permute-done.5.refs_1_.refs_0_ = bf16[64,1152]{1,0:T(8,128)(2,1)S(1)} collective-permute-done((bf16[64,1152]{1,0:T(8,128)(2,1)S(1)}, bf16[64,1152]{1,0:T(8,128)(2,1)S(1)}, u32[]{:S(2)}, u32[]{:S(2)}) %collective-permute-start.5) | collective-permute-done | bytes 147488 | tf_op jit(solution)/shard_map/ppermute | solution.py:201
  18.6 1.2 %collective-permute-start.11 = (bf16[64,1152]{1,0:T(8,128)(2,1)S(1)}, bf16[64,1152]{1,0:T(8,128)(2,1)S(1)}, u32[]{:S(2)}, u32[]{:S(2)}) collective-permute-start(bf16[64,1152]{1,0:T(8,128)(2,1)S(1)} %collective-permute-done.5.refs_1_.refs_0_), channel_id=1, source_target_pairs={{0,2},{1,3},{2,0},{3,1},{4,6},{5,7},{6,4},{7,5},{8,10},{9,11},{10,... | collective-permute-start | bytes 442376 | tf_op jit(solution)/shard_map/ppermute | solution.py:201
  19.9 2.9 %expert.4 = (f32[128,1152]{1,0:T(8,128)S(1)}, bf16[64,1152]{1,0:T(8,128)(2,1)S(1)}, bf16[64,1152]{1,0:T(8,128)(2,1)S(1)}, bf16[16,1024]{1,0:T(8,128)(2,1)S(1)}, ...) custom-call(bf16[64,1152]{1,0:T(8,128)(2,1)S(1)} %get-tuple-element., ...), custom_call_target="tpu_custom_call", output_to_operand_aliasing={{3}: (4, {}), {4}: (5, {}), {5}: (6, {})} | custom-call | bytes 10000 | tf_op jit(solution)/shard_map/expert/pallas_call | solution.py:180
  23.5 1.3 %collective-permute-done.11.refs_3_ = bf16[64,1152]{1,0:T(8,128)(2,1)S(1)} collective-permute-done((bf16[64,1152]{1,0:T(8,128)(2,1)S(1)}, bf16[64,1152]{1,0:T(8,128)(2,1)S(1)}, u32[]{:S(2)}, u32[]{:S(2)}) %collective-permute-start.11) | collective-permute-done | bytes 147488 | tf_op jit(solution)/shard_map/ppermute | solution.py:201
  24.8 1.2 %collective-permute-start.15 = (bf16[64,1152]{1,0:T(8,128)(2,1)S(1)}, bf16[64,1152]{1,0:T(8,128)(2,1)S(1)}, u32[]{:S(2)}, u32[]{:S(2)}) collective-permute-start(bf16[64,1152]{1,0:T(8,128)(2,1)S(1)} %collective-permute-done.3.refs_0_), channel_id=1, source_target_pairs={{0,2},{1,3},{2,0},{3,1},{4,6},{5,7},{6,4},{7,5},{8,10},{9,11},{10,... | collective-permute-start | bytes 442376 | tf_op jit(solution)/shard_map/ppermute | solution.py:201
  26.1 0.9 %collective-permute-start.12 = (bf16[64,1152]{1,0:T(8,128)(2,1)S(1)}, bf16[64,1152]{1,0:T(8,128)(2,1)S(1)}, u32[]{:S(2)}, u32[]{:S(2)}) collective-permute-start(bf16[64,1152]{1,0:T(8,128)(2,1)S(1)} %get-tuple-element.97), channel_id=1, source_target_pairs={{0,2},{1,3},{2,0},{3,1},{4,6},{5,7},{6,4},{7,5},{8,10},{9,11},{10,... | collective-permute-start | bytes 442376 | tf_op jit(solution)/shard_map/ppermute | solution.py:201
  27.0 2.9 %expert.5 = (f32[128,1152]{1,0:T(8,128)S(1)}, bf16[64,1152]{1,0:T(8,128)(2,1)S(1)}, bf16[64,1152]{1,0:T(8,128)(2,1)S(1)}, bf16[16,1024]{1,0:T(8,128)(2,1)S(1)}, ...) custom-call(bf16[64,1152]{1,0:T(8,128)(2,1)S(1)} %collective-permute, ...), custom_call_target="tpu_custom_call", output_to_operand_aliasing={{3}: (4, {}), {4}: (5, {}), {5}: (6, {})} | custom-call | bytes 10000 | tf_op jit(solution)/shard_map/expert/pallas_call | solution.py:180
  30.5 0.9 %collective-permute-done.15.refs_4_ = bf16[64,1152]{1,0:T(8,128)(2,1)S(1)} collective-permute-done((bf16[64,1152]{1,0:T(8,128)(2,1)S(1)}, bf16[64,1152]{1,0:T(8,128)(2,1)S(1)}, u32[]{:S(2)}, u32[]{:S(2)}) %collective-permute-start.15) | collective-permute-done | bytes 147488 | tf_op jit(solution)/shard_map/ppermute | solution.py:201
  31.5 2.8 %collective-permute-done.12.refs_0_.refs_1_ = bf16[64,1152]{1,0:T(8,128)(2,1)S(1)} collective-permute-done((bf16[64,1152]{1,0:T(8,128)(2,1)S(1)}, bf16[64,1152]{1,0:T(8,128)(2,1)S(1)}, u32[]{:S(2)}, u32[]{:S(2)}) %collective-permute-start.12) | collective-permute-done | bytes 147488 | tf_op jit(solution)/shard_map/ppermute | solution.py:201
  34.3 1.3 %collective-permute-start.22 = (bf16[64,1152]{1,0:T(8,128)(2,1)S(1)}, bf16[64,1152]{1,0:T(8,128)(2,1)S(1)}, u32[]{:S(2)}, u32[]{:S(2)}) collective-permute-start(bf16[64,1152]{1,0:T(8,128)(2,1)S(1)} %get-tuple-element.119), channel_id=1, source_target_pairs={{0,2},{1,3},{2,0},{3,1},{4,6},{5,7},{6,4},{7,5},{8,10},{9,11},{10,... | collective-permute-start | bytes 442376 | tf_op jit(solution)/shard_map/ppermute | solution.py:201
  35.6 2.9 %expert.6 = (f32[128,1152]{1,0:T(8,128)S(1)}, bf16[64,1152]{1,0:T(8,128)(2,1)S(1)}, bf16[64,1152]{1,0:T(8,128)(2,1)S(1)}, bf16[16,1024]{1,0:T(8,128)(2,1)S(1)}, ...) custom-call(bf16[64,1152]{1,0:T(8,128)(2,1)S(1)} %collective-permute, ...), custom_call_target="tpu_custom_call", output_to_operand_aliasing={{3}: (4, {}), {4}: (5, {}), {5}: (6, {})} | custom-call | bytes 10000 | tf_op jit(solution)/shard_map/expert/pallas_call | solution.py:180
  39.6 1.0 %collective-permute-done.22.refs_1_ = bf16[64,1152]{1,0:T(8,128)(2,1)S(1)} collective-permute-done((bf16[64,1152]{1,0:T(8,128)(2,1)S(1)}, bf16[64,1152]{1,0:T(8,128)(2,1)S(1)}, u32[]{:S(2)}, u32[]{:S(2)}) %collective-permute-start.22) | collective-permute-done | bytes 147488 | tf_op jit(solution)/shard_map/ppermute | solution.py:201
  40.7 1.6 %collective-permute-start.26 = (bf16[64,1152]{1,0:T(8,128)(2,1)S(1)}, bf16[64,1152]{1,0:T(8,128)(2,1)S(1)}, u32[]{:S(2)}, u32[]{:S(2)}) collective-permute-start(bf16[64,1152]{1,0:T(8,128)(2,1)S(1)} %get-tuple-element.135), channel_id=1, source_target_pairs={{0,4},{1,5},{2,6},{3,7},{4,0},{5,1},{6,2},{7,3},{8,12},{9,13},{10,... | collective-permute-start | bytes 442376 | tf_op jit(solution)/shard_map/ppermute | solution.py:201
  43.2 2.9 %expert.7 = (f32[128,1152]{1,0:T(8,128)S(1)}, bf16[64,1152]{1,0:T(8,128)(2,1)S(1)}, bf16[64,1152]{1,0:T(8,128)(2,1)S(1)}, bf16[16,1024]{1,0:T(8,128)(2,1)S(1)}, ...) custom-call(bf16[64,1152]{1,0:T(8,128)(2,1)S(1)} %pack.1.refs_3_.ref, ...), custom_call_target="tpu_custom_call", output_to_operand_aliasing={{3}: (4, {}), {4}: (5, {}), {5}: (6, {})} | custom-call | bytes 10000 | tf_op jit(solution)/shard_map/expert/pallas_call | solution.py:180
  46.7 2.7 %collective-permute-start.27 = (bf16[64,1152]{1,0:T(8,128)(2,1)S(1)}, bf16[64,1152]{1,0:T(8,128)(2,1)S(1)}, u32[]{:S(2)}, u32[]{:S(2)}) collective-permute-start(bf16[64,1152]{1,0:T(8,128)(2,1)S(1)} %get-tuple-element.146), channel_id=1, source_target_pairs={{0,8},{1,9},{2,10},{3,11},{4,12},{5,13},{6,14},{7,15},{8,0},{9,1},... | collective-permute-start | bytes 442376 | tf_op jit(solution)/shard_map/ppermute | solution.py:201
  49.5 1.6 %collective-permute-start.29 = (bf16[64,1152]{1,0:T(8,128)(2,1)S(1)}, bf16[64,1152]{1,0:T(8,128)(2,1)S(1)}, u32[]{:S(2)}, u32[]{:S(2)}) collective-permute-start(bf16[64,1152]{1,0:T(8,128)(2,1)S(1)} %get-tuple-element.148), channel_id=1, source_target_pairs={{0,2},{1,3},{2,0},{3,1},{4,6},{5,7},{6,4},{7,5},{8,10},{9,11},{10,... | collective-permute-start | bytes 442376 | tf_op jit(solution)/shard_map/ppermute | solution.py:201
  51.8 5.0 %collective-permute-done.27.refs_1_ = bf16[64,1152]{1,0:T(8,128)(2,1)S(1)} collective-permute-done((bf16[64,1152]{1,0:T(8,128)(2,1)S(1)}, bf16[64,1152]{1,0:T(8,128)(2,1)S(1)}, u32[]{:S(2)}, u32[]{:S(2)}) %collective-permute-start.27) | collective-permute-done | bytes 147488 | tf_op jit(solution)/shard_map/ppermute | solution.py:201
  56.8 1.2 %collective-permute-done.28.refs_2_ = bf16[64,1152]{1,0:T(8,128)(2,1)S(1)} collective-permute-done((bf16[64,1152]{1,0:T(8,128)(2,1)S(1)}, bf16[64,1152]{1,0:T(8,128)(2,1)S(1)}, u32[]{:S(2)}, u32[]{:S(2)}) %collective-permute-start.28) | collective-permute-done | bytes 147488 | tf_op jit(solution)/shard_map/ppermute | solution.py:201
  (54 shorter events, 6.8 us)
Async XLA Ops:
  0.9 11.9 %collective-permute-start.4 = (bf16[64,1152]{1,0:T(8,128)(2,1)S(1)}, bf16[64,1152]{1,0:T(8,128)(2,1)S(1)}, u32[]{:S(2)}, u32[]{:S(2)}) collective-permute-start(bf16[64,1152]{1,0:T(8,128)(2,1)S(1)} %pack.1.refs_3_.refs_0_), channel_id=1, source_target_pairs={{0,8},{1,9},{2,10},{3,11},{4,12},{5,13},{6,14},{7,15},{8,0},{9,1},... | collective-permute-start | bytes 442376 | tf_op jit(solution)/shard_map/ppermute | solution.py:201
  5.0 9.3 %collective-permute-start.3 = (bf16[64,1152]{1,0:T(8,128)(2,1)S(1)}, bf16[64,1152]{1,0:T(8,128)(2,1)S(1)}, u32[]{:S(2)}, u32[]{:S(2)}) collective-permute-start(bf16[64,1152]{1,0:T(8,128)(2,1)S(1)} %pack.1.refs_3_.refs_0_), channel_id=1, source_target_pairs={{0,4},{1,5},{2,6},{3,7},{4,0},{5,1},{6,2},{7,3},{8,12},{9,13},{10,... | collective-permute-start | bytes 442376 | tf_op jit(solution)/shard_map/ppermute | solution.py:201
  6.6 7.7 %collective-permute-start = (bf16[64,1152]{1,0:T(8,128)(2,1)S(1)}, bf16[64,1152]{1,0:T(8,128)(2,1)S(1)}, u32[]{:S(2)}, u32[]{:S(2)}) collective-permute-start(bf16[64,1152]{1,0:T(8,128)(2,1)S(1)} %pack.1.refs_3_.refs_0_), channel_id=1, source_target_pairs={{0,2},{1,3},{2,0},{3,1},{4,6},{5,7},{6,4},{7,5},{8,10},{9,11},{10,... | collective-permute-start | bytes 442376 | tf_op jit(solution)/shard_map/ppermute | solution.py:201
  12.9 5.2 %collective-permute-start.5 = (bf16[64,1152]{1,0:T(8,128)(2,1)S(1)}, bf16[64,1152]{1,0:T(8,128)(2,1)S(1)}, u32[]{:S(2)}, u32[]{:S(2)}) collective-permute-start(bf16[64,1152]{1,0:T(8,128)(2,1)S(1)} %get-tuple-element.80.refs_0_), channel_id=1, source_target_pairs={{0,4},{1,5},{2,6},{3,7},{4,0},{5,1},{6,2},{7,3},{8,12},{9,13},{10,... | collective-permute-start | bytes 442376 | tf_op jit(solution)/shard_map/ppermute | solution.py:201
  13.4 5.1 %collective-permute-start.6 = (bf16[64,1152]{1,0:T(8,128)(2,1)S(1)}, bf16[64,1152]{1,0:T(8,128)(2,1)S(1)}, u32[]{:S(2)}, u32[]{:S(2)}) collective-permute-start(bf16[64,1152]{1,0:T(8,128)(2,1)S(1)} %get-tuple-element.80.refs_0_), channel_id=1, source_target_pairs={{0,2},{1,3},{2,0},{3,1},{4,6},{5,7},{6,4},{7,5},{8,10},{9,11},{10,... | collective-permute-start | bytes 442376 | tf_op jit(solution)/shard_map/ppermute | solution.py:201
  14.3 5.5 %collective-permute-start.7 = (bf16[64,1152]{1,0:T(8,128)(2,1)S(1)}, bf16[64,1152]{1,0:T(8,128)(2,1)S(1)}, u32[]{:S(2)}, u32[]{:S(2)}) collective-permute-start(bf16[64,1152]{1,0:T(8,128)(2,1)S(1)} %get-tuple-element.80.refs_0_), channel_id=1, source_target_pairs={{0,1},{1,0},{2,3},{3,2},{4,5},{5,4},{6,7},{7,6},{8,9},{9,8},{10,11... | collective-permute-start | bytes 442376 | tf_op jit(solution)/shard_map/ppermute | solution.py:201
  18.6 6.3 %collective-permute-start.11 = (bf16[64,1152]{1,0:T(8,128)(2,1)S(1)}, bf16[64,1152]{1,0:T(8,128)(2,1)S(1)}, u32[]{:S(2)}, u32[]{:S(2)}) collective-permute-start(bf16[64,1152]{1,0:T(8,128)(2,1)S(1)} %collective-permute-done.5.refs_1_.refs_0_), channel_id=1, source_target_pairs={{0,2},{1,3},{2,0},{3,1},{4,6},{5,7},{6,4},{7,5},{8,10},{9,11},{10,... | collective-permute-start | bytes 442376 | tf_op jit(solution)/shard_map/ppermute | solution.py:201
  23.4 3.6 %collective-permute-start.13 = (bf16[64,1152]{1,0:T(8,128)(2,1)S(1)}, bf16[64,1152]{1,0:T(8,128)(2,1)S(1)}, u32[]{:S(2)}, u32[]{:S(2)}) collective-permute-start(bf16[64,1152]{1,0:T(8,128)(2,1)S(1)} %collective-permute-done.5.refs_1_.refs_0_), channel_id=1, source_target_pairs={{0,1},{1,0},{2,3},{3,2},{4,5},{5,4},{6,7},{7,6},{8,9},{9,8},{10,11... | collective-permute-start | bytes 442376 | tf_op jit(solution)/shard_map/ppermute | solution.py:201
  24.8 6.6 %collective-permute-start.15 = (bf16[64,1152]{1,0:T(8,128)(2,1)S(1)}, bf16[64,1152]{1,0:T(8,128)(2,1)S(1)}, u32[]{:S(2)}, u32[]{:S(2)}) collective-permute-start(bf16[64,1152]{1,0:T(8,128)(2,1)S(1)} %collective-permute-done.3.refs_0_), channel_id=1, source_target_pairs={{0,2},{1,3},{2,0},{3,1},{4,6},{5,7},{6,4},{7,5},{8,10},{9,11},{10,... | collective-permute-start | bytes 442376 | tf_op jit(solution)/shard_map/ppermute | solution.py:201
  26.1 8.1 %collective-permute-start.12 = (bf16[64,1152]{1,0:T(8,128)(2,1)S(1)}, bf16[64,1152]{1,0:T(8,128)(2,1)S(1)}, u32[]{:S(2)}, u32[]{:S(2)}) collective-permute-start(bf16[64,1152]{1,0:T(8,128)(2,1)S(1)} %get-tuple-element.97), channel_id=1, source_target_pairs={{0,2},{1,3},{2,0},{3,1},{4,6},{5,7},{6,4},{7,5},{8,10},{9,11},{10,... | collective-permute-start | bytes 442376 | tf_op jit(solution)/shard_map/ppermute | solution.py:201
  29.9 4.4 %collective-permute-start.18 = (bf16[64,1152]{1,0:T(8,128)(2,1)S(1)}, bf16[64,1152]{1,0:T(8,128)(2,1)S(1)}, u32[]{:S(2)}, u32[]{:S(2)}) collective-permute-start(bf16[64,1152]{1,0:T(8,128)(2,1)S(1)} %get-tuple-element.107), channel_id=1, source_target_pairs={{0,1},{1,0},{2,3},{3,2},{4,5},{5,4},{6,7},{7,6},{8,9},{9,8},{10,11... | collective-permute-start | bytes 442376 | tf_op jit(solution)/shard_map/ppermute | solution.py:201
  30.0 4.3 %collective-permute-start.19 = (bf16[64,1152]{1,0:T(8,128)(2,1)S(1)}, bf16[64,1152]{1,0:T(8,128)(2,1)S(1)}, u32[]{:S(2)}, u32[]{:S(2)}) collective-permute-start(bf16[64,1152]{1,0:T(8,128)(2,1)S(1)} %get-tuple-element.108), channel_id=1, source_target_pairs={{0,1},{1,0},{2,3},{3,2},{4,5},{5,4},{6,7},{7,6},{8,9},{9,8},{10,11... | collective-permute-start | bytes 442376 | tf_op jit(solution)/shard_map/ppermute | solution.py:201
  30.5 5.2 %collective-permute-start.16 = (bf16[64,1152]{1,0:T(8,128)(2,1)S(1)}, bf16[64,1152]{1,0:T(8,128)(2,1)S(1)}, u32[]{:S(2)}, u32[]{:S(2)}) collective-permute-start(bf16[64,1152]{1,0:T(8,128)(2,1)S(1)} %collective-permute-done.3.refs_0_), channel_id=1, source_target_pairs={{0,1},{1,0},{2,3},{3,2},{4,5},{5,4},{6,7},{7,6},{8,9},{9,8},{10,11... | collective-permute-start | bytes 442376 | tf_op jit(solution)/shard_map/ppermute | solution.py:201
  34.3 6.3 %collective-permute-start.22 = (bf16[64,1152]{1,0:T(8,128)(2,1)S(1)}, bf16[64,1152]{1,0:T(8,128)(2,1)S(1)}, u32[]{:S(2)}, u32[]{:S(2)}) collective-permute-start(bf16[64,1152]{1,0:T(8,128)(2,1)S(1)} %get-tuple-element.119), channel_id=1, source_target_pairs={{0,2},{1,3},{2,0},{3,1},{4,6},{5,7},{6,4},{7,5},{8,10},{9,11},{10,... | collective-permute-start | bytes 442376 | tf_op jit(solution)/shard_map/ppermute | solution.py:201
  38.5 3.8 %collective-permute-start.20 = (bf16[64,1152]{1,0:T(8,128)(2,1)S(1)}, bf16[64,1152]{1,0:T(8,128)(2,1)S(1)}, u32[]{:S(2)}, u32[]{:S(2)}) collective-permute-start(bf16[64,1152]{1,0:T(8,128)(2,1)S(1)} %get-tuple-element.116), channel_id=1, source_target_pairs={{0,1},{1,0},{2,3},{3,2},{4,5},{5,4},{6,7},{7,6},{8,9},{9,8},{10,11... | collective-permute-start | bytes 442376 | tf_op jit(solution)/shard_map/ppermute | solution.py:201
  38.8 3.5 %collective-permute-start.21 = (bf16[64,1152]{1,0:T(8,128)(2,1)S(1)}, bf16[64,1152]{1,0:T(8,128)(2,1)S(1)}, u32[]{:S(2)}, u32[]{:S(2)}) collective-permute-start(bf16[64,1152]{1,0:T(8,128)(2,1)S(1)} %get-tuple-element.117), channel_id=1, source_target_pairs={{0,1},{1,0},{2,3},{3,2},{4,5},{5,4},{6,7},{7,6},{8,9},{9,8},{10,11... | collective-permute-start | bytes 442376 | tf_op jit(solution)/shard_map/ppermute | solution.py:201
  39.1 4.1 %collective-permute-start.1 = (bf16[64,1152]{1,0:T(8,128)(2,1)S(1)}, bf16[64,1152]{1,0:T(8,128)(2,1)S(1)}, u32[]{:S(2)}, u32[]{:S(2)}) collective-permute-start(bf16[64,1152]{1,0:T(8,128)(2,1)S(1)} %pack.1.refs_3_.refs_0_), channel_id=1, source_target_pairs={{0,1},{1,0},{2,3},{3,2},{4,5},{5,4},{6,7},{7,6},{8,9},{9,8},{10,11... | collective-permute-start | bytes 442376 | tf_op jit(solution)/shard_map/ppermute | solution.py:201
  39.3 3.9 %collective-permute-start.2 = (bf16[64,1152]{1,0:T(8,128)(2,1)S(1)}, bf16[64,1152]{1,0:T(8,128)(2,1)S(1)}, u32[]{:S(2)}, u32[]{:S(2)}) collective-permute-start(bf16[64,1152]{1,0:T(8,128)(2,1)S(1)} %collective-permute-done.refs_2_.refs_1_), channel_id=1, source_target_pairs={{0,1},{1,0},{2,3},{3,2},{4,5},{5,4},{6,7},{7,6},{8,9},{9,8},{10,11... | collective-permute-start | bytes 442376 | tf_op jit(solution)/shard_map/ppermute | solution.py:201
  40.7 6.0 %collective-permute-start.26 = (bf16[64,1152]{1,0:T(8,128)(2,1)S(1)}, bf16[64,1152]{1,0:T(8,128)(2,1)S(1)}, u32[]{:S(2)}, u32[]{:S(2)}) collective-permute-start(bf16[64,1152]{1,0:T(8,128)(2,1)S(1)} %get-tuple-element.135), channel_id=1, source_target_pairs={{0,4},{1,5},{2,6},{3,7},{4,0},{5,1},{6,2},{7,3},{8,12},{9,13},{10,... | collective-permute-start | bytes 442376 | tf_op jit(solution)/shard_map/ppermute | solution.py:201
  42.4 7.0 %collective-permute-start.25 = (bf16[64,1152]{1,0:T(8,128)(2,1)S(1)}, bf16[64,1152]{1,0:T(8,128)(2,1)S(1)}, u32[]{:S(2)}, u32[]{:S(2)}) collective-permute-start(bf16[64,1152]{1,0:T(8,128)(2,1)S(1)} %get-tuple-element.133), channel_id=1, source_target_pairs={{0,2},{1,3},{2,0},{3,1},{4,6},{5,7},{6,4},{7,5},{8,10},{9,11},{10,... | collective-permute-start | bytes 442376 | tf_op jit(solution)/shard_map/ppermute | solution.py:201
  46.1 3.3 %collective-permute-start.23 = (bf16[64,1152]{1,0:T(8,128)(2,1)S(1)}, bf16[64,1152]{1,0:T(8,128)(2,1)S(1)}, u32[]{:S(2)}, u32[]{:S(2)}) collective-permute-start(bf16[64,1152]{1,0:T(8,128)(2,1)S(1)} %get-tuple-element.130), channel_id=1, source_target_pairs={{0,1},{1,0},{2,3},{3,2},{4,5},{5,4},{6,7},{7,6},{8,9},{9,8},{10,11... | collective-permute-start | bytes 442376 | tf_op jit(solution)/shard_map/ppermute | solution.py:201
  46.7 10.1 %collective-permute-start.27 = (bf16[64,1152]{1,0:T(8,128)(2,1)S(1)}, bf16[64,1152]{1,0:T(8,128)(2,1)S(1)}, u32[]{:S(2)}, u32[]{:S(2)}) collective-permute-start(bf16[64,1152]{1,0:T(8,128)(2,1)S(1)} %get-tuple-element.146), channel_id=1, source_target_pairs={{0,8},{1,9},{2,10},{3,11},{4,12},{5,13},{6,14},{7,15},{8,0},{9,1},... | collective-permute-start | bytes 442376 | tf_op jit(solution)/shard_map/ppermute | solution.py:201
  49.5 7.3 %collective-permute-start.29 = (bf16[64,1152]{1,0:T(8,128)(2,1)S(1)}, bf16[64,1152]{1,0:T(8,128)(2,1)S(1)}, u32[]{:S(2)}, u32[]{:S(2)}) collective-permute-start(bf16[64,1152]{1,0:T(8,128)(2,1)S(1)} %get-tuple-element.148), channel_id=1, source_target_pairs={{0,2},{1,3},{2,0},{3,1},{4,6},{5,7},{6,4},{7,5},{8,10},{9,11},{10,... | collective-permute-start | bytes 442376 | tf_op jit(solution)/shard_map/ppermute | solution.py:201
  51.1 6.9 %collective-permute-start.28 = (bf16[64,1152]{1,0:T(8,128)(2,1)S(1)}, bf16[64,1152]{1,0:T(8,128)(2,1)S(1)}, u32[]{:S(2)}, u32[]{:S(2)}) collective-permute-start(bf16[64,1152]{1,0:T(8,128)(2,1)S(1)} %get-tuple-element.147), channel_id=1, source_target_pairs={{0,4},{1,5},{2,6},{3,7},{4,0},{5,1},{6,2},{7,3},{8,12},{9,13},{10,... | collective-permute-start | bytes 442376 | tf_op jit(solution)/shard_map/ppermute | solution.py:201
  (6 other events, 14.5 us)

commit v13 on v12

--- a/solution.py
+++ b/solution.py
@@ -8,7 +8,7 @@
 from jax.sharding import PartitionSpec as P
 
 GROUP = 16
-SCOPED = 2 * 1024 * 1024
+SCOPED = 8 * 1024 * 1024
 TAIL = 128
 SCALE = 2.0**40
 STEP = 256
@@ -48,67 +48,72 @@
         copy.wait()
 
 
-def expert_kernel(
-    a_ref, b_ref, c_ref, d_ref, columns_ref, up_ref, down_ref, keep_ref, *refs
-):
-    *send_refs, inner_ref, result_ref = refs
-    blocks = (a_ref, b_ref, c_ref, d_ref)
-    rows, wide = a_ref.shape
+def expert_kernel(count, *refs):
+    blocks, refs = refs[: 4 * count], refs[4 * count :]
+    (columns_ref, up_ref, down_ref), refs = refs[:3], refs[3:]
+    keep_refs, refs = refs[:count], refs[count:]
+    send_refs, (packed_ref, inner_ref, result_ref) = refs[: 2 * count], refs[2 * count :]
+    rows, wide = blocks[0].shape
     half, lat = 2 * rows, wide - TAIL
     local, eff, _ = down_ref.shape
-    slots = result_ref.shape[0] // local
-    x = jnp.concatenate([ref[:, :lat] for ref in blocks], axis=0)
-    tail = jnp.concatenate([ref[:, lat:] for ref in blocks], axis=0).astype(jnp.float32)
-
-    def put(lanes, value):
-        keep_ref[:, lanes] = value[:half]
-        for i, ref in enumerate(send_refs):
-            ref[:, lanes] = value[half + i * rows : half + (i + 1) * rows].astype(jnp.bfloat16)
+    slots = packed_ref.shape[1] // count
+
+    def put(i, lanes, value):
+        keep_refs[i][:, lanes] = value[:half]
+        for j, ref in enumerate(send_refs[2 * i : 2 * i + 2]):
+            ref[:, lanes] = value[half + j * rows : half + (j + 1) * rows].astype(jnp.bfloat16)
 
     def logits_of(values):
         return lax.dot_general(
             values, columns_ref[...], (((1,), (1,)), ((), ())), preferred_element_type=jnp.float32
         )
 
-    logits = logits_of(x)
     lane = lax.broadcasted_iota(jnp.int32, (2 * half, TAIL), 1)
-    masks, sums = [], jnp.zeros((2 * half, 1), jnp.float32)
-    marks = jnp.zeros((2 * half, TAIL), jnp.float32)
-    for e in range(local):
-        label = (lax.axis_index("exp") * local + e).astype(jnp.float32)
-        mask = jnp.max(jnp.where(tail == label, 1.0, 0.0), axis=1, keepdims=True)
-        sums = sums + jax.nn.sigmoid(logits[:, e : e + 1]) * (mask * SCALE)
-        marks = jnp.where(lane == e, mask, marks)
-        masks.append(mask)
     row = lax.broadcasted_iota(jnp.int32, (2 * half, 2 * half), 0)
     col = lax.broadcasted_iota(jnp.int32, (2 * half, 2 * half), 1)
     before = jnp.where(col < row, 1.0, 0.0).astype(jnp.bfloat16)
-    place = jnp.dot(before, marks.astype(jnp.bfloat16), preferred_element_type=jnp.float32)
     slot = lax.broadcasted_iota(jnp.int32, (2 * half, slots), 1).astype(jnp.float32)
-    spread = jnp.concatenate(
-        [jnp.where((slot == place[:, e : e + 1]) & (masks[e] > 0.0), 1.0, 0.0) for e in range(local)], axis=1
-    ).astype(jnp.bfloat16)
-    packed = lax.dot_general(
-        spread, x, (((0,), (0,)), ((), ())), preferred_element_type=jnp.float32
-    ).astype(jnp.bfloat16)
-    scores = jax.nn.sigmoid(logits_of(packed)) * SCALE
+    spreads = []
+    for i in range(count):
+        batch = blocks[4 * i : 4 * i + 4]
+        x = jnp.concatenate([ref[:, :lat] for ref in batch], axis=0)
+        tail = jnp.concatenate([ref[:, lat:] for ref in batch], axis=0).astype(jnp.float32)
+        logits = logits_of(x)
+        masks, sums = [], jnp.zeros((2 * half, 1), jnp.float32)
+        marks = jnp.zeros((2 * half, TAIL), jnp.float32)
+        for e in range(local):
+            label = (lax.axis_index("exp") * local + e).astype(jnp.float32)
+            mask = jnp.max(jnp.where(tail == label, 1.0, 0.0), axis=1, keepdims=True)
+            sums = sums + jax.nn.sigmoid(logits[:, e : e + 1]) * (mask * SCALE)
+            marks = jnp.where(lane == e, mask, marks)
+            masks.append(mask)
+        put(i, slice(lat, wide), jnp.where(lane == 0, sums, 0.0))
+        place = jnp.dot(before, marks.astype(jnp.bfloat16), preferred_element_type=jnp.float32)
+        spread = jnp.concatenate(
+            [jnp.where((slot == place[:, e : e + 1]) & (masks[e] > 0.0), 1.0, 0.0) for e in range(local)],
+            axis=1,
+        ).astype(jnp.bfloat16)
+        packed = lax.dot_general(
+            spread, x, (((0,), (0,)), ((), ())), preferred_element_type=jnp.float32
+        ).astype(jnp.bfloat16)
+        for e in range(local):
+            packed_ref[e, i * slots : (i + 1) * slots, :] = packed[e * slots : (e + 1) * slots]
+        spreads.append(spread)
     for e in range(local):
-        mine = slice(e * slots, (e + 1) * slots)
-        chosen = packed[mine]
-        score = scores[mine, e : e + 1]
+        chosen = packed_ref[e]
+        score = jax.nn.sigmoid(logits_of(chosen)[:, e : e + 1]) * SCALE
         for c in range(0, eff, STEP):
             gate = jnp.dot(chosen, up_ref[e, :, c : c + STEP], preferred_element_type=jnp.float32)
             up = jnp.dot(chosen, up_ref[e, :, eff + c : eff + c + STEP], preferred_element_type=jnp.float32)
-            inner_ref[mine, c : c + STEP] = (gate / (1.0 + jnp.exp(-gate)) * up * score).astype(jnp.bfloat16)
+            inner_ref[e, :, c : c + STEP] = (gate / (1.0 + jnp.exp(-gate)) * up * score).astype(jnp.bfloat16)
     for e in range(local):
-        mine = slice(e * slots, (e + 1) * slots)
-        result_ref[mine, :] = jnp.dot(
-            inner_ref[mine, :], down_ref[e], preferred_element_type=jnp.float32
-        ).astype(jnp.bfloat16)
-    for c in range(0, lat, STEP):
-        part = jnp.dot(spread, result_ref[:, c : c + STEP], preferred_element_type=jnp.float32)
-        put(slice(c, c + STEP), part)
-    put(slice(lat, wide), jnp.where(lane == 0, sums, 0.0))
+        result = jnp.dot(inner_ref[e], down_ref[e], preferred_element_type=jnp.float32).astype(jnp.bfloat16)
+        for i in range(count):
+            result_ref[i, e * slots : (e + 1) * slots, :] = result[i * slots : (i + 1) * slots]
+    for i in range(count):
+        for c in range(0, lat, STEP):
+            part = jnp.dot(spreads[i], result_ref[i, :, c : c + STEP], preferred_element_type=jnp.float32)
+            put(i, slice(c, c + STEP), part)
 
 
 def tie_kernel():
@@ -158,6 +163,8 @@
 
 
 def call(kernel, outs, args=(), deps=(), chain=(), hbm=(), scratch=()):
+    plain = getattr(kernel, "func", kernel)
+    reads_chain = plain is expert_kernel
     n_in = len(args) + len(hbm)
     n_skip = n_in + len(deps)
     n_outs = n_skip + len(chain)
@@ -178,7 +185,7 @@
     operands = [in_vmem(a) for a in args] + [in_hbm(h) for h in hbm]
     operands += [in_vmem(x) for x in (*deps, *chain)]
     return pl.pallas_call(
-        body_with_chain if kernel is expert_kernel else body,
+        body_with_chain if reads_chain else body,
         out_shape=list(outs) + [pltpu.VMEM(x.shape, x.dtype) for x in chain],
         in_specs=specs,
         out_specs=[VMEM] * (len(outs) + len(chain)),
@@ -186,7 +193,7 @@
         compiler_params=pltpu.CompilerParams(vmem_limit_bytes=SCOPED),
         cost_estimate=pl.CostEstimate(flops=0, bytes_accessed=10_000, transcendentals=0),
         input_output_aliases={n_skip + i: len(outs) + i for i in range(len(chain))},
-        name=kernel.__name__.removesuffix("_kernel"),
+        name=plain.__name__.removesuffix("_kernel"),
     )(*operands)
 
 
@@ -239,23 +246,29 @@
         def gather(k, deps=()):
             other[k] = tie(swap(block[k], 2), deps)
 
-        def compute(k):
-            blocks = [block[k], other[k]]
-            blocks += [swap(one, 1) for one in blocks]
-            keep[k], *send[k] = step(
-                expert_kernel,
-                [space(2 * rows, jnp.float32), space(rows, jnp.bfloat16), space(rows, jnp.bfloat16)],
+        def compute(*ks):
+            count = len(ks)
+            blocks = []
+            for k in ks:
+                near = [block[k], other[k]]
+                blocks += near + [swap(one, 1) for one in near]
+            result = step(
+                functools.partial(expert_kernel, count),
+                [space(2 * rows, jnp.float32)] * count + [space(rows, jnp.bfloat16)] * (2 * count),
                 blocks,
                 scratch=[
-                    pltpu.VMEM((local * slots, eff), jnp.bfloat16),
-                    pltpu.VMEM((local * slots, lat), jnp.bfloat16),
+                    pltpu.VMEM((local, count * slots, lat), jnp.bfloat16),
+                    pltpu.VMEM((local, count * slots, eff), jnp.bfloat16),
+                    pltpu.VMEM((count, local * slots, lat), jnp.bfloat16),
                 ],
             )
-            came[k] = [swap(part, 1) for part in send[k]]
-
-        def reduce_core(k):
+            for i, k in enumerate(ks):
+                keep[k] = result[i]
+                came[k] = [swap(part, 1) for part in result[count + 2 * i : count + 2 * i + 2]]
+
+        def reduce_core(k, deps=()):
             fold_keep[k], fold_send[k] = step(
-                fold_kernel, [space(rows, jnp.float32), space(rows, jnp.bfloat16)], [keep[k], *came[k]]
+                fold_kernel, [space(rows, jnp.float32), space(rows, jnp.bfloat16)], [keep[k], *came[k]], deps
             )
             y_came[k] = swap(fold_send[k], 2)
 
@@ -270,16 +283,15 @@
         compute(2)
         gather(3)
         reduce_core(2)
+        gather(1)
         compute(3)
-        gather(1, [y_came[2]])
-        reduce_core(3)
-        compute(1)
+        reduce_core(3, [y_came[2]])
+        compute(1, 0)
         z_3 = swap(reduce_y(3), 4)
         reduce_core(1)
-        compute(0)
+        reduce_core(0)
         z_2 = swap(reduce_y(2, z_3), 8)
         z_1 = swap(reduce_y(1), 4)
-        reduce_core(0)
         return fold_keep[0], z_2, z_1, y_came[0]
 
     packet = call(

time: 59 us -> 59.1 us (level)
  Pallas kernels: 18.3 us -> 17.6 us
    pallas_call x17 -> x16, Pallas kernels: 17.5 us -> 16.9 us  [call(): pl.pallas_call(body_with_chain if reads_chain else body, out_shape=list(o...]
  transfers between devices with their start and end apart: 30 -> 30, of which waited for: 9 -> 9; matrix products, arithmetic and copies ran while one was open for 0% -> 0% of each run, Pallas kernels for 28% -> 27%
where the time goes in v13:
time: 59.1 us; the launch traced here: 58.9 us
  starting transfers between devices  23.9 us (40%)
  Pallas kernels  17.6 us (30%)
  waiting for transfers between devices  17.2 us (29%)
    ppermute x30, starting transfers between devices, swap(): return lax.ppermute(x, 'exp', [(i, i ^ bits) for i in range(n_dev)])  23.9 us
    ppermute x30, waiting for transfers between devices, swap(): return lax.ppermute(x, 'exp', [(i, i ^ bits) for i in range(n_dev)])  17.2 us
    pallas_call x16, Pallas kernels, call(): pl.pallas_call(body_with_chain if reads_chain else body, out_shape=list(o...  16.9 us
  transfers between devices with their start and end apart: 30, of which 9 were waited for; matrix products, arithmetic and copies ran while one was open for 0% of the time, Pallas kernels for 27%

profile of v13, /device:TPU:0, one launch (start us, length us, event | category | flops | bytes accessed | tf_op | source)
XLA Modules:
  0.0 58.9 jit_solution(11832598734412220119)
XLA Ops:
  0.0 0.9 %pack.1.refs_3_.refs_4_ = bf16[64,1152]{1,0:T(8,128)(2,1)S(1)} custom-call(s32[8,64]{1,0:T(8,128)} %bitcast.2, bf16[64,1024]{1,0:T(8,128)(2,1)} %refs_1_.2), custom_call_target="tpu_custom_call" | custom-call | bytes 10000 | tf_op jit(solution)/shard_map/pack/pallas_call | solution.py:187
  0.9 4.1 %collective-permute-start.1 = (bf16[64,1152]{1,0:T(8,128)(2,1)S(1)}, bf16[64,1152]{1,0:T(8,128)(2,1)S(1)}, u32[]{:S(2)}, u32[]{:S(2)}) collective-permute-start(bf16[64,1152]{1,0:T(8,128)(2,1)S(1)} %pack.1.refs_3_.refs_4_), channel_id=1, source_target_pairs={{0,8},{1,9},{2,10},{3,11},{4,12},{5,13},{6,14},{7,15},{8,0},{9,1},... | collective-permute-start | bytes 442376 | tf_op jit(solution)/shard_map/ppermute | solution.py:208
  5.0 1.5 %collective-permute-start.3 = (bf16[64,1152]{1,0:T(8,128)(2,1)S(1)}, bf16[64,1152]{1,0:T(8,128)(2,1)S(1)}, u32[]{:S(2)}, u32[]{:S(2)}) collective-permute-start(bf16[64,1152]{1,0:T(8,128)(2,1)S(1)} %pack.1.refs_3_.refs_4_), channel_id=1, source_target_pairs={{0,2},{1,3},{2,0},{3,1},{4,6},{5,7},{6,4},{7,5},{8,10},{9,11},{10,... | collective-permute-start | bytes 442376 | tf_op jit(solution)/shard_map/ppermute | solution.py:208
  6.6 1.6 %collective-permute-start = (bf16[64,1152]{1,0:T(8,128)(2,1)S(1)}, bf16[64,1152]{1,0:T(8,128)(2,1)S(1)}, u32[]{:S(2)}, u32[]{:S(2)}) collective-permute-start(bf16[64,1152]{1,0:T(8,128)(2,1)S(1)} %pack.1.refs_3_.refs_4_), channel_id=1, source_target_pairs={{0,4},{1,5},{2,6},{3,7},{4,0},{5,1},{6,2},{7,3},{8,12},{9,13},{10,... | collective-permute-start | bytes 442376 | tf_op jit(solution)/shard_map/ppermute | solution.py:208
  8.1 4.7 %load.1 = (bf16[16,1024]{1,0:T(8,128)(2,1)S(1)}, bf16[2,1024,2048]{2,1,0:T(8,128)(2,1)S(1)}, bf16[2,1024,1024]{2,1,0:T(8,128)(2,1)S(1)}) custom-call(bf16[2,1024]{1,0:T(2,128)(2,1)} %bitcast.3, bf16[2,1024,2048]{2,1,0:T(8,128)(2,1)} %refs_1_.3, bf16[2,1024,1024]{2,1,0:T(8,128)(2,1)} %refs_2_.1, bf16[64,1152]{1,0:T(8,128)(2,1)S(1)} %pack.1.refs_3_.refs_4_), custom_call_target="tpu_custom_call" | custom-call | bytes 10000 | tf_op jit(solution)/shard_map/load/pallas_call | solution.py:187
  12.9 0.8 %collective-permute-start.4 = (bf16[64,1152]{1,0:T(8,128)(2,1)S(1)}, bf16[64,1152]{1,0:T(8,128)(2,1)S(1)}, u32[]{:S(2)}, u32[]{:S(2)}) collective-permute-start(bf16[64,1152]{1,0:T(8,128)(2,1)S(1)} %get-tuple-element.77.refs_0_), channel_id=1, source_target_pairs={{0,2},{1,3},{2,0},{3,1},{4,6},{5,7},{6,4},{7,5},{8,10},{9,11},{10,... | collective-permute-start | bytes 442376 | tf_op jit(solution)/shard_map/ppermute | solution.py:208
  14.3 3.8 %collective-permute-done.4.refs_6_ = bf16[64,1152]{1,0:T(8,128)(2,1)S(1)} collective-permute-done((bf16[64,1152]{1,0:T(8,128)(2,1)S(1)}, bf16[64,1152]{1,0:T(8,128)(2,1)S(1)}, u32[]{:S(2)}, u32[]{:S(2)}) %collective-permute-start.4) | collective-permute-done | bytes 147488 | tf_op jit(solution)/shard_map/ppermute | solution.py:208
  18.1 0.8 %collective-permute-done.2.refs_1_.refs_0_ = bf16[64,1152]{1,0:T(8,128)(2,1)S(1)} collective-permute-done((bf16[64,1152]{1,0:T(8,128)(2,1)S(1)}, bf16[64,1152]{1,0:T(8,128)(2,1)S(1)}, u32[]{:S(2)}, u32[]{:S(2)}) %collective-permute-start.2) | collective-permute-done | bytes 147488 | tf_op jit(solution)/shard_map/ppermute | solution.py:208
  18.9 1.3 %collective-permute-start.9 = (bf16[64,1152]{1,0:T(8,128)(2,1)S(1)}, bf16[64,1152]{1,0:T(8,128)(2,1)S(1)}, u32[]{:S(2)}, u32[]{:S(2)}) collective-permute-start(bf16[64,1152]{1,0:T(8,128)(2,1)S(1)} %collective-permute-done.2.refs_1_.refs_0_), channel_id=1, source_target_pairs={{0,2},{1,3},{2,0},{3,1},{4,6},{5,7},{6,4},{7,5},{8,10},{9,11},{10,... | collective-permute-start | bytes 442376 | tf_op jit(solution)/shard_map/ppermute | solution.py:208
  20.2 2.9 %expert.3 = (f32[128,1152]{1,0:T(8,128)S(1)}, bf16[64,1152]{1,0:T(8,128)(2,1)S(1)}, bf16[64,1152]{1,0:T(8,128)(2,1)S(1)}, bf16[16,1024]{1,0:T(8,128)(2,1)S(1)}, ...) custom-call(bf16[64,1152]{1,0:T(8,128)(2,1)S(1)} %get-tuple-element., ...), custom_call_target="tpu_custom_call", output_to_operand_aliasing={{3}: (4, {}), {4}: (5, {}), {5}: (6, {})} | custom-call | bytes 10000 | tf_op jit(solution)/shard_map/expert/pallas_call | solution.py:187
  23.7 1.3 %collective-permute-start.10 = (bf16[64,1152]{1,0:T(8,128)(2,1)S(1)}, bf16[64,1152]{1,0:T(8,128)(2,1)S(1)}, u32[]{:S(2)}, u32[]{:S(2)}) collective-permute-start(bf16[64,1152]{1,0:T(8,128)(2,1)S(1)} %collective-permute-done.refs_0_), channel_id=1, source_target_pairs={{0,2},{1,3},{2,0},{3,1},{4,6},{5,7},{6,4},{7,5},{8,10},{9,11},{10,... | collective-permute-start | bytes 442376 | tf_op jit(solution)/shard_map/ppermute | solution.py:208
  25.5 1.0 %collective-permute-start.19 = (bf16[64,1152]{1,0:T(8,128)(2,1)S(1)}, bf16[64,1152]{1,0:T(8,128)(2,1)S(1)}, u32[]{:S(2)}, u32[]{:S(2)}) collective-permute-start(bf16[64,1152]{1,0:T(8,128)(2,1)S(1)} %get-tuple-element.105), channel_id=1, source_target_pairs={{0,2},{1,3},{2,0},{3,1},{4,6},{5,7},{6,4},{7,5},{8,10},{9,11},{10,... | collective-permute-start | bytes 442376 | tf_op jit(solution)/shard_map/ppermute | solution.py:208
  26.5 3.9 %collective-permute-done.10.refs_3_ = bf16[64,1152]{1,0:T(8,128)(2,1)S(1)} collective-permute-done((bf16[64,1152]{1,0:T(8,128)(2,1)S(1)}, bf16[64,1152]{1,0:T(8,128)(2,1)S(1)}, u32[]{:S(2)}, u32[]{:S(2)}) %collective-permute-start.10) | collective-permute-done | bytes 147488 | tf_op jit(solution)/shard_map/ppermute | solution.py:208
  30.4 2.9 %expert.4 = (f32[128,1152]{1,0:T(8,128)S(1)}, bf16[64,1152]{1,0:T(8,128)(2,1)S(1)}, bf16[64,1152]{1,0:T(8,128)(2,1)S(1)}, bf16[16,1024]{1,0:T(8,128)(2,1)S(1)}, ...) custom-call(bf16[64,1152]{1,0:T(8,128)(2,1)S(1)} %collective-permute, ...), custom_call_target="tpu_custom_call", output_to_operand_aliasing={{3}: (4, {}), {4}: (5, {}), {5}: (6, {})} | custom-call | bytes 10000 | tf_op jit(solution)/shard_map/expert/pallas_call | solution.py:187
  35.0 1.3 %collective-permute-start.24 = (bf16[64,1152]{1,0:T(8,128)(2,1)S(1)}, bf16[64,1152]{1,0:T(8,128)(2,1)S(1)}, u32[]{:S(2)}, u32[]{:S(2)}) collective-permute-start(bf16[64,1152]{1,0:T(8,128)(2,1)S(1)} %get-tuple-element.119), channel_id=1, source_target_pairs={{0,2},{1,3},{2,0},{3,1},{4,6},{5,7},{6,4},{7,5},{8,10},{9,11},{10,... | collective-permute-start | bytes 442376 | tf_op jit(solution)/shard_map/ppermute | solution.py:208
  36.3 5.2 %expert.5 = (f32[128,1152]{1,0:T(8,128)S(1)}, f32[128,1152]{1,0:T(8,128)S(1)}, bf16[64,1152]{1,0:T(8,128)(2,1)S(1)}, bf16[64,1152]{1,0:T(8,128)(2,1)S(1)}, bf16[...) custom-call(bf16[64,1152]{1,0:T(8,128)(2,1)S(1)} %collective-permute, ...), custom_call_target="tpu_custom_call", output_to_operand_aliasing={{6}: (8, {}), {7}: (9, {}), {8}: (10, {})} | custom-call | bytes 10000 | tf_op jit(solution)/shard_map/expert/pallas_call | solution.py:187
  42.6 0.7 %collective-permute-start.25 = (bf16[64,1152]{1,0:T(8,128)(2,1)S(1)}, bf16[64,1152]{1,0:T(8,128)(2,1)S(1)}, u32[]{:S(2)}, u32[]{:S(2)}) collective-permute-start(bf16[64,1152]{1,0:T(8,128)(2,1)S(1)} %get-tuple-element.131), channel_id=1, source_target_pairs={{0,4},{1,5},{2,6},{3,7},{4,0},{5,1},{6,2},{7,3},{8,12},{9,13},{10,... | collective-permute-start | bytes 442376 | tf_op jit(solution)/shard_map/ppermute | solution.py:208
  43.4 1.1 %collective-permute-start.27 = (bf16[64,1152]{1,0:T(8,128)(2,1)S(1)}, bf16[64,1152]{1,0:T(8,128)(2,1)S(1)}, u32[]{:S(2)}, u32[]{:S(2)}) collective-permute-start(bf16[64,1152]{1,0:T(8,128)(2,1)S(1)} %get-tuple-element.137), channel_id=1, source_target_pairs={{0,2},{1,3},{2,0},{3,1},{4,6},{5,7},{6,4},{7,5},{8,10},{9,11},{10,... | collective-permute-start | bytes 442376 | tf_op jit(solution)/shard_map/ppermute | solution.py:208
  44.6 1.1 %collective-permute-start.29 = (bf16[64,1152]{1,0:T(8,128)(2,1)S(1)}, bf16[64,1152]{1,0:T(8,128)(2,1)S(1)}, u32[]{:S(2)}, u32[]{:S(2)}) collective-permute-start(bf16[64,1152]{1,0:T(8,128)(2,1)S(1)} %get-tuple-element.142), channel_id=1, source_target_pairs={{0,2},{1,3},{2,0},{3,1},{4,6},{5,7},{6,4},{7,5},{8,10},{9,11},{10,... | collective-permute-start | bytes 442376 | tf_op jit(solution)/shard_map/ppermute | solution.py:208
  45.6 2.9 %collective-permute-done.25.refs_2_ = bf16[64,1152]{1,0:T(8,128)(2,1)S(1)} collective-permute-done((bf16[64,1152]{1,0:T(8,128)(2,1)S(1)}, bf16[64,1152]{1,0:T(8,128)(2,1)S(1)}, u32[]{:S(2)}, u32[]{:S(2)}) %collective-permute-start.25) | collective-permute-done | bytes 147488 | tf_op jit(solution)/shard_map/ppermute | solution.py:208
  48.6 2.5 %collective-permute-start.26 = (bf16[64,1152]{1,0:T(8,128)(2,1)S(1)}, bf16[64,1152]{1,0:T(8,128)(2,1)S(1)}, u32[]{:S(2)}, u32[]{:S(2)}) collective-permute-start(bf16[64,1152]{1,0:T(8,128)(2,1)S(1)} %get-tuple-element.135), channel_id=1, source_target_pairs={{0,8},{1,9},{2,10},{3,11},{4,12},{5,13},{6,14},{7,15},{8,0},{9,1},... | collective-permute-start | bytes 442376 | tf_op jit(solution)/shard_map/ppermute | solution.py:208
  51.1 1.8 %collective-permute-start.28 = (bf16[64,1152]{1,0:T(8,128)(2,1)S(1)}, bf16[64,1152]{1,0:T(8,128)(2,1)S(1)}, u32[]{:S(2)}, u32[]{:S(2)}) collective-permute-start(bf16[64,1152]{1,0:T(8,128)(2,1)S(1)} %get-tuple-element.141), channel_id=1, source_target_pairs={{0,4},{1,5},{2,6},{3,7},{4,0},{5,1},{6,2},{7,3},{8,12},{9,13},{10,... | collective-permute-start | bytes 442376 | tf_op jit(solution)/shard_map/ppermute | solution.py:208
  52.9 4.9 %collective-permute-done.26.refs_1_ = bf16[64,1152]{1,0:T(8,128)(2,1)S(1)} collective-permute-done((bf16[64,1152]{1,0:T(8,128)(2,1)S(1)}, bf16[64,1152]{1,0:T(8,128)(2,1)S(1)}, u32[]{:S(2)}, u32[]{:S(2)}) %collective-permute-start.26) | collective-permute-done | bytes 147488 | tf_op jit(solution)/shard_map/ppermute | solution.py:208
  58.1 0.8 %finish.1 = bf16[64,1024]{1,0:T(8,128)(2,1)} custom-call(f32[64,1152]{1,0:T(8,128)S(1)} %get-tuple-element.129.refs_0_, bf16[64,1152]{1,0:T(8,128)(2,1)S(1)} %collective-permute-done.26.refs_1_, bf16[64,1152]{1,0:T(8,128)(2,1)S(1)} %collective-permute-done.28.refs_2_, bf16[64,1152]{1,0:T(8,128)(2,1)S(1)} %collective-permute-done.29.refs_3_), custom_call_target="tpu_custom_call" | custom-call | tf_op jit(solution)/shard_map/finish/pallas_call | solution.py:305
  (53 shorter events, 5.2 us)
Async XLA Ops:
  0.9 11.9 %collective-permute-start.1 = (bf16[64,1152]{1,0:T(8,128)(2,1)S(1)}, bf16[64,1152]{1,0:T(8,128)(2,1)S(1)}, u32[]{:S(2)}, u32[]{:S(2)}) collective-permute-start(bf16[64,1152]{1,0:T(8,128)(2,1)S(1)} %pack.1.refs_3_.refs_4_), channel_id=1, source_target_pairs={{0,8},{1,9},{2,10},{3,11},{4,12},{5,13},{6,14},{7,15},{8,0},{9,1},... | collective-permute-start | bytes 442376 | tf_op jit(solution)/shard_map/ppermute | solution.py:208
  5.0 9.3 %collective-permute-start.3 = (bf16[64,1152]{1,0:T(8,128)(2,1)S(1)}, bf16[64,1152]{1,0:T(8,128)(2,1)S(1)}, u32[]{:S(2)}, u32[]{:S(2)}) collective-permute-start(bf16[64,1152]{1,0:T(8,128)(2,1)S(1)} %pack.1.refs_3_.refs_4_), channel_id=1, source_target_pairs={{0,2},{1,3},{2,0},{3,1},{4,6},{5,7},{6,4},{7,5},{8,10},{9,11},{10,... | collective-permute-start | bytes 442376 | tf_op jit(solution)/shard_map/ppermute | solution.py:208
  6.6 7.7 %collective-permute-start = (bf16[64,1152]{1,0:T(8,128)(2,1)S(1)}, bf16[64,1152]{1,0:T(8,128)(2,1)S(1)}, u32[]{:S(2)}, u32[]{:S(2)}) collective-permute-start(bf16[64,1152]{1,0:T(8,128)(2,1)S(1)} %pack.1.refs_3_.refs_4_), channel_id=1, source_target_pairs={{0,4},{1,5},{2,6},{3,7},{4,0},{5,1},{6,2},{7,3},{8,12},{9,13},{10,... | collective-permute-start | bytes 442376 | tf_op jit(solution)/shard_map/ppermute | solution.py:208
  12.9 5.2 %collective-permute-start.4 = (bf16[64,1152]{1,0:T(8,128)(2,1)S(1)}, bf16[64,1152]{1,0:T(8,128)(2,1)S(1)}, u32[]{:S(2)}, u32[]{:S(2)}) collective-permute-start(bf16[64,1152]{1,0:T(8,128)(2,1)S(1)} %get-tuple-element.77.refs_0_), channel_id=1, source_target_pairs={{0,2},{1,3},{2,0},{3,1},{4,6},{5,7},{6,4},{7,5},{8,10},{9,11},{10,... | collective-permute-start | bytes 442376 | tf_op jit(solution)/shard_map/ppermute | solution.py:208
  13.7 5.1 %collective-permute-start.2 = (bf16[64,1152]{1,0:T(8,128)(2,1)S(1)}, bf16[64,1152]{1,0:T(8,128)(2,1)S(1)}, u32[]{:S(2)}, u32[]{:S(2)}) collective-permute-start(bf16[64,1152]{1,0:T(8,128)(2,1)S(1)} %get-tuple-element.77.refs_0_), channel_id=1, source_target_pairs={{0,4},{1,5},{2,6},{3,7},{4,0},{5,1},{6,2},{7,3},{8,12},{9,13},{10,... | collective-permute-start | bytes 442376 | tf_op jit(solution)/shard_map/ppermute | solution.py:208
  14.3 5.8 %collective-permute-start.5 = (bf16[64,1152]{1,0:T(8,128)(2,1)S(1)}, bf16[64,1152]{1,0:T(8,128)(2,1)S(1)}, u32[]{:S(2)}, u32[]{:S(2)}) collective-permute-start(bf16[64,1152]{1,0:T(8,128)(2,1)S(1)} %get-tuple-element.77.refs_0_), channel_id=1, source_target_pairs={{0,1},{1,0},{2,3},{3,2},{4,5},{5,4},{6,7},{7,6},{8,9},{9,8},{10,11... | collective-permute-start | bytes 442376 | tf_op jit(solution)/shard_map/ppermute | solution.py:208
  18.9 6.3 %collective-permute-start.9 = (bf16[64,1152]{1,0:T(8,128)(2,1)S(1)}, bf16[64,1152]{1,0:T(8,128)(2,1)S(1)}, u32[]{:S(2)}, u32[]{:S(2)}) collective-permute-start(bf16[64,1152]{1,0:T(8,128)(2,1)S(1)} %collective-permute-done.2.refs_1_.refs_0_), channel_id=1, source_target_pairs={{0,2},{1,3},{2,0},{3,1},{4,6},{5,7},{6,4},{7,5},{8,10},{9,11},{10,... | collective-permute-start | bytes 442376 | tf_op jit(solution)/shard_map/ppermute | solution.py:208
  23.1 2.3 %collective-permute-start.7 = (bf16[64,1152]{1,0:T(8,128)(2,1)S(1)}, bf16[64,1152]{1,0:T(8,128)(2,1)S(1)}, u32[]{:S(2)}, u32[]{:S(2)}) collective-permute-start(bf16[64,1152]{1,0:T(8,128)(2,1)S(1)} %get-tuple-element.86), channel_id=1, source_target_pairs={{0,1},{1,0},{2,3},{3,2},{4,5},{5,4},{6,7},{7,6},{8,9},{9,8},{10,11... | collective-permute-start | bytes 442376 | tf_op jit(solution)/shard_map/ppermute | solution.py:208
  23.3 2.1 %collective-permute-start.8 = (bf16[64,1152]{1,0:T(8,128)(2,1)S(1)}, bf16[64,1152]{1,0:T(8,128)(2,1)S(1)}, u32[]{:S(2)}, u32[]{:S(2)}) collective-permute-start(bf16[64,1152]{1,0:T(8,128)(2,1)S(1)} %get-tuple-element.87), channel_id=1, source_target_pairs={{0,1},{1,0},{2,3},{3,2},{4,5},{5,4},{6,7},{7,6},{8,9},{9,8},{10,11... | collective-permute-start | bytes 442376 | tf_op jit(solution)/shard_map/ppermute | solution.py:208
  23.7 6.7 %collective-permute-start.10 = (bf16[64,1152]{1,0:T(8,128)(2,1)S(1)}, bf16[64,1152]{1,0:T(8,128)(2,1)S(1)}, u32[]{:S(2)}, u32[]{:S(2)}) collective-permute-start(bf16[64,1152]{1,0:T(8,128)(2,1)S(1)} %collective-permute-done.refs_0_), channel_id=1, source_target_pairs={{0,2},{1,3},{2,0},{3,1},{4,6},{5,7},{6,4},{7,5},{8,10},{9,11},{10,... | collective-permute-start | bytes 442376 | tf_op jit(solution)/shard_map/ppermute | solution.py:208
  24.9 5.4 %collective-permute-start.15 = (bf16[64,1152]{1,0:T(8,128)(2,1)S(1)}, bf16[64,1152]{1,0:T(8,128)(2,1)S(1)}, u32[]{:S(2)}, u32[]{:S(2)}) collective-permute-start(bf16[64,1152]{1,0:T(8,128)(2,1)S(1)} %collective-permute-done.2.refs_1_.refs_0_), channel_id=1, source_target_pairs={{0,1},{1,0},{2,3},{3,2},{4,5},{5,4},{6,7},{7,6},{8,9},{9,8},{10,11... | collective-permute-start | bytes 442376 | tf_op jit(solution)/shard_map/ppermute | solution.py:208
  25.1 5.3 %collective-permute-start.16 = (bf16[64,1152]{1,0:T(8,128)(2,1)S(1)}, bf16[64,1152]{1,0:T(8,128)(2,1)S(1)}, u32[]{:S(2)}, u32[]{:S(2)}) collective-permute-start(bf16[64,1152]{1,0:T(8,128)(2,1)S(1)} %get-tuple-element.98.refs_1_), channel_id=1, source_target_pairs={{0,1},{1,0},{2,3},{3,2},{4,5},{5,4},{6,7},{7,6},{8,9},{9,8},{10,11... | collective-permute-start | bytes 442376 | tf_op jit(solution)/shard_map/ppermute | solution.py:208
  25.5 8.8 %collective-permute-start.19 = (bf16[64,1152]{1,0:T(8,128)(2,1)S(1)}, bf16[64,1152]{1,0:T(8,128)(2,1)S(1)}, u32[]{:S(2)}, u32[]{:S(2)}) collective-permute-start(bf16[64,1152]{1,0:T(8,128)(2,1)S(1)} %get-tuple-element.105), channel_id=1, source_target_pairs={{0,2},{1,3},{2,0},{3,1},{4,6},{5,7},{6,4},{7,5},{8,10},{9,11},{10,... | collective-permute-start | bytes 442376 | tf_op jit(solution)/shard_map/ppermute | solution.py:208
  33.8 2.4 %collective-permute-start.13 = (bf16[64,1152]{1,0:T(8,128)(2,1)S(1)}, bf16[64,1152]{1,0:T(8,128)(2,1)S(1)}, u32[]{:S(2)}, u32[]{:S(2)}) collective-permute-start(bf16[64,1152]{1,0:T(8,128)(2,1)S(1)} %pack.1.refs_3_.refs_4_), channel_id=1, source_target_pairs={{0,1},{1,0},{2,3},{3,2},{4,5},{5,4},{6,7},{7,6},{8,9},{9,8},{10,11... | collective-permute-start | bytes 442376 | tf_op jit(solution)/shard_map/ppermute | solution.py:208
  33.9 2.4 %collective-permute-start.14 = (bf16[64,1152]{1,0:T(8,128)(2,1)S(1)}, bf16[64,1152]{1,0:T(8,128)(2,1)S(1)}, u32[]{:S(2)}, u32[]{:S(2)}) collective-permute-start(bf16[64,1152]{1,0:T(8,128)(2,1)S(1)} %collective-permute-done.3.refs_2_.refs_5_), channel_id=1, source_target_pairs={{0,1},{1,0},{2,3},{3,2},{4,5},{5,4},{6,7},{7,6},{8,9},{9,8},{10,11... | collective-permute-start | bytes 442376 | tf_op jit(solution)/shard_map/ppermute | solution.py:208
  34.4 1.9 %collective-permute-start.11 = (bf16[64,1152]{1,0:T(8,128)(2,1)S(1)}, bf16[64,1152]{1,0:T(8,128)(2,1)S(1)}, u32[]{:S(2)}, u32[]{:S(2)}) collective-permute-start(bf16[64,1152]{1,0:T(8,128)(2,1)S(1)} %collective-permute-done.refs_0_), channel_id=1, source_target_pairs={{0,1},{1,0},{2,3},{3,2},{4,5},{5,4},{6,7},{7,6},{8,9},{9,8},{10,11... | collective-permute-start | bytes 442376 | tf_op jit(solution)/shard_map/ppermute | solution.py:208
  35.0 7.6 %collective-permute-start.24 = (bf16[64,1152]{1,0:T(8,128)(2,1)S(1)}, bf16[64,1152]{1,0:T(8,128)(2,1)S(1)}, u32[]{:S(2)}, u32[]{:S(2)}) collective-permute-start(bf16[64,1152]{1,0:T(8,128)(2,1)S(1)} %get-tuple-element.119), channel_id=1, source_target_pairs={{0,2},{1,3},{2,0},{3,1},{4,6},{5,7},{6,4},{7,5},{8,10},{9,11},{10,... | collective-permute-start | bytes 442376 | tf_op jit(solution)/shard_map/ppermute | solution.py:208
  42.1 2.4 %collective-permute-start.20 = (bf16[64,1152]{1,0:T(8,128)(2,1)S(1)}, bf16[64,1152]{1,0:T(8,128)(2,1)S(1)}, u32[]{:S(2)}, u32[]{:S(2)}) collective-permute-start(bf16[64,1152]{1,0:T(8,128)(2,1)S(1)} %get-tuple-element.113), channel_id=1, source_target_pairs={{0,1},{1,0},{2,3},{3,2},{4,5},{5,4},{6,7},{7,6},{8,9},{9,8},{10,11... | collective-permute-start | bytes 442376 | tf_op jit(solution)/shard_map/ppermute | solution.py:208
  42.1 2.4 %collective-permute-start.21 = (bf16[64,1152]{1,0:T(8,128)(2,1)S(1)}, bf16[64,1152]{1,0:T(8,128)(2,1)S(1)}, u32[]{:S(2)}, u32[]{:S(2)}) collective-permute-start(bf16[64,1152]{1,0:T(8,128)(2,1)S(1)} %get-tuple-element.114), channel_id=1, source_target_pairs={{0,1},{1,0},{2,3},{3,2},{4,5},{5,4},{6,7},{7,6},{8,9},{9,8},{10,11... | collective-permute-start | bytes 442376 | tf_op jit(solution)/shard_map/ppermute | solution.py:208
  42.6 5.9 %collective-permute-start.25 = (bf16[64,1152]{1,0:T(8,128)(2,1)S(1)}, bf16[64,1152]{1,0:T(8,128)(2,1)S(1)}, u32[]{:S(2)}, u32[]{:S(2)}) collective-permute-start(bf16[64,1152]{1,0:T(8,128)(2,1)S(1)} %get-tuple-element.131), channel_id=1, source_target_pairs={{0,4},{1,5},{2,6},{3,7},{4,0},{5,1},{6,2},{7,3},{8,12},{9,13},{10,... | collective-permute-start | bytes 442376 | tf_op jit(solution)/shard_map/ppermute | solution.py:208
  43.4 7.6 %collective-permute-start.27 = (bf16[64,1152]{1,0:T(8,128)(2,1)S(1)}, bf16[64,1152]{1,0:T(8,128)(2,1)S(1)}, u32[]{:S(2)}, u32[]{:S(2)}) collective-permute-start(bf16[64,1152]{1,0:T(8,128)(2,1)S(1)} %get-tuple-element.137), channel_id=1, source_target_pairs={{0,2},{1,3},{2,0},{3,1},{4,6},{5,7},{6,4},{7,5},{8,10},{9,11},{10,... | collective-permute-start | bytes 442376 | tf_op jit(solution)/shard_map/ppermute | solution.py:208
  44.6 8.3 %collective-permute-start.29 = (bf16[64,1152]{1,0:T(8,128)(2,1)S(1)}, bf16[64,1152]{1,0:T(8,128)(2,1)S(1)}, u32[]{:S(2)}, u32[]{:S(2)}) collective-permute-start(bf16[64,1152]{1,0:T(8,128)(2,1)S(1)} %get-tuple-element.142), channel_id=1, source_target_pairs={{0,2},{1,3},{2,0},{3,1},{4,6},{5,7},{6,4},{7,5},{8,10},{9,11},{10,... | collective-permute-start | bytes 442376 | tf_op jit(solution)/shard_map/ppermute | solution.py:208
  48.6 9.2 %collective-permute-start.26 = (bf16[64,1152]{1,0:T(8,128)(2,1)S(1)}, bf16[64,1152]{1,0:T(8,128)(2,1)S(1)}, u32[]{:S(2)}, u32[]{:S(2)}) collective-permute-start(bf16[64,1152]{1,0:T(8,128)(2,1)S(1)} %get-tuple-element.135), channel_id=1, source_target_pairs={{0,8},{1,9},{2,10},{3,11},{4,12},{5,13},{6,14},{7,15},{8,0},{9,1},... | collective-permute-start | bytes 442376 | tf_op jit(solution)/shard_map/ppermute | solution.py:208
  51.1 7.1 %collective-permute-start.28 = (bf16[64,1152]{1,0:T(8,128)(2,1)S(1)}, bf16[64,1152]{1,0:T(8,128)(2,1)S(1)}, u32[]{:S(2)}, u32[]{:S(2)}) collective-permute-start(bf16[64,1152]{1,0:T(8,128)(2,1)S(1)} %get-tuple-element.141), channel_id=1, source_target_pairs={{0,4},{1,5},{2,6},{3,7},{4,0},{5,1},{6,2},{7,3},{8,12},{9,13},{10,... | collective-permute-start | bytes 442376 | tf_op jit(solution)/shard_map/ppermute | solution.py:208
  (6 other events, 9.6 us)

commit v14 on v13

--- a/solution.py
+++ b/solution.py
@@ -41,9 +41,12 @@
                 copies.append(pltpu.make_async_copy(src.at[at], dst.at[at], sems.at[1 + len(copies)]))
     for copy in copies:
         copy.start()
-    columns_ref[...] = jnp.zeros_like(columns_ref)
     get_router.wait()
-    columns_ref[: router_ref.shape[0], :] = router_ref[...]
+    local, lat = router_ref.shape
+    wide = jnp.concatenate(
+        [router_ref[...].astype(jnp.float32), jnp.zeros((TAIL - local, lat), jnp.float32)], axis=0
+    )
+    columns_ref[...] = wide.T.astype(jnp.bfloat16)
     for copy in copies:
         copy.wait()
 
@@ -64,38 +67,49 @@
             ref[:, lanes] = value[half + j * rows : half + (j + 1) * rows].astype(jnp.bfloat16)
 
     def logits_of(values):
-        return lax.dot_general(
-            values, columns_ref[...], (((1,), (1,)), ((), ())), preferred_element_type=jnp.float32
-        )
-
-    lane = lax.broadcasted_iota(jnp.int32, (2 * half, TAIL), 1)
-    row = lax.broadcasted_iota(jnp.int32, (2 * half, 2 * half), 0)
-    col = lax.broadcasted_iota(jnp.int32, (2 * half, 2 * half), 1)
+        return jnp.dot(values, columns_ref[...], preferred_element_type=jnp.float32)
+
+    size = 2 * half
+    row = lax.broadcasted_iota(jnp.int32, (size, size), 0)
+    col = lax.broadcasted_iota(jnp.int32, (size, size), 1)
     before = jnp.where(col < row, 1.0, 0.0).astype(jnp.bfloat16)
-    slot = lax.broadcasted_iota(jnp.int32, (2 * half, slots), 1).astype(jnp.float32)
+    after = jnp.where(row < col, 1.0, 0.0).astype(jnp.bfloat16)
+    lane = lax.broadcasted_iota(jnp.int32, (size, TAIL), 1)
+    line = lax.broadcasted_iota(jnp.int32, (16, size), 0)
+    slot = lax.broadcasted_iota(jnp.int32, (size, slots), 1).astype(jnp.float32)
+    slot_t = lax.broadcasted_iota(jnp.int32, (slots, size), 0).astype(jnp.float32)
+    labels = [(lax.axis_index("exp") * local + e).astype(jnp.float32) for e in range(local)]
     spreads = []
     for i in range(count):
         batch = blocks[4 * i : 4 * i + 4]
         x = jnp.concatenate([ref[:, :lat] for ref in batch], axis=0)
         tail = jnp.concatenate([ref[:, lat:] for ref in batch], axis=0).astype(jnp.float32)
-        logits = logits_of(x)
-        masks, sums = [], jnp.zeros((2 * half, 1), jnp.float32)
-        marks = jnp.zeros((2 * half, TAIL), jnp.float32)
+        masks = [jnp.max(jnp.where(tail == label, 1.0, 0.0), axis=1, keepdims=True) for label in labels]
+        tail_t = tail.T[:16]
+        masks_t = [jnp.max(jnp.where(tail_t == label, 1.0, 0.0), axis=0, keepdims=True) for label in labels]
+        marks, marks_t = jnp.zeros((size, TAIL), jnp.float32), jnp.zeros((16, size), jnp.float32)
         for e in range(local):
-            label = (lax.axis_index("exp") * local + e).astype(jnp.float32)
-            mask = jnp.max(jnp.where(tail == label, 1.0, 0.0), axis=1, keepdims=True)
-            sums = sums + jax.nn.sigmoid(logits[:, e : e + 1]) * (mask * SCALE)
-            marks = jnp.where(lane == e, mask, marks)
-            masks.append(mask)
-        put(i, slice(lat, wide), jnp.where(lane == 0, sums, 0.0))
+            marks = jnp.where(lane == e, masks[e], marks)
+            marks_t = jnp.where(line == e, masks_t[e], marks_t)
+        place_t = jnp.dot(marks_t.astype(jnp.bfloat16), after, preferred_element_type=jnp.float32)
         place = jnp.dot(before, marks.astype(jnp.bfloat16), preferred_element_type=jnp.float32)
+        gather = jnp.concatenate(
+            [
+                jnp.where((slot_t == place_t[e : e + 1]) & (masks_t[e] > 0.0), 1.0, 0.0)
+                for e in range(local)
+            ],
+            axis=0,
+        ).astype(jnp.bfloat16)
+        packed = jnp.dot(gather, x, preferred_element_type=jnp.float32).astype(jnp.bfloat16)
         spread = jnp.concatenate(
             [jnp.where((slot == place[:, e : e + 1]) & (masks[e] > 0.0), 1.0, 0.0) for e in range(local)],
             axis=1,
         ).astype(jnp.bfloat16)
-        packed = lax.dot_general(
-            spread, x, (((0,), (0,)), ((), ())), preferred_element_type=jnp.float32
-        ).astype(jnp.bfloat16)
+        logits = logits_of(x)
+        sums = jnp.zeros((size, 1), jnp.float32)
+        for e in range(local):
+            sums = sums + jax.nn.sigmoid(logits[:, e : e + 1]) * (masks[e] * SCALE)
+        put(i, slice(lat, wide), jnp.where(lane == 0, sums, 0.0))
         for e in range(local):
             packed_ref[e, i * slots : (i + 1) * slots, :] = packed[e * slots : (e + 1) * slots]
         spreads.append(spread)
@@ -214,7 +228,7 @@
         return call(
             load_kernel,
             [
-                pltpu.VMEM((16, lat), jnp.bfloat16),
+                pltpu.VMEM((lat, TAIL), jnp.bfloat16),
                 pltpu.VMEM(gate_up.shape, gate_up.dtype),
                 pltpu.VMEM(expert_down.shape, expert_down.dtype),
             ],
@@ -283,8 +297,8 @@
         compute(2)
         gather(3)
         reduce_core(2)
+        compute(3)
         gather(1)
-        compute(3)
         reduce_core(3, [y_came[2]])
         compute(1, 0)
         z_3 = swap(reduce_y(3), 4)

time: 59.1 us -> 59.1 us (level)
  waiting for transfers between devices: 17.2 us -> 18.4 us
  starting transfers between devices: 23.9 us -> 23.3 us
    ppermute x30, waiting for transfers between devices: 17.2 us -> 18.4 us  [swap(): return lax.ppermute(x, 'exp', [(i, i ^ bits) for i in range(n_dev)])]
  transfers between devices with their start and end apart: 30 -> 30, of which waited for: 9 -> 9; matrix products, arithmetic and copies ran while one was open for 0% -> 0% of each run, Pallas kernels for 27% -> 26%
where the time goes in v14:
time: 59.1 us; the launch traced here: 58.9 us
  starting transfers between devices  23.3 us (39%)
  waiting for transfers between devices  18.4 us (31%)
  Pallas kernels  17.1 us (29%)
    ppermute x30, starting transfers between devices, swap(): return lax.ppermute(x, 'exp', [(i, i ^ bits) for i in range(n_dev)])  23.3 us
    ppermute x30, waiting for transfers between devices, swap(): return lax.ppermute(x, 'exp', [(i, i ^ bits) for i in range(n_dev)])  18.4 us
    pallas_call x16, Pallas kernels, call(): pl.pallas_call(body_with_chain if reads_chain else body, out_shape=list(o...  16.3 us
  transfers between devices with their start and end apart: 30, of which 9 were waited for; matrix products, arithmetic and copies ran while one was open for 0% of the time, Pallas kernels for 26%

profile of v14, /device:TPU:0, one launch (start us, length us, event | category | flops | bytes accessed | tf_op | source)
XLA Modules:
  0.0 58.9 jit_solution(5476395051082158998)
XLA Ops:
  0.0 0.9 %pack.1.refs_3_.refs_4_ = bf16[64,1152]{1,0:T(8,128)(2,1)S(1)} custom-call(s32[8,64]{1,0:T(8,128)} %bitcast.2, bf16[64,1024]{1,0:T(8,128)(2,1)} %refs_1_.2), custom_call_target="tpu_custom_call" | custom-call | bytes 10000 | tf_op jit(solution)/shard_map/pack/pallas_call | solution.py:201
  0.9 4.1 %collective-permute-start.1 = (bf16[64,1152]{1,0:T(8,128)(2,1)S(1)}, bf16[64,1152]{1,0:T(8,128)(2,1)S(1)}, u32[]{:S(2)}, u32[]{:S(2)}) collective-permute-start(bf16[64,1152]{1,0:T(8,128)(2,1)S(1)} %pack.1.refs_3_.refs_4_), channel_id=1, source_target_pairs={{0,8},{1,9},{2,10},{3,11},{4,12},{5,13},{6,14},{7,15},{8,0},{9,1},... | collective-permute-start | bytes 442376 | tf_op jit(solution)/shard_map/ppermute | solution.py:222
  5.0 1.5 %collective-permute-start.3 = (bf16[64,1152]{1,0:T(8,128)(2,1)S(1)}, bf16[64,1152]{1,0:T(8,128)(2,1)S(1)}, u32[]{:S(2)}, u32[]{:S(2)}) collective-permute-start(bf16[64,1152]{1,0:T(8,128)(2,1)S(1)} %pack.1.refs_3_.refs_4_), channel_id=1, source_target_pairs={{0,2},{1,3},{2,0},{3,1},{4,6},{5,7},{6,4},{7,5},{8,10},{9,11},{10,... | collective-permute-start | bytes 442376 | tf_op jit(solution)/shard_map/ppermute | solution.py:222
  6.6 1.6 %collective-permute-start = (bf16[64,1152]{1,0:T(8,128)(2,1)S(1)}, bf16[64,1152]{1,0:T(8,128)(2,1)S(1)}, u32[]{:S(2)}, u32[]{:S(2)}) collective-permute-start(bf16[64,1152]{1,0:T(8,128)(2,1)S(1)} %pack.1.refs_3_.refs_4_), channel_id=1, source_target_pairs={{0,4},{1,5},{2,6},{3,7},{4,0},{5,1},{6,2},{7,3},{8,12},{9,13},{10,... | collective-permute-start | bytes 442376 | tf_op jit(solution)/shard_map/ppermute | solution.py:222
  8.1 4.7 %load.1 = (bf16[1024,128]{1,0:T(8,128)(2,1)S(1)}, bf16[2,1024,2048]{2,1,0:T(8,128)(2,1)S(1)}, bf16[2,1024,1024]{2,1,0:T(8,128)(2,1)S(1)}) custom-call(bf16[2,1024]{1,0:T(2,128)(2,1)} %bitcast.3, bf16[2,1024,2048]{2,1,0:T(8,128)(2,1)} %refs_1_.3, bf16[2,1024,1024]{2,1,0:T(8,128)(2,1)} %refs_2_.1, bf16[64,1152]{1,0:T(8,128)(2,1)S(1)} %pack.1.refs_3_.refs_4_), custom_call_target="tpu_custom_call" | custom-call | bytes 10000 | tf_op jit(solution)/shard_map/load/pallas_call | solution.py:201
  12.9 0.8 %collective-permute-start.4 = (bf16[64,1152]{1,0:T(8,128)(2,1)S(1)}, bf16[64,1152]{1,0:T(8,128)(2,1)S(1)}, u32[]{:S(2)}, u32[]{:S(2)}) collective-permute-start(bf16[64,1152]{1,0:T(8,128)(2,1)S(1)} %get-tuple-element.77.refs_0_), channel_id=1, source_target_pairs={{0,2},{1,3},{2,0},{3,1},{4,6},{5,7},{6,4},{7,5},{8,10},{9,11},{10,... | collective-permute-start | bytes 442376 | tf_op jit(solution)/shard_map/ppermute | solution.py:222
  14.3 3.8 %collective-permute-done.4.refs_6_ = bf16[64,1152]{1,0:T(8,128)(2,1)S(1)} collective-permute-done((bf16[64,1152]{1,0:T(8,128)(2,1)S(1)}, bf16[64,1152]{1,0:T(8,128)(2,1)S(1)}, u32[]{:S(2)}, u32[]{:S(2)}) %collective-permute-start.4) | collective-permute-done | bytes 147488 | tf_op jit(solution)/shard_map/ppermute | solution.py:222
  18.1 0.8 %collective-permute-done.2.refs_1_.refs_0_ = bf16[64,1152]{1,0:T(8,128)(2,1)S(1)} collective-permute-done((bf16[64,1152]{1,0:T(8,128)(2,1)S(1)}, bf16[64,1152]{1,0:T(8,128)(2,1)S(1)}, u32[]{:S(2)}, u32[]{:S(2)}) %collective-permute-start.2) | collective-permute-done | bytes 147488 | tf_op jit(solution)/shard_map/ppermute | solution.py:222
  18.9 1.3 %collective-permute-start.7 = (bf16[64,1152]{1,0:T(8,128)(2,1)S(1)}, bf16[64,1152]{1,0:T(8,128)(2,1)S(1)}, u32[]{:S(2)}, u32[]{:S(2)}) collective-permute-start(bf16[64,1152]{1,0:T(8,128)(2,1)S(1)} %collective-permute-done.2.refs_1_.refs_0_), channel_id=1, source_target_pairs={{0,2},{1,3},{2,0},{3,1},{4,6},{5,7},{6,4},{7,5},{8,10},{9,11},{10,... | collective-permute-start | bytes 442376 | tf_op jit(solution)/shard_map/ppermute | solution.py:222
  20.2 2.7 %expert.3 = (f32[128,1152]{1,0:T(8,128)S(1)}, bf16[64,1152]{1,0:T(8,128)(2,1)S(1)}, bf16[64,1152]{1,0:T(8,128)(2,1)S(1)}, bf16[1024,128]{1,0:T(8,128)(2,1)S(1)},...) custom-call(bf16[64,1152]{1,0:T(8,128)(2,1)S(1)} %get-tuple-element., ...), custom_call_target="tpu_custom_call", output_to_operand_aliasing={{3}: (4, {}), {4}: (5, {}), {5}: (6, {})} | custom-call | bytes 10000 | tf_op jit(solution)/shard_map/expert/pallas_call | solution.py:201
  23.7 1.5 %collective-permute-done.7.refs_3_ = bf16[64,1152]{1,0:T(8,128)(2,1)S(1)} collective-permute-done((bf16[64,1152]{1,0:T(8,128)(2,1)S(1)}, bf16[64,1152]{1,0:T(8,128)(2,1)S(1)}, u32[]{:S(2)}, u32[]{:S(2)}) %collective-permute-start.7) | collective-permute-done | bytes 147488 | tf_op jit(solution)/shard_map/ppermute | solution.py:222
  25.1 1.3 %collective-permute-start.12 = (bf16[64,1152]{1,0:T(8,128)(2,1)S(1)}, bf16[64,1152]{1,0:T(8,128)(2,1)S(1)}, u32[]{:S(2)}, u32[]{:S(2)}) collective-permute-start(bf16[64,1152]{1,0:T(8,128)(2,1)S(1)} %collective-permute-done.refs_0_), channel_id=1, source_target_pairs={{0,2},{1,3},{2,0},{3,1},{4,6},{5,7},{6,4},{7,5},{8,10},{9,11},{10,... | collective-permute-start | bytes 442376 | tf_op jit(solution)/shard_map/ppermute | solution.py:222
  26.5 0.8 %collective-permute-start.19 = (bf16[64,1152]{1,0:T(8,128)(2,1)S(1)}, bf16[64,1152]{1,0:T(8,128)(2,1)S(1)}, u32[]{:S(2)}, u32[]{:S(2)}) collective-permute-start(bf16[64,1152]{1,0:T(8,128)(2,1)S(1)} %get-tuple-element.105), channel_id=1, source_target_pairs={{0,2},{1,3},{2,0},{3,1},{4,6},{5,7},{6,4},{7,5},{8,10},{9,11},{10,... | collective-permute-start | bytes 442376 | tf_op jit(solution)/shard_map/ppermute | solution.py:222
  27.3 2.7 %expert.4 = (f32[128,1152]{1,0:T(8,128)S(1)}, bf16[64,1152]{1,0:T(8,128)(2,1)S(1)}, bf16[64,1152]{1,0:T(8,128)(2,1)S(1)}, bf16[1024,128]{1,0:T(8,128)(2,1)S(1)},...) custom-call(bf16[64,1152]{1,0:T(8,128)(2,1)S(1)} %collective-permute, ...), custom_call_target="tpu_custom_call", output_to_operand_aliasing={{3}: (4, {}), {4}: (5, {}), {5}: (6, {})} | custom-call | bytes 10000 | tf_op jit(solution)/shard_map/expert/pallas_call | solution.py:201
  30.7 1.1 %collective-permute-done.12.refs_3_ = bf16[64,1152]{1,0:T(8,128)(2,1)S(1)} collective-permute-done((bf16[64,1152]{1,0:T(8,128)(2,1)S(1)}, bf16[64,1152]{1,0:T(8,128)(2,1)S(1)}, u32[]{:S(2)}, u32[]{:S(2)}) %collective-permute-start.12) | collective-permute-done | bytes 147488 | tf_op jit(solution)/shard_map/ppermute | solution.py:222
  31.8 2.8 %collective-permute-done.19.refs_3_.refs_1_ = bf16[64,1152]{1,0:T(8,128)(2,1)S(1)} collective-permute-done((bf16[64,1152]{1,0:T(8,128)(2,1)S(1)}, bf16[64,1152]{1,0:T(8,128)(2,1)S(1)}, u32[]{:S(2)}, u32[]{:S(2)}) %collective-permute-start.19) | collective-permute-done | bytes 147488 | tf_op jit(solution)/shard_map/ppermute | solution.py:222
  35.1 1.3 %collective-permute-start.24 = (bf16[64,1152]{1,0:T(8,128)(2,1)S(1)}, bf16[64,1152]{1,0:T(8,128)(2,1)S(1)}, u32[]{:S(2)}, u32[]{:S(2)}) collective-permute-start(bf16[64,1152]{1,0:T(8,128)(2,1)S(1)} %get-tuple-element.119), channel_id=1, source_target_pairs={{0,2},{1,3},{2,0},{3,1},{4,6},{5,7},{6,4},{7,5},{8,10},{9,11},{10,... | collective-permute-start | bytes 442376 | tf_op jit(solution)/shard_map/ppermute | solution.py:222
  36.5 4.9 %expert.5 = (f32[128,1152]{1,0:T(8,128)S(1)}, f32[128,1152]{1,0:T(8,128)S(1)}, bf16[64,1152]{1,0:T(8,128)(2,1)S(1)}, bf16[64,1152]{1,0:T(8,128)(2,1)S(1)}, bf16[...) custom-call(bf16[64,1152]{1,0:T(8,128)(2,1)S(1)} %collective-permute, ...), custom_call_target="tpu_custom_call", output_to_operand_aliasing={{6}: (8, {}), {7}: (9, {}), {8}: (10, {})} | custom-call | bytes 10000 | tf_op jit(solution)/shard_map/expert/pallas_call | solution.py:201
  43.3 1.2 %collective-permute-start.27 = (bf16[64,1152]{1,0:T(8,128)(2,1)S(1)}, bf16[64,1152]{1,0:T(8,128)(2,1)S(1)}, u32[]{:S(2)}, u32[]{:S(2)}) collective-permute-start(bf16[64,1152]{1,0:T(8,128)(2,1)S(1)} %get-tuple-element.137), channel_id=1, source_target_pairs={{0,2},{1,3},{2,0},{3,1},{4,6},{5,7},{6,4},{7,5},{8,10},{9,11},{10,... | collective-permute-start | bytes 442376 | tf_op jit(solution)/shard_map/ppermute | solution.py:222
  44.5 1.0 %collective-permute-start.29 = (bf16[64,1152]{1,0:T(8,128)(2,1)S(1)}, bf16[64,1152]{1,0:T(8,128)(2,1)S(1)}, u32[]{:S(2)}, u32[]{:S(2)}) collective-permute-start(bf16[64,1152]{1,0:T(8,128)(2,1)S(1)} %get-tuple-element.142), channel_id=1, source_target_pairs={{0,2},{1,3},{2,0},{3,1},{4,6},{5,7},{6,4},{7,5},{8,10},{9,11},{10,... | collective-permute-start | bytes 442376 | tf_op jit(solution)/shard_map/ppermute | solution.py:222
  45.5 3.0 %collective-permute-done.25.refs_2_ = bf16[64,1152]{1,0:T(8,128)(2,1)S(1)} collective-permute-done((bf16[64,1152]{1,0:T(8,128)(2,1)S(1)}, bf16[64,1152]{1,0:T(8,128)(2,1)S(1)}, u32[]{:S(2)}, u32[]{:S(2)}) %collective-permute-start.25) | collective-permute-done | bytes 147488 | tf_op jit(solution)/shard_map/ppermute | solution.py:222
  48.5 2.5 %collective-permute-start.26 = (bf16[64,1152]{1,0:T(8,128)(2,1)S(1)}, bf16[64,1152]{1,0:T(8,128)(2,1)S(1)}, u32[]{:S(2)}, u32[]{:S(2)}) collective-permute-start(bf16[64,1152]{1,0:T(8,128)(2,1)S(1)} %get-tuple-element.135), channel_id=1, source_target_pairs={{0,8},{1,9},{2,10},{3,11},{4,12},{5,13},{6,14},{7,15},{8,0},{9,1},... | collective-permute-start | bytes 442376 | tf_op jit(solution)/shard_map/ppermute | solution.py:222
  51.0 1.8 %collective-permute-start.28 = (bf16[64,1152]{1,0:T(8,128)(2,1)S(1)}, bf16[64,1152]{1,0:T(8,128)(2,1)S(1)}, u32[]{:S(2)}, u32[]{:S(2)}) collective-permute-start(bf16[64,1152]{1,0:T(8,128)(2,1)S(1)} %get-tuple-element.141), channel_id=1, source_target_pairs={{0,4},{1,5},{2,6},{3,7},{4,0},{5,1},{6,2},{7,3},{8,12},{9,13},{10,... | collective-permute-start | bytes 442376 | tf_op jit(solution)/shard_map/ppermute | solution.py:222
  52.9 4.9 %collective-permute-done.26.refs_1_ = bf16[64,1152]{1,0:T(8,128)(2,1)S(1)} collective-permute-done((bf16[64,1152]{1,0:T(8,128)(2,1)S(1)}, bf16[64,1152]{1,0:T(8,128)(2,1)S(1)}, u32[]{:S(2)}, u32[]{:S(2)}) %collective-permute-start.26) | collective-permute-done | bytes 147488 | tf_op jit(solution)/shard_map/ppermute | solution.py:222
  (53 shorter events, 5.8 us)
Async XLA Ops:
  0.9 11.9 %collective-permute-start.1 = (bf16[64,1152]{1,0:T(8,128)(2,1)S(1)}, bf16[64,1152]{1,0:T(8,128)(2,1)S(1)}, u32[]{:S(2)}, u32[]{:S(2)}) collective-permute-start(bf16[64,1152]{1,0:T(8,128)(2,1)S(1)} %pack.1.refs_3_.refs_4_), channel_id=1, source_target_pairs={{0,8},{1,9},{2,10},{3,11},{4,12},{5,13},{6,14},{7,15},{8,0},{9,1},... | collective-permute-start | bytes 442376 | tf_op jit(solution)/shard_map/ppermute | solution.py:222
  5.0 9.3 %collective-permute-start.3 = (bf16[64,1152]{1,0:T(8,128)(2,1)S(1)}, bf16[64,1152]{1,0:T(8,128)(2,1)S(1)}, u32[]{:S(2)}, u32[]{:S(2)}) collective-permute-start(bf16[64,1152]{1,0:T(8,128)(2,1)S(1)} %pack.1.refs_3_.refs_4_), channel_id=1, source_target_pairs={{0,2},{1,3},{2,0},{3,1},{4,6},{5,7},{6,4},{7,5},{8,10},{9,11},{10,... | collective-permute-start | bytes 442376 | tf_op jit(solution)/shard_map/ppermute | solution.py:222
  6.6 7.7 %collective-permute-start = (bf16[64,1152]{1,0:T(8,128)(2,1)S(1)}, bf16[64,1152]{1,0:T(8,128)(2,1)S(1)}, u32[]{:S(2)}, u32[]{:S(2)}) collective-permute-start(bf16[64,1152]{1,0:T(8,128)(2,1)S(1)} %pack.1.refs_3_.refs_4_), channel_id=1, source_target_pairs={{0,4},{1,5},{2,6},{3,7},{4,0},{5,1},{6,2},{7,3},{8,12},{9,13},{10,... | collective-permute-start | bytes 442376 | tf_op jit(solution)/shard_map/ppermute | solution.py:222
  12.9 5.2 %collective-permute-start.4 = (bf16[64,1152]{1,0:T(8,128)(2,1)S(1)}, bf16[64,1152]{1,0:T(8,128)(2,1)S(1)}, u32[]{:S(2)}, u32[]{:S(2)}) collective-permute-start(bf16[64,1152]{1,0:T(8,128)(2,1)S(1)} %get-tuple-element.77.refs_0_), channel_id=1, source_target_pairs={{0,2},{1,3},{2,0},{3,1},{4,6},{5,7},{6,4},{7,5},{8,10},{9,11},{10,... | collective-permute-start | bytes 442376 | tf_op jit(solution)/shard_map/ppermute | solution.py:222
  13.7 5.1 %collective-permute-start.2 = (bf16[64,1152]{1,0:T(8,128)(2,1)S(1)}, bf16[64,1152]{1,0:T(8,128)(2,1)S(1)}, u32[]{:S(2)}, u32[]{:S(2)}) collective-permute-start(bf16[64,1152]{1,0:T(8,128)(2,1)S(1)} %get-tuple-element.77.refs_0_), channel_id=1, source_target_pairs={{0,4},{1,5},{2,6},{3,7},{4,0},{5,1},{6,2},{7,3},{8,12},{9,13},{10,... | collective-permute-start | bytes 442376 | tf_op jit(solution)/shard_map/ppermute | solution.py:222
  14.3 5.8 %collective-permute-start.5 = (bf16[64,1152]{1,0:T(8,128)(2,1)S(1)}, bf16[64,1152]{1,0:T(8,128)(2,1)S(1)}, u32[]{:S(2)}, u32[]{:S(2)}) collective-permute-start(bf16[64,1152]{1,0:T(8,128)(2,1)S(1)} %get-tuple-element.77.refs_0_), channel_id=1, source_target_pairs={{0,1},{1,0},{2,3},{3,2},{4,5},{5,4},{6,7},{7,6},{8,9},{9,8},{10,11... | collective-permute-start | bytes 442376 | tf_op jit(solution)/shard_map/ppermute | solution.py:222
  18.9 6.3 %collective-permute-start.7 = (bf16[64,1152]{1,0:T(8,128)(2,1)S(1)}, bf16[64,1152]{1,0:T(8,128)(2,1)S(1)}, u32[]{:S(2)}, u32[]{:S(2)}) collective-permute-start(bf16[64,1152]{1,0:T(8,128)(2,1)S(1)} %collective-permute-done.2.refs_1_.refs_0_), channel_id=1, source_target_pairs={{0,2},{1,3},{2,0},{3,1},{4,6},{5,7},{6,4},{7,5},{8,10},{9,11},{10,... | collective-permute-start | bytes 442376 | tf_op jit(solution)/shard_map/ppermute | solution.py:222
  22.9 3.5 %collective-permute-start.10 = (bf16[64,1152]{1,0:T(8,128)(2,1)S(1)}, bf16[64,1152]{1,0:T(8,128)(2,1)S(1)}, u32[]{:S(2)}, u32[]{:S(2)}) collective-permute-start(bf16[64,1152]{1,0:T(8,128)(2,1)S(1)} %get-tuple-element.90), channel_id=1, source_target_pairs={{0,1},{1,0},{2,3},{3,2},{4,5},{5,4},{6,7},{7,6},{8,9},{9,8},{10,11... | collective-permute-start | bytes 442376 | tf_op jit(solution)/shard_map/ppermute | solution.py:222
  23.1 3.3 %collective-permute-start.11 = (bf16[64,1152]{1,0:T(8,128)(2,1)S(1)}, bf16[64,1152]{1,0:T(8,128)(2,1)S(1)}, u32[]{:S(2)}, u32[]{:S(2)}) collective-permute-start(bf16[64,1152]{1,0:T(8,128)(2,1)S(1)} %get-tuple-element.91), channel_id=1, source_target_pairs={{0,1},{1,0},{2,3},{3,2},{4,5},{5,4},{6,7},{7,6},{8,9},{9,8},{10,11... | collective-permute-start | bytes 442376 | tf_op jit(solution)/shard_map/ppermute | solution.py:222
  23.5 3.8 %collective-permute-start.8 = (bf16[64,1152]{1,0:T(8,128)(2,1)S(1)}, bf16[64,1152]{1,0:T(8,128)(2,1)S(1)}, u32[]{:S(2)}, u32[]{:S(2)}) collective-permute-start(bf16[64,1152]{1,0:T(8,128)(2,1)S(1)} %collective-permute-done.2.refs_1_.refs_0_), channel_id=1, source_target_pairs={{0,1},{1,0},{2,3},{3,2},{4,5},{5,4},{6,7},{7,6},{8,9},{9,8},{10,11... | collective-permute-start | bytes 442376 | tf_op jit(solution)/shard_map/ppermute | solution.py:222
  25.1 6.6 %collective-permute-start.12 = (bf16[64,1152]{1,0:T(8,128)(2,1)S(1)}, bf16[64,1152]{1,0:T(8,128)(2,1)S(1)}, u32[]{:S(2)}, u32[]{:S(2)}) collective-permute-start(bf16[64,1152]{1,0:T(8,128)(2,1)S(1)} %collective-permute-done.refs_0_), channel_id=1, source_target_pairs={{0,2},{1,3},{2,0},{3,1},{4,6},{5,7},{6,4},{7,5},{8,10},{9,11},{10,... | collective-permute-start | bytes 442376 | tf_op jit(solution)/shard_map/ppermute | solution.py:222
  26.5 8.1 %collective-permute-start.19 = (bf16[64,1152]{1,0:T(8,128)(2,1)S(1)}, bf16[64,1152]{1,0:T(8,128)(2,1)S(1)}, u32[]{:S(2)}, u32[]{:S(2)}) collective-permute-start(bf16[64,1152]{1,0:T(8,128)(2,1)S(1)} %get-tuple-element.105), channel_id=1, source_target_pairs={{0,2},{1,3},{2,0},{3,1},{4,6},{5,7},{6,4},{7,5},{8,10},{9,11},{10,... | collective-permute-start | bytes 442376 | tf_op jit(solution)/shard_map/ppermute | solution.py:222
  30.0 4.6 %collective-permute-start.17 = (bf16[64,1152]{1,0:T(8,128)(2,1)S(1)}, bf16[64,1152]{1,0:T(8,128)(2,1)S(1)}, u32[]{:S(2)}, u32[]{:S(2)}) collective-permute-start(bf16[64,1152]{1,0:T(8,128)(2,1)S(1)} %get-tuple-element.103), channel_id=1, source_target_pairs={{0,1},{1,0},{2,3},{3,2},{4,5},{5,4},{6,7},{7,6},{8,9},{9,8},{10,11... | collective-permute-start | bytes 442376 | tf_op jit(solution)/shard_map/ppermute | solution.py:222
  30.1 6.4 %collective-permute-start.15 = (bf16[64,1152]{1,0:T(8,128)(2,1)S(1)}, bf16[64,1152]{1,0:T(8,128)(2,1)S(1)}, u32[]{:S(2)}, u32[]{:S(2)}) collective-permute-start(bf16[64,1152]{1,0:T(8,128)(2,1)S(1)} %pack.1.refs_3_.refs_4_), channel_id=1, source_target_pairs={{0,1},{1,0},{2,3},{3,2},{4,5},{5,4},{6,7},{7,6},{8,9},{9,8},{10,11... | collective-permute-start | bytes 442376 | tf_op jit(solution)/shard_map/ppermute | solution.py:222
  30.6 4.5 %collective-permute-start.18 = (bf16[64,1152]{1,0:T(8,128)(2,1)S(1)}, bf16[64,1152]{1,0:T(8,128)(2,1)S(1)}, u32[]{:S(2)}, u32[]{:S(2)}) collective-permute-start(bf16[64,1152]{1,0:T(8,128)(2,1)S(1)} %get-tuple-element.104), channel_id=1, source_target_pairs={{0,1},{1,0},{2,3},{3,2},{4,5},{5,4},{6,7},{7,6},{8,9},{9,8},{10,11... | collective-permute-start | bytes 442376 | tf_op jit(solution)/shard_map/ppermute | solution.py:222
  31.8 4.7 %collective-permute-start.16 = (bf16[64,1152]{1,0:T(8,128)(2,1)S(1)}, bf16[64,1152]{1,0:T(8,128)(2,1)S(1)}, u32[]{:S(2)}, u32[]{:S(2)}) collective-permute-start(bf16[64,1152]{1,0:T(8,128)(2,1)S(1)} %collective-permute-done.3.refs_2_.refs_5_), channel_id=1, source_target_pairs={{0,1},{1,0},{2,3},{3,2},{4,5},{5,4},{6,7},{7,6},{8,9},{9,8},{10,11... | collective-permute-start | bytes 442376 | tf_op jit(solution)/shard_map/ppermute | solution.py:222
  35.1 7.4 %collective-permute-start.24 = (bf16[64,1152]{1,0:T(8,128)(2,1)S(1)}, bf16[64,1152]{1,0:T(8,128)(2,1)S(1)}, u32[]{:S(2)}, u32[]{:S(2)}) collective-permute-start(bf16[64,1152]{1,0:T(8,128)(2,1)S(1)} %get-tuple-element.119), channel_id=1, source_target_pairs={{0,2},{1,3},{2,0},{3,1},{4,6},{5,7},{6,4},{7,5},{8,10},{9,11},{10,... | collective-permute-start | bytes 442376 | tf_op jit(solution)/shard_map/ppermute | solution.py:222
  42.0 2.4 %collective-permute-start.20 = (bf16[64,1152]{1,0:T(8,128)(2,1)S(1)}, bf16[64,1152]{1,0:T(8,128)(2,1)S(1)}, u32[]{:S(2)}, u32[]{:S(2)}) collective-permute-start(bf16[64,1152]{1,0:T(8,128)(2,1)S(1)} %get-tuple-element.113), channel_id=1, source_target_pairs={{0,1},{1,0},{2,3},{3,2},{4,5},{5,4},{6,7},{7,6},{8,9},{9,8},{10,11... | collective-permute-start | bytes 442376 | tf_op jit(solution)/shard_map/ppermute | solution.py:222
  42.1 2.4 %collective-permute-start.21 = (bf16[64,1152]{1,0:T(8,128)(2,1)S(1)}, bf16[64,1152]{1,0:T(8,128)(2,1)S(1)}, u32[]{:S(2)}, u32[]{:S(2)}) collective-permute-start(bf16[64,1152]{1,0:T(8,128)(2,1)S(1)} %get-tuple-element.114), channel_id=1, source_target_pairs={{0,1},{1,0},{2,3},{3,2},{4,5},{5,4},{6,7},{7,6},{8,9},{9,8},{10,11... | collective-permute-start | bytes 442376 | tf_op jit(solution)/shard_map/ppermute | solution.py:222
  42.6 5.9 %collective-permute-start.25 = (bf16[64,1152]{1,0:T(8,128)(2,1)S(1)}, bf16[64,1152]{1,0:T(8,128)(2,1)S(1)}, u32[]{:S(2)}, u32[]{:S(2)}) collective-permute-start(bf16[64,1152]{1,0:T(8,128)(2,1)S(1)} %get-tuple-element.131), channel_id=1, source_target_pairs={{0,4},{1,5},{2,6},{3,7},{4,0},{5,1},{6,2},{7,3},{8,12},{9,13},{10,... | collective-permute-start | bytes 442376 | tf_op jit(solution)/shard_map/ppermute | solution.py:222
  43.3 7.7 %collective-permute-start.27 = (bf16[64,1152]{1,0:T(8,128)(2,1)S(1)}, bf16[64,1152]{1,0:T(8,128)(2,1)S(1)}, u32[]{:S(2)}, u32[]{:S(2)}) collective-permute-start(bf16[64,1152]{1,0:T(8,128)(2,1)S(1)} %get-tuple-element.137), channel_id=1, source_target_pairs={{0,2},{1,3},{2,0},{3,1},{4,6},{5,7},{6,4},{7,5},{8,10},{9,11},{10,... | collective-permute-start | bytes 442376 | tf_op jit(solution)/shard_map/ppermute | solution.py:222
  44.5 8.4 %collective-permute-start.29 = (bf16[64,1152]{1,0:T(8,128)(2,1)S(1)}, bf16[64,1152]{1,0:T(8,128)(2,1)S(1)}, u32[]{:S(2)}, u32[]{:S(2)}) collective-permute-start(bf16[64,1152]{1,0:T(8,128)(2,1)S(1)} %get-tuple-element.142), channel_id=1, source_target_pairs={{0,2},{1,3},{2,0},{3,1},{4,6},{5,7},{6,4},{7,5},{8,10},{9,11},{10,... | collective-permute-start | bytes 442376 | tf_op jit(solution)/shard_map/ppermute | solution.py:222
  48.5 9.3 %collective-permute-start.26 = (bf16[64,1152]{1,0:T(8,128)(2,1)S(1)}, bf16[64,1152]{1,0:T(8,128)(2,1)S(1)}, u32[]{:S(2)}, u32[]{:S(2)}) collective-permute-start(bf16[64,1152]{1,0:T(8,128)(2,1)S(1)} %get-tuple-element.135), channel_id=1, source_target_pairs={{0,8},{1,9},{2,10},{3,11},{4,12},{5,13},{6,14},{7,15},{8,0},{9,1},... | collective-permute-start | bytes 442376 | tf_op jit(solution)/shard_map/ppermute | solution.py:222
  51.0 7.1 %collective-permute-start.28 = (bf16[64,1152]{1,0:T(8,128)(2,1)S(1)}, bf16[64,1152]{1,0:T(8,128)(2,1)S(1)}, u32[]{:S(2)}, u32[]{:S(2)}) collective-permute-start(bf16[64,1152]{1,0:T(8,128)(2,1)S(1)} %get-tuple-element.141), channel_id=1, source_target_pairs={{0,4},{1,5},{2,6},{3,7},{4,0},{5,1},{6,2},{7,3},{8,12},{9,13},{10,... | collective-permute-start | bytes 442376 | tf_op jit(solution)/shard_map/ppermute | solution.py:222
  (6 other events, 10.8 us)

commit v15 on v14

--- a/solution.py
+++ b/solution.py
@@ -294,11 +294,11 @@
         block[3] = swap(block[2], 4)
         other[0] = y_0
         gather(2, [block[1], block[3], y_0])
+        gather(1)
         compute(2)
         gather(3)
         reduce_core(2)
         compute(3)
-        gather(1)
         reduce_core(3, [y_came[2]])
         compute(1, 0)
         z_3 = swap(reduce_y(3), 4)

time: 59.1 us -> 56.7 us (0.959)
  waiting for transfers between devices: 18.4 us -> 15.5 us
    ppermute x30, waiting for transfers between devices: 18.4 us -> 15.5 us  [swap(): return lax.ppermute(x, 'exp', [(i, i ^ bits) for i in range(n_dev)])]
  transfers between devices with their start and end apart: 30 -> 30, of which waited for: 9 -> 10; matrix products, arithmetic and copies ran while one was open for 0% -> 0% of each run, Pallas kernels for 26% -> 27%
where the time goes in v15:
time: 56.7 us; the launch traced here: 56.5 us
  starting transfers between devices  23.8 us (42%)
  Pallas kernels  17 us (30%)
  waiting for transfers between devices  15.5 us (27%)
    ppermute x30, starting transfers between devices, swap(): return lax.ppermute(x, 'exp', [(i, i ^ bits) for i in range(n_dev)])  23.8 us
    pallas_call x16, Pallas kernels, call(): pl.pallas_call(body_with_chain if reads_chain else body, out_shape=list(o...  16.3 us
    ppermute x30, waiting for transfers between devices, swap(): return lax.ppermute(x, 'exp', [(i, i ^ bits) for i in range(n_dev)])  15.5 us
  transfers between devices with their start and end apart: 30, of which 10 were waited for; matrix products, arithmetic and copies ran while one was open for 0% of the time, Pallas kernels for 27%

profile of v15, /device:TPU:0, one launch (start us, length us, event | category | flops | bytes accessed | tf_op | source)
XLA Modules:
  0.0 56.5 jit_solution(13702621042460776187)
XLA Ops:
  0.0 0.9 %pack.1.refs_3_.refs_4_ = bf16[64,1152]{1,0:T(8,128)(2,1)S(1)} custom-call(s32[8,64]{1,0:T(8,128)} %bitcast.2, bf16[64,1024]{1,0:T(8,128)(2,1)} %refs_1_.2), custom_call_target="tpu_custom_call" | custom-call | bytes 10000 | tf_op jit(solution)/shard_map/pack/pallas_call | solution.py:201
  0.9 4.1 %collective-permute-start.1 = (bf16[64,1152]{1,0:T(8,128)(2,1)S(1)}, bf16[64,1152]{1,0:T(8,128)(2,1)S(1)}, u32[]{:S(2)}, u32[]{:S(2)}) collective-permute-start(bf16[64,1152]{1,0:T(8,128)(2,1)S(1)} %pack.1.refs_3_.refs_4_), channel_id=1, source_target_pairs={{0,8},{1,9},{2,10},{3,11},{4,12},{5,13},{6,14},{7,15},{8,0},{9,1},... | collective-permute-start | bytes 442376 | tf_op jit(solution)/shard_map/ppermute | solution.py:222
  5.0 1.5 %collective-permute-start.3 = (bf16[64,1152]{1,0:T(8,128)(2,1)S(1)}, bf16[64,1152]{1,0:T(8,128)(2,1)S(1)}, u32[]{:S(2)}, u32[]{:S(2)}) collective-permute-start(bf16[64,1152]{1,0:T(8,128)(2,1)S(1)} %pack.1.refs_3_.refs_4_), channel_id=1, source_target_pairs={{0,2},{1,3},{2,0},{3,1},{4,6},{5,7},{6,4},{7,5},{8,10},{9,11},{10,... | collective-permute-start | bytes 442376 | tf_op jit(solution)/shard_map/ppermute | solution.py:222
  6.6 1.6 %collective-permute-start = (bf16[64,1152]{1,0:T(8,128)(2,1)S(1)}, bf16[64,1152]{1,0:T(8,128)(2,1)S(1)}, u32[]{:S(2)}, u32[]{:S(2)}) collective-permute-start(bf16[64,1152]{1,0:T(8,128)(2,1)S(1)} %pack.1.refs_3_.refs_4_), channel_id=1, source_target_pairs={{0,4},{1,5},{2,6},{3,7},{4,0},{5,1},{6,2},{7,3},{8,12},{9,13},{10,... | collective-permute-start | bytes 442376 | tf_op jit(solution)/shard_map/ppermute | solution.py:222
  8.1 4.7 %load.1 = (bf16[1024,128]{1,0:T(8,128)(2,1)S(1)}, bf16[2,1024,2048]{2,1,0:T(8,128)(2,1)S(1)}, bf16[2,1024,1024]{2,1,0:T(8,128)(2,1)S(1)}) custom-call(bf16[2,1024]{1,0:T(2,128)(2,1)} %bitcast.3, bf16[2,1024,2048]{2,1,0:T(8,128)(2,1)} %refs_1_.3, bf16[2,1024,1024]{2,1,0:T(8,128)(2,1)} %refs_2_.1, bf16[64,1152]{1,0:T(8,128)(2,1)S(1)} %pack.1.refs_3_.refs_4_), custom_call_target="tpu_custom_call" | custom-call | bytes 10000 | tf_op jit(solution)/shard_map/load/pallas_call | solution.py:201
  12.9 0.8 %collective-permute-start.4 = (bf16[64,1152]{1,0:T(8,128)(2,1)S(1)}, bf16[64,1152]{1,0:T(8,128)(2,1)S(1)}, u32[]{:S(2)}, u32[]{:S(2)}) collective-permute-start(bf16[64,1152]{1,0:T(8,128)(2,1)S(1)} %get-tuple-element.77.refs_0_), channel_id=1, source_target_pairs={{0,2},{1,3},{2,0},{3,1},{4,6},{5,7},{6,4},{7,5},{8,10},{9,11},{10,... | collective-permute-start | bytes 442376 | tf_op jit(solution)/shard_map/ppermute | solution.py:222
  14.3 1.1 %collective-permute-start.5 = (bf16[64,1152]{1,0:T(8,128)(2,1)S(1)}, bf16[64,1152]{1,0:T(8,128)(2,1)S(1)}, u32[]{:S(2)}, u32[]{:S(2)}) collective-permute-start(bf16[64,1152]{1,0:T(8,128)(2,1)S(1)} %collective-permute-done.refs_0_), channel_id=1, source_target_pairs={{0,2},{1,3},{2,0},{3,1},{4,6},{5,7},{6,4},{7,5},{8,10},{9,11},{10,... | collective-permute-start | bytes 442376 | tf_op jit(solution)/shard_map/ppermute | solution.py:222
  15.4 3.4 %collective-permute-done.4.refs_6_ = bf16[64,1152]{1,0:T(8,128)(2,1)S(1)} collective-permute-done((bf16[64,1152]{1,0:T(8,128)(2,1)S(1)}, bf16[64,1152]{1,0:T(8,128)(2,1)S(1)}, u32[]{:S(2)}, u32[]{:S(2)}) %collective-permute-start.4) | collective-permute-done | bytes 147488 | tf_op jit(solution)/shard_map/ppermute | solution.py:222
  18.9 1.3 %collective-permute-start.12 = (bf16[64,1152]{1,0:T(8,128)(2,1)S(1)}, bf16[64,1152]{1,0:T(8,128)(2,1)S(1)}, u32[]{:S(2)}, u32[]{:S(2)}) collective-permute-start(bf16[64,1152]{1,0:T(8,128)(2,1)S(1)} %collective-permute-done.2.refs_1_.refs_0_), channel_id=1, source_target_pairs={{0,2},{1,3},{2,0},{3,1},{4,6},{5,7},{6,4},{7,5},{8,10},{9,11},{10,... | collective-permute-start | bytes 442376 | tf_op jit(solution)/shard_map/ppermute | solution.py:222
  20.1 1.1 %collective-permute-done.5.refs_3_ = bf16[64,1152]{1,0:T(8,128)(2,1)S(1)} collective-permute-done((bf16[64,1152]{1,0:T(8,128)(2,1)S(1)}, bf16[64,1152]{1,0:T(8,128)(2,1)S(1)}, u32[]{:S(2)}, u32[]{:S(2)}) %collective-permute-start.5) | collective-permute-done | bytes 147488 | tf_op jit(solution)/shard_map/ppermute | solution.py:222
  21.3 2.7 %expert.3 = (f32[128,1152]{1,0:T(8,128)S(1)}, bf16[64,1152]{1,0:T(8,128)(2,1)S(1)}, bf16[64,1152]{1,0:T(8,128)(2,1)S(1)}, bf16[1024,128]{1,0:T(8,128)(2,1)S(1)},...) custom-call(bf16[64,1152]{1,0:T(8,128)(2,1)S(1)} %get-tuple-element., ...), custom_call_target="tpu_custom_call", output_to_operand_aliasing={{3}: (4, {}), {4}: (5, {}), {5}: (6, {})} | custom-call | bytes 10000 | tf_op jit(solution)/shard_map/expert/pallas_call | solution.py:201
  25.7 0.9 %collective-permute-start.19 = (bf16[64,1152]{1,0:T(8,128)(2,1)S(1)}, bf16[64,1152]{1,0:T(8,128)(2,1)S(1)}, u32[]{:S(2)}, u32[]{:S(2)}) collective-permute-start(bf16[64,1152]{1,0:T(8,128)(2,1)S(1)} %get-tuple-element.105), channel_id=1, source_target_pairs={{0,2},{1,3},{2,0},{3,1},{4,6},{5,7},{6,4},{7,5},{8,10},{9,11},{10,... | collective-permute-start | bytes 442376 | tf_op jit(solution)/shard_map/ppermute | solution.py:222
  26.5 2.7 %expert.4 = (f32[128,1152]{1,0:T(8,128)S(1)}, bf16[64,1152]{1,0:T(8,128)(2,1)S(1)}, bf16[64,1152]{1,0:T(8,128)(2,1)S(1)}, bf16[1024,128]{1,0:T(8,128)(2,1)S(1)},...) custom-call(bf16[64,1152]{1,0:T(8,128)(2,1)S(1)} %collective-permute, ...), custom_call_target="tpu_custom_call", output_to_operand_aliasing={{3}: (4, {}), {4}: (5, {}), {5}: (6, {})} | custom-call | bytes 10000 | tf_op jit(solution)/shard_map/expert/pallas_call | solution.py:201
  30.3 1.4 %collective-permute-done.19.refs_3_.refs_1_ = bf16[64,1152]{1,0:T(8,128)(2,1)S(1)} collective-permute-done((bf16[64,1152]{1,0:T(8,128)(2,1)S(1)}, bf16[64,1152]{1,0:T(8,128)(2,1)S(1)}, u32[]{:S(2)}, u32[]{:S(2)}) %collective-permute-start.19) | collective-permute-done | bytes 147488 | tf_op jit(solution)/shard_map/ppermute | solution.py:222
  32.3 1.1 %collective-permute-start.24 = (bf16[64,1152]{1,0:T(8,128)(2,1)S(1)}, bf16[64,1152]{1,0:T(8,128)(2,1)S(1)}, u32[]{:S(2)}, u32[]{:S(2)}) collective-permute-start(bf16[64,1152]{1,0:T(8,128)(2,1)S(1)} %get-tuple-element.119), channel_id=1, source_target_pairs={{0,2},{1,3},{2,0},{3,1},{4,6},{5,7},{6,4},{7,5},{8,10},{9,11},{10,... | collective-permute-start | bytes 442376 | tf_op jit(solution)/shard_map/ppermute | solution.py:222
  33.4 4.9 %expert.5 = (f32[128,1152]{1,0:T(8,128)S(1)}, f32[128,1152]{1,0:T(8,128)S(1)}, bf16[64,1152]{1,0:T(8,128)(2,1)S(1)}, bf16[64,1152]{1,0:T(8,128)(2,1)S(1)}, bf16[...) custom-call(bf16[64,1152]{1,0:T(8,128)(2,1)S(1)} %collective-permute, ...), custom_call_target="tpu_custom_call", output_to_operand_aliasing={{6}: (8, {}), {7}: (9, {}), {8}: (10, {})} | custom-call | bytes 10000 | tf_op jit(solution)/shard_map/expert/pallas_call | solution.py:201
  39.5 1.1 %collective-permute-start.25 = (bf16[64,1152]{1,0:T(8,128)(2,1)S(1)}, bf16[64,1152]{1,0:T(8,128)(2,1)S(1)}, u32[]{:S(2)}, u32[]{:S(2)}) collective-permute-start(bf16[64,1152]{1,0:T(8,128)(2,1)S(1)} %get-tuple-element.131), channel_id=1, source_target_pairs={{0,4},{1,5},{2,6},{3,7},{4,0},{5,1},{6,2},{7,3},{8,12},{9,13},{10,... | collective-permute-start | bytes 442376 | tf_op jit(solution)/shard_map/ppermute | solution.py:222
  40.7 1.0 %collective-permute-start.27 = (bf16[64,1152]{1,0:T(8,128)(2,1)S(1)}, bf16[64,1152]{1,0:T(8,128)(2,1)S(1)}, u32[]{:S(2)}, u32[]{:S(2)}) collective-permute-start(bf16[64,1152]{1,0:T(8,128)(2,1)S(1)} %get-tuple-element.137), channel_id=1, source_target_pairs={{0,2},{1,3},{2,0},{3,1},{4,6},{5,7},{6,4},{7,5},{8,10},{9,11},{10,... | collective-permute-start | bytes 442376 | tf_op jit(solution)/shard_map/ppermute | solution.py:222
  41.7 1.2 %collective-permute-start.29 = (bf16[64,1152]{1,0:T(8,128)(2,1)S(1)}, bf16[64,1152]{1,0:T(8,128)(2,1)S(1)}, u32[]{:S(2)}, u32[]{:S(2)}) collective-permute-start(bf16[64,1152]{1,0:T(8,128)(2,1)S(1)} %get-tuple-element.142), channel_id=1, source_target_pairs={{0,2},{1,3},{2,0},{3,1},{4,6},{5,7},{6,4},{7,5},{8,10},{9,11},{10,... | collective-permute-start | bytes 442376 | tf_op jit(solution)/shard_map/ppermute | solution.py:222
  42.9 2.7 %collective-permute-done.25.refs_2_ = bf16[64,1152]{1,0:T(8,128)(2,1)S(1)} collective-permute-done((bf16[64,1152]{1,0:T(8,128)(2,1)S(1)}, bf16[64,1152]{1,0:T(8,128)(2,1)S(1)}, u32[]{:S(2)}, u32[]{:S(2)}) %collective-permute-start.25) | collective-permute-done | bytes 147488 | tf_op jit(solution)/shard_map/ppermute | solution.py:222
  45.6 2.7 %collective-permute-start.26 = (bf16[64,1152]{1,0:T(8,128)(2,1)S(1)}, bf16[64,1152]{1,0:T(8,128)(2,1)S(1)}, u32[]{:S(2)}, u32[]{:S(2)}) collective-permute-start(bf16[64,1152]{1,0:T(8,128)(2,1)S(1)} %get-tuple-element.135), channel_id=1, source_target_pairs={{0,8},{1,9},{2,10},{3,11},{4,12},{5,13},{6,14},{7,15},{8,0},{9,1},... | collective-permute-start | bytes 442376 | tf_op jit(solution)/shard_map/ppermute | solution.py:222
  48.4 1.6 %collective-permute-start.28 = (bf16[64,1152]{1,0:T(8,128)(2,1)S(1)}, bf16[64,1152]{1,0:T(8,128)(2,1)S(1)}, u32[]{:S(2)}, u32[]{:S(2)}) collective-permute-start(bf16[64,1152]{1,0:T(8,128)(2,1)S(1)} %get-tuple-element.141), channel_id=1, source_target_pairs={{0,4},{1,5},{2,6},{3,7},{4,0},{5,1},{6,2},{7,3},{8,12},{9,13},{10,... | collective-permute-start | bytes 442376 | tf_op jit(solution)/shard_map/ppermute | solution.py:222
  50.0 5.1 %collective-permute-done.26.refs_1_ = bf16[64,1152]{1,0:T(8,128)(2,1)S(1)} collective-permute-done((bf16[64,1152]{1,0:T(8,128)(2,1)S(1)}, bf16[64,1152]{1,0:T(8,128)(2,1)S(1)}, u32[]{:S(2)}, u32[]{:S(2)}) %collective-permute-start.26) | collective-permute-done | bytes 147488 | tf_op jit(solution)/shard_map/ppermute | solution.py:222
  55.8 0.8 %finish.1 = bf16[64,1024]{1,0:T(8,128)(2,1)} custom-call(f32[64,1152]{1,0:T(8,128)S(1)} %get-tuple-element.129.refs_0_, bf16[64,1152]{1,0:T(8,128)(2,1)S(1)} %collective-permute-done.26.refs_1_, bf16[64,1152]{1,0:T(8,128)(2,1)S(1)} %collective-permute-done.28.refs_2_, bf16[64,1152]{1,0:T(8,128)(2,1)S(1)} %collective-permute-done.29.refs_3_), custom_call_target="tpu_custom_call" | custom-call | tf_op jit(solution)/shard_map/finish/pallas_call | solution.py:319
  (53 shorter events, 6.0 us)
Async XLA Ops:
  0.9 11.9 %collective-permute-start.1 = (bf16[64,1152]{1,0:T(8,128)(2,1)S(1)}, bf16[64,1152]{1,0:T(8,128)(2,1)S(1)}, u32[]{:S(2)}, u32[]{:S(2)}) collective-permute-start(bf16[64,1152]{1,0:T(8,128)(2,1)S(1)} %pack.1.refs_3_.refs_4_), channel_id=1, source_target_pairs={{0,8},{1,9},{2,10},{3,11},{4,12},{5,13},{6,14},{7,15},{8,0},{9,1},... | collective-permute-start | bytes 442376 | tf_op jit(solution)/shard_map/ppermute | solution.py:222
  5.0 10.4 %collective-permute-start.3 = (bf16[64,1152]{1,0:T(8,128)(2,1)S(1)}, bf16[64,1152]{1,0:T(8,128)(2,1)S(1)}, u32[]{:S(2)}, u32[]{:S(2)}) collective-permute-start(bf16[64,1152]{1,0:T(8,128)(2,1)S(1)} %pack.1.refs_3_.refs_4_), channel_id=1, source_target_pairs={{0,2},{1,3},{2,0},{3,1},{4,6},{5,7},{6,4},{7,5},{8,10},{9,11},{10,... | collective-permute-start | bytes 442376 | tf_op jit(solution)/shard_map/ppermute | solution.py:222
  6.6 7.7 %collective-permute-start = (bf16[64,1152]{1,0:T(8,128)(2,1)S(1)}, bf16[64,1152]{1,0:T(8,128)(2,1)S(1)}, u32[]{:S(2)}, u32[]{:S(2)}) collective-permute-start(bf16[64,1152]{1,0:T(8,128)(2,1)S(1)} %pack.1.refs_3_.refs_4_), channel_id=1, source_target_pairs={{0,4},{1,5},{2,6},{3,7},{4,0},{5,1},{6,2},{7,3},{8,12},{9,13},{10,... | collective-permute-start | bytes 442376 | tf_op jit(solution)/shard_map/ppermute | solution.py:222
  12.9 5.9 %collective-permute-start.4 = (bf16[64,1152]{1,0:T(8,128)(2,1)S(1)}, bf16[64,1152]{1,0:T(8,128)(2,1)S(1)}, u32[]{:S(2)}, u32[]{:S(2)}) collective-permute-start(bf16[64,1152]{1,0:T(8,128)(2,1)S(1)} %get-tuple-element.77.refs_0_), channel_id=1, source_target_pairs={{0,2},{1,3},{2,0},{3,1},{4,6},{5,7},{6,4},{7,5},{8,10},{9,11},{10,... | collective-permute-start | bytes 442376 | tf_op jit(solution)/shard_map/ppermute | solution.py:222
  13.7 5.1 %collective-permute-start.2 = (bf16[64,1152]{1,0:T(8,128)(2,1)S(1)}, bf16[64,1152]{1,0:T(8,128)(2,1)S(1)}, u32[]{:S(2)}, u32[]{:S(2)}) collective-permute-start(bf16[64,1152]{1,0:T(8,128)(2,1)S(1)} %get-tuple-element.77.refs_0_), channel_id=1, source_target_pairs={{0,4},{1,5},{2,6},{3,7},{4,0},{5,1},{6,2},{7,3},{8,12},{9,13},{10,... | collective-permute-start | bytes 442376 | tf_op jit(solution)/shard_map/ppermute | solution.py:222
  14.3 7.0 %collective-permute-start.10 = (bf16[64,1152]{1,0:T(8,128)(2,1)S(1)}, bf16[64,1152]{1,0:T(8,128)(2,1)S(1)}, u32[]{:S(2)}, u32[]{:S(2)}) collective-permute-start(bf16[64,1152]{1,0:T(8,128)(2,1)S(1)} %get-tuple-element.77.refs_0_), channel_id=1, source_target_pairs={{0,1},{1,0},{2,3},{3,2},{4,5},{5,4},{6,7},{7,6},{8,9},{9,8},{10,11... | collective-permute-start | bytes 442376 | tf_op jit(solution)/shard_map/ppermute | solution.py:222
  14.3 7.0 %collective-permute-start.5 = (bf16[64,1152]{1,0:T(8,128)(2,1)S(1)}, bf16[64,1152]{1,0:T(8,128)(2,1)S(1)}, u32[]{:S(2)}, u32[]{:S(2)}) collective-permute-start(bf16[64,1152]{1,0:T(8,128)(2,1)S(1)} %collective-permute-done.refs_0_), channel_id=1, source_target_pairs={{0,2},{1,3},{2,0},{3,1},{4,6},{5,7},{6,4},{7,5},{8,10},{9,11},{10,... | collective-permute-start | bytes 442376 | tf_op jit(solution)/shard_map/ppermute | solution.py:222
  18.9 2.4 %collective-permute-start.11 = (bf16[64,1152]{1,0:T(8,128)(2,1)S(1)}, bf16[64,1152]{1,0:T(8,128)(2,1)S(1)}, u32[]{:S(2)}, u32[]{:S(2)}) collective-permute-start(bf16[64,1152]{1,0:T(8,128)(2,1)S(1)} %get-tuple-element.85.refs_1_), channel_id=1, source_target_pairs={{0,1},{1,0},{2,3},{3,2},{4,5},{5,4},{6,7},{7,6},{8,9},{9,8},{10,11... | collective-permute-start | bytes 442376 | tf_op jit(solution)/shard_map/ppermute | solution.py:222
  18.9 6.3 %collective-permute-start.12 = (bf16[64,1152]{1,0:T(8,128)(2,1)S(1)}, bf16[64,1152]{1,0:T(8,128)(2,1)S(1)}, u32[]{:S(2)}, u32[]{:S(2)}) collective-permute-start(bf16[64,1152]{1,0:T(8,128)(2,1)S(1)} %collective-permute-done.2.refs_1_.refs_0_), channel_id=1, source_target_pairs={{0,2},{1,3},{2,0},{3,1},{4,6},{5,7},{6,4},{7,5},{8,10},{9,11},{10,... | collective-permute-start | bytes 442376 | tf_op jit(solution)/shard_map/ppermute | solution.py:222
  24.5 2.0 %collective-permute-start.13 = (bf16[64,1152]{1,0:T(8,128)(2,1)S(1)}, bf16[64,1152]{1,0:T(8,128)(2,1)S(1)}, u32[]{:S(2)}, u32[]{:S(2)}) collective-permute-start(bf16[64,1152]{1,0:T(8,128)(2,1)S(1)} %collective-permute-done.2.refs_1_.refs_0_), channel_id=1, source_target_pairs={{0,1},{1,0},{2,3},{3,2},{4,5},{5,4},{6,7},{7,6},{8,9},{9,8},{10,11... | collective-permute-start | bytes 442376 | tf_op jit(solution)/shard_map/ppermute | solution.py:222
  25.7 6.1 %collective-permute-start.19 = (bf16[64,1152]{1,0:T(8,128)(2,1)S(1)}, bf16[64,1152]{1,0:T(8,128)(2,1)S(1)}, u32[]{:S(2)}, u32[]{:S(2)}) collective-permute-start(bf16[64,1152]{1,0:T(8,128)(2,1)S(1)} %get-tuple-element.105), channel_id=1, source_target_pairs={{0,2},{1,3},{2,0},{3,1},{4,6},{5,7},{6,4},{7,5},{8,10},{9,11},{10,... | collective-permute-start | bytes 442376 | tf_op jit(solution)/shard_map/ppermute | solution.py:222
  29.2 2.5 %collective-permute-start.17 = (bf16[64,1152]{1,0:T(8,128)(2,1)S(1)}, bf16[64,1152]{1,0:T(8,128)(2,1)S(1)}, u32[]{:S(2)}, u32[]{:S(2)}) collective-permute-start(bf16[64,1152]{1,0:T(8,128)(2,1)S(1)} %get-tuple-element.103), channel_id=1, source_target_pairs={{0,1},{1,0},{2,3},{3,2},{4,5},{5,4},{6,7},{7,6},{8,9},{9,8},{10,11... | collective-permute-start | bytes 442376 | tf_op jit(solution)/shard_map/ppermute | solution.py:222
  29.5 2.8 %collective-permute-start.18 = (bf16[64,1152]{1,0:T(8,128)(2,1)S(1)}, bf16[64,1152]{1,0:T(8,128)(2,1)S(1)}, u32[]{:S(2)}, u32[]{:S(2)}) collective-permute-start(bf16[64,1152]{1,0:T(8,128)(2,1)S(1)} %get-tuple-element.104), channel_id=1, source_target_pairs={{0,1},{1,0},{2,3},{3,2},{4,5},{5,4},{6,7},{7,6},{8,9},{9,8},{10,11... | collective-permute-start | bytes 442376 | tf_op jit(solution)/shard_map/ppermute | solution.py:222
  29.8 3.6 %collective-permute-start.8 = (bf16[64,1152]{1,0:T(8,128)(2,1)S(1)}, bf16[64,1152]{1,0:T(8,128)(2,1)S(1)}, u32[]{:S(2)}, u32[]{:S(2)}) collective-permute-start(bf16[64,1152]{1,0:T(8,128)(2,1)S(1)} %pack.1.refs_3_.refs_4_), channel_id=1, source_target_pairs={{0,1},{1,0},{2,3},{3,2},{4,5},{5,4},{6,7},{7,6},{8,9},{9,8},{10,11... | collective-permute-start | bytes 442376 | tf_op jit(solution)/shard_map/ppermute | solution.py:222
  30.0 3.4 %collective-permute-start.9 = (bf16[64,1152]{1,0:T(8,128)(2,1)S(1)}, bf16[64,1152]{1,0:T(8,128)(2,1)S(1)}, u32[]{:S(2)}, u32[]{:S(2)}) collective-permute-start(bf16[64,1152]{1,0:T(8,128)(2,1)S(1)} %collective-permute-done.3.refs_2_.refs_5_), channel_id=1, source_target_pairs={{0,1},{1,0},{2,3},{3,2},{4,5},{5,4},{6,7},{7,6},{8,9},{9,8},{10,11... | collective-permute-start | bytes 442376 | tf_op jit(solution)/shard_map/ppermute | solution.py:222
  32.3 7.1 %collective-permute-start.24 = (bf16[64,1152]{1,0:T(8,128)(2,1)S(1)}, bf16[64,1152]{1,0:T(8,128)(2,1)S(1)}, u32[]{:S(2)}, u32[]{:S(2)}) collective-permute-start(bf16[64,1152]{1,0:T(8,128)(2,1)S(1)} %get-tuple-element.119), channel_id=1, source_target_pairs={{0,2},{1,3},{2,0},{3,1},{4,6},{5,7},{6,4},{7,5},{8,10},{9,11},{10,... | collective-permute-start | bytes 442376 | tf_op jit(solution)/shard_map/ppermute | solution.py:222
  38.4 2.2 %collective-permute-start.22 = (bf16[64,1152]{1,0:T(8,128)(2,1)S(1)}, bf16[64,1152]{1,0:T(8,128)(2,1)S(1)}, u32[]{:S(2)}, u32[]{:S(2)}) collective-permute-start(bf16[64,1152]{1,0:T(8,128)(2,1)S(1)} %get-tuple-element.116), channel_id=1, source_target_pairs={{0,1},{1,0},{2,3},{3,2},{4,5},{5,4},{6,7},{7,6},{8,9},{9,8},{10,11... | collective-permute-start | bytes 442376 | tf_op jit(solution)/shard_map/ppermute | solution.py:222
  39.0 2.7 %collective-permute-start.20 = (bf16[64,1152]{1,0:T(8,128)(2,1)S(1)}, bf16[64,1152]{1,0:T(8,128)(2,1)S(1)}, u32[]{:S(2)}, u32[]{:S(2)}) collective-permute-start(bf16[64,1152]{1,0:T(8,128)(2,1)S(1)} %get-tuple-element.113), channel_id=1, source_target_pairs={{0,1},{1,0},{2,3},{3,2},{4,5},{5,4},{6,7},{7,6},{8,9},{9,8},{10,11... | collective-permute-start | bytes 442376 | tf_op jit(solution)/shard_map/ppermute | solution.py:222
  39.2 2.5 %collective-permute-start.21 = (bf16[64,1152]{1,0:T(8,128)(2,1)S(1)}, bf16[64,1152]{1,0:T(8,128)(2,1)S(1)}, u32[]{:S(2)}, u32[]{:S(2)}) collective-permute-start(bf16[64,1152]{1,0:T(8,128)(2,1)S(1)} %get-tuple-element.114), channel_id=1, source_target_pairs={{0,1},{1,0},{2,3},{3,2},{4,5},{5,4},{6,7},{7,6},{8,9},{9,8},{10,11... | collective-permute-start | bytes 442376 | tf_op jit(solution)/shard_map/ppermute | solution.py:222
  39.5 6.0 %collective-permute-start.25 = (bf16[64,1152]{1,0:T(8,128)(2,1)S(1)}, bf16[64,1152]{1,0:T(8,128)(2,1)S(1)}, u32[]{:S(2)}, u32[]{:S(2)}) collective-permute-start(bf16[64,1152]{1,0:T(8,128)(2,1)S(1)} %get-tuple-element.131), channel_id=1, source_target_pairs={{0,4},{1,5},{2,6},{3,7},{4,0},{5,1},{6,2},{7,3},{8,12},{9,13},{10,... | collective-permute-start | bytes 442376 | tf_op jit(solution)/shard_map/ppermute | solution.py:222
  40.7 7.7 %collective-permute-start.27 = (bf16[64,1152]{1,0:T(8,128)(2,1)S(1)}, bf16[64,1152]{1,0:T(8,128)(2,1)S(1)}, u32[]{:S(2)}, u32[]{:S(2)}) collective-permute-start(bf16[64,1152]{1,0:T(8,128)(2,1)S(1)} %get-tuple-element.137), channel_id=1, source_target_pairs={{0,2},{1,3},{2,0},{3,1},{4,6},{5,7},{6,4},{7,5},{8,10},{9,11},{10,... | collective-permute-start | bytes 442376 | tf_op jit(solution)/shard_map/ppermute | solution.py:222
  41.7 8.3 %collective-permute-start.29 = (bf16[64,1152]{1,0:T(8,128)(2,1)S(1)}, bf16[64,1152]{1,0:T(8,128)(2,1)S(1)}, u32[]{:S(2)}, u32[]{:S(2)}) collective-permute-start(bf16[64,1152]{1,0:T(8,128)(2,1)S(1)} %get-tuple-element.142), channel_id=1, source_target_pairs={{0,2},{1,3},{2,0},{3,1},{4,6},{5,7},{6,4},{7,5},{8,10},{9,11},{10,... | collective-permute-start | bytes 442376 | tf_op jit(solution)/shard_map/ppermute | solution.py:222
  45.6 9.5 %collective-permute-start.26 = (bf16[64,1152]{1,0:T(8,128)(2,1)S(1)}, bf16[64,1152]{1,0:T(8,128)(2,1)S(1)}, u32[]{:S(2)}, u32[]{:S(2)}) collective-permute-start(bf16[64,1152]{1,0:T(8,128)(2,1)S(1)} %get-tuple-element.135), channel_id=1, source_target_pairs={{0,8},{1,9},{2,10},{3,11},{4,12},{5,13},{6,14},{7,15},{8,0},{9,1},... | collective-permute-start | bytes 442376 | tf_op jit(solution)/shard_map/ppermute | solution.py:222
  48.4 7.4 %collective-permute-start.28 = (bf16[64,1152]{1,0:T(8,128)(2,1)S(1)}, bf16[64,1152]{1,0:T(8,128)(2,1)S(1)}, u32[]{:S(2)}, u32[]{:S(2)}) collective-permute-start(bf16[64,1152]{1,0:T(8,128)(2,1)S(1)} %get-tuple-element.141), channel_id=1, source_target_pairs={{0,4},{1,5},{2,6},{3,7},{4,0},{5,1},{6,2},{7,3},{8,12},{9,13},{10,... | collective-permute-start | bytes 442376 | tf_op jit(solution)/shard_map/ppermute | solution.py:222
  (6 other events, 9.7 us)

commit v16 on v15

--- a/solution.py
+++ b/solution.py
@@ -286,8 +286,9 @@
             )
             y_came[k] = swap(fold_send[k], 2)
 
-        def reduce_y(k, *more):
-            return step(add_kernel, [space(rows, jnp.bfloat16)], [fold_keep[k], y_came[k], *more])[0]
+        def reduce_y(k, deps=()):
+            sums = step(add_kernel, [space(rows, jnp.bfloat16)], [fold_keep[k], y_came[k]], deps)[0]
+            return swap(sums, 4 * k)
 
         z_2, z_1, y_0 = swap(mine, 8), swap(mine, 4), swap(mine, 2)
         block = {0: mine, 2: tie(z_2), 1: z_1}
@@ -299,14 +300,14 @@
         gather(3)
         reduce_core(2)
         compute(3)
-        reduce_core(3, [y_came[2]])
+        z_2 = reduce_y(2)
+        reduce_core(3)
         compute(1, 0)
-        z_3 = swap(reduce_y(3), 4)
+        z_3 = reduce_y(3, [z_2])
         reduce_core(1)
+        z_1 = reduce_y(1)
         reduce_core(0)
-        z_2 = swap(reduce_y(2, z_3), 8)
-        z_1 = swap(reduce_y(1), 4)
-        return fold_keep[0], z_2, z_1, y_came[0]
+        return fold_keep[0], z_3, z_1, y_came[0], z_2
 
     packet = call(
         pack_kernel,

time: 56.7 us -> 56.5 us (level)
  waiting for transfers between devices: 15.5 us -> 13.1 us
  starting transfers between devices: 23.8 us -> 26 us
    ppermute x30, waiting for transfers between devices: 15.5 us -> 13.1 us  [swap(): return lax.ppermute(x, 'exp', [(i, i ^ bits) for i in range(n_dev)])]
    ppermute x30, starting transfers between devices: 23.8 us -> 26 us  [swap(): return lax.ppermute(x, 'exp', [(i, i ^ bits) for i in range(n_dev)])]
  transfers between devices with their start and end apart: 30 -> 30, of which waited for: 10 -> 12; matrix products, arithmetic and copies ran while one was open for 0% -> 0% of each run, Pallas kernels for 27% -> 27%
where the time goes in v16:
time: 56.5 us; the launch traced here: 56.3 us
  starting transfers between devices  26 us (46%)
  Pallas kernels  17 us (30%)
  waiting for transfers between devices  13.1 us (23%)
    ppermute x30, starting transfers between devices, swap(): return lax.ppermute(x, 'exp', [(i, i ^ bits) for i in range(n_dev)])  26 us
    pallas_call x16, Pallas kernels, call(): pl.pallas_call(body_with_chain if reads_chain else body, out_shape=list(o...  16.3 us
    ppermute x30, waiting for transfers between devices, swap(): return lax.ppermute(x, 'exp', [(i, i ^ bits) for i in range(n_dev)])  13.1 us
  transfers between devices with their start and end apart: 30, of which 12 were waited for; matrix products, arithmetic and copies ran while one was open for 0% of the time, Pallas kernels for 27%

profile of v16, /device:TPU:0, one launch (start us, length us, event | category | flops | bytes accessed | tf_op | source)
XLA Modules:
  0.0 56.3 jit_solution(13595800308578550672)
XLA Ops:
  0.0 0.9 %pack.1.refs_3_.refs_4_ = bf16[64,1152]{1,0:T(8,128)(2,1)S(1)} custom-call(s32[8,64]{1,0:T(8,128)} %bitcast.2, bf16[64,1024]{1,0:T(8,128)(2,1)} %refs_1_.2), custom_call_target="tpu_custom_call" | custom-call | bytes 10000 | tf_op jit(solution)/shard_map/pack/pallas_call | solution.py:201
  0.9 4.1 %collective-permute-start.1 = (bf16[64,1152]{1,0:T(8,128)(2,1)S(1)}, bf16[64,1152]{1,0:T(8,128)(2,1)S(1)}, u32[]{:S(2)}, u32[]{:S(2)}) collective-permute-start(bf16[64,1152]{1,0:T(8,128)(2,1)S(1)} %pack.1.refs_3_.refs_4_), channel_id=1, source_target_pairs={{0,8},{1,9},{2,10},{3,11},{4,12},{5,13},{6,14},{7,15},{8,0},{9,1},... | collective-permute-start | bytes 442376 | tf_op jit(solution)/shard_map/ppermute | solution.py:222
  5.0 1.5 %collective-permute-start.3 = (bf16[64,1152]{1,0:T(8,128)(2,1)S(1)}, bf16[64,1152]{1,0:T(8,128)(2,1)S(1)}, u32[]{:S(2)}, u32[]{:S(2)}) collective-permute-start(bf16[64,1152]{1,0:T(8,128)(2,1)S(1)} %pack.1.refs_3_.refs_4_), channel_id=1, source_target_pairs={{0,2},{1,3},{2,0},{3,1},{4,6},{5,7},{6,4},{7,5},{8,10},{9,11},{10,... | collective-permute-start | bytes 442376 | tf_op jit(solution)/shard_map/ppermute | solution.py:222
  6.6 1.6 %collective-permute-start = (bf16[64,1152]{1,0:T(8,128)(2,1)S(1)}, bf16[64,1152]{1,0:T(8,128)(2,1)S(1)}, u32[]{:S(2)}, u32[]{:S(2)}) collective-permute-start(bf16[64,1152]{1,0:T(8,128)(2,1)S(1)} %pack.1.refs_3_.refs_4_), channel_id=1, source_target_pairs={{0,4},{1,5},{2,6},{3,7},{4,0},{5,1},{6,2},{7,3},{8,12},{9,13},{10,... | collective-permute-start | bytes 442376 | tf_op jit(solution)/shard_map/ppermute | solution.py:222
  8.1 4.7 %load.1 = (bf16[1024,128]{1,0:T(8,128)(2,1)S(1)}, bf16[2,1024,2048]{2,1,0:T(8,128)(2,1)S(1)}, bf16[2,1024,1024]{2,1,0:T(8,128)(2,1)S(1)}) custom-call(bf16[2,1024]{1,0:T(2,128)(2,1)} %bitcast.3, bf16[2,1024,2048]{2,1,0:T(8,128)(2,1)} %refs_1_.3, bf16[2,1024,1024]{2,1,0:T(8,128)(2,1)} %refs_2_.1, bf16[64,1152]{1,0:T(8,128)(2,1)S(1)} %pack.1.refs_3_.refs_4_), custom_call_target="tpu_custom_call" | custom-call | bytes 10000 | tf_op jit(solution)/shard_map/load/pallas_call | solution.py:201
  14.3 1.1 %collective-permute-start.5 = (bf16[64,1152]{1,0:T(8,128)(2,1)S(1)}, bf16[64,1152]{1,0:T(8,128)(2,1)S(1)}, u32[]{:S(2)}, u32[]{:S(2)}) collective-permute-start(bf16[64,1152]{1,0:T(8,128)(2,1)S(1)} %collective-permute-done.refs_0_), channel_id=1, source_target_pairs={{0,2},{1,3},{2,0},{3,1},{4,6},{5,7},{6,4},{7,5},{8,10},{9,11},{10,... | collective-permute-start | bytes 442376 | tf_op jit(solution)/shard_map/ppermute | solution.py:222
  15.4 3.4 %collective-permute-done.4.refs_6_ = bf16[64,1152]{1,0:T(8,128)(2,1)S(1)} collective-permute-done((bf16[64,1152]{1,0:T(8,128)(2,1)S(1)}, bf16[64,1152]{1,0:T(8,128)(2,1)S(1)}, u32[]{:S(2)}, u32[]{:S(2)}) %collective-permute-start.4) | collective-permute-done | bytes 147488 | tf_op jit(solution)/shard_map/ppermute | solution.py:222
  18.9 1.3 %collective-permute-start.12 = (bf16[64,1152]{1,0:T(8,128)(2,1)S(1)}, bf16[64,1152]{1,0:T(8,128)(2,1)S(1)}, u32[]{:S(2)}, u32[]{:S(2)}) collective-permute-start(bf16[64,1152]{1,0:T(8,128)(2,1)S(1)} %collective-permute-done.2.refs_1_.refs_0_), channel_id=1, source_target_pairs={{0,2},{1,3},{2,0},{3,1},{4,6},{5,7},{6,4},{7,5},{8,10},{9,11},{10,... | collective-permute-start | bytes 442376 | tf_op jit(solution)/shard_map/ppermute | solution.py:222
  20.1 1.1 %collective-permute-done.5.refs_3_ = bf16[64,1152]{1,0:T(8,128)(2,1)S(1)} collective-permute-done((bf16[64,1152]{1,0:T(8,128)(2,1)S(1)}, bf16[64,1152]{1,0:T(8,128)(2,1)S(1)}, u32[]{:S(2)}, u32[]{:S(2)}) %collective-permute-start.5) | collective-permute-done | bytes 147488 | tf_op jit(solution)/shard_map/ppermute | solution.py:222
  21.3 2.7 %expert.3 = (f32[128,1152]{1,0:T(8,128)S(1)}, bf16[64,1152]{1,0:T(8,128)(2,1)S(1)}, bf16[64,1152]{1,0:T(8,128)(2,1)S(1)}, bf16[1024,128]{1,0:T(8,128)(2,1)S(1)},...) custom-call(bf16[64,1152]{1,0:T(8,128)(2,1)S(1)} %get-tuple-element., ...), custom_call_target="tpu_custom_call", output_to_operand_aliasing={{3}: (4, {}), {4}: (5, {}), {5}: (6, {})} | custom-call | bytes 10000 | tf_op jit(solution)/shard_map/expert/pallas_call | solution.py:201
  25.7 0.9 %collective-permute-start.19 = (bf16[64,1152]{1,0:T(8,128)(2,1)S(1)}, bf16[64,1152]{1,0:T(8,128)(2,1)S(1)}, u32[]{:S(2)}, u32[]{:S(2)}) collective-permute-start(bf16[64,1152]{1,0:T(8,128)(2,1)S(1)} %get-tuple-element.106), channel_id=1, source_target_pairs={{0,2},{1,3},{2,0},{3,1},{4,6},{5,7},{6,4},{7,5},{8,10},{9,11},{10,... | collective-permute-start | bytes 442376 | tf_op jit(solution)/shard_map/ppermute | solution.py:222
  26.5 2.7 %expert.4 = (f32[128,1152]{1,0:T(8,128)S(1)}, bf16[64,1152]{1,0:T(8,128)(2,1)S(1)}, bf16[64,1152]{1,0:T(8,128)(2,1)S(1)}, bf16[1024,128]{1,0:T(8,128)(2,1)S(1)},...) custom-call(bf16[64,1152]{1,0:T(8,128)(2,1)S(1)} %collective-permute, ...), custom_call_target="tpu_custom_call", output_to_operand_aliasing={{3}: (4, {}), {4}: (5, {}), {5}: (6, {})} | custom-call | bytes 10000 | tf_op jit(solution)/shard_map/expert/pallas_call | solution.py:201
  30.3 1.4 %collective-permute-done.19.refs_1_ = bf16[64,1152]{1,0:T(8,128)(2,1)S(1)} collective-permute-done((bf16[64,1152]{1,0:T(8,128)(2,1)S(1)}, bf16[64,1152]{1,0:T(8,128)(2,1)S(1)}, u32[]{:S(2)}, u32[]{:S(2)}) %collective-permute-start.19) | collective-permute-done | bytes 147488 | tf_op jit(solution)/shard_map/ppermute | solution.py:222
  32.4 1.1 %collective-permute-start.24 = (bf16[64,1152]{1,0:T(8,128)(2,1)S(1)}, bf16[64,1152]{1,0:T(8,128)(2,1)S(1)}, u32[]{:S(2)}, u32[]{:S(2)}) collective-permute-start(bf16[64,1152]{1,0:T(8,128)(2,1)S(1)} %get-tuple-element.123), channel_id=1, source_target_pairs={{0,2},{1,3},{2,0},{3,1},{4,6},{5,7},{6,4},{7,5},{8,10},{9,11},{10,... | collective-permute-start | bytes 442376 | tf_op jit(solution)/shard_map/ppermute | solution.py:222
  33.5 2.3 %collective-permute-start.25 = (bf16[64,1152]{1,0:T(8,128)(2,1)S(1)}, bf16[64,1152]{1,0:T(8,128)(2,1)S(1)}, u32[]{:S(2)}, u32[]{:S(2)}) collective-permute-start(bf16[64,1152]{1,0:T(8,128)(2,1)S(1)} %get-tuple-element.124), channel_id=1, source_target_pairs={{0,8},{1,9},{2,10},{3,11},{4,12},{5,13},{6,14},{7,15},{8,0},{9,1},... | collective-permute-start | bytes 442376 | tf_op jit(solution)/shard_map/ppermute | solution.py:222
  35.8 4.9 %expert.5 = (f32[128,1152]{1,0:T(8,128)S(1)}, f32[128,1152]{1,0:T(8,128)S(1)}, bf16[64,1152]{1,0:T(8,128)(2,1)S(1)}, bf16[64,1152]{1,0:T(8,128)(2,1)S(1)}, bf16[...) custom-call(bf16[64,1152]{1,0:T(8,128)(2,1)S(1)} %collective-permute, ...), custom_call_target="tpu_custom_call", output_to_operand_aliasing={{6}: (8, {}), {7}: (9, {}), {8}: (10, {})} | custom-call | bytes 10000 | tf_op jit(solution)/shard_map/expert/pallas_call | solution.py:201
  41.3 1.7 %collective-permute-done.25.refs_2_.refs_4_ = bf16[64,1152]{1,0:T(8,128)(2,1)S(1)} collective-permute-done((bf16[64,1152]{1,0:T(8,128)(2,1)S(1)}, bf16[64,1152]{1,0:T(8,128)(2,1)S(1)}, u32[]{:S(2)}, u32[]{:S(2)}) %collective-permute-start.25) | collective-permute-done | bytes 147488 | tf_op jit(solution)/shard_map/ppermute | solution.py:222
  43.1 1.1 %collective-permute-start.26 = (bf16[64,1152]{1,0:T(8,128)(2,1)S(1)}, bf16[64,1152]{1,0:T(8,128)(2,1)S(1)}, u32[]{:S(2)}, u32[]{:S(2)}) collective-permute-start(bf16[64,1152]{1,0:T(8,128)(2,1)S(1)} %get-tuple-element.132), channel_id=1, source_target_pairs={{0,2},{1,3},{2,0},{3,1},{4,6},{5,7},{6,4},{7,5},{8,10},{9,11},{10,... | collective-permute-start | bytes 442376 | tf_op jit(solution)/shard_map/ppermute | solution.py:222
  44.8 3.4 %collective-permute-start.27 = (bf16[64,1152]{1,0:T(8,128)(2,1)S(1)}, bf16[64,1152]{1,0:T(8,128)(2,1)S(1)}, u32[]{:S(2)}, u32[]{:S(2)}) collective-permute-start(bf16[64,1152]{1,0:T(8,128)(2,1)S(1)} %get-tuple-element.140), channel_id=1, source_target_pairs={{0,12},{1,13},{2,14},{3,15},{4,8},{5,9},{6,10},{7,11},{8,4},{9,5},... | collective-permute-start | bytes 442376 | tf_op jit(solution)/shard_map/ppermute | solution.py:222
  48.7 1.5 %collective-permute-start.29 = (bf16[64,1152]{1,0:T(8,128)(2,1)S(1)}, bf16[64,1152]{1,0:T(8,128)(2,1)S(1)}, u32[]{:S(2)}, u32[]{:S(2)}) collective-permute-start(bf16[64,1152]{1,0:T(8,128)(2,1)S(1)} %get-tuple-element.142), channel_id=1, source_target_pairs={{0,2},{1,3},{2,0},{3,1},{4,6},{5,7},{6,4},{7,5},{8,10},{9,11},{10,... | collective-permute-start | bytes 442376 | tf_op jit(solution)/shard_map/ppermute | solution.py:222
  50.1 1.4 %collective-permute-start.28 = (bf16[64,1152]{1,0:T(8,128)(2,1)S(1)}, bf16[64,1152]{1,0:T(8,128)(2,1)S(1)}, u32[]{:S(2)}, u32[]{:S(2)}) collective-permute-start(bf16[64,1152]{1,0:T(8,128)(2,1)S(1)} %get-tuple-element.141), channel_id=1, source_target_pairs={{0,4},{1,5},{2,6},{3,7},{4,0},{5,1},{6,2},{7,3},{8,12},{9,13},{10,... | collective-permute-start | bytes 442376 | tf_op jit(solution)/shard_map/ppermute | solution.py:222
  51.5 1.0 %collective-permute-done.27.refs_1_ = bf16[64,1152]{1,0:T(8,128)(2,1)S(1)} collective-permute-done((bf16[64,1152]{1,0:T(8,128)(2,1)S(1)}, bf16[64,1152]{1,0:T(8,128)(2,1)S(1)}, u32[]{:S(2)}, u32[]{:S(2)}) %collective-permute-start.27) | collective-permute-done | bytes 147488 | tf_op jit(solution)/shard_map/ppermute | solution.py:222
  52.5 1.4 %collective-permute-done.29.refs_3_ = bf16[64,1152]{1,0:T(8,128)(2,1)S(1)} collective-permute-done((bf16[64,1152]{1,0:T(8,128)(2,1)S(1)}, bf16[64,1152]{1,0:T(8,128)(2,1)S(1)}, u32[]{:S(2)}, u32[]{:S(2)}) %collective-permute-start.29) | collective-permute-done | bytes 147488 | tf_op jit(solution)/shard_map/ppermute | solution.py:222
  53.9 1.7 %collective-permute-done.28.refs_2_ = bf16[64,1152]{1,0:T(8,128)(2,1)S(1)} collective-permute-done((bf16[64,1152]{1,0:T(8,128)(2,1)S(1)}, bf16[64,1152]{1,0:T(8,128)(2,1)S(1)}, u32[]{:S(2)}, u32[]{:S(2)}) %collective-permute-start.28) | collective-permute-done | bytes 147488 | tf_op jit(solution)/shard_map/ppermute | solution.py:222
  (53 shorter events, 7.2 us)
Async XLA Ops:
  0.9 11.9 %collective-permute-start.1 = (bf16[64,1152]{1,0:T(8,128)(2,1)S(1)}, bf16[64,1152]{1,0:T(8,128)(2,1)S(1)}, u32[]{:S(2)}, u32[]{:S(2)}) collective-permute-start(bf16[64,1152]{1,0:T(8,128)(2,1)S(1)} %pack.1.refs_3_.refs_4_), channel_id=1, source_target_pairs={{0,8},{1,9},{2,10},{3,11},{4,12},{5,13},{6,14},{7,15},{8,0},{9,1},... | collective-permute-start | bytes 442376 | tf_op jit(solution)/shard_map/ppermute | solution.py:222
  5.0 10.4 %collective-permute-start.3 = (bf16[64,1152]{1,0:T(8,128)(2,1)S(1)}, bf16[64,1152]{1,0:T(8,128)(2,1)S(1)}, u32[]{:S(2)}, u32[]{:S(2)}) collective-permute-start(bf16[64,1152]{1,0:T(8,128)(2,1)S(1)} %pack.1.refs_3_.refs_4_), channel_id=1, source_target_pairs={{0,2},{1,3},{2,0},{3,1},{4,6},{5,7},{6,4},{7,5},{8,10},{9,11},{10,... | collective-permute-start | bytes 442376 | tf_op jit(solution)/shard_map/ppermute | solution.py:222
  6.6 7.7 %collective-permute-start = (bf16[64,1152]{1,0:T(8,128)(2,1)S(1)}, bf16[64,1152]{1,0:T(8,128)(2,1)S(1)}, u32[]{:S(2)}, u32[]{:S(2)}) collective-permute-start(bf16[64,1152]{1,0:T(8,128)(2,1)S(1)} %pack.1.refs_3_.refs_4_), channel_id=1, source_target_pairs={{0,4},{1,5},{2,6},{3,7},{4,0},{5,1},{6,2},{7,3},{8,12},{9,13},{10,... | collective-permute-start | bytes 442376 | tf_op jit(solution)/shard_map/ppermute | solution.py:222
  12.9 5.9 %collective-permute-start.4 = (bf16[64,1152]{1,0:T(8,128)(2,1)S(1)}, bf16[64,1152]{1,0:T(8,128)(2,1)S(1)}, u32[]{:S(2)}, u32[]{:S(2)}) collective-permute-start(bf16[64,1152]{1,0:T(8,128)(2,1)S(1)} %get-tuple-element.77.refs_0_), channel_id=1, source_target_pairs={{0,2},{1,3},{2,0},{3,1},{4,6},{5,7},{6,4},{7,5},{8,10},{9,11},{10,... | collective-permute-start | bytes 442376 | tf_op jit(solution)/shard_map/ppermute | solution.py:222
  13.7 5.1 %collective-permute-start.2 = (bf16[64,1152]{1,0:T(8,128)(2,1)S(1)}, bf16[64,1152]{1,0:T(8,128)(2,1)S(1)}, u32[]{:S(2)}, u32[]{:S(2)}) collective-permute-start(bf16[64,1152]{1,0:T(8,128)(2,1)S(1)} %get-tuple-element.77.refs_0_), channel_id=1, source_target_pairs={{0,4},{1,5},{2,6},{3,7},{4,0},{5,1},{6,2},{7,3},{8,12},{9,13},{10,... | collective-permute-start | bytes 442376 | tf_op jit(solution)/shard_map/ppermute | solution.py:222
  14.3 7.0 %collective-permute-start.10 = (bf16[64,1152]{1,0:T(8,128)(2,1)S(1)}, bf16[64,1152]{1,0:T(8,128)(2,1)S(1)}, u32[]{:S(2)}, u32[]{:S(2)}) collective-permute-start(bf16[64,1152]{1,0:T(8,128)(2,1)S(1)} %get-tuple-element.77.refs_0_), channel_id=1, source_target_pairs={{0,1},{1,0},{2,3},{3,2},{4,5},{5,4},{6,7},{7,6},{8,9},{9,8},{10,11... | collective-permute-start | bytes 442376 | tf_op jit(solution)/shard_map/ppermute | solution.py:222
  14.3 7.0 %collective-permute-start.5 = (bf16[64,1152]{1,0:T(8,128)(2,1)S(1)}, bf16[64,1152]{1,0:T(8,128)(2,1)S(1)}, u32[]{:S(2)}, u32[]{:S(2)}) collective-permute-start(bf16[64,1152]{1,0:T(8,128)(2,1)S(1)} %collective-permute-done.refs_0_), channel_id=1, source_target_pairs={{0,2},{1,3},{2,0},{3,1},{4,6},{5,7},{6,4},{7,5},{8,10},{9,11},{10,... | collective-permute-start | bytes 442376 | tf_op jit(solution)/shard_map/ppermute | solution.py:222
  18.9 2.4 %collective-permute-start.11 = (bf16[64,1152]{1,0:T(8,128)(2,1)S(1)}, bf16[64,1152]{1,0:T(8,128)(2,1)S(1)}, u32[]{:S(2)}, u32[]{:S(2)}) collective-permute-start(bf16[64,1152]{1,0:T(8,128)(2,1)S(1)} %get-tuple-element.85.refs_1_), channel_id=1, source_target_pairs={{0,1},{1,0},{2,3},{3,2},{4,5},{5,4},{6,7},{7,6},{8,9},{9,8},{10,11... | collective-permute-start | bytes 442376 | tf_op jit(solution)/shard_map/ppermute | solution.py:222
  18.9 6.3 %collective-permute-start.12 = (bf16[64,1152]{1,0:T(8,128)(2,1)S(1)}, bf16[64,1152]{1,0:T(8,128)(2,1)S(1)}, u32[]{:S(2)}, u32[]{:S(2)}) collective-permute-start(bf16[64,1152]{1,0:T(8,128)(2,1)S(1)} %collective-permute-done.2.refs_1_.refs_0_), channel_id=1, source_target_pairs={{0,2},{1,3},{2,0},{3,1},{4,6},{5,7},{6,4},{7,5},{8,10},{9,11},{10,... | collective-permute-start | bytes 442376 | tf_op jit(solution)/shard_map/ppermute | solution.py:222
  25.7 6.1 %collective-permute-start.19 = (bf16[64,1152]{1,0:T(8,128)(2,1)S(1)}, bf16[64,1152]{1,0:T(8,128)(2,1)S(1)}, u32[]{:S(2)}, u32[]{:S(2)}) collective-permute-start(bf16[64,1152]{1,0:T(8,128)(2,1)S(1)} %get-tuple-element.106), channel_id=1, source_target_pairs={{0,2},{1,3},{2,0},{3,1},{4,6},{5,7},{6,4},{7,5},{8,10},{9,11},{10,... | collective-permute-start | bytes 442376 | tf_op jit(solution)/shard_map/ppermute | solution.py:222
  29.2 2.5 %collective-permute-start.17 = (bf16[64,1152]{1,0:T(8,128)(2,1)S(1)}, bf16[64,1152]{1,0:T(8,128)(2,1)S(1)}, u32[]{:S(2)}, u32[]{:S(2)}) collective-permute-start(bf16[64,1152]{1,0:T(8,128)(2,1)S(1)} %get-tuple-element.103), channel_id=1, source_target_pairs={{0,1},{1,0},{2,3},{3,2},{4,5},{5,4},{6,7},{7,6},{8,9},{9,8},{10,11... | collective-permute-start | bytes 442376 | tf_op jit(solution)/shard_map/ppermute | solution.py:222
  29.5 2.8 %collective-permute-start.18 = (bf16[64,1152]{1,0:T(8,128)(2,1)S(1)}, bf16[64,1152]{1,0:T(8,128)(2,1)S(1)}, u32[]{:S(2)}, u32[]{:S(2)}) collective-permute-start(bf16[64,1152]{1,0:T(8,128)(2,1)S(1)} %get-tuple-element.104), channel_id=1, source_target_pairs={{0,1},{1,0},{2,3},{3,2},{4,5},{5,4},{6,7},{7,6},{8,9},{9,8},{10,11... | collective-permute-start | bytes 442376 | tf_op jit(solution)/shard_map/ppermute | solution.py:222
  29.8 3.7 %collective-permute-start.8 = (bf16[64,1152]{1,0:T(8,128)(2,1)S(1)}, bf16[64,1152]{1,0:T(8,128)(2,1)S(1)}, u32[]{:S(2)}, u32[]{:S(2)}) collective-permute-start(bf16[64,1152]{1,0:T(8,128)(2,1)S(1)} %pack.1.refs_3_.refs_4_), channel_id=1, source_target_pairs={{0,1},{1,0},{2,3},{3,2},{4,5},{5,4},{6,7},{7,6},{8,9},{9,8},{10,11... | collective-permute-start | bytes 442376 | tf_op jit(solution)/shard_map/ppermute | solution.py:222
  30.0 5.7 %collective-permute-start.9 = (bf16[64,1152]{1,0:T(8,128)(2,1)S(1)}, bf16[64,1152]{1,0:T(8,128)(2,1)S(1)}, u32[]{:S(2)}, u32[]{:S(2)}) collective-permute-start(bf16[64,1152]{1,0:T(8,128)(2,1)S(1)} %collective-permute-done.3.refs_2_.refs_5_), channel_id=1, source_target_pairs={{0,1},{1,0},{2,3},{3,2},{4,5},{5,4},{6,7},{7,6},{8,9},{9,8},{10,11... | collective-permute-start | bytes 442376 | tf_op jit(solution)/shard_map/ppermute | solution.py:222
  31.8 4.0 %collective-permute-start.6 = (bf16[64,1152]{1,0:T(8,128)(2,1)S(1)}, bf16[64,1152]{1,0:T(8,128)(2,1)S(1)}, u32[]{:S(2)}, u32[]{:S(2)}) collective-permute-start(bf16[64,1152]{1,0:T(8,128)(2,1)S(1)} %collective-permute-done.refs_0_), channel_id=1, source_target_pairs={{0,1},{1,0},{2,3},{3,2},{4,5},{5,4},{6,7},{7,6},{8,9},{9,8},{10,11... | collective-permute-start | bytes 442376 | tf_op jit(solution)/shard_map/ppermute | solution.py:222
  31.8 4.0 %collective-permute-start.7 = (bf16[64,1152]{1,0:T(8,128)(2,1)S(1)}, bf16[64,1152]{1,0:T(8,128)(2,1)S(1)}, u32[]{:S(2)}, u32[]{:S(2)}) collective-permute-start(bf16[64,1152]{1,0:T(8,128)(2,1)S(1)} %get-tuple-element.84.refs_1_), channel_id=1, source_target_pairs={{0,1},{1,0},{2,3},{3,2},{4,5},{5,4},{6,7},{7,6},{8,9},{9,8},{10,11... | collective-permute-start | bytes 442376 | tf_op jit(solution)/shard_map/ppermute | solution.py:222
  32.4 8.9 %collective-permute-start.24 = (bf16[64,1152]{1,0:T(8,128)(2,1)S(1)}, bf16[64,1152]{1,0:T(8,128)(2,1)S(1)}, u32[]{:S(2)}, u32[]{:S(2)}) collective-permute-start(bf16[64,1152]{1,0:T(8,128)(2,1)S(1)} %get-tuple-element.123), channel_id=1, source_target_pairs={{0,2},{1,3},{2,0},{3,1},{4,6},{5,7},{6,4},{7,5},{8,10},{9,11},{10,... | collective-permute-start | bytes 442376 | tf_op jit(solution)/shard_map/ppermute | solution.py:222
  33.5 9.5 %collective-permute-start.25 = (bf16[64,1152]{1,0:T(8,128)(2,1)S(1)}, bf16[64,1152]{1,0:T(8,128)(2,1)S(1)}, u32[]{:S(2)}, u32[]{:S(2)}) collective-permute-start(bf16[64,1152]{1,0:T(8,128)(2,1)S(1)} %get-tuple-element.124), channel_id=1, source_target_pairs={{0,8},{1,9},{2,10},{3,11},{4,12},{5,13},{6,14},{7,15},{8,0},{9,1},... | collective-permute-start | bytes 442376 | tf_op jit(solution)/shard_map/ppermute | solution.py:222
  43.1 5.4 %collective-permute-start.26 = (bf16[64,1152]{1,0:T(8,128)(2,1)S(1)}, bf16[64,1152]{1,0:T(8,128)(2,1)S(1)}, u32[]{:S(2)}, u32[]{:S(2)}) collective-permute-start(bf16[64,1152]{1,0:T(8,128)(2,1)S(1)} %get-tuple-element.132), channel_id=1, source_target_pairs={{0,2},{1,3},{2,0},{3,1},{4,6},{5,7},{6,4},{7,5},{8,10},{9,11},{10,... | collective-permute-start | bytes 442376 | tf_op jit(solution)/shard_map/ppermute | solution.py:222
  44.2 4.3 %collective-permute-start.20 = (bf16[64,1152]{1,0:T(8,128)(2,1)S(1)}, bf16[64,1152]{1,0:T(8,128)(2,1)S(1)}, u32[]{:S(2)}, u32[]{:S(2)}) collective-permute-start(bf16[64,1152]{1,0:T(8,128)(2,1)S(1)} %get-tuple-element.117), channel_id=1, source_target_pairs={{0,1},{1,0},{2,3},{3,2},{4,5},{5,4},{6,7},{7,6},{8,9},{9,8},{10,11... | collective-permute-start | bytes 442376 | tf_op jit(solution)/shard_map/ppermute | solution.py:222
  44.3 4.3 %collective-permute-start.21 = (bf16[64,1152]{1,0:T(8,128)(2,1)S(1)}, bf16[64,1152]{1,0:T(8,128)(2,1)S(1)}, u32[]{:S(2)}, u32[]{:S(2)}) collective-permute-start(bf16[64,1152]{1,0:T(8,128)(2,1)S(1)} %get-tuple-element.118), channel_id=1, source_target_pairs={{0,1},{1,0},{2,3},{3,2},{4,5},{5,4},{6,7},{7,6},{8,9},{9,8},{10,11... | collective-permute-start | bytes 442376 | tf_op jit(solution)/shard_map/ppermute | solution.py:222
  44.8 7.7 %collective-permute-start.27 = (bf16[64,1152]{1,0:T(8,128)(2,1)S(1)}, bf16[64,1152]{1,0:T(8,128)(2,1)S(1)}, u32[]{:S(2)}, u32[]{:S(2)}) collective-permute-start(bf16[64,1152]{1,0:T(8,128)(2,1)S(1)} %get-tuple-element.140), channel_id=1, source_target_pairs={{0,12},{1,13},{2,14},{3,15},{4,8},{5,9},{6,10},{7,11},{8,4},{9,5},... | collective-permute-start | bytes 442376 | tf_op jit(solution)/shard_map/ppermute | solution.py:222
  48.7 5.2 %collective-permute-start.29 = (bf16[64,1152]{1,0:T(8,128)(2,1)S(1)}, bf16[64,1152]{1,0:T(8,128)(2,1)S(1)}, u32[]{:S(2)}, u32[]{:S(2)}) collective-permute-start(bf16[64,1152]{1,0:T(8,128)(2,1)S(1)} %get-tuple-element.142), channel_id=1, source_target_pairs={{0,2},{1,3},{2,0},{3,1},{4,6},{5,7},{6,4},{7,5},{8,10},{9,11},{10,... | collective-permute-start | bytes 442376 | tf_op jit(solution)/shard_map/ppermute | solution.py:222
  50.1 5.4 %collective-permute-start.28 = (bf16[64,1152]{1,0:T(8,128)(2,1)S(1)}, bf16[64,1152]{1,0:T(8,128)(2,1)S(1)}, u32[]{:S(2)}, u32[]{:S(2)}) collective-permute-start(bf16[64,1152]{1,0:T(8,128)(2,1)S(1)} %get-tuple-element.141), channel_id=1, source_target_pairs={{0,4},{1,5},{2,6},{3,7},{4,0},{5,1},{6,2},{7,3},{8,12},{9,13},{10,... | collective-permute-start | bytes 442376 | tf_op jit(solution)/shard_map/ppermute | solution.py:222
  (6 other events, 11.0 us)

commit v17 on v16

--- a/solution.py
+++ b/solution.py
@@ -293,21 +293,21 @@
         z_2, z_1, y_0 = swap(mine, 8), swap(mine, 4), swap(mine, 2)
         block = {0: mine, 2: tie(z_2), 1: z_1}
         block[3] = swap(block[2], 4)
-        other[0] = y_0
-        gather(2, [block[1], block[3], y_0])
+        other[0] = tie(y_0)
+        compute(0)
+        gather(2, [block[1], block[3]])
         gather(1)
+        reduce_core(0)
         compute(2)
         gather(3)
         reduce_core(2)
-        compute(3)
-        z_2 = reduce_y(2)
+        compute(3, 1)
+        z_2 = reduce_y(2, [y_came[0]])
         reduce_core(3)
-        compute(1, 0)
+        reduce_core(1)
         z_3 = reduce_y(3, [z_2])
-        reduce_core(1)
         z_1 = reduce_y(1)
-        reduce_core(0)
-        return fold_keep[0], z_3, z_1, y_came[0], z_2
+        return fold_keep[0], y_came[0], z_2, z_3, z_1
 
     packet = call(
         pack_kernel,

time: 56.5 us -> 57.7 us (1.021)
  waiting for transfers between devices: 13.1 us -> 16.9 us
  starting transfers between devices: 26 us -> 23.3 us
    ppermute x30, waiting for transfers between devices: 13.1 us -> 16.9 us  [swap(): return lax.ppermute(x, 'exp', [(i, i ^ bits) for i in range(n_dev)])]
    ppermute x30, starting transfers between devices: 26 us -> 23.3 us  [swap(): return lax.ppermute(x, 'exp', [(i, i ^ bits) for i in range(n_dev)])]
    pallas_call x16 -> x17, Pallas kernels: 16.3 us -> 16.3 us  [call(): pl.pallas_call(body_with_chain if reads_chain else body, out_shape=list(o...]
  transfers between devices with their start and end apart: 30 -> 30, of which waited for: 12 -> 7; matrix products, arithmetic and copies ran while one was open for 0% -> 0% of each run, Pallas kernels for 27% -> 27%
where the time goes in v17:
time: 57.7 us; the launch traced here: 57.5 us
  starting transfers between devices  23.3 us (40%)
  Pallas kernels  17 us (29%)
  waiting for transfers between devices  16.9 us (29%)
    ppermute x30, starting transfers between devices, swap(): return lax.ppermute(x, 'exp', [(i, i ^ bits) for i in range(n_dev)])  23.3 us
    ppermute x30, waiting for transfers between devices, swap(): return lax.ppermute(x, 'exp', [(i, i ^ bits) for i in range(n_dev)])  16.9 us
    pallas_call x17, Pallas kernels, call(): pl.pallas_call(body_with_chain if reads_chain else body, out_shape=list(o...  16.3 us
  transfers between devices with their start and end apart: 30, of which 7 were waited for; matrix products, arithmetic and copies ran while one was open for 0% of the time, Pallas kernels for 27%

profile of v17, /device:TPU:0, one launch (start us, length us, event | category | flops | bytes accessed | tf_op | source)
XLA Modules:
  0.0 57.5 jit_solution(17512821750378642014)
XLA Ops:
  0.0 0.9 %pack.1.refs_3_.refs_0_ = bf16[64,1152]{1,0:T(8,128)(2,1)S(1)} custom-call(s32[8,64]{1,0:T(8,128)} %bitcast.2, bf16[64,1024]{1,0:T(8,128)(2,1)} %refs_1_.2), custom_call_target="tpu_custom_call" | custom-call | bytes 10000 | tf_op jit(solution)/shard_map/pack/pallas_call | solution.py:201
  0.9 4.1 %collective-permute-start = (bf16[64,1152]{1,0:T(8,128)(2,1)S(1)}, bf16[64,1152]{1,0:T(8,128)(2,1)S(1)}, u32[]{:S(2)}, u32[]{:S(2)}) collective-permute-start(bf16[64,1152]{1,0:T(8,128)(2,1)S(1)} %pack.1.refs_3_.refs_0_), channel_id=1, source_target_pairs={{0,8},{1,9},{2,10},{3,11},{4,12},{5,13},{6,14},{7,15},{8,0},{9,1},... | collective-permute-start | bytes 442376 | tf_op jit(solution)/shard_map/ppermute | solution.py:222
  5.0 1.5 %collective-permute-start.1 = (bf16[64,1152]{1,0:T(8,128)(2,1)S(1)}, bf16[64,1152]{1,0:T(8,128)(2,1)S(1)}, u32[]{:S(2)}, u32[]{:S(2)}) collective-permute-start(bf16[64,1152]{1,0:T(8,128)(2,1)S(1)} %pack.1.refs_3_.refs_0_), channel_id=1, source_target_pairs={{0,2},{1,3},{2,0},{3,1},{4,6},{5,7},{6,4},{7,5},{8,10},{9,11},{10,... | collective-permute-start | bytes 442376 | tf_op jit(solution)/shard_map/ppermute | solution.py:222
  6.6 1.6 %collective-permute-start.6 = (bf16[64,1152]{1,0:T(8,128)(2,1)S(1)}, bf16[64,1152]{1,0:T(8,128)(2,1)S(1)}, u32[]{:S(2)}, u32[]{:S(2)}) collective-permute-start(bf16[64,1152]{1,0:T(8,128)(2,1)S(1)} %pack.1.refs_3_.refs_0_), channel_id=1, source_target_pairs={{0,4},{1,5},{2,6},{3,7},{4,0},{5,1},{6,2},{7,3},{8,12},{9,13},{10,... | collective-permute-start | bytes 442376 | tf_op jit(solution)/shard_map/ppermute | solution.py:222
  8.1 4.7 %load.1 = (bf16[1024,128]{1,0:T(8,128)(2,1)S(1)}, bf16[2,1024,2048]{2,1,0:T(8,128)(2,1)S(1)}, bf16[2,1024,1024]{2,1,0:T(8,128)(2,1)S(1)}) custom-call(bf16[2,1024]{1,0:T(2,128)(2,1)} %bitcast.3, bf16[2,1024,2048]{2,1,0:T(8,128)(2,1)} %refs_1_.3, bf16[2,1024,1024]{2,1,0:T(8,128)(2,1)} %refs_2_.1, bf16[64,1152]{1,0:T(8,128)(2,1)S(1)} %pack.1.refs_3_.refs_0_), custom_call_target="tpu_custom_call" | custom-call | bytes 10000 | tf_op jit(solution)/shard_map/load/pallas_call | solution.py:201
  14.5 1.6 %collective-permute-start.9 = (bf16[64,1152]{1,0:T(8,128)(2,1)S(1)}, bf16[64,1152]{1,0:T(8,128)(2,1)S(1)}, u32[]{:S(2)}, u32[]{:S(2)}) collective-permute-start(bf16[64,1152]{1,0:T(8,128)(2,1)S(1)} %collective-permute-done.6.refs_0_.refs_4_), channel_id=1, source_target_pairs={{0,2},{1,3},{2,0},{3,1},{4,6},{5,7},{6,4},{7,5},{8,10},{9,11},{10,... | collective-permute-start | bytes 442376 | tf_op jit(solution)/shard_map/ppermute | solution.py:222
  16.0 2.7 %expert.3 = (f32[128,1152]{1,0:T(8,128)S(1)}, bf16[64,1152]{1,0:T(8,128)(2,1)S(1)}, bf16[64,1152]{1,0:T(8,128)(2,1)S(1)}, bf16[1024,128]{1,0:T(8,128)(2,1)S(1)},...) custom-call(bf16[64,1152]{1,0:T(8,128)(2,1)S(1)} %pack.1.refs_3_.ref, ...), custom_call_target="tpu_custom_call", output_to_operand_aliasing={{3}: (4, {}), {4}: (5, {}), {5}: (6, {})} | custom-call | bytes 10000 | tf_op jit(solution)/shard_map/expert/pallas_call | solution.py:201
  19.0 1.2 %collective-permute-done.8.refs_5_ = bf16[64,1152]{1,0:T(8,128)(2,1)S(1)} collective-permute-done((bf16[64,1152]{1,0:T(8,128)(2,1)S(1)}, bf16[64,1152]{1,0:T(8,128)(2,1)S(1)}, u32[]{:S(2)}, u32[]{:S(2)}) %collective-permute-start.8) | collective-permute-done | bytes 147488 | tf_op jit(solution)/shard_map/ppermute | solution.py:222
  20.7 1.8 %collective-permute-done.9.refs_3_ = bf16[64,1152]{1,0:T(8,128)(2,1)S(1)} collective-permute-done((bf16[64,1152]{1,0:T(8,128)(2,1)S(1)}, bf16[64,1152]{1,0:T(8,128)(2,1)S(1)}, u32[]{:S(2)}, u32[]{:S(2)}) %collective-permute-start.9) | collective-permute-done | bytes 147488 | tf_op jit(solution)/shard_map/ppermute | solution.py:222
  22.5 0.7 %collective-permute-start.15 = (bf16[64,1152]{1,0:T(8,128)(2,1)S(1)}, bf16[64,1152]{1,0:T(8,128)(2,1)S(1)}, u32[]{:S(2)}, u32[]{:S(2)}) collective-permute-start(bf16[64,1152]{1,0:T(8,128)(2,1)S(1)} %collective-permute-done.7.refs_1_.refs_0_), channel_id=1, source_target_pairs={{0,2},{1,3},{2,0},{3,1},{4,6},{5,7},{6,4},{7,5},{8,10},{9,11},{10,... | collective-permute-start | bytes 442376 | tf_op jit(solution)/shard_map/ppermute | solution.py:222
  23.2 2.7 %expert.4 = (f32[128,1152]{1,0:T(8,128)S(1)}, bf16[64,1152]{1,0:T(8,128)(2,1)S(1)}, bf16[64,1152]{1,0:T(8,128)(2,1)S(1)}, bf16[1024,128]{1,0:T(8,128)(2,1)S(1)},...) custom-call(bf16[64,1152]{1,0:T(8,128)(2,1)S(1)} %get-tuple-element., ...), custom_call_target="tpu_custom_call", output_to_operand_aliasing={{3}: (4, {}), {4}: (5, {}), {5}: (6, {})} | custom-call | bytes 10000 | tf_op jit(solution)/shard_map/expert/pallas_call | solution.py:201
  27.0 0.6 %collective-permute-done.15.refs_3_ = bf16[64,1152]{1,0:T(8,128)(2,1)S(1)} collective-permute-done((bf16[64,1152]{1,0:T(8,128)(2,1)S(1)}, bf16[64,1152]{1,0:T(8,128)(2,1)S(1)}, u32[]{:S(2)}, u32[]{:S(2)}) %collective-permute-start.15) | collective-permute-done | bytes 147488 | tf_op jit(solution)/shard_map/ppermute | solution.py:222
  28.1 0.8 %collective-permute-start.10 = (bf16[64,1152]{1,0:T(8,128)(2,1)S(1)}, bf16[64,1152]{1,0:T(8,128)(2,1)S(1)}, u32[]{:S(2)}, u32[]{:S(2)}) collective-permute-start(bf16[64,1152]{1,0:T(8,128)(2,1)S(1)} %get-tuple-element.102), channel_id=1, source_target_pairs={{0,2},{1,3},{2,0},{3,1},{4,6},{5,7},{6,4},{7,5},{8,10},{9,11},{10,... | collective-permute-start | bytes 442376 | tf_op jit(solution)/shard_map/ppermute | solution.py:222
  29.0 1.3 %collective-permute-start.16 = (bf16[64,1152]{1,0:T(8,128)(2,1)S(1)}, bf16[64,1152]{1,0:T(8,128)(2,1)S(1)}, u32[]{:S(2)}, u32[]{:S(2)}) collective-permute-start(bf16[64,1152]{1,0:T(8,128)(2,1)S(1)} %get-tuple-element.117), channel_id=1, source_target_pairs={{0,2},{1,3},{2,0},{3,1},{4,6},{5,7},{6,4},{7,5},{8,10},{9,11},{10,... | collective-permute-start | bytes 442376 | tf_op jit(solution)/shard_map/ppermute | solution.py:222
  30.3 4.9 %expert.5 = (f32[128,1152]{1,0:T(8,128)S(1)}, f32[128,1152]{1,0:T(8,128)S(1)}, bf16[64,1152]{1,0:T(8,128)(2,1)S(1)}, bf16[64,1152]{1,0:T(8,128)(2,1)S(1)}, bf16[...) custom-call(bf16[64,1152]{1,0:T(8,128)(2,1)S(1)} %collective-permute, ...), custom_call_target="tpu_custom_call", output_to_operand_aliasing={{6}: (8, {}), {7}: (9, {}), {8}: (10, {})} | custom-call | bytes 10000 | tf_op jit(solution)/shard_map/expert/pallas_call | solution.py:201
  36.4 0.8 %collective-permute-done.16.refs_1_ = bf16[64,1152]{1,0:T(8,128)(2,1)S(1)} collective-permute-done((bf16[64,1152]{1,0:T(8,128)(2,1)S(1)}, bf16[64,1152]{1,0:T(8,128)(2,1)S(1)}, u32[]{:S(2)}, u32[]{:S(2)}) %collective-permute-start.16) | collective-permute-done | bytes 147488 | tf_op jit(solution)/shard_map/ppermute | solution.py:222
  37.2 1.9 %collective-permute-start.21 = (bf16[64,1152]{1,0:T(8,128)(2,1)S(1)}, bf16[64,1152]{1,0:T(8,128)(2,1)S(1)}, u32[]{:S(2)}, u32[]{:S(2)}) collective-permute-start(bf16[64,1152]{1,0:T(8,128)(2,1)S(1)} %get-tuple-element.126), channel_id=1, source_target_pairs={{0,8},{1,9},{2,10},{3,11},{4,12},{5,13},{6,14},{7,15},{8,0},{9,1},... | collective-permute-start | bytes 442376 | tf_op jit(solution)/shard_map/ppermute | solution.py:222
  39.1 0.8 %collective-permute-start.24 = (bf16[64,1152]{1,0:T(8,128)(2,1)S(1)}, bf16[64,1152]{1,0:T(8,128)(2,1)S(1)}, u32[]{:S(2)}, u32[]{:S(2)}) collective-permute-start(bf16[64,1152]{1,0:T(8,128)(2,1)S(1)} %get-tuple-element.134), channel_id=1, source_target_pairs={{0,2},{1,3},{2,0},{3,1},{4,6},{5,7},{6,4},{7,5},{8,10},{9,11},{10,... | collective-permute-start | bytes 442376 | tf_op jit(solution)/shard_map/ppermute | solution.py:222
  40.0 1.3 %collective-permute-start.28 = (bf16[64,1152]{1,0:T(8,128)(2,1)S(1)}, bf16[64,1152]{1,0:T(8,128)(2,1)S(1)}, u32[]{:S(2)}, u32[]{:S(2)}) collective-permute-start(bf16[64,1152]{1,0:T(8,128)(2,1)S(1)} %get-tuple-element.146), channel_id=1, source_target_pairs={{0,2},{1,3},{2,0},{3,1},{4,6},{5,7},{6,4},{7,5},{8,10},{9,11},{10,... | collective-permute-start | bytes 442376 | tf_op jit(solution)/shard_map/ppermute | solution.py:222
  41.3 5.0 %collective-permute-done.21.refs_2_ = bf16[64,1152]{1,0:T(8,128)(2,1)S(1)} collective-permute-done((bf16[64,1152]{1,0:T(8,128)(2,1)S(1)}, bf16[64,1152]{1,0:T(8,128)(2,1)S(1)}, u32[]{:S(2)}, u32[]{:S(2)}) %collective-permute-start.21) | collective-permute-done | bytes 147488 | tf_op jit(solution)/shard_map/ppermute | solution.py:222
  46.4 2.8 %collective-permute-start.27 = (bf16[64,1152]{1,0:T(8,128)(2,1)S(1)}, bf16[64,1152]{1,0:T(8,128)(2,1)S(1)}, u32[]{:S(2)}, u32[]{:S(2)}) collective-permute-start(bf16[64,1152]{1,0:T(8,128)(2,1)S(1)} %get-tuple-element.144), channel_id=1, source_target_pairs={{0,12},{1,13},{2,14},{3,15},{4,8},{5,9},{6,10},{7,11},{8,4},{9,5},... | collective-permute-start | bytes 442376 | tf_op jit(solution)/shard_map/ppermute | solution.py:222
  49.3 5.8 %collective-permute-done.27.refs_3_ = bf16[64,1152]{1,0:T(8,128)(2,1)S(1)} collective-permute-done((bf16[64,1152]{1,0:T(8,128)(2,1)S(1)}, bf16[64,1152]{1,0:T(8,128)(2,1)S(1)}, u32[]{:S(2)}, u32[]{:S(2)}) %collective-permute-start.27) | collective-permute-done | bytes 147488 | tf_op jit(solution)/shard_map/ppermute | solution.py:222
  55.0 1.7 %collective-permute-done.29.refs_4_ = bf16[64,1152]{1,0:T(8,128)(2,1)S(1)} collective-permute-done((bf16[64,1152]{1,0:T(8,128)(2,1)S(1)}, bf16[64,1152]{1,0:T(8,128)(2,1)S(1)}, u32[]{:S(2)}, u32[]{:S(2)}) %collective-permute-start.29) | collective-permute-done | bytes 147488 | tf_op jit(solution)/shard_map/ppermute | solution.py:222
  56.7 0.8 %finish.1 = bf16[64,1024]{1,0:T(8,128)(2,1)} custom-call(f32[64,1152]{1,0:T(8,128)S(1)} %get-tuple-element.101.refs_0_, bf16[64,1152]{1,0:T(8,128)(2,1)S(1)} %collective-permute-done.10.refs_2_.refs_1_, bf16[64,1152]{1,0:T(8,128)(2,1)S(1)} %collective-permute-done.21.refs_2_, bf16[64,1152]{1,0:T(8,128)(2,1)S(1)} %collective-permute-done.27.refs_3_, ...), custom_call_target="tpu_custom_call" | custom-call | tf_op jit(solution)/shard_map/finish/pallas_call | solution.py:320
  (54 shorter events, 5.4 us)
Async XLA Ops:
  0.9 11.9 %collective-permute-start = (bf16[64,1152]{1,0:T(8,128)(2,1)S(1)}, bf16[64,1152]{1,0:T(8,128)(2,1)S(1)}, u32[]{:S(2)}, u32[]{:S(2)}) collective-permute-start(bf16[64,1152]{1,0:T(8,128)(2,1)S(1)} %pack.1.refs_3_.refs_0_), channel_id=1, source_target_pairs={{0,8},{1,9},{2,10},{3,11},{4,12},{5,13},{6,14},{7,15},{8,0},{9,1},... | collective-permute-start | bytes 442376 | tf_op jit(solution)/shard_map/ppermute | solution.py:222
  5.0 7.9 %collective-permute-start.1 = (bf16[64,1152]{1,0:T(8,128)(2,1)S(1)}, bf16[64,1152]{1,0:T(8,128)(2,1)S(1)}, u32[]{:S(2)}, u32[]{:S(2)}) collective-permute-start(bf16[64,1152]{1,0:T(8,128)(2,1)S(1)} %pack.1.refs_3_.refs_0_), channel_id=1, source_target_pairs={{0,2},{1,3},{2,0},{3,1},{4,6},{5,7},{6,4},{7,5},{8,10},{9,11},{10,... | collective-permute-start | bytes 442376 | tf_op jit(solution)/shard_map/ppermute | solution.py:222
  6.6 7.9 %collective-permute-start.6 = (bf16[64,1152]{1,0:T(8,128)(2,1)S(1)}, bf16[64,1152]{1,0:T(8,128)(2,1)S(1)}, u32[]{:S(2)}, u32[]{:S(2)}) collective-permute-start(bf16[64,1152]{1,0:T(8,128)(2,1)S(1)} %pack.1.refs_3_.refs_0_), channel_id=1, source_target_pairs={{0,4},{1,5},{2,6},{3,7},{4,0},{5,1},{6,2},{7,3},{8,12},{9,13},{10,... | collective-permute-start | bytes 442376 | tf_op jit(solution)/shard_map/ppermute | solution.py:222
  8.1 6.3 %collective-permute-start.2 = (bf16[64,1152]{1,0:T(8,128)(2,1)S(1)}, bf16[64,1152]{1,0:T(8,128)(2,1)S(1)}, u32[]{:S(2)}, u32[]{:S(2)}) collective-permute-start(bf16[64,1152]{1,0:T(8,128)(2,1)S(1)} %pack.1.refs_3_.refs_0_), channel_id=1, source_target_pairs={{0,1},{1,0},{2,3},{3,2},{4,5},{5,4},{6,7},{7,6},{8,9},{9,8},{10,11... | collective-permute-start | bytes 442376 | tf_op jit(solution)/shard_map/ppermute | solution.py:222
  12.9 3.1 %collective-permute-start.3 = (bf16[64,1152]{1,0:T(8,128)(2,1)S(1)}, bf16[64,1152]{1,0:T(8,128)(2,1)S(1)}, u32[]{:S(2)}, u32[]{:S(2)}) collective-permute-start(bf16[64,1152]{1,0:T(8,128)(2,1)S(1)} %get-tuple-element.84.refs_1_), channel_id=1, source_target_pairs={{0,1},{1,0},{2,3},{3,2},{4,5},{5,4},{6,7},{7,6},{8,9},{9,8},{10,11... | collective-permute-start | bytes 442376 | tf_op jit(solution)/shard_map/ppermute | solution.py:222
  13.5 6.7 %collective-permute-start.8 = (bf16[64,1152]{1,0:T(8,128)(2,1)S(1)}, bf16[64,1152]{1,0:T(8,128)(2,1)S(1)}, u32[]{:S(2)}, u32[]{:S(2)}) collective-permute-start(bf16[64,1152]{1,0:T(8,128)(2,1)S(1)} %get-tuple-element.91.refs_0_), channel_id=1, source_target_pairs={{0,2},{1,3},{2,0},{3,1},{4,6},{5,7},{6,4},{7,5},{8,10},{9,11},{10,... | collective-permute-start | bytes 442376 | tf_op jit(solution)/shard_map/ppermute | solution.py:222
  14.0 6.2 %collective-permute-start.7 = (bf16[64,1152]{1,0:T(8,128)(2,1)S(1)}, bf16[64,1152]{1,0:T(8,128)(2,1)S(1)}, u32[]{:S(2)}, u32[]{:S(2)}) collective-permute-start(bf16[64,1152]{1,0:T(8,128)(2,1)S(1)} %get-tuple-element.91.refs_0_), channel_id=1, source_target_pairs={{0,4},{1,5},{2,6},{3,7},{4,0},{5,1},{6,2},{7,3},{8,12},{9,13},{10,... | collective-permute-start | bytes 442376 | tf_op jit(solution)/shard_map/ppermute | solution.py:222
  14.5 8.8 %collective-permute-start.11 = (bf16[64,1152]{1,0:T(8,128)(2,1)S(1)}, bf16[64,1152]{1,0:T(8,128)(2,1)S(1)}, u32[]{:S(2)}, u32[]{:S(2)}) collective-permute-start(bf16[64,1152]{1,0:T(8,128)(2,1)S(1)} %get-tuple-element.91.refs_0_), channel_id=1, source_target_pairs={{0,1},{1,0},{2,3},{3,2},{4,5},{5,4},{6,7},{7,6},{8,9},{9,8},{10,11... | collective-permute-start | bytes 442376 | tf_op jit(solution)/shard_map/ppermute | solution.py:222
  14.5 8.0 %collective-permute-start.9 = (bf16[64,1152]{1,0:T(8,128)(2,1)S(1)}, bf16[64,1152]{1,0:T(8,128)(2,1)S(1)}, u32[]{:S(2)}, u32[]{:S(2)}) collective-permute-start(bf16[64,1152]{1,0:T(8,128)(2,1)S(1)} %collective-permute-done.6.refs_0_.refs_4_), channel_id=1, source_target_pairs={{0,2},{1,3},{2,0},{3,1},{4,6},{5,7},{6,4},{7,5},{8,10},{9,11},{10,... | collective-permute-start | bytes 442376 | tf_op jit(solution)/shard_map/ppermute | solution.py:222
  18.8 4.4 %collective-permute-start.4 = (bf16[64,1152]{1,0:T(8,128)(2,1)S(1)}, bf16[64,1152]{1,0:T(8,128)(2,1)S(1)}, u32[]{:S(2)}, u32[]{:S(2)}) collective-permute-start(bf16[64,1152]{1,0:T(8,128)(2,1)S(1)} %get-tuple-element.89), channel_id=1, source_target_pairs={{0,1},{1,0},{2,3},{3,2},{4,5},{5,4},{6,7},{7,6},{8,9},{9,8},{10,11... | collective-permute-start | bytes 442376 | tf_op jit(solution)/shard_map/ppermute | solution.py:222
  20.2 3.0 %collective-permute-start.12 = (bf16[64,1152]{1,0:T(8,128)(2,1)S(1)}, bf16[64,1152]{1,0:T(8,128)(2,1)S(1)}, u32[]{:S(2)}, u32[]{:S(2)}) collective-permute-start(bf16[64,1152]{1,0:T(8,128)(2,1)S(1)} %get-tuple-element.103.refs_1_), channel_id=1, source_target_pairs={{0,1},{1,0},{2,3},{3,2},{4,5},{5,4},{6,7},{7,6},{8,9},{9,8},{10,11... | collective-permute-start | bytes 442376 | tf_op jit(solution)/shard_map/ppermute | solution.py:222
  22.5 5.1 %collective-permute-start.15 = (bf16[64,1152]{1,0:T(8,128)(2,1)S(1)}, bf16[64,1152]{1,0:T(8,128)(2,1)S(1)}, u32[]{:S(2)}, u32[]{:S(2)}) collective-permute-start(bf16[64,1152]{1,0:T(8,128)(2,1)S(1)} %collective-permute-done.7.refs_1_.refs_0_), channel_id=1, source_target_pairs={{0,2},{1,3},{2,0},{3,1},{4,6},{5,7},{6,4},{7,5},{8,10},{9,11},{10,... | collective-permute-start | bytes 442376 | tf_op jit(solution)/shard_map/ppermute | solution.py:222
  26.6 3.7 %collective-permute-start.20 = (bf16[64,1152]{1,0:T(8,128)(2,1)S(1)}, bf16[64,1152]{1,0:T(8,128)(2,1)S(1)}, u32[]{:S(2)}, u32[]{:S(2)}) collective-permute-start(bf16[64,1152]{1,0:T(8,128)(2,1)S(1)} %get-tuple-element.119.refs_5_), channel_id=1, source_target_pairs={{0,1},{1,0},{2,3},{3,2},{4,5},{5,4},{6,7},{7,6},{8,9},{9,8},{10,11... | collective-permute-start | bytes 442376 | tf_op jit(solution)/shard_map/ppermute | solution.py:222
  28.1 7.8 %collective-permute-start.10 = (bf16[64,1152]{1,0:T(8,128)(2,1)S(1)}, bf16[64,1152]{1,0:T(8,128)(2,1)S(1)}, u32[]{:S(2)}, u32[]{:S(2)}) collective-permute-start(bf16[64,1152]{1,0:T(8,128)(2,1)S(1)} %get-tuple-element.102), channel_id=1, source_target_pairs={{0,2},{1,3},{2,0},{3,1},{4,6},{5,7},{6,4},{7,5},{8,10},{9,11},{10,... | collective-permute-start | bytes 442376 | tf_op jit(solution)/shard_map/ppermute | solution.py:222
  29.0 8.1 %collective-permute-start.16 = (bf16[64,1152]{1,0:T(8,128)(2,1)S(1)}, bf16[64,1152]{1,0:T(8,128)(2,1)S(1)}, u32[]{:S(2)}, u32[]{:S(2)}) collective-permute-start(bf16[64,1152]{1,0:T(8,128)(2,1)S(1)} %get-tuple-element.117), channel_id=1, source_target_pairs={{0,2},{1,3},{2,0},{3,1},{4,6},{5,7},{6,4},{7,5},{8,10},{9,11},{10,... | collective-permute-start | bytes 442376 | tf_op jit(solution)/shard_map/ppermute | solution.py:222
  35.3 3.8 %collective-permute-start.22 = (bf16[64,1152]{1,0:T(8,128)(2,1)S(1)}, bf16[64,1152]{1,0:T(8,128)(2,1)S(1)}, u32[]{:S(2)}, u32[]{:S(2)}) collective-permute-start(bf16[64,1152]{1,0:T(8,128)(2,1)S(1)} %get-tuple-element.128), channel_id=1, source_target_pairs={{0,1},{1,0},{2,3},{3,2},{4,5},{5,4},{6,7},{7,6},{8,9},{9,8},{10,11... | collective-permute-start | bytes 442376 | tf_op jit(solution)/shard_map/ppermute | solution.py:222
  35.4 3.7 %collective-permute-start.23 = (bf16[64,1152]{1,0:T(8,128)(2,1)S(1)}, bf16[64,1152]{1,0:T(8,128)(2,1)S(1)}, u32[]{:S(2)}, u32[]{:S(2)}) collective-permute-start(bf16[64,1152]{1,0:T(8,128)(2,1)S(1)} %get-tuple-element.129), channel_id=1, source_target_pairs={{0,1},{1,0},{2,3},{3,2},{4,5},{5,4},{6,7},{7,6},{8,9},{9,8},{10,11... | collective-permute-start | bytes 442376 | tf_op jit(solution)/shard_map/ppermute | solution.py:222
  35.8 4.1 %collective-permute-start.25 = (bf16[64,1152]{1,0:T(8,128)(2,1)S(1)}, bf16[64,1152]{1,0:T(8,128)(2,1)S(1)}, u32[]{:S(2)}, u32[]{:S(2)}) collective-permute-start(bf16[64,1152]{1,0:T(8,128)(2,1)S(1)} %get-tuple-element.136), channel_id=1, source_target_pairs={{0,1},{1,0},{2,3},{3,2},{4,5},{5,4},{6,7},{7,6},{8,9},{9,8},{10,11... | collective-permute-start | bytes 442376 | tf_op jit(solution)/shard_map/ppermute | solution.py:222
  35.9 4.0 %collective-permute-start.26 = (bf16[64,1152]{1,0:T(8,128)(2,1)S(1)}, bf16[64,1152]{1,0:T(8,128)(2,1)S(1)}, u32[]{:S(2)}, u32[]{:S(2)}) collective-permute-start(bf16[64,1152]{1,0:T(8,128)(2,1)S(1)} %get-tuple-element.137), channel_id=1, source_target_pairs={{0,1},{1,0},{2,3},{3,2},{4,5},{5,4},{6,7},{7,6},{8,9},{9,8},{10,11... | collective-permute-start | bytes 442376 | tf_op jit(solution)/shard_map/ppermute | solution.py:222
  37.2 9.2 %collective-permute-start.21 = (bf16[64,1152]{1,0:T(8,128)(2,1)S(1)}, bf16[64,1152]{1,0:T(8,128)(2,1)S(1)}, u32[]{:S(2)}, u32[]{:S(2)}) collective-permute-start(bf16[64,1152]{1,0:T(8,128)(2,1)S(1)} %get-tuple-element.126), channel_id=1, source_target_pairs={{0,8},{1,9},{2,10},{3,11},{4,12},{5,13},{6,14},{7,15},{8,0},{9,1},... | collective-permute-start | bytes 442376 | tf_op jit(solution)/shard_map/ppermute | solution.py:222
  39.1 7.3 %collective-permute-start.24 = (bf16[64,1152]{1,0:T(8,128)(2,1)S(1)}, bf16[64,1152]{1,0:T(8,128)(2,1)S(1)}, u32[]{:S(2)}, u32[]{:S(2)}) collective-permute-start(bf16[64,1152]{1,0:T(8,128)(2,1)S(1)} %get-tuple-element.134), channel_id=1, source_target_pairs={{0,2},{1,3},{2,0},{3,1},{4,6},{5,7},{6,4},{7,5},{8,10},{9,11},{10,... | collective-permute-start | bytes 442376 | tf_op jit(solution)/shard_map/ppermute | solution.py:222
  40.0 9.2 %collective-permute-start.28 = (bf16[64,1152]{1,0:T(8,128)(2,1)S(1)}, bf16[64,1152]{1,0:T(8,128)(2,1)S(1)}, u32[]{:S(2)}, u32[]{:S(2)}) collective-permute-start(bf16[64,1152]{1,0:T(8,128)(2,1)S(1)} %get-tuple-element.146), channel_id=1, source_target_pairs={{0,2},{1,3},{2,0},{3,1},{4,6},{5,7},{6,4},{7,5},{8,10},{9,11},{10,... | collective-permute-start | bytes 442376 | tf_op jit(solution)/shard_map/ppermute | solution.py:222
  46.4 8.6 %collective-permute-start.27 = (bf16[64,1152]{1,0:T(8,128)(2,1)S(1)}, bf16[64,1152]{1,0:T(8,128)(2,1)S(1)}, u32[]{:S(2)}, u32[]{:S(2)}) collective-permute-start(bf16[64,1152]{1,0:T(8,128)(2,1)S(1)} %get-tuple-element.144), channel_id=1, source_target_pairs={{0,12},{1,13},{2,14},{3,15},{4,8},{5,9},{6,10},{7,11},{8,4},{9,5},... | collective-permute-start | bytes 442376 | tf_op jit(solution)/shard_map/ppermute | solution.py:222
  49.2 7.5 %collective-permute-start.29 = (bf16[64,1152]{1,0:T(8,128)(2,1)S(1)}, bf16[64,1152]{1,0:T(8,128)(2,1)S(1)}, u32[]{:S(2)}, u32[]{:S(2)}) collective-permute-start(bf16[64,1152]{1,0:T(8,128)(2,1)S(1)} %get-tuple-element.150), channel_id=1, source_target_pairs={{0,4},{1,5},{2,6},{3,7},{4,0},{5,1},{6,2},{7,3},{8,12},{9,13},{10,... | collective-permute-start | bytes 442376 | tf_op jit(solution)/shard_map/ppermute | solution.py:222
  (6 other events, 14.6 us)

commit v18 on v17

--- a/solution.py
+++ b/solution.py
@@ -291,22 +291,22 @@
             return swap(sums, 4 * k)
 
         z_2, z_1, y_0 = swap(mine, 8), swap(mine, 4), swap(mine, 2)
-        block = {0: mine, 2: tie(z_2), 1: z_1}
+        block = {0: mine, 2: tie(z_2, [z_1]), 1: z_1}
         block[3] = swap(block[2], 4)
         other[0] = tie(y_0)
         compute(0)
         gather(2, [block[1], block[3]])
-        gather(1)
         reduce_core(0)
         compute(2)
+        gather(1)
         gather(3)
         reduce_core(2)
         compute(3, 1)
-        z_2 = reduce_y(2, [y_came[0]])
-        reduce_core(3)
+        z_2 = reduce_y(2)
+        reduce_core(3, [y_came[0]])
         reduce_core(1)
-        z_3 = reduce_y(3, [z_2])
-        z_1 = reduce_y(1)
+        z_3 = reduce_y(3)
+        z_1 = reduce_y(1, [z_2])
         return fold_keep[0], y_came[0], z_2, z_3, z_1
 
     packet = call(

time: 57.7 us -> 57.2 us (level)
  waiting for transfers between devices: 16.9 us -> 15.5 us
  starting transfers between devices: 23.3 us -> 24.3 us
    ppermute x30, waiting for transfers between devices: 16.9 us -> 15.5 us  [swap(): return lax.ppermute(x, 'exp', [(i, i ^ bits) for i in range(n_dev)])]
    ppermute x30, starting transfers between devices: 23.3 us -> 24.3 us  [swap(): return lax.ppermute(x, 'exp', [(i, i ^ bits) for i in range(n_dev)])]
  transfers between devices with their start and end apart: 30 -> 30, of which waited for: 7 -> 8; matrix products, arithmetic and copies ran while one was open for 0% -> 0% of each run, Pallas kernels for 27% -> 27%
where the time goes in v18:
time: 57.2 us; the launch traced here: 57 us
  starting transfers between devices  24.3 us (42%)
  Pallas kernels  17.1 us (30%)
  waiting for transfers between devices  15.5 us (27%)
    ppermute x30, starting transfers between devices, swap(): return lax.ppermute(x, 'exp', [(i, i ^ bits) for i in range(n_dev)])  24.3 us
    pallas_call x17, Pallas kernels, call(): pl.pallas_call(body_with_chain if reads_chain else body, out_shape=list(o...  16.3 us
    ppermute x30, waiting for transfers between devices, swap(): return lax.ppermute(x, 'exp', [(i, i ^ bits) for i in range(n_dev)])  15.5 us
  transfers between devices with their start and end apart: 30, of which 8 were waited for; matrix products, arithmetic and copies ran while one was open for 0% of the time, Pallas kernels for 27%

profile of v18, /device:TPU:0, one launch (start us, length us, event | category | flops | bytes accessed | tf_op | source)
XLA Modules:
  0.0 57.0 jit_solution(4087845852983633437)
XLA Ops:
  0.0 0.9 %pack.1.refs_3_.refs_0_ = bf16[64,1152]{1,0:T(8,128)(2,1)S(1)} custom-call(s32[8,64]{1,0:T(8,128)} %bitcast.2, bf16[64,1024]{1,0:T(8,128)(2,1)} %refs_1_.2), custom_call_target="tpu_custom_call" | custom-call | bytes 10000 | tf_op jit(solution)/shard_map/pack/pallas_call | solution.py:201
  0.9 4.1 %collective-permute-start.1 = (bf16[64,1152]{1,0:T(8,128)(2,1)S(1)}, bf16[64,1152]{1,0:T(8,128)(2,1)S(1)}, u32[]{:S(2)}, u32[]{:S(2)}) collective-permute-start(bf16[64,1152]{1,0:T(8,128)(2,1)S(1)} %pack.1.refs_3_.refs_0_), channel_id=1, source_target_pairs={{0,8},{1,9},{2,10},{3,11},{4,12},{5,13},{6,14},{7,15},{8,0},{9,1},... | collective-permute-start | bytes 442376 | tf_op jit(solution)/shard_map/ppermute | solution.py:222
  5.0 1.6 %collective-permute-start = (bf16[64,1152]{1,0:T(8,128)(2,1)S(1)}, bf16[64,1152]{1,0:T(8,128)(2,1)S(1)}, u32[]{:S(2)}, u32[]{:S(2)}) collective-permute-start(bf16[64,1152]{1,0:T(8,128)(2,1)S(1)} %pack.1.refs_3_.refs_0_), channel_id=1, source_target_pairs={{0,4},{1,5},{2,6},{3,7},{4,0},{5,1},{6,2},{7,3},{8,12},{9,13},{10,... | collective-permute-start | bytes 442376 | tf_op jit(solution)/shard_map/ppermute | solution.py:222
  6.6 1.5 %collective-permute-start.2 = (bf16[64,1152]{1,0:T(8,128)(2,1)S(1)}, bf16[64,1152]{1,0:T(8,128)(2,1)S(1)}, u32[]{:S(2)}, u32[]{:S(2)}) collective-permute-start(bf16[64,1152]{1,0:T(8,128)(2,1)S(1)} %pack.1.refs_3_.refs_0_), channel_id=1, source_target_pairs={{0,2},{1,3},{2,0},{3,1},{4,6},{5,7},{6,4},{7,5},{8,10},{9,11},{10,... | collective-permute-start | bytes 442376 | tf_op jit(solution)/shard_map/ppermute | solution.py:222
  8.1 4.7 %load.1 = (bf16[1024,128]{1,0:T(8,128)(2,1)S(1)}, bf16[2,1024,2048]{2,1,0:T(8,128)(2,1)S(1)}, bf16[2,1024,1024]{2,1,0:T(8,128)(2,1)S(1)}) custom-call(bf16[2,1024]{1,0:T(2,128)(2,1)} %bitcast.3, bf16[2,1024,2048]{2,1,0:T(8,128)(2,1)} %refs_1_.3, bf16[2,1024,1024]{2,1,0:T(8,128)(2,1)} %refs_2_.1, bf16[64,1152]{1,0:T(8,128)(2,1)S(1)} %pack.1.refs_3_.refs_0_), custom_call_target="tpu_custom_call" | custom-call | bytes 10000 | tf_op jit(solution)/shard_map/load/pallas_call | solution.py:201
  14.0 1.4 %collective-permute-start.7 = (bf16[64,1152]{1,0:T(8,128)(2,1)S(1)}, bf16[64,1152]{1,0:T(8,128)(2,1)S(1)}, u32[]{:S(2)}, u32[]{:S(2)}) collective-permute-start(bf16[64,1152]{1,0:T(8,128)(2,1)S(1)} %get-tuple-element.91.refs_0_), channel_id=1, source_target_pairs={{0,4},{1,5},{2,6},{3,7},{4,0},{5,1},{6,2},{7,3},{8,12},{9,13},{10,... | collective-permute-start | bytes 442376 | tf_op jit(solution)/shard_map/ppermute | solution.py:222
  15.4 2.7 %expert.3 = (f32[128,1152]{1,0:T(8,128)S(1)}, bf16[64,1152]{1,0:T(8,128)(2,1)S(1)}, bf16[64,1152]{1,0:T(8,128)(2,1)S(1)}, bf16[1024,128]{1,0:T(8,128)(2,1)S(1)},...) custom-call(bf16[64,1152]{1,0:T(8,128)(2,1)S(1)} %pack.1.refs_3_.ref, ...), custom_call_target="tpu_custom_call", output_to_operand_aliasing={{3}: (4, {}), {4}: (5, {}), {5}: (6, {})} | custom-call | bytes 10000 | tf_op jit(solution)/shard_map/expert/pallas_call | solution.py:201
  19.9 1.2 %collective-permute-start.14 = (bf16[64,1152]{1,0:T(8,128)(2,1)S(1)}, bf16[64,1152]{1,0:T(8,128)(2,1)S(1)}, u32[]{:S(2)}, u32[]{:S(2)}) collective-permute-start(bf16[64,1152]{1,0:T(8,128)(2,1)S(1)} %collective-permute-done.refs_0_.refs_4_), channel_id=1, source_target_pairs={{0,2},{1,3},{2,0},{3,1},{4,6},{5,7},{6,4},{7,5},{8,10},{9,11},{10,... | collective-permute-start | bytes 442376 | tf_op jit(solution)/shard_map/ppermute | solution.py:222
  21.1 0.9 %collective-permute-start.15 = (bf16[64,1152]{1,0:T(8,128)(2,1)S(1)}, bf16[64,1152]{1,0:T(8,128)(2,1)S(1)}, u32[]{:S(2)}, u32[]{:S(2)}) collective-permute-start(bf16[64,1152]{1,0:T(8,128)(2,1)S(1)} %collective-permute-done.7.refs_1_.refs_0_), channel_id=1, source_target_pairs={{0,2},{1,3},{2,0},{3,1},{4,6},{5,7},{6,4},{7,5},{8,10},{9,11},{10,... | collective-permute-start | bytes 442376 | tf_op jit(solution)/shard_map/ppermute | solution.py:222
  22.0 2.7 %expert.4 = (f32[128,1152]{1,0:T(8,128)S(1)}, bf16[64,1152]{1,0:T(8,128)(2,1)S(1)}, bf16[64,1152]{1,0:T(8,128)(2,1)S(1)}, bf16[1024,128]{1,0:T(8,128)(2,1)S(1)},...) custom-call(bf16[64,1152]{1,0:T(8,128)(2,1)S(1)} %get-tuple-element., ...), custom_call_target="tpu_custom_call", output_to_operand_aliasing={{3}: (4, {}), {4}: (5, {}), {5}: (6, {})} | custom-call | bytes 10000 | tf_op jit(solution)/shard_map/expert/pallas_call | solution.py:201
  25.4 1.2 %collective-permute-done.14.refs_3_ = bf16[64,1152]{1,0:T(8,128)(2,1)S(1)} collective-permute-done((bf16[64,1152]{1,0:T(8,128)(2,1)S(1)}, bf16[64,1152]{1,0:T(8,128)(2,1)S(1)}, u32[]{:S(2)}, u32[]{:S(2)}) %collective-permute-start.14) | collective-permute-done | bytes 147488 | tf_op jit(solution)/shard_map/ppermute | solution.py:222
  26.6 2.8 %collective-permute-done.15.refs_3_ = bf16[64,1152]{1,0:T(8,128)(2,1)S(1)} collective-permute-done((bf16[64,1152]{1,0:T(8,128)(2,1)S(1)}, bf16[64,1152]{1,0:T(8,128)(2,1)S(1)}, u32[]{:S(2)}, u32[]{:S(2)}) %collective-permute-start.15) | collective-permute-done | bytes 147488 | tf_op jit(solution)/shard_map/ppermute | solution.py:222
  29.9 1.2 %collective-permute-start.16 = (bf16[64,1152]{1,0:T(8,128)(2,1)S(1)}, bf16[64,1152]{1,0:T(8,128)(2,1)S(1)}, u32[]{:S(2)}, u32[]{:S(2)}) collective-permute-start(bf16[64,1152]{1,0:T(8,128)(2,1)S(1)} %get-tuple-element.117), channel_id=1, source_target_pairs={{0,2},{1,3},{2,0},{3,1},{4,6},{5,7},{6,4},{7,5},{8,10},{9,11},{10,... | collective-permute-start | bytes 442376 | tf_op jit(solution)/shard_map/ppermute | solution.py:222
  31.1 0.9 %collective-permute-start.9 = (bf16[64,1152]{1,0:T(8,128)(2,1)S(1)}, bf16[64,1152]{1,0:T(8,128)(2,1)S(1)}, u32[]{:S(2)}, u32[]{:S(2)}) collective-permute-start(bf16[64,1152]{1,0:T(8,128)(2,1)S(1)} %get-tuple-element.99), channel_id=1, source_target_pairs={{0,2},{1,3},{2,0},{3,1},{4,6},{5,7},{6,4},{7,5},{8,10},{9,11},{10,... | collective-permute-start | bytes 442376 | tf_op jit(solution)/shard_map/ppermute | solution.py:222
  32.0 4.9 %expert.5 = (f32[128,1152]{1,0:T(8,128)S(1)}, f32[128,1152]{1,0:T(8,128)S(1)}, bf16[64,1152]{1,0:T(8,128)(2,1)S(1)}, bf16[64,1152]{1,0:T(8,128)(2,1)S(1)}, bf16[...) custom-call(bf16[64,1152]{1,0:T(8,128)(2,1)S(1)} %collective-permute, ...), custom_call_target="tpu_custom_call", output_to_operand_aliasing={{6}: (8, {}), {7}: (9, {}), {8}: (10, {})} | custom-call | bytes 10000 | tf_op jit(solution)/shard_map/expert/pallas_call | solution.py:201
  38.1 0.9 %collective-permute-done.9.refs_3_.refs_1_ = bf16[64,1152]{1,0:T(8,128)(2,1)S(1)} collective-permute-done((bf16[64,1152]{1,0:T(8,128)(2,1)S(1)}, bf16[64,1152]{1,0:T(8,128)(2,1)S(1)}, u32[]{:S(2)}, u32[]{:S(2)}) %collective-permute-start.9) | collective-permute-done | bytes 147488 | tf_op jit(solution)/shard_map/ppermute | solution.py:222
  39.0 2.1 %collective-permute-start.21 = (bf16[64,1152]{1,0:T(8,128)(2,1)S(1)}, bf16[64,1152]{1,0:T(8,128)(2,1)S(1)}, u32[]{:S(2)}, u32[]{:S(2)}) collective-permute-start(bf16[64,1152]{1,0:T(8,128)(2,1)S(1)} %get-tuple-element.126), channel_id=1, source_target_pairs={{0,8},{1,9},{2,10},{3,11},{4,12},{5,13},{6,14},{7,15},{8,0},{9,1},... | collective-permute-start | bytes 442376 | tf_op jit(solution)/shard_map/ppermute | solution.py:222
  41.8 1.6 %collective-permute-start.28 = (bf16[64,1152]{1,0:T(8,128)(2,1)S(1)}, bf16[64,1152]{1,0:T(8,128)(2,1)S(1)}, u32[]{:S(2)}, u32[]{:S(2)}) collective-permute-start(bf16[64,1152]{1,0:T(8,128)(2,1)S(1)} %get-tuple-element.146), channel_id=1, source_target_pairs={{0,2},{1,3},{2,0},{3,1},{4,6},{5,7},{6,4},{7,5},{8,10},{9,11},{10,... | collective-permute-start | bytes 442376 | tf_op jit(solution)/shard_map/ppermute | solution.py:222
  43.3 4.2 %collective-permute-done.24.refs_1_ = bf16[64,1152]{1,0:T(8,128)(2,1)S(1)} collective-permute-done((bf16[64,1152]{1,0:T(8,128)(2,1)S(1)}, bf16[64,1152]{1,0:T(8,128)(2,1)S(1)}, u32[]{:S(2)}, u32[]{:S(2)}) %collective-permute-start.24) | collective-permute-done | bytes 147488 | tf_op jit(solution)/shard_map/ppermute | solution.py:222
  47.6 2.2 %collective-permute-start.27 = (bf16[64,1152]{1,0:T(8,128)(2,1)S(1)}, bf16[64,1152]{1,0:T(8,128)(2,1)S(1)}, u32[]{:S(2)}, u32[]{:S(2)}) collective-permute-start(bf16[64,1152]{1,0:T(8,128)(2,1)S(1)} %get-tuple-element.144), channel_id=1, source_target_pairs={{0,12},{1,13},{2,14},{3,15},{4,8},{5,9},{6,10},{7,11},{8,4},{9,5},... | collective-permute-start | bytes 442376 | tf_op jit(solution)/shard_map/ppermute | solution.py:222
  49.8 1.2 %collective-permute-start.29 = (bf16[64,1152]{1,0:T(8,128)(2,1)S(1)}, bf16[64,1152]{1,0:T(8,128)(2,1)S(1)}, u32[]{:S(2)}, u32[]{:S(2)}) collective-permute-start(bf16[64,1152]{1,0:T(8,128)(2,1)S(1)} %get-tuple-element.150), channel_id=1, source_target_pairs={{0,4},{1,5},{2,6},{3,7},{4,0},{5,1},{6,2},{7,3},{8,12},{9,13},{10,... | collective-permute-start | bytes 442376 | tf_op jit(solution)/shard_map/ppermute | solution.py:222
  51.0 4.6 %collective-permute-done.27.refs_3_ = bf16[64,1152]{1,0:T(8,128)(2,1)S(1)} collective-permute-done((bf16[64,1152]{1,0:T(8,128)(2,1)S(1)}, bf16[64,1152]{1,0:T(8,128)(2,1)S(1)}, u32[]{:S(2)}, u32[]{:S(2)}) %collective-permute-start.27) | collective-permute-done | bytes 147488 | tf_op jit(solution)/shard_map/ppermute | solution.py:222
  55.6 0.7 %collective-permute-done.29.refs_4_ = bf16[64,1152]{1,0:T(8,128)(2,1)S(1)} collective-permute-done((bf16[64,1152]{1,0:T(8,128)(2,1)S(1)}, bf16[64,1152]{1,0:T(8,128)(2,1)S(1)}, u32[]{:S(2)}, u32[]{:S(2)}) %collective-permute-start.29) | collective-permute-done | bytes 147488 | tf_op jit(solution)/shard_map/ppermute | solution.py:222
  56.3 0.8 %finish.1 = bf16[64,1024]{1,0:T(8,128)(2,1)} custom-call(f32[64,1152]{1,0:T(8,128)S(1)} %get-tuple-element.98.refs_0_, bf16[64,1152]{1,0:T(8,128)(2,1)S(1)} %collective-permute-done.9.refs_3_.refs_1_, bf16[64,1152]{1,0:T(8,128)(2,1)S(1)} %collective-permute-done.21.refs_2_, bf16[64,1152]{1,0:T(8,128)(2,1)S(1)} %collective-permute-done.27.refs_3_, ...), custom_call_target="tpu_custom_call" | custom-call | tf_op jit(solution)/shard_map/finish/pallas_call | solution.py:320
  (54 shorter events, 6.0 us)
Async XLA Ops:
  0.9 11.9 %collective-permute-start.1 = (bf16[64,1152]{1,0:T(8,128)(2,1)S(1)}, bf16[64,1152]{1,0:T(8,128)(2,1)S(1)}, u32[]{:S(2)}, u32[]{:S(2)}) collective-permute-start(bf16[64,1152]{1,0:T(8,128)(2,1)S(1)} %pack.1.refs_3_.refs_0_), channel_id=1, source_target_pairs={{0,8},{1,9},{2,10},{3,11},{4,12},{5,13},{6,14},{7,15},{8,0},{9,1},... | collective-permute-start | bytes 442376 | tf_op jit(solution)/shard_map/ppermute | solution.py:222
  5.0 7.8 %collective-permute-start = (bf16[64,1152]{1,0:T(8,128)(2,1)S(1)}, bf16[64,1152]{1,0:T(8,128)(2,1)S(1)}, u32[]{:S(2)}, u32[]{:S(2)}) collective-permute-start(bf16[64,1152]{1,0:T(8,128)(2,1)S(1)} %pack.1.refs_3_.refs_0_), channel_id=1, source_target_pairs={{0,4},{1,5},{2,6},{3,7},{4,0},{5,1},{6,2},{7,3},{8,12},{9,13},{10,... | collective-permute-start | bytes 442376 | tf_op jit(solution)/shard_map/ppermute | solution.py:222
  6.6 6.3 %collective-permute-start.2 = (bf16[64,1152]{1,0:T(8,128)(2,1)S(1)}, bf16[64,1152]{1,0:T(8,128)(2,1)S(1)}, u32[]{:S(2)}, u32[]{:S(2)}) collective-permute-start(bf16[64,1152]{1,0:T(8,128)(2,1)S(1)} %pack.1.refs_3_.refs_0_), channel_id=1, source_target_pairs={{0,2},{1,3},{2,0},{3,1},{4,6},{5,7},{6,4},{7,5},{8,10},{9,11},{10,... | collective-permute-start | bytes 442376 | tf_op jit(solution)/shard_map/ppermute | solution.py:222
  8.1 7.3 %collective-permute-start.3 = (bf16[64,1152]{1,0:T(8,128)(2,1)S(1)}, bf16[64,1152]{1,0:T(8,128)(2,1)S(1)}, u32[]{:S(2)}, u32[]{:S(2)}) collective-permute-start(bf16[64,1152]{1,0:T(8,128)(2,1)S(1)} %pack.1.refs_3_.refs_0_), channel_id=1, source_target_pairs={{0,1},{1,0},{2,3},{3,2},{4,5},{5,4},{6,7},{7,6},{8,9},{9,8},{10,11... | collective-permute-start | bytes 442376 | tf_op jit(solution)/shard_map/ppermute | solution.py:222
  13.5 5.8 %collective-permute-start.8 = (bf16[64,1152]{1,0:T(8,128)(2,1)S(1)}, bf16[64,1152]{1,0:T(8,128)(2,1)S(1)}, u32[]{:S(2)}, u32[]{:S(2)}) collective-permute-start(bf16[64,1152]{1,0:T(8,128)(2,1)S(1)} %get-tuple-element.91.refs_0_), channel_id=1, source_target_pairs={{0,2},{1,3},{2,0},{3,1},{4,6},{5,7},{6,4},{7,5},{8,10},{9,11},{10,... | collective-permute-start | bytes 442376 | tf_op jit(solution)/shard_map/ppermute | solution.py:222
  14.0 5.9 %collective-permute-start.7 = (bf16[64,1152]{1,0:T(8,128)(2,1)S(1)}, bf16[64,1152]{1,0:T(8,128)(2,1)S(1)}, u32[]{:S(2)}, u32[]{:S(2)}) collective-permute-start(bf16[64,1152]{1,0:T(8,128)(2,1)S(1)} %get-tuple-element.91.refs_0_), channel_id=1, source_target_pairs={{0,4},{1,5},{2,6},{3,7},{4,0},{5,1},{6,2},{7,3},{8,12},{9,13},{10,... | collective-permute-start | bytes 442376 | tf_op jit(solution)/shard_map/ppermute | solution.py:222
  15.4 6.6 %collective-permute-start.10 = (bf16[64,1152]{1,0:T(8,128)(2,1)S(1)}, bf16[64,1152]{1,0:T(8,128)(2,1)S(1)}, u32[]{:S(2)}, u32[]{:S(2)}) collective-permute-start(bf16[64,1152]{1,0:T(8,128)(2,1)S(1)} %get-tuple-element.91.refs_0_), channel_id=1, source_target_pairs={{0,1},{1,0},{2,3},{3,2},{4,5},{5,4},{6,7},{7,6},{8,9},{9,8},{10,11... | collective-permute-start | bytes 442376 | tf_op jit(solution)/shard_map/ppermute | solution.py:222
  19.9 6.6 %collective-permute-start.14 = (bf16[64,1152]{1,0:T(8,128)(2,1)S(1)}, bf16[64,1152]{1,0:T(8,128)(2,1)S(1)}, u32[]{:S(2)}, u32[]{:S(2)}) collective-permute-start(bf16[64,1152]{1,0:T(8,128)(2,1)S(1)} %collective-permute-done.refs_0_.refs_4_), channel_id=1, source_target_pairs={{0,2},{1,3},{2,0},{3,1},{4,6},{5,7},{6,4},{7,5},{8,10},{9,11},{10,... | collective-permute-start | bytes 442376 | tf_op jit(solution)/shard_map/ppermute | solution.py:222
  21.1 8.3 %collective-permute-start.15 = (bf16[64,1152]{1,0:T(8,128)(2,1)S(1)}, bf16[64,1152]{1,0:T(8,128)(2,1)S(1)}, u32[]{:S(2)}, u32[]{:S(2)}) collective-permute-start(bf16[64,1152]{1,0:T(8,128)(2,1)S(1)} %collective-permute-done.7.refs_1_.refs_0_), channel_id=1, source_target_pairs={{0,2},{1,3},{2,0},{3,1},{4,6},{5,7},{6,4},{7,5},{8,10},{9,11},{10,... | collective-permute-start | bytes 442376 | tf_op jit(solution)/shard_map/ppermute | solution.py:222
  24.7 4.6 %collective-permute-start.12 = (bf16[64,1152]{1,0:T(8,128)(2,1)S(1)}, bf16[64,1152]{1,0:T(8,128)(2,1)S(1)}, u32[]{:S(2)}, u32[]{:S(2)}) collective-permute-start(bf16[64,1152]{1,0:T(8,128)(2,1)S(1)} %get-tuple-element.105), channel_id=1, source_target_pairs={{0,1},{1,0},{2,3},{3,2},{4,5},{5,4},{6,7},{7,6},{8,9},{9,8},{10,11... | collective-permute-start | bytes 442376 | tf_op jit(solution)/shard_map/ppermute | solution.py:222
  24.8 5.1 %collective-permute-start.13 = (bf16[64,1152]{1,0:T(8,128)(2,1)S(1)}, bf16[64,1152]{1,0:T(8,128)(2,1)S(1)}, u32[]{:S(2)}, u32[]{:S(2)}) collective-permute-start(bf16[64,1152]{1,0:T(8,128)(2,1)S(1)} %get-tuple-element.106), channel_id=1, source_target_pairs={{0,1},{1,0},{2,3},{3,2},{4,5},{5,4},{6,7},{7,6},{8,9},{9,8},{10,11... | collective-permute-start | bytes 442376 | tf_op jit(solution)/shard_map/ppermute | solution.py:222
  25.3 5.8 %collective-permute-start.19 = (bf16[64,1152]{1,0:T(8,128)(2,1)S(1)}, bf16[64,1152]{1,0:T(8,128)(2,1)S(1)}, u32[]{:S(2)}, u32[]{:S(2)}) collective-permute-start(bf16[64,1152]{1,0:T(8,128)(2,1)S(1)} %collective-permute-done.refs_0_.refs_4_), channel_id=1, source_target_pairs={{0,1},{1,0},{2,3},{3,2},{4,5},{5,4},{6,7},{7,6},{8,9},{9,8},{10,11... | collective-permute-start | bytes 442376 | tf_op jit(solution)/shard_map/ppermute | solution.py:222
  26.6 5.4 %collective-permute-start.17 = (bf16[64,1152]{1,0:T(8,128)(2,1)S(1)}, bf16[64,1152]{1,0:T(8,128)(2,1)S(1)}, u32[]{:S(2)}, u32[]{:S(2)}) collective-permute-start(bf16[64,1152]{1,0:T(8,128)(2,1)S(1)} %collective-permute-done.7.refs_1_.refs_0_), channel_id=1, source_target_pairs={{0,1},{1,0},{2,3},{3,2},{4,5},{5,4},{6,7},{7,6},{8,9},{9,8},{10,11... | collective-permute-start | bytes 442376 | tf_op jit(solution)/shard_map/ppermute | solution.py:222
  29.9 7.7 %collective-permute-start.16 = (bf16[64,1152]{1,0:T(8,128)(2,1)S(1)}, bf16[64,1152]{1,0:T(8,128)(2,1)S(1)}, u32[]{:S(2)}, u32[]{:S(2)}) collective-permute-start(bf16[64,1152]{1,0:T(8,128)(2,1)S(1)} %get-tuple-element.117), channel_id=1, source_target_pairs={{0,2},{1,3},{2,0},{3,1},{4,6},{5,7},{6,4},{7,5},{8,10},{9,11},{10,... | collective-permute-start | bytes 442376 | tf_op jit(solution)/shard_map/ppermute | solution.py:222
  31.1 7.8 %collective-permute-start.9 = (bf16[64,1152]{1,0:T(8,128)(2,1)S(1)}, bf16[64,1152]{1,0:T(8,128)(2,1)S(1)}, u32[]{:S(2)}, u32[]{:S(2)}) collective-permute-start(bf16[64,1152]{1,0:T(8,128)(2,1)S(1)} %get-tuple-element.99), channel_id=1, source_target_pairs={{0,2},{1,3},{2,0},{3,1},{4,6},{5,7},{6,4},{7,5},{8,10},{9,11},{10,... | collective-permute-start | bytes 442376 | tf_op jit(solution)/shard_map/ppermute | solution.py:222
  37.0 4.1 %collective-permute-start.22 = (bf16[64,1152]{1,0:T(8,128)(2,1)S(1)}, bf16[64,1152]{1,0:T(8,128)(2,1)S(1)}, u32[]{:S(2)}, u32[]{:S(2)}) collective-permute-start(bf16[64,1152]{1,0:T(8,128)(2,1)S(1)} %get-tuple-element.128), channel_id=1, source_target_pairs={{0,1},{1,0},{2,3},{3,2},{4,5},{5,4},{6,7},{7,6},{8,9},{9,8},{10,11... | collective-permute-start | bytes 442376 | tf_op jit(solution)/shard_map/ppermute | solution.py:222
  37.1 4.0 %collective-permute-start.23 = (bf16[64,1152]{1,0:T(8,128)(2,1)S(1)}, bf16[64,1152]{1,0:T(8,128)(2,1)S(1)}, u32[]{:S(2)}, u32[]{:S(2)}) collective-permute-start(bf16[64,1152]{1,0:T(8,128)(2,1)S(1)} %get-tuple-element.129), channel_id=1, source_target_pairs={{0,1},{1,0},{2,3},{3,2},{4,5},{5,4},{6,7},{7,6},{8,9},{9,8},{10,11... | collective-permute-start | bytes 442376 | tf_op jit(solution)/shard_map/ppermute | solution.py:222
  37.6 4.2 %collective-permute-start.25 = (bf16[64,1152]{1,0:T(8,128)(2,1)S(1)}, bf16[64,1152]{1,0:T(8,128)(2,1)S(1)}, u32[]{:S(2)}, u32[]{:S(2)}) collective-permute-start(bf16[64,1152]{1,0:T(8,128)(2,1)S(1)} %get-tuple-element.136), channel_id=1, source_target_pairs={{0,1},{1,0},{2,3},{3,2},{4,5},{5,4},{6,7},{7,6},{8,9},{9,8},{10,11... | collective-permute-start | bytes 442376 | tf_op jit(solution)/shard_map/ppermute | solution.py:222
  37.6 4.1 %collective-permute-start.26 = (bf16[64,1152]{1,0:T(8,128)(2,1)S(1)}, bf16[64,1152]{1,0:T(8,128)(2,1)S(1)}, u32[]{:S(2)}, u32[]{:S(2)}) collective-permute-start(bf16[64,1152]{1,0:T(8,128)(2,1)S(1)} %get-tuple-element.137), channel_id=1, source_target_pairs={{0,1},{1,0},{2,3},{3,2},{4,5},{5,4},{6,7},{7,6},{8,9},{9,8},{10,11... | collective-permute-start | bytes 442376 | tf_op jit(solution)/shard_map/ppermute | solution.py:222
  39.0 10.8 %collective-permute-start.21 = (bf16[64,1152]{1,0:T(8,128)(2,1)S(1)}, bf16[64,1152]{1,0:T(8,128)(2,1)S(1)}, u32[]{:S(2)}, u32[]{:S(2)}) collective-permute-start(bf16[64,1152]{1,0:T(8,128)(2,1)S(1)} %get-tuple-element.126), channel_id=1, source_target_pairs={{0,8},{1,9},{2,10},{3,11},{4,12},{5,13},{6,14},{7,15},{8,0},{9,1},... | collective-permute-start | bytes 442376 | tf_op jit(solution)/shard_map/ppermute | solution.py:222
  41.1 6.4 %collective-permute-start.24 = (bf16[64,1152]{1,0:T(8,128)(2,1)S(1)}, bf16[64,1152]{1,0:T(8,128)(2,1)S(1)}, u32[]{:S(2)}, u32[]{:S(2)}) collective-permute-start(bf16[64,1152]{1,0:T(8,128)(2,1)S(1)} %get-tuple-element.134), channel_id=1, source_target_pairs={{0,2},{1,3},{2,0},{3,1},{4,6},{5,7},{6,4},{7,5},{8,10},{9,11},{10,... | collective-permute-start | bytes 442376 | tf_op jit(solution)/shard_map/ppermute | solution.py:222
  41.8 8.0 %collective-permute-start.28 = (bf16[64,1152]{1,0:T(8,128)(2,1)S(1)}, bf16[64,1152]{1,0:T(8,128)(2,1)S(1)}, u32[]{:S(2)}, u32[]{:S(2)}) collective-permute-start(bf16[64,1152]{1,0:T(8,128)(2,1)S(1)} %get-tuple-element.146), channel_id=1, source_target_pairs={{0,2},{1,3},{2,0},{3,1},{4,6},{5,7},{6,4},{7,5},{8,10},{9,11},{10,... | collective-permute-start | bytes 442376 | tf_op jit(solution)/shard_map/ppermute | solution.py:222
  47.6 8.0 %collective-permute-start.27 = (bf16[64,1152]{1,0:T(8,128)(2,1)S(1)}, bf16[64,1152]{1,0:T(8,128)(2,1)S(1)}, u32[]{:S(2)}, u32[]{:S(2)}) collective-permute-start(bf16[64,1152]{1,0:T(8,128)(2,1)S(1)} %get-tuple-element.144), channel_id=1, source_target_pairs={{0,12},{1,13},{2,14},{3,15},{4,8},{5,9},{6,10},{7,11},{8,4},{9,5},... | collective-permute-start | bytes 442376 | tf_op jit(solution)/shard_map/ppermute | solution.py:222
  49.8 6.5 %collective-permute-start.29 = (bf16[64,1152]{1,0:T(8,128)(2,1)S(1)}, bf16[64,1152]{1,0:T(8,128)(2,1)S(1)}, u32[]{:S(2)}, u32[]{:S(2)}) collective-permute-start(bf16[64,1152]{1,0:T(8,128)(2,1)S(1)} %get-tuple-element.150), channel_id=1, source_target_pairs={{0,4},{1,5},{2,6},{3,7},{4,0},{5,1},{6,2},{7,3},{8,12},{9,13},{10,... | collective-permute-start | bytes 442376 | tf_op jit(solution)/shard_map/ppermute | solution.py:222
  (6 other events, 16.2 us)

commit v19 on v18

--- a/solution.py
+++ b/solution.py
@@ -244,7 +244,8 @@
     slots = 4 * bound
 
     def group_pass(mine):
-        held = weights(mine)
+        block, other = {0: mine}, {0: swap(mine, 2)}
+        held = weights(other[0])
 
         def step(kernel, outs, args=(), deps=(), hand_on=(), **more):
             nonlocal held
@@ -255,10 +256,7 @@
         def tie(x, deps=()):
             return step(tie_kernel, [], deps=deps, hand_on=[x])[0]
 
-        other, keep, send, came, fold_keep, fold_send, y_came = {}, {}, {}, {}, {}, {}, {}
-
-        def gather(k, deps=()):
-            other[k] = tie(swap(block[k], 2), deps)
+        keep, send, came, fold_keep, fold_send, y_came = {}, {}, {}, {}, {}, {}
 
         def compute(*ks):
             count = len(ks)
@@ -290,20 +288,20 @@
             sums = step(add_kernel, [space(rows, jnp.bfloat16)], [fold_keep[k], y_came[k]], deps)[0]
             return swap(sums, 4 * k)
 
-        z_2, z_1, y_0 = swap(mine, 8), swap(mine, 4), swap(mine, 2)
-        block = {0: mine, 2: tie(z_2, [z_1]), 1: z_1}
+        block[1], block[2] = swap(mine, 4), swap(mine, 8)
+        other[1], other[2] = swap(other[0], 4), swap(other[0], 8)
+        block[2] = tie(block[2])
         block[3] = swap(block[2], 4)
-        other[0] = tie(y_0)
         compute(0)
-        gather(2, [block[1], block[3]])
+        other[1] = tie(other[1], [other[2], block[3]])
+        other[3] = swap(other[2], 4)
         reduce_core(0)
         compute(2)
-        gather(1)
-        gather(3)
-        reduce_core(2)
+        other[3] = tie(other[3])
+        reduce_core(2, [y_came[0]])
         compute(3, 1)
         z_2 = reduce_y(2)
-        reduce_core(3, [y_came[0]])
+        reduce_core(3)
         reduce_core(1)
         z_3 = reduce_y(3)
         z_1 = reduce_y(1, [z_2])

time: 57.2 us -> 58.9 us (1.030)
  starting transfers between devices: 24.3 us -> 27.6 us
  waiting for transfers between devices: 15.5 us -> 13.9 us
    ppermute x30, starting transfers between devices: 24.3 us -> 27.6 us  [swap(): return lax.ppermute(x, 'exp', [(i, i ^ bits) for i in range(n_dev)])]
    ppermute x30, waiting for transfers between devices: 15.5 us -> 13.9 us  [swap(): return lax.ppermute(x, 'exp', [(i, i ^ bits) for i in range(n_dev)])]
    pallas_call x17 -> x15, Pallas kernels: 16.3 us -> 16.3 us  [call(): pl.pallas_call(body_with_chain if reads_chain else body, out_shape=list(o...]
  transfers between devices with their start and end apart: 30 -> 30, of which waited for: 8 -> 7; matrix products, arithmetic and copies ran while one was open for 0% -> 0% of each run, Pallas kernels for 27% -> 26%
where the time goes in v19:
time: 58.9 us; the launch traced here: 58.7 us
  starting transfers between devices  27.6 us (47%)
  Pallas kernels  17.1 us (29%)
  waiting for transfers between devices  13.9 us (24%)
    ppermute x30, starting transfers between devices, swap(): return lax.ppermute(x, 'exp', [(i, i ^ bits) for i in range(n_dev)])  27.6 us
    pallas_call x15, Pallas kernels, call(): pl.pallas_call(body_with_chain if reads_chain else body, out_shape=list(o...  16.3 us
    ppermute x30, waiting for transfers between devices, swap(): return lax.ppermute(x, 'exp', [(i, i ^ bits) for i in range(n_dev)])  13.9 us
  transfers between devices with their start and end apart: 30, of which 7 were waited for; matrix products, arithmetic and copies ran while one was open for 0% of the time, Pallas kernels for 26%

profile of v19, /device:TPU:0, one launch (start us, length us, event | category | flops | bytes accessed | tf_op | source)
XLA Modules:
  0.0 58.7 jit_solution(5232909497052696118)
XLA Ops:
  0.0 0.9 %pack.1.refs_0_ = bf16[64,1152]{1,0:T(8,128)(2,1)S(1)} custom-call(s32[8,64]{1,0:T(8,128)} %bitcast.2, bf16[64,1024]{1,0:T(8,128)(2,1)} %refs_1_.2), custom_call_target="tpu_custom_call" | custom-call | bytes 10000 | tf_op jit(solution)/shard_map/pack/pallas_call | solution.py:201
  0.9 3.0 %collective-permute-start = (bf16[64,1152]{1,0:T(8,128)(2,1)S(1)}, bf16[64,1152]{1,0:T(8,128)(2,1)S(1)}, u32[]{:S(2)}, u32[]{:S(2)}) collective-permute-start(bf16[64,1152]{1,0:T(8,128)(2,1)S(1)} %pack.1.refs_0_), channel_id=1, source_target_pairs={{0,2},{1,3},{2,0},{3,1},{4,6},{5,7},{6,4},{7,5},{8,10},{9,11},{10,... | collective-permute-start | bytes 442376 | tf_op jit(solution)/shard_map/ppermute | solution.py:222
  4.0 2.6 %collective-permute-start.3 = (bf16[64,1152]{1,0:T(8,128)(2,1)S(1)}, bf16[64,1152]{1,0:T(8,128)(2,1)S(1)}, u32[]{:S(2)}, u32[]{:S(2)}) collective-permute-start(bf16[64,1152]{1,0:T(8,128)(2,1)S(1)} %pack.1.refs_0_), channel_id=1, source_target_pairs={{0,8},{1,9},{2,10},{3,11},{4,12},{5,13},{6,14},{7,15},{8,0},{9,1},... | collective-permute-start | bytes 442376 | tf_op jit(solution)/shard_map/ppermute | solution.py:222
  6.6 1.3 %collective-permute-done.refs_3_.refs_1_ = bf16[64,1152]{1,0:T(8,128)(2,1)S(1)} collective-permute-done((bf16[64,1152]{1,0:T(8,128)(2,1)S(1)}, bf16[64,1152]{1,0:T(8,128)(2,1)S(1)}, u32[]{:S(2)}, u32[]{:S(2)}) %collective-permute-start) | collective-permute-done | bytes 147488 | tf_op jit(solution)/shard_map/ppermute | solution.py:222
  7.8 1.8 %collective-permute-start.8 = (bf16[64,1152]{1,0:T(8,128)(2,1)S(1)}, bf16[64,1152]{1,0:T(8,128)(2,1)S(1)}, u32[]{:S(2)}, u32[]{:S(2)}) collective-permute-start(bf16[64,1152]{1,0:T(8,128)(2,1)S(1)} %collective-permute-done.refs_3_.refs_1_), channel_id=1, source_target_pairs={{0,4},{1,5},{2,6},{3,7},{4,0},{5,1},{6,2},{7,3},{8,12},{9,13},{10,... | collective-permute-start | bytes 442376 | tf_op jit(solution)/shard_map/ppermute | solution.py:222
  9.6 2.6 %collective-permute-start.6 = (bf16[64,1152]{1,0:T(8,128)(2,1)S(1)}, bf16[64,1152]{1,0:T(8,128)(2,1)S(1)}, u32[]{:S(2)}, u32[]{:S(2)}) collective-permute-start(bf16[64,1152]{1,0:T(8,128)(2,1)S(1)} %collective-permute-done.refs_3_.refs_1_), channel_id=1, source_target_pairs={{0,8},{1,9},{2,10},{3,11},{4,12},{5,13},{6,14},{7,15},{8,0},{9,1},... | collective-permute-start | bytes 442376 | tf_op jit(solution)/shard_map/ppermute | solution.py:222
  12.2 4.7 %load.1 = (bf16[1024,128]{1,0:T(8,128)(2,1)S(1)}, bf16[2,1024,2048]{2,1,0:T(8,128)(2,1)S(1)}, bf16[2,1024,1024]{2,1,0:T(8,128)(2,1)S(1)}) custom-call(bf16[2,1024]{1,0:T(2,128)(2,1)} %bitcast.3, bf16[2,1024,2048]{2,1,0:T(8,128)(2,1)} %refs_1_.3, bf16[2,1024,1024]{2,1,0:T(8,128)(2,1)} %refs_2_.1, bf16[64,1152]{1,0:T(8,128)(2,1)S(1)} %collective-permute-done.refs_3_.refs_1_), custom_call_target="tpu_custom_call" | custom-call | bytes 10000 | tf_op jit(solution)/shard_map/load/pallas_call | solution.py:201
  17.5 2.7 %expert.3 = (f32[128,1152]{1,0:T(8,128)S(1)}, bf16[64,1152]{1,0:T(8,128)(2,1)S(1)}, bf16[64,1152]{1,0:T(8,128)(2,1)S(1)}, bf16[1024,128]{1,0:T(8,128)(2,1)S(1)},...) custom-call(bf16[64,1152]{1,0:T(8,128)(2,1)S(1)} %pack.1.refs_0_, ...), custom_call_target="tpu_custom_call", output_to_operand_aliasing={{3}: (4, {}), {4}: (5, {}), {5}: (6, {})} | custom-call | bytes 10000 | tf_op jit(solution)/shard_map/expert/pallas_call | solution.py:201
  21.3 1.5 %collective-permute-done.7.refs_1_.refs_0_ = bf16[64,1152]{1,0:T(8,128)(2,1)S(1)} collective-permute-done((bf16[64,1152]{1,0:T(8,128)(2,1)S(1)}, bf16[64,1152]{1,0:T(8,128)(2,1)S(1)}, u32[]{:S(2)}, u32[]{:S(2)}) %collective-permute-start.7) | collective-permute-done | bytes 147488 | tf_op jit(solution)/shard_map/ppermute | solution.py:222
  23.2 1.7 %collective-permute-start.14 = (bf16[64,1152]{1,0:T(8,128)(2,1)S(1)}, bf16[64,1152]{1,0:T(8,128)(2,1)S(1)}, u32[]{:S(2)}, u32[]{:S(2)}) collective-permute-start(bf16[64,1152]{1,0:T(8,128)(2,1)S(1)} %collective-permute-done.6.refs_0_.refs_1_), channel_id=1, source_target_pairs={{0,4},{1,5},{2,6},{3,7},{4,0},{5,1},{6,2},{7,3},{8,12},{9,13},{10,... | collective-permute-start | bytes 442376 | tf_op jit(solution)/shard_map/ppermute | solution.py:222
  24.9 1.6 %collective-permute-start.9 = (bf16[64,1152]{1,0:T(8,128)(2,1)S(1)}, bf16[64,1152]{1,0:T(8,128)(2,1)S(1)}, u32[]{:S(2)}, u32[]{:S(2)}) collective-permute-start(bf16[64,1152]{1,0:T(8,128)(2,1)S(1)} %get-tuple-element.87), channel_id=1, source_target_pairs={{0,2},{1,3},{2,0},{3,1},{4,6},{5,7},{6,4},{7,5},{8,10},{9,11},{10,... | collective-permute-start | bytes 442376 | tf_op jit(solution)/shard_map/ppermute | solution.py:222
  26.5 2.7 %expert.4 = (f32[128,1152]{1,0:T(8,128)S(1)}, bf16[64,1152]{1,0:T(8,128)(2,1)S(1)}, bf16[64,1152]{1,0:T(8,128)(2,1)S(1)}, bf16[1024,128]{1,0:T(8,128)(2,1)S(1)},...) custom-call(bf16[64,1152]{1,0:T(8,128)(2,1)S(1)} %get-tuple-element., ...), custom_call_target="tpu_custom_call", output_to_operand_aliasing={{3}: (4, {}), {4}: (5, {}), {5}: (6, {})} | custom-call | bytes 10000 | tf_op jit(solution)/shard_map/expert/pallas_call | solution.py:201
  29.9 1.0 %collective-permute-done.14.refs_3_ = bf16[64,1152]{1,0:T(8,128)(2,1)S(1)} collective-permute-done((bf16[64,1152]{1,0:T(8,128)(2,1)S(1)}, bf16[64,1152]{1,0:T(8,128)(2,1)S(1)}, u32[]{:S(2)}, u32[]{:S(2)}) %collective-permute-start.14) | collective-permute-done | bytes 147488 | tf_op jit(solution)/shard_map/ppermute | solution.py:222
  31.6 1.6 %collective-permute-start.15 = (bf16[64,1152]{1,0:T(8,128)(2,1)S(1)}, bf16[64,1152]{1,0:T(8,128)(2,1)S(1)}, u32[]{:S(2)}, u32[]{:S(2)}) collective-permute-start(bf16[64,1152]{1,0:T(8,128)(2,1)S(1)} %get-tuple-element.101), channel_id=1, source_target_pairs={{0,2},{1,3},{2,0},{3,1},{4,6},{5,7},{6,4},{7,5},{8,10},{9,11},{10,... | collective-permute-start | bytes 442376 | tf_op jit(solution)/shard_map/ppermute | solution.py:222
  33.2 4.9 %expert.5 = (f32[128,1152]{1,0:T(8,128)S(1)}, f32[128,1152]{1,0:T(8,128)S(1)}, bf16[64,1152]{1,0:T(8,128)(2,1)S(1)}, bf16[64,1152]{1,0:T(8,128)(2,1)S(1)}, bf16[...) custom-call(bf16[64,1152]{1,0:T(8,128)(2,1)S(1)} %collective-permute, ...), custom_call_target="tpu_custom_call", output_to_operand_aliasing={{6}: (8, {}), {7}: (9, {}), {8}: (10, {})} | custom-call | bytes 10000 | tf_op jit(solution)/shard_map/expert/pallas_call | solution.py:201
  39.3 2.9 %collective-permute-start.21 = (bf16[64,1152]{1,0:T(8,128)(2,1)S(1)}, bf16[64,1152]{1,0:T(8,128)(2,1)S(1)}, u32[]{:S(2)}, u32[]{:S(2)}) collective-permute-start(bf16[64,1152]{1,0:T(8,128)(2,1)S(1)} %get-tuple-element.110), channel_id=1, source_target_pairs={{0,8},{1,9},{2,10},{3,11},{4,12},{5,13},{6,14},{7,15},{8,0},{9,1},... | collective-permute-start | bytes 442376 | tf_op jit(solution)/shard_map/ppermute | solution.py:222
  42.2 0.9 %collective-permute-start.24 = (bf16[64,1152]{1,0:T(8,128)(2,1)S(1)}, bf16[64,1152]{1,0:T(8,128)(2,1)S(1)}, u32[]{:S(2)}, u32[]{:S(2)}) collective-permute-start(bf16[64,1152]{1,0:T(8,128)(2,1)S(1)} %get-tuple-element.118), channel_id=1, source_target_pairs={{0,2},{1,3},{2,0},{3,1},{4,6},{5,7},{6,4},{7,5},{8,10},{9,11},{10,... | collective-permute-start | bytes 442376 | tf_op jit(solution)/shard_map/ppermute | solution.py:222
  43.2 1.2 %collective-permute-start.28 = (bf16[64,1152]{1,0:T(8,128)(2,1)S(1)}, bf16[64,1152]{1,0:T(8,128)(2,1)S(1)}, u32[]{:S(2)}, u32[]{:S(2)}) collective-permute-start(bf16[64,1152]{1,0:T(8,128)(2,1)S(1)} %get-tuple-element.130), channel_id=1, source_target_pairs={{0,2},{1,3},{2,0},{3,1},{4,6},{5,7},{6,4},{7,5},{8,10},{9,11},{10,... | collective-permute-start | bytes 442376 | tf_op jit(solution)/shard_map/ppermute | solution.py:222
  44.4 4.6 %collective-permute-done.24.refs_1_ = bf16[64,1152]{1,0:T(8,128)(2,1)S(1)} collective-permute-done((bf16[64,1152]{1,0:T(8,128)(2,1)S(1)}, bf16[64,1152]{1,0:T(8,128)(2,1)S(1)}, u32[]{:S(2)}, u32[]{:S(2)}) %collective-permute-start.24) | collective-permute-done | bytes 147488 | tf_op jit(solution)/shard_map/ppermute | solution.py:222
  49.0 1.6 %collective-permute-start.27 = (bf16[64,1152]{1,0:T(8,128)(2,1)S(1)}, bf16[64,1152]{1,0:T(8,128)(2,1)S(1)}, u32[]{:S(2)}, u32[]{:S(2)}) collective-permute-start(bf16[64,1152]{1,0:T(8,128)(2,1)S(1)} %get-tuple-element.128), channel_id=1, source_target_pairs={{0,12},{1,13},{2,14},{3,15},{4,8},{5,9},{6,10},{7,11},{8,4},{9,5},... | collective-permute-start | bytes 442376 | tf_op jit(solution)/shard_map/ppermute | solution.py:222
  51.1 1.8 %collective-permute-start.29 = (bf16[64,1152]{1,0:T(8,128)(2,1)S(1)}, bf16[64,1152]{1,0:T(8,128)(2,1)S(1)}, u32[]{:S(2)}, u32[]{:S(2)}) collective-permute-start(bf16[64,1152]{1,0:T(8,128)(2,1)S(1)} %get-tuple-element.134), channel_id=1, source_target_pairs={{0,4},{1,5},{2,6},{3,7},{4,0},{5,1},{6,2},{7,3},{8,12},{9,13},{10,... | collective-permute-start | bytes 442376 | tf_op jit(solution)/shard_map/ppermute | solution.py:222
  53.0 4.3 %collective-permute-done.27.refs_3_ = bf16[64,1152]{1,0:T(8,128)(2,1)S(1)} collective-permute-done((bf16[64,1152]{1,0:T(8,128)(2,1)S(1)}, bf16[64,1152]{1,0:T(8,128)(2,1)S(1)}, u32[]{:S(2)}, u32[]{:S(2)}) %collective-permute-start.27) | collective-permute-done | bytes 147488 | tf_op jit(solution)/shard_map/ppermute | solution.py:222
  57.3 0.7 %collective-permute-done.29.refs_4_ = bf16[64,1152]{1,0:T(8,128)(2,1)S(1)} collective-permute-done((bf16[64,1152]{1,0:T(8,128)(2,1)S(1)}, bf16[64,1152]{1,0:T(8,128)(2,1)S(1)}, u32[]{:S(2)}, u32[]{:S(2)}) %collective-permute-start.29) | collective-permute-done | bytes 147488 | tf_op jit(solution)/shard_map/ppermute | solution.py:222
  57.9 0.8 %finish.1 = bf16[64,1024]{1,0:T(8,128)(2,1)} custom-call(f32[64,1152]{1,0:T(8,128)S(1)} %get-tuple-element.86.refs_0_, bf16[64,1152]{1,0:T(8,128)(2,1)S(1)} %collective-permute-done.9.refs_3_.refs_1_, bf16[64,1152]{1,0:T(8,128)(2,1)S(1)} %collective-permute-done.21.refs_2_, bf16[64,1152]{1,0:T(8,128)(2,1)S(1)} %collective-permute-done.27.refs_3_, ...), custom_call_target="tpu_custom_call" | custom-call | tf_op jit(solution)/shard_map/finish/pallas_call | solution.py:318
  (52 shorter events, 5.1 us)
Async XLA Ops:
  0.9 6.9 %collective-permute-start = (bf16[64,1152]{1,0:T(8,128)(2,1)S(1)}, bf16[64,1152]{1,0:T(8,128)(2,1)S(1)}, u32[]{:S(2)}, u32[]{:S(2)}) collective-permute-start(bf16[64,1152]{1,0:T(8,128)(2,1)S(1)} %pack.1.refs_0_), channel_id=1, source_target_pairs={{0,2},{1,3},{2,0},{3,1},{4,6},{5,7},{6,4},{7,5},{8,10},{9,11},{10,... | collective-permute-start | bytes 442376 | tf_op jit(solution)/shard_map/ppermute | solution.py:222
  4.0 13.0 %collective-permute-start.3 = (bf16[64,1152]{1,0:T(8,128)(2,1)S(1)}, bf16[64,1152]{1,0:T(8,128)(2,1)S(1)}, u32[]{:S(2)}, u32[]{:S(2)}) collective-permute-start(bf16[64,1152]{1,0:T(8,128)(2,1)S(1)} %pack.1.refs_0_), channel_id=1, source_target_pairs={{0,8},{1,9},{2,10},{3,11},{4,12},{5,13},{6,14},{7,15},{8,0},{9,1},... | collective-permute-start | bytes 442376 | tf_op jit(solution)/shard_map/ppermute | solution.py:222
  6.6 10.9 %collective-permute-start.1 = (bf16[64,1152]{1,0:T(8,128)(2,1)S(1)}, bf16[64,1152]{1,0:T(8,128)(2,1)S(1)}, u32[]{:S(2)}, u32[]{:S(2)}) collective-permute-start(bf16[64,1152]{1,0:T(8,128)(2,1)S(1)} %pack.1.refs_0_), channel_id=1, source_target_pairs={{0,1},{1,0},{2,3},{3,2},{4,5},{5,4},{6,7},{7,6},{8,9},{9,8},{10,11... | collective-permute-start | bytes 442376 | tf_op jit(solution)/shard_map/ppermute | solution.py:222
  7.8 9.7 %collective-permute-start.2 = (bf16[64,1152]{1,0:T(8,128)(2,1)S(1)}, bf16[64,1152]{1,0:T(8,128)(2,1)S(1)}, u32[]{:S(2)}, u32[]{:S(2)}) collective-permute-start(bf16[64,1152]{1,0:T(8,128)(2,1)S(1)} %collective-permute-done.refs_3_.refs_1_), channel_id=1, source_target_pairs={{0,1},{1,0},{2,3},{3,2},{4,5},{5,4},{6,7},{7,6},{8,9},{9,8},{10,11... | collective-permute-start | bytes 442376 | tf_op jit(solution)/shard_map/ppermute | solution.py:222
  7.8 12.9 %collective-permute-start.8 = (bf16[64,1152]{1,0:T(8,128)(2,1)S(1)}, bf16[64,1152]{1,0:T(8,128)(2,1)S(1)}, u32[]{:S(2)}, u32[]{:S(2)}) collective-permute-start(bf16[64,1152]{1,0:T(8,128)(2,1)S(1)} %collective-permute-done.refs_3_.refs_1_), channel_id=1, source_target_pairs={{0,4},{1,5},{2,6},{3,7},{4,0},{5,1},{6,2},{7,3},{8,12},{9,13},{10,... | collective-permute-start | bytes 442376 | tf_op jit(solution)/shard_map/ppermute | solution.py:222
  9.6 11.2 %collective-permute-start.6 = (bf16[64,1152]{1,0:T(8,128)(2,1)S(1)}, bf16[64,1152]{1,0:T(8,128)(2,1)S(1)}, u32[]{:S(2)}, u32[]{:S(2)}) collective-permute-start(bf16[64,1152]{1,0:T(8,128)(2,1)S(1)} %collective-permute-done.refs_3_.refs_1_), channel_id=1, source_target_pairs={{0,8},{1,9},{2,10},{3,11},{4,12},{5,13},{6,14},{7,15},{8,0},{9,1},... | collective-permute-start | bytes 442376 | tf_op jit(solution)/shard_map/ppermute | solution.py:222
  17.0 5.9 %collective-permute-start.7 = (bf16[64,1152]{1,0:T(8,128)(2,1)S(1)}, bf16[64,1152]{1,0:T(8,128)(2,1)S(1)}, u32[]{:S(2)}, u32[]{:S(2)}) collective-permute-start(bf16[64,1152]{1,0:T(8,128)(2,1)S(1)} %get-tuple-element.79.refs_0_), channel_id=1, source_target_pairs={{0,4},{1,5},{2,6},{3,7},{4,0},{5,1},{6,2},{7,3},{8,12},{9,13},{10,... | collective-permute-start | bytes 442376 | tf_op jit(solution)/shard_map/ppermute | solution.py:222
  20.3 4.6 %collective-permute-start.5 = (bf16[64,1152]{1,0:T(8,128)(2,1)S(1)}, bf16[64,1152]{1,0:T(8,128)(2,1)S(1)}, u32[]{:S(2)}, u32[]{:S(2)}) collective-permute-start(bf16[64,1152]{1,0:T(8,128)(2,1)S(1)} %get-tuple-element.78), channel_id=1, source_target_pairs={{0,1},{1,0},{2,3},{3,2},{4,5},{5,4},{6,7},{7,6},{8,9},{9,8},{10,11... | collective-permute-start | bytes 442376 | tf_op jit(solution)/shard_map/ppermute | solution.py:222
  20.8 5.7 %collective-permute-start.10 = (bf16[64,1152]{1,0:T(8,128)(2,1)S(1)}, bf16[64,1152]{1,0:T(8,128)(2,1)S(1)}, u32[]{:S(2)}, u32[]{:S(2)}) collective-permute-start(bf16[64,1152]{1,0:T(8,128)(2,1)S(1)} %get-tuple-element.79.refs_0_), channel_id=1, source_target_pairs={{0,1},{1,0},{2,3},{3,2},{4,5},{5,4},{6,7},{7,6},{8,9},{9,8},{10,11... | collective-permute-start | bytes 442376 | tf_op jit(solution)/shard_map/ppermute | solution.py:222
  20.9 5.6 %collective-permute-start.11 = (bf16[64,1152]{1,0:T(8,128)(2,1)S(1)}, bf16[64,1152]{1,0:T(8,128)(2,1)S(1)}, u32[]{:S(2)}, u32[]{:S(2)}) collective-permute-start(bf16[64,1152]{1,0:T(8,128)(2,1)S(1)} %collective-permute-done.6.refs_0_.refs_1_), channel_id=1, source_target_pairs={{0,1},{1,0},{2,3},{3,2},{4,5},{5,4},{6,7},{7,6},{8,9},{9,8},{10,11... | collective-permute-start | bytes 442376 | tf_op jit(solution)/shard_map/ppermute | solution.py:222
  22.8 6.5 %collective-permute-start.18 = (bf16[64,1152]{1,0:T(8,128)(2,1)S(1)}, bf16[64,1152]{1,0:T(8,128)(2,1)S(1)}, u32[]{:S(2)}, u32[]{:S(2)}) collective-permute-start(bf16[64,1152]{1,0:T(8,128)(2,1)S(1)} %pack.1.refs_0_), channel_id=1, source_target_pairs={{0,4},{1,5},{2,6},{3,7},{4,0},{5,1},{6,2},{7,3},{8,12},{9,13},{10,... | collective-permute-start | bytes 442376 | tf_op jit(solution)/shard_map/ppermute | solution.py:222
  23.2 7.7 %collective-permute-start.14 = (bf16[64,1152]{1,0:T(8,128)(2,1)S(1)}, bf16[64,1152]{1,0:T(8,128)(2,1)S(1)}, u32[]{:S(2)}, u32[]{:S(2)}) collective-permute-start(bf16[64,1152]{1,0:T(8,128)(2,1)S(1)} %collective-permute-done.6.refs_0_.refs_1_), channel_id=1, source_target_pairs={{0,4},{1,5},{2,6},{3,7},{4,0},{5,1},{6,2},{7,3},{8,12},{9,13},{10,... | collective-permute-start | bytes 442376 | tf_op jit(solution)/shard_map/ppermute | solution.py:222
  24.9 6.0 %collective-permute-start.9 = (bf16[64,1152]{1,0:T(8,128)(2,1)S(1)}, bf16[64,1152]{1,0:T(8,128)(2,1)S(1)}, u32[]{:S(2)}, u32[]{:S(2)}) collective-permute-start(bf16[64,1152]{1,0:T(8,128)(2,1)S(1)} %get-tuple-element.87), channel_id=1, source_target_pairs={{0,2},{1,3},{2,0},{3,1},{4,6},{5,7},{6,4},{7,5},{8,10},{9,11},{10,... | collective-permute-start | bytes 442376 | tf_op jit(solution)/shard_map/ppermute | solution.py:222
  29.3 3.8 %collective-permute-start.19 = (bf16[64,1152]{1,0:T(8,128)(2,1)S(1)}, bf16[64,1152]{1,0:T(8,128)(2,1)S(1)}, u32[]{:S(2)}, u32[]{:S(2)}) collective-permute-start(bf16[64,1152]{1,0:T(8,128)(2,1)S(1)} %collective-permute-done.18.refs_4_), channel_id=1, source_target_pairs={{0,1},{1,0},{2,3},{3,2},{4,5},{5,4},{6,7},{7,6},{8,9},{9,8},{10,11... | collective-permute-start | bytes 442376 | tf_op jit(solution)/shard_map/ppermute | solution.py:222
  31.6 7.7 %collective-permute-start.15 = (bf16[64,1152]{1,0:T(8,128)(2,1)S(1)}, bf16[64,1152]{1,0:T(8,128)(2,1)S(1)}, u32[]{:S(2)}, u32[]{:S(2)}) collective-permute-start(bf16[64,1152]{1,0:T(8,128)(2,1)S(1)} %get-tuple-element.101), channel_id=1, source_target_pairs={{0,2},{1,3},{2,0},{3,1},{4,6},{5,7},{6,4},{7,5},{8,10},{9,11},{10,... | collective-permute-start | bytes 442376 | tf_op jit(solution)/shard_map/ppermute | solution.py:222
  38.1 4.0 %collective-permute-start.22 = (bf16[64,1152]{1,0:T(8,128)(2,1)S(1)}, bf16[64,1152]{1,0:T(8,128)(2,1)S(1)}, u32[]{:S(2)}, u32[]{:S(2)}) collective-permute-start(bf16[64,1152]{1,0:T(8,128)(2,1)S(1)} %get-tuple-element.112), channel_id=1, source_target_pairs={{0,1},{1,0},{2,3},{3,2},{4,5},{5,4},{6,7},{7,6},{8,9},{9,8},{10,11... | collective-permute-start | bytes 442376 | tf_op jit(solution)/shard_map/ppermute | solution.py:222
  38.4 3.8 %collective-permute-start.23 = (bf16[64,1152]{1,0:T(8,128)(2,1)S(1)}, bf16[64,1152]{1,0:T(8,128)(2,1)S(1)}, u32[]{:S(2)}, u32[]{:S(2)}) collective-permute-start(bf16[64,1152]{1,0:T(8,128)(2,1)S(1)} %get-tuple-element.113), channel_id=1, source_target_pairs={{0,1},{1,0},{2,3},{3,2},{4,5},{5,4},{6,7},{7,6},{8,9},{9,8},{10,11... | collective-permute-start | bytes 442376 | tf_op jit(solution)/shard_map/ppermute | solution.py:222
  38.7 4.4 %collective-permute-start.25 = (bf16[64,1152]{1,0:T(8,128)(2,1)S(1)}, bf16[64,1152]{1,0:T(8,128)(2,1)S(1)}, u32[]{:S(2)}, u32[]{:S(2)}) collective-permute-start(bf16[64,1152]{1,0:T(8,128)(2,1)S(1)} %get-tuple-element.120), channel_id=1, source_target_pairs={{0,1},{1,0},{2,3},{3,2},{4,5},{5,4},{6,7},{7,6},{8,9},{9,8},{10,11... | collective-permute-start | bytes 442376 | tf_op jit(solution)/shard_map/ppermute | solution.py:222
  38.9 4.3 %collective-permute-start.26 = (bf16[64,1152]{1,0:T(8,128)(2,1)S(1)}, bf16[64,1152]{1,0:T(8,128)(2,1)S(1)}, u32[]{:S(2)}, u32[]{:S(2)}) collective-permute-start(bf16[64,1152]{1,0:T(8,128)(2,1)S(1)} %get-tuple-element.121), channel_id=1, source_target_pairs={{0,1},{1,0},{2,3},{3,2},{4,5},{5,4},{6,7},{7,6},{8,9},{9,8},{10,11... | collective-permute-start | bytes 442376 | tf_op jit(solution)/shard_map/ppermute | solution.py:222
  39.3 11.4 %collective-permute-start.21 = (bf16[64,1152]{1,0:T(8,128)(2,1)S(1)}, bf16[64,1152]{1,0:T(8,128)(2,1)S(1)}, u32[]{:S(2)}, u32[]{:S(2)}) collective-permute-start(bf16[64,1152]{1,0:T(8,128)(2,1)S(1)} %get-tuple-element.110), channel_id=1, source_target_pairs={{0,8},{1,9},{2,10},{3,11},{4,12},{5,13},{6,14},{7,15},{8,0},{9,1},... | collective-permute-start | bytes 442376 | tf_op jit(solution)/shard_map/ppermute | solution.py:222
  42.2 6.8 %collective-permute-start.24 = (bf16[64,1152]{1,0:T(8,128)(2,1)S(1)}, bf16[64,1152]{1,0:T(8,128)(2,1)S(1)}, u32[]{:S(2)}, u32[]{:S(2)}) collective-permute-start(bf16[64,1152]{1,0:T(8,128)(2,1)S(1)} %get-tuple-element.118), channel_id=1, source_target_pairs={{0,2},{1,3},{2,0},{3,1},{4,6},{5,7},{6,4},{7,5},{8,10},{9,11},{10,... | collective-permute-start | bytes 442376 | tf_op jit(solution)/shard_map/ppermute | solution.py:222
  43.2 7.9 %collective-permute-start.28 = (bf16[64,1152]{1,0:T(8,128)(2,1)S(1)}, bf16[64,1152]{1,0:T(8,128)(2,1)S(1)}, u32[]{:S(2)}, u32[]{:S(2)}) collective-permute-start(bf16[64,1152]{1,0:T(8,128)(2,1)S(1)} %get-tuple-element.130), channel_id=1, source_target_pairs={{0,2},{1,3},{2,0},{3,1},{4,6},{5,7},{6,4},{7,5},{8,10},{9,11},{10,... | collective-permute-start | bytes 442376 | tf_op jit(solution)/shard_map/ppermute | solution.py:222
  49.0 8.2 %collective-permute-start.27 = (bf16[64,1152]{1,0:T(8,128)(2,1)S(1)}, bf16[64,1152]{1,0:T(8,128)(2,1)S(1)}, u32[]{:S(2)}, u32[]{:S(2)}) collective-permute-start(bf16[64,1152]{1,0:T(8,128)(2,1)S(1)} %get-tuple-element.128), channel_id=1, source_target_pairs={{0,12},{1,13},{2,14},{3,15},{4,8},{5,9},{6,10},{7,11},{8,4},{9,5},... | collective-permute-start | bytes 442376 | tf_op jit(solution)/shard_map/ppermute | solution.py:222
  51.1 6.8 %collective-permute-start.29 = (bf16[64,1152]{1,0:T(8,128)(2,1)S(1)}, bf16[64,1152]{1,0:T(8,128)(2,1)S(1)}, u32[]{:S(2)}, u32[]{:S(2)}) collective-permute-start(bf16[64,1152]{1,0:T(8,128)(2,1)S(1)} %get-tuple-element.134), channel_id=1, source_target_pairs={{0,4},{1,5},{2,6},{3,7},{4,0},{5,1},{6,2},{7,3},{8,12},{9,13},{10,... | collective-permute-start | bytes 442376 | tf_op jit(solution)/shard_map/ppermute | solution.py:222
  (6 other events, 13.2 us)

commit v20 on v15

--- a/solution.py
+++ b/solution.py
@@ -299,12 +299,14 @@
         gather(3)
         reduce_core(2)
         compute(3)
-        reduce_core(3, [y_came[2]])
-        compute(1, 0)
+        other[0] = tie(other[0], [y_came[2]])
+        reduce_core(3)
+        compute(1)
         z_3 = swap(reduce_y(3), 4)
+        compute(0)
         reduce_core(1)
+        z_2 = swap(reduce_y(2, z_3), 8)
         reduce_core(0)
-        z_2 = swap(reduce_y(2, z_3), 8)
         z_1 = swap(reduce_y(1), 4)
         return fold_keep[0], z_2, z_1, y_came[0]
 

time: 56.7 us -> 56.8 us (level)
    pallas_call x16 -> x18, Pallas kernels: 16.3 us -> 16.7 us  [call(): pl.pallas_call(body_with_chain if reads_chain else body, out_shape=list(o...]
  transfers between devices with their start and end apart: 30 -> 30, of which waited for: 10 -> 12; matrix products, arithmetic and copies ran while one was open for 0% -> 0% of each run, Pallas kernels for 27% -> 28%
where the time goes in v20:
time: 56.8 us; the launch traced here: 56.6 us
  starting transfers between devices  24 us (42%)
  Pallas kernels  17.5 us (31%)
  waiting for transfers between devices  15 us (26%)
    ppermute x30, starting transfers between devices, swap(): return lax.ppermute(x, 'exp', [(i, i ^ bits) for i in range(n_dev)])  24 us
    pallas_call x18, Pallas kernels, call(): pl.pallas_call(body_with_chain if reads_chain else body, out_shape=list(o...  16.7 us
    ppermute x30, waiting for transfers between devices, swap(): return lax.ppermute(x, 'exp', [(i, i ^ bits) for i in range(n_dev)])  15 us
  transfers between devices with their start and end apart: 30, of which 12 were waited for; matrix products, arithmetic and copies ran while one was open for 0% of the time, Pallas kernels for 28%

profile of v20, /device:TPU:0, one launch (start us, length us, event | category | flops | bytes accessed | tf_op | source)
XLA Modules:
  0.0 56.6 jit_solution(28345434662563617)
XLA Ops:
  0.0 0.9 %pack.1.refs_3_.refs_0_ = bf16[64,1152]{1,0:T(8,128)(2,1)S(1)} custom-call(s32[8,64]{1,0:T(8,128)} %bitcast.2, bf16[64,1024]{1,0:T(8,128)(2,1)} %refs_1_.2), custom_call_target="tpu_custom_call" | custom-call | bytes 10000 | tf_op jit(solution)/shard_map/pack/pallas_call | solution.py:201
  0.9 4.1 %collective-permute-start = (bf16[64,1152]{1,0:T(8,128)(2,1)S(1)}, bf16[64,1152]{1,0:T(8,128)(2,1)S(1)}, u32[]{:S(2)}, u32[]{:S(2)}) collective-permute-start(bf16[64,1152]{1,0:T(8,128)(2,1)S(1)} %pack.1.refs_3_.refs_0_), channel_id=1, source_target_pairs={{0,8},{1,9},{2,10},{3,11},{4,12},{5,13},{6,14},{7,15},{8,0},{9,1},... | collective-permute-start | bytes 442376 | tf_op jit(solution)/shard_map/ppermute | solution.py:222
  5.0 1.5 %collective-permute-start.3 = (bf16[64,1152]{1,0:T(8,128)(2,1)S(1)}, bf16[64,1152]{1,0:T(8,128)(2,1)S(1)}, u32[]{:S(2)}, u32[]{:S(2)}) collective-permute-start(bf16[64,1152]{1,0:T(8,128)(2,1)S(1)} %pack.1.refs_3_.refs_0_), channel_id=1, source_target_pairs={{0,2},{1,3},{2,0},{3,1},{4,6},{5,7},{6,4},{7,5},{8,10},{9,11},{10,... | collective-permute-start | bytes 442376 | tf_op jit(solution)/shard_map/ppermute | solution.py:222
  6.6 1.6 %collective-permute-start.1 = (bf16[64,1152]{1,0:T(8,128)(2,1)S(1)}, bf16[64,1152]{1,0:T(8,128)(2,1)S(1)}, u32[]{:S(2)}, u32[]{:S(2)}) collective-permute-start(bf16[64,1152]{1,0:T(8,128)(2,1)S(1)} %pack.1.refs_3_.refs_0_), channel_id=1, source_target_pairs={{0,4},{1,5},{2,6},{3,7},{4,0},{5,1},{6,2},{7,3},{8,12},{9,13},{10,... | collective-permute-start | bytes 442376 | tf_op jit(solution)/shard_map/ppermute | solution.py:222
  8.1 4.7 %load.1 = (bf16[1024,128]{1,0:T(8,128)(2,1)S(1)}, bf16[2,1024,2048]{2,1,0:T(8,128)(2,1)S(1)}, bf16[2,1024,1024]{2,1,0:T(8,128)(2,1)S(1)}) custom-call(bf16[2,1024]{1,0:T(2,128)(2,1)} %bitcast.3, bf16[2,1024,2048]{2,1,0:T(8,128)(2,1)} %refs_1_.3, bf16[2,1024,1024]{2,1,0:T(8,128)(2,1)} %refs_2_.1, bf16[64,1152]{1,0:T(8,128)(2,1)S(1)} %pack.1.refs_3_.refs_0_), custom_call_target="tpu_custom_call" | custom-call | bytes 10000 | tf_op jit(solution)/shard_map/load/pallas_call | solution.py:201
  14.3 1.1 %collective-permute-start.7 = (bf16[64,1152]{1,0:T(8,128)(2,1)S(1)}, bf16[64,1152]{1,0:T(8,128)(2,1)S(1)}, u32[]{:S(2)}, u32[]{:S(2)}) collective-permute-start(bf16[64,1152]{1,0:T(8,128)(2,1)S(1)} %collective-permute-done.1.refs_0_), channel_id=1, source_target_pairs={{0,2},{1,3},{2,0},{3,1},{4,6},{5,7},{6,4},{7,5},{8,10},{9,11},{10,... | collective-permute-start | bytes 442376 | tf_op jit(solution)/shard_map/ppermute | solution.py:222
  15.4 3.4 %collective-permute-done.4.refs_6_ = bf16[64,1152]{1,0:T(8,128)(2,1)S(1)} collective-permute-done((bf16[64,1152]{1,0:T(8,128)(2,1)S(1)}, bf16[64,1152]{1,0:T(8,128)(2,1)S(1)}, u32[]{:S(2)}, u32[]{:S(2)}) %collective-permute-start.4) | collective-permute-done | bytes 147488 | tf_op jit(solution)/shard_map/ppermute | solution.py:222
  18.9 1.3 %collective-permute-start.10 = (bf16[64,1152]{1,0:T(8,128)(2,1)S(1)}, bf16[64,1152]{1,0:T(8,128)(2,1)S(1)}, u32[]{:S(2)}, u32[]{:S(2)}) collective-permute-start(bf16[64,1152]{1,0:T(8,128)(2,1)S(1)} %collective-permute-done.2.refs_1_.refs_0_), channel_id=1, source_target_pairs={{0,2},{1,3},{2,0},{3,1},{4,6},{5,7},{6,4},{7,5},{8,10},{9,11},{10,... | collective-permute-start | bytes 442376 | tf_op jit(solution)/shard_map/ppermute | solution.py:222
  20.1 1.1 %collective-permute-done.7.refs_3_ = bf16[64,1152]{1,0:T(8,128)(2,1)S(1)} collective-permute-done((bf16[64,1152]{1,0:T(8,128)(2,1)S(1)}, bf16[64,1152]{1,0:T(8,128)(2,1)S(1)}, u32[]{:S(2)}, u32[]{:S(2)}) %collective-permute-start.7) | collective-permute-done | bytes 147488 | tf_op jit(solution)/shard_map/ppermute | solution.py:222
  21.3 2.7 %expert.4 = (f32[128,1152]{1,0:T(8,128)S(1)}, bf16[64,1152]{1,0:T(8,128)(2,1)S(1)}, bf16[64,1152]{1,0:T(8,128)(2,1)S(1)}, bf16[1024,128]{1,0:T(8,128)(2,1)S(1)},...) custom-call(bf16[64,1152]{1,0:T(8,128)(2,1)S(1)} %get-tuple-element., ...), custom_call_target="tpu_custom_call", output_to_operand_aliasing={{3}: (4, {}), {4}: (5, {}), {5}: (6, {})} | custom-call | bytes 10000 | tf_op jit(solution)/shard_map/expert/pallas_call | solution.py:201
  26.5 2.7 %expert.5 = (f32[128,1152]{1,0:T(8,128)S(1)}, bf16[64,1152]{1,0:T(8,128)(2,1)S(1)}, bf16[64,1152]{1,0:T(8,128)(2,1)S(1)}, bf16[1024,128]{1,0:T(8,128)(2,1)S(1)},...) custom-call(bf16[64,1152]{1,0:T(8,128)(2,1)S(1)} %collective-permute, ...), custom_call_target="tpu_custom_call", output_to_operand_aliasing={{3}: (4, {}), {4}: (5, {}), {5}: (6, {})} | custom-call | bytes 10000 | tf_op jit(solution)/shard_map/expert/pallas_call | solution.py:201
  30.3 1.4 %collective-permute-done.11.refs_0_.refs_1_ = bf16[64,1152]{1,0:T(8,128)(2,1)S(1)} collective-permute-done((bf16[64,1152]{1,0:T(8,128)(2,1)S(1)}, bf16[64,1152]{1,0:T(8,128)(2,1)S(1)}, u32[]{:S(2)}, u32[]{:S(2)}) %collective-permute-start.11) | collective-permute-done | bytes 147488 | tf_op jit(solution)/shard_map/ppermute | solution.py:222
  31.8 1.1 %collective-permute-start.18 = (bf16[64,1152]{1,0:T(8,128)(2,1)S(1)}, bf16[64,1152]{1,0:T(8,128)(2,1)S(1)}, u32[]{:S(2)}, u32[]{:S(2)}) collective-permute-start(bf16[64,1152]{1,0:T(8,128)(2,1)S(1)} %get-tuple-element.120), channel_id=1, source_target_pairs={{0,2},{1,3},{2,0},{3,1},{4,6},{5,7},{6,4},{7,5},{8,10},{9,11},{10,... | collective-permute-start | bytes 442376 | tf_op jit(solution)/shard_map/ppermute | solution.py:222
  33.4 2.7 %expert.6 = (f32[128,1152]{1,0:T(8,128)S(1)}, bf16[64,1152]{1,0:T(8,128)(2,1)S(1)}, bf16[64,1152]{1,0:T(8,128)(2,1)S(1)}, bf16[1024,128]{1,0:T(8,128)(2,1)S(1)},...) custom-call(bf16[64,1152]{1,0:T(8,128)(2,1)S(1)} %collective-permute, ...), custom_call_target="tpu_custom_call", output_to_operand_aliasing={{3}: (4, {}), {4}: (5, {}), {5}: (6, {})} | custom-call | bytes 10000 | tf_op jit(solution)/shard_map/expert/pallas_call | solution.py:201
  37.2 1.2 %collective-permute-start.23 = (bf16[64,1152]{1,0:T(8,128)(2,1)S(1)}, bf16[64,1152]{1,0:T(8,128)(2,1)S(1)}, u32[]{:S(2)}, u32[]{:S(2)}) collective-permute-start(bf16[64,1152]{1,0:T(8,128)(2,1)S(1)} %get-tuple-element.135), channel_id=1, source_target_pairs={{0,4},{1,5},{2,6},{3,7},{4,0},{5,1},{6,2},{7,3},{8,12},{9,13},{10,... | collective-permute-start | bytes 442376 | tf_op jit(solution)/shard_map/ppermute | solution.py:222
  38.4 2.7 %expert.7 = (f32[128,1152]{1,0:T(8,128)S(1)}, bf16[64,1152]{1,0:T(8,128)(2,1)S(1)}, bf16[64,1152]{1,0:T(8,128)(2,1)S(1)}, bf16[1024,128]{1,0:T(8,128)(2,1)S(1)},...) custom-call(bf16[64,1152]{1,0:T(8,128)(2,1)S(1)} %pack.1.refs_3_.ref, ...), custom_call_target="tpu_custom_call", output_to_operand_aliasing={{3}: (4, {}), {4}: (5, {}), {5}: (6, {})} | custom-call | bytes 10000 | tf_op jit(solution)/shard_map/expert/pallas_call | solution.py:201
  41.7 1.0 %collective-permute-start.27 = (bf16[64,1152]{1,0:T(8,128)(2,1)S(1)}, bf16[64,1152]{1,0:T(8,128)(2,1)S(1)}, u32[]{:S(2)}, u32[]{:S(2)}) collective-permute-start(bf16[64,1152]{1,0:T(8,128)(2,1)S(1)} %get-tuple-element.151), channel_id=1, source_target_pairs={{0,2},{1,3},{2,0},{3,1},{4,6},{5,7},{6,4},{7,5},{8,10},{9,11},{10,... | collective-permute-start | bytes 442376 | tf_op jit(solution)/shard_map/ppermute | solution.py:222
  42.8 1.2 %collective-permute-start.29 = (bf16[64,1152]{1,0:T(8,128)(2,1)S(1)}, bf16[64,1152]{1,0:T(8,128)(2,1)S(1)}, u32[]{:S(2)}, u32[]{:S(2)}) collective-permute-start(bf16[64,1152]{1,0:T(8,128)(2,1)S(1)} %get-tuple-element.156), channel_id=1, source_target_pairs={{0,2},{1,3},{2,0},{3,1},{4,6},{5,7},{6,4},{7,5},{8,10},{9,11},{10,... | collective-permute-start | bytes 442376 | tf_op jit(solution)/shard_map/ppermute | solution.py:222
  44.0 3.3 %collective-permute-start.26 = (bf16[64,1152]{1,0:T(8,128)(2,1)S(1)}, bf16[64,1152]{1,0:T(8,128)(2,1)S(1)}, u32[]{:S(2)}, u32[]{:S(2)}) collective-permute-start(bf16[64,1152]{1,0:T(8,128)(2,1)S(1)} %get-tuple-element.149), channel_id=1, source_target_pairs={{0,8},{1,9},{2,10},{3,11},{4,12},{5,13},{6,14},{7,15},{8,0},{9,1},... | collective-permute-start | bytes 442376 | tf_op jit(solution)/shard_map/ppermute | solution.py:222
  47.3 1.1 %collective-permute-done.27.refs_1_ = bf16[64,1152]{1,0:T(8,128)(2,1)S(1)} collective-permute-done((bf16[64,1152]{1,0:T(8,128)(2,1)S(1)}, bf16[64,1152]{1,0:T(8,128)(2,1)S(1)}, u32[]{:S(2)}, u32[]{:S(2)}) %collective-permute-start.27) | collective-permute-done | bytes 147488 | tf_op jit(solution)/shard_map/ppermute | solution.py:222
  48.5 1.0 %collective-permute-start.28 = (bf16[64,1152]{1,0:T(8,128)(2,1)S(1)}, bf16[64,1152]{1,0:T(8,128)(2,1)S(1)}, u32[]{:S(2)}, u32[]{:S(2)}) collective-permute-start(bf16[64,1152]{1,0:T(8,128)(2,1)S(1)} %get-tuple-element.155), channel_id=1, source_target_pairs={{0,4},{1,5},{2,6},{3,7},{4,0},{5,1},{6,2},{7,3},{8,12},{9,13},{10,... | collective-permute-start | bytes 442376 | tf_op jit(solution)/shard_map/ppermute | solution.py:222
  49.5 1.3 %collective-permute-done.29.refs_3_ = bf16[64,1152]{1,0:T(8,128)(2,1)S(1)} collective-permute-done((bf16[64,1152]{1,0:T(8,128)(2,1)S(1)}, bf16[64,1152]{1,0:T(8,128)(2,1)S(1)}, u32[]{:S(2)}, u32[]{:S(2)}) %collective-permute-start.29) | collective-permute-done | bytes 147488 | tf_op jit(solution)/shard_map/ppermute | solution.py:222
  50.8 3.6 %collective-permute-done.26.refs_1_ = bf16[64,1152]{1,0:T(8,128)(2,1)S(1)} collective-permute-done((bf16[64,1152]{1,0:T(8,128)(2,1)S(1)}, bf16[64,1152]{1,0:T(8,128)(2,1)S(1)}, u32[]{:S(2)}, u32[]{:S(2)}) %collective-permute-start.26) | collective-permute-done | bytes 147488 | tf_op jit(solution)/shard_map/ppermute | solution.py:222
  54.4 1.5 %collective-permute-done.28.refs_2_ = bf16[64,1152]{1,0:T(8,128)(2,1)S(1)} collective-permute-done((bf16[64,1152]{1,0:T(8,128)(2,1)S(1)}, bf16[64,1152]{1,0:T(8,128)(2,1)S(1)}, u32[]{:S(2)}, u32[]{:S(2)}) %collective-permute-start.28) | collective-permute-done | bytes 147488 | tf_op jit(solution)/shard_map/ppermute | solution.py:222
  (55 shorter events, 8.3 us)
Async XLA Ops:
  0.9 11.9 %collective-permute-start = (bf16[64,1152]{1,0:T(8,128)(2,1)S(1)}, bf16[64,1152]{1,0:T(8,128)(2,1)S(1)}, u32[]{:S(2)}, u32[]{:S(2)}) collective-permute-start(bf16[64,1152]{1,0:T(8,128)(2,1)S(1)} %pack.1.refs_3_.refs_0_), channel_id=1, source_target_pairs={{0,8},{1,9},{2,10},{3,11},{4,12},{5,13},{6,14},{7,15},{8,0},{9,1},... | collective-permute-start | bytes 442376 | tf_op jit(solution)/shard_map/ppermute | solution.py:222
  5.0 10.4 %collective-permute-start.3 = (bf16[64,1152]{1,0:T(8,128)(2,1)S(1)}, bf16[64,1152]{1,0:T(8,128)(2,1)S(1)}, u32[]{:S(2)}, u32[]{:S(2)}) collective-permute-start(bf16[64,1152]{1,0:T(8,128)(2,1)S(1)} %pack.1.refs_3_.refs_0_), channel_id=1, source_target_pairs={{0,2},{1,3},{2,0},{3,1},{4,6},{5,7},{6,4},{7,5},{8,10},{9,11},{10,... | collective-permute-start | bytes 442376 | tf_op jit(solution)/shard_map/ppermute | solution.py:222
  6.6 7.7 %collective-permute-start.1 = (bf16[64,1152]{1,0:T(8,128)(2,1)S(1)}, bf16[64,1152]{1,0:T(8,128)(2,1)S(1)}, u32[]{:S(2)}, u32[]{:S(2)}) collective-permute-start(bf16[64,1152]{1,0:T(8,128)(2,1)S(1)} %pack.1.refs_3_.refs_0_), channel_id=1, source_target_pairs={{0,4},{1,5},{2,6},{3,7},{4,0},{5,1},{6,2},{7,3},{8,12},{9,13},{10,... | collective-permute-start | bytes 442376 | tf_op jit(solution)/shard_map/ppermute | solution.py:222
  12.9 5.9 %collective-permute-start.4 = (bf16[64,1152]{1,0:T(8,128)(2,1)S(1)}, bf16[64,1152]{1,0:T(8,128)(2,1)S(1)}, u32[]{:S(2)}, u32[]{:S(2)}) collective-permute-start(bf16[64,1152]{1,0:T(8,128)(2,1)S(1)} %get-tuple-element.84.refs_0_), channel_id=1, source_target_pairs={{0,2},{1,3},{2,0},{3,1},{4,6},{5,7},{6,4},{7,5},{8,10},{9,11},{10,... | collective-permute-start | bytes 442376 | tf_op jit(solution)/shard_map/ppermute | solution.py:222
  13.7 5.1 %collective-permute-start.2 = (bf16[64,1152]{1,0:T(8,128)(2,1)S(1)}, bf16[64,1152]{1,0:T(8,128)(2,1)S(1)}, u32[]{:S(2)}, u32[]{:S(2)}) collective-permute-start(bf16[64,1152]{1,0:T(8,128)(2,1)S(1)} %get-tuple-element.84.refs_0_), channel_id=1, source_target_pairs={{0,4},{1,5},{2,6},{3,7},{4,0},{5,1},{6,2},{7,3},{8,12},{9,13},{10,... | collective-permute-start | bytes 442376 | tf_op jit(solution)/shard_map/ppermute | solution.py:222
  14.3 7.0 %collective-permute-start.5 = (bf16[64,1152]{1,0:T(8,128)(2,1)S(1)}, bf16[64,1152]{1,0:T(8,128)(2,1)S(1)}, u32[]{:S(2)}, u32[]{:S(2)}) collective-permute-start(bf16[64,1152]{1,0:T(8,128)(2,1)S(1)} %get-tuple-element.84.refs_0_), channel_id=1, source_target_pairs={{0,1},{1,0},{2,3},{3,2},{4,5},{5,4},{6,7},{7,6},{8,9},{9,8},{10,11... | collective-permute-start | bytes 442376 | tf_op jit(solution)/shard_map/ppermute | solution.py:222
  14.3 7.0 %collective-permute-start.7 = (bf16[64,1152]{1,0:T(8,128)(2,1)S(1)}, bf16[64,1152]{1,0:T(8,128)(2,1)S(1)}, u32[]{:S(2)}, u32[]{:S(2)}) collective-permute-start(bf16[64,1152]{1,0:T(8,128)(2,1)S(1)} %collective-permute-done.1.refs_0_), channel_id=1, source_target_pairs={{0,2},{1,3},{2,0},{3,1},{4,6},{5,7},{6,4},{7,5},{8,10},{9,11},{10,... | collective-permute-start | bytes 442376 | tf_op jit(solution)/shard_map/ppermute | solution.py:222
  18.9 2.4 %collective-permute-start.6 = (bf16[64,1152]{1,0:T(8,128)(2,1)S(1)}, bf16[64,1152]{1,0:T(8,128)(2,1)S(1)}, u32[]{:S(2)}, u32[]{:S(2)}) collective-permute-start(bf16[64,1152]{1,0:T(8,128)(2,1)S(1)} %get-tuple-element.88.refs_1_), channel_id=1, source_target_pairs={{0,1},{1,0},{2,3},{3,2},{4,5},{5,4},{6,7},{7,6},{8,9},{9,8},{10,11... | collective-permute-start | bytes 442376 | tf_op jit(solution)/shard_map/ppermute | solution.py:222
  18.9 6.3 %collective-permute-start.10 = (bf16[64,1152]{1,0:T(8,128)(2,1)S(1)}, bf16[64,1152]{1,0:T(8,128)(2,1)S(1)}, u32[]{:S(2)}, u32[]{:S(2)}) collective-permute-start(bf16[64,1152]{1,0:T(8,128)(2,1)S(1)} %collective-permute-done.2.refs_1_.refs_0_), channel_id=1, source_target_pairs={{0,2},{1,3},{2,0},{3,1},{4,6},{5,7},{6,4},{7,5},{8,10},{9,11},{10,... | collective-permute-start | bytes 442376 | tf_op jit(solution)/shard_map/ppermute | solution.py:222
  25.7 6.1 %collective-permute-start.11 = (bf16[64,1152]{1,0:T(8,128)(2,1)S(1)}, bf16[64,1152]{1,0:T(8,128)(2,1)S(1)}, u32[]{:S(2)}, u32[]{:S(2)}) collective-permute-start(bf16[64,1152]{1,0:T(8,128)(2,1)S(1)} %get-tuple-element.104), channel_id=1, source_target_pairs={{0,2},{1,3},{2,0},{3,1},{4,6},{5,7},{6,4},{7,5},{8,10},{9,11},{10,... | collective-permute-start | bytes 442376 | tf_op jit(solution)/shard_map/ppermute | solution.py:222
  29.2 2.5 %collective-permute-start.16 = (bf16[64,1152]{1,0:T(8,128)(2,1)S(1)}, bf16[64,1152]{1,0:T(8,128)(2,1)S(1)}, u32[]{:S(2)}, u32[]{:S(2)}) collective-permute-start(bf16[64,1152]{1,0:T(8,128)(2,1)S(1)} %get-tuple-element.114), channel_id=1, source_target_pairs={{0,1},{1,0},{2,3},{3,2},{4,5},{5,4},{6,7},{7,6},{8,9},{9,8},{10,11... | collective-permute-start | bytes 442376 | tf_op jit(solution)/shard_map/ppermute | solution.py:222
  29.5 2.3 %collective-permute-start.17 = (bf16[64,1152]{1,0:T(8,128)(2,1)S(1)}, bf16[64,1152]{1,0:T(8,128)(2,1)S(1)}, u32[]{:S(2)}, u32[]{:S(2)}) collective-permute-start(bf16[64,1152]{1,0:T(8,128)(2,1)S(1)} %get-tuple-element.115), channel_id=1, source_target_pairs={{0,1},{1,0},{2,3},{3,2},{4,5},{5,4},{6,7},{7,6},{8,9},{9,8},{10,11... | collective-permute-start | bytes 442376 | tf_op jit(solution)/shard_map/ppermute | solution.py:222
  29.8 3.6 %collective-permute-start.19 = (bf16[64,1152]{1,0:T(8,128)(2,1)S(1)}, bf16[64,1152]{1,0:T(8,128)(2,1)S(1)}, u32[]{:S(2)}, u32[]{:S(2)}) collective-permute-start(bf16[64,1152]{1,0:T(8,128)(2,1)S(1)} %collective-permute-done.1.refs_0_), channel_id=1, source_target_pairs={{0,1},{1,0},{2,3},{3,2},{4,5},{5,4},{6,7},{7,6},{8,9},{9,8},{10,11... | collective-permute-start | bytes 442376 | tf_op jit(solution)/shard_map/ppermute | solution.py:222
  30.0 3.4 %collective-permute-start.20 = (bf16[64,1152]{1,0:T(8,128)(2,1)S(1)}, bf16[64,1152]{1,0:T(8,128)(2,1)S(1)}, u32[]{:S(2)}, u32[]{:S(2)}) collective-permute-start(bf16[64,1152]{1,0:T(8,128)(2,1)S(1)} %get-tuple-element.121.refs_1_), channel_id=1, source_target_pairs={{0,1},{1,0},{2,3},{3,2},{4,5},{5,4},{6,7},{7,6},{8,9},{9,8},{10,11... | collective-permute-start | bytes 442376 | tf_op jit(solution)/shard_map/ppermute | solution.py:222
  31.8 5.3 %collective-permute-start.18 = (bf16[64,1152]{1,0:T(8,128)(2,1)S(1)}, bf16[64,1152]{1,0:T(8,128)(2,1)S(1)}, u32[]{:S(2)}, u32[]{:S(2)}) collective-permute-start(bf16[64,1152]{1,0:T(8,128)(2,1)S(1)} %get-tuple-element.120), channel_id=1, source_target_pairs={{0,2},{1,3},{2,0},{3,1},{4,6},{5,7},{6,4},{7,5},{8,10},{9,11},{10,... | collective-permute-start | bytes 442376 | tf_op jit(solution)/shard_map/ppermute | solution.py:222
  32.9 5.4 %collective-permute-start.14 = (bf16[64,1152]{1,0:T(8,128)(2,1)S(1)}, bf16[64,1152]{1,0:T(8,128)(2,1)S(1)}, u32[]{:S(2)}, u32[]{:S(2)}) collective-permute-start(bf16[64,1152]{1,0:T(8,128)(2,1)S(1)} %pack.1.refs_3_.refs_0_), channel_id=1, source_target_pairs={{0,1},{1,0},{2,3},{3,2},{4,5},{5,4},{6,7},{7,6},{8,9},{9,8},{10,11... | collective-permute-start | bytes 442376 | tf_op jit(solution)/shard_map/ppermute | solution.py:222
  32.9 5.4 %collective-permute-start.15 = (bf16[64,1152]{1,0:T(8,128)(2,1)S(1)}, bf16[64,1152]{1,0:T(8,128)(2,1)S(1)}, u32[]{:S(2)}, u32[]{:S(2)}) collective-permute-start(bf16[64,1152]{1,0:T(8,128)(2,1)S(1)} %get-tuple-element.112.refs_1_), channel_id=1, source_target_pairs={{0,1},{1,0},{2,3},{3,2},{4,5},{5,4},{6,7},{7,6},{8,9},{9,8},{10,11... | collective-permute-start | bytes 442376 | tf_op jit(solution)/shard_map/ppermute | solution.py:222
  36.1 5.5 %collective-permute-start.24 = (bf16[64,1152]{1,0:T(8,128)(2,1)S(1)}, bf16[64,1152]{1,0:T(8,128)(2,1)S(1)}, u32[]{:S(2)}, u32[]{:S(2)}) collective-permute-start(bf16[64,1152]{1,0:T(8,128)(2,1)S(1)} %get-tuple-element.137), channel_id=1, source_target_pairs={{0,1},{1,0},{2,3},{3,2},{4,5},{5,4},{6,7},{7,6},{8,9},{9,8},{10,11... | collective-permute-start | bytes 442376 | tf_op jit(solution)/shard_map/ppermute | solution.py:222
  36.2 5.4 %collective-permute-start.25 = (bf16[64,1152]{1,0:T(8,128)(2,1)S(1)}, bf16[64,1152]{1,0:T(8,128)(2,1)S(1)}, u32[]{:S(2)}, u32[]{:S(2)}) collective-permute-start(bf16[64,1152]{1,0:T(8,128)(2,1)S(1)} %get-tuple-element.138), channel_id=1, source_target_pairs={{0,1},{1,0},{2,3},{3,2},{4,5},{5,4},{6,7},{7,6},{8,9},{9,8},{10,11... | collective-permute-start | bytes 442376 | tf_op jit(solution)/shard_map/ppermute | solution.py:222
  37.2 5.5 %collective-permute-start.23 = (bf16[64,1152]{1,0:T(8,128)(2,1)S(1)}, bf16[64,1152]{1,0:T(8,128)(2,1)S(1)}, u32[]{:S(2)}, u32[]{:S(2)}) collective-permute-start(bf16[64,1152]{1,0:T(8,128)(2,1)S(1)} %get-tuple-element.135), channel_id=1, source_target_pairs={{0,4},{1,5},{2,6},{3,7},{4,0},{5,1},{6,2},{7,3},{8,12},{9,13},{10,... | collective-permute-start | bytes 442376 | tf_op jit(solution)/shard_map/ppermute | solution.py:222
  41.7 6.8 %collective-permute-start.27 = (bf16[64,1152]{1,0:T(8,128)(2,1)S(1)}, bf16[64,1152]{1,0:T(8,128)(2,1)S(1)}, u32[]{:S(2)}, u32[]{:S(2)}) collective-permute-start(bf16[64,1152]{1,0:T(8,128)(2,1)S(1)} %get-tuple-element.151), channel_id=1, source_target_pairs={{0,2},{1,3},{2,0},{3,1},{4,6},{5,7},{6,4},{7,5},{8,10},{9,11},{10,... | collective-permute-start | bytes 442376 | tf_op jit(solution)/shard_map/ppermute | solution.py:222
  42.8 8.0 %collective-permute-start.29 = (bf16[64,1152]{1,0:T(8,128)(2,1)S(1)}, bf16[64,1152]{1,0:T(8,128)(2,1)S(1)}, u32[]{:S(2)}, u32[]{:S(2)}) collective-permute-start(bf16[64,1152]{1,0:T(8,128)(2,1)S(1)} %get-tuple-element.156), channel_id=1, source_target_pairs={{0,2},{1,3},{2,0},{3,1},{4,6},{5,7},{6,4},{7,5},{8,10},{9,11},{10,... | collective-permute-start | bytes 442376 | tf_op jit(solution)/shard_map/ppermute | solution.py:222
  44.0 10.4 %collective-permute-start.26 = (bf16[64,1152]{1,0:T(8,128)(2,1)S(1)}, bf16[64,1152]{1,0:T(8,128)(2,1)S(1)}, u32[]{:S(2)}, u32[]{:S(2)}) collective-permute-start(bf16[64,1152]{1,0:T(8,128)(2,1)S(1)} %get-tuple-element.149), channel_id=1, source_target_pairs={{0,8},{1,9},{2,10},{3,11},{4,12},{5,13},{6,14},{7,15},{8,0},{9,1},... | collective-permute-start | bytes 442376 | tf_op jit(solution)/shard_map/ppermute | solution.py:222
  48.5 7.3 %collective-permute-start.28 = (bf16[64,1152]{1,0:T(8,128)(2,1)S(1)}, bf16[64,1152]{1,0:T(8,128)(2,1)S(1)}, u32[]{:S(2)}, u32[]{:S(2)}) collective-permute-start(bf16[64,1152]{1,0:T(8,128)(2,1)S(1)} %get-tuple-element.155), channel_id=1, source_target_pairs={{0,4},{1,5},{2,6},{3,7},{4,0},{5,1},{6,2},{7,3},{8,12},{9,13},{10,... | collective-permute-start | bytes 442376 | tf_op jit(solution)/shard_map/ppermute | solution.py:222
  (6 other events, 9.7 us)

commit v21 on v15

--- a/solution.py
+++ b/solution.py
@@ -10,24 +10,35 @@
 GROUP = 16
 SCOPED = 8 * 1024 * 1024
 TAIL = 128
+LINE = 16
 SCALE = 2.0**40
 STEP = 256
 PIECE = 256
 
 
-def pack_kernel(ids_hbm, row_hbm, out_ref, ids_ref, sems):
+def pack_kernel(ids_hbm, row_hbm, router_hbm, out_ref, ids_ref, router_ref, sems):
     rows, lat = row_hbm.shape
+    local = router_hbm.shape[0]
     top = ids_hbm.shape[0]
-    get_ids = pltpu.make_async_copy(ids_hbm, ids_ref, sems.at[0])
-    get_rows = pltpu.make_async_copy(row_hbm, out_ref.at[:, pl.ds(0, lat)], sems.at[1])
-    get_ids.start()
-    get_rows.start()
-    get_ids.wait()
+    copies = [
+        pltpu.make_async_copy(ids_hbm, ids_ref, sems.at[0]),
+        pltpu.make_async_copy(router_hbm, router_ref, sems.at[1]),
+        pltpu.make_async_copy(row_hbm, out_ref.at[:, pl.ds(0, lat)], sems.at[2]),
+    ]
+    for copy in copies:
+        copy.start()
+    copies[0].wait()
+    copies[1].wait()
     ids = ids_ref[...].astype(jnp.float32)
-    ids = jnp.concatenate([ids, jnp.full((top, TAIL - rows), -1.0, jnp.float32)], axis=1)
-    ids = jnp.concatenate([ids, jnp.full((TAIL - top, TAIL), -1.0, jnp.float32)], axis=0)
-    out_ref[:, lat:] = ids.T[:rows].astype(jnp.bfloat16)
-    get_rows.wait()
+    router = router_ref[...].astype(jnp.float32)
+    lines = [jnp.concatenate([ids, jnp.full((top, TAIL - rows), -1.0, jnp.float32)], axis=1)]
+    lines.append(jnp.full((LINE - top, TAIL), -1.0, jnp.float32))
+    for e in range(local):
+        for c in range(0, lat, TAIL):
+            lines.append(router[e : e + 1, c : c + TAIL])
+    lines.append(jnp.full((rows - LINE - local * lat // TAIL, TAIL), -1.0, jnp.float32))
+    out_ref[:, lat:] = jnp.concatenate(lines, axis=0).astype(jnp.bfloat16)
+    copies[2].wait()
 
 
 def load_kernel(router_hbm, up_hbm, down_hbm, columns_ref, up_ref, down_ref, router_ref, sems):
@@ -56,8 +67,8 @@
     (columns_ref, up_ref, down_ref), refs = refs[:3], refs[3:]
     keep_refs, refs = refs[:count], refs[count:]
     send_refs, (packed_ref, inner_ref, result_ref) = refs[: 2 * count], refs[2 * count :]
-    rows, wide = blocks[0].shape
-    half, lat = 2 * rows, wide - TAIL
+    rows, lat = blocks[0].shape[0], blocks[0].shape[1] - TAIL
+    half = 2 * rows
     local, eff, _ = down_ref.shape
     slots = packed_ref.shape[1] // count
 
@@ -74,8 +85,7 @@
     col = lax.broadcasted_iota(jnp.int32, (size, size), 1)
     before = jnp.where(col < row, 1.0, 0.0).astype(jnp.bfloat16)
     after = jnp.where(row < col, 1.0, 0.0).astype(jnp.bfloat16)
-    lane = lax.broadcasted_iota(jnp.int32, (size, TAIL), 1)
-    line = lax.broadcasted_iota(jnp.int32, (16, size), 0)
+    line = lax.broadcasted_iota(jnp.int32, (LINE, size), 0)
     slot = lax.broadcasted_iota(jnp.int32, (size, slots), 1).astype(jnp.float32)
     slot_t = lax.broadcasted_iota(jnp.int32, (slots, size), 0).astype(jnp.float32)
     labels = [(lax.axis_index("exp") * local + e).astype(jnp.float32) for e in range(local)]
@@ -83,14 +93,12 @@
     for i in range(count):
         batch = blocks[4 * i : 4 * i + 4]
         x = jnp.concatenate([ref[:, :lat] for ref in batch], axis=0)
-        tail = jnp.concatenate([ref[:, lat:] for ref in batch], axis=0).astype(jnp.float32)
-        masks = [jnp.max(jnp.where(tail == label, 1.0, 0.0), axis=1, keepdims=True) for label in labels]
-        tail_t = tail.T[:16]
-        masks_t = [jnp.max(jnp.where(tail_t == label, 1.0, 0.0), axis=0, keepdims=True) for label in labels]
-        marks, marks_t = jnp.zeros((size, TAIL), jnp.float32), jnp.zeros((16, size), jnp.float32)
+        ids_t = jnp.concatenate([ref[:LINE, lat:].astype(jnp.float32)[:, :rows] for ref in batch], axis=1)
+        masks_t = [jnp.max(jnp.where(ids_t == label, 1.0, 0.0), axis=0, keepdims=True) for label in labels]
+        marks_t = jnp.zeros((LINE, size), jnp.float32)
         for e in range(local):
-            marks = jnp.where(lane == e, masks[e], marks)
             marks_t = jnp.where(line == e, masks_t[e], marks_t)
+        marks = jnp.concatenate([marks_t, jnp.zeros((TAIL - LINE, size), jnp.float32)], axis=0).T
         place_t = jnp.dot(marks_t.astype(jnp.bfloat16), after, preferred_element_type=jnp.float32)
         place = jnp.dot(before, marks.astype(jnp.bfloat16), preferred_element_type=jnp.float32)
         gather = jnp.concatenate(
@@ -102,14 +110,9 @@
         ).astype(jnp.bfloat16)
         packed = jnp.dot(gather, x, preferred_element_type=jnp.float32).astype(jnp.bfloat16)
         spread = jnp.concatenate(
-            [jnp.where((slot == place[:, e : e + 1]) & (masks[e] > 0.0), 1.0, 0.0) for e in range(local)],
+            [jnp.where((slot == place[:, e : e + 1]) & (marks[:, e : e + 1] > 0.0), 1.0, 0.0) for e in range(local)],
             axis=1,
         ).astype(jnp.bfloat16)
-        logits = logits_of(x)
-        sums = jnp.zeros((size, 1), jnp.float32)
-        for e in range(local):
-            sums = sums + jax.nn.sigmoid(logits[:, e : e + 1]) * (masks[e] * SCALE)
-        put(i, slice(lat, wide), jnp.where(lane == 0, sums, 0.0))
         for e in range(local):
             packed_ref[e, i * slots : (i + 1) * slots, :] = packed[e * slots : (e + 1) * slots]
         spreads.append(spread)
@@ -155,13 +158,41 @@
     total_ref[...] = total
 
 
-def finish_kernel(*refs):
-    out_ref = refs[-1]
-    lat = out_ref.shape[1]
+def scores_kernel(mine_ref, *refs):
+    *packet_refs, out_ref, lines_ref = refs
+    rows, lat = mine_ref.shape[0], mine_ref.shape[1] - TAIL
+    chunks = lat // TAIL
+    height = lines_ref.shape[0] // len(packet_refs)
+    local = height // chunks
+    for i, ref in enumerate(packet_refs):
+        lines_ref[i * height : (i + 1) * height, :] = ref[LINE : LINE + height, lat:].astype(jnp.float32)
+    number = len(packet_refs) * local
+    logits = jnp.zeros((number, rows), jnp.float32)
+    for c in range(chunks):
+        columns = lines_ref[pl.ds(c, number, stride=chunks), :].astype(jnp.bfloat16)
+        logits = logits + lax.dot_general(
+            columns,
+            mine_ref[:, c * TAIL : (c + 1) * TAIL],
+            (((1,), (1,)), ((), ())),
+            preferred_element_type=jnp.float32,
+        )
+    at = lax.broadcasted_iota(jnp.int32, (number, rows), 0)
+    label = ((lax.axis_index("exp") ^ (at // local)) * local + at % local).astype(jnp.float32)
+    ids = mine_ref[:LINE, lat:].astype(jnp.float32)[:, :rows]
+    mask = jnp.zeros((number, rows), jnp.float32)
+    for k in range(LINE):
+        mask = jnp.where(ids[k : k + 1] == label, 1.0, mask)
+    total = jnp.sum(jax.nn.sigmoid(logits) * (mask * SCALE), axis=0, keepdims=True)
+    total = jnp.broadcast_to(total, (TAIL, rows))
+    total = jnp.concatenate([total, jnp.ones((TAIL, TAIL - rows), jnp.float32)], axis=1)
+    out_ref[...] = total.T[:rows]
+
+
+def finish_kernel(scores_ref, *refs):
     total = refs[0][...]
     for ref in refs[1:-1]:
         total = total + ref[...].astype(jnp.float32)
-    out_ref[...] = (total[:, :lat] / total[:, lat : lat + 1]).astype(jnp.bfloat16)
+    refs[-1][...] = (total / scores_ref[:, :1]).astype(jnp.bfloat16)
 
 
 def in_vmem(x):
@@ -222,7 +253,7 @@
         return lax.ppermute(x, "exp", [(i, i ^ bits) for i in range(n_dev)])
 
     def space(height, dtype):
-        return pltpu.VMEM((height, wide), dtype)
+        return pltpu.VMEM((height, lat), dtype)
 
     def weights(dep):
         return call(
@@ -255,7 +286,7 @@
         def tie(x, deps=()):
             return step(tie_kernel, [], deps=deps, hand_on=[x])[0]
 
-        other, keep, send, came, fold_keep, fold_send, y_came = {}, {}, {}, {}, {}, {}, {}
+        other, keep, send, came, fold_keep, fold_send, y_came, far = {}, {}, {}, {}, {}, {}, {}, {}
 
         def gather(k, deps=()):
             other[k] = tie(swap(block[k], 2), deps)
@@ -265,7 +296,8 @@
             blocks = []
             for k in ks:
                 near = [block[k], other[k]]
-                blocks += near + [swap(one, 1) for one in near]
+                far[k] = [swap(one, 1) for one in near]
+                blocks += near + far[k]
             result = step(
                 functools.partial(expert_kernel, count),
                 [space(2 * rows, jnp.float32)] * count + [space(rows, jnp.bfloat16)] * (2 * count),
@@ -304,41 +336,59 @@
         z_3 = swap(reduce_y(3), 4)
         reduce_core(1)
         reduce_core(0)
+        scores = None
+        if n_dev == GROUP:
+            packets = [p for k in range(4) for p in (block[k], far[k][0], other[k], far[k][1])]
+            scores = step(
+                scores_kernel,
+                [pltpu.VMEM((rows, TAIL), jnp.float32)],
+                [mine, *packets],
+                scratch=[pltpu.VMEM((n_dev * local * lat // TAIL, TAIL), jnp.float32)],
+            )[0]
         z_2 = swap(reduce_y(2, z_3), 8)
         z_1 = swap(reduce_y(1), 4)
-        return fold_keep[0], z_2, z_1, y_came[0]
+        return scores, (fold_keep[0], z_2, z_1, y_came[0])
 
     packet = call(
         pack_kernel,
-        [space(rows, jnp.bfloat16)],
-        hbm=[routes.T, latent_in],
-        scratch=[pltpu.VMEM(routes.shape[::-1], routes.dtype), pltpu.SemaphoreType.DMA((2,))],
+        [pltpu.VMEM((rows, wide), jnp.bfloat16)],
+        hbm=[routes.T, latent_in, router.T],
+        scratch=[
+            pltpu.VMEM(routes.shape[::-1], routes.dtype),
+            pltpu.VMEM((local, lat), jnp.bfloat16),
+            pltpu.SemaphoreType.DMA((3,)),
+        ],
     )[0]
 
-    def finish(parts):
+    def finish(scores, parts):
         return pl.pallas_call(
             finish_kernel,
             out_shape=jax.ShapeDtypeStruct((rows, lat), jnp.bfloat16),
-            in_specs=[VMEM] * len(parts),
+            in_specs=[VMEM] * (1 + len(parts)),
             out_specs=VMEM,
             compiler_params=pltpu.CompilerParams(vmem_limit_bytes=SCOPED),
             name="finish",
-        )(*[in_vmem(p) for p in parts])
+        )(*[in_vmem(p) for p in (scores, *parts)])
 
     if n_dev == GROUP:
-        return finish(group_pass(packet))
+        return finish(*group_pass(packet))
 
     def next_group(x):
         return lax.ppermute(x, "exp", [(i, (i + GROUP) % n_dev) for i in range(n_dev)])
 
     def step(carry, _):
         mine, total = carry
-        total = call(total_kernel, [space(rows, jnp.float32)], [total, *group_pass(mine)])[0]
+        total = call(total_kernel, [space(rows, jnp.float32)], [total, *group_pass(mine)[1]])[0]
         return (next_group(mine), next_group(total)), None
 
-    start = (packet, jnp.zeros((rows, wide), jnp.float32))
+    start = (packet, jnp.zeros((rows, lat), jnp.float32))
     (_, total), _ = lax.scan(step, start, None, length=n_dev // GROUP)
-    return finish([total])
+    columns = lax.all_gather(router, "exp", axis=1, tiled=True)
+    logits = jnp.dot(latent_in, columns, preferred_element_type=jnp.float32)
+    labels = jnp.arange(n_dev * local, dtype=jnp.int32)
+    mask = jnp.any(routes[:, :, None] == labels[None, None, :], axis=1)
+    scores = jnp.sum(jnp.where(mask, jax.nn.sigmoid(logits), 0.0), axis=1, keepdims=True) * SCALE
+    return finish(jnp.broadcast_to(scores, (rows, TAIL)), [total])
 
 
 def solution(mesh):

time: 56.7 us -> 57.3 us (1.011)
    pallas_call x16 -> x17, Pallas kernels: 16.3 us -> 16 us  [call(): pl.pallas_call(body_with_chain if reads_chain else body, out_shape=list(o...]
  transfers between devices with their start and end apart: 30 -> 30, of which waited for: 10 -> 11; matrix products, arithmetic and copies ran while one was open for 0% -> 0% of each run, Pallas kernels for 27% -> 26%
where the time goes in v21:
time: 57.3 us; the launch traced here: 57.1 us
  starting transfers between devices  24.1 us (42%)
  Pallas kernels  16.8 us (29%)
  waiting for transfers between devices  16 us (28%)
    ppermute x30, starting transfers between devices, swap(): return lax.ppermute(x, 'exp', [(i, i ^ bits) for i in range(n_dev)])  24.1 us
    ppermute x30, waiting for transfers between devices, swap(): return lax.ppermute(x, 'exp', [(i, i ^ bits) for i in range(n_dev)])  16 us
    pallas_call x17, Pallas kernels, call(): pl.pallas_call(body_with_chain if reads_chain else body, out_shape=list(o...  16 us
  transfers between devices with their start and end apart: 30, of which 11 were waited for; matrix products, arithmetic and copies ran while one was open for 0% of the time, Pallas kernels for 26%

profile of v21, /device:TPU:0, one launch (start us, length us, event | category | flops | bytes accessed | tf_op | source)
XLA Modules:
  0.0 57.1 jit_solution(10661551958792214792)
XLA Ops:
  0.0 1.0 %pack.1.refs_3_.refs_4_.refs_0_.refs_1_ = bf16[64,1152]{1,0:T(8,128)(2,1)S(1)} custom-call(s32[8,64]{1,0:T(8,128)} %bitcast.4, bf16[64,1024]{1,0:T(8,128)(2,1)} %refs_1_.2, bf16[2,1024]{1,0:T(2,128)(2,1)} %bitcast.2), custom_call_target="tpu_custom_call" | custom-call | bytes 10000 | tf_op jit(solution)/shard_map/pack/pallas_call | solution.py:232
  1.0 4.1 %collective-permute-start.5 = (bf16[64,1152]{1,0:T(8,128)(2,1)S(1)}, bf16[64,1152]{1,0:T(8,128)(2,1)S(1)}, u32[]{:S(2)}, u32[]{:S(2)}) collective-permute-start(bf16[64,1152]{1,0:T(8,128)(2,1)S(1)} %pack.1.refs_3_.refs_4_.refs_0_.refs_1_), channel_id=1, source_target_pairs={{0,8},{1,9},{2,10},{3,11},{4,12},{5,13},{6,14},{7,15},{8,0},{9,1},... | collective-permute-start | bytes 442376 | tf_op jit(solution)/shard_map/ppermute | solution.py:253
  5.1 1.6 %collective-permute-start.3 = (bf16[64,1152]{1,0:T(8,128)(2,1)S(1)}, bf16[64,1152]{1,0:T(8,128)(2,1)S(1)}, u32[]{:S(2)}, u32[]{:S(2)}) collective-permute-start(bf16[64,1152]{1,0:T(8,128)(2,1)S(1)} %pack.1.refs_3_.refs_4_.refs_0_.refs_1_), channel_id=1, source_target_pairs={{0,4},{1,5},{2,6},{3,7},{4,0},{5,1},{6,2},{7,3},{8,12},{9,13},{10,... | collective-permute-start | bytes 442376 | tf_op jit(solution)/shard_map/ppermute | solution.py:253
  6.6 1.5 %collective-permute-start.1 = (bf16[64,1152]{1,0:T(8,128)(2,1)S(1)}, bf16[64,1152]{1,0:T(8,128)(2,1)S(1)}, u32[]{:S(2)}, u32[]{:S(2)}) collective-permute-start(bf16[64,1152]{1,0:T(8,128)(2,1)S(1)} %pack.1.refs_3_.refs_4_.refs_0_.refs_1_), channel_id=1, source_target_pairs={{0,2},{1,3},{2,0},{3,1},{4,6},{5,7},{6,4},{7,5},{8,10},{9,11},{10,... | collective-permute-start | bytes 442376 | tf_op jit(solution)/shard_map/ppermute | solution.py:253
  8.2 4.7 %load.1 = (bf16[1024,128]{1,0:T(8,128)(2,1)S(1)}, bf16[2,1024,2048]{2,1,0:T(8,128)(2,1)S(1)}, bf16[2,1024,1024]{2,1,0:T(8,128)(2,1)S(1)}) custom-call(bf16[2,1024]{1,0:T(2,128)(2,1)} %bitcast.3, bf16[2,1024,2048]{2,1,0:T(8,128)(2,1)} %refs_1_.3, bf16[2,1024,1024]{2,1,0:T(8,128)(2,1)} %refs_2_.1, bf16[64,1152]{1,0:T(8,128)(2,1)S(1)} %pack.1.refs_3_.refs_4_.refs_0_.refs_1_), custom_call_target="tpu_custom_call" | custom-call | bytes 10000 | tf_op jit(solution)/shard_map/load/pallas_call | solution.py:232
  12.9 0.8 %collective-permute-start.7 = (bf16[64,1152]{1,0:T(8,128)(2,1)S(1)}, bf16[64,1152]{1,0:T(8,128)(2,1)S(1)}, u32[]{:S(2)}, u32[]{:S(2)}) collective-permute-start(bf16[64,1152]{1,0:T(8,128)(2,1)S(1)} %get-tuple-element.81.refs_0_.refs_9_), channel_id=1, source_target_pairs={{0,2},{1,3},{2,0},{3,1},{4,6},{5,7},{6,4},{7,5},{8,10},{9,11},{10,... | collective-permute-start | bytes 442376 | tf_op jit(solution)/shard_map/ppermute | solution.py:253
  14.3 1.1 %collective-permute-start.8 = (bf16[64,1152]{1,0:T(8,128)(2,1)S(1)}, bf16[64,1152]{1,0:T(8,128)(2,1)S(1)}, u32[]{:S(2)}, u32[]{:S(2)}) collective-permute-start(bf16[64,1152]{1,0:T(8,128)(2,1)S(1)} %collective-permute-done.3.refs_0_.refs_5_), channel_id=1, source_target_pairs={{0,2},{1,3},{2,0},{3,1},{4,6},{5,7},{6,4},{7,5},{8,10},{9,11},{10,... | collective-permute-start | bytes 442376 | tf_op jit(solution)/shard_map/ppermute | solution.py:253
  15.5 3.4 %collective-permute-done.7.refs_6_ = bf16[64,1152]{1,0:T(8,128)(2,1)S(1)} collective-permute-done((bf16[64,1152]{1,0:T(8,128)(2,1)S(1)}, bf16[64,1152]{1,0:T(8,128)(2,1)S(1)}, u32[]{:S(2)}, u32[]{:S(2)}) %collective-permute-start.7) | collective-permute-done | bytes 147488 | tf_op jit(solution)/shard_map/ppermute | solution.py:253
  18.9 1.3 %collective-permute-start.13 = (bf16[64,1152]{1,0:T(8,128)(2,1)S(1)}, bf16[64,1152]{1,0:T(8,128)(2,1)S(1)}, u32[]{:S(2)}, u32[]{:S(2)}) collective-permute-start(bf16[64,1152]{1,0:T(8,128)(2,1)S(1)} %collective-permute-done.6.refs_1_.refs_0_.refs_13_), channel_id=1, source_target_pairs={{0,2},{1,3},{2,0},{3,1},{4,6},{5,7},{6,4},{7,5},{8,10},{9,11},{10,... | collective-permute-start | bytes 442376 | tf_op jit(solution)/shard_map/ppermute | solution.py:253
  20.4 0.9 %collective-permute-done.8.refs_3_ = bf16[64,1152]{1,0:T(8,128)(2,1)S(1)} collective-permute-done((bf16[64,1152]{1,0:T(8,128)(2,1)S(1)}, bf16[64,1152]{1,0:T(8,128)(2,1)S(1)}, u32[]{:S(2)}, u32[]{:S(2)}) %collective-permute-start.8) | collective-permute-done | bytes 147488 | tf_op jit(solution)/shard_map/ppermute | solution.py:253
  21.3 2.5 %expert.3 = (f32[128,1024]{1,0:T(8,128)S(1)}, bf16[64,1024]{1,0:T(8,128)(2,1)S(1)}, bf16[64,1024]{1,0:T(8,128)(2,1)S(1)}, bf16[1024,128]{1,0:T(8,128)(2,1)S(1)},...) custom-call(bf16[64,1152]{1,0:T(8,128)(2,1)S(1)} %get-tuple-element., ...), custom_call_target="tpu_custom_call", output_to_operand_aliasing={{3}: (4, {}), {4}: (5, {}), {5}: (6, {})} | custom-call | bytes 10000 | tf_op jit(solution)/shard_map/expert/pallas_call | solution.py:232
  23.8 1.3 %collective-permute-done.13.refs_3_ = bf16[64,1152]{1,0:T(8,128)(2,1)S(1)} collective-permute-done((bf16[64,1152]{1,0:T(8,128)(2,1)S(1)}, bf16[64,1152]{1,0:T(8,128)(2,1)S(1)}, u32[]{:S(2)}, u32[]{:S(2)}) %collective-permute-start.13) | collective-permute-done | bytes 147488 | tf_op jit(solution)/shard_map/ppermute | solution.py:253
  25.7 1.0 %collective-permute-done.15.refs_1_ = bf16[64,1024]{1,0:T(8,128)(2,1)S(1)} collective-permute-done((bf16[64,1024]{1,0:T(8,128)(2,1)S(1)}, bf16[64,1024]{1,0:T(8,128)(2,1)S(1)}, u32[]{:S(2)}, u32[]{:S(2)}) %collective-permute-start.15) | collective-permute-done | bytes 131104 | tf_op jit(solution)/shard_map/ppermute | solution.py:253
  27.1 1.3 %collective-permute-start.19 = (bf16[64,1024]{1,0:T(8,128)(2,1)S(1)}, bf16[64,1024]{1,0:T(8,128)(2,1)S(1)}, u32[]{:S(2)}, u32[]{:S(2)}) collective-permute-start(bf16[64,1024]{1,0:T(8,128)(2,1)S(1)} %get-tuple-element.109), channel_id=1, source_target_pairs={{0,2},{1,3},{2,0},{3,1},{4,6},{5,7},{6,4},{7,5},{8,10},{9,11},{10,... | collective-permute-start | bytes 393224 | tf_op jit(solution)/shard_map/ppermute | solution.py:253
  28.4 2.6 %expert.4 = (f32[128,1024]{1,0:T(8,128)S(1)}, bf16[64,1024]{1,0:T(8,128)(2,1)S(1)}, bf16[64,1024]{1,0:T(8,128)(2,1)S(1)}, bf16[1024,128]{1,0:T(8,128)(2,1)S(1)},...) custom-call(bf16[64,1152]{1,0:T(8,128)(2,1)S(1)} %collective-permute, ...), custom_call_target="tpu_custom_call", output_to_operand_aliasing={{3}: (4, {}), {4}: (5, {}), {5}: (6, {})} | custom-call | bytes 10000 | tf_op jit(solution)/shard_map/expert/pallas_call | solution.py:232
  33.2 1.0 %collective-permute-done.18.refs_2_ = bf16[64,1024]{1,0:T(8,128)(2,1)S(1)} collective-permute-done((bf16[64,1024]{1,0:T(8,128)(2,1)S(1)}, bf16[64,1024]{1,0:T(8,128)(2,1)S(1)}, u32[]{:S(2)}, u32[]{:S(2)}) %collective-permute-start.18) | collective-permute-done | bytes 131104 | tf_op jit(solution)/shard_map/ppermute | solution.py:253
  34.3 1.3 %collective-permute-start.24 = (bf16[64,1024]{1,0:T(8,128)(2,1)S(1)}, bf16[64,1024]{1,0:T(8,128)(2,1)S(1)}, u32[]{:S(2)}, u32[]{:S(2)}) collective-permute-start(bf16[64,1024]{1,0:T(8,128)(2,1)S(1)} %get-tuple-element.123), channel_id=1, source_target_pairs={{0,2},{1,3},{2,0},{3,1},{4,6},{5,7},{6,4},{7,5},{8,10},{9,11},{10,... | collective-permute-start | bytes 393224 | tf_op jit(solution)/shard_map/ppermute | solution.py:253
  35.7 4.7 %expert.5 = (f32[128,1024]{1,0:T(8,128)S(1)}, f32[128,1024]{1,0:T(8,128)S(1)}, bf16[64,1024]{1,0:T(8,128)(2,1)S(1)}, bf16[64,1024]{1,0:T(8,128)(2,1)S(1)}, bf16[...) custom-call(bf16[64,1152]{1,0:T(8,128)(2,1)S(1)} %collective-permute, ...), custom_call_target="tpu_custom_call", output_to_operand_aliasing={{6}: (8, {}), {7}: (9, {}), {8}: (10, {})} | custom-call | bytes 10000 | tf_op jit(solution)/shard_map/expert/pallas_call | solution.py:232
  42.1 1.3 %collective-permute-start.27 = (bf16[64,1024]{1,0:T(8,128)(2,1)S(1)}, bf16[64,1024]{1,0:T(8,128)(2,1)S(1)}, u32[]{:S(2)}, u32[]{:S(2)}) collective-permute-start(bf16[64,1024]{1,0:T(8,128)(2,1)S(1)} %get-tuple-element.145), channel_id=1, source_target_pairs={{0,2},{1,3},{2,0},{3,1},{4,6},{5,7},{6,4},{7,5},{8,10},{9,11},{10,... | collective-permute-start | bytes 393224 | tf_op jit(solution)/shard_map/ppermute | solution.py:253
  43.4 0.9 %collective-permute-start.29 = (bf16[64,1024]{1,0:T(8,128)(2,1)S(1)}, bf16[64,1024]{1,0:T(8,128)(2,1)S(1)}, u32[]{:S(2)}, u32[]{:S(2)}) collective-permute-start(bf16[64,1024]{1,0:T(8,128)(2,1)S(1)} %get-tuple-element.150), channel_id=1, source_target_pairs={{0,2},{1,3},{2,0},{3,1},{4,6},{5,7},{6,4},{7,5},{8,10},{9,11},{10,... | collective-permute-start | bytes 393224 | tf_op jit(solution)/shard_map/ppermute | solution.py:253
  44.6 2.5 %collective-permute-done.25.refs_2_ = bf16[64,1024]{1,0:T(8,128)(2,1)S(1)} collective-permute-done((bf16[64,1024]{1,0:T(8,128)(2,1)S(1)}, bf16[64,1024]{1,0:T(8,128)(2,1)S(1)}, u32[]{:S(2)}, u32[]{:S(2)}) %collective-permute-start.25) | collective-permute-done | bytes 131104 | tf_op jit(solution)/shard_map/ppermute | solution.py:253
  47.1 2.6 %collective-permute-start.26 = (bf16[64,1024]{1,0:T(8,128)(2,1)S(1)}, bf16[64,1024]{1,0:T(8,128)(2,1)S(1)}, u32[]{:S(2)}, u32[]{:S(2)}) collective-permute-start(bf16[64,1024]{1,0:T(8,128)(2,1)S(1)} %get-tuple-element.143), channel_id=1, source_target_pairs={{0,8},{1,9},{2,10},{3,11},{4,12},{5,13},{6,14},{7,15},{8,0},{9,1},... | collective-permute-start | bytes 393224 | tf_op jit(solution)/shard_map/ppermute | solution.py:253
  49.7 1.8 %collective-permute-start.28 = (bf16[64,1024]{1,0:T(8,128)(2,1)S(1)}, bf16[64,1024]{1,0:T(8,128)(2,1)S(1)}, u32[]{:S(2)}, u32[]{:S(2)}) collective-permute-start(bf16[64,1024]{1,0:T(8,128)(2,1)S(1)} %get-tuple-element.149), channel_id=1, source_target_pairs={{0,4},{1,5},{2,6},{3,7},{4,0},{5,1},{6,2},{7,3},{8,12},{9,13},{10,... | collective-permute-start | bytes 393224 | tf_op jit(solution)/shard_map/ppermute | solution.py:253
  51.5 4.2 %collective-permute-done.26.refs_1_ = bf16[64,1024]{1,0:T(8,128)(2,1)S(1)} collective-permute-done((bf16[64,1024]{1,0:T(8,128)(2,1)S(1)}, bf16[64,1024]{1,0:T(8,128)(2,1)S(1)}, u32[]{:S(2)}, u32[]{:S(2)}) %collective-permute-start.26) | collective-permute-done | bytes 131104 | tf_op jit(solution)/shard_map/ppermute | solution.py:253
  (54 shorter events, 7.4 us)
Async XLA Ops:
  1.0 11.9 %collective-permute-start.5 = (bf16[64,1152]{1,0:T(8,128)(2,1)S(1)}, bf16[64,1152]{1,0:T(8,128)(2,1)S(1)}, u32[]{:S(2)}, u32[]{:S(2)}) collective-permute-start(bf16[64,1152]{1,0:T(8,128)(2,1)S(1)} %pack.1.refs_3_.refs_4_.refs_0_.refs_1_), channel_id=1, source_target_pairs={{0,8},{1,9},{2,10},{3,11},{4,12},{5,13},{6,14},{7,15},{8,0},{9,1},... | collective-permute-start | bytes 442376 | tf_op jit(solution)/shard_map/ppermute | solution.py:253
  5.1 9.3 %collective-permute-start.3 = (bf16[64,1152]{1,0:T(8,128)(2,1)S(1)}, bf16[64,1152]{1,0:T(8,128)(2,1)S(1)}, u32[]{:S(2)}, u32[]{:S(2)}) collective-permute-start(bf16[64,1152]{1,0:T(8,128)(2,1)S(1)} %pack.1.refs_3_.refs_4_.refs_0_.refs_1_), channel_id=1, source_target_pairs={{0,4},{1,5},{2,6},{3,7},{4,0},{5,1},{6,2},{7,3},{8,12},{9,13},{10,... | collective-permute-start | bytes 442376 | tf_op jit(solution)/shard_map/ppermute | solution.py:253
  6.6 8.8 %collective-permute-start.1 = (bf16[64,1152]{1,0:T(8,128)(2,1)S(1)}, bf16[64,1152]{1,0:T(8,128)(2,1)S(1)}, u32[]{:S(2)}, u32[]{:S(2)}) collective-permute-start(bf16[64,1152]{1,0:T(8,128)(2,1)S(1)} %pack.1.refs_3_.refs_4_.refs_0_.refs_1_), channel_id=1, source_target_pairs={{0,2},{1,3},{2,0},{3,1},{4,6},{5,7},{6,4},{7,5},{8,10},{9,11},{10,... | collective-permute-start | bytes 442376 | tf_op jit(solution)/shard_map/ppermute | solution.py:253
  12.9 5.9 %collective-permute-start.7 = (bf16[64,1152]{1,0:T(8,128)(2,1)S(1)}, bf16[64,1152]{1,0:T(8,128)(2,1)S(1)}, u32[]{:S(2)}, u32[]{:S(2)}) collective-permute-start(bf16[64,1152]{1,0:T(8,128)(2,1)S(1)} %get-tuple-element.81.refs_0_.refs_9_), channel_id=1, source_target_pairs={{0,2},{1,3},{2,0},{3,1},{4,6},{5,7},{6,4},{7,5},{8,10},{9,11},{10,... | collective-permute-start | bytes 442376 | tf_op jit(solution)/shard_map/ppermute | solution.py:253
  13.8 5.1 %collective-permute-start.6 = (bf16[64,1152]{1,0:T(8,128)(2,1)S(1)}, bf16[64,1152]{1,0:T(8,128)(2,1)S(1)}, u32[]{:S(2)}, u32[]{:S(2)}) collective-permute-start(bf16[64,1152]{1,0:T(8,128)(2,1)S(1)} %get-tuple-element.81.refs_0_.refs_9_), channel_id=1, source_target_pairs={{0,4},{1,5},{2,6},{3,7},{4,0},{5,1},{6,2},{7,3},{8,12},{9,13},{10,... | collective-permute-start | bytes 442376 | tf_op jit(solution)/shard_map/ppermute | solution.py:253
  14.3 7.0 %collective-permute-start.10 = (bf16[64,1152]{1,0:T(8,128)(2,1)S(1)}, bf16[64,1152]{1,0:T(8,128)(2,1)S(1)}, u32[]{:S(2)}, u32[]{:S(2)}) collective-permute-start(bf16[64,1152]{1,0:T(8,128)(2,1)S(1)} %get-tuple-element.81.refs_0_.refs_9_), channel_id=1, source_target_pairs={{0,1},{1,0},{2,3},{3,2},{4,5},{5,4},{6,7},{7,6},{8,9},{9,8},{10,11... | collective-permute-start | bytes 442376 | tf_op jit(solution)/shard_map/ppermute | solution.py:253
  14.3 7.0 %collective-permute-start.8 = (bf16[64,1152]{1,0:T(8,128)(2,1)S(1)}, bf16[64,1152]{1,0:T(8,128)(2,1)S(1)}, u32[]{:S(2)}, u32[]{:S(2)}) collective-permute-start(bf16[64,1152]{1,0:T(8,128)(2,1)S(1)} %collective-permute-done.3.refs_0_.refs_5_), channel_id=1, source_target_pairs={{0,2},{1,3},{2,0},{3,1},{4,6},{5,7},{6,4},{7,5},{8,10},{9,11},{10,... | collective-permute-start | bytes 442376 | tf_op jit(solution)/shard_map/ppermute | solution.py:253
  18.9 2.4 %collective-permute-start.11 = (bf16[64,1152]{1,0:T(8,128)(2,1)S(1)}, bf16[64,1152]{1,0:T(8,128)(2,1)S(1)}, u32[]{:S(2)}, u32[]{:S(2)}) collective-permute-start(bf16[64,1152]{1,0:T(8,128)(2,1)S(1)} %get-tuple-element.89.refs_1_.refs_11_), channel_id=1, source_target_pairs={{0,1},{1,0},{2,3},{3,2},{4,5},{5,4},{6,7},{7,6},{8,9},{9,8},{10,11... | collective-permute-start | bytes 442376 | tf_op jit(solution)/shard_map/ppermute | solution.py:253
  18.9 6.3 %collective-permute-start.13 = (bf16[64,1152]{1,0:T(8,128)(2,1)S(1)}, bf16[64,1152]{1,0:T(8,128)(2,1)S(1)}, u32[]{:S(2)}, u32[]{:S(2)}) collective-permute-start(bf16[64,1152]{1,0:T(8,128)(2,1)S(1)} %collective-permute-done.6.refs_1_.refs_0_.refs_13_), channel_id=1, source_target_pairs={{0,2},{1,3},{2,0},{3,1},{4,6},{5,7},{6,4},{7,5},{8,10},{9,11},{10,... | collective-permute-start | bytes 442376 | tf_op jit(solution)/shard_map/ppermute | solution.py:253
  20.2 8.2 %collective-permute-start.12 = (bf16[64,1152]{1,0:T(8,128)(2,1)S(1)}, bf16[64,1152]{1,0:T(8,128)(2,1)S(1)}, u32[]{:S(2)}, u32[]{:S(2)}) collective-permute-start(bf16[64,1152]{1,0:T(8,128)(2,1)S(1)} %collective-permute-done.6.refs_1_.refs_0_.refs_13_), channel_id=1, source_target_pairs={{0,1},{1,0},{2,3},{3,2},{4,5},{5,4},{6,7},{7,6},{8,9},{9,8},{10,11... | collective-permute-start | bytes 442376 | tf_op jit(solution)/shard_map/ppermute | solution.py:253
  25.2 3.2 %collective-permute-start.14 = (bf16[64,1152]{1,0:T(8,128)(2,1)S(1)}, bf16[64,1152]{1,0:T(8,128)(2,1)S(1)}, u32[]{:S(2)}, u32[]{:S(2)}) collective-permute-start(bf16[64,1152]{1,0:T(8,128)(2,1)S(1)} %get-tuple-element.96.refs_1_.refs_15_), channel_id=1, source_target_pairs={{0,1},{1,0},{2,3},{3,2},{4,5},{5,4},{6,7},{7,6},{8,9},{9,8},{10,11... | collective-permute-start | bytes 442376 | tf_op jit(solution)/shard_map/ppermute | solution.py:253
  27.1 5.7 %collective-permute-start.19 = (bf16[64,1024]{1,0:T(8,128)(2,1)S(1)}, bf16[64,1024]{1,0:T(8,128)(2,1)S(1)}, u32[]{:S(2)}, u32[]{:S(2)}) collective-permute-start(bf16[64,1024]{1,0:T(8,128)(2,1)S(1)} %get-tuple-element.109), channel_id=1, source_target_pairs={{0,2},{1,3},{2,0},{3,1},{4,6},{5,7},{6,4},{7,5},{8,10},{9,11},{10,... | collective-permute-start | bytes 393224 | tf_op jit(solution)/shard_map/ppermute | solution.py:253
  31.0 4.6 %collective-permute-start = (bf16[64,1152]{1,0:T(8,128)(2,1)S(1)}, bf16[64,1152]{1,0:T(8,128)(2,1)S(1)}, u32[]{:S(2)}, u32[]{:S(2)}) collective-permute-start(bf16[64,1152]{1,0:T(8,128)(2,1)S(1)} %pack.1.refs_3_.refs_4_.refs_0_.refs_1_), channel_id=1, source_target_pairs={{0,1},{1,0},{2,3},{3,2},{4,5},{5,4},{6,7},{7,6},{8,9},{9,8},{10,11... | collective-permute-start | bytes 442376 | tf_op jit(solution)/shard_map/ppermute | solution.py:253
  31.5 4.1 %collective-permute-start.4 = (bf16[64,1152]{1,0:T(8,128)(2,1)S(1)}, bf16[64,1152]{1,0:T(8,128)(2,1)S(1)}, u32[]{:S(2)}, u32[]{:S(2)}) collective-permute-start(bf16[64,1152]{1,0:T(8,128)(2,1)S(1)} %collective-permute-done.3.refs_0_.refs_5_), channel_id=1, source_target_pairs={{0,1},{1,0},{2,3},{3,2},{4,5},{5,4},{6,7},{7,6},{8,9},{9,8},{10,11... | collective-permute-start | bytes 442376 | tf_op jit(solution)/shard_map/ppermute | solution.py:253
  31.6 4.1 %collective-permute-start.2 = (bf16[64,1152]{1,0:T(8,128)(2,1)S(1)}, bf16[64,1152]{1,0:T(8,128)(2,1)S(1)}, u32[]{:S(2)}, u32[]{:S(2)}) collective-permute-start(bf16[64,1152]{1,0:T(8,128)(2,1)S(1)} %collective-permute-done.1.refs_2_.refs_5_.refs_3_), channel_id=1, source_target_pairs={{0,1},{1,0},{2,3},{3,2},{4,5},{5,4},{6,7},{7,6},{8,9},{9,8},{10,11... | collective-permute-start | bytes 442376 | tf_op jit(solution)/shard_map/ppermute | solution.py:253
  32.7 2.9 %collective-permute-start.9 = (bf16[64,1152]{1,0:T(8,128)(2,1)S(1)}, bf16[64,1152]{1,0:T(8,128)(2,1)S(1)}, u32[]{:S(2)}, u32[]{:S(2)}) collective-permute-start(bf16[64,1152]{1,0:T(8,128)(2,1)S(1)} %get-tuple-element.88.refs_1_.refs_7_), channel_id=1, source_target_pairs={{0,1},{1,0},{2,3},{3,2},{4,5},{5,4},{6,7},{7,6},{8,9},{9,8},{10,11... | collective-permute-start | bytes 442376 | tf_op jit(solution)/shard_map/ppermute | solution.py:253
  34.3 7.1 %collective-permute-start.24 = (bf16[64,1024]{1,0:T(8,128)(2,1)S(1)}, bf16[64,1024]{1,0:T(8,128)(2,1)S(1)}, u32[]{:S(2)}, u32[]{:S(2)}) collective-permute-start(bf16[64,1024]{1,0:T(8,128)(2,1)S(1)} %get-tuple-element.123), channel_id=1, source_target_pairs={{0,2},{1,3},{2,0},{3,1},{4,6},{5,7},{6,4},{7,5},{8,10},{9,11},{10,... | collective-permute-start | bytes 393224 | tf_op jit(solution)/shard_map/ppermute | solution.py:253
  41.0 2.4 %collective-permute-start.20 = (bf16[64,1024]{1,0:T(8,128)(2,1)S(1)}, bf16[64,1024]{1,0:T(8,128)(2,1)S(1)}, u32[]{:S(2)}, u32[]{:S(2)}) collective-permute-start(bf16[64,1024]{1,0:T(8,128)(2,1)S(1)} %get-tuple-element.117), channel_id=1, source_target_pairs={{0,1},{1,0},{2,3},{3,2},{4,5},{5,4},{6,7},{7,6},{8,9},{9,8},{10,11... | collective-permute-start | bytes 393224 | tf_op jit(solution)/shard_map/ppermute | solution.py:253
  41.0 2.3 %collective-permute-start.21 = (bf16[64,1024]{1,0:T(8,128)(2,1)S(1)}, bf16[64,1024]{1,0:T(8,128)(2,1)S(1)}, u32[]{:S(2)}, u32[]{:S(2)}) collective-permute-start(bf16[64,1024]{1,0:T(8,128)(2,1)S(1)} %get-tuple-element.118), channel_id=1, source_target_pairs={{0,1},{1,0},{2,3},{3,2},{4,5},{5,4},{6,7},{7,6},{8,9},{9,8},{10,11... | collective-permute-start | bytes 393224 | tf_op jit(solution)/shard_map/ppermute | solution.py:253
  41.5 5.5 %collective-permute-start.25 = (bf16[64,1024]{1,0:T(8,128)(2,1)S(1)}, bf16[64,1024]{1,0:T(8,128)(2,1)S(1)}, u32[]{:S(2)}, u32[]{:S(2)}) collective-permute-start(bf16[64,1024]{1,0:T(8,128)(2,1)S(1)} %get-tuple-element.139), channel_id=1, source_target_pairs={{0,4},{1,5},{2,6},{3,7},{4,0},{5,1},{6,2},{7,3},{8,12},{9,13},{10,... | collective-permute-start | bytes 393224 | tf_op jit(solution)/shard_map/ppermute | solution.py:253
  42.1 7.6 %collective-permute-start.27 = (bf16[64,1024]{1,0:T(8,128)(2,1)S(1)}, bf16[64,1024]{1,0:T(8,128)(2,1)S(1)}, u32[]{:S(2)}, u32[]{:S(2)}) collective-permute-start(bf16[64,1024]{1,0:T(8,128)(2,1)S(1)} %get-tuple-element.145), channel_id=1, source_target_pairs={{0,2},{1,3},{2,0},{3,1},{4,6},{5,7},{6,4},{7,5},{8,10},{9,11},{10,... | collective-permute-start | bytes 393224 | tf_op jit(solution)/shard_map/ppermute | solution.py:253
  43.4 8.1 %collective-permute-start.29 = (bf16[64,1024]{1,0:T(8,128)(2,1)S(1)}, bf16[64,1024]{1,0:T(8,128)(2,1)S(1)}, u32[]{:S(2)}, u32[]{:S(2)}) collective-permute-start(bf16[64,1024]{1,0:T(8,128)(2,1)S(1)} %get-tuple-element.150), channel_id=1, source_target_pairs={{0,2},{1,3},{2,0},{3,1},{4,6},{5,7},{6,4},{7,5},{8,10},{9,11},{10,... | collective-permute-start | bytes 393224 | tf_op jit(solution)/shard_map/ppermute | solution.py:253
  47.1 8.7 %collective-permute-start.26 = (bf16[64,1024]{1,0:T(8,128)(2,1)S(1)}, bf16[64,1024]{1,0:T(8,128)(2,1)S(1)}, u32[]{:S(2)}, u32[]{:S(2)}) collective-permute-start(bf16[64,1024]{1,0:T(8,128)(2,1)S(1)} %get-tuple-element.143), channel_id=1, source_target_pairs={{0,8},{1,9},{2,10},{3,11},{4,12},{5,13},{6,14},{7,15},{8,0},{9,1},... | collective-permute-start | bytes 393224 | tf_op jit(solution)/shard_map/ppermute | solution.py:253
  49.7 6.6 %collective-permute-start.28 = (bf16[64,1024]{1,0:T(8,128)(2,1)S(1)}, bf16[64,1024]{1,0:T(8,128)(2,1)S(1)}, u32[]{:S(2)}, u32[]{:S(2)}) collective-permute-start(bf16[64,1024]{1,0:T(8,128)(2,1)S(1)} %get-tuple-element.149), channel_id=1, source_target_pairs={{0,4},{1,5},{2,6},{3,7},{4,0},{5,1},{6,2},{7,3},{8,12},{9,13},{10,... | collective-permute-start | bytes 393224 | tf_op jit(solution)/shard_map/ppermute | solution.py:253
  (6 other events, 9.4 us)

commit v22 on v21

--- a/solution.py
+++ b/solution.py
@@ -296,7 +296,7 @@
             blocks = []
             for k in ks:
                 near = [block[k], other[k]]
-                far[k] = [swap(one, 1) for one in near]
+                far[k] = far.get(k) or [swap(one, 1) for one in near]
                 blocks += near + far[k]
             result = step(
                 functools.partial(expert_kernel, count),
@@ -325,13 +325,15 @@
         block = {0: mine, 2: tie(z_2), 1: z_1}
         block[3] = swap(block[2], 4)
         other[0] = y_0
-        gather(2, [block[1], block[3], y_0])
-        gather(1)
+        far[0] = [swap(mine, 1), swap(y_0, 1)]
+        gather(2, [block[1], block[3], far[0][0]])
+        gather(1, [far[0][1]])
         compute(2)
-        gather(3)
+        gather(3, came[2])
         reduce_core(2)
         compute(3)
-        reduce_core(3, [y_came[2]])
+        other[0] = tie(other[0], [y_came[2]])
+        reduce_core(3)
         compute(1, 0)
         z_3 = swap(reduce_y(3), 4)
         reduce_core(1)

time: 57.3 us -> 55.3 us (0.965)
  starting transfers between devices: 24.1 us -> 22.4 us
    ppermute x30, starting transfers between devices: 24.1 us -> 22.4 us  [swap(): return lax.ppermute(x, 'exp', [(i, i ^ bits) for i in range(n_dev)])]
    pallas_call x17 -> x18, Pallas kernels: 16 us -> 16 us  [call(): pl.pallas_call(body_with_chain if reads_chain else body, out_shape=list(o...]
  transfers between devices with their start and end apart: 30 -> 30, of which waited for: 11 -> 9; matrix products, arithmetic and copies ran while one was open for 0% -> 0% of each run, Pallas kernels for 26% -> 27%
where the time goes in v22:
time: 55.3 us; the launch traced here: 55.1 us
  starting transfers between devices  22.4 us (41%)
  Pallas kernels  16.8 us (30%)
  waiting for transfers between devices  15.8 us (29%)
    ppermute x30, starting transfers between devices, swap(): return lax.ppermute(x, 'exp', [(i, i ^ bits) for i in range(n_dev)])  22.4 us
    pallas_call x18, Pallas kernels, call(): pl.pallas_call(body_with_chain if reads_chain else body, out_shape=list(o...  16 us
    ppermute x30, waiting for transfers between devices, swap(): return lax.ppermute(x, 'exp', [(i, i ^ bits) for i in range(n_dev)])  15.8 us
  transfers between devices with their start and end apart: 30, of which 9 were waited for; matrix products, arithmetic and copies ran while one was open for 0% of the time, Pallas kernels for 27%

profile of v22, /device:TPU:0, one launch (start us, length us, event | category | flops | bytes accessed | tf_op | source)
XLA Modules:
  0.0 55.1 jit_solution(12752493653920925331)
XLA Ops:
  0.0 1.0 %pack.1.refs_3_.refs_4_.refs_0_.refs_1_ = bf16[64,1152]{1,0:T(8,128)(2,1)S(1)} custom-call(s32[8,64]{1,0:T(8,128)} %bitcast.4, bf16[64,1024]{1,0:T(8,128)(2,1)} %refs_1_.2, bf16[2,1024]{1,0:T(2,128)(2,1)} %bitcast.2), custom_call_target="tpu_custom_call" | custom-call | bytes 10000 | tf_op jit(solution)/shard_map/pack/pallas_call | solution.py:232
  1.0 4.1 %collective-permute-start.1 = (bf16[64,1152]{1,0:T(8,128)(2,1)S(1)}, bf16[64,1152]{1,0:T(8,128)(2,1)S(1)}, u32[]{:S(2)}, u32[]{:S(2)}) collective-permute-start(bf16[64,1152]{1,0:T(8,128)(2,1)S(1)} %pack.1.refs_3_.refs_4_.refs_0_.refs_1_), channel_id=1, source_target_pairs={{0,8},{1,9},{2,10},{3,11},{4,12},{5,13},{6,14},{7,15},{8,0},{9,1},... | collective-permute-start | bytes 442376 | tf_op jit(solution)/shard_map/ppermute | solution.py:253
  5.1 1.5 %collective-permute-start.7 = (bf16[64,1152]{1,0:T(8,128)(2,1)S(1)}, bf16[64,1152]{1,0:T(8,128)(2,1)S(1)}, u32[]{:S(2)}, u32[]{:S(2)}) collective-permute-start(bf16[64,1152]{1,0:T(8,128)(2,1)S(1)} %pack.1.refs_3_.refs_4_.refs_0_.refs_1_), channel_id=1, source_target_pairs={{0,2},{1,3},{2,0},{3,1},{4,6},{5,7},{6,4},{7,5},{8,10},{9,11},{10,... | collective-permute-start | bytes 442376 | tf_op jit(solution)/shard_map/ppermute | solution.py:253
  6.6 1.6 %collective-permute-start.2 = (bf16[64,1152]{1,0:T(8,128)(2,1)S(1)}, bf16[64,1152]{1,0:T(8,128)(2,1)S(1)}, u32[]{:S(2)}, u32[]{:S(2)}) collective-permute-start(bf16[64,1152]{1,0:T(8,128)(2,1)S(1)} %pack.1.refs_3_.refs_4_.refs_0_.refs_1_), channel_id=1, source_target_pairs={{0,4},{1,5},{2,6},{3,7},{4,0},{5,1},{6,2},{7,3},{8,12},{9,13},{10,... | collective-permute-start | bytes 442376 | tf_op jit(solution)/shard_map/ppermute | solution.py:253
  8.2 4.7 %load.1 = (bf16[1024,128]{1,0:T(8,128)(2,1)S(1)}, bf16[2,1024,2048]{2,1,0:T(8,128)(2,1)S(1)}, bf16[2,1024,1024]{2,1,0:T(8,128)(2,1)S(1)}) custom-call(bf16[2,1024]{1,0:T(2,128)(2,1)} %bitcast.3, bf16[2,1024,2048]{2,1,0:T(8,128)(2,1)} %refs_1_.3, bf16[2,1024,1024]{2,1,0:T(8,128)(2,1)} %refs_2_.1, bf16[64,1152]{1,0:T(8,128)(2,1)S(1)} %pack.1.refs_3_.refs_4_.refs_0_.refs_1_), custom_call_target="tpu_custom_call" | custom-call | bytes 10000 | tf_op jit(solution)/shard_map/load/pallas_call | solution.py:232
  12.9 0.8 %collective-permute-start.4 = (bf16[64,1152]{1,0:T(8,128)(2,1)S(1)}, bf16[64,1152]{1,0:T(8,128)(2,1)S(1)}, u32[]{:S(2)}, u32[]{:S(2)}) collective-permute-start(bf16[64,1152]{1,0:T(8,128)(2,1)S(1)} %get-tuple-element.85.refs_0_.refs_9_), channel_id=1, source_target_pairs={{0,2},{1,3},{2,0},{3,1},{4,6},{5,7},{6,4},{7,5},{8,10},{9,11},{10,... | collective-permute-start | bytes 442376 | tf_op jit(solution)/shard_map/ppermute | solution.py:253
  13.8 0.6 %collective-permute-start.3 = (bf16[64,1152]{1,0:T(8,128)(2,1)S(1)}, bf16[64,1152]{1,0:T(8,128)(2,1)S(1)}, u32[]{:S(2)}, u32[]{:S(2)}) collective-permute-start(bf16[64,1152]{1,0:T(8,128)(2,1)S(1)} %get-tuple-element.85.refs_0_.refs_9_), channel_id=1, source_target_pairs={{0,4},{1,5},{2,6},{3,7},{4,0},{5,1},{6,2},{7,3},{8,12},{9,13},{10,... | collective-permute-start | bytes 442376 | tf_op jit(solution)/shard_map/ppermute | solution.py:253
  14.8 1.1 %collective-permute-start.9 = (bf16[64,1152]{1,0:T(8,128)(2,1)S(1)}, bf16[64,1152]{1,0:T(8,128)(2,1)S(1)}, u32[]{:S(2)}, u32[]{:S(2)}) collective-permute-start(bf16[64,1152]{1,0:T(8,128)(2,1)S(1)} %collective-permute-done.2.refs_0_.refs_5_), channel_id=1, source_target_pairs={{0,2},{1,3},{2,0},{3,1},{4,6},{5,7},{6,4},{7,5},{8,10},{9,11},{10,... | collective-permute-start | bytes 442376 | tf_op jit(solution)/shard_map/ppermute | solution.py:253
  16.0 3.6 %collective-permute-done.4.refs_6_ = bf16[64,1152]{1,0:T(8,128)(2,1)S(1)} collective-permute-done((bf16[64,1152]{1,0:T(8,128)(2,1)S(1)}, bf16[64,1152]{1,0:T(8,128)(2,1)S(1)}, u32[]{:S(2)}, u32[]{:S(2)}) %collective-permute-start.4) | collective-permute-done | bytes 147488 | tf_op jit(solution)/shard_map/ppermute | solution.py:253
  19.6 1.4 %collective-permute-start.12 = (bf16[64,1152]{1,0:T(8,128)(2,1)S(1)}, bf16[64,1152]{1,0:T(8,128)(2,1)S(1)}, u32[]{:S(2)}, u32[]{:S(2)}) collective-permute-start(bf16[64,1152]{1,0:T(8,128)(2,1)S(1)} %collective-permute-done.3.refs_1_.refs_0_.refs_13_), channel_id=1, source_target_pairs={{0,2},{1,3},{2,0},{3,1},{4,6},{5,7},{6,4},{7,5},{8,10},{9,11},{10,... | collective-permute-start | bytes 442376 | tf_op jit(solution)/shard_map/ppermute | solution.py:253
  21.0 1.4 %collective-permute-done.9.refs_4_ = bf16[64,1152]{1,0:T(8,128)(2,1)S(1)} collective-permute-done((bf16[64,1152]{1,0:T(8,128)(2,1)S(1)}, bf16[64,1152]{1,0:T(8,128)(2,1)S(1)}, u32[]{:S(2)}, u32[]{:S(2)}) %collective-permute-start.9) | collective-permute-done | bytes 147488 | tf_op jit(solution)/shard_map/ppermute | solution.py:253
  22.4 2.5 %expert.3 = (f32[128,1024]{1,0:T(8,128)S(1)}, bf16[64,1024]{1,0:T(8,128)(2,1)S(1)}, bf16[64,1024]{1,0:T(8,128)(2,1)S(1)}, bf16[1024,128]{1,0:T(8,128)(2,1)S(1)},...) custom-call(bf16[64,1152]{1,0:T(8,128)(2,1)S(1)} %get-tuple-element., ...), custom_call_target="tpu_custom_call", output_to_operand_aliasing={{3}: (4, {}), {4}: (5, {}), {5}: (6, {})} | custom-call | bytes 10000 | tf_op jit(solution)/shard_map/expert/pallas_call | solution.py:232
  27.4 0.6 %collective-permute-start.13 = (bf16[64,1024]{1,0:T(8,128)(2,1)S(1)}, bf16[64,1024]{1,0:T(8,128)(2,1)S(1)}, u32[]{:S(2)}, u32[]{:S(2)}) collective-permute-start(bf16[64,1024]{1,0:T(8,128)(2,1)S(1)} %get-tuple-element.105), channel_id=1, source_target_pairs={{0,2},{1,3},{2,0},{3,1},{4,6},{5,7},{6,4},{7,5},{8,10},{9,11},{10,... | collective-permute-start | bytes 393224 | tf_op jit(solution)/shard_map/ppermute | solution.py:253
  28.0 2.6 %expert.4 = (f32[128,1024]{1,0:T(8,128)S(1)}, bf16[64,1024]{1,0:T(8,128)(2,1)S(1)}, bf16[64,1024]{1,0:T(8,128)(2,1)S(1)}, bf16[1024,128]{1,0:T(8,128)(2,1)S(1)},...) custom-call(bf16[64,1152]{1,0:T(8,128)(2,1)S(1)} %collective-permute, ...), custom_call_target="tpu_custom_call", output_to_operand_aliasing={{3}: (4, {}), {4}: (5, {}), {5}: (6, {})} | custom-call | bytes 10000 | tf_op jit(solution)/shard_map/expert/pallas_call | solution.py:232
  31.2 1.9 %collective-permute-done.13.refs_0_.refs_1_ = bf16[64,1024]{1,0:T(8,128)(2,1)S(1)} collective-permute-done((bf16[64,1024]{1,0:T(8,128)(2,1)S(1)}, bf16[64,1024]{1,0:T(8,128)(2,1)S(1)}, u32[]{:S(2)}, u32[]{:S(2)}) %collective-permute-start.13) | collective-permute-done | bytes 131104 | tf_op jit(solution)/shard_map/ppermute | solution.py:253
  33.2 0.8 %collective-permute-start.24 = (bf16[64,1024]{1,0:T(8,128)(2,1)S(1)}, bf16[64,1024]{1,0:T(8,128)(2,1)S(1)}, u32[]{:S(2)}, u32[]{:S(2)}) collective-permute-start(bf16[64,1024]{1,0:T(8,128)(2,1)S(1)} %get-tuple-element.131), channel_id=1, source_target_pairs={{0,2},{1,3},{2,0},{3,1},{4,6},{5,7},{6,4},{7,5},{8,10},{9,11},{10,... | collective-permute-start | bytes 393224 | tf_op jit(solution)/shard_map/ppermute | solution.py:253
  34.0 4.7 %expert.5 = (f32[128,1024]{1,0:T(8,128)S(1)}, f32[128,1024]{1,0:T(8,128)S(1)}, bf16[64,1024]{1,0:T(8,128)(2,1)S(1)}, bf16[64,1024]{1,0:T(8,128)(2,1)S(1)}, bf16[...) custom-call(bf16[64,1152]{1,0:T(8,128)(2,1)S(1)} %collective-permute, ...), custom_call_target="tpu_custom_call", output_to_operand_aliasing={{6}: (8, {}), {7}: (9, {}), {8}: (10, {})} | custom-call | bytes 10000 | tf_op jit(solution)/shard_map/expert/pallas_call | solution.py:232
  40.4 1.3 %collective-permute-start.27 = (bf16[64,1024]{1,0:T(8,128)(2,1)S(1)}, bf16[64,1024]{1,0:T(8,128)(2,1)S(1)}, u32[]{:S(2)}, u32[]{:S(2)}) collective-permute-start(bf16[64,1024]{1,0:T(8,128)(2,1)S(1)} %get-tuple-element.153), channel_id=1, source_target_pairs={{0,2},{1,3},{2,0},{3,1},{4,6},{5,7},{6,4},{7,5},{8,10},{9,11},{10,... | collective-permute-start | bytes 393224 | tf_op jit(solution)/shard_map/ppermute | solution.py:253
  41.8 0.8 %collective-permute-start.29 = (bf16[64,1024]{1,0:T(8,128)(2,1)S(1)}, bf16[64,1024]{1,0:T(8,128)(2,1)S(1)}, u32[]{:S(2)}, u32[]{:S(2)}) collective-permute-start(bf16[64,1024]{1,0:T(8,128)(2,1)S(1)} %get-tuple-element.158), channel_id=1, source_target_pairs={{0,2},{1,3},{2,0},{3,1},{4,6},{5,7},{6,4},{7,5},{8,10},{9,11},{10,... | collective-permute-start | bytes 393224 | tf_op jit(solution)/shard_map/ppermute | solution.py:253
  42.9 2.5 %collective-permute-done.25.refs_2_ = bf16[64,1024]{1,0:T(8,128)(2,1)S(1)} collective-permute-done((bf16[64,1024]{1,0:T(8,128)(2,1)S(1)}, bf16[64,1024]{1,0:T(8,128)(2,1)S(1)}, u32[]{:S(2)}, u32[]{:S(2)}) %collective-permute-start.25) | collective-permute-done | bytes 131104 | tf_op jit(solution)/shard_map/ppermute | solution.py:253
  45.4 1.8 %collective-permute-start.26 = (bf16[64,1024]{1,0:T(8,128)(2,1)S(1)}, bf16[64,1024]{1,0:T(8,128)(2,1)S(1)}, u32[]{:S(2)}, u32[]{:S(2)}) collective-permute-start(bf16[64,1024]{1,0:T(8,128)(2,1)S(1)} %get-tuple-element.151), channel_id=1, source_target_pairs={{0,8},{1,9},{2,10},{3,11},{4,12},{5,13},{6,14},{7,15},{8,0},{9,1},... | collective-permute-start | bytes 393224 | tf_op jit(solution)/shard_map/ppermute | solution.py:253
  47.2 1.8 %collective-permute-start.28 = (bf16[64,1024]{1,0:T(8,128)(2,1)S(1)}, bf16[64,1024]{1,0:T(8,128)(2,1)S(1)}, u32[]{:S(2)}, u32[]{:S(2)}) collective-permute-start(bf16[64,1024]{1,0:T(8,128)(2,1)S(1)} %get-tuple-element.157), channel_id=1, source_target_pairs={{0,4},{1,5},{2,6},{3,7},{4,0},{5,1},{6,2},{7,3},{8,12},{9,13},{10,... | collective-permute-start | bytes 393224 | tf_op jit(solution)/shard_map/ppermute | solution.py:253
  49.0 4.9 %collective-permute-done.26.refs_1_ = bf16[64,1024]{1,0:T(8,128)(2,1)S(1)} collective-permute-done((bf16[64,1024]{1,0:T(8,128)(2,1)S(1)}, bf16[64,1024]{1,0:T(8,128)(2,1)S(1)}, u32[]{:S(2)}, u32[]{:S(2)}) %collective-permute-start.26) | collective-permute-done | bytes 131104 | tf_op jit(solution)/shard_map/ppermute | solution.py:253
  54.4 0.8 %finish.1 = bf16[64,1024]{1,0:T(8,128)(2,1)} custom-call(f32[64,128]{1,0:T(8,128)S(1)} %get-tuple-element.144.scores_ref, f32[64,1024]{1,0:T(8,128)S(1)} %get-tuple-element.145.refs_0_, bf16[64,1024]{1,0:T(8,128)(2,1)S(1)} %collective-permute-done.26.refs_1_, bf16[64,1024]{1,0:T(8,128)(2,1)S(1)} %collective-permute-done.28.refs_2_, ...), custom_call_target="tpu_custom_call" | custom-call | tf_op jit(solution)/shard_map/finish/pallas_call | solution.py:366
  (55 shorter events, 6.2 us)
Async XLA Ops:
  1.0 11.9 %collective-permute-start.1 = (bf16[64,1152]{1,0:T(8,128)(2,1)S(1)}, bf16[64,1152]{1,0:T(8,128)(2,1)S(1)}, u32[]{:S(2)}, u32[]{:S(2)}) collective-permute-start(bf16[64,1152]{1,0:T(8,128)(2,1)S(1)} %pack.1.refs_3_.refs_4_.refs_0_.refs_1_), channel_id=1, source_target_pairs={{0,8},{1,9},{2,10},{3,11},{4,12},{5,13},{6,14},{7,15},{8,0},{9,1},... | collective-permute-start | bytes 442376 | tf_op jit(solution)/shard_map/ppermute | solution.py:253
  5.1 9.3 %collective-permute-start.7 = (bf16[64,1152]{1,0:T(8,128)(2,1)S(1)}, bf16[64,1152]{1,0:T(8,128)(2,1)S(1)}, u32[]{:S(2)}, u32[]{:S(2)}) collective-permute-start(bf16[64,1152]{1,0:T(8,128)(2,1)S(1)} %pack.1.refs_3_.refs_4_.refs_0_.refs_1_), channel_id=1, source_target_pairs={{0,2},{1,3},{2,0},{3,1},{4,6},{5,7},{6,4},{7,5},{8,10},{9,11},{10,... | collective-permute-start | bytes 442376 | tf_op jit(solution)/shard_map/ppermute | solution.py:253
  6.6 7.7 %collective-permute-start.2 = (bf16[64,1152]{1,0:T(8,128)(2,1)S(1)}, bf16[64,1152]{1,0:T(8,128)(2,1)S(1)}, u32[]{:S(2)}, u32[]{:S(2)}) collective-permute-start(bf16[64,1152]{1,0:T(8,128)(2,1)S(1)} %pack.1.refs_3_.refs_4_.refs_0_.refs_1_), channel_id=1, source_target_pairs={{0,4},{1,5},{2,6},{3,7},{4,0},{5,1},{6,2},{7,3},{8,12},{9,13},{10,... | collective-permute-start | bytes 442376 | tf_op jit(solution)/shard_map/ppermute | solution.py:253
  8.2 6.7 %collective-permute-start = (bf16[64,1152]{1,0:T(8,128)(2,1)S(1)}, bf16[64,1152]{1,0:T(8,128)(2,1)S(1)}, u32[]{:S(2)}, u32[]{:S(2)}) collective-permute-start(bf16[64,1152]{1,0:T(8,128)(2,1)S(1)} %pack.1.refs_3_.refs_4_.refs_0_.refs_1_), channel_id=1, source_target_pairs={{0,1},{1,0},{2,3},{3,2},{4,5},{5,4},{6,7},{7,6},{8,9},{9,8},{10,11... | collective-permute-start | bytes 442376 | tf_op jit(solution)/shard_map/ppermute | solution.py:253
  12.9 6.7 %collective-permute-start.4 = (bf16[64,1152]{1,0:T(8,128)(2,1)S(1)}, bf16[64,1152]{1,0:T(8,128)(2,1)S(1)}, u32[]{:S(2)}, u32[]{:S(2)}) collective-permute-start(bf16[64,1152]{1,0:T(8,128)(2,1)S(1)} %get-tuple-element.85.refs_0_.refs_9_), channel_id=1, source_target_pairs={{0,2},{1,3},{2,0},{3,1},{4,6},{5,7},{6,4},{7,5},{8,10},{9,11},{10,... | collective-permute-start | bytes 442376 | tf_op jit(solution)/shard_map/ppermute | solution.py:253
  13.8 5.9 %collective-permute-start.3 = (bf16[64,1152]{1,0:T(8,128)(2,1)S(1)}, bf16[64,1152]{1,0:T(8,128)(2,1)S(1)}, u32[]{:S(2)}, u32[]{:S(2)}) collective-permute-start(bf16[64,1152]{1,0:T(8,128)(2,1)S(1)} %get-tuple-element.85.refs_0_.refs_9_), channel_id=1, source_target_pairs={{0,4},{1,5},{2,6},{3,7},{4,0},{5,1},{6,2},{7,3},{8,12},{9,13},{10,... | collective-permute-start | bytes 442376 | tf_op jit(solution)/shard_map/ppermute | solution.py:253
  14.3 8.1 %collective-permute-start.5 = (bf16[64,1152]{1,0:T(8,128)(2,1)S(1)}, bf16[64,1152]{1,0:T(8,128)(2,1)S(1)}, u32[]{:S(2)}, u32[]{:S(2)}) collective-permute-start(bf16[64,1152]{1,0:T(8,128)(2,1)S(1)} %get-tuple-element.85.refs_0_.refs_9_), channel_id=1, source_target_pairs={{0,1},{1,0},{2,3},{3,2},{4,5},{5,4},{6,7},{7,6},{8,9},{9,8},{10,11... | collective-permute-start | bytes 442376 | tf_op jit(solution)/shard_map/ppermute | solution.py:253
  14.3 6.7 %collective-permute-start.8 = (bf16[64,1152]{1,0:T(8,128)(2,1)S(1)}, bf16[64,1152]{1,0:T(8,128)(2,1)S(1)}, u32[]{:S(2)}, u32[]{:S(2)}) collective-permute-start(bf16[64,1152]{1,0:T(8,128)(2,1)S(1)} %collective-permute-done.7.refs_4_), channel_id=1, source_target_pairs={{0,1},{1,0},{2,3},{3,2},{4,5},{5,4},{6,7},{7,6},{8,9},{9,8},{10,11... | collective-permute-start | bytes 442376 | tf_op jit(solution)/shard_map/ppermute | solution.py:253
  14.8 7.6 %collective-permute-start.9 = (bf16[64,1152]{1,0:T(8,128)(2,1)S(1)}, bf16[64,1152]{1,0:T(8,128)(2,1)S(1)}, u32[]{:S(2)}, u32[]{:S(2)}) collective-permute-start(bf16[64,1152]{1,0:T(8,128)(2,1)S(1)} %collective-permute-done.2.refs_0_.refs_5_), channel_id=1, source_target_pairs={{0,2},{1,3},{2,0},{3,1},{4,6},{5,7},{6,4},{7,5},{8,10},{9,11},{10,... | collective-permute-start | bytes 442376 | tf_op jit(solution)/shard_map/ppermute | solution.py:253
  19.6 2.8 %collective-permute-start.6 = (bf16[64,1152]{1,0:T(8,128)(2,1)S(1)}, bf16[64,1152]{1,0:T(8,128)(2,1)S(1)}, u32[]{:S(2)}, u32[]{:S(2)}) collective-permute-start(bf16[64,1152]{1,0:T(8,128)(2,1)S(1)} %get-tuple-element.89.refs_1_.refs_11_), channel_id=1, source_target_pairs={{0,1},{1,0},{2,3},{3,2},{4,5},{5,4},{6,7},{7,6},{8,9},{9,8},{10,11... | collective-permute-start | bytes 442376 | tf_op jit(solution)/shard_map/ppermute | solution.py:253
  19.6 6.3 %collective-permute-start.12 = (bf16[64,1152]{1,0:T(8,128)(2,1)S(1)}, bf16[64,1152]{1,0:T(8,128)(2,1)S(1)}, u32[]{:S(2)}, u32[]{:S(2)}) collective-permute-start(bf16[64,1152]{1,0:T(8,128)(2,1)S(1)} %collective-permute-done.3.refs_1_.refs_0_.refs_13_), channel_id=1, source_target_pairs={{0,2},{1,3},{2,0},{3,1},{4,6},{5,7},{6,4},{7,5},{8,10},{9,11},{10,... | collective-permute-start | bytes 442376 | tf_op jit(solution)/shard_map/ppermute | solution.py:253
  25.5 2.5 %collective-permute-start.14 = (bf16[64,1152]{1,0:T(8,128)(2,1)S(1)}, bf16[64,1152]{1,0:T(8,128)(2,1)S(1)}, u32[]{:S(2)}, u32[]{:S(2)}) collective-permute-start(bf16[64,1152]{1,0:T(8,128)(2,1)S(1)} %collective-permute-done.3.refs_1_.refs_0_.refs_13_), channel_id=1, source_target_pairs={{0,1},{1,0},{2,3},{3,2},{4,5},{5,4},{6,7},{7,6},{8,9},{9,8},{10,11... | collective-permute-start | bytes 442376 | tf_op jit(solution)/shard_map/ppermute | solution.py:253
  26.9 7.1 %collective-permute-start.16 = (bf16[64,1152]{1,0:T(8,128)(2,1)S(1)}, bf16[64,1152]{1,0:T(8,128)(2,1)S(1)}, u32[]{:S(2)}, u32[]{:S(2)}) collective-permute-start(bf16[64,1152]{1,0:T(8,128)(2,1)S(1)} %collective-permute-done.2.refs_0_.refs_5_), channel_id=1, source_target_pairs={{0,1},{1,0},{2,3},{3,2},{4,5},{5,4},{6,7},{7,6},{8,9},{9,8},{10,11... | collective-permute-start | bytes 442376 | tf_op jit(solution)/shard_map/ppermute | solution.py:253
  27.1 6.9 %collective-permute-start.17 = (bf16[64,1152]{1,0:T(8,128)(2,1)S(1)}, bf16[64,1152]{1,0:T(8,128)(2,1)S(1)}, u32[]{:S(2)}, u32[]{:S(2)}) collective-permute-start(bf16[64,1152]{1,0:T(8,128)(2,1)S(1)} %get-tuple-element.114.refs_1_.refs_7_), channel_id=1, source_target_pairs={{0,1},{1,0},{2,3},{3,2},{4,5},{5,4},{6,7},{7,6},{8,9},{9,8},{10,11... | collective-permute-start | bytes 442376 | tf_op jit(solution)/shard_map/ppermute | solution.py:253
  27.4 5.7 %collective-permute-start.13 = (bf16[64,1024]{1,0:T(8,128)(2,1)S(1)}, bf16[64,1024]{1,0:T(8,128)(2,1)S(1)}, u32[]{:S(2)}, u32[]{:S(2)}) collective-permute-start(bf16[64,1024]{1,0:T(8,128)(2,1)S(1)} %get-tuple-element.105), channel_id=1, source_target_pairs={{0,2},{1,3},{2,0},{3,1},{4,6},{5,7},{6,4},{7,5},{8,10},{9,11},{10,... | collective-permute-start | bytes 393224 | tf_op jit(solution)/shard_map/ppermute | solution.py:253
  30.6 2.5 %collective-permute-start.18 = (bf16[64,1024]{1,0:T(8,128)(2,1)S(1)}, bf16[64,1024]{1,0:T(8,128)(2,1)S(1)}, u32[]{:S(2)}, u32[]{:S(2)}) collective-permute-start(bf16[64,1024]{1,0:T(8,128)(2,1)S(1)} %get-tuple-element.116), channel_id=1, source_target_pairs={{0,1},{1,0},{2,3},{3,2},{4,5},{5,4},{6,7},{7,6},{8,9},{9,8},{10,11... | collective-permute-start | bytes 393224 | tf_op jit(solution)/shard_map/ppermute | solution.py:253
  33.2 6.6 %collective-permute-start.24 = (bf16[64,1024]{1,0:T(8,128)(2,1)S(1)}, bf16[64,1024]{1,0:T(8,128)(2,1)S(1)}, u32[]{:S(2)}, u32[]{:S(2)}) collective-permute-start(bf16[64,1024]{1,0:T(8,128)(2,1)S(1)} %get-tuple-element.131), channel_id=1, source_target_pairs={{0,2},{1,3},{2,0},{3,1},{4,6},{5,7},{6,4},{7,5},{8,10},{9,11},{10,... | collective-permute-start | bytes 393224 | tf_op jit(solution)/shard_map/ppermute | solution.py:253
  39.3 2.4 %collective-permute-start.20 = (bf16[64,1024]{1,0:T(8,128)(2,1)S(1)}, bf16[64,1024]{1,0:T(8,128)(2,1)S(1)}, u32[]{:S(2)}, u32[]{:S(2)}) collective-permute-start(bf16[64,1024]{1,0:T(8,128)(2,1)S(1)} %get-tuple-element.125), channel_id=1, source_target_pairs={{0,1},{1,0},{2,3},{3,2},{4,5},{5,4},{6,7},{7,6},{8,9},{9,8},{10,11... | collective-permute-start | bytes 393224 | tf_op jit(solution)/shard_map/ppermute | solution.py:253
  39.4 2.4 %collective-permute-start.21 = (bf16[64,1024]{1,0:T(8,128)(2,1)S(1)}, bf16[64,1024]{1,0:T(8,128)(2,1)S(1)}, u32[]{:S(2)}, u32[]{:S(2)}) collective-permute-start(bf16[64,1024]{1,0:T(8,128)(2,1)S(1)} %get-tuple-element.126), channel_id=1, source_target_pairs={{0,1},{1,0},{2,3},{3,2},{4,5},{5,4},{6,7},{7,6},{8,9},{9,8},{10,11... | collective-permute-start | bytes 393224 | tf_op jit(solution)/shard_map/ppermute | solution.py:253
  39.8 5.5 %collective-permute-start.25 = (bf16[64,1024]{1,0:T(8,128)(2,1)S(1)}, bf16[64,1024]{1,0:T(8,128)(2,1)S(1)}, u32[]{:S(2)}, u32[]{:S(2)}) collective-permute-start(bf16[64,1024]{1,0:T(8,128)(2,1)S(1)} %get-tuple-element.147), channel_id=1, source_target_pairs={{0,4},{1,5},{2,6},{3,7},{4,0},{5,1},{6,2},{7,3},{8,12},{9,13},{10,... | collective-permute-start | bytes 393224 | tf_op jit(solution)/shard_map/ppermute | solution.py:253
  40.4 6.8 %collective-permute-start.27 = (bf16[64,1024]{1,0:T(8,128)(2,1)S(1)}, bf16[64,1024]{1,0:T(8,128)(2,1)S(1)}, u32[]{:S(2)}, u32[]{:S(2)}) collective-permute-start(bf16[64,1024]{1,0:T(8,128)(2,1)S(1)} %get-tuple-element.153), channel_id=1, source_target_pairs={{0,2},{1,3},{2,0},{3,1},{4,6},{5,7},{6,4},{7,5},{8,10},{9,11},{10,... | collective-permute-start | bytes 393224 | tf_op jit(solution)/shard_map/ppermute | solution.py:253
  41.8 7.3 %collective-permute-start.29 = (bf16[64,1024]{1,0:T(8,128)(2,1)S(1)}, bf16[64,1024]{1,0:T(8,128)(2,1)S(1)}, u32[]{:S(2)}, u32[]{:S(2)}) collective-permute-start(bf16[64,1024]{1,0:T(8,128)(2,1)S(1)} %get-tuple-element.158), channel_id=1, source_target_pairs={{0,2},{1,3},{2,0},{3,1},{4,6},{5,7},{6,4},{7,5},{8,10},{9,11},{10,... | collective-permute-start | bytes 393224 | tf_op jit(solution)/shard_map/ppermute | solution.py:253
  45.4 8.5 %collective-permute-start.26 = (bf16[64,1024]{1,0:T(8,128)(2,1)S(1)}, bf16[64,1024]{1,0:T(8,128)(2,1)S(1)}, u32[]{:S(2)}, u32[]{:S(2)}) collective-permute-start(bf16[64,1024]{1,0:T(8,128)(2,1)S(1)} %get-tuple-element.151), channel_id=1, source_target_pairs={{0,8},{1,9},{2,10},{3,11},{4,12},{5,13},{6,14},{7,15},{8,0},{9,1},... | collective-permute-start | bytes 393224 | tf_op jit(solution)/shard_map/ppermute | solution.py:253
  47.2 7.2 %collective-permute-start.28 = (bf16[64,1024]{1,0:T(8,128)(2,1)S(1)}, bf16[64,1024]{1,0:T(8,128)(2,1)S(1)}, u32[]{:S(2)}, u32[]{:S(2)}) collective-permute-start(bf16[64,1024]{1,0:T(8,128)(2,1)S(1)} %get-tuple-element.157), channel_id=1, source_target_pairs={{0,4},{1,5},{2,6},{3,7},{4,0},{5,1},{6,2},{7,3},{8,12},{9,13},{10,... | collective-permute-start | bytes 393224 | tf_op jit(solution)/shard_map/ppermute | solution.py:253
  (6 other events, 9.8 us)

commit v23 on v22

--- a/solution.py
+++ b/solution.py
@@ -12,7 +12,7 @@
 TAIL = 128
 LINE = 16
 SCALE = 2.0**40
-STEP = 256
+STEP = 512
 PIECE = 256
 
 
@@ -326,11 +326,11 @@
         block[3] = swap(block[2], 4)
         other[0] = y_0
         far[0] = [swap(mine, 1), swap(y_0, 1)]
-        gather(2, [block[1], block[3], far[0][0]])
-        gather(1, [far[0][1]])
+        gather(2, [block[1], block[3], y_0])
+        gather(1)
         compute(2)
         gather(3, came[2])
-        reduce_core(2)
+        reduce_core(2, far[0])
         compute(3)
         other[0] = tie(other[0], [y_came[2]])
         reduce_core(3)

time: 55.3 us -> 54.8 us (level)
  waiting for transfers between devices: 15.8 us -> 13.2 us
  starting transfers between devices: 22.4 us -> 24.5 us
    ppermute x30, waiting for transfers between devices: 15.8 us -> 13.2 us  [swap(): return lax.ppermute(x, 'exp', [(i, i ^ bits) for i in range(n_dev)])]
    ppermute x30, starting transfers between devices: 22.4 us -> 24.5 us  [swap(): return lax.ppermute(x, 'exp', [(i, i ^ bits) for i in range(n_dev)])]
where the time goes in v23:
time: 54.8 us; the launch traced here: 54.6 us
  starting transfers between devices  24.5 us (45%)
  Pallas kernels  16.7 us (30%)
  waiting for transfers between devices  13.2 us (24%)
    ppermute x30, starting transfers between devices, swap(): return lax.ppermute(x, 'exp', [(i, i ^ bits) for i in range(n_dev)])  24.5 us
    pallas_call x18, Pallas kernels, call(): pl.pallas_call(body_with_chain if reads_chain else body, out_shape=list(o...  15.9 us
    ppermute x30, waiting for transfers between devices, swap(): return lax.ppermute(x, 'exp', [(i, i ^ bits) for i in range(n_dev)])  13.2 us
  transfers between devices with their start and end apart: 30, of which 9 were waited for; matrix products, arithmetic and copies ran while one was open for 0% of the time, Pallas kernels for 27%

profile of v23, /device:TPU:0, one launch (start us, length us, event | category | flops | bytes accessed | tf_op | source)
XLA Modules:
  0.0 54.6 jit_solution(6713753264988105632)
XLA Ops:
  0.0 1.0 %pack.1.refs_3_.refs_4_.refs_0_.refs_1_ = bf16[64,1152]{1,0:T(8,128)(2,1)S(1)} custom-call(s32[8,64]{1,0:T(8,128)} %bitcast.4, bf16[64,1024]{1,0:T(8,128)(2,1)} %refs_1_.2, bf16[2,1024]{1,0:T(2,128)(2,1)} %bitcast.2), custom_call_target="tpu_custom_call" | custom-call | bytes 10000 | tf_op jit(solution)/shard_map/pack/pallas_call | solution.py:232
  1.0 4.1 %collective-permute-start.1 = (bf16[64,1152]{1,0:T(8,128)(2,1)S(1)}, bf16[64,1152]{1,0:T(8,128)(2,1)S(1)}, u32[]{:S(2)}, u32[]{:S(2)}) collective-permute-start(bf16[64,1152]{1,0:T(8,128)(2,1)S(1)} %pack.1.refs_3_.refs_4_.refs_0_.refs_1_), channel_id=1, source_target_pairs={{0,8},{1,9},{2,10},{3,11},{4,12},{5,13},{6,14},{7,15},{8,0},{9,1},... | collective-permute-start | bytes 442376 | tf_op jit(solution)/shard_map/ppermute | solution.py:253
  5.1 1.5 %collective-permute-start.4 = (bf16[64,1152]{1,0:T(8,128)(2,1)S(1)}, bf16[64,1152]{1,0:T(8,128)(2,1)S(1)}, u32[]{:S(2)}, u32[]{:S(2)}) collective-permute-start(bf16[64,1152]{1,0:T(8,128)(2,1)S(1)} %pack.1.refs_3_.refs_4_.refs_0_.refs_1_), channel_id=1, source_target_pairs={{0,2},{1,3},{2,0},{3,1},{4,6},{5,7},{6,4},{7,5},{8,10},{9,11},{10,... | collective-permute-start | bytes 442376 | tf_op jit(solution)/shard_map/ppermute | solution.py:253
  6.6 1.6 %collective-permute-start.2 = (bf16[64,1152]{1,0:T(8,128)(2,1)S(1)}, bf16[64,1152]{1,0:T(8,128)(2,1)S(1)}, u32[]{:S(2)}, u32[]{:S(2)}) collective-permute-start(bf16[64,1152]{1,0:T(8,128)(2,1)S(1)} %pack.1.refs_3_.refs_4_.refs_0_.refs_1_), channel_id=1, source_target_pairs={{0,4},{1,5},{2,6},{3,7},{4,0},{5,1},{6,2},{7,3},{8,12},{9,13},{10,... | collective-permute-start | bytes 442376 | tf_op jit(solution)/shard_map/ppermute | solution.py:253
  8.2 4.7 %load.1 = (bf16[1024,128]{1,0:T(8,128)(2,1)S(1)}, bf16[2,1024,2048]{2,1,0:T(8,128)(2,1)S(1)}, bf16[2,1024,1024]{2,1,0:T(8,128)(2,1)S(1)}) custom-call(bf16[2,1024]{1,0:T(2,128)(2,1)} %bitcast.3, bf16[2,1024,2048]{2,1,0:T(8,128)(2,1)} %refs_1_.3, bf16[2,1024,1024]{2,1,0:T(8,128)(2,1)} %refs_2_.1, bf16[64,1152]{1,0:T(8,128)(2,1)S(1)} %pack.1.refs_3_.refs_4_.refs_0_.refs_1_), custom_call_target="tpu_custom_call" | custom-call | bytes 10000 | tf_op jit(solution)/shard_map/load/pallas_call | solution.py:232
  12.9 0.8 %collective-permute-start.5 = (bf16[64,1152]{1,0:T(8,128)(2,1)S(1)}, bf16[64,1152]{1,0:T(8,128)(2,1)S(1)}, u32[]{:S(2)}, u32[]{:S(2)}) collective-permute-start(bf16[64,1152]{1,0:T(8,128)(2,1)S(1)} %get-tuple-element.85.refs_0_.refs_9_), channel_id=1, source_target_pairs={{0,2},{1,3},{2,0},{3,1},{4,6},{5,7},{6,4},{7,5},{8,10},{9,11},{10,... | collective-permute-start | bytes 442376 | tf_op jit(solution)/shard_map/ppermute | solution.py:253
  14.3 1.1 %collective-permute-start.8 = (bf16[64,1152]{1,0:T(8,128)(2,1)S(1)}, bf16[64,1152]{1,0:T(8,128)(2,1)S(1)}, u32[]{:S(2)}, u32[]{:S(2)}) collective-permute-start(bf16[64,1152]{1,0:T(8,128)(2,1)S(1)} %collective-permute-done.2.refs_0_.refs_5_), channel_id=1, source_target_pairs={{0,2},{1,3},{2,0},{3,1},{4,6},{5,7},{6,4},{7,5},{8,10},{9,11},{10,... | collective-permute-start | bytes 442376 | tf_op jit(solution)/shard_map/ppermute | solution.py:253
  15.5 3.4 %collective-permute-done.5.refs_6_ = bf16[64,1152]{1,0:T(8,128)(2,1)S(1)} collective-permute-done((bf16[64,1152]{1,0:T(8,128)(2,1)S(1)}, bf16[64,1152]{1,0:T(8,128)(2,1)S(1)}, u32[]{:S(2)}, u32[]{:S(2)}) %collective-permute-start.5) | collective-permute-done | bytes 147488 | tf_op jit(solution)/shard_map/ppermute | solution.py:253
  18.9 1.3 %collective-permute-start.12 = (bf16[64,1152]{1,0:T(8,128)(2,1)S(1)}, bf16[64,1152]{1,0:T(8,128)(2,1)S(1)}, u32[]{:S(2)}, u32[]{:S(2)}) collective-permute-start(bf16[64,1152]{1,0:T(8,128)(2,1)S(1)} %collective-permute-done.3.refs_1_.refs_0_.refs_13_), channel_id=1, source_target_pairs={{0,2},{1,3},{2,0},{3,1},{4,6},{5,7},{6,4},{7,5},{8,10},{9,11},{10,... | collective-permute-start | bytes 442376 | tf_op jit(solution)/shard_map/ppermute | solution.py:253
  20.2 1.1 %collective-permute-done.8.refs_3_ = bf16[64,1152]{1,0:T(8,128)(2,1)S(1)} collective-permute-done((bf16[64,1152]{1,0:T(8,128)(2,1)S(1)}, bf16[64,1152]{1,0:T(8,128)(2,1)S(1)}, u32[]{:S(2)}, u32[]{:S(2)}) %collective-permute-start.8) | collective-permute-done | bytes 147488 | tf_op jit(solution)/shard_map/ppermute | solution.py:253
  21.3 2.5 %expert.3 = (f32[128,1024]{1,0:T(8,128)S(1)}, bf16[64,1024]{1,0:T(8,128)(2,1)S(1)}, bf16[64,1024]{1,0:T(8,128)(2,1)S(1)}, bf16[1024,128]{1,0:T(8,128)(2,1)S(1)},...) custom-call(bf16[64,1152]{1,0:T(8,128)(2,1)S(1)} %get-tuple-element., ...), custom_call_target="tpu_custom_call", output_to_operand_aliasing={{3}: (4, {}), {4}: (5, {}), {5}: (6, {})} | custom-call | bytes 10000 | tf_op jit(solution)/shard_map/expert/pallas_call | solution.py:232
  26.3 1.3 %collective-permute-start.13 = (bf16[64,1024]{1,0:T(8,128)(2,1)S(1)}, bf16[64,1024]{1,0:T(8,128)(2,1)S(1)}, u32[]{:S(2)}, u32[]{:S(2)}) collective-permute-start(bf16[64,1024]{1,0:T(8,128)(2,1)S(1)} %get-tuple-element.105), channel_id=1, source_target_pairs={{0,2},{1,3},{2,0},{3,1},{4,6},{5,7},{6,4},{7,5},{8,10},{9,11},{10,... | collective-permute-start | bytes 393224 | tf_op jit(solution)/shard_map/ppermute | solution.py:253
  27.6 2.5 %expert.4 = (f32[128,1024]{1,0:T(8,128)S(1)}, bf16[64,1024]{1,0:T(8,128)(2,1)S(1)}, bf16[64,1024]{1,0:T(8,128)(2,1)S(1)}, bf16[1024,128]{1,0:T(8,128)(2,1)S(1)},...) custom-call(bf16[64,1152]{1,0:T(8,128)(2,1)S(1)} %collective-permute, ...), custom_call_target="tpu_custom_call", output_to_operand_aliasing={{3}: (4, {}), {4}: (5, {}), {5}: (6, {})} | custom-call | bytes 10000 | tf_op jit(solution)/shard_map/expert/pallas_call | solution.py:232
  30.7 1.3 %collective-permute-done.13.refs_0_.refs_1_ = bf16[64,1024]{1,0:T(8,128)(2,1)S(1)} collective-permute-done((bf16[64,1024]{1,0:T(8,128)(2,1)S(1)}, bf16[64,1024]{1,0:T(8,128)(2,1)S(1)}, u32[]{:S(2)}, u32[]{:S(2)}) %collective-permute-start.13) | collective-permute-done | bytes 131104 | tf_op jit(solution)/shard_map/ppermute | solution.py:253
  32.0 1.2 %collective-permute-start.24 = (bf16[64,1024]{1,0:T(8,128)(2,1)S(1)}, bf16[64,1024]{1,0:T(8,128)(2,1)S(1)}, u32[]{:S(2)}, u32[]{:S(2)}) collective-permute-start(bf16[64,1024]{1,0:T(8,128)(2,1)S(1)} %get-tuple-element.131), channel_id=1, source_target_pairs={{0,2},{1,3},{2,0},{3,1},{4,6},{5,7},{6,4},{7,5},{8,10},{9,11},{10,... | collective-permute-start | bytes 393224 | tf_op jit(solution)/shard_map/ppermute | solution.py:253
  33.2 4.7 %expert.5 = (f32[128,1024]{1,0:T(8,128)S(1)}, f32[128,1024]{1,0:T(8,128)S(1)}, bf16[64,1024]{1,0:T(8,128)(2,1)S(1)}, bf16[64,1024]{1,0:T(8,128)(2,1)S(1)}, bf16[...) custom-call(bf16[64,1152]{1,0:T(8,128)(2,1)S(1)} %collective-permute, ...), custom_call_target="tpu_custom_call", output_to_operand_aliasing={{6}: (8, {}), {7}: (9, {}), {8}: (10, {})} | custom-call | bytes 10000 | tf_op jit(solution)/shard_map/expert/pallas_call | solution.py:232
  39.0 1.0 %collective-permute-start.25 = (bf16[64,1024]{1,0:T(8,128)(2,1)S(1)}, bf16[64,1024]{1,0:T(8,128)(2,1)S(1)}, u32[]{:S(2)}, u32[]{:S(2)}) collective-permute-start(bf16[64,1024]{1,0:T(8,128)(2,1)S(1)} %get-tuple-element.147), channel_id=1, source_target_pairs={{0,4},{1,5},{2,6},{3,7},{4,0},{5,1},{6,2},{7,3},{8,12},{9,13},{10,... | collective-permute-start | bytes 393224 | tf_op jit(solution)/shard_map/ppermute | solution.py:253
  40.0 0.9 %collective-permute-start.27 = (bf16[64,1024]{1,0:T(8,128)(2,1)S(1)}, bf16[64,1024]{1,0:T(8,128)(2,1)S(1)}, u32[]{:S(2)}, u32[]{:S(2)}) collective-permute-start(bf16[64,1024]{1,0:T(8,128)(2,1)S(1)} %get-tuple-element.153), channel_id=1, source_target_pairs={{0,2},{1,3},{2,0},{3,1},{4,6},{5,7},{6,4},{7,5},{8,10},{9,11},{10,... | collective-permute-start | bytes 393224 | tf_op jit(solution)/shard_map/ppermute | solution.py:253
  40.9 1.3 %collective-permute-start.29 = (bf16[64,1024]{1,0:T(8,128)(2,1)S(1)}, bf16[64,1024]{1,0:T(8,128)(2,1)S(1)}, u32[]{:S(2)}, u32[]{:S(2)}) collective-permute-start(bf16[64,1024]{1,0:T(8,128)(2,1)S(1)} %get-tuple-element.158), channel_id=1, source_target_pairs={{0,2},{1,3},{2,0},{3,1},{4,6},{5,7},{6,4},{7,5},{8,10},{9,11},{10,... | collective-permute-start | bytes 393224 | tf_op jit(solution)/shard_map/ppermute | solution.py:253
  42.5 2.0 %collective-permute-done.25.refs_2_ = bf16[64,1024]{1,0:T(8,128)(2,1)S(1)} collective-permute-done((bf16[64,1024]{1,0:T(8,128)(2,1)S(1)}, bf16[64,1024]{1,0:T(8,128)(2,1)S(1)}, u32[]{:S(2)}, u32[]{:S(2)}) %collective-permute-start.25) | collective-permute-done | bytes 131104 | tf_op jit(solution)/shard_map/ppermute | solution.py:253
  44.6 2.6 %collective-permute-start.26 = (bf16[64,1024]{1,0:T(8,128)(2,1)S(1)}, bf16[64,1024]{1,0:T(8,128)(2,1)S(1)}, u32[]{:S(2)}, u32[]{:S(2)}) collective-permute-start(bf16[64,1024]{1,0:T(8,128)(2,1)S(1)} %get-tuple-element.151), channel_id=1, source_target_pairs={{0,8},{1,9},{2,10},{3,11},{4,12},{5,13},{6,14},{7,15},{8,0},{9,1},... | collective-permute-start | bytes 393224 | tf_op jit(solution)/shard_map/ppermute | solution.py:253
  47.2 1.8 %collective-permute-start.28 = (bf16[64,1024]{1,0:T(8,128)(2,1)S(1)}, bf16[64,1024]{1,0:T(8,128)(2,1)S(1)}, u32[]{:S(2)}, u32[]{:S(2)}) collective-permute-start(bf16[64,1024]{1,0:T(8,128)(2,1)S(1)} %get-tuple-element.157), channel_id=1, source_target_pairs={{0,4},{1,5},{2,6},{3,7},{4,0},{5,1},{6,2},{7,3},{8,12},{9,13},{10,... | collective-permute-start | bytes 393224 | tf_op jit(solution)/shard_map/ppermute | solution.py:253
  49.0 4.2 %collective-permute-done.26.refs_1_ = bf16[64,1024]{1,0:T(8,128)(2,1)S(1)} collective-permute-done((bf16[64,1024]{1,0:T(8,128)(2,1)S(1)}, bf16[64,1024]{1,0:T(8,128)(2,1)S(1)}, u32[]{:S(2)}, u32[]{:S(2)}) %collective-permute-start.26) | collective-permute-done | bytes 131104 | tf_op jit(solution)/shard_map/ppermute | solution.py:253
  53.8 0.8 %finish.1 = bf16[64,1024]{1,0:T(8,128)(2,1)} custom-call(f32[64,128]{1,0:T(8,128)S(1)} %get-tuple-element.144.scores_ref, f32[64,1024]{1,0:T(8,128)S(1)} %get-tuple-element.145.refs_0_, bf16[64,1024]{1,0:T(8,128)(2,1)S(1)} %collective-permute-done.26.refs_1_, bf16[64,1024]{1,0:T(8,128)(2,1)S(1)} %collective-permute-done.28.refs_2_, ...), custom_call_target="tpu_custom_call" | custom-call | tf_op jit(solution)/shard_map/finish/pallas_call | solution.py:366
  (55 shorter events, 5.8 us)
Async XLA Ops:
  1.0 11.9 %collective-permute-start.1 = (bf16[64,1152]{1,0:T(8,128)(2,1)S(1)}, bf16[64,1152]{1,0:T(8,128)(2,1)S(1)}, u32[]{:S(2)}, u32[]{:S(2)}) collective-permute-start(bf16[64,1152]{1,0:T(8,128)(2,1)S(1)} %pack.1.refs_3_.refs_4_.refs_0_.refs_1_), channel_id=1, source_target_pairs={{0,8},{1,9},{2,10},{3,11},{4,12},{5,13},{6,14},{7,15},{8,0},{9,1},... | collective-permute-start | bytes 442376 | tf_op jit(solution)/shard_map/ppermute | solution.py:253
  5.1 10.4 %collective-permute-start.4 = (bf16[64,1152]{1,0:T(8,128)(2,1)S(1)}, bf16[64,1152]{1,0:T(8,128)(2,1)S(1)}, u32[]{:S(2)}, u32[]{:S(2)}) collective-permute-start(bf16[64,1152]{1,0:T(8,128)(2,1)S(1)} %pack.1.refs_3_.refs_4_.refs_0_.refs_1_), channel_id=1, source_target_pairs={{0,2},{1,3},{2,0},{3,1},{4,6},{5,7},{6,4},{7,5},{8,10},{9,11},{10,... | collective-permute-start | bytes 442376 | tf_op jit(solution)/shard_map/ppermute | solution.py:253
  6.6 7.7 %collective-permute-start.2 = (bf16[64,1152]{1,0:T(8,128)(2,1)S(1)}, bf16[64,1152]{1,0:T(8,128)(2,1)S(1)}, u32[]{:S(2)}, u32[]{:S(2)}) collective-permute-start(bf16[64,1152]{1,0:T(8,128)(2,1)S(1)} %pack.1.refs_3_.refs_4_.refs_0_.refs_1_), channel_id=1, source_target_pairs={{0,4},{1,5},{2,6},{3,7},{4,0},{5,1},{6,2},{7,3},{8,12},{9,13},{10,... | collective-permute-start | bytes 442376 | tf_op jit(solution)/shard_map/ppermute | solution.py:253
  12.9 5.9 %collective-permute-start.5 = (bf16[64,1152]{1,0:T(8,128)(2,1)S(1)}, bf16[64,1152]{1,0:T(8,128)(2,1)S(1)}, u32[]{:S(2)}, u32[]{:S(2)}) collective-permute-start(bf16[64,1152]{1,0:T(8,128)(2,1)S(1)} %get-tuple-element.85.refs_0_.refs_9_), channel_id=1, source_target_pairs={{0,2},{1,3},{2,0},{3,1},{4,6},{5,7},{6,4},{7,5},{8,10},{9,11},{10,... | collective-permute-start | bytes 442376 | tf_op jit(solution)/shard_map/ppermute | solution.py:253
  13.8 5.1 %collective-permute-start.3 = (bf16[64,1152]{1,0:T(8,128)(2,1)S(1)}, bf16[64,1152]{1,0:T(8,128)(2,1)S(1)}, u32[]{:S(2)}, u32[]{:S(2)}) collective-permute-start(bf16[64,1152]{1,0:T(8,128)(2,1)S(1)} %get-tuple-element.85.refs_0_.refs_9_), channel_id=1, source_target_pairs={{0,4},{1,5},{2,6},{3,7},{4,0},{5,1},{6,2},{7,3},{8,12},{9,13},{10,... | collective-permute-start | bytes 442376 | tf_op jit(solution)/shard_map/ppermute | solution.py:253
  14.3 7.0 %collective-permute-start.6 = (bf16[64,1152]{1,0:T(8,128)(2,1)S(1)}, bf16[64,1152]{1,0:T(8,128)(2,1)S(1)}, u32[]{:S(2)}, u32[]{:S(2)}) collective-permute-start(bf16[64,1152]{1,0:T(8,128)(2,1)S(1)} %get-tuple-element.85.refs_0_.refs_9_), channel_id=1, source_target_pairs={{0,1},{1,0},{2,3},{3,2},{4,5},{5,4},{6,7},{7,6},{8,9},{9,8},{10,11... | collective-permute-start | bytes 442376 | tf_op jit(solution)/shard_map/ppermute | solution.py:253
  14.3 7.0 %collective-permute-start.8 = (bf16[64,1152]{1,0:T(8,128)(2,1)S(1)}, bf16[64,1152]{1,0:T(8,128)(2,1)S(1)}, u32[]{:S(2)}, u32[]{:S(2)}) collective-permute-start(bf16[64,1152]{1,0:T(8,128)(2,1)S(1)} %collective-permute-done.2.refs_0_.refs_5_), channel_id=1, source_target_pairs={{0,2},{1,3},{2,0},{3,1},{4,6},{5,7},{6,4},{7,5},{8,10},{9,11},{10,... | collective-permute-start | bytes 442376 | tf_op jit(solution)/shard_map/ppermute | solution.py:253
  18.9 2.4 %collective-permute-start.7 = (bf16[64,1152]{1,0:T(8,128)(2,1)S(1)}, bf16[64,1152]{1,0:T(8,128)(2,1)S(1)}, u32[]{:S(2)}, u32[]{:S(2)}) collective-permute-start(bf16[64,1152]{1,0:T(8,128)(2,1)S(1)} %get-tuple-element.89.refs_1_.refs_11_), channel_id=1, source_target_pairs={{0,1},{1,0},{2,3},{3,2},{4,5},{5,4},{6,7},{7,6},{8,9},{9,8},{10,11... | collective-permute-start | bytes 442376 | tf_op jit(solution)/shard_map/ppermute | solution.py:253
  18.9 6.3 %collective-permute-start.12 = (bf16[64,1152]{1,0:T(8,128)(2,1)S(1)}, bf16[64,1152]{1,0:T(8,128)(2,1)S(1)}, u32[]{:S(2)}, u32[]{:S(2)}) collective-permute-start(bf16[64,1152]{1,0:T(8,128)(2,1)S(1)} %collective-permute-done.3.refs_1_.refs_0_.refs_13_), channel_id=1, source_target_pairs={{0,2},{1,3},{2,0},{3,1},{4,6},{5,7},{6,4},{7,5},{8,10},{9,11},{10,... | collective-permute-start | bytes 442376 | tf_op jit(solution)/shard_map/ppermute | solution.py:253
  25.2 2.4 %collective-permute-start.14 = (bf16[64,1152]{1,0:T(8,128)(2,1)S(1)}, bf16[64,1152]{1,0:T(8,128)(2,1)S(1)}, u32[]{:S(2)}, u32[]{:S(2)}) collective-permute-start(bf16[64,1152]{1,0:T(8,128)(2,1)S(1)} %collective-permute-done.3.refs_1_.refs_0_.refs_13_), channel_id=1, source_target_pairs={{0,1},{1,0},{2,3},{3,2},{4,5},{5,4},{6,7},{7,6},{8,9},{9,8},{10,11... | collective-permute-start | bytes 442376 | tf_op jit(solution)/shard_map/ppermute | solution.py:253
  25.4 2.2 %collective-permute-start.15 = (bf16[64,1152]{1,0:T(8,128)(2,1)S(1)}, bf16[64,1152]{1,0:T(8,128)(2,1)S(1)}, u32[]{:S(2)}, u32[]{:S(2)}) collective-permute-start(bf16[64,1152]{1,0:T(8,128)(2,1)S(1)} %get-tuple-element.106.refs_1_.refs_15_), channel_id=1, source_target_pairs={{0,1},{1,0},{2,3},{3,2},{4,5},{5,4},{6,7},{7,6},{8,9},{9,8},{10,11... | collective-permute-start | bytes 442376 | tf_op jit(solution)/shard_map/ppermute | solution.py:253
  25.7 7.5 %collective-permute-start.16 = (bf16[64,1152]{1,0:T(8,128)(2,1)S(1)}, bf16[64,1152]{1,0:T(8,128)(2,1)S(1)}, u32[]{:S(2)}, u32[]{:S(2)}) collective-permute-start(bf16[64,1152]{1,0:T(8,128)(2,1)S(1)} %collective-permute-done.2.refs_0_.refs_5_), channel_id=1, source_target_pairs={{0,1},{1,0},{2,3},{3,2},{4,5},{5,4},{6,7},{7,6},{8,9},{9,8},{10,11... | collective-permute-start | bytes 442376 | tf_op jit(solution)/shard_map/ppermute | solution.py:253
  25.9 7.3 %collective-permute-start.17 = (bf16[64,1152]{1,0:T(8,128)(2,1)S(1)}, bf16[64,1152]{1,0:T(8,128)(2,1)S(1)}, u32[]{:S(2)}, u32[]{:S(2)}) collective-permute-start(bf16[64,1152]{1,0:T(8,128)(2,1)S(1)} %get-tuple-element.114.refs_1_.refs_7_), channel_id=1, source_target_pairs={{0,1},{1,0},{2,3},{3,2},{4,5},{5,4},{6,7},{7,6},{8,9},{9,8},{10,11... | collective-permute-start | bytes 442376 | tf_op jit(solution)/shard_map/ppermute | solution.py:253
  26.3 5.7 %collective-permute-start.13 = (bf16[64,1024]{1,0:T(8,128)(2,1)S(1)}, bf16[64,1024]{1,0:T(8,128)(2,1)S(1)}, u32[]{:S(2)}, u32[]{:S(2)}) collective-permute-start(bf16[64,1024]{1,0:T(8,128)(2,1)S(1)} %get-tuple-element.105), channel_id=1, source_target_pairs={{0,2},{1,3},{2,0},{3,1},{4,6},{5,7},{6,4},{7,5},{8,10},{9,11},{10,... | collective-permute-start | bytes 393224 | tf_op jit(solution)/shard_map/ppermute | solution.py:253
  32.0 7.0 %collective-permute-start.24 = (bf16[64,1024]{1,0:T(8,128)(2,1)S(1)}, bf16[64,1024]{1,0:T(8,128)(2,1)S(1)}, u32[]{:S(2)}, u32[]{:S(2)}) collective-permute-start(bf16[64,1024]{1,0:T(8,128)(2,1)S(1)} %get-tuple-element.131), channel_id=1, source_target_pairs={{0,2},{1,3},{2,0},{3,1},{4,6},{5,7},{6,4},{7,5},{8,10},{9,11},{10,... | collective-permute-start | bytes 393224 | tf_op jit(solution)/shard_map/ppermute | solution.py:253
  37.9 2.1 %collective-permute-start.22 = (bf16[64,1024]{1,0:T(8,128)(2,1)S(1)}, bf16[64,1024]{1,0:T(8,128)(2,1)S(1)}, u32[]{:S(2)}, u32[]{:S(2)}) collective-permute-start(bf16[64,1024]{1,0:T(8,128)(2,1)S(1)} %get-tuple-element.128), channel_id=1, source_target_pairs={{0,1},{1,0},{2,3},{3,2},{4,5},{5,4},{6,7},{7,6},{8,9},{9,8},{10,11... | collective-permute-start | bytes 393224 | tf_op jit(solution)/shard_map/ppermute | solution.py:253
  38.0 2.0 %collective-permute-start.23 = (bf16[64,1024]{1,0:T(8,128)(2,1)S(1)}, bf16[64,1024]{1,0:T(8,128)(2,1)S(1)}, u32[]{:S(2)}, u32[]{:S(2)}) collective-permute-start(bf16[64,1024]{1,0:T(8,128)(2,1)S(1)} %get-tuple-element.129), channel_id=1, source_target_pairs={{0,1},{1,0},{2,3},{3,2},{4,5},{5,4},{6,7},{7,6},{8,9},{9,8},{10,11... | collective-permute-start | bytes 393224 | tf_op jit(solution)/shard_map/ppermute | solution.py:253
  38.5 2.4 %collective-permute-start.20 = (bf16[64,1024]{1,0:T(8,128)(2,1)S(1)}, bf16[64,1024]{1,0:T(8,128)(2,1)S(1)}, u32[]{:S(2)}, u32[]{:S(2)}) collective-permute-start(bf16[64,1024]{1,0:T(8,128)(2,1)S(1)} %get-tuple-element.125), channel_id=1, source_target_pairs={{0,1},{1,0},{2,3},{3,2},{4,5},{5,4},{6,7},{7,6},{8,9},{9,8},{10,11... | collective-permute-start | bytes 393224 | tf_op jit(solution)/shard_map/ppermute | solution.py:253
  38.5 2.3 %collective-permute-start.21 = (bf16[64,1024]{1,0:T(8,128)(2,1)S(1)}, bf16[64,1024]{1,0:T(8,128)(2,1)S(1)}, u32[]{:S(2)}, u32[]{:S(2)}) collective-permute-start(bf16[64,1024]{1,0:T(8,128)(2,1)S(1)} %get-tuple-element.126), channel_id=1, source_target_pairs={{0,1},{1,0},{2,3},{3,2},{4,5},{5,4},{6,7},{7,6},{8,9},{9,8},{10,11... | collective-permute-start | bytes 393224 | tf_op jit(solution)/shard_map/ppermute | solution.py:253
  39.0 5.5 %collective-permute-start.25 = (bf16[64,1024]{1,0:T(8,128)(2,1)S(1)}, bf16[64,1024]{1,0:T(8,128)(2,1)S(1)}, u32[]{:S(2)}, u32[]{:S(2)}) collective-permute-start(bf16[64,1024]{1,0:T(8,128)(2,1)S(1)} %get-tuple-element.147), channel_id=1, source_target_pairs={{0,4},{1,5},{2,6},{3,7},{4,0},{5,1},{6,2},{7,3},{8,12},{9,13},{10,... | collective-permute-start | bytes 393224 | tf_op jit(solution)/shard_map/ppermute | solution.py:253
  40.0 7.2 %collective-permute-start.27 = (bf16[64,1024]{1,0:T(8,128)(2,1)S(1)}, bf16[64,1024]{1,0:T(8,128)(2,1)S(1)}, u32[]{:S(2)}, u32[]{:S(2)}) collective-permute-start(bf16[64,1024]{1,0:T(8,128)(2,1)S(1)} %get-tuple-element.153), channel_id=1, source_target_pairs={{0,2},{1,3},{2,0},{3,1},{4,6},{5,7},{6,4},{7,5},{8,10},{9,11},{10,... | collective-permute-start | bytes 393224 | tf_op jit(solution)/shard_map/ppermute | solution.py:253
  40.9 8.1 %collective-permute-start.29 = (bf16[64,1024]{1,0:T(8,128)(2,1)S(1)}, bf16[64,1024]{1,0:T(8,128)(2,1)S(1)}, u32[]{:S(2)}, u32[]{:S(2)}) collective-permute-start(bf16[64,1024]{1,0:T(8,128)(2,1)S(1)} %get-tuple-element.158), channel_id=1, source_target_pairs={{0,2},{1,3},{2,0},{3,1},{4,6},{5,7},{6,4},{7,5},{8,10},{9,11},{10,... | collective-permute-start | bytes 393224 | tf_op jit(solution)/shard_map/ppermute | solution.py:253
  44.6 8.7 %collective-permute-start.26 = (bf16[64,1024]{1,0:T(8,128)(2,1)S(1)}, bf16[64,1024]{1,0:T(8,128)(2,1)S(1)}, u32[]{:S(2)}, u32[]{:S(2)}) collective-permute-start(bf16[64,1024]{1,0:T(8,128)(2,1)S(1)} %get-tuple-element.151), channel_id=1, source_target_pairs={{0,8},{1,9},{2,10},{3,11},{4,12},{5,13},{6,14},{7,15},{8,0},{9,1},... | collective-permute-start | bytes 393224 | tf_op jit(solution)/shard_map/ppermute | solution.py:253
  47.2 6.6 %collective-permute-start.28 = (bf16[64,1024]{1,0:T(8,128)(2,1)S(1)}, bf16[64,1024]{1,0:T(8,128)(2,1)S(1)}, u32[]{:S(2)}, u32[]{:S(2)}) collective-permute-start(bf16[64,1024]{1,0:T(8,128)(2,1)S(1)} %get-tuple-element.157), channel_id=1, source_target_pairs={{0,4},{1,5},{2,6},{3,7},{4,0},{5,1},{6,2},{7,3},{8,12},{9,13},{10,... | collective-permute-start | bytes 393224 | tf_op jit(solution)/shard_map/ppermute | solution.py:253
  (6 other events, 9.9 us)

commit v24 on v23

--- a/solution.py
+++ b/solution.py
@@ -334,9 +334,12 @@
         compute(3)
         other[0] = tie(other[0], [y_came[2]])
         reduce_core(3)
-        compute(1, 0)
+        compute(1)
         z_3 = swap(reduce_y(3), 4)
+        compute(0)
         reduce_core(1)
+        z_2 = swap(reduce_y(2, z_3), 8)
+        z_1 = swap(reduce_y(1), 4)
         reduce_core(0)
         scores = None
         if n_dev == GROUP:
@@ -347,9 +350,8 @@
                 [mine, *packets],
                 scratch=[pltpu.VMEM((n_dev * local * lat // TAIL, TAIL), jnp.float32)],
             )[0]
-        z_2 = swap(reduce_y(2, z_3), 8)
-        z_1 = swap(reduce_y(1), 4)
-        return scores, (fold_keep[0], z_2, z_1, y_came[0])
+        keep_0 = call(tie_kernel, [], deps=[z_2], chain=[fold_keep[0]])[0]
+        return scores, (keep_0, z_2, z_1, y_came[0])
 
     packet = call(
         pack_kernel,

time: 54.8 us -> 55.9 us (1.020)
  waiting for transfers between devices: 13.2 us -> 14.3 us
    ppermute x30, waiting for transfers between devices: 13.2 us -> 14.3 us  [swap(): return lax.ppermute(x, 'exp', [(i, i ^ bits) for i in range(n_dev)])]
    pallas_call x18 -> x20, Pallas kernels: 15.9 us -> 16.2 us  [call(): pl.pallas_call(body_with_chain if reads_chain else body, out_shape=list(o...]
  transfers between devices with their start and end apart: 30 -> 30, of which waited for: 9 -> 11; matrix products, arithmetic and copies ran while one was open for 0% -> 0% of each run, Pallas kernels for 27% -> 27%
where the time goes in v24:
time: 55.9 us; the launch traced here: 55.6 us
  starting transfers between devices  24.3 us (43%)
  Pallas kernels  16.9 us (30%)
  waiting for transfers between devices  14.3 us (26%)
    ppermute x30, starting transfers between devices, swap(): return lax.ppermute(x, 'exp', [(i, i ^ bits) for i in range(n_dev)])  24.3 us
    pallas_call x20, Pallas kernels, call(): pl.pallas_call(body_with_chain if reads_chain else body, out_shape=list(o...  16.2 us
    ppermute x30, waiting for transfers between devices, swap(): return lax.ppermute(x, 'exp', [(i, i ^ bits) for i in range(n_dev)])  14.3 us
  transfers between devices with their start and end apart: 30, of which 11 were waited for; matrix products, arithmetic and copies ran while one was open for 0% of the time, Pallas kernels for 27%

profile of v24, /device:TPU:0, one launch (start us, length us, event | category | flops | bytes accessed | tf_op | source)
XLA Modules:
  0.0 55.6 jit_solution(4098783013094980558)
XLA Ops:
  0.0 1.0 %pack.1.refs_3_.refs_0_.refs_1_ = bf16[64,1152]{1,0:T(8,128)(2,1)S(1)} custom-call(s32[8,64]{1,0:T(8,128)} %bitcast.4, bf16[64,1024]{1,0:T(8,128)(2,1)} %refs_1_.2, bf16[2,1024]{1,0:T(2,128)(2,1)} %bitcast.2), custom_call_target="tpu_custom_call" | custom-call | bytes 10000 | tf_op jit(solution)/shard_map/pack/pallas_call | solution.py:232
  1.0 4.1 %collective-permute-start.1 = (bf16[64,1152]{1,0:T(8,128)(2,1)S(1)}, bf16[64,1152]{1,0:T(8,128)(2,1)S(1)}, u32[]{:S(2)}, u32[]{:S(2)}) collective-permute-start(bf16[64,1152]{1,0:T(8,128)(2,1)S(1)} %pack.1.refs_3_.refs_0_.refs_1_), channel_id=1, source_target_pairs={{0,8},{1,9},{2,10},{3,11},{4,12},{5,13},{6,14},{7,15},{8,0},{9,1},... | collective-permute-start | bytes 442376 | tf_op jit(solution)/shard_map/ppermute | solution.py:253
  5.1 1.5 %collective-permute-start.4 = (bf16[64,1152]{1,0:T(8,128)(2,1)S(1)}, bf16[64,1152]{1,0:T(8,128)(2,1)S(1)}, u32[]{:S(2)}, u32[]{:S(2)}) collective-permute-start(bf16[64,1152]{1,0:T(8,128)(2,1)S(1)} %pack.1.refs_3_.refs_0_.refs_1_), channel_id=1, source_target_pairs={{0,2},{1,3},{2,0},{3,1},{4,6},{5,7},{6,4},{7,5},{8,10},{9,11},{10,... | collective-permute-start | bytes 442376 | tf_op jit(solution)/shard_map/ppermute | solution.py:253
  6.6 1.6 %collective-permute-start.2 = (bf16[64,1152]{1,0:T(8,128)(2,1)S(1)}, bf16[64,1152]{1,0:T(8,128)(2,1)S(1)}, u32[]{:S(2)}, u32[]{:S(2)}) collective-permute-start(bf16[64,1152]{1,0:T(8,128)(2,1)S(1)} %pack.1.refs_3_.refs_0_.refs_1_), channel_id=1, source_target_pairs={{0,4},{1,5},{2,6},{3,7},{4,0},{5,1},{6,2},{7,3},{8,12},{9,13},{10,... | collective-permute-start | bytes 442376 | tf_op jit(solution)/shard_map/ppermute | solution.py:253
  8.2 4.7 %load.1 = (bf16[1024,128]{1,0:T(8,128)(2,1)S(1)}, bf16[2,1024,2048]{2,1,0:T(8,128)(2,1)S(1)}, bf16[2,1024,1024]{2,1,0:T(8,128)(2,1)S(1)}) custom-call(bf16[2,1024]{1,0:T(2,128)(2,1)} %bitcast.3, bf16[2,1024,2048]{2,1,0:T(8,128)(2,1)} %refs_1_.3, bf16[2,1024,1024]{2,1,0:T(8,128)(2,1)} %refs_2_.1, bf16[64,1152]{1,0:T(8,128)(2,1)S(1)} %pack.1.refs_3_.refs_0_.refs_1_), custom_call_target="tpu_custom_call" | custom-call | bytes 10000 | tf_op jit(solution)/shard_map/load/pallas_call | solution.py:232
  14.3 1.1 %collective-permute-start.8 = (bf16[64,1152]{1,0:T(8,128)(2,1)S(1)}, bf16[64,1152]{1,0:T(8,128)(2,1)S(1)}, u32[]{:S(2)}, u32[]{:S(2)}) collective-permute-start(bf16[64,1152]{1,0:T(8,128)(2,1)S(1)} %collective-permute-done.2.refs_0_.refs_5_), channel_id=1, source_target_pairs={{0,2},{1,3},{2,0},{3,1},{4,6},{5,7},{6,4},{7,5},{8,10},{9,11},{10,... | collective-permute-start | bytes 442376 | tf_op jit(solution)/shard_map/ppermute | solution.py:253
  15.5 3.4 %collective-permute-done.5.refs_6_ = bf16[64,1152]{1,0:T(8,128)(2,1)S(1)} collective-permute-done((bf16[64,1152]{1,0:T(8,128)(2,1)S(1)}, bf16[64,1152]{1,0:T(8,128)(2,1)S(1)}, u32[]{:S(2)}, u32[]{:S(2)}) %collective-permute-start.5) | collective-permute-done | bytes 147488 | tf_op jit(solution)/shard_map/ppermute | solution.py:253
  18.9 1.3 %collective-permute-start.12 = (bf16[64,1152]{1,0:T(8,128)(2,1)S(1)}, bf16[64,1152]{1,0:T(8,128)(2,1)S(1)}, u32[]{:S(2)}, u32[]{:S(2)}) collective-permute-start(bf16[64,1152]{1,0:T(8,128)(2,1)S(1)} %collective-permute-done.3.refs_1_.refs_0_.refs_13_), channel_id=1, source_target_pairs={{0,2},{1,3},{2,0},{3,1},{4,6},{5,7},{6,4},{7,5},{8,10},{9,11},{10,... | collective-permute-start | bytes 442376 | tf_op jit(solution)/shard_map/ppermute | solution.py:253
  20.2 1.1 %collective-permute-done.8.refs_3_ = bf16[64,1152]{1,0:T(8,128)(2,1)S(1)} collective-permute-done((bf16[64,1152]{1,0:T(8,128)(2,1)S(1)}, bf16[64,1152]{1,0:T(8,128)(2,1)S(1)}, u32[]{:S(2)}, u32[]{:S(2)}) %collective-permute-start.8) | collective-permute-done | bytes 147488 | tf_op jit(solution)/shard_map/ppermute | solution.py:253
  21.3 2.5 %expert.4 = (f32[128,1024]{1,0:T(8,128)S(1)}, bf16[64,1024]{1,0:T(8,128)(2,1)S(1)}, bf16[64,1024]{1,0:T(8,128)(2,1)S(1)}, bf16[1024,128]{1,0:T(8,128)(2,1)S(1)},...) custom-call(bf16[64,1152]{1,0:T(8,128)(2,1)S(1)} %get-tuple-element., ...), custom_call_target="tpu_custom_call", output_to_operand_aliasing={{3}: (4, {}), {4}: (5, {}), {5}: (6, {})} | custom-call | bytes 10000 | tf_op jit(solution)/shard_map/expert/pallas_call | solution.py:232
  26.3 1.3 %collective-permute-start.13 = (bf16[64,1024]{1,0:T(8,128)(2,1)S(1)}, bf16[64,1024]{1,0:T(8,128)(2,1)S(1)}, u32[]{:S(2)}, u32[]{:S(2)}) collective-permute-start(bf16[64,1024]{1,0:T(8,128)(2,1)S(1)} %get-tuple-element.108), channel_id=1, source_target_pairs={{0,2},{1,3},{2,0},{3,1},{4,6},{5,7},{6,4},{7,5},{8,10},{9,11},{10,... | collective-permute-start | bytes 393224 | tf_op jit(solution)/shard_map/ppermute | solution.py:253
  27.6 2.5 %expert.5 = (f32[128,1024]{1,0:T(8,128)S(1)}, bf16[64,1024]{1,0:T(8,128)(2,1)S(1)}, bf16[64,1024]{1,0:T(8,128)(2,1)S(1)}, bf16[1024,128]{1,0:T(8,128)(2,1)S(1)},...) custom-call(bf16[64,1152]{1,0:T(8,128)(2,1)S(1)} %collective-permute, ...), custom_call_target="tpu_custom_call", output_to_operand_aliasing={{3}: (4, {}), {4}: (5, {}), {5}: (6, {})} | custom-call | bytes 10000 | tf_op jit(solution)/shard_map/expert/pallas_call | solution.py:232
  30.7 1.3 %collective-permute-done.13.refs_0_.refs_1_ = bf16[64,1024]{1,0:T(8,128)(2,1)S(1)} collective-permute-done((bf16[64,1024]{1,0:T(8,128)(2,1)S(1)}, bf16[64,1024]{1,0:T(8,128)(2,1)S(1)}, u32[]{:S(2)}, u32[]{:S(2)}) %collective-permute-start.13) | collective-permute-done | bytes 131104 | tf_op jit(solution)/shard_map/ppermute | solution.py:253
  32.0 1.2 %collective-permute-start.20 = (bf16[64,1024]{1,0:T(8,128)(2,1)S(1)}, bf16[64,1024]{1,0:T(8,128)(2,1)S(1)}, u32[]{:S(2)}, u32[]{:S(2)}) collective-permute-start(bf16[64,1024]{1,0:T(8,128)(2,1)S(1)} %get-tuple-element.125), channel_id=1, source_target_pairs={{0,2},{1,3},{2,0},{3,1},{4,6},{5,7},{6,4},{7,5},{8,10},{9,11},{10,... | collective-permute-start | bytes 393224 | tf_op jit(solution)/shard_map/ppermute | solution.py:253
  33.2 2.5 %expert.6 = (f32[128,1024]{1,0:T(8,128)S(1)}, bf16[64,1024]{1,0:T(8,128)(2,1)S(1)}, bf16[64,1024]{1,0:T(8,128)(2,1)S(1)}, bf16[1024,128]{1,0:T(8,128)(2,1)S(1)},...) custom-call(bf16[64,1152]{1,0:T(8,128)(2,1)S(1)} %collective-permute, ...), custom_call_target="tpu_custom_call", output_to_operand_aliasing={{3}: (4, {}), {4}: (5, {}), {5}: (6, {})} | custom-call | bytes 10000 | tf_op jit(solution)/shard_map/expert/pallas_call | solution.py:232
  36.3 1.3 %collective-permute-done.20.refs_1_ = bf16[64,1024]{1,0:T(8,128)(2,1)S(1)} collective-permute-done((bf16[64,1024]{1,0:T(8,128)(2,1)S(1)}, bf16[64,1024]{1,0:T(8,128)(2,1)S(1)}, u32[]{:S(2)}, u32[]{:S(2)}) %collective-permute-start.20) | collective-permute-done | bytes 131104 | tf_op jit(solution)/shard_map/ppermute | solution.py:253
  37.5 0.9 %collective-permute-start.26 = (bf16[64,1024]{1,0:T(8,128)(2,1)S(1)}, bf16[64,1024]{1,0:T(8,128)(2,1)S(1)}, u32[]{:S(2)}, u32[]{:S(2)}) collective-permute-start(bf16[64,1024]{1,0:T(8,128)(2,1)S(1)} %get-tuple-element.147), channel_id=1, source_target_pairs={{0,4},{1,5},{2,6},{3,7},{4,0},{5,1},{6,2},{7,3},{8,12},{9,13},{10,... | collective-permute-start | bytes 393224 | tf_op jit(solution)/shard_map/ppermute | solution.py:253
  38.4 2.5 %expert.7 = (f32[128,1024]{1,0:T(8,128)S(1)}, bf16[64,1024]{1,0:T(8,128)(2,1)S(1)}, bf16[64,1024]{1,0:T(8,128)(2,1)S(1)}, bf16[1024,128]{1,0:T(8,128)(2,1)S(1)},...) custom-call(bf16[64,1152]{1,0:T(8,128)(2,1)S(1)} %pack.1.refs_3_.ref, ...), custom_call_target="tpu_custom_call", output_to_operand_aliasing={{3}: (4, {}), {4}: (5, {}), {5}: (6, {})} | custom-call | bytes 10000 | tf_op jit(solution)/shard_map/expert/pallas_call | solution.py:232
  41.0 1.0 %collective-permute-start.25 = (bf16[64,1024]{1,0:T(8,128)(2,1)S(1)}, bf16[64,1024]{1,0:T(8,128)(2,1)S(1)}, u32[]{:S(2)}, u32[]{:S(2)}) collective-permute-start(bf16[64,1024]{1,0:T(8,128)(2,1)S(1)} %get-tuple-element.145), channel_id=1, source_target_pairs={{0,2},{1,3},{2,0},{3,1},{4,6},{5,7},{6,4},{7,5},{8,10},{9,11},{10,... | collective-permute-start | bytes 393224 | tf_op jit(solution)/shard_map/ppermute | solution.py:253
  42.6 3.3 %collective-permute-start.27 = (bf16[64,1024]{1,0:T(8,128)(2,1)S(1)}, bf16[64,1024]{1,0:T(8,128)(2,1)S(1)}, u32[]{:S(2)}, u32[]{:S(2)}) collective-permute-start(bf16[64,1024]{1,0:T(8,128)(2,1)S(1)} %get-tuple-element.161), channel_id=1, source_target_pairs={{0,8},{1,9},{2,10},{3,11},{4,12},{5,13},{6,14},{7,15},{8,0},{9,1},... | collective-permute-start | bytes 393224 | tf_op jit(solution)/shard_map/ppermute | solution.py:253
  46.1 1.2 %collective-permute-start.29 = (bf16[64,1024]{1,0:T(8,128)(2,1)S(1)}, bf16[64,1024]{1,0:T(8,128)(2,1)S(1)}, u32[]{:S(2)}, u32[]{:S(2)}) collective-permute-start(bf16[64,1024]{1,0:T(8,128)(2,1)S(1)} %get-tuple-element.164), channel_id=1, source_target_pairs={{0,2},{1,3},{2,0},{3,1},{4,6},{5,7},{6,4},{7,5},{8,10},{9,11},{10,... | collective-permute-start | bytes 393224 | tf_op jit(solution)/shard_map/ppermute | solution.py:253
  47.3 0.9 %collective-permute-start.28 = (bf16[64,1024]{1,0:T(8,128)(2,1)S(1)}, bf16[64,1024]{1,0:T(8,128)(2,1)S(1)}, u32[]{:S(2)}, u32[]{:S(2)}) collective-permute-start(bf16[64,1024]{1,0:T(8,128)(2,1)S(1)} %get-tuple-element.163), channel_id=1, source_target_pairs={{0,4},{1,5},{2,6},{3,7},{4,0},{5,1},{6,2},{7,3},{8,12},{9,13},{10,... | collective-permute-start | bytes 393224 | tf_op jit(solution)/shard_map/ppermute | solution.py:253
  48.5 3.9 %collective-permute-done.27.refs_0_.refs_1_ = bf16[64,1024]{1,0:T(8,128)(2,1)S(1)} collective-permute-done((bf16[64,1024]{1,0:T(8,128)(2,1)S(1)}, bf16[64,1024]{1,0:T(8,128)(2,1)S(1)}, u32[]{:S(2)}, u32[]{:S(2)}) %collective-permute-start.27) | collective-permute-done | bytes 131104 | tf_op jit(solution)/shard_map/ppermute | solution.py:253
  52.4 2.5 %collective-permute-done.28.refs_2_ = bf16[64,1024]{1,0:T(8,128)(2,1)S(1)} collective-permute-done((bf16[64,1024]{1,0:T(8,128)(2,1)S(1)}, bf16[64,1024]{1,0:T(8,128)(2,1)S(1)}, u32[]{:S(2)}, u32[]{:S(2)}) %collective-permute-start.28) | collective-permute-done | bytes 131104 | tf_op jit(solution)/shard_map/ppermute | solution.py:253
  (57 shorter events, 7.1 us)
Async XLA Ops:
  1.0 11.9 %collective-permute-start.1 = (bf16[64,1152]{1,0:T(8,128)(2,1)S(1)}, bf16[64,1152]{1,0:T(8,128)(2,1)S(1)}, u32[]{:S(2)}, u32[]{:S(2)}) collective-permute-start(bf16[64,1152]{1,0:T(8,128)(2,1)S(1)} %pack.1.refs_3_.refs_0_.refs_1_), channel_id=1, source_target_pairs={{0,8},{1,9},{2,10},{3,11},{4,12},{5,13},{6,14},{7,15},{8,0},{9,1},... | collective-permute-start | bytes 442376 | tf_op jit(solution)/shard_map/ppermute | solution.py:253
  5.1 10.4 %collective-permute-start.4 = (bf16[64,1152]{1,0:T(8,128)(2,1)S(1)}, bf16[64,1152]{1,0:T(8,128)(2,1)S(1)}, u32[]{:S(2)}, u32[]{:S(2)}) collective-permute-start(bf16[64,1152]{1,0:T(8,128)(2,1)S(1)} %pack.1.refs_3_.refs_0_.refs_1_), channel_id=1, source_target_pairs={{0,2},{1,3},{2,0},{3,1},{4,6},{5,7},{6,4},{7,5},{8,10},{9,11},{10,... | collective-permute-start | bytes 442376 | tf_op jit(solution)/shard_map/ppermute | solution.py:253
  6.6 7.7 %collective-permute-start.2 = (bf16[64,1152]{1,0:T(8,128)(2,1)S(1)}, bf16[64,1152]{1,0:T(8,128)(2,1)S(1)}, u32[]{:S(2)}, u32[]{:S(2)}) collective-permute-start(bf16[64,1152]{1,0:T(8,128)(2,1)S(1)} %pack.1.refs_3_.refs_0_.refs_1_), channel_id=1, source_target_pairs={{0,4},{1,5},{2,6},{3,7},{4,0},{5,1},{6,2},{7,3},{8,12},{9,13},{10,... | collective-permute-start | bytes 442376 | tf_op jit(solution)/shard_map/ppermute | solution.py:253
  12.9 5.9 %collective-permute-start.5 = (bf16[64,1152]{1,0:T(8,128)(2,1)S(1)}, bf16[64,1152]{1,0:T(8,128)(2,1)S(1)}, u32[]{:S(2)}, u32[]{:S(2)}) collective-permute-start(bf16[64,1152]{1,0:T(8,128)(2,1)S(1)} %get-tuple-element.88.refs_0_.refs_9_), channel_id=1, source_target_pairs={{0,2},{1,3},{2,0},{3,1},{4,6},{5,7},{6,4},{7,5},{8,10},{9,11},{10,... | collective-permute-start | bytes 442376 | tf_op jit(solution)/shard_map/ppermute | solution.py:253
  13.8 5.1 %collective-permute-start.3 = (bf16[64,1152]{1,0:T(8,128)(2,1)S(1)}, bf16[64,1152]{1,0:T(8,128)(2,1)S(1)}, u32[]{:S(2)}, u32[]{:S(2)}) collective-permute-start(bf16[64,1152]{1,0:T(8,128)(2,1)S(1)} %get-tuple-element.88.refs_0_.refs_9_), channel_id=1, source_target_pairs={{0,4},{1,5},{2,6},{3,7},{4,0},{5,1},{6,2},{7,3},{8,12},{9,13},{10,... | collective-permute-start | bytes 442376 | tf_op jit(solution)/shard_map/ppermute | solution.py:253
  14.3 7.0 %collective-permute-start.6 = (bf16[64,1152]{1,0:T(8,128)(2,1)S(1)}, bf16[64,1152]{1,0:T(8,128)(2,1)S(1)}, u32[]{:S(2)}, u32[]{:S(2)}) collective-permute-start(bf16[64,1152]{1,0:T(8,128)(2,1)S(1)} %get-tuple-element.88.refs_0_.refs_9_), channel_id=1, source_target_pairs={{0,1},{1,0},{2,3},{3,2},{4,5},{5,4},{6,7},{7,6},{8,9},{9,8},{10,11... | collective-permute-start | bytes 442376 | tf_op jit(solution)/shard_map/ppermute | solution.py:253
  14.3 7.0 %collective-permute-start.8 = (bf16[64,1152]{1,0:T(8,128)(2,1)S(1)}, bf16[64,1152]{1,0:T(8,128)(2,1)S(1)}, u32[]{:S(2)}, u32[]{:S(2)}) collective-permute-start(bf16[64,1152]{1,0:T(8,128)(2,1)S(1)} %collective-permute-done.2.refs_0_.refs_5_), channel_id=1, source_target_pairs={{0,2},{1,3},{2,0},{3,1},{4,6},{5,7},{6,4},{7,5},{8,10},{9,11},{10,... | collective-permute-start | bytes 442376 | tf_op jit(solution)/shard_map/ppermute | solution.py:253
  18.9 2.4 %collective-permute-start.7 = (bf16[64,1152]{1,0:T(8,128)(2,1)S(1)}, bf16[64,1152]{1,0:T(8,128)(2,1)S(1)}, u32[]{:S(2)}, u32[]{:S(2)}) collective-permute-start(bf16[64,1152]{1,0:T(8,128)(2,1)S(1)} %get-tuple-element.92.refs_1_.refs_11_), channel_id=1, source_target_pairs={{0,1},{1,0},{2,3},{3,2},{4,5},{5,4},{6,7},{7,6},{8,9},{9,8},{10,11... | collective-permute-start | bytes 442376 | tf_op jit(solution)/shard_map/ppermute | solution.py:253
  18.9 6.3 %collective-permute-start.12 = (bf16[64,1152]{1,0:T(8,128)(2,1)S(1)}, bf16[64,1152]{1,0:T(8,128)(2,1)S(1)}, u32[]{:S(2)}, u32[]{:S(2)}) collective-permute-start(bf16[64,1152]{1,0:T(8,128)(2,1)S(1)} %collective-permute-done.3.refs_1_.refs_0_.refs_13_), channel_id=1, source_target_pairs={{0,2},{1,3},{2,0},{3,1},{4,6},{5,7},{6,4},{7,5},{8,10},{9,11},{10,... | collective-permute-start | bytes 442376 | tf_op jit(solution)/shard_map/ppermute | solution.py:253
  25.2 2.4 %collective-permute-start.14 = (bf16[64,1152]{1,0:T(8,128)(2,1)S(1)}, bf16[64,1152]{1,0:T(8,128)(2,1)S(1)}, u32[]{:S(2)}, u32[]{:S(2)}) collective-permute-start(bf16[64,1152]{1,0:T(8,128)(2,1)S(1)} %collective-permute-done.3.refs_1_.refs_0_.refs_13_), channel_id=1, source_target_pairs={{0,1},{1,0},{2,3},{3,2},{4,5},{5,4},{6,7},{7,6},{8,9},{9,8},{10,11... | collective-permute-start | bytes 442376 | tf_op jit(solution)/shard_map/ppermute | solution.py:253
  25.4 2.2 %collective-permute-start.15 = (bf16[64,1152]{1,0:T(8,128)(2,1)S(1)}, bf16[64,1152]{1,0:T(8,128)(2,1)S(1)}, u32[]{:S(2)}, u32[]{:S(2)}) collective-permute-start(bf16[64,1152]{1,0:T(8,128)(2,1)S(1)} %get-tuple-element.109.refs_1_.refs_15_), channel_id=1, source_target_pairs={{0,1},{1,0},{2,3},{3,2},{4,5},{5,4},{6,7},{7,6},{8,9},{9,8},{10,11... | collective-permute-start | bytes 442376 | tf_op jit(solution)/shard_map/ppermute | solution.py:253
  25.7 7.5 %collective-permute-start.16 = (bf16[64,1152]{1,0:T(8,128)(2,1)S(1)}, bf16[64,1152]{1,0:T(8,128)(2,1)S(1)}, u32[]{:S(2)}, u32[]{:S(2)}) collective-permute-start(bf16[64,1152]{1,0:T(8,128)(2,1)S(1)} %collective-permute-done.2.refs_0_.refs_5_), channel_id=1, source_target_pairs={{0,1},{1,0},{2,3},{3,2},{4,5},{5,4},{6,7},{7,6},{8,9},{9,8},{10,11... | collective-permute-start | bytes 442376 | tf_op jit(solution)/shard_map/ppermute | solution.py:253
  25.9 7.3 %collective-permute-start.17 = (bf16[64,1152]{1,0:T(8,128)(2,1)S(1)}, bf16[64,1152]{1,0:T(8,128)(2,1)S(1)}, u32[]{:S(2)}, u32[]{:S(2)}) collective-permute-start(bf16[64,1152]{1,0:T(8,128)(2,1)S(1)} %get-tuple-element.117.refs_1_.refs_7_), channel_id=1, source_target_pairs={{0,1},{1,0},{2,3},{3,2},{4,5},{5,4},{6,7},{7,6},{8,9},{9,8},{10,11... | collective-permute-start | bytes 442376 | tf_op jit(solution)/shard_map/ppermute | solution.py:253
  26.3 5.7 %collective-permute-start.13 = (bf16[64,1024]{1,0:T(8,128)(2,1)S(1)}, bf16[64,1024]{1,0:T(8,128)(2,1)S(1)}, u32[]{:S(2)}, u32[]{:S(2)}) collective-permute-start(bf16[64,1024]{1,0:T(8,128)(2,1)S(1)} %get-tuple-element.108), channel_id=1, source_target_pairs={{0,2},{1,3},{2,0},{3,1},{4,6},{5,7},{6,4},{7,5},{8,10},{9,11},{10,... | collective-permute-start | bytes 393224 | tf_op jit(solution)/shard_map/ppermute | solution.py:253
  32.0 5.5 %collective-permute-start.20 = (bf16[64,1024]{1,0:T(8,128)(2,1)S(1)}, bf16[64,1024]{1,0:T(8,128)(2,1)S(1)}, u32[]{:S(2)}, u32[]{:S(2)}) collective-permute-start(bf16[64,1024]{1,0:T(8,128)(2,1)S(1)} %get-tuple-element.125), channel_id=1, source_target_pairs={{0,2},{1,3},{2,0},{3,1},{4,6},{5,7},{6,4},{7,5},{8,10},{9,11},{10,... | collective-permute-start | bytes 393224 | tf_op jit(solution)/shard_map/ppermute | solution.py:253
  35.7 5.2 %collective-permute-start.23 = (bf16[64,1024]{1,0:T(8,128)(2,1)S(1)}, bf16[64,1024]{1,0:T(8,128)(2,1)S(1)}, u32[]{:S(2)}, u32[]{:S(2)}) collective-permute-start(bf16[64,1024]{1,0:T(8,128)(2,1)S(1)} %get-tuple-element.139), channel_id=1, source_target_pairs={{0,1},{1,0},{2,3},{3,2},{4,5},{5,4},{6,7},{7,6},{8,9},{9,8},{10,11... | collective-permute-start | bytes 393224 | tf_op jit(solution)/shard_map/ppermute | solution.py:253
  35.8 5.2 %collective-permute-start.24 = (bf16[64,1024]{1,0:T(8,128)(2,1)S(1)}, bf16[64,1024]{1,0:T(8,128)(2,1)S(1)}, u32[]{:S(2)}, u32[]{:S(2)}) collective-permute-start(bf16[64,1024]{1,0:T(8,128)(2,1)S(1)} %get-tuple-element.140), channel_id=1, source_target_pairs={{0,1},{1,0},{2,3},{3,2},{4,5},{5,4},{6,7},{7,6},{8,9},{9,8},{10,11... | collective-permute-start | bytes 393224 | tf_op jit(solution)/shard_map/ppermute | solution.py:253
  37.5 5.0 %collective-permute-start.26 = (bf16[64,1024]{1,0:T(8,128)(2,1)S(1)}, bf16[64,1024]{1,0:T(8,128)(2,1)S(1)}, u32[]{:S(2)}, u32[]{:S(2)}) collective-permute-start(bf16[64,1024]{1,0:T(8,128)(2,1)S(1)} %get-tuple-element.147), channel_id=1, source_target_pairs={{0,4},{1,5},{2,6},{3,7},{4,0},{5,1},{6,2},{7,3},{8,12},{9,13},{10,... | collective-permute-start | bytes 393224 | tf_op jit(solution)/shard_map/ppermute | solution.py:253
  41.0 5.0 %collective-permute-start.25 = (bf16[64,1024]{1,0:T(8,128)(2,1)S(1)}, bf16[64,1024]{1,0:T(8,128)(2,1)S(1)}, u32[]{:S(2)}, u32[]{:S(2)}) collective-permute-start(bf16[64,1024]{1,0:T(8,128)(2,1)S(1)} %get-tuple-element.145), channel_id=1, source_target_pairs={{0,2},{1,3},{2,0},{3,1},{4,6},{5,7},{6,4},{7,5},{8,10},{9,11},{10,... | collective-permute-start | bytes 393224 | tf_op jit(solution)/shard_map/ppermute | solution.py:253
  41.9 4.1 %collective-permute-start.21 = (bf16[64,1024]{1,0:T(8,128)(2,1)S(1)}, bf16[64,1024]{1,0:T(8,128)(2,1)S(1)}, u32[]{:S(2)}, u32[]{:S(2)}) collective-permute-start(bf16[64,1024]{1,0:T(8,128)(2,1)S(1)} %get-tuple-element.136), channel_id=1, source_target_pairs={{0,1},{1,0},{2,3},{3,2},{4,5},{5,4},{6,7},{7,6},{8,9},{9,8},{10,11... | collective-permute-start | bytes 393224 | tf_op jit(solution)/shard_map/ppermute | solution.py:253
  41.9 4.1 %collective-permute-start.22 = (bf16[64,1024]{1,0:T(8,128)(2,1)S(1)}, bf16[64,1024]{1,0:T(8,128)(2,1)S(1)}, u32[]{:S(2)}, u32[]{:S(2)}) collective-permute-start(bf16[64,1024]{1,0:T(8,128)(2,1)S(1)} %get-tuple-element.137), channel_id=1, source_target_pairs={{0,1},{1,0},{2,3},{3,2},{4,5},{5,4},{6,7},{7,6},{8,9},{9,8},{10,11... | collective-permute-start | bytes 393224 | tf_op jit(solution)/shard_map/ppermute | solution.py:253
  42.6 9.8 %collective-permute-start.27 = (bf16[64,1024]{1,0:T(8,128)(2,1)S(1)}, bf16[64,1024]{1,0:T(8,128)(2,1)S(1)}, u32[]{:S(2)}, u32[]{:S(2)}) collective-permute-start(bf16[64,1024]{1,0:T(8,128)(2,1)S(1)} %get-tuple-element.161), channel_id=1, source_target_pairs={{0,8},{1,9},{2,10},{3,11},{4,12},{5,13},{6,14},{7,15},{8,0},{9,1},... | collective-permute-start | bytes 393224 | tf_op jit(solution)/shard_map/ppermute | solution.py:253
  46.1 6.3 %collective-permute-start.29 = (bf16[64,1024]{1,0:T(8,128)(2,1)S(1)}, bf16[64,1024]{1,0:T(8,128)(2,1)S(1)}, u32[]{:S(2)}, u32[]{:S(2)}) collective-permute-start(bf16[64,1024]{1,0:T(8,128)(2,1)S(1)} %get-tuple-element.164), channel_id=1, source_target_pairs={{0,2},{1,3},{2,0},{3,1},{4,6},{5,7},{6,4},{7,5},{8,10},{9,11},{10,... | collective-permute-start | bytes 393224 | tf_op jit(solution)/shard_map/ppermute | solution.py:253
  47.3 7.6 %collective-permute-start.28 = (bf16[64,1024]{1,0:T(8,128)(2,1)S(1)}, bf16[64,1024]{1,0:T(8,128)(2,1)S(1)}, u32[]{:S(2)}, u32[]{:S(2)}) collective-permute-start(bf16[64,1024]{1,0:T(8,128)(2,1)S(1)} %get-tuple-element.163), channel_id=1, source_target_pairs={{0,4},{1,5},{2,6},{3,7},{4,0},{5,1},{6,2},{7,3},{8,12},{9,13},{10,... | collective-permute-start | bytes 393224 | tf_op jit(solution)/shard_map/ppermute | solution.py:253
  (6 other events, 9.9 us)

commit v25 on v23

--- a/solution.py
+++ b/solution.py
@@ -13,7 +13,7 @@
 LINE = 16
 SCALE = 2.0**40
 STEP = 512
-PIECE = 256
+PIECE = 128
 
 
 def pack_kernel(ids_hbm, row_hbm, router_hbm, out_ref, ids_ref, router_ref, sems):

time: 54.8 us -> 54.8 us (level)
  transfers between devices with their start and end apart: 30 -> 30, of which waited for: 9 -> 8; matrix products, arithmetic and copies ran while one was open for 0% -> 0% of each run, Pallas kernels for 27% -> 28%
where the time goes in v25:
time: 54.8 us; the launch traced here: 54.6 us
  starting transfers between devices  24.3 us (44%)
  Pallas kernels  16.8 us (31%)
  waiting for transfers between devices  13.3 us (24%)
    ppermute x30, starting transfers between devices, swap(): return lax.ppermute(x, 'exp', [(i, i ^ bits) for i in range(n_dev)])  24.3 us
    pallas_call x18, Pallas kernels, call(): pl.pallas_call(body_with_chain if reads_chain else body, out_shape=list(o...  16 us
    ppermute x30, waiting for transfers between devices, swap(): return lax.ppermute(x, 'exp', [(i, i ^ bits) for i in range(n_dev)])  13.3 us
  transfers between devices with their start and end apart: 30, of which 8 were waited for; matrix products, arithmetic and copies ran while one was open for 0% of the time, Pallas kernels for 28%

profile of v25, /device:TPU:0, one launch (start us, length us, event | category | flops | bytes accessed | tf_op | source)
XLA Modules:
  0.0 54.6 jit_solution(9442586325876317889)
XLA Ops:
  0.0 1.0 %pack.1.refs_3_.refs_4_.refs_0_.refs_1_ = bf16[64,1152]{1,0:T(8,128)(2,1)S(1)} custom-call(s32[8,64]{1,0:T(8,128)} %bitcast.4, bf16[64,1024]{1,0:T(8,128)(2,1)} %refs_1_.2, bf16[2,1024]{1,0:T(2,128)(2,1)} %bitcast.2), custom_call_target="tpu_custom_call" | custom-call | bytes 10000 | tf_op jit(solution)/shard_map/pack/pallas_call | solution.py:232
  1.0 4.1 %collective-permute-start.1 = (bf16[64,1152]{1,0:T(8,128)(2,1)S(1)}, bf16[64,1152]{1,0:T(8,128)(2,1)S(1)}, u32[]{:S(2)}, u32[]{:S(2)}) collective-permute-start(bf16[64,1152]{1,0:T(8,128)(2,1)S(1)} %pack.1.refs_3_.refs_4_.refs_0_.refs_1_), channel_id=1, source_target_pairs={{0,8},{1,9},{2,10},{3,11},{4,12},{5,13},{6,14},{7,15},{8,0},{9,1},... | collective-permute-start | bytes 442376 | tf_op jit(solution)/shard_map/ppermute | solution.py:253
  5.1 1.5 %collective-permute-start.4 = (bf16[64,1152]{1,0:T(8,128)(2,1)S(1)}, bf16[64,1152]{1,0:T(8,128)(2,1)S(1)}, u32[]{:S(2)}, u32[]{:S(2)}) collective-permute-start(bf16[64,1152]{1,0:T(8,128)(2,1)S(1)} %pack.1.refs_3_.refs_4_.refs_0_.refs_1_), channel_id=1, source_target_pairs={{0,2},{1,3},{2,0},{3,1},{4,6},{5,7},{6,4},{7,5},{8,10},{9,11},{10,... | collective-permute-start | bytes 442376 | tf_op jit(solution)/shard_map/ppermute | solution.py:253
  6.6 1.6 %collective-permute-start.2 = (bf16[64,1152]{1,0:T(8,128)(2,1)S(1)}, bf16[64,1152]{1,0:T(8,128)(2,1)S(1)}, u32[]{:S(2)}, u32[]{:S(2)}) collective-permute-start(bf16[64,1152]{1,0:T(8,128)(2,1)S(1)} %pack.1.refs_3_.refs_4_.refs_0_.refs_1_), channel_id=1, source_target_pairs={{0,4},{1,5},{2,6},{3,7},{4,0},{5,1},{6,2},{7,3},{8,12},{9,13},{10,... | collective-permute-start | bytes 442376 | tf_op jit(solution)/shard_map/ppermute | solution.py:253
  8.2 4.8 %load.1 = (bf16[1024,128]{1,0:T(8,128)(2,1)S(1)}, bf16[2,1024,2048]{2,1,0:T(8,128)(2,1)S(1)}, bf16[2,1024,1024]{2,1,0:T(8,128)(2,1)S(1)}) custom-call(bf16[2,1024]{1,0:T(2,128)(2,1)} %bitcast.3, bf16[2,1024,2048]{2,1,0:T(8,128)(2,1)} %refs_1_.3, bf16[2,1024,1024]{2,1,0:T(8,128)(2,1)} %refs_2_.1, bf16[64,1152]{1,0:T(8,128)(2,1)S(1)} %pack.1.refs_3_.refs_4_.refs_0_.refs_1_), custom_call_target="tpu_custom_call" | custom-call | bytes 10000 | tf_op jit(solution)/shard_map/load/pallas_call | solution.py:232
  13.0 0.7 %collective-permute-start.5 = (bf16[64,1152]{1,0:T(8,128)(2,1)S(1)}, bf16[64,1152]{1,0:T(8,128)(2,1)S(1)}, u32[]{:S(2)}, u32[]{:S(2)}) collective-permute-start(bf16[64,1152]{1,0:T(8,128)(2,1)S(1)} %get-tuple-element.85.refs_0_.refs_9_), channel_id=1, source_target_pairs={{0,2},{1,3},{2,0},{3,1},{4,6},{5,7},{6,4},{7,5},{8,10},{9,11},{10,... | collective-permute-start | bytes 442376 | tf_op jit(solution)/shard_map/ppermute | solution.py:253
  14.3 1.3 %collective-permute-start.8 = (bf16[64,1152]{1,0:T(8,128)(2,1)S(1)}, bf16[64,1152]{1,0:T(8,128)(2,1)S(1)}, u32[]{:S(2)}, u32[]{:S(2)}) collective-permute-start(bf16[64,1152]{1,0:T(8,128)(2,1)S(1)} %collective-permute-done.2.refs_0_.refs_5_), channel_id=1, source_target_pairs={{0,2},{1,3},{2,0},{3,1},{4,6},{5,7},{6,4},{7,5},{8,10},{9,11},{10,... | collective-permute-start | bytes 442376 | tf_op jit(solution)/shard_map/ppermute | solution.py:253
  15.6 3.5 %collective-permute-done.5.refs_6_ = bf16[64,1152]{1,0:T(8,128)(2,1)S(1)} collective-permute-done((bf16[64,1152]{1,0:T(8,128)(2,1)S(1)}, bf16[64,1152]{1,0:T(8,128)(2,1)S(1)}, u32[]{:S(2)}, u32[]{:S(2)}) %collective-permute-start.5) | collective-permute-done | bytes 147488 | tf_op jit(solution)/shard_map/ppermute | solution.py:253
  19.1 1.2 %collective-permute-start.12 = (bf16[64,1152]{1,0:T(8,128)(2,1)S(1)}, bf16[64,1152]{1,0:T(8,128)(2,1)S(1)}, u32[]{:S(2)}, u32[]{:S(2)}) collective-permute-start(bf16[64,1152]{1,0:T(8,128)(2,1)S(1)} %collective-permute-done.3.refs_1_.refs_0_.refs_13_), channel_id=1, source_target_pairs={{0,2},{1,3},{2,0},{3,1},{4,6},{5,7},{6,4},{7,5},{8,10},{9,11},{10,... | collective-permute-start | bytes 442376 | tf_op jit(solution)/shard_map/ppermute | solution.py:253
  20.3 1.1 %collective-permute-done.8.refs_3_ = bf16[64,1152]{1,0:T(8,128)(2,1)S(1)} collective-permute-done((bf16[64,1152]{1,0:T(8,128)(2,1)S(1)}, bf16[64,1152]{1,0:T(8,128)(2,1)S(1)}, u32[]{:S(2)}, u32[]{:S(2)}) %collective-permute-start.8) | collective-permute-done | bytes 147488 | tf_op jit(solution)/shard_map/ppermute | solution.py:253
  21.4 2.5 %expert.3 = (f32[128,1024]{1,0:T(8,128)S(1)}, bf16[64,1024]{1,0:T(8,128)(2,1)S(1)}, bf16[64,1024]{1,0:T(8,128)(2,1)S(1)}, bf16[1024,128]{1,0:T(8,128)(2,1)S(1)},...) custom-call(bf16[64,1152]{1,0:T(8,128)(2,1)S(1)} %get-tuple-element., ...), custom_call_target="tpu_custom_call", output_to_operand_aliasing={{3}: (4, {}), {4}: (5, {}), {5}: (6, {})} | custom-call | bytes 10000 | tf_op jit(solution)/shard_map/expert/pallas_call | solution.py:232
  26.5 1.2 %collective-permute-start.13 = (bf16[64,1024]{1,0:T(8,128)(2,1)S(1)}, bf16[64,1024]{1,0:T(8,128)(2,1)S(1)}, u32[]{:S(2)}, u32[]{:S(2)}) collective-permute-start(bf16[64,1024]{1,0:T(8,128)(2,1)S(1)} %get-tuple-element.105), channel_id=1, source_target_pairs={{0,2},{1,3},{2,0},{3,1},{4,6},{5,7},{6,4},{7,5},{8,10},{9,11},{10,... | collective-permute-start | bytes 393224 | tf_op jit(solution)/shard_map/ppermute | solution.py:253
  27.7 2.5 %expert.4 = (f32[128,1024]{1,0:T(8,128)S(1)}, bf16[64,1024]{1,0:T(8,128)(2,1)S(1)}, bf16[64,1024]{1,0:T(8,128)(2,1)S(1)}, bf16[1024,128]{1,0:T(8,128)(2,1)S(1)},...) custom-call(bf16[64,1152]{1,0:T(8,128)(2,1)S(1)} %collective-permute, ...), custom_call_target="tpu_custom_call", output_to_operand_aliasing={{3}: (4, {}), {4}: (5, {}), {5}: (6, {})} | custom-call | bytes 10000 | tf_op jit(solution)/shard_map/expert/pallas_call | solution.py:232
  30.8 1.3 %collective-permute-done.13.refs_0_.refs_1_ = bf16[64,1024]{1,0:T(8,128)(2,1)S(1)} collective-permute-done((bf16[64,1024]{1,0:T(8,128)(2,1)S(1)}, bf16[64,1024]{1,0:T(8,128)(2,1)S(1)}, u32[]{:S(2)}, u32[]{:S(2)}) %collective-permute-start.13) | collective-permute-done | bytes 131104 | tf_op jit(solution)/shard_map/ppermute | solution.py:253
  32.1 1.2 %collective-permute-start.24 = (bf16[64,1024]{1,0:T(8,128)(2,1)S(1)}, bf16[64,1024]{1,0:T(8,128)(2,1)S(1)}, u32[]{:S(2)}, u32[]{:S(2)}) collective-permute-start(bf16[64,1024]{1,0:T(8,128)(2,1)S(1)} %get-tuple-element.131), channel_id=1, source_target_pairs={{0,2},{1,3},{2,0},{3,1},{4,6},{5,7},{6,4},{7,5},{8,10},{9,11},{10,... | collective-permute-start | bytes 393224 | tf_op jit(solution)/shard_map/ppermute | solution.py:253
  33.3 4.7 %expert.5 = (f32[128,1024]{1,0:T(8,128)S(1)}, f32[128,1024]{1,0:T(8,128)S(1)}, bf16[64,1024]{1,0:T(8,128)(2,1)S(1)}, bf16[64,1024]{1,0:T(8,128)(2,1)S(1)}, bf16[...) custom-call(bf16[64,1152]{1,0:T(8,128)(2,1)S(1)} %collective-permute, ...), custom_call_target="tpu_custom_call", output_to_operand_aliasing={{6}: (8, {}), {7}: (9, {}), {8}: (10, {})} | custom-call | bytes 10000 | tf_op jit(solution)/shard_map/expert/pallas_call | solution.py:232
  39.1 1.0 %collective-permute-start.25 = (bf16[64,1024]{1,0:T(8,128)(2,1)S(1)}, bf16[64,1024]{1,0:T(8,128)(2,1)S(1)}, u32[]{:S(2)}, u32[]{:S(2)}) collective-permute-start(bf16[64,1024]{1,0:T(8,128)(2,1)S(1)} %get-tuple-element.147), channel_id=1, source_target_pairs={{0,4},{1,5},{2,6},{3,7},{4,0},{5,1},{6,2},{7,3},{8,12},{9,13},{10,... | collective-permute-start | bytes 393224 | tf_op jit(solution)/shard_map/ppermute | solution.py:253
  40.1 0.7 %collective-permute-start.27 = (bf16[64,1024]{1,0:T(8,128)(2,1)S(1)}, bf16[64,1024]{1,0:T(8,128)(2,1)S(1)}, u32[]{:S(2)}, u32[]{:S(2)}) collective-permute-start(bf16[64,1024]{1,0:T(8,128)(2,1)S(1)} %get-tuple-element.153), channel_id=1, source_target_pairs={{0,2},{1,3},{2,0},{3,1},{4,6},{5,7},{6,4},{7,5},{8,10},{9,11},{10,... | collective-permute-start | bytes 393224 | tf_op jit(solution)/shard_map/ppermute | solution.py:253
  40.9 1.4 %collective-permute-start.29 = (bf16[64,1024]{1,0:T(8,128)(2,1)S(1)}, bf16[64,1024]{1,0:T(8,128)(2,1)S(1)}, u32[]{:S(2)}, u32[]{:S(2)}) collective-permute-start(bf16[64,1024]{1,0:T(8,128)(2,1)S(1)} %get-tuple-element.158), channel_id=1, source_target_pairs={{0,2},{1,3},{2,0},{3,1},{4,6},{5,7},{6,4},{7,5},{8,10},{9,11},{10,... | collective-permute-start | bytes 393224 | tf_op jit(solution)/shard_map/ppermute | solution.py:253
  42.6 2.0 %collective-permute-done.25.refs_2_ = bf16[64,1024]{1,0:T(8,128)(2,1)S(1)} collective-permute-done((bf16[64,1024]{1,0:T(8,128)(2,1)S(1)}, bf16[64,1024]{1,0:T(8,128)(2,1)S(1)}, u32[]{:S(2)}, u32[]{:S(2)}) %collective-permute-start.25) | collective-permute-done | bytes 131104 | tf_op jit(solution)/shard_map/ppermute | solution.py:253
  44.7 2.5 %collective-permute-start.26 = (bf16[64,1024]{1,0:T(8,128)(2,1)S(1)}, bf16[64,1024]{1,0:T(8,128)(2,1)S(1)}, u32[]{:S(2)}, u32[]{:S(2)}) collective-permute-start(bf16[64,1024]{1,0:T(8,128)(2,1)S(1)} %get-tuple-element.151), channel_id=1, source_target_pairs={{0,8},{1,9},{2,10},{3,11},{4,12},{5,13},{6,14},{7,15},{8,0},{9,1},... | collective-permute-start | bytes 393224 | tf_op jit(solution)/shard_map/ppermute | solution.py:253
  47.2 1.8 %collective-permute-start.28 = (bf16[64,1024]{1,0:T(8,128)(2,1)S(1)}, bf16[64,1024]{1,0:T(8,128)(2,1)S(1)}, u32[]{:S(2)}, u32[]{:S(2)}) collective-permute-start(bf16[64,1024]{1,0:T(8,128)(2,1)S(1)} %get-tuple-element.157), channel_id=1, source_target_pairs={{0,4},{1,5},{2,6},{3,7},{4,0},{5,1},{6,2},{7,3},{8,12},{9,13},{10,... | collective-permute-start | bytes 393224 | tf_op jit(solution)/shard_map/ppermute | solution.py:253
  49.0 4.2 %collective-permute-done.26.refs_1_ = bf16[64,1024]{1,0:T(8,128)(2,1)S(1)} collective-permute-done((bf16[64,1024]{1,0:T(8,128)(2,1)S(1)}, bf16[64,1024]{1,0:T(8,128)(2,1)S(1)}, u32[]{:S(2)}, u32[]{:S(2)}) %collective-permute-start.26) | collective-permute-done | bytes 131104 | tf_op jit(solution)/shard_map/ppermute | solution.py:253
  53.8 0.8 %finish.1 = bf16[64,1024]{1,0:T(8,128)(2,1)} custom-call(f32[64,128]{1,0:T(8,128)S(1)} %get-tuple-element.144.scores_ref, f32[64,1024]{1,0:T(8,128)S(1)} %get-tuple-element.145.refs_0_, bf16[64,1024]{1,0:T(8,128)(2,1)S(1)} %collective-permute-done.26.refs_1_, bf16[64,1024]{1,0:T(8,128)(2,1)S(1)} %collective-permute-done.28.refs_2_, ...), custom_call_target="tpu_custom_call" | custom-call | tf_op jit(solution)/shard_map/finish/pallas_call | solution.py:366
  (55 shorter events, 5.8 us)
Async XLA Ops:
  1.0 12.1 %collective-permute-start.1 = (bf16[64,1152]{1,0:T(8,128)(2,1)S(1)}, bf16[64,1152]{1,0:T(8,128)(2,1)S(1)}, u32[]{:S(2)}, u32[]{:S(2)}) collective-permute-start(bf16[64,1152]{1,0:T(8,128)(2,1)S(1)} %pack.1.refs_3_.refs_4_.refs_0_.refs_1_), channel_id=1, source_target_pairs={{0,8},{1,9},{2,10},{3,11},{4,12},{5,13},{6,14},{7,15},{8,0},{9,1},... | collective-permute-start | bytes 442376 | tf_op jit(solution)/shard_map/ppermute | solution.py:253
  5.1 10.5 %collective-permute-start.4 = (bf16[64,1152]{1,0:T(8,128)(2,1)S(1)}, bf16[64,1152]{1,0:T(8,128)(2,1)S(1)}, u32[]{:S(2)}, u32[]{:S(2)}) collective-permute-start(bf16[64,1152]{1,0:T(8,128)(2,1)S(1)} %pack.1.refs_3_.refs_4_.refs_0_.refs_1_), channel_id=1, source_target_pairs={{0,2},{1,3},{2,0},{3,1},{4,6},{5,7},{6,4},{7,5},{8,10},{9,11},{10,... | collective-permute-start | bytes 442376 | tf_op jit(solution)/shard_map/ppermute | solution.py:253
  6.6 7.7 %collective-permute-start.2 = (bf16[64,1152]{1,0:T(8,128)(2,1)S(1)}, bf16[64,1152]{1,0:T(8,128)(2,1)S(1)}, u32[]{:S(2)}, u32[]{:S(2)}) collective-permute-start(bf16[64,1152]{1,0:T(8,128)(2,1)S(1)} %pack.1.refs_3_.refs_4_.refs_0_.refs_1_), channel_id=1, source_target_pairs={{0,4},{1,5},{2,6},{3,7},{4,0},{5,1},{6,2},{7,3},{8,12},{9,13},{10,... | collective-permute-start | bytes 442376 | tf_op jit(solution)/shard_map/ppermute | solution.py:253
  13.0 6.1 %collective-permute-start.5 = (bf16[64,1152]{1,0:T(8,128)(2,1)S(1)}, bf16[64,1152]{1,0:T(8,128)(2,1)S(1)}, u32[]{:S(2)}, u32[]{:S(2)}) collective-permute-start(bf16[64,1152]{1,0:T(8,128)(2,1)S(1)} %get-tuple-element.85.refs_0_.refs_9_), channel_id=1, source_target_pairs={{0,2},{1,3},{2,0},{3,1},{4,6},{5,7},{6,4},{7,5},{8,10},{9,11},{10,... | collective-permute-start | bytes 442376 | tf_op jit(solution)/shard_map/ppermute | solution.py:253
  13.8 5.4 %collective-permute-start.3 = (bf16[64,1152]{1,0:T(8,128)(2,1)S(1)}, bf16[64,1152]{1,0:T(8,128)(2,1)S(1)}, u32[]{:S(2)}, u32[]{:S(2)}) collective-permute-start(bf16[64,1152]{1,0:T(8,128)(2,1)S(1)} %get-tuple-element.85.refs_0_.refs_9_), channel_id=1, source_target_pairs={{0,4},{1,5},{2,6},{3,7},{4,0},{5,1},{6,2},{7,3},{8,12},{9,13},{10,... | collective-permute-start | bytes 442376 | tf_op jit(solution)/shard_map/ppermute | solution.py:253
  14.3 7.1 %collective-permute-start.6 = (bf16[64,1152]{1,0:T(8,128)(2,1)S(1)}, bf16[64,1152]{1,0:T(8,128)(2,1)S(1)}, u32[]{:S(2)}, u32[]{:S(2)}) collective-permute-start(bf16[64,1152]{1,0:T(8,128)(2,1)S(1)} %get-tuple-element.85.refs_0_.refs_9_), channel_id=1, source_target_pairs={{0,1},{1,0},{2,3},{3,2},{4,5},{5,4},{6,7},{7,6},{8,9},{9,8},{10,11... | collective-permute-start | bytes 442376 | tf_op jit(solution)/shard_map/ppermute | solution.py:253
  14.3 7.1 %collective-permute-start.8 = (bf16[64,1152]{1,0:T(8,128)(2,1)S(1)}, bf16[64,1152]{1,0:T(8,128)(2,1)S(1)}, u32[]{:S(2)}, u32[]{:S(2)}) collective-permute-start(bf16[64,1152]{1,0:T(8,128)(2,1)S(1)} %collective-permute-done.2.refs_0_.refs_5_), channel_id=1, source_target_pairs={{0,2},{1,3},{2,0},{3,1},{4,6},{5,7},{6,4},{7,5},{8,10},{9,11},{10,... | collective-permute-start | bytes 442376 | tf_op jit(solution)/shard_map/ppermute | solution.py:253
  19.1 2.3 %collective-permute-start.7 = (bf16[64,1152]{1,0:T(8,128)(2,1)S(1)}, bf16[64,1152]{1,0:T(8,128)(2,1)S(1)}, u32[]{:S(2)}, u32[]{:S(2)}) collective-permute-start(bf16[64,1152]{1,0:T(8,128)(2,1)S(1)} %get-tuple-element.89.refs_1_.refs_11_), channel_id=1, source_target_pairs={{0,1},{1,0},{2,3},{3,2},{4,5},{5,4},{6,7},{7,6},{8,9},{9,8},{10,11... | collective-permute-start | bytes 442376 | tf_op jit(solution)/shard_map/ppermute | solution.py:253
  19.1 6.3 %collective-permute-start.12 = (bf16[64,1152]{1,0:T(8,128)(2,1)S(1)}, bf16[64,1152]{1,0:T(8,128)(2,1)S(1)}, u32[]{:S(2)}, u32[]{:S(2)}) collective-permute-start(bf16[64,1152]{1,0:T(8,128)(2,1)S(1)} %collective-permute-done.3.refs_1_.refs_0_.refs_13_), channel_id=1, source_target_pairs={{0,2},{1,3},{2,0},{3,1},{4,6},{5,7},{6,4},{7,5},{8,10},{9,11},{10,... | collective-permute-start | bytes 442376 | tf_op jit(solution)/shard_map/ppermute | solution.py:253
  25.4 2.3 %collective-permute-start.14 = (bf16[64,1152]{1,0:T(8,128)(2,1)S(1)}, bf16[64,1152]{1,0:T(8,128)(2,1)S(1)}, u32[]{:S(2)}, u32[]{:S(2)}) collective-permute-start(bf16[64,1152]{1,0:T(8,128)(2,1)S(1)} %collective-permute-done.3.refs_1_.refs_0_.refs_13_), channel_id=1, source_target_pairs={{0,1},{1,0},{2,3},{3,2},{4,5},{5,4},{6,7},{7,6},{8,9},{9,8},{10,11... | collective-permute-start | bytes 442376 | tf_op jit(solution)/shard_map/ppermute | solution.py:253
  25.5 2.2 %collective-permute-start.15 = (bf16[64,1152]{1,0:T(8,128)(2,1)S(1)}, bf16[64,1152]{1,0:T(8,128)(2,1)S(1)}, u32[]{:S(2)}, u32[]{:S(2)}) collective-permute-start(bf16[64,1152]{1,0:T(8,128)(2,1)S(1)} %get-tuple-element.106.refs_1_.refs_15_), channel_id=1, source_target_pairs={{0,1},{1,0},{2,3},{3,2},{4,5},{5,4},{6,7},{7,6},{8,9},{9,8},{10,11... | collective-permute-start | bytes 442376 | tf_op jit(solution)/shard_map/ppermute | solution.py:253
  25.9 7.4 %collective-permute-start.16 = (bf16[64,1152]{1,0:T(8,128)(2,1)S(1)}, bf16[64,1152]{1,0:T(8,128)(2,1)S(1)}, u32[]{:S(2)}, u32[]{:S(2)}) collective-permute-start(bf16[64,1152]{1,0:T(8,128)(2,1)S(1)} %collective-permute-done.2.refs_0_.refs_5_), channel_id=1, source_target_pairs={{0,1},{1,0},{2,3},{3,2},{4,5},{5,4},{6,7},{7,6},{8,9},{9,8},{10,11... | collective-permute-start | bytes 442376 | tf_op jit(solution)/shard_map/ppermute | solution.py:253
  26.0 7.3 %collective-permute-start.17 = (bf16[64,1152]{1,0:T(8,128)(2,1)S(1)}, bf16[64,1152]{1,0:T(8,128)(2,1)S(1)}, u32[]{:S(2)}, u32[]{:S(2)}) collective-permute-start(bf16[64,1152]{1,0:T(8,128)(2,1)S(1)} %get-tuple-element.114.refs_1_.refs_7_), channel_id=1, source_target_pairs={{0,1},{1,0},{2,3},{3,2},{4,5},{5,4},{6,7},{7,6},{8,9},{9,8},{10,11... | collective-permute-start | bytes 442376 | tf_op jit(solution)/shard_map/ppermute | solution.py:253
  26.5 5.6 %collective-permute-start.13 = (bf16[64,1024]{1,0:T(8,128)(2,1)S(1)}, bf16[64,1024]{1,0:T(8,128)(2,1)S(1)}, u32[]{:S(2)}, u32[]{:S(2)}) collective-permute-start(bf16[64,1024]{1,0:T(8,128)(2,1)S(1)} %get-tuple-element.105), channel_id=1, source_target_pairs={{0,2},{1,3},{2,0},{3,1},{4,6},{5,7},{6,4},{7,5},{8,10},{9,11},{10,... | collective-permute-start | bytes 393224 | tf_op jit(solution)/shard_map/ppermute | solution.py:253
  32.1 7.0 %collective-permute-start.24 = (bf16[64,1024]{1,0:T(8,128)(2,1)S(1)}, bf16[64,1024]{1,0:T(8,128)(2,1)S(1)}, u32[]{:S(2)}, u32[]{:S(2)}) collective-permute-start(bf16[64,1024]{1,0:T(8,128)(2,1)S(1)} %get-tuple-element.131), channel_id=1, source_target_pairs={{0,2},{1,3},{2,0},{3,1},{4,6},{5,7},{6,4},{7,5},{8,10},{9,11},{10,... | collective-permute-start | bytes 393224 | tf_op jit(solution)/shard_map/ppermute | solution.py:253
  38.0 2.1 %collective-permute-start.22 = (bf16[64,1024]{1,0:T(8,128)(2,1)S(1)}, bf16[64,1024]{1,0:T(8,128)(2,1)S(1)}, u32[]{:S(2)}, u32[]{:S(2)}) collective-permute-start(bf16[64,1024]{1,0:T(8,128)(2,1)S(1)} %get-tuple-element.128), channel_id=1, source_target_pairs={{0,1},{1,0},{2,3},{3,2},{4,5},{5,4},{6,7},{7,6},{8,9},{9,8},{10,11... | collective-permute-start | bytes 393224 | tf_op jit(solution)/shard_map/ppermute | solution.py:253
  38.1 2.0 %collective-permute-start.23 = (bf16[64,1024]{1,0:T(8,128)(2,1)S(1)}, bf16[64,1024]{1,0:T(8,128)(2,1)S(1)}, u32[]{:S(2)}, u32[]{:S(2)}) collective-permute-start(bf16[64,1024]{1,0:T(8,128)(2,1)S(1)} %get-tuple-element.129), channel_id=1, source_target_pairs={{0,1},{1,0},{2,3},{3,2},{4,5},{5,4},{6,7},{7,6},{8,9},{9,8},{10,11... | collective-permute-start | bytes 393224 | tf_op jit(solution)/shard_map/ppermute | solution.py:253
  38.6 2.3 %collective-permute-start.20 = (bf16[64,1024]{1,0:T(8,128)(2,1)S(1)}, bf16[64,1024]{1,0:T(8,128)(2,1)S(1)}, u32[]{:S(2)}, u32[]{:S(2)}) collective-permute-start(bf16[64,1024]{1,0:T(8,128)(2,1)S(1)} %get-tuple-element.125), channel_id=1, source_target_pairs={{0,1},{1,0},{2,3},{3,2},{4,5},{5,4},{6,7},{7,6},{8,9},{9,8},{10,11... | collective-permute-start | bytes 393224 | tf_op jit(solution)/shard_map/ppermute | solution.py:253
  38.7 2.2 %collective-permute-start.21 = (bf16[64,1024]{1,0:T(8,128)(2,1)S(1)}, bf16[64,1024]{1,0:T(8,128)(2,1)S(1)}, u32[]{:S(2)}, u32[]{:S(2)}) collective-permute-start(bf16[64,1024]{1,0:T(8,128)(2,1)S(1)} %get-tuple-element.126), channel_id=1, source_target_pairs={{0,1},{1,0},{2,3},{3,2},{4,5},{5,4},{6,7},{7,6},{8,9},{9,8},{10,11... | collective-permute-start | bytes 393224 | tf_op jit(solution)/shard_map/ppermute | solution.py:253
  39.1 5.5 %collective-permute-start.25 = (bf16[64,1024]{1,0:T(8,128)(2,1)S(1)}, bf16[64,1024]{1,0:T(8,128)(2,1)S(1)}, u32[]{:S(2)}, u32[]{:S(2)}) collective-permute-start(bf16[64,1024]{1,0:T(8,128)(2,1)S(1)} %get-tuple-element.147), channel_id=1, source_target_pairs={{0,4},{1,5},{2,6},{3,7},{4,0},{5,1},{6,2},{7,3},{8,12},{9,13},{10,... | collective-permute-start | bytes 393224 | tf_op jit(solution)/shard_map/ppermute | solution.py:253
  40.1 7.0 %collective-permute-start.27 = (bf16[64,1024]{1,0:T(8,128)(2,1)S(1)}, bf16[64,1024]{1,0:T(8,128)(2,1)S(1)}, u32[]{:S(2)}, u32[]{:S(2)}) collective-permute-start(bf16[64,1024]{1,0:T(8,128)(2,1)S(1)} %get-tuple-element.153), channel_id=1, source_target_pairs={{0,2},{1,3},{2,0},{3,1},{4,6},{5,7},{6,4},{7,5},{8,10},{9,11},{10,... | collective-permute-start | bytes 393224 | tf_op jit(solution)/shard_map/ppermute | solution.py:253
  40.9 8.1 %collective-permute-start.29 = (bf16[64,1024]{1,0:T(8,128)(2,1)S(1)}, bf16[64,1024]{1,0:T(8,128)(2,1)S(1)}, u32[]{:S(2)}, u32[]{:S(2)}) collective-permute-start(bf16[64,1024]{1,0:T(8,128)(2,1)S(1)} %get-tuple-element.158), channel_id=1, source_target_pairs={{0,2},{1,3},{2,0},{3,1},{4,6},{5,7},{6,4},{7,5},{8,10},{9,11},{10,... | collective-permute-start | bytes 393224 | tf_op jit(solution)/shard_map/ppermute | solution.py:253
  44.7 8.6 %collective-permute-start.26 = (bf16[64,1024]{1,0:T(8,128)(2,1)S(1)}, bf16[64,1024]{1,0:T(8,128)(2,1)S(1)}, u32[]{:S(2)}, u32[]{:S(2)}) collective-permute-start(bf16[64,1024]{1,0:T(8,128)(2,1)S(1)} %get-tuple-element.151), channel_id=1, source_target_pairs={{0,8},{1,9},{2,10},{3,11},{4,12},{5,13},{6,14},{7,15},{8,0},{9,1},... | collective-permute-start | bytes 393224 | tf_op jit(solution)/shard_map/ppermute | solution.py:253
  47.2 6.6 %collective-permute-start.28 = (bf16[64,1024]{1,0:T(8,128)(2,1)S(1)}, bf16[64,1024]{1,0:T(8,128)(2,1)S(1)}, u32[]{:S(2)}, u32[]{:S(2)}) collective-permute-start(bf16[64,1024]{1,0:T(8,128)(2,1)S(1)} %get-tuple-element.157), channel_id=1, source_target_pairs={{0,4},{1,5},{2,6},{3,7},{4,0},{5,1},{6,2},{7,3},{8,12},{9,13},{10,... | collective-permute-start | bytes 393224 | tf_op jit(solution)/shard_map/ppermute | solution.py:253
  (6 other events, 10.0 us)

commit v26 on v25

--- a/solution.py
+++ b/solution.py
@@ -13,7 +13,7 @@
 LINE = 16
 SCALE = 2.0**40
 STEP = 512
-PIECE = 128
+PIECE = 512
 
 
 def pack_kernel(ids_hbm, row_hbm, router_hbm, out_ref, ids_ref, router_ref, sems):
@@ -345,7 +345,7 @@
                 scores_kernel,
                 [pltpu.VMEM((rows, TAIL), jnp.float32)],
                 [mine, *packets],
-                scratch=[pltpu.VMEM((n_dev * local * lat // TAIL, TAIL), jnp.float32)],
+                scratch=[pltpu.VMEM((n_dev * local * lat // TAIL + 8, TAIL), jnp.float32)],
             )[0]
         z_2 = swap(reduce_y(2, z_3), 8)
         z_1 = swap(reduce_y(1), 4)

time: 54.8 us -> 54.8 us (level)
  transfers between devices with their start and end apart: 30 -> 30, of which waited for: 8 -> 9; matrix products, arithmetic and copies ran while one was open for 0% -> 0% of each run, Pallas kernels for 28% -> 27%
where the time goes in v26:
time: 54.8 us; the launch traced here: 54.6 us
  starting transfers between devices  24.5 us (45%)
  Pallas kernels  16.6 us (30%)
  waiting for transfers between devices  13.3 us (24%)
    ppermute x30, starting transfers between devices, swap(): return lax.ppermute(x, 'exp', [(i, i ^ bits) for i in range(n_dev)])  24.5 us
    pallas_call x18, Pallas kernels, call(): pl.pallas_call(body_with_chain if reads_chain else body, out_shape=list(o...  15.8 us
    ppermute x30, waiting for transfers between devices, swap(): return lax.ppermute(x, 'exp', [(i, i ^ bits) for i in range(n_dev)])  13.3 us
  transfers between devices with their start and end apart: 30, of which 9 were waited for; matrix products, arithmetic and copies ran while one was open for 0% of the time, Pallas kernels for 27%

profile of v26, /device:TPU:0, one launch (start us, length us, event | category | flops | bytes accessed | tf_op | source)
XLA Modules:
  0.0 54.6 jit_solution(10373701390202858790)
XLA Ops:
  0.0 1.0 %pack.1.refs_3_.refs_4_.refs_0_.refs_1_ = bf16[64,1152]{1,0:T(8,128)(2,1)S(1)} custom-call(s32[8,64]{1,0:T(8,128)} %bitcast.4, bf16[64,1024]{1,0:T(8,128)(2,1)} %refs_1_.2, bf16[2,1024]{1,0:T(2,128)(2,1)} %bitcast.2), custom_call_target="tpu_custom_call" | custom-call | bytes 10000 | tf_op jit(solution)/shard_map/pack/pallas_call | solution.py:232
  1.0 4.1 %collective-permute-start.1 = (bf16[64,1152]{1,0:T(8,128)(2,1)S(1)}, bf16[64,1152]{1,0:T(8,128)(2,1)S(1)}, u32[]{:S(2)}, u32[]{:S(2)}) collective-permute-start(bf16[64,1152]{1,0:T(8,128)(2,1)S(1)} %pack.1.refs_3_.refs_4_.refs_0_.refs_1_), channel_id=1, source_target_pairs={{0,8},{1,9},{2,10},{3,11},{4,12},{5,13},{6,14},{7,15},{8,0},{9,1},... | collective-permute-start | bytes 442376 | tf_op jit(solution)/shard_map/ppermute | solution.py:253
  5.1 1.5 %collective-permute-start.4 = (bf16[64,1152]{1,0:T(8,128)(2,1)S(1)}, bf16[64,1152]{1,0:T(8,128)(2,1)S(1)}, u32[]{:S(2)}, u32[]{:S(2)}) collective-permute-start(bf16[64,1152]{1,0:T(8,128)(2,1)S(1)} %pack.1.refs_3_.refs_4_.refs_0_.refs_1_), channel_id=1, source_target_pairs={{0,2},{1,3},{2,0},{3,1},{4,6},{5,7},{6,4},{7,5},{8,10},{9,11},{10,... | collective-permute-start | bytes 442376 | tf_op jit(solution)/shard_map/ppermute | solution.py:253
  6.6 1.6 %collective-permute-start.2 = (bf16[64,1152]{1,0:T(8,128)(2,1)S(1)}, bf16[64,1152]{1,0:T(8,128)(2,1)S(1)}, u32[]{:S(2)}, u32[]{:S(2)}) collective-permute-start(bf16[64,1152]{1,0:T(8,128)(2,1)S(1)} %pack.1.refs_3_.refs_4_.refs_0_.refs_1_), channel_id=1, source_target_pairs={{0,4},{1,5},{2,6},{3,7},{4,0},{5,1},{6,2},{7,3},{8,12},{9,13},{10,... | collective-permute-start | bytes 442376 | tf_op jit(solution)/shard_map/ppermute | solution.py:253
  8.2 4.7 %load.1 = (bf16[1024,128]{1,0:T(8,128)(2,1)S(1)}, bf16[2,1024,2048]{2,1,0:T(8,128)(2,1)S(1)}, bf16[2,1024,1024]{2,1,0:T(8,128)(2,1)S(1)}) custom-call(bf16[2,1024]{1,0:T(2,128)(2,1)} %bitcast.3, bf16[2,1024,2048]{2,1,0:T(8,128)(2,1)} %refs_1_.3, bf16[2,1024,1024]{2,1,0:T(8,128)(2,1)} %refs_2_.1, bf16[64,1152]{1,0:T(8,128)(2,1)S(1)} %pack.1.refs_3_.refs_4_.refs_0_.refs_1_), custom_call_target="tpu_custom_call" | custom-call | bytes 10000 | tf_op jit(solution)/shard_map/load/pallas_call | solution.py:232
  12.9 0.9 %collective-permute-start.5 = (bf16[64,1152]{1,0:T(8,128)(2,1)S(1)}, bf16[64,1152]{1,0:T(8,128)(2,1)S(1)}, u32[]{:S(2)}, u32[]{:S(2)}) collective-permute-start(bf16[64,1152]{1,0:T(8,128)(2,1)S(1)} %get-tuple-element.85.refs_0_.refs_9_), channel_id=1, source_target_pairs={{0,2},{1,3},{2,0},{3,1},{4,6},{5,7},{6,4},{7,5},{8,10},{9,11},{10,... | collective-permute-start | bytes 442376 | tf_op jit(solution)/shard_map/ppermute | solution.py:253
  14.3 1.1 %collective-permute-start.8 = (bf16[64,1152]{1,0:T(8,128)(2,1)S(1)}, bf16[64,1152]{1,0:T(8,128)(2,1)S(1)}, u32[]{:S(2)}, u32[]{:S(2)}) collective-permute-start(bf16[64,1152]{1,0:T(8,128)(2,1)S(1)} %collective-permute-done.2.refs_0_.refs_5_), channel_id=1, source_target_pairs={{0,2},{1,3},{2,0},{3,1},{4,6},{5,7},{6,4},{7,5},{8,10},{9,11},{10,... | collective-permute-start | bytes 442376 | tf_op jit(solution)/shard_map/ppermute | solution.py:253
  15.4 3.3 %collective-permute-done.5.refs_6_ = bf16[64,1152]{1,0:T(8,128)(2,1)S(1)} collective-permute-done((bf16[64,1152]{1,0:T(8,128)(2,1)S(1)}, bf16[64,1152]{1,0:T(8,128)(2,1)S(1)}, u32[]{:S(2)}, u32[]{:S(2)}) %collective-permute-start.5) | collective-permute-done | bytes 147488 | tf_op jit(solution)/shard_map/ppermute | solution.py:253
  18.9 1.2 %collective-permute-start.12 = (bf16[64,1152]{1,0:T(8,128)(2,1)S(1)}, bf16[64,1152]{1,0:T(8,128)(2,1)S(1)}, u32[]{:S(2)}, u32[]{:S(2)}) collective-permute-start(bf16[64,1152]{1,0:T(8,128)(2,1)S(1)} %collective-permute-done.3.refs_1_.refs_0_.refs_13_), channel_id=1, source_target_pairs={{0,2},{1,3},{2,0},{3,1},{4,6},{5,7},{6,4},{7,5},{8,10},{9,11},{10,... | collective-permute-start | bytes 442376 | tf_op jit(solution)/shard_map/ppermute | solution.py:253
  20.1 1.1 %collective-permute-done.8.refs_3_ = bf16[64,1152]{1,0:T(8,128)(2,1)S(1)} collective-permute-done((bf16[64,1152]{1,0:T(8,128)(2,1)S(1)}, bf16[64,1152]{1,0:T(8,128)(2,1)S(1)}, u32[]{:S(2)}, u32[]{:S(2)}) %collective-permute-start.8) | collective-permute-done | bytes 147488 | tf_op jit(solution)/shard_map/ppermute | solution.py:253
  21.2 2.5 %expert.3 = (f32[128,1024]{1,0:T(8,128)S(1)}, bf16[64,1024]{1,0:T(8,128)(2,1)S(1)}, bf16[64,1024]{1,0:T(8,128)(2,1)S(1)}, bf16[1024,128]{1,0:T(8,128)(2,1)S(1)},...) custom-call(bf16[64,1152]{1,0:T(8,128)(2,1)S(1)} %get-tuple-element., ...), custom_call_target="tpu_custom_call", output_to_operand_aliasing={{3}: (4, {}), {4}: (5, {}), {5}: (6, {})} | custom-call | bytes 10000 | tf_op jit(solution)/shard_map/expert/pallas_call | solution.py:232
  26.3 1.3 %collective-permute-start.13 = (bf16[64,1024]{1,0:T(8,128)(2,1)S(1)}, bf16[64,1024]{1,0:T(8,128)(2,1)S(1)}, u32[]{:S(2)}, u32[]{:S(2)}) collective-permute-start(bf16[64,1024]{1,0:T(8,128)(2,1)S(1)} %get-tuple-element.105), channel_id=1, source_target_pairs={{0,2},{1,3},{2,0},{3,1},{4,6},{5,7},{6,4},{7,5},{8,10},{9,11},{10,... | collective-permute-start | bytes 393224 | tf_op jit(solution)/shard_map/ppermute | solution.py:253
  27.5 2.5 %expert.4 = (f32[128,1024]{1,0:T(8,128)S(1)}, bf16[64,1024]{1,0:T(8,128)(2,1)S(1)}, bf16[64,1024]{1,0:T(8,128)(2,1)S(1)}, bf16[1024,128]{1,0:T(8,128)(2,1)S(1)},...) custom-call(bf16[64,1152]{1,0:T(8,128)(2,1)S(1)} %collective-permute, ...), custom_call_target="tpu_custom_call", output_to_operand_aliasing={{3}: (4, {}), {4}: (5, {}), {5}: (6, {})} | custom-call | bytes 10000 | tf_op jit(solution)/shard_map/expert/pallas_call | solution.py:232
  30.6 1.3 %collective-permute-done.13.refs_0_.refs_1_ = bf16[64,1024]{1,0:T(8,128)(2,1)S(1)} collective-permute-done((bf16[64,1024]{1,0:T(8,128)(2,1)S(1)}, bf16[64,1024]{1,0:T(8,128)(2,1)S(1)}, u32[]{:S(2)}, u32[]{:S(2)}) %collective-permute-start.13) | collective-permute-done | bytes 131104 | tf_op jit(solution)/shard_map/ppermute | solution.py:253
  32.0 1.2 %collective-permute-start.24 = (bf16[64,1024]{1,0:T(8,128)(2,1)S(1)}, bf16[64,1024]{1,0:T(8,128)(2,1)S(1)}, u32[]{:S(2)}, u32[]{:S(2)}) collective-permute-start(bf16[64,1024]{1,0:T(8,128)(2,1)S(1)} %get-tuple-element.131), channel_id=1, source_target_pairs={{0,2},{1,3},{2,0},{3,1},{4,6},{5,7},{6,4},{7,5},{8,10},{9,11},{10,... | collective-permute-start | bytes 393224 | tf_op jit(solution)/shard_map/ppermute | solution.py:253
  33.1 4.7 %expert.5 = (f32[128,1024]{1,0:T(8,128)S(1)}, f32[128,1024]{1,0:T(8,128)S(1)}, bf16[64,1024]{1,0:T(8,128)(2,1)S(1)}, bf16[64,1024]{1,0:T(8,128)(2,1)S(1)}, bf16[...) custom-call(bf16[64,1152]{1,0:T(8,128)(2,1)S(1)} %collective-permute, ...), custom_call_target="tpu_custom_call", output_to_operand_aliasing={{6}: (8, {}), {7}: (9, {}), {8}: (10, {})} | custom-call | bytes 10000 | tf_op jit(solution)/shard_map/expert/pallas_call | solution.py:232
  39.0 1.0 %collective-permute-start.25 = (bf16[64,1024]{1,0:T(8,128)(2,1)S(1)}, bf16[64,1024]{1,0:T(8,128)(2,1)S(1)}, u32[]{:S(2)}, u32[]{:S(2)}) collective-permute-start(bf16[64,1024]{1,0:T(8,128)(2,1)S(1)} %get-tuple-element.147), channel_id=1, source_target_pairs={{0,4},{1,5},{2,6},{3,7},{4,0},{5,1},{6,2},{7,3},{8,12},{9,13},{10,... | collective-permute-start | bytes 393224 | tf_op jit(solution)/shard_map/ppermute | solution.py:253
  40.0 0.9 %collective-permute-start.27 = (bf16[64,1024]{1,0:T(8,128)(2,1)S(1)}, bf16[64,1024]{1,0:T(8,128)(2,1)S(1)}, u32[]{:S(2)}, u32[]{:S(2)}) collective-permute-start(bf16[64,1024]{1,0:T(8,128)(2,1)S(1)} %get-tuple-element.153), channel_id=1, source_target_pairs={{0,2},{1,3},{2,0},{3,1},{4,6},{5,7},{6,4},{7,5},{8,10},{9,11},{10,... | collective-permute-start | bytes 393224 | tf_op jit(solution)/shard_map/ppermute | solution.py:253
  40.9 1.3 %collective-permute-start.29 = (bf16[64,1024]{1,0:T(8,128)(2,1)S(1)}, bf16[64,1024]{1,0:T(8,128)(2,1)S(1)}, u32[]{:S(2)}, u32[]{:S(2)}) collective-permute-start(bf16[64,1024]{1,0:T(8,128)(2,1)S(1)} %get-tuple-element.158), channel_id=1, source_target_pairs={{0,2},{1,3},{2,0},{3,1},{4,6},{5,7},{6,4},{7,5},{8,10},{9,11},{10,... | collective-permute-start | bytes 393224 | tf_op jit(solution)/shard_map/ppermute | solution.py:253
  42.5 2.0 %collective-permute-done.25.refs_2_ = bf16[64,1024]{1,0:T(8,128)(2,1)S(1)} collective-permute-done((bf16[64,1024]{1,0:T(8,128)(2,1)S(1)}, bf16[64,1024]{1,0:T(8,128)(2,1)S(1)}, u32[]{:S(2)}, u32[]{:S(2)}) %collective-permute-start.25) | collective-permute-done | bytes 131104 | tf_op jit(solution)/shard_map/ppermute | solution.py:253
  44.5 2.6 %collective-permute-start.26 = (bf16[64,1024]{1,0:T(8,128)(2,1)S(1)}, bf16[64,1024]{1,0:T(8,128)(2,1)S(1)}, u32[]{:S(2)}, u32[]{:S(2)}) collective-permute-start(bf16[64,1024]{1,0:T(8,128)(2,1)S(1)} %get-tuple-element.151), channel_id=1, source_target_pairs={{0,8},{1,9},{2,10},{3,11},{4,12},{5,13},{6,14},{7,15},{8,0},{9,1},... | collective-permute-start | bytes 393224 | tf_op jit(solution)/shard_map/ppermute | solution.py:253
  47.2 1.8 %collective-permute-start.28 = (bf16[64,1024]{1,0:T(8,128)(2,1)S(1)}, bf16[64,1024]{1,0:T(8,128)(2,1)S(1)}, u32[]{:S(2)}, u32[]{:S(2)}) collective-permute-start(bf16[64,1024]{1,0:T(8,128)(2,1)S(1)} %get-tuple-element.157), channel_id=1, source_target_pairs={{0,4},{1,5},{2,6},{3,7},{4,0},{5,1},{6,2},{7,3},{8,12},{9,13},{10,... | collective-permute-start | bytes 393224 | tf_op jit(solution)/shard_map/ppermute | solution.py:253
  49.0 4.2 %collective-permute-done.26.refs_1_ = bf16[64,1024]{1,0:T(8,128)(2,1)S(1)} collective-permute-done((bf16[64,1024]{1,0:T(8,128)(2,1)S(1)}, bf16[64,1024]{1,0:T(8,128)(2,1)S(1)}, u32[]{:S(2)}, u32[]{:S(2)}) %collective-permute-start.26) | collective-permute-done | bytes 131104 | tf_op jit(solution)/shard_map/ppermute | solution.py:253
  53.8 0.8 %finish.1 = bf16[64,1024]{1,0:T(8,128)(2,1)} custom-call(f32[64,128]{1,0:T(8,128)S(1)} %get-tuple-element.144.scores_ref, f32[64,1024]{1,0:T(8,128)S(1)} %get-tuple-element.145.refs_0_, bf16[64,1024]{1,0:T(8,128)(2,1)S(1)} %collective-permute-done.26.refs_1_, bf16[64,1024]{1,0:T(8,128)(2,1)S(1)} %collective-permute-done.28.refs_2_, ...), custom_call_target="tpu_custom_call" | custom-call | tf_op jit(solution)/shard_map/finish/pallas_call | solution.py:366
  (55 shorter events, 6.0 us)
Async XLA Ops:
  1.0 11.9 %collective-permute-start.1 = (bf16[64,1152]{1,0:T(8,128)(2,1)S(1)}, bf16[64,1152]{1,0:T(8,128)(2,1)S(1)}, u32[]{:S(2)}, u32[]{:S(2)}) collective-permute-start(bf16[64,1152]{1,0:T(8,128)(2,1)S(1)} %pack.1.refs_3_.refs_4_.refs_0_.refs_1_), channel_id=1, source_target_pairs={{0,8},{1,9},{2,10},{3,11},{4,12},{5,13},{6,14},{7,15},{8,0},{9,1},... | collective-permute-start | bytes 442376 | tf_op jit(solution)/shard_map/ppermute | solution.py:253
  5.1 10.4 %collective-permute-start.4 = (bf16[64,1152]{1,0:T(8,128)(2,1)S(1)}, bf16[64,1152]{1,0:T(8,128)(2,1)S(1)}, u32[]{:S(2)}, u32[]{:S(2)}) collective-permute-start(bf16[64,1152]{1,0:T(8,128)(2,1)S(1)} %pack.1.refs_3_.refs_4_.refs_0_.refs_1_), channel_id=1, source_target_pairs={{0,2},{1,3},{2,0},{3,1},{4,6},{5,7},{6,4},{7,5},{8,10},{9,11},{10,... | collective-permute-start | bytes 442376 | tf_op jit(solution)/shard_map/ppermute | solution.py:253
  6.6 7.7 %collective-permute-start.2 = (bf16[64,1152]{1,0:T(8,128)(2,1)S(1)}, bf16[64,1152]{1,0:T(8,128)(2,1)S(1)}, u32[]{:S(2)}, u32[]{:S(2)}) collective-permute-start(bf16[64,1152]{1,0:T(8,128)(2,1)S(1)} %pack.1.refs_3_.refs_4_.refs_0_.refs_1_), channel_id=1, source_target_pairs={{0,4},{1,5},{2,6},{3,7},{4,0},{5,1},{6,2},{7,3},{8,12},{9,13},{10,... | collective-permute-start | bytes 442376 | tf_op jit(solution)/shard_map/ppermute | solution.py:253
  12.9 5.9 %collective-permute-start.5 = (bf16[64,1152]{1,0:T(8,128)(2,1)S(1)}, bf16[64,1152]{1,0:T(8,128)(2,1)S(1)}, u32[]{:S(2)}, u32[]{:S(2)}) collective-permute-start(bf16[64,1152]{1,0:T(8,128)(2,1)S(1)} %get-tuple-element.85.refs_0_.refs_9_), channel_id=1, source_target_pairs={{0,2},{1,3},{2,0},{3,1},{4,6},{5,7},{6,4},{7,5},{8,10},{9,11},{10,... | collective-permute-start | bytes 442376 | tf_op jit(solution)/shard_map/ppermute | solution.py:253
  13.8 5.1 %collective-permute-start.3 = (bf16[64,1152]{1,0:T(8,128)(2,1)S(1)}, bf16[64,1152]{1,0:T(8,128)(2,1)S(1)}, u32[]{:S(2)}, u32[]{:S(2)}) collective-permute-start(bf16[64,1152]{1,0:T(8,128)(2,1)S(1)} %get-tuple-element.85.refs_0_.refs_9_), channel_id=1, source_target_pairs={{0,4},{1,5},{2,6},{3,7},{4,0},{5,1},{6,2},{7,3},{8,12},{9,13},{10,... | collective-permute-start | bytes 442376 | tf_op jit(solution)/shard_map/ppermute | solution.py:253
  14.3 6.9 %collective-permute-start.6 = (bf16[64,1152]{1,0:T(8,128)(2,1)S(1)}, bf16[64,1152]{1,0:T(8,128)(2,1)S(1)}, u32[]{:S(2)}, u32[]{:S(2)}) collective-permute-start(bf16[64,1152]{1,0:T(8,128)(2,1)S(1)} %get-tuple-element.85.refs_0_.refs_9_), channel_id=1, source_target_pairs={{0,1},{1,0},{2,3},{3,2},{4,5},{5,4},{6,7},{7,6},{8,9},{9,8},{10,11... | collective-permute-start | bytes 442376 | tf_op jit(solution)/shard_map/ppermute | solution.py:253
  14.3 6.9 %collective-permute-start.8 = (bf16[64,1152]{1,0:T(8,128)(2,1)S(1)}, bf16[64,1152]{1,0:T(8,128)(2,1)S(1)}, u32[]{:S(2)}, u32[]{:S(2)}) collective-permute-start(bf16[64,1152]{1,0:T(8,128)(2,1)S(1)} %collective-permute-done.2.refs_0_.refs_5_), channel_id=1, source_target_pairs={{0,2},{1,3},{2,0},{3,1},{4,6},{5,7},{6,4},{7,5},{8,10},{9,11},{10,... | collective-permute-start | bytes 442376 | tf_op jit(solution)/shard_map/ppermute | solution.py:253
  18.9 2.3 %collective-permute-start.7 = (bf16[64,1152]{1,0:T(8,128)(2,1)S(1)}, bf16[64,1152]{1,0:T(8,128)(2,1)S(1)}, u32[]{:S(2)}, u32[]{:S(2)}) collective-permute-start(bf16[64,1152]{1,0:T(8,128)(2,1)S(1)} %get-tuple-element.89.refs_1_.refs_11_), channel_id=1, source_target_pairs={{0,1},{1,0},{2,3},{3,2},{4,5},{5,4},{6,7},{7,6},{8,9},{9,8},{10,11... | collective-permute-start | bytes 442376 | tf_op jit(solution)/shard_map/ppermute | solution.py:253
  18.9 6.3 %collective-permute-start.12 = (bf16[64,1152]{1,0:T(8,128)(2,1)S(1)}, bf16[64,1152]{1,0:T(8,128)(2,1)S(1)}, u32[]{:S(2)}, u32[]{:S(2)}) collective-permute-start(bf16[64,1152]{1,0:T(8,128)(2,1)S(1)} %collective-permute-done.3.refs_1_.refs_0_.refs_13_), channel_id=1, source_target_pairs={{0,2},{1,3},{2,0},{3,1},{4,6},{5,7},{6,4},{7,5},{8,10},{9,11},{10,... | collective-permute-start | bytes 442376 | tf_op jit(solution)/shard_map/ppermute | solution.py:253
  25.2 2.4 %collective-permute-start.14 = (bf16[64,1152]{1,0:T(8,128)(2,1)S(1)}, bf16[64,1152]{1,0:T(8,128)(2,1)S(1)}, u32[]{:S(2)}, u32[]{:S(2)}) collective-permute-start(bf16[64,1152]{1,0:T(8,128)(2,1)S(1)} %collective-permute-done.3.refs_1_.refs_0_.refs_13_), channel_id=1, source_target_pairs={{0,1},{1,0},{2,3},{3,2},{4,5},{5,4},{6,7},{7,6},{8,9},{9,8},{10,11... | collective-permute-start | bytes 442376 | tf_op jit(solution)/shard_map/ppermute | solution.py:253
  25.4 2.2 %collective-permute-start.15 = (bf16[64,1152]{1,0:T(8,128)(2,1)S(1)}, bf16[64,1152]{1,0:T(8,128)(2,1)S(1)}, u32[]{:S(2)}, u32[]{:S(2)}) collective-permute-start(bf16[64,1152]{1,0:T(8,128)(2,1)S(1)} %get-tuple-element.106.refs_1_.refs_15_), channel_id=1, source_target_pairs={{0,1},{1,0},{2,3},{3,2},{4,5},{5,4},{6,7},{7,6},{8,9},{9,8},{10,11... | collective-permute-start | bytes 442376 | tf_op jit(solution)/shard_map/ppermute | solution.py:253
  25.7 7.5 %collective-permute-start.16 = (bf16[64,1152]{1,0:T(8,128)(2,1)S(1)}, bf16[64,1152]{1,0:T(8,128)(2,1)S(1)}, u32[]{:S(2)}, u32[]{:S(2)}) collective-permute-start(bf16[64,1152]{1,0:T(8,128)(2,1)S(1)} %collective-permute-done.2.refs_0_.refs_5_), channel_id=1, source_target_pairs={{0,1},{1,0},{2,3},{3,2},{4,5},{5,4},{6,7},{7,6},{8,9},{9,8},{10,11... | collective-permute-start | bytes 442376 | tf_op jit(solution)/shard_map/ppermute | solution.py:253
  25.9 7.3 %collective-permute-start.17 = (bf16[64,1152]{1,0:T(8,128)(2,1)S(1)}, bf16[64,1152]{1,0:T(8,128)(2,1)S(1)}, u32[]{:S(2)}, u32[]{:S(2)}) collective-permute-start(bf16[64,1152]{1,0:T(8,128)(2,1)S(1)} %get-tuple-element.114.refs_1_.refs_7_), channel_id=1, source_target_pairs={{0,1},{1,0},{2,3},{3,2},{4,5},{5,4},{6,7},{7,6},{8,9},{9,8},{10,11... | collective-permute-start | bytes 442376 | tf_op jit(solution)/shard_map/ppermute | solution.py:253
  26.3 5.6 %collective-permute-start.13 = (bf16[64,1024]{1,0:T(8,128)(2,1)S(1)}, bf16[64,1024]{1,0:T(8,128)(2,1)S(1)}, u32[]{:S(2)}, u32[]{:S(2)}) collective-permute-start(bf16[64,1024]{1,0:T(8,128)(2,1)S(1)} %get-tuple-element.105), channel_id=1, source_target_pairs={{0,2},{1,3},{2,0},{3,1},{4,6},{5,7},{6,4},{7,5},{8,10},{9,11},{10,... | collective-permute-start | bytes 393224 | tf_op jit(solution)/shard_map/ppermute | solution.py:253
  32.0 7.0 %collective-permute-start.24 = (bf16[64,1024]{1,0:T(8,128)(2,1)S(1)}, bf16[64,1024]{1,0:T(8,128)(2,1)S(1)}, u32[]{:S(2)}, u32[]{:S(2)}) collective-permute-start(bf16[64,1024]{1,0:T(8,128)(2,1)S(1)} %get-tuple-element.131), channel_id=1, source_target_pairs={{0,2},{1,3},{2,0},{3,1},{4,6},{5,7},{6,4},{7,5},{8,10},{9,11},{10,... | collective-permute-start | bytes 393224 | tf_op jit(solution)/shard_map/ppermute | solution.py:253
  37.8 2.1 %collective-permute-start.22 = (bf16[64,1024]{1,0:T(8,128)(2,1)S(1)}, bf16[64,1024]{1,0:T(8,128)(2,1)S(1)}, u32[]{:S(2)}, u32[]{:S(2)}) collective-permute-start(bf16[64,1024]{1,0:T(8,128)(2,1)S(1)} %get-tuple-element.128), channel_id=1, source_target_pairs={{0,1},{1,0},{2,3},{3,2},{4,5},{5,4},{6,7},{7,6},{8,9},{9,8},{10,11... | collective-permute-start | bytes 393224 | tf_op jit(solution)/shard_map/ppermute | solution.py:253
  37.9 2.0 %collective-permute-start.23 = (bf16[64,1024]{1,0:T(8,128)(2,1)S(1)}, bf16[64,1024]{1,0:T(8,128)(2,1)S(1)}, u32[]{:S(2)}, u32[]{:S(2)}) collective-permute-start(bf16[64,1024]{1,0:T(8,128)(2,1)S(1)} %get-tuple-element.129), channel_id=1, source_target_pairs={{0,1},{1,0},{2,3},{3,2},{4,5},{5,4},{6,7},{7,6},{8,9},{9,8},{10,11... | collective-permute-start | bytes 393224 | tf_op jit(solution)/shard_map/ppermute | solution.py:253
  38.4 2.5 %collective-permute-start.20 = (bf16[64,1024]{1,0:T(8,128)(2,1)S(1)}, bf16[64,1024]{1,0:T(8,128)(2,1)S(1)}, u32[]{:S(2)}, u32[]{:S(2)}) collective-permute-start(bf16[64,1024]{1,0:T(8,128)(2,1)S(1)} %get-tuple-element.125), channel_id=1, source_target_pairs={{0,1},{1,0},{2,3},{3,2},{4,5},{5,4},{6,7},{7,6},{8,9},{9,8},{10,11... | collective-permute-start | bytes 393224 | tf_op jit(solution)/shard_map/ppermute | solution.py:253
  38.5 2.4 %collective-permute-start.21 = (bf16[64,1024]{1,0:T(8,128)(2,1)S(1)}, bf16[64,1024]{1,0:T(8,128)(2,1)S(1)}, u32[]{:S(2)}, u32[]{:S(2)}) collective-permute-start(bf16[64,1024]{1,0:T(8,128)(2,1)S(1)} %get-tuple-element.126), channel_id=1, source_target_pairs={{0,1},{1,0},{2,3},{3,2},{4,5},{5,4},{6,7},{7,6},{8,9},{9,8},{10,11... | collective-permute-start | bytes 393224 | tf_op jit(solution)/shard_map/ppermute | solution.py:253
  39.0 5.5 %collective-permute-start.25 = (bf16[64,1024]{1,0:T(8,128)(2,1)S(1)}, bf16[64,1024]{1,0:T(8,128)(2,1)S(1)}, u32[]{:S(2)}, u32[]{:S(2)}) collective-permute-start(bf16[64,1024]{1,0:T(8,128)(2,1)S(1)} %get-tuple-element.147), channel_id=1, source_target_pairs={{0,4},{1,5},{2,6},{3,7},{4,0},{5,1},{6,2},{7,3},{8,12},{9,13},{10,... | collective-permute-start | bytes 393224 | tf_op jit(solution)/shard_map/ppermute | solution.py:253
  40.0 7.2 %collective-permute-start.27 = (bf16[64,1024]{1,0:T(8,128)(2,1)S(1)}, bf16[64,1024]{1,0:T(8,128)(2,1)S(1)}, u32[]{:S(2)}, u32[]{:S(2)}) collective-permute-start(bf16[64,1024]{1,0:T(8,128)(2,1)S(1)} %get-tuple-element.153), channel_id=1, source_target_pairs={{0,2},{1,3},{2,0},{3,1},{4,6},{5,7},{6,4},{7,5},{8,10},{9,11},{10,... | collective-permute-start | bytes 393224 | tf_op jit(solution)/shard_map/ppermute | solution.py:253
  40.9 8.1 %collective-permute-start.29 = (bf16[64,1024]{1,0:T(8,128)(2,1)S(1)}, bf16[64,1024]{1,0:T(8,128)(2,1)S(1)}, u32[]{:S(2)}, u32[]{:S(2)}) collective-permute-start(bf16[64,1024]{1,0:T(8,128)(2,1)S(1)} %get-tuple-element.158), channel_id=1, source_target_pairs={{0,2},{1,3},{2,0},{3,1},{4,6},{5,7},{6,4},{7,5},{8,10},{9,11},{10,... | collective-permute-start | bytes 393224 | tf_op jit(solution)/shard_map/ppermute | solution.py:253
  44.5 8.7 %collective-permute-start.26 = (bf16[64,1024]{1,0:T(8,128)(2,1)S(1)}, bf16[64,1024]{1,0:T(8,128)(2,1)S(1)}, u32[]{:S(2)}, u32[]{:S(2)}) collective-permute-start(bf16[64,1024]{1,0:T(8,128)(2,1)S(1)} %get-tuple-element.151), channel_id=1, source_target_pairs={{0,8},{1,9},{2,10},{3,11},{4,12},{5,13},{6,14},{7,15},{8,0},{9,1},... | collective-permute-start | bytes 393224 | tf_op jit(solution)/shard_map/ppermute | solution.py:253
  47.2 6.6 %collective-permute-start.28 = (bf16[64,1024]{1,0:T(8,128)(2,1)S(1)}, bf16[64,1024]{1,0:T(8,128)(2,1)S(1)}, u32[]{:S(2)}, u32[]{:S(2)}) collective-permute-start(bf16[64,1024]{1,0:T(8,128)(2,1)S(1)} %get-tuple-element.157), channel_id=1, source_target_pairs={{0,4},{1,5},{2,6},{3,7},{4,0},{5,1},{6,2},{7,3},{8,12},{9,13},{10,... | collective-permute-start | bytes 393224 | tf_op jit(solution)/shard_map/ppermute | solution.py:253
  (6 other events, 10.0 us)
